TPU v7x, 32 devices: a whole 2x2x4 slice. The times are simulated.
32 devices in a mesh: rep: 2 (over y), dev: 4 (over z), side: 4 (over x, core).
Axes of the slice: x: 2, y: 2, z: 4, core: 2. Of those that a mesh axis runs over, the one named last changes fastest.
Arguments:
- prompts: bfloat16 [2048, 7168], P(('rep', 'dev', 'side')), parts along dimension 0, may hold values from -6 to 6
- latent_weight: bfloat16 [7168, 576], P(('dev', 'side')), may hold values from -0.0625 to 0.0625
- latent_gain: float32 [512], replicated, may hold values from 0.25 to 1.75
- row_request: int32 [2048], P('rep'), parts along dimension 0, may hold values from 0 to 15, as said below
- context_len: int32 [32], P('rep'), parts along dimension 0, may hold values from 1 to 256, as said below
- request_slot: int32 [32], P('rep'), parts along dimension 0, may hold values from 0 to 31, as said below
- latent_cache: bfloat16 [64, 256, 576], P(('rep', 'dev')), parts along dimension 0, may hold values from -6 to 6
- new_latent: bfloat16 [64, 2, 576], P(('rep', 'dev')), parts along dimension 0, may hold values from -6 to 6
- queries: bfloat16 [64, 2, 128, 192], P(('rep', 'dev'), None, 'side'), parts along dimension 0, may hold values from -80 to 80
- key_absorb: bfloat16 [128, 128, 512], P('side'), may hold values from -0.5 to 0.5
- value_absorb: bfloat16 [128, 512, 128], P('side'), may hold values from -0.25 to 0.25
- out_weight: bfloat16 [16384, 7168], P('side', 'dev'), may hold values from -0.125 to 0.125
Outputs:
- decoded: bfloat16 [128, 7168], P(('rep', 'side'), 'dev'), parts along dimension 0
There are 2 independent parts, one for each index of `rep`. A program takes and returns all parts, laid end to end along the dimension named above; an argument that names none is the same for every part. Nothing has to cross between parts.
Inputs may be any that keep to these rules, and one draw needn't show every extreme that they name: `request_slot`: slots are distinct; each decode group (slots g*8 to g*8 + 7) holds at least one request, and one group is full. `row_request`: in each aligned block of 64 rows, at most 32 rows belong to requests of one decode group (request_slot // 8); one group receives exactly 32 rows from every block. `context_len`: some request has exactly 256 cached rows.
All inputs are finite; a program needn't handle non-finite values.
Results may differ from a plain program's by a relative error of at most 0.0081.
Values may be sent and summed in bfloat16 or wider, within the bound.
No kernel may reach another device: no remote copies, remote signals or barrier semaphores. Data moves between devices by JAX's collectives and lax.ppermute only.
A program may use at most 128 MiB of HBM per device.

v0:
```python
import jax
import jax.numpy as jnp
from jax import lax
from jax.sharding import PartitionSpec as P

masked_score = -1e30


def prefix(shard, axis, combine, identity):
    count, here = (lax.axis_size(axis), lax.axis_index(axis))
    everything = lax.all_gather(shard, axis)
    start = jnp.broadcast_to(jnp.asarray(identity, shard.dtype), shard.shape)

    def hop(k, before):
        reached = k < here
        new = combine(before, everything[k])
        return jnp.where(reached, new, before)

    return lax.fori_loop(0, count, hop, start)


def rotate_pairs(values, position):
    half_width = values.shape[-1] // 2
    inverse = 1.0 / 10000.0 ** (
        jnp.arange(half_width, dtype=jnp.float32) * (2.0 / values.shape[-1])
    )
    angles = position.astype(jnp.float32)[:, None] * inverse[None, :]
    cosine = jnp.cos(angles)
    sine = jnp.sin(angles)
    first_half = values[:, :half_width]
    second_half = values[:, half_width:]
    return jnp.concatenate(
        [first_half * cosine - second_half * sine, second_half * cosine + first_half * sine], axis=1
    )


def norm_and_rotate(raw, gain, position, lat_width):
    latent = raw[:, :lat_width]
    spread = jnp.mean(latent * latent, axis=1, keepdims=True)
    normed = latent * lax.rsqrt(spread + 1e-06) * gain[None, :]
    return jnp.concatenate([normed, rotate_pairs(raw[:, lat_width:], position)], axis=1).astype(
        jnp.bfloat16
    )


def on_device(
    prompts,
    latent_weight,
    latent_gain,
    row_request,
    context_len,
    request_slot,
    latent_cache,
    new_latent,
    queries,
    key_absorb,
    value_absorb,
    out_weight,
):
    dev_count = lax.axis_size("dev")
    side_count = lax.axis_size("side")
    block_count = dev_count * side_count
    tok_rows = prompts.shape[0]
    kv_width = latent_weight.shape[1]
    lat_width = latent_gain.shape[0]
    nope_width = key_absorb.shape[1]
    req_count = request_slot.shape[0]
    cap_slots = latent_cache.shape[0]
    step_count = new_latent.shape[1]
    bucket_rows = 2 * tok_rows // dev_count
    my_block = lax.axis_index(("dev", "side"))
    my_group = lax.axis_index("dev")
    raw = jnp.dot(
        prompts,
        lax.all_gather(latent_weight, ("dev", "side"), axis=0, tiled=True),
        preferred_element_type=jnp.float32,
    )
    all_requests = row_request.reshape(block_count, tok_rows)
    my_requests = lax.dynamic_index_in_dim(all_requests, my_block, 0, keepdims=False)
    request_ids = jnp.arange(req_count, dtype=jnp.int32)
    req_hit = (my_requests[:, None] == request_ids[None, :]).astype(jnp.int32)
    counts = jnp.sum(req_hit, axis=0)
    earlier = prefix(counts, ("dev", "side"), lambda a, b: a + b, jnp.zeros_like(counts))
    rank_local = jnp.cumsum(req_hit, axis=0) - req_hit
    position = jnp.sum(req_hit * ((context_len + earlier)[None, :] + rank_local), axis=1)
    latent_rows = norm_and_rotate(raw, latent_gain, position, lat_width)
    slot_table = jnp.sum(
        (all_requests[:, :, None] == request_ids[None, None, :]).astype(jnp.int32)
        * request_slot[None, None, :],
        axis=2,
    )
    row_group = slot_table // cap_slots
    group_hit = (
        row_group[:, :, None] == jnp.arange(dev_count, dtype=jnp.int32)[None, None, :]
    ).astype(jnp.int32)
    group_rank = jnp.sum((jnp.cumsum(group_hit, axis=1) - group_hit) * group_hit, axis=2)
    destination = row_group * bucket_rows + group_rank
    my_destination = lax.dynamic_index_in_dim(destination, my_block, 0, keepdims=False)
    send_rows = (
        jnp.zeros((dev_count * bucket_rows, kv_width), jnp.bfloat16)
        .at[my_destination]
        .set(latent_rows)
    )
    send_rows = send_rows.reshape(dev_count, bucket_rows, kv_width)
    position_table = jnp.full((block_count, dev_count * bucket_rows), -1, jnp.int32)
    position_table = position_table.at[jnp.arange(block_count)[:, None], destination].set(
        slot_table
    )
    own_table = lax.dynamic_slice_in_dim(position_table, my_group * bucket_rows, bucket_rows, 1)
    copies = jnp.broadcast_to(
        send_rows[:, None], (dev_count, side_count, bucket_rows, kv_width)
    ).reshape(block_count, bucket_rows, kv_width)
    group_rows = lax.all_to_all(copies, ("dev", "side"), split_axis=0, concat_axis=0, tiled=True)
    row_slot = own_table.reshape(-1)
    group_rows = group_rows.reshape(-1, kv_width)
    own_slots = my_group * cap_slots + jnp.arange(cap_slots, dtype=jnp.int32)
    slot_hit = (own_slots[:, None] == request_slot[None, :]).astype(jnp.int32)
    occupied = (jnp.sum(slot_hit, axis=1) > 0).astype(jnp.float32)
    ctx_rows = jnp.sum(slot_hit * context_len[None, :], axis=1)
    query_latent = jnp.einsum(
        "sthn,hnc->sthc", queries[..., :nope_width], key_absorb, preferred_element_type=jnp.float32
    ).astype(jnp.bfloat16)
    query_full = jnp.concatenate([query_latent, queries[..., nope_width:]], axis=-1)
    score_scale = queries.shape[-1] ** (-0.5)
    score_cache = (
        jnp.einsum("sthc,sjc->sthj", query_full, latent_cache, preferred_element_type=jnp.float32)
        * score_scale
    )
    score_prompt = (
        jnp.einsum("sthc,pc->sthp", query_full, group_rows, preferred_element_type=jnp.float32)
        * score_scale
    )
    score_fresh = (
        jnp.einsum("sthc,suc->sthu", query_full, new_latent, preferred_element_type=jnp.float32)
        * score_scale
    )
    mask_cache = (jnp.arange(latent_cache.shape[1])[None, :] < ctx_rows[:, None])[:, None, None, :]
    mask_prompt = (row_slot[None, :] == own_slots[:, None])[:, None, None, :]
    mask_fresh = (jnp.arange(step_count)[None, :] <= jnp.arange(step_count)[:, None])[
        None, :, None, :
    ]
    score_cache = jnp.where(mask_cache, score_cache, masked_score)
    score_prompt = jnp.where(mask_prompt, score_prompt, masked_score)
    score_fresh = jnp.where(mask_fresh, score_fresh, masked_score)
    largest = jnp.maximum(
        jnp.maximum(
            jnp.max(score_cache, axis=-1, keepdims=True),
            jnp.max(score_prompt, axis=-1, keepdims=True),
        ),
        jnp.max(score_fresh, axis=-1, keepdims=True),
    )
    exp_cache = jnp.where(mask_cache, jnp.exp(score_cache - largest), 0.0)
    exp_prompt = jnp.where(mask_prompt, jnp.exp(score_prompt - largest), 0.0)
    exp_fresh = jnp.where(mask_fresh, jnp.exp(score_fresh - largest), 0.0)
    denominator = (
        jnp.sum(exp_cache, axis=-1, keepdims=True)
        + jnp.sum(exp_prompt, axis=-1, keepdims=True)
        + jnp.sum(exp_fresh, axis=-1, keepdims=True)
    )
    weight_cache = (exp_cache / denominator).astype(jnp.bfloat16)
    weight_prompt = (exp_prompt / denominator).astype(jnp.bfloat16)
    weight_fresh = (exp_fresh / denominator).astype(jnp.bfloat16)
    head_latent = jnp.einsum(
        "sthj,sjc->sthc",
        weight_cache,
        latent_cache[..., :lat_width],
        preferred_element_type=jnp.float32,
    )
    head_latent = head_latent + jnp.einsum(
        "sthp,pc->sthc",
        weight_prompt,
        group_rows[:, :lat_width],
        preferred_element_type=jnp.float32,
    )
    head_latent = head_latent + jnp.einsum(
        "sthu,suc->sthc",
        weight_fresh,
        new_latent[..., :lat_width],
        preferred_element_type=jnp.float32,
    )
    head_latent = head_latent.astype(jnp.bfloat16)
    head_out = (
        jnp.einsum("sthc,hcn->sthn", head_latent, value_absorb, preferred_element_type=jnp.float32)
        * occupied[:, None, None, None]
    )
    head_out = head_out.astype(jnp.bfloat16).reshape(cap_slots * step_count, -1)
    partial_out = jnp.dot(
        lax.all_gather(head_out, "dev", axis=0, tiled=True),
        out_weight,
        preferred_element_type=jnp.float32,
    )
    return lax.psum_scatter(partial_out, "side", scatter_dimension=0, tiled=True).astype(
        jnp.bfloat16
    )


def solution(mesh):
    placed = (
        P(("rep", "dev", "side"), None),
        P(("dev", "side"), None),
        P(),
        P("rep"),
        P("rep"),
        P("rep"),
        P(("rep", "dev"), None, None),
        P(("rep", "dev"), None, None),
        P(("rep", "dev"), None, "side", None),
        P("side", None, None),
        P("side", None, None),
        P("side", "dev"),
    )
    return jax.shard_map(
        on_device, mesh=mesh, in_specs=placed, out_specs=P(("rep", "side"), "dev"), check_vma=False
    )
```

profile of v0, /device:TPU:0, one launch (start us, length us, event | category | flops | bytes accessed | tf_op | source)
XLA Modules:
  0.0 181.0 jit_solution(1660358885452730926)
XLA Ops:
  6.5 0.7 all-gather.3.cloned.1.call-update
  7.3 0.9 slice.27
  8.2 0.9 slice.28
  9.1 0.8 eq.78
  9.9 0.8 select_reduce_fusion.1
  10.7 1.3 dynamic-slice
  12.6 0.1 fusion.61
  12.7 0.2 dynamic-update-slice
  13.0 13.8 %all-reduce = s32[256]{0:T(256)S(1)} all-reduce(s32[256]{0:T(256)S(1)} %dynamic-update-slice), channel_id=2, replica_groups=mesh['rep'=2,'dev'=4,'side'=4] {'dev','side'}, use_global_device_ids=true, to_apply=%add | all-reduce | flops 256 | bytes 2048
  27.0 1.4 select_reduce_fusion
  28.5 0.7 multiply_reduce_fusion.1
  29.2 0.7 and_reduce_fusion
  30.1 4.3 %scatter_custom_fusion.1 = s32[2048]{0:T(1024)S(1)} fusion(s32[1024]{0:T(1024)S(1)} %reshape.234, s32[1024]{0:T(1024)S(1)} %reshape.236, s32[]{:T(128)} %constant.89.clone.1), kind=kCustom, calls=%fused_computation.116 | custom fusion | bytes 8196
  34.6 0.1 reduce_window_sum.23
  34.7 0.6 while.14
  35.4 0.7 add.162
  36.0 0.2 select_reduce_fusion.2
  36.4 0.9 fusion.82
  37.2 2.8 %fusion.14 = bf16[8,2,32,512]{3,0,1,2:T(8,128)(2,1)S(1)} fusion(bf16[32,128,512]{2,1,0:T(8,128)(2,1)} %param.23, bf16[8,2,32,128]{3,2,1,0:T(8,128)(2,1)S(1)} %slice.27), kind=kOutput, calls=%fused_computation.19 | convolution fusion | flops 67371008 | bytes 4849664 | tf_op jit(solution)/shard_map/sthn,hnc->sthc/dot_general | solution.py:120
  40.1 0.9 pad_maximum_fusion
  41.0 0.5 compare_convert_fusion.1
  41.5 50.7 %all-gather.3.cloned.1.call-done = bf16[7168,576]{1,0:T(8,128)(2,1)} async-done(((bf16[448,576]{1,0:T(8,128)(2,1)}), bf16[7168,576]{1,0:T(8,128)(2,1)}) %all-gather.3.cloned.1.call-update) | async-done | bytes 8257552 | tf_op jit(solution)/shard_map/all_gather | solution.py:75
  92.3 5.2 %fusion.97 = f32[64,576]{1,0:T(8,128)S(1)} fusion(bf16[64,7168]{1,0:T(8,128)(2,1)S(1)} %copy-done, bf16[7168,576]{1,0:T(8,128)(2,1)} %all-gather.3.cloned.1.call-done), kind=kOutput, calls=%fused_computation.141 | convolution fusion | flops 528482304 | bytes 9322496 | tf_op jit(solution)/shard_map/dot_general | solution.py:73
  97.5 0.1 multiply_reduce_fusion
  97.8 0.2 fusion.68
  98.0 0.1 copy.103
  98.1 0.1 copy.104
  98.3 1.0 scatter_custom_fusion
  99.3 0.9 broadcast_in_dim.113
  100.2 4.3 %all-to-all-start = ((bf16[16,32,576]{2,1,0:T(8,128)(2,1)}), bf16[16,32,576]{2,1,0:T(8,128)(2,1)}, u32[]{:S(2)}, u32[]{:S(2)}) async-start(bf16[16,32,576]{2,1,0:T(8,128)(2,1)} %bitcast.13), calls=%async_computation | async-start | bytes 1310720 | tf_op jit(solution)/shard_map/all_to_all | solution.py:113
  104.6 0.7 broadcast_compare_fusion
  105.2 2.5 %fusion.94 = (f32[8,2,32]{2,1,0:T(2,128)}, f32[8,2,32,2]{2,3,1,0:T(2,128)S(1)}) fusion(bf16[8,2,576]{2,1,0:T(2,128)(2,1)S(1)} %copy-done.6, bf16[8,2,32,576]{3,0,1,2:T(8,128)(2,1)} %pad_maximum_fusion, pred[2,2]{1,0:T(4,128)(4,1)S(1)} %iota_compare_fusion.5), kind=kOutput, calls=%fused_computation.138 | convolution fusion | flops 1182208 | bytes 614404 | tf_op jit(solution)/shard_map/sthc,suc->sthu/dot_general | solution.py:134
  107.7 3.1 %fusion.95 = (f32[8,2,32]{2,1,0:T(2,128)}, f32[8,2,32,256]{3,2,1,0:T(8,128)S(1)}) fusion(bf16[8,256,576]{1,2,0:T(8,128)(2,1)} %param.20, bf16[8,2,32,576]{3,0,1,2:T(8,128)(2,1)} %pad_maximum_fusion, pred[8,256]{1,0:T(8,128)(4,1)S(1)} %iota_compare_fusion.4), kind=kOutput, calls=%fused_computation.139 | convolution fusion | flops 151387648 | bytes 3477504 | tf_op jit(solution)/shard_map/sthc,sjc->sthj/dot_general | solution.py:126
  110.9 10.2 %all-to-all-done = bf16[16,32,576]{2,1,0:T(8,128)(2,1)} async-done(((bf16[16,32,576]{2,1,0:T(8,128)(2,1)}), bf16[16,32,576]{2,1,0:T(8,128)(2,1)}, u32[]{:S(2)}, u32[]{:S(2)}) %all-to-all-start) | async-done | bytes 589856 | tf_op jit(solution)/shard_map/all_to_all | solution.py:113
  121.1 2.1 %fusion.96 = (f32[8,2,32]{2,1,0:T(2,128)S(1)}, f32[8,2,32,512]{3,2,1,0:T(8,128)S(1)}) fusion(bf16[512,576,1,1]{1,0,3,2:T(8,128)(2,1)} %bitcast.15, bf16[8,2,32,576]{3,0,1,2:T(8,128)(2,1)} %pad_maximum_fusion, pred[8,512]{1,0:T(8,128)(4,1)} %broadcast_compare_fusion), kind=kOutput, calls=%fused_computation.140 | convolution fusion | flops 302775808 | bytes 2234368 | tf_op jit(solution)/shard_map/sthc,pc->sthp/dot_general | solution.py:130
  123.2 0.9 maximum_maximum_fusion
  124.1 0.7 fusion.89
  124.8 1.0 fusion.33
  125.9 0.9 fusion.46
  126.9 0.8 fusion.6
  127.7 1.9 %convolution_add_fusion.1 = f32[8,2,32,512]{3,2,1,0:T(8,128)S(1)} fusion(f32[8,2,32,512]{3,2,1,0:T(8,128)S(1)} %fusion.6, f32[8,2,32,512]{3,2,1,0:T(8,128)S(1)} %get-tuple-element.119, bf16[512,576]{1,0:T(8,128)(2,1)} %bitcast.14, f32[8,2,32]{2,1,0:T(2,128)S(1)} %bitcast.125, f32[8,2,32]{2,1,0:T(2,128)S(1)} %bitcast.122, pred[8,512]{1,0:T(8,128)(4,1)S(1)} %copy-done.5), kind=kOutput, calls=%fused_computation.14 | convolution fusion | flops 269746176 | bytes 3678208 | tf_op jit(solution)/shard_map/sthp,pc->sthc/dot_general | solution.py:169
  129.7 0.4 fusion.10
  130.1 0.3 copy-done.1
  130.4 0.8 fusion.29
  131.3 15.5 %all_gather.15 = bf16[64,4096]{1,0:T(8,128)(2,1)S(1)} all-gather(bf16[16,4096]{1,0:T(8,128)(2,1)S(1)} %bitcast.116), channel_id=1, replica_groups=mesh['rep'=2,'dev'=4,'side'=4] {'dev'}, dimensions={0}, use_global_device_ids=true | all-gather | bytes 655360 | tf_op jit(solution)/shard_map/all_gather | solution.py:188
  146.9 3.4 %fusion.98 = f32[64,1792]{1,0:T(8,128)} fusion(bf16[64,4096]{1,0:T(8,128)(2,1)S(1)} %all_gather.15, bf16[4096,1792]{1,0:T(8,128)(2,1)S(1)} %bitcast.114), kind=kOutput, calls=%fused_computation.142 | convolution fusion | flops 939524096 | bytes 15663104 | tf_op jit(solution)/shard_map/dot_general | solution.py:187
  150.3 22.3 %reduce-scatter.2.cloned.1.call-done = f32[16,1792]{1,0:T(8,128)} async-done(((f32[64,1792]{1,0:T(8,128)}), f32[16,1792]{1,0:T(8,128)}) %reduce-scatter.2.cloned.1.call-update) | async-done | bytes 114704 | tf_op jit(solution)/shard_map/reduce_scatter | solution.py:192
  172.6 1.5 convert_element_type.65
  (81 shorter events, 1.7 us)
Async XLA Ops:
  6.5 85.7 %copy-start = (bf16[64,7168]{1,0:T(8,128)(2,1)S(1)}, bf16[64,7168]{1,0:T(8,128)(2,1)}, u32[]{:S(2)}) copy-start(bf16[64,7168]{1,0:T(8,128)(2,1)} %param.14) | copy-start | bytes 2752516
  6.5 85.7 %all-gather.3.cloned.1.call-start = ((), (), s32[]{:S(2)}) async-start(), calls=%async_computation.2 | async-start | bytes 9748480 | tf_op jit(solution)/shard_map/all_gather | solution.py:75
  41.5 56.6 %copy-start.8 = (f32[512]{0:T(512)S(1)}, f32[512]{0:T(512)}, u32[]{:S(2)}) copy-start(f32[512]{0:T(512)} %param.16) | copy-start | bytes 6148
  41.5 63.7 %copy-start.6 = (bf16[8,2,576]{2,1,0:T(2,128)(2,1)S(1)}, bf16[8,2,576]{2,1,0:T(2,128)(2,1)}, u32[]{:S(2)}) copy-start(bf16[8,2,576]{2,1,0:T(2,128)(2,1)} %param.21) | copy-start | bytes 55300
  100.2 20.9 %all-to-all-start = ((bf16[16,32,576]{2,1,0:T(8,128)(2,1)}), bf16[16,32,576]{2,1,0:T(8,128)(2,1)}, u32[]{:S(2)}, u32[]{:S(2)}) async-start(bf16[16,32,576]{2,1,0:T(8,128)(2,1)} %bitcast.13), calls=%async_computation | async-start | bytes 1310720 | tf_op jit(solution)/shard_map/all_to_all | solution.py:113
  104.4 68.2 %reduce-scatter.2.cloned.1.call-start = ((), (), s32[]{:S(2)}) async-start(), calls=%async_computation.3 | async-start | bytes 573440 | tf_op jit(solution)/shard_map/reduce_scatter | solution.py:192
  104.5 0.7 copy-start.9
  104.6 3.1 %copy-start.3 = (pred[8,256]{1,0:T(8,128)(4,1)}, pred[8,256]{1,0:T(8,128)(4,1)S(1)}, u32[]{:S(2)}) copy-start(pred[8,256]{1,0:T(8,128)(4,1)S(1)} %iota_compare_fusion.4) | copy-start | bytes 6148
  105.2 41.6 %slice-start = ((s8[14680064]{0:T(1024)(128)(4,1)}), s8[2097152]{0:T(1024)(128)(4,1)S(1)}, s32[]{:S(2)}) async-start(s8[14680064]{0:T(1024)(128)(4,1)} %bitcast.113), calls=%async_computation.4 | async-start | bytes 4194304
  121.0 5.8 %copy-start.2 = (bf16[8,256,576]{1,2,0:T(8,128)(2,1)S(1)}, bf16[8,256,576]{1,2,0:T(8,128)(2,1)}, u32[]{:S(2)}) copy-start(bf16[8,256,576]{1,2,0:T(8,128)(2,1)} %param.20) | copy-start | bytes 7077892
  121.0 5.8 %copy-start.4 = (pred[8,256]{1,0:T(8,128)(4,1)S(1)}, pred[8,256]{1,0:T(8,128)(4,1)}, u32[]{:S(2)}) copy-start(pred[8,256]{1,0:T(8,128)(4,1)} %copy-done.3) | copy-start | bytes 6148
  121.0 6.6 %copy-start.5 = (pred[8,512]{1,0:T(8,128)(4,1)S(1)}, pred[8,512]{1,0:T(8,128)(4,1)}, u32[]{:S(2)}) copy-start(pred[8,512]{1,0:T(8,128)(4,1)} %broadcast_compare_fusion) | copy-start | bytes 12292
  121.0 25.8 %slice-start.1 = ((s8[14680064]{0:T(1024)(128)(4,1)}), s8[4194304]{0:T(1024)(128)(4,1)S(1)}, s32[]{:S(2)}) async-start(s8[14680064]{0:T(1024)(128)(4,1)} %bitcast.113), calls=%async_computation.5 | async-start | bytes 8388608
  126.9 20.0 %slice-start.2 = ((s8[14680064]{0:T(1024)(128)(4,1)}), s8[4194304]{0:T(1024)(128)(4,1)S(1)}, s32[]{:S(2)}) async-start(s8[14680064]{0:T(1024)(128)(4,1)} %bitcast.113), calls=%async_computation.6 | async-start | bytes 8388608
  127.6 2.0 %copy-start.7 = (bf16[8,2,576]{2,1,0:T(2,128)(2,1)S(1)}, bf16[8,2,576]{2,1,0:T(2,128)(2,1)}, u32[]{:S(2)}) copy-start(bf16[8,2,576]{2,1,0:T(2,128)(2,1)} %param.21) | copy-start | bytes 55300
  127.7 2.0 %copy-start.10 = (pred[2,2]{1,0:T(4,128)(4,1)S(1)}, pred[2,2]{1,0:T(4,128)(4,1)}, u32[]{:S(2)}) copy-start(pred[2,2]{1,0:T(4,128)(4,1)} %copy-done.9) | copy-start | bytes 16
  127.7 2.7 %copy-start.1 = (bf16[32,512,128]{2,1,0:T(8,128)(2,1)S(1)}, bf16[32,512,128]{2,1,0:T(8,128)(2,1)}, u32[]{:S(2)}) copy-start(bf16[32,512,128]{2,1,0:T(8,128)(2,1)} %param.24) | copy-start | bytes 12582916
  127.7 2.7 %copy-start.11 = (f32[8]{0:T(128)S(1)}, f32[8]{0:T(128)}, u32[]{:S(2)}) copy-start(f32[8]{0:T(128)} %compare_convert_fusion.1) | copy-start | bytes 100
  129.6 17.2 %slice-start.3 = ((s8[14680064]{0:T(1024)(128)(4,1)}), s8[4194304]{0:T(1024)(128)(4,1)S(1)}, s32[]{:S(2)}) async-start(s8[14680064]{0:T(1024)(128)(4,1)} %bitcast.113), calls=%async_computation.7 | async-start | bytes 8388608
Sparse Core Ops, SparseCore 0:
  9.6 82.5 all-gather.2
  150.4 22.1 reduce-scatter.1
where the time goes:
time: 182 us; the launch traced here: 181 us
  waiting for transfers between devices  84 us (46%)
  blocking collectives  29.3 us (16%)
  matrix products  23.1 us (13%)
  other arithmetic  14.7 us (8%)
  between operations  14.4 us (8%)
  local copies, waits for them, and re-layouts  10.9 us (6%)
  starting transfers between devices  4.31 us (2%)
    all_gather x1, waiting for transfers between devices, on_device(): lax.all_gather(latent_weight, ('dev', 'side'), axis=0, tiled=True)  50.7 us
    reduce_scatter x1, waiting for transfers between devices, on_device(): lax.psum_scatter(partial_out, 'side', scatter_dimension=0, tiled=True)  22.3 us
    all_gather x1, blocking collectives, on_device(): lax.all_gather(head_out, 'dev', axis=0, tiled=True)  15.5 us
    unnamed x1, blocking collectives  13.8 us
    all_to_all x1, waiting for transfers between devices, on_device(): lax.all_to_all(copies, ('dev', 'side'), split_axis=0, concat_axis=0, tile...  10.2 us
    unnamed x41, local copies, waits for them, and re-layouts  6.59 us
    dot_general x1, matrix products, on_device(): jnp.dot(prompts, lax.all_gather(latent_weight, ('dev', 'side'), axis=0, t...  5.19 us
    all_to_all x1, starting transfers between devices, on_device(): lax.all_to_all(copies, ('dev', 'side'), split_axis=0, concat_axis=0, tile...  4.26 us
  transfers between devices with their start and end apart: 3, of which 3 were waited for; matrix products, arithmetic and copies ran while one was open for 14% of the time, Pallas kernels for 0%

commit v1 on v0

v1 whole, which is shorter than its diff:
```python
import jax
import jax.numpy as jnp
from jax import lax
from jax.sharding import PartitionSpec as P

masked_score = -1e30


def swap(value, axis, step):
    count = lax.axis_size(axis)
    return lax.ppermute(value, axis, [(i, i ^ step) for i in range(count)])


def pick(pieces, index):
    out = pieces[0]
    for k in range(1, len(pieces)):
        out = jnp.where(index == k, pieces[k], out)
    return out


def on_device(
    prompts,
    latent_weight,
    latent_gain,
    row_request,
    context_len,
    request_slot,
    latent_cache,
    new_latent,
    queries,
    key_absorb,
    value_absorb,
    out_weight,
):
    dev_count = lax.axis_size("dev")
    side_count = lax.axis_size("side")
    block_count = dev_count * side_count
    tok_rows, model_width = prompts.shape
    shard_rows, kv_width = latent_weight.shape
    lat_width = latent_gain.shape[0]
    head_count, nope_width, _ = key_absorb.shape
    rope_width = kv_width - lat_width
    req_count = request_slot.shape[0]
    cap_slots, ctx_len, _ = latent_cache.shape
    step_count = new_latent.shape[1]
    bucket_rows = 2 * tok_rows // dev_count
    slab = model_width // dev_count
    row_count = head_count * cap_slots * step_count
    my_dev = lax.axis_index("dev")
    my_side = lax.axis_index("side")
    bf16, f32 = jnp.bfloat16, jnp.float32

    columns = [prompts[:, k * slab : (k + 1) * slab] for k in range(dev_count)]
    x_pieces = [None] * dev_count
    for k in sorted(range(dev_count), reverse=True):
        mine = pick(columns, my_dev ^ k)
        x_pieces[k] = swap(mine, "dev", k) if k else mine

    held = jnp.zeros((side_count, shard_rows, kv_width), bf16)
    for k in range(0, side_count, 2):
        piece = swap(latent_weight, "side", k) if k else latent_weight
        held = lax.dynamic_update_slice(held, piece[None], (my_side ^ k, 0, 0))
    same_core = held.reshape(side_count // 2, 2, shard_rows, kv_width)
    my_core = my_side % 2
    same_core = lax.dynamic_slice_in_dim(same_core, my_core, 1, 1)
    other_core = swap(same_core, "side", 1)
    held = lax.dynamic_update_slice(
        held.reshape(side_count // 2, 2, shard_rows, kv_width), other_core, (0, 1 - my_core, 0, 0)
    )
    slab_weight = held.reshape(slab, kv_width)

    request_ids = jnp.arange(req_count, dtype=jnp.int32)
    all_requests = row_request.reshape(block_count, tok_rows)
    hit = (all_requests[:, :, None] == request_ids).astype(f32)
    below = (jnp.arange(tok_rows)[:, None] > jnp.arange(tok_rows)[None, :]).astype(f32)
    rank_local = jnp.einsum("ij,bjr->bir", below, hit, preferred_element_type=f32)
    counts = jnp.sum(hit, axis=1)
    before = (jnp.arange(block_count)[:, None] > jnp.arange(block_count)[None, :]).astype(f32)
    earlier = jnp.einsum("ab,br->ar", before, counts, precision=lax.Precision.HIGHEST)
    position = jnp.sum(
        hit * (rank_local + earlier[:, None, :] + context_len.astype(f32)), axis=2
    )
    slot_table = jnp.sum(hit * request_slot.astype(f32), axis=2).astype(jnp.int32)
    row_group = slot_table // cap_slots
    group_ids = jnp.arange(dev_count, dtype=jnp.int32)
    group_hit = (row_group[:, :, None] == group_ids).astype(f32)
    group_rank = jnp.sum(
        jnp.einsum("ij,bjg->big", below, group_hit, preferred_element_type=f32) * group_hit, axis=2
    ).astype(jnp.int32)
    placed = (
        (row_group[:, None, None, :] == group_ids[None, :, None, None])
        & (
            group_rank[:, None, None, :]
            == jnp.arange(bucket_rows, dtype=jnp.int32)[None, None, :, None]
        )
    )
    line = lax.dynamic_index_in_dim(
        placed.reshape(dev_count, side_count, dev_count, bucket_rows, tok_rows),
        my_side, 1, keepdims=False,
    )
    to_me = lax.dynamic_index_in_dim(line, my_dev, 1, keepdims=False).astype(f32)
    line_position = lax.dynamic_index_in_dim(
        position.reshape(dev_count, side_count, tok_rows), my_side, 1, keepdims=False
    )
    routed_position = jnp.sum(to_me * line_position[:, None, :], axis=2).reshape(-1)
    group_placed = lax.dynamic_index_in_dim(placed, my_dev, 1, keepdims=False)
    row_slot = jnp.max(jnp.where(group_placed, slot_table[:, None, :], -1), axis=2)
    row_slot = jnp.swapaxes(row_slot.reshape(dev_count, side_count, bucket_rows), 0, 1)

    order = my_dev ^ jnp.arange(dev_count, dtype=jnp.int32)
    by_step = jnp.take(line, order, axis=1).astype(bf16)
    same = (jnp.arange(dev_count)[:, None] == order[None, :]).astype(bf16)
    route = jnp.swapaxes(by_step, 0, 1)[:, :, :, None, :] * same[None, :, None, :, None]
    route = route.reshape(dev_count * dev_count * bucket_rows, dev_count * tok_rows)

    half = rope_width // 2
    inverse = 1.0 / 10000.0 ** (jnp.arange(half, dtype=f32) * (2.0 / rope_width))
    angles = routed_position[:, None] * inverse[None, :]
    cosine, sine = jnp.cos(angles), jnp.sin(angles)

    query_latent = jnp.einsum(
        "sthn,hnc->hstc", queries[..., :nope_width], key_absorb, preferred_element_type=f32
    ).astype(bf16)
    query_full = jnp.concatenate(
        [query_latent, jnp.transpose(queries[..., nope_width:], (2, 0, 1, 3))], axis=-1
    )
    score_scale = queries.shape[-1] ** (-0.5)
    own_slots = my_dev * cap_slots + jnp.arange(cap_slots, dtype=jnp.int32)
    slot_hit = (own_slots[:, None] == request_slot[None, :]).astype(jnp.int32)
    occupied = (jnp.sum(slot_hit, axis=1) > 0).astype(f32)
    ctx_rows = jnp.sum(slot_hit * context_len[None, :], axis=1)
    score_cache = score_scale * jnp.einsum(
        "hstc,sjc->hstj", query_full, latent_cache, preferred_element_type=f32
    )
    score_fresh = score_scale * jnp.einsum(
        "hstc,suc->hstu", query_full, new_latent, preferred_element_type=f32
    )
    mask_cache = (jnp.arange(ctx_len)[None, :] < ctx_rows[:, None])[None, :, None, :]
    mask_fresh = (jnp.arange(step_count)[None, :] <= jnp.arange(step_count)[:, None])[None, None]
    score_cache = jnp.where(mask_cache, score_cache, masked_score)
    score_fresh = jnp.where(mask_fresh, score_fresh, masked_score)
    top_held = jnp.maximum(
        jnp.max(score_cache, axis=-1, keepdims=True), jnp.max(score_fresh, axis=-1, keepdims=True)
    )
    exp_cache = jnp.exp(score_cache - top_held)
    exp_fresh = jnp.exp(score_fresh - top_held)
    sum_held = jnp.sum(exp_cache, -1, keepdims=True) + jnp.sum(exp_fresh, -1, keepdims=True)
    mix_held = jnp.einsum(
        "hstj,sjc->hstc", exp_cache.astype(bf16), latent_cache[..., :lat_width],
        preferred_element_type=f32,
    ) + jnp.einsum(
        "hstu,suc->hstc", exp_fresh.astype(bf16), new_latent[..., :lat_width],
        preferred_element_type=f32,
    )
    query_rows = query_full.reshape(row_count, kv_width)
    top_held = top_held.reshape(row_count, 1)
    sum_held = sum_held.reshape(row_count, 1)
    mix_held = mix_held.reshape(row_count, lat_width)
    query_slot = jnp.broadcast_to(
        own_slots[None, :, None], (head_count, cap_slots, step_count)
    ).reshape(row_count, 1)
    live = jnp.broadcast_to(occupied[:, None], (cap_slots, step_count)).reshape(1, -1, 1)

    x_rows = jnp.concatenate(x_pieces, axis=0)
    partial_raw = jnp.dot(x_rows, slab_weight, preferred_element_type=f32).astype(bf16)
    routed = jnp.dot(route, partial_raw, preferred_element_type=f32).astype(bf16)
    routed = routed.reshape(dev_count, dev_count * bucket_rows, kv_width)
    total = None
    for k in sorted(range(dev_count), reverse=True):
        got = (swap(routed[k], "dev", k) if k else routed[0]).astype(f32)
        total = got if total is None else total + got
    latent = total[:, :lat_width]
    spread = jnp.mean(latent * latent, axis=1, keepdims=True)
    normed = latent * lax.rsqrt(spread + 1e-06) * latent_gain[None, :]
    first = total[:, lat_width : lat_width + half]
    second = total[:, lat_width + half :]
    latent_rows = jnp.concatenate(
        [normed, first * cosine - second * sine, second * cosine + first * sine], axis=1
    ).astype(bf16)
    pieces = [latent_rows] + [swap(latent_rows, "side", k) for k in range(1, side_count)]
    group_rows = jnp.concatenate(pieces, axis=0)
    side_order = my_side ^ jnp.arange(side_count)
    row_slot = jnp.take(row_slot, side_order, axis=0).reshape(1, -1)

    score = score_scale * lax.dot_general(
        query_rows, group_rows, (((1,), (1,)), ((), ())), preferred_element_type=f32
    )
    score = jnp.where(row_slot == query_slot, score, masked_score)
    top = jnp.maximum(top_held, jnp.max(score, axis=1, keepdims=True))
    weight = jnp.exp(score - top)
    scale_held = jnp.exp(top_held - top)
    denominator = sum_held * scale_held + jnp.sum(weight, axis=1, keepdims=True)
    mix = mix_held * scale_held + jnp.dot(
        weight.astype(bf16), group_rows[:, :lat_width], preferred_element_type=f32
    )
    head_latent = (mix / denominator).astype(bf16).reshape(head_count, -1, lat_width)
    head_out = jnp.einsum(
        "hrc,hcn->hrn", head_latent, value_absorb, preferred_element_type=f32
    ) * live
    head_out = jnp.transpose(head_out.astype(bf16), (1, 0, 2)).reshape(
        cap_slots * step_count, -1
    )

    outs = [head_out] + [swap(head_out, "dev", k) for k in range(1, dev_count)]
    partial_out = jnp.dot(
        jnp.concatenate(outs, axis=0), out_weight, preferred_element_type=f32
    ).reshape(dev_count, cap_slots * step_count, -1)
    per_side = partial_out.shape[0] // side_count
    result = None
    for k in sorted(range(side_count), reverse=True):
        rows = [
            lax.dynamic_index_in_dim(
                partial_out, my_dev ^ ((my_side ^ k) * per_side + q), 0, keepdims=False
            )
            for q in range(per_side)
        ]
        rows = jnp.concatenate(rows, axis=0)
        got = swap(rows.astype(bf16), "side", k).astype(f32) if k else rows
        result = got if result is None else result + got
    return result.astype(bf16)


def solution(mesh):
    placed = (
        P(("rep", "dev", "side"), None),
        P(("dev", "side"), None),
        P(),
        P("rep"),
        P("rep"),
        P("rep"),
        P(("rep", "dev"), None, None),
        P(("rep", "dev"), None, None),
        P(("rep", "dev"), None, "side", None),
        P("side", None, None),
        P("side", None, None),
        P("side", "dev"),
    )
    return jax.shard_map(
        on_device, mesh=mesh, in_specs=placed, out_specs=P(("rep", "side"), "dev"), check_vma=False
    )
```

time: 182 us -> 104 us (0.57)
  waiting for transfers between devices: 84 us -> 26.6 us
  blocking collectives: 29.3 us -> 0 us
  starting transfers between devices: 4.31 us -> 20.2 us
  between operations: 14.4 us -> 0.56 us
  local copies, waits for them, and re-layouts: 10.9 us -> 17.9 us
    all_gather x1 -> x0, waiting for transfers between devices: 50.7 us -> none  [on_device(): lax.all_gather(latent_weight, ('dev', 'side'), axis=0, tiled=True)]
    ppermute x0 -> x17, waiting for transfers between devices: none -> 26.6 us  [swap(): return lax.ppermute(value, axis, [(i, i ^ step) for i in range(count)])]
    reduce_scatter x1 -> x0, waiting for transfers between devices: 22.3 us -> none  [on_device(): lax.psum_scatter(partial_out, 'side', scatter_dimension=0, tiled=True)]
    ppermute x0 -> x17, starting transfers between devices: none -> 20.2 us  [swap(): return lax.ppermute(value, axis, [(i, i ^ step) for i in range(count)])]
    all_gather x1 -> x0, blocking collectives: 15.5 us -> none  [on_device(): lax.all_gather(head_out, 'dev', axis=0, tiled=True)]
    unnamed x1 -> x0, blocking collectives: 13.8 us -> none
    all_to_all x1 -> x0, waiting for transfers between devices: 10.2 us -> none  [on_device(): lax.all_to_all(copies, ('dev', 'side'), split_axis=0, concat_axis=0, tile...]
    unnamed x41 -> x47, local copies, waits for them, and re-layouts: 6.59 us -> 1.76 us
  transfers between devices with their start and end apart: 3 -> 17, of which waited for: 3 -> 9; matrix products, arithmetic and copies ran while one was open for 14% -> 36% of each run, Pallas kernels for 0% -> 0%
where the time goes in v1:
time: 104 us; the launch traced here: 103 us
  waiting for transfers between devices  26.6 us (26%)
  matrix products  21.4 us (21%)
  starting transfers between devices  20.2 us (19%)
  local copies, waits for them, and re-layouts  17.9 us (17%)
  other arithmetic  16.2 us (16%)
    ppermute x17, waiting for transfers between devices, swap(): return lax.ppermute(value, axis, [(i, i ^ step) for i in range(count)])  26.6 us
    ppermute x17, starting transfers between devices, swap(): return lax.ppermute(value, axis, [(i, i ^ step) for i in range(count)])  20.2 us
    dot_general x1, matrix products, on_device(): jnp.dot(jnp.concatenate(outs, axis=0), out_weight, preferred_element_type...  7.79 us
    select_n x2, other arithmetic, pick(): out = jnp.where(index == k, pieces[k], out)  4.23 us
    dot_general x1, matrix products, on_device(): jnp.dot(route, partial_raw, preferred_element_type=f32).astype(bf16)  3.22 us
    dot_general x1, matrix products, on_device(): jnp.einsum('sthn,hnc->hstc', queries[..., :nope_width], key_absorb, prefe...  2.98 us
    dynamic_update_slice x2, local copies, waits for them, and re-layouts, on_device(): held = lax.dynamic_update_slice(held, piece[None], (my_side ^ k, 0, 0))  2.8 us
    mul x1, local copies, waits for them, and re-layouts, on_device(): jnp.swapaxes(by_step, 0, 1)[:, :, :, None, :] * same[None, :, None, :, None]  2.17 us
  transfers between devices with their start and end apart: 17, of which 9 were waited for; matrix products, arithmetic and copies ran while one was open for 36% of the time, Pallas kernels for 0%

profile of v1, /device:TPU:0, one launch (start us, length us, event | category | flops | bytes accessed | tf_op | source)
XLA Modules:
  0.0 102.9 jit_solution(14928297285588710756)
XLA Ops:
  0.0 3.0 %collective-permute-start.3 = (bf16[448,576]{1,0:T(8,128)(2,1)}, bf16[448,576]{1,0:T(8,128)(2,1)}, u32[]{:S(2)}, u32[]{:S(2)}) collective-permute-start(bf16[448,576]{1,0:T(8,128)(2,1)} %param.13), channel_id=1, source_target_pairs={{0,2},{1,3},{2,0},{3,1},{4,6},{5,7},{6,4},{7,5},{8,10},{9,11},{10,... | collective-permute-start | bytes 1548296 | tf_op jit(solution)/shard_map/ppermute | solution.py:11
  3.0 2.1 %select_select_fusion.2 = (bf16[64,1792]{1,0:T(8,128)(2,1)}, bf16[64,1792]{1,0:T(8,128)(2,1)}) fusion(pred[]{:T(512)S(6)} %eq.195, pred[]{:T(512)S(6)} %eq.194, pred[]{:T(512)S(6)} %eq.193, bf16[64,7168]{1,0:T(8,128)(2,1)} %param.12, pred[]{:T(512)S(6)} %eq.201, pred[]{:T(512)S(6)} %eq.200, pred[]{:T(512)S(6)} %eq.199), kind=kLoop, calls=%fused_computation.98 | loop fusion | flops 688128 | bytes 1376262 | tf_op jit(solution)/shard_map/jit(_where)/select_n | solution.py:17
  5.1 1.6 %collective-permute-start = (bf16[64,1792]{1,0:T(8,128)(2,1)}, bf16[64,1792]{1,0:T(8,128)(2,1)}, u32[]{:S(2)}, u32[]{:S(2)}) collective-permute-start(bf16[64,1792]{1,0:T(8,128)(2,1)} %get-tuple-element.13), channel_id=1, source_target_pairs={{0,4},{4,0},{8,12},{12,8},{1,5},{5,1},{9,13},{13,9},{2,6},{6,2},{1... | collective-permute-start | bytes 688136 | tf_op jit(solution)/shard_map/ppermute | solution.py:11
  6.7 2.5 %collective-permute-start.2 = (bf16[64,1792]{1,0:T(8,128)(2,1)}, bf16[64,1792]{1,0:T(8,128)(2,1)}, u32[]{:S(2)}, u32[]{:S(2)}) collective-permute-start(bf16[64,1792]{1,0:T(8,128)(2,1)} %get-tuple-element.14), channel_id=1, source_target_pairs={{0,12},{4,8},{8,4},{12,0},{1,13},{5,9},{9,5},{13,1},{2,14},{6,10},... | collective-permute-start | bytes 688136 | tf_op jit(solution)/shard_map/ppermute | solution.py:11
  9.2 2.1 %select_select_fusion.3 = (bf16[64,1792]{1,0:T(8,128)(2,1)}, bf16[64,1792]{1,0:T(8,128)(2,1)}) fusion(pred[]{:T(512)S(6)} %eq.192, pred[]{:T(512)S(6)} %eq.191, pred[]{:T(512)S(6)} %eq.190, bf16[64,7168]{1,0:T(8,128)(2,1)} %param.12, pred[]{:T(512)S(6)} %eq.198, pred[]{:T(512)S(6)} %eq.197, pred[]{:T(512)S(6)} %eq.196), kind=kLoop, calls=%fused_computation.99 | loop fusion | flops 688128 | bytes 1376262 | tf_op jit(solution)/shard_map/jit(_where)/select_n | solution.py:17
  13.1 0.7 fusion.116
  14.0 0.7 fusion.118
  15.8 1.1 %broadcast_multiply_fusion = bf16[4,4,32,4,64]{4,3,2,1,0:T(4,128)(2,1)} fusion(bf16[4,4]{1,0:T(4,128)(2,1)S(1)} %fusion.119, bf16[4,4,32,64]{3,2,1,0:T(8,128)(2,1)S(1)} %select_convert_fusion), kind=kLoop, calls=%fused_computation.89 | loop fusion | flops 131072 | bytes 327712 | tf_op jit(solution)/shard_map/mul | solution.py:113
  16.9 0.9 select_reduce_fusion
  17.8 3.0 %fusion.11 = bf16[32,8,2,512]{3,1,2,0:T(8,128)(2,1)S(1)} fusion(bf16[32,128,512]{2,1,0:T(8,128)(2,1)} %param.21, bf16[8,2,32,128]{3,2,1,0:T(8,128)(2,1)S(1)} %slice-done), kind=kOutput, calls=%fused_computation.17 | convolution fusion | flops 67371008 | bytes 4849664 | tf_op jit(solution)/shard_map/sthn,hnc->hstc/dot_general | solution.py:121
  21.6 1.8 %fusion.129 = (f32[32,8,2]{0,2,1:T(2,128)}, f32[32,8,2,2]{0,3,2,1:T(2,128)}) fusion(bf16[8,2,576]{2,1,0:T(2,128)(2,1)S(1)} %copy-done.12, bf16[32,8,2,576]{3,1,2,0:T(8,128)(2,1)S(1)} %pad_maximum_fusion, pred[2,2]{1,0:T(4,128)(4,1)S(1)} %copy-done.22), kind=kOutput, calls=%fused_computation.193 | convolution fusion | flops 1182208 | bytes 614404 | tf_op jit(solution)/shard_map/hstc,suc->hstu/dot_general | solution.py:135
  24.0 1.2 %convert_element_type.156 = f32[16]{0:T(128)} convert(s32[16]{0:T(128)} %param.16) | non-fusion elementwise | flops 16 | bytes 128 | tf_op jit(solution)/shard_map/convert_element_type | solution.py:81
  25.2 2.2 %mul.169 = bf16[512,256]{1,0:T(8,128)(2,1)} reshape(bf16[4,4,32,4,64]{4,3,2,1,0:T(4,128)(2,1)} %broadcast_multiply_fusion) | data formatting | bytes 524288 | tf_op jit(solution)/shard_map/mul | solution.py:113
  27.3 0.7 copy.99
  28.0 1.3 %gather_fusion = s32[4,4,32]{2,1,0:T(4,128)} fusion(s32[4,4,32]{2,1,0:T(4,128)S(1)} %bitcast.122, s32[1024]{0:T(1024)} %pad_clamp_fusion.1), kind=kCustom, calls=%fused_computation | custom fusion | bytes 4112 | tf_op jit(solution)/shard_map/jit(_take)/gather | solution.py:183
  29.3 0.8 max.39
  30.1 1.0 fusion.28
  31.3 1.6 %broadcast_in_dim.77 = bf16[4,448,576]{2,1,0:T(8,128)(2,1)} broadcast(bf16[]{:T(256)} %constant.142.clone.1), dimensions={} | broadcast | bytes 2064386 | tf_op jit(solution)/shard_map/broadcast_in_dim | solution.py:59
  32.9 0.9 bitcast_dynamic-update-slice_fusion.1
  33.8 1.9 %bitcast_dynamic-update-slice_fusion = bf16[4,448,576]{2,1,0:T(8,128)(2,1)} fusion(bf16[4,448,576]{2,1,0:T(8,128)(2,1)} %bitcast_dynamic-update-slice_fusion.1, s32[]{:T(128)S(6)} %select_n.246, bf16[448,576]{1,0:T(8,128)(2,1)} %collective-permute-done.3), kind=kLoop, calls=%fused_computation.60 | loop fusion | bytes 1146884 | tf_op jit(solution)/shard_map/dynamic_update_slice | solution.py:62
  35.7 1.4 %constant_dynamic-slice_fusion.1 = bf16[2,1,448,576]{3,2,1,0:T(8,128)(2,1)S(1)} fusion(bf16[2,2,448,576]{3,2,1,0:T(8,128)(2,1)} %bitcast.26, s32[]{:T(128)S(6)} %select_n.248), kind=kLoop, calls=%fused_computation.167 | loop fusion | bytes 2064388 | tf_op jit(solution)/shard_map/dynamic_slice | solution.py:65
  37.8 0.7 broadcast_select_fusion
  38.5 0.8 fusion.4
  40.0 1.1 %constant_dynamic-update-slice_fusion = bf16[2,2,448,576]{3,2,1,0:T(8,128)(2,1)} fusion(bf16[2,2,448,576]{3,2,1,0:T(8,128)(2,1)} %bitcast.26, bf16[2,1,448,576]{3,2,1,0:T(8,128)(2,1)S(1)} %collective-permute-done.4, s32[]{:T(128)S(6)} %select_n.249), kind=kLoop, calls=%fused_computation.166 | loop fusion | bytes 2179076 | tf_op jit(solution)/shard_map/dynamic_update_slice | solution.py:67
  41.1 3.2 %convolution_convert_fusion = bf16[512,576]{0,1:T(8,128)(2,1)S(1)} fusion(bf16[512,256]{1,0:T(8,128)(2,1)S(1)} %copy-done.5, bf16[1792,576]{1,0:T(8,128)(2,1)} %bitcast.27, bf16[64,1792]{1,0:T(8,128)(2,1)} %collective-permute-done.2, bf16[64,1792]{1,0:T(8,128)(2,1)} %collective-permute-done.1, bf16[64,1792]{1,0:T(8,128)(2,1)} %collective-permute-done, ...), kind=kOutput, calls=%fused_computation.15 | convolution fusion | flops 683589632 | bytes 3833856 | tf_op jit(solution)/shard_map/dot_general | solution.py:166
  44.4 0.8 fusion.127
  45.2 2.9 %collective-permute-start.5 = (bf16[128,576]{0,1:T(8,128)(2,1)}, bf16[128,576]{0,1:T(8,128)(2,1)}, u32[]{:S(2)}, u32[]{:S(2)}) collective-permute-start(bf16[128,576]{0,1:T(8,128)(2,1)} %get-tuple-element.15), channel_id=1, source_target_pairs={{0,12},{4,8},{8,4},{12,0},{1,13},{5,9},{9,5},{13,1},{2,14},{6,10},... | collective-permute-start | bytes 442376 | tf_op jit(solution)/shard_map/ppermute | solution.py:11
  48.4 1.1 %collective-permute-start.7 = (bf16[128,576]{0,1:T(8,128)(2,1)}, bf16[128,576]{0,1:T(8,128)(2,1)}, u32[]{:S(2)}, u32[]{:S(2)}) collective-permute-start(bf16[128,576]{0,1:T(8,128)(2,1)} %get-tuple-element.16), channel_id=1, source_target_pairs={{0,4},{4,0},{8,12},{12,8},{1,5},{5,1},{9,13},{13,9},{2,6},{6,2},{1... | collective-permute-start | bytes 442376 | tf_op jit(solution)/shard_map/ppermute | solution.py:11
  49.5 0.8 select_reduce_fusion.2
  52.4 0.8 copy.67
  53.2 0.7 reshape.340
  54.1 8.1 %collective-permute-done.6 = bf16[128,576]{0,1:T(8,128)(2,1)} collective-permute-done((bf16[128,576]{0,1:T(8,128)(2,1)}, bf16[128,576]{0,1:T(8,128)(2,1)}, u32[]{:S(2)}, u32[]{:S(2)}) %collective-permute-start.6) | collective-permute-done | bytes 147488 | tf_op jit(solution)/shard_map/ppermute | solution.py:11
  62.2 1.2 %convert_add_fusion = f32[128,576]{0,1:T(8,128)S(1)} fusion(bf16[128,576]{0,1:T(8,128)(2,1)} %collective-permute-done.7, bf16[128,576]{0,1:T(8,128)(2,1)} %collective-permute-done.6, bf16[128,576]{0,1:T(8,128)(2,1)} %collective-permute-done.5, bf16[512,576]{0,1:T(8,128)(2,1)} %copy-done.2), kind=kLoop, calls=%fused_computation.86 | loop fusion | flops 516096 | bytes 884736 | tf_op jit(solution)/shard_map/add | solution.py:171
  64.5 1.5 %collective-permute-start.9 = (bf16[128,576]{0,1:T(8,128)(2,1)S(1)}, bf16[128,576]{0,1:T(8,128)(2,1)S(1)}, u32[]{:S(2)}, u32[]{:S(2)}) collective-permute-start(bf16[128,576]{0,1:T(8,128)(2,1)S(1)} %pad_maximum_fusion.1), channel_id=1, source_target_pairs={{0,2},{1,3},{2,0},{3,1},{4,6},{5,7},{6,4},{7,5},{8,10},{9,11},{10,... | collective-permute-start | bytes 442376 | tf_op jit(solution)/shard_map/ppermute | solution.py:11
  66.1 3.8 %collective-permute-done.10 = bf16[128,576]{0,1:T(8,128)(2,1)S(1)} collective-permute-done((bf16[128,576]{0,1:T(8,128)(2,1)S(1)}, bf16[128,576]{0,1:T(8,128)(2,1)S(1)}, u32[]{:S(2)}, u32[]{:S(2)}) %collective-permute-start.10) | collective-permute-done | bytes 147488 | tf_op jit(solution)/shard_map/ppermute | solution.py:11
  70.0 2.5 %collective-permute-done.9 = bf16[128,576]{0,1:T(8,128)(2,1)S(1)} collective-permute-done((bf16[128,576]{0,1:T(8,128)(2,1)S(1)}, bf16[128,576]{0,1:T(8,128)(2,1)S(1)}, u32[]{:S(2)}, u32[]{:S(2)}) %collective-permute-start.9) | collective-permute-done | bytes 147488 | tf_op jit(solution)/shard_map/ppermute | solution.py:11
  73.3 0.7 fusion.10
  74.1 1.5 %copy-done.1 = bf16[32,512,128]{2,1,0:T(8,128)(2,1)S(1)} copy-done((bf16[32,512,128]{2,1,0:T(8,128)(2,1)S(1)}, bf16[32,512,128]{2,1,0:T(8,128)(2,1)}, u32[]{:S(2)}) %copy-start.1) | copy-done | bytes 4194328
  75.5 0.7 fusion.24
  76.3 3.0 %collective-permute-start.12 = (bf16[16,4096]{1,0:T(8,128)(2,1)S(1)}, bf16[16,4096]{1,0:T(8,128)(2,1)S(1)}, u32[]{:S(2)}, u32[]{:S(2)}) collective-permute-start(bf16[16,4096]{1,0:T(8,128)(2,1)S(1)} %bitcast.115), channel_id=1, source_target_pairs={{0,8},{4,12},{8,0},{12,4},{1,9},{5,13},{9,1},{13,5},{2,10},{6,14},... | collective-permute-start | bytes 393224 | tf_op jit(solution)/shard_map/ppermute | solution.py:11
  79.3 1.4 %collective-permute-start.13 = (bf16[16,4096]{1,0:T(8,128)(2,1)S(1)}, bf16[16,4096]{1,0:T(8,128)(2,1)S(1)}, u32[]{:S(2)}, u32[]{:S(2)}) collective-permute-start(bf16[16,4096]{1,0:T(8,128)(2,1)S(1)} %bitcast.116), channel_id=1, source_target_pairs={{0,12},{4,8},{8,4},{12,0},{1,13},{5,9},{9,5},{13,1},{2,14},{6,10},... | collective-permute-start | bytes 393224 | tf_op jit(solution)/shard_map/ppermute | solution.py:11
  80.7 3.5 %collective-permute-done.11 = bf16[16,4096]{1,0:T(8,128)(2,1)S(1)} collective-permute-done((bf16[16,4096]{1,0:T(8,128)(2,1)S(1)}, bf16[16,4096]{1,0:T(8,128)(2,1)S(1)}, u32[]{:S(2)}, u32[]{:S(2)}) %collective-permute-start.11) | collective-permute-done | bytes 131104 | tf_op jit(solution)/shard_map/ppermute | solution.py:11
  84.1 5.1 %collective-permute-done.12 = bf16[16,4096]{1,0:T(8,128)(2,1)S(1)} collective-permute-done((bf16[16,4096]{1,0:T(8,128)(2,1)S(1)}, bf16[16,4096]{1,0:T(8,128)(2,1)S(1)}, u32[]{:S(2)}, u32[]{:S(2)}) %collective-permute-start.12) | collective-permute-done | bytes 131104 | tf_op jit(solution)/shard_map/ppermute | solution.py:11
  89.3 7.8 %fusion.74 = f32[64,1792]{1,0:T(8,128)S(1)} fusion(bf16[4096,1792]{1,0:T(8,128)(2,1)} %param.23, bf16[16,4096]{1,0:T(8,128)(2,1)S(1)} %collective-permute-done.13, bf16[16,4096]{1,0:T(8,128)(2,1)S(1)} %collective-permute-done.12, bf16[16,4096]{1,0:T(8,128)(2,1)S(1)} %collective-permute-done.11, bf16[16,4096]{1,0:T(8,128)(2,1)S(1)} %bitcast.117), kind=kOutput, calls=%fused_computation.73 | convolution fusion | flops 941621248 | bytes 15663104 | tf_op jit(solution)/shard_map/dot_general | solution.py:205
  97.2 1.3 %collective-permute-start.15 = (bf16[16,1792]{1,0:T(8,128)(2,1)S(1)}, bf16[16,1792]{1,0:T(8,128)(2,1)S(1)}, u32[]{:S(2)}, u32[]{:S(2)}) collective-permute-start(bf16[16,1792]{1,0:T(8,128)(2,1)S(1)} %get-tuple-element.20), channel_id=1, source_target_pairs={{0,2},{1,3},{2,0},{3,1},{4,6},{5,7},{6,4},{7,5},{8,10},{9,11},{10,... | collective-permute-start | bytes 172040 | tf_op jit(solution)/shard_map/ppermute | solution.py:11
  99.0 2.4 %collective-permute-done.14 = bf16[16,1792]{1,0:T(8,128)(2,1)S(1)} collective-permute-done((bf16[16,1792]{1,0:T(8,128)(2,1)S(1)}, bf16[16,1792]{1,0:T(8,128)(2,1)S(1)}, u32[]{:S(2)}, u32[]{:S(2)}) %collective-permute-start.14) | collective-permute-done | bytes 57376 | tf_op jit(solution)/shard_map/ppermute | solution.py:11
  101.4 0.8 collective-permute-done.15
  102.2 0.7 fusion.88
  (128 shorter events, 11.2 us)
Async XLA Ops:
  0.0 11.4 %copy-start.14 = (s32[1024]{0:T(1024)S(1)}, s32[1024]{0:T(1024)}, u32[]{:S(2)}) copy-start(s32[1024]{0:T(1024)} %param.15) | copy-start | bytes 12292
  0.0 11.5 %copy-start.19 = (s32[16]{0:T(128)S(1)}, s32[16]{0:T(128)}, u32[]{:S(2)}) copy-start(s32[16]{0:T(128)} %param.17) | copy-start | bytes 196
  0.0 13.9 %slice-start.1 = ((bf16[8,2,32,192]{3,2,1,0:T(8,128)(2,1)}), bf16[8,2,32,64]{3,2,1,0:T(8,128)(2,1)S(1)}, s32[]{:S(2)}) async-start(bf16[8,2,32,192]{3,2,1,0:T(8,128)(2,1)} %param.20), calls=%async_computation.1 | async-start | bytes 262144 | tf_op jit(solution)/shard_map/slice | solution.py:125
  0.0 14.0 %copy-start.20 = (s32[16]{0:T(128)S(1)}, s32[16]{0:T(128)}, u32[]{:S(2)}) copy-start(s32[16]{0:T(128)} %param.16) | copy-start | bytes 196
  0.0 33.8 %collective-permute-start.3 = (bf16[448,576]{1,0:T(8,128)(2,1)}, bf16[448,576]{1,0:T(8,128)(2,1)}, u32[]{:S(2)}, u32[]{:S(2)}) collective-permute-start(bf16[448,576]{1,0:T(8,128)(2,1)} %param.13), channel_id=1, source_target_pairs={{0,2},{1,3},{2,0},{3,1},{4,6},{5,7},{6,4},{7,5},{8,10},{9,11},{10,... | collective-permute-start | bytes 1548296 | tf_op jit(solution)/shard_map/ppermute | solution.py:11
  5.1 12.7 %slice-start = ((bf16[8,2,32,192]{3,2,1,0:T(8,128)(2,1)}), bf16[8,2,32,128]{3,2,1,0:T(8,128)(2,1)S(1)}, s32[]{:S(2)}) async-start(bf16[8,2,32,192]{3,2,1,0:T(8,128)(2,1)} %param.20), calls=%async_computation | async-start | bytes 262144 | tf_op jit(solution)/shard_map/slice | solution.py:122
  5.1 35.9 %collective-permute-start = (bf16[64,1792]{1,0:T(8,128)(2,1)}, bf16[64,1792]{1,0:T(8,128)(2,1)}, u32[]{:S(2)}, u32[]{:S(2)}) collective-permute-start(bf16[64,1792]{1,0:T(8,128)(2,1)} %get-tuple-element.13), channel_id=1, source_target_pairs={{0,4},{4,0},{8,12},{12,8},{1,5},{5,1},{9,13},{13,9},{2,6},{6,2},{1... | collective-permute-start | bytes 688136 | tf_op jit(solution)/shard_map/ppermute | solution.py:11
  6.7 34.4 %collective-permute-start.2 = (bf16[64,1792]{1,0:T(8,128)(2,1)}, bf16[64,1792]{1,0:T(8,128)(2,1)}, u32[]{:S(2)}, u32[]{:S(2)}) collective-permute-start(bf16[64,1792]{1,0:T(8,128)(2,1)} %get-tuple-element.14), channel_id=1, source_target_pairs={{0,12},{4,8},{8,4},{12,0},{1,13},{5,9},{9,5},{13,1},{2,14},{6,10},... | collective-permute-start | bytes 688136 | tf_op jit(solution)/shard_map/ppermute | solution.py:11
  11.3 29.8 %collective-permute-start.1 = (bf16[64,1792]{1,0:T(8,128)(2,1)}, bf16[64,1792]{1,0:T(8,128)(2,1)}, u32[]{:S(2)}, u32[]{:S(2)}) collective-permute-start(bf16[64,1792]{1,0:T(8,128)(2,1)} %get-tuple-element.12), channel_id=1, source_target_pairs={{0,8},{4,12},{8,0},{12,4},{1,9},{5,13},{9,1},{13,5},{2,10},{6,14},... | collective-permute-start | bytes 688136 | tf_op jit(solution)/shard_map/ppermute | solution.py:11
  11.5 0.9 copy-start.8
  13.9 0.9 copy-start.16
  14.9 0.7 copy-start.4
  17.8 3.1 %copy-start = (bf16[8,256,576]{1,2,0:T(8,128)(2,1)S(1)}, bf16[8,256,576]{1,2,0:T(8,128)(2,1)}, u32[]{:S(2)}) copy-start(bf16[8,256,576]{1,2,0:T(8,128)(2,1)} %param.18) | copy-start | bytes 7077892
  20.8 0.7 copy-start.12
  20.8 0.8 copy-start.22
  29.3 3.6 %copy-start.3 = (bf16[448,576]{1,0:T(8,128)(2,1)S(1)}, bf16[448,576]{1,0:T(8,128)(2,1)}, u32[]{:S(2)}) copy-start(bf16[448,576]{1,0:T(8,128)(2,1)} %param.13) | copy-start | bytes 1548292
  32.9 4.3 %copy-start.7 = (f32[32,8,2,2]{0,3,2,1:T(2,128)S(1)}, f32[32,8,2,2]{0,3,2,1:T(2,128)}, u32[]{:S(2)}) copy-start(f32[32,8,2,2]{0,3,2,1:T(2,128)} %get-tuple-element.26) | copy-start | bytes 12292
  32.9 4.9 %copy-start.11 = (s32[4,4,32]{2,1,0:T(4,128)S(1)}, s32[4,4,32]{2,1,0:T(4,128)}, u32[]{:S(2)}) copy-start(s32[4,4,32]{2,1,0:T(4,128)} %gather_fusion) | copy-start | bytes 6148
  32.9 4.9 %copy-start.18 = (pred[4]{0:T(512)(128)(4,1)S(1)}, pred[4]{0:T(512)(128)(4,1)}, u32[]{:S(2)}) copy-start(pred[4]{0:T(512)(128)(4,1)} %get-tuple-element.30) | copy-start | bytes 16
  37.1 2.2 %copy-start.13 = (bf16[8,2,576]{2,1,0:T(2,128)(2,1)S(1)}, bf16[8,2,576]{2,1,0:T(2,128)(2,1)}, u32[]{:S(2)}) copy-start(bf16[8,2,576]{2,1,0:T(2,128)(2,1)} %param.19) | copy-start | bytes 55300
  37.1 2.9 %collective-permute-start.4 = (bf16[2,1,448,576]{3,2,1,0:T(8,128)(2,1)S(1)}, bf16[2,1,448,576]{3,2,1,0:T(8,128)(2,1)S(1)}, u32[]{:S(2)}, u32[]{:S(2)}) collective-permute-start(bf16[2,1,448,576]{3,2,1,0:T(8,128)(2,1)S(1)} %constant_dynamic-slice_fusion.1), channel_id=1, source_target_pairs={{0,1},{1,0},{2,3},{3,2},{4,5},{5,4},{6,7},{7,6},{8,9},{9,8},{10,11... | collective-permute-start | bytes 3096584 | tf_op jit(solution)/shard_map/ppermute | solution.py:11
  39.3 1.8 %copy-start.5 = (bf16[512,256]{1,0:T(8,128)(2,1)S(1)}, bf16[512,256]{1,0:T(8,128)(2,1)}, u32[]{:S(2)}) copy-start(bf16[512,256]{1,0:T(8,128)(2,1)} %mul.169) | copy-start | bytes 786436
  39.3 1.8 %copy-start.6 = (bf16[64,1792]{1,0:T(8,128)(2,1)S(1)}, bf16[64,1792]{1,0:T(8,128)(2,1)}, u32[]{:S(2)}) copy-start(bf16[64,1792]{1,0:T(8,128)(2,1)} %get-tuple-element.11) | copy-start | bytes 688132
  44.3 6.9 %copy-start.2 = (bf16[512,576]{0,1:T(8,128)(2,1)}, bf16[512,576]{0,1:T(8,128)(2,1)S(1)}, u32[]{:S(2)}) copy-start(bf16[512,576]{0,1:T(8,128)(2,1)S(1)} %convolution_convert_fusion) | copy-start | bytes 1769476
  44.3 6.8 %copy-start.9 = (s32[4,4,32]{2,1,0:T(4,128)S(1)}, s32[4,4,32]{2,1,0:T(4,128)}, u32[]{:S(2)}) copy-start(s32[4,4,32]{2,1,0:T(4,128)} %broadcast_select_fusion) | copy-start | bytes 6148
  44.4 6.8 %copy-start.17 = (s32[8]{0:T(128)S(1)}, s32[8]{0:T(128)}, u32[]{:S(2)}) copy-start(s32[8]{0:T(128)} %copy-done.16) | copy-start | bytes 100
  44.4 7.7 %copy-start.10 = (f32[32,8,2]{0,2,1:T(2,128)S(1)}, f32[32,8,2]{0,2,1:T(2,128)}, u32[]{:S(2)}) copy-start(f32[32,8,2]{0,2,1:T(2,128)} %fusion.108) | copy-start | bytes 6148
  45.2 8.9 %collective-permute-start.5 = (bf16[128,576]{0,1:T(8,128)(2,1)}, bf16[128,576]{0,1:T(8,128)(2,1)}, u32[]{:S(2)}, u32[]{:S(2)}) collective-permute-start(bf16[128,576]{0,1:T(8,128)(2,1)} %get-tuple-element.15), channel_id=1, source_target_pairs={{0,12},{4,8},{8,4},{12,0},{1,13},{5,9},{9,5},{13,1},{2,14},{6,10},... | collective-permute-start | bytes 442376 | tf_op jit(solution)/shard_map/ppermute | solution.py:11
  48.1 14.1 %collective-permute-start.6 = (bf16[128,576]{0,1:T(8,128)(2,1)}, bf16[128,576]{0,1:T(8,128)(2,1)}, u32[]{:S(2)}, u32[]{:S(2)}) collective-permute-start(bf16[128,576]{0,1:T(8,128)(2,1)} %get-tuple-element.17), channel_id=1, source_target_pairs={{0,8},{4,12},{8,0},{12,4},{1,9},{5,13},{9,1},{13,5},{2,10},{6,14},... | collective-permute-start | bytes 442376 | tf_op jit(solution)/shard_map/ppermute | solution.py:11
  48.4 13.8 %collective-permute-start.7 = (bf16[128,576]{0,1:T(8,128)(2,1)}, bf16[128,576]{0,1:T(8,128)(2,1)}, u32[]{:S(2)}, u32[]{:S(2)}) collective-permute-start(bf16[128,576]{0,1:T(8,128)(2,1)} %get-tuple-element.16), channel_id=1, source_target_pairs={{0,4},{4,0},{8,12},{12,8},{1,5},{5,1},{9,13},{13,9},{2,6},{6,2},{1... | collective-permute-start | bytes 442376 | tf_op jit(solution)/shard_map/ppermute | solution.py:11
  52.4 11.1 %copy-start.15 = (f32[512]{0:T(512)S(1)}, f32[512]{0:T(512)}, u32[]{:S(2)}) copy-start(f32[512]{0:T(512)} %param.14) | copy-start | bytes 6148
  53.2 12.8 %copy-start.21 = (s32[8]{0:T(128)S(1)}, s32[8]{0:T(128)}, u32[]{:S(2)}) copy-start(s32[8]{0:T(128)} %get-tuple-element.7) | copy-start | bytes 100
  63.8 6.2 %collective-permute-start.10 = (bf16[128,576]{0,1:T(8,128)(2,1)S(1)}, bf16[128,576]{0,1:T(8,128)(2,1)S(1)}, u32[]{:S(2)}, u32[]{:S(2)}) collective-permute-start(bf16[128,576]{0,1:T(8,128)(2,1)S(1)} %pad_maximum_fusion.1), channel_id=1, source_target_pairs={{0,3},{1,2},{2,1},{3,0},{4,7},{5,6},{6,5},{7,4},{8,11},{9,10},{10,... | collective-permute-start | bytes 442376 | tf_op jit(solution)/shard_map/ppermute | solution.py:11
  63.9 6.1 %collective-permute-start.8 = (bf16[128,576]{0,1:T(8,128)(2,1)S(1)}, bf16[128,576]{0,1:T(8,128)(2,1)S(1)}, u32[]{:S(2)}, u32[]{:S(2)}) collective-permute-start(bf16[128,576]{0,1:T(8,128)(2,1)S(1)} %pad_maximum_fusion.1), channel_id=1, source_target_pairs={{0,1},{1,0},{2,3},{3,2},{4,5},{5,4},{6,7},{7,6},{8,9},{9,8},{10,11... | collective-permute-start | bytes 442376 | tf_op jit(solution)/shard_map/ppermute | solution.py:11
  64.5 8.0 %collective-permute-start.9 = (bf16[128,576]{0,1:T(8,128)(2,1)S(1)}, bf16[128,576]{0,1:T(8,128)(2,1)S(1)}, u32[]{:S(2)}, u32[]{:S(2)}) collective-permute-start(bf16[128,576]{0,1:T(8,128)(2,1)S(1)} %pad_maximum_fusion.1), channel_id=1, source_target_pairs={{0,2},{1,3},{2,0},{3,1},{4,6},{5,7},{6,4},{7,5},{8,10},{9,11},{10,... | collective-permute-start | bytes 442376 | tf_op jit(solution)/shard_map/ppermute | solution.py:11
  73.3 2.2 %copy-start.1 = (bf16[32,512,128]{2,1,0:T(8,128)(2,1)S(1)}, bf16[32,512,128]{2,1,0:T(8,128)(2,1)}, u32[]{:S(2)}) copy-start(bf16[32,512,128]{2,1,0:T(8,128)(2,1)} %param.22) | copy-start | bytes 12582916
  76.2 7.9 %collective-permute-start.11 = (bf16[16,4096]{1,0:T(8,128)(2,1)S(1)}, bf16[16,4096]{1,0:T(8,128)(2,1)S(1)}, u32[]{:S(2)}, u32[]{:S(2)}) collective-permute-start(bf16[16,4096]{1,0:T(8,128)(2,1)S(1)} %bitcast.114), channel_id=1, source_target_pairs={{0,4},{4,0},{8,12},{12,8},{1,5},{5,1},{9,13},{13,9},{2,6},{6,2},{1... | collective-permute-start | bytes 393224 | tf_op jit(solution)/shard_map/ppermute | solution.py:11
  76.3 13.0 %collective-permute-start.12 = (bf16[16,4096]{1,0:T(8,128)(2,1)S(1)}, bf16[16,4096]{1,0:T(8,128)(2,1)S(1)}, u32[]{:S(2)}, u32[]{:S(2)}) collective-permute-start(bf16[16,4096]{1,0:T(8,128)(2,1)S(1)} %bitcast.115), channel_id=1, source_target_pairs={{0,8},{4,12},{8,0},{12,4},{1,9},{5,13},{9,1},{13,5},{2,10},{6,14},... | collective-permute-start | bytes 393224 | tf_op jit(solution)/shard_map/ppermute | solution.py:11
  79.3 10.0 %collective-permute-start.13 = (bf16[16,4096]{1,0:T(8,128)(2,1)S(1)}, bf16[16,4096]{1,0:T(8,128)(2,1)S(1)}, u32[]{:S(2)}, u32[]{:S(2)}) collective-permute-start(bf16[16,4096]{1,0:T(8,128)(2,1)S(1)} %bitcast.116), channel_id=1, source_target_pairs={{0,12},{4,8},{8,4},{12,0},{1,13},{5,9},{9,5},{13,1},{2,14},{6,10},... | collective-permute-start | bytes 393224 | tf_op jit(solution)/shard_map/ppermute | solution.py:11
  97.1 4.3 %collective-permute-start.14 = (bf16[16,1792]{1,0:T(8,128)(2,1)S(1)}, bf16[16,1792]{1,0:T(8,128)(2,1)S(1)}, u32[]{:S(2)}, u32[]{:S(2)}) collective-permute-start(bf16[16,1792]{1,0:T(8,128)(2,1)S(1)} %get-tuple-element.18), channel_id=1, source_target_pairs={{0,3},{1,2},{2,1},{3,0},{4,7},{5,6},{6,5},{7,4},{8,11},{9,10},{10,... | collective-permute-start | bytes 172040 | tf_op jit(solution)/shard_map/ppermute | solution.py:11
  97.2 5.0 %collective-permute-start.15 = (bf16[16,1792]{1,0:T(8,128)(2,1)S(1)}, bf16[16,1792]{1,0:T(8,128)(2,1)S(1)}, u32[]{:S(2)}, u32[]{:S(2)}) collective-permute-start(bf16[16,1792]{1,0:T(8,128)(2,1)S(1)} %get-tuple-element.20), channel_id=1, source_target_pairs={{0,2},{1,3},{2,0},{3,1},{4,6},{5,7},{6,4},{7,5},{8,10},{9,11},{10,... | collective-permute-start | bytes 172040 | tf_op jit(solution)/shard_map/ppermute | solution.py:11
  98.5 3.7 %collective-permute-start.16 = (bf16[16,1792]{1,0:T(8,128)(2,1)S(1)}, bf16[16,1792]{1,0:T(8,128)(2,1)S(1)}, u32[]{:S(2)}, u32[]{:S(2)}) collective-permute-start(bf16[16,1792]{1,0:T(8,128)(2,1)S(1)} %get-tuple-element.19), channel_id=1, source_target_pairs={{0,1},{1,0},{2,3},{3,2},{4,5},{5,4},{6,7},{7,6},{8,9},{9,8},{10,11... | collective-permute-start | bytes 172040 | tf_op jit(solution)/shard_map/ppermute | solution.py:11

commit v2 on v1

v2 whole, which is shorter than its diff:
```python
import functools

import jax
import jax.numpy as jnp
from jax import lax
from jax.experimental import pallas as pl
from jax.experimental.pallas import tpu as pltpu
from jax.sharding import PartitionSpec as P

masked_score = -1e30
bf16, f32 = jnp.bfloat16, jnp.float32
in_vmem = pl.BlockSpec(memory_space=pltpu.VMEM)
in_smem = pl.BlockSpec(memory_space=pltpu.SMEM)
anywhere = pl.BlockSpec(memory_space=pl.ANY)
mib = 1024 * 1024


def swap(value, axis, step):
    count = lax.axis_size(axis)
    return lax.ppermute(value, axis, [(i, i ^ step) for i in range(count)])


def pick(pieces, index):
    out = pieces[0]
    for k in range(1, len(pieces)):
        out = jnp.where(index == k, pieces[k], out)
    return out


def split_kernel(slab, here_ref, prompts_ref, *refs):
    out_refs, sems = refs[:-1], refs[-1]
    copies = []
    for n, out_ref in enumerate(out_refs):
        first = pl.multiple_of((here_ref[0] ^ (n + 1)) * slab, 128)
        copies.append(
            pltpu.make_async_copy(prompts_ref.at[:, pl.ds(first, slab)], out_ref, sems.at[n])
        )
    for copy in copies:
        copy.start()
    for copy in copies:
        copy.wait()


def split_columns(prompts, here, count):
    rows, width = prompts.shape
    slab = width // count
    if slab % 128:
        columns = [prompts[:, k * slab : (k + 1) * slab] for k in range(count)]
        return [pick(columns, here[0] ^ k) for k in range(1, count)]
    return pl.pallas_call(
        functools.partial(split_kernel, slab),
        out_shape=[jax.ShapeDtypeStruct((rows, slab), prompts.dtype)] * (count - 1),
        in_specs=[in_smem, anywhere],
        out_specs=[anywhere] * (count - 1),
        scratch_shapes=[pltpu.SemaphoreType.DMA((count - 1,))],
        name="split_columns",
    )(here, prompts)


def project_kernel(dev_count, side_count, here_ref, target_ref, *refs):
    x_refs = refs[:dev_count]
    weight_refs = refs[dev_count : dev_count + side_count]
    out_refs = refs[dev_count + side_count : -2]
    slab_weight, rows = refs[-2:]
    shard = weight_refs[0].shape[0]
    tok_rows = x_refs[0].shape[0]
    if side_count > 1:
        for k in range(side_count):
            first = pl.multiple_of((here_ref[1] ^ k) * shard, 16)
            slab_weight[pl.ds(first, shard), :] = weight_refs[k][...]
    for k in range(dev_count):
        rows[k * tok_rows : (k + 1) * tok_rows, :] = jnp.dot(
            x_refs[k][...], slab_weight[...] if side_count > 1 else weight_refs[0][...],
            preferred_element_type=f32,
        ).astype(bf16)
    group_rows = out_refs[0].shape[0]
    target = target_ref[...]
    for j in range(dev_count):
        ids = lax.broadcasted_iota(jnp.int32, (group_rows, target.shape[1]), 0) + j * group_rows
        route = jnp.where(ids == target, 1.0, 0.0).astype(bf16)
        out_refs[j][...] = jnp.dot(
            route, rows[...], preferred_element_type=f32
        ).astype(out_refs[j].dtype)


def project(x_pieces, weights, here, target, group_rows):
    dev_count, width = len(x_pieces), weights[0].shape[1]
    tok_rows, slab = x_pieces[0].shape
    return pl.pallas_call(
        functools.partial(project_kernel, dev_count, len(weights)),
        out_shape=[
            jax.ShapeDtypeStruct((group_rows, width), f32 if j == 0 else bf16)
            for j in range(dev_count)
        ],
        in_specs=[in_smem] + [in_vmem] * (1 + dev_count + len(weights)),
        out_specs=[in_vmem] * dev_count,
        scratch_shapes=[
            pltpu.VMEM((slab, width), bf16),
            pltpu.VMEM((dev_count * tok_rows, width), bf16),
        ],
        compiler_params=pltpu.CompilerParams(vmem_limit_bytes=16 * mib),
        name="project",
    )(here, target, *x_pieces, *weights)


def finish_kernel(gain_ref, cos_ref, sin_ref, *refs):
    parts, out_ref = refs[:-1], refs[-1]
    lat_width = gain_ref.shape[1]
    half = cos_ref.shape[1]
    total = parts[0][...].astype(f32)
    for part in parts[1:]:
        total = total + part[...].astype(f32)
    latent = total[:, :lat_width]
    spread = jnp.mean(latent * latent, axis=1, keepdims=True)
    out_ref[:, :lat_width] = (latent * lax.rsqrt(spread + 1e-06) * gain_ref[...]).astype(bf16)
    first = total[:, lat_width : lat_width + half]
    second = total[:, lat_width + half :]
    cosine, sine = cos_ref[...], sin_ref[...]
    turned = jnp.concatenate(
        [first * cosine - second * sine, second * cosine + first * sine], axis=1
    )
    out_ref[:, lat_width:] = turned.astype(bf16)


def finish(parts, gain, cosine, sine):
    return pl.pallas_call(
        finish_kernel,
        out_shape=jax.ShapeDtypeStruct(parts[0].shape, bf16),
        in_specs=[in_vmem] * (3 + len(parts)),
        out_specs=in_vmem,
        compiler_params=pltpu.CompilerParams(vmem_limit_bytes=8 * mib),
        name="finish_rows",
    )(gain, cosine, sine, *parts)


def attend_kernel(
    scale, cap_slots, step_count, base_ref, query_ref, fresh_ref, slot_ref, top_ref, sum_ref,
    mix_ref, live_ref, value_ref, *refs
):
    pieces, out_ref = refs[:-1], refs[-1]
    lat_width = mix_ref.shape[1]
    per_head = cap_slots * step_count
    heads = value_ref.shape[0]
    chunk_heads = min(8, heads)
    chunk = chunk_heads * per_head
    piece_rows = pieces[0].shape[0]
    contract = (((1,), (1,)), ((), ()))
    row = lax.broadcasted_iota(jnp.int32, (chunk, 1), 0)
    row_slot = (row // step_count) % cap_slots
    row_step = row % step_count
    key = lax.broadcasted_iota(jnp.int32, (1, per_head), 1)
    see_fresh = (key // step_count == row_slot) & (key % step_count <= row_step)
    for c in range(heads // chunk_heads):
        here = slice(c * chunk, (c + 1) * chunk)
        query = query_ref[here, :]
        fresh = lax.dot_general(query, fresh_ref[...], contract, preferred_element_type=f32)
        fresh = jnp.where(see_fresh, fresh * scale, masked_score)
        top = jnp.maximum(top_ref[here, :], jnp.max(fresh, axis=1, keepdims=True))
        scores = []
        for n, piece in enumerate(pieces):
            score = lax.dot_general(query, piece[...], contract, preferred_element_type=f32)
            slots = slot_ref[:, n * piece_rows : (n + 1) * piece_rows] - base_ref[0] * cap_slots
            score = jnp.where(slots == row_slot, score * scale, masked_score)
            top = jnp.maximum(top, jnp.max(score, axis=1, keepdims=True))
            scores.append(score)
        held = jnp.exp(top_ref[here, :] - top)
        weight = jnp.exp(fresh - top)
        total = sum_ref[here, :] * held + jnp.sum(weight, axis=1, keepdims=True)
        mix = mix_ref[here, :] * held + jnp.dot(
            weight.astype(bf16), fresh_ref[:, :lat_width], preferred_element_type=f32
        )
        for score, piece in zip(scores, pieces):
            weight = jnp.exp(score - top)
            total = total + jnp.sum(weight, axis=1, keepdims=True)
            mix = mix + jnp.dot(
                weight.astype(bf16), piece[:, :lat_width], preferred_element_type=f32
            )
        latent = (mix / total).astype(bf16)
        for h in range(chunk_heads):
            head = c * chunk_heads + h
            value = jnp.dot(
                latent[h * per_head : (h + 1) * per_head, :], value_ref[head],
                preferred_element_type=f32,
            )
            width = value.shape[1]
            out_ref[:, head * width : (head + 1) * width] = (value * live_ref[...]).astype(bf16)


def attend(scale, here, query, fresh, row_slot, top, total, mix, live, value, pieces, cap_slots):
    heads, _, width = value.shape
    step_count = fresh.shape[0] // cap_slots
    return pl.pallas_call(
        functools.partial(attend_kernel, scale, cap_slots, step_count),
        out_shape=jax.ShapeDtypeStruct((cap_slots * step_count, heads * width), bf16),
        in_specs=[in_smem] + [in_vmem] * (8 + len(pieces)),
        out_specs=in_vmem,
        compiler_params=pltpu.CompilerParams(vmem_limit_bytes=24 * mib),
        name="attend",
    )(here, query, fresh, row_slot, top, total, mix, live, value, *pieces)


def output_kernel(dev_count, side_count, here_ref, *refs):
    head_refs = refs[:dev_count]
    weight_ref = refs[dev_count]
    out_refs = refs[dev_count + 1 : -1]
    held = refs[-1]
    rows = head_refs[0].shape[0]
    per_side = dev_count // side_count
    for j in range(dev_count):
        group = here_ref[0] ^ j
        place = ((group // per_side) ^ here_ref[1]) * per_side + group % per_side
        held[pl.ds(pl.multiple_of(place * rows, 16), rows), :] = head_refs[j][...]
    columns = weight_ref.shape[1]
    tile = 256 if columns % 256 == 0 else columns
    side_rows = rows * per_side
    for n in range(columns // tile):
        here = slice(n * tile, (n + 1) * tile)
        product = jnp.dot(held[...], weight_ref[:, here], preferred_element_type=f32)
        for k in range(side_count):
            out_refs[k][:, here] = product[k * side_rows : (k + 1) * side_rows, :].astype(
                out_refs[k].dtype
            )


def output_product(head_pieces, weight, here, side_count):
    dev_count = len(head_pieces)
    rows, depth = head_pieces[0].shape
    columns = weight.shape[1]
    side_rows = rows * dev_count // side_count
    return pl.pallas_call(
        functools.partial(output_kernel, dev_count, side_count),
        out_shape=[
            jax.ShapeDtypeStruct((side_rows, columns), f32 if k == 0 else bf16)
            for k in range(side_count)
        ],
        in_specs=[in_smem] + [in_vmem] * (dev_count + 1),
        out_specs=[in_vmem] * side_count,
        scratch_shapes=[pltpu.VMEM((dev_count * rows, depth), bf16)],
        compiler_params=pltpu.CompilerParams(vmem_limit_bytes=24 * mib),
        name="output_product",
    )(here, *head_pieces, weight)


def on_device(
    prompts,
    latent_weight,
    latent_gain,
    row_request,
    context_len,
    request_slot,
    latent_cache,
    new_latent,
    queries,
    key_absorb,
    value_absorb,
    out_weight,
):
    dev_count = lax.axis_size("dev")
    side_count = lax.axis_size("side")
    block_count = dev_count * side_count
    tok_rows, model_width = prompts.shape
    shard_rows, kv_width = latent_weight.shape
    lat_width = latent_gain.shape[0]
    head_count, nope_width, _ = key_absorb.shape
    rope_width = kv_width - lat_width
    req_count = request_slot.shape[0]
    cap_slots, ctx_len, _ = latent_cache.shape
    step_count = new_latent.shape[1]
    bucket_rows = 2 * tok_rows // dev_count
    group_rows = dev_count * bucket_rows
    slab = model_width // dev_count
    row_count = head_count * cap_slots * step_count
    my_dev = lax.axis_index("dev")
    my_side = lax.axis_index("side")
    here = jnp.stack([my_dev, my_side]).astype(jnp.int32)

    mine = split_columns(prompts, here, dev_count)
    x_pieces = [lax.dynamic_slice_in_dim(prompts, my_dev * slab, slab, 1)] + [None] * (dev_count - 1)
    for k in sorted(range(1, dev_count), reverse=True):
        x_pieces[k] = swap(mine[k - 1], "dev", k)

    weights = [None] * side_count
    for k in range(0, side_count, 2):
        weights[k] = swap(latent_weight, "side", k) if k else latent_weight
    for k in range(0, side_count, 2):
        weights[k + 1] = swap(weights[k], "side", 1)
    if shard_rows % 16:
        held = jnp.zeros((side_count, shard_rows, kv_width), bf16)
        for k in range(side_count):
            held = lax.dynamic_update_slice(held, weights[k][None], (my_side ^ k, 0, 0))
        weights = [held.reshape(slab, kv_width)]

    request_ids = jnp.arange(req_count, dtype=jnp.int32)
    all_requests = row_request.reshape(block_count, 1, tok_rows)
    hit = (all_requests == request_ids[:, None]).astype(f32)
    below = (jnp.arange(tok_rows)[:, None] < jnp.arange(tok_rows)[None, :]).astype(f32)
    rank_local = jnp.einsum("bri,ij->brj", hit, below, preferred_element_type=f32)
    counts = jnp.sum(hit, axis=2)
    before = (jnp.arange(block_count)[:, None] > jnp.arange(block_count)[None, :]).astype(f32)
    earlier = jnp.einsum("ab,br->ar", before, counts, precision=lax.Precision.HIGHEST)
    position = jnp.sum(hit * (rank_local + (earlier + context_len.astype(f32))[:, :, None]), axis=1)
    slot_table = jnp.sum(hit * request_slot.astype(f32)[:, None], axis=1).astype(jnp.int32)
    row_group = slot_table // cap_slots
    group_ids = jnp.arange(dev_count, dtype=jnp.int32)
    group_hit = (row_group[:, None, :] == group_ids[:, None]).astype(f32)
    group_rank = jnp.sum(
        jnp.einsum("bgi,ij->bgj", group_hit, below, preferred_element_type=f32) * group_hit, axis=1
    ).astype(jnp.int32)
    by_dev = jnp.arange(block_count, dtype=jnp.int32)[:, None] // side_count
    place = by_dev * bucket_rows + group_rank
    order = my_dev ^ jnp.arange(dev_count, dtype=jnp.int32)
    line_of = lambda table: lax.dynamic_index_in_dim(
        table.reshape(dev_count, side_count, tok_rows), my_side, 1, keepdims=False
    )
    line_group, line_place, line_position = (line_of(t) for t in (row_group, place, position))
    target = (line_group ^ my_dev) * group_rows + line_place
    target = jnp.take(target, order, axis=0).reshape(1, -1)
    line_mine = jnp.where(line_group == my_dev, line_place, -1).reshape(1, -1)
    routed_position = jnp.sum(
        jnp.where(
            line_mine == jnp.arange(group_rows, dtype=jnp.int32)[:, None],
            line_position.reshape(1, -1), 0.0,
        ),
        axis=1,
    )
    half = rope_width // 2
    inverse = 1.0 / 10000.0 ** (jnp.arange(half, dtype=f32) * (2.0 / rope_width))
    angles = routed_position[:, None] * inverse[None, :]
    cosine, sine = jnp.cos(angles), jnp.sin(angles)
    side_order = my_side ^ jnp.arange(side_count, dtype=jnp.int32)
    side_table = lambda table: jnp.take(
        table.reshape(dev_count, side_count, tok_rows), side_order, axis=1
    )
    side_place = jnp.where(side_table(row_group) == my_dev, side_table(place), -1)
    side_place = jnp.swapaxes(side_place, 0, 1).reshape(side_count, 1, -1)
    side_slot = jnp.swapaxes(side_table(slot_table), 0, 1).reshape(side_count, 1, -1)
    row_slot = jnp.max(
        jnp.where(
            side_place == jnp.arange(group_rows, dtype=jnp.int32)[:, None], side_slot, -1
        ),
        axis=2,
    ).reshape(1, -1)

    query_latent = jnp.einsum(
        "sthn,hnc->hstc", queries[..., :nope_width], key_absorb, preferred_element_type=f32
    ).astype(bf16)
    query_full = jnp.concatenate(
        [query_latent, jnp.transpose(queries[..., nope_width:], (2, 0, 1, 3))], axis=-1
    )
    score_scale = queries.shape[-1] ** (-0.5)
    own_slots = my_dev * cap_slots + jnp.arange(cap_slots, dtype=jnp.int32)
    slot_hit = (own_slots[:, None] == request_slot[None, :]).astype(jnp.int32)
    occupied = (jnp.sum(slot_hit, axis=1) > 0).astype(f32)
    ctx_rows = jnp.sum(slot_hit * context_len[None, :], axis=1)
    score_cache = score_scale * jnp.einsum(
        "hstc,sjc->hstj", query_full, latent_cache, preferred_element_type=f32
    )
    mask_cache = (jnp.arange(ctx_len)[None, :] < ctx_rows[:, None])[None, :, None, :]
    score_cache = jnp.where(mask_cache, score_cache, masked_score)
    top_held = jnp.max(score_cache, axis=-1, keepdims=True)
    exp_cache = jnp.exp(score_cache - top_held)
    sum_held = jnp.sum(exp_cache, -1, keepdims=True)
    mix_held = jnp.einsum(
        "hstj,sjc->hstc", exp_cache.astype(bf16), latent_cache[..., :lat_width],
        preferred_element_type=f32,
    )
    live = jnp.broadcast_to(occupied[:, None], (cap_slots, step_count)).reshape(-1, 1)

    routed = project(x_pieces, weights, here, target, group_rows)
    parts = [routed[0]] + [None] * (dev_count - 1)
    for k in sorted(range(1, dev_count), reverse=True):
        parts[k] = swap(routed[k], "dev", k)
    latent_rows = finish(parts, latent_gain.reshape(1, -1), cosine, sine)
    pieces = [latent_rows] + [swap(latent_rows, "side", k) for k in range(1, side_count)]
    head_out = attend(
        score_scale, here, query_full.reshape(row_count, kv_width),
        new_latent.reshape(-1, kv_width), row_slot, top_held.reshape(row_count, 1),
        sum_held.reshape(row_count, 1), mix_held.reshape(row_count, lat_width), live,
        value_absorb, pieces, cap_slots,
    )
    heads = [head_out] + [swap(head_out, "dev", k) for k in range(1, dev_count)]
    products = output_product(heads, out_weight, here, side_count)
    result = products[0]
    for k in sorted(range(1, side_count), reverse=True):
        result = result + swap(products[k], "side", k).astype(f32)
    return result.astype(bf16)


def solution(mesh):
    placed = (
        P(("rep", "dev", "side"), None),
        P(("dev", "side"), None),
        P(),
        P("rep"),
        P("rep"),
        P("rep"),
        P(("rep", "dev"), None, None),
        P(("rep", "dev"), None, None),
        P(("rep", "dev"), None, "side", None),
        P("side", None, None),
        P("side", None, None),
        P("side", "dev"),
    )
    return jax.shard_map(
        on_device, mesh=mesh, in_specs=placed, out_specs=P(("rep", "side"), "dev"), check_vma=False
    )
```

time: 104 us -> 118 us (1.13)
  Pallas kernels: 0 us -> 33.6 us
  matrix products: 21.4 us -> 4.82 us
  other arithmetic: 16.2 us -> 6.63 us
  local copies, waits for them, and re-layouts: 17.9 us -> 21.4 us
  starting transfers between devices: 20.2 us -> 23.7 us
    pallas_call x0 -> x5, Pallas kernels: none -> 33.6 us  [the longest x1 22.6 us: split_columns(): pl.pallas_call(functools.partial(split_kernel, slab), out_shape=[jax.Shap...]
    dot_general x9 -> x2, matrix products: 16.3 us -> 0.32 us  [the longest x1 0.19 us: on_device(): jnp.einsum('bri,ij->brj', hit, below, preferred_element_type=f32)]
    unnamed x47 -> x23, local copies, waits for them, and re-layouts: 1.76 us -> 7.49 us
    select_n x4, other arithmetic: 4.91 us -> 0.76 us  [the longest x2 0.68 us: on_device(): jnp.take(table.reshape(dev_count, side_count, tok_rows), side_order, axis=1)]
    dynamic_update_slice x3 -> x0, local copies, waits for them, and re-layouts: 3.91 us -> none  [the longest x2 2.8 us: on_device(): held = lax.dynamic_update_slice(held, piece[None], (my_side ^ k, 0, 0))]
    ppermute x17 -> x18, starting transfers between devices: 20.2 us -> 23.7 us  [swap(): return lax.ppermute(value, axis, [(i, i ^ step) for i in range(count)])]
    mul x3 -> x0, local copies, waits for them, and re-layouts: 2.33 us -> none  [the longest x1 2.17 us: on_device(): jnp.swapaxes(by_step, 0, 1)[:, :, :, None, :] * same[None, :, None, :, None]]
    reshape x4, local copies, waits for them, and re-layouts: 1.95 us -> 4.19 us  [the longest x1 2.14 us: on_device(): query_full.reshape(row_count, kv_width)]
  transfers between devices with their start and end apart: 17 -> 18, of which waited for: 9 -> 7; matrix products, arithmetic and copies ran while one was open for 36% -> 21% of each run, Pallas kernels for 0% -> 19%
where the time goes in v2:
time: 118 us
  Pallas kernels  33.6 us (28%)
  waiting for transfers between devices  27.2 us (23%)
  starting transfers between devices  23.7 us (20%)
  local copies, waits for them, and re-layouts  21.4 us (18%)
  other arithmetic  6.63 us (6%)
  matrix products  4.82 us (4%)
    ppermute x18, waiting for transfers between devices, swap(): return lax.ppermute(value, axis, [(i, i ^ step) for i in range(count)])  27.2 us
    ppermute x18, starting transfers between devices, swap(): return lax.ppermute(value, axis, [(i, i ^ step) for i in range(count)])  23.7 us
    pallas_call x1, Pallas kernels, split_columns(): pl.pallas_call(functools.partial(split_kernel, slab), out_shape=[jax.Shap...  22.6 us
    unnamed x23, local copies, waits for them, and re-layouts  7.49 us
    pallas_call x1, Pallas kernels, attend(): pl.pallas_call(functools.partial(attend_kernel, scale, cap_slots, step_co...  4.97 us
    pallas_call x1, Pallas kernels, output_product(): pl.pallas_call(functools.partial(output_kernel, dev_count, side_count), o...  3.2 us
    dot_general x1, matrix products, on_device(): jnp.einsum('sthn,hnc->hstc', queries[..., :nope_width], key_absorb, prefe...  2.98 us
    pallas_call x1, Pallas kernels, project(): pl.pallas_call(functools.partial(project_kernel, dev_count, len(weights))...  2.55 us
  transfers between devices with their start and end apart: 18, of which 7 were waited for; matrix products, arithmetic and copies ran while one was open for 21% of the time, Pallas kernels for 19%

profile of v2, /device:TPU:0, one launch (start us, length us, event | category | flops | bytes accessed | tf_op | source)
XLA Modules:
  0.0 117.8 jit_solution(15179739817022267389)
XLA Ops:
  0.0 2.9 %collective-permute-start.4 = (bf16[448,576]{1,0:T(8,128)(2,1)}, bf16[448,576]{1,0:T(8,128)(2,1)S(1)}, u32[]{:S(2)}, u32[]{:S(2)}) collective-permute-start(bf16[448,576]{1,0:T(8,128)(2,1)} %refs_4_.2), channel_id=1, source_target_pairs={{0,2},{1,3},{2,0},{3,1},{4,6},{5,7},{6,4},{7,5},{8,10},{9,11},{10,... | collective-permute-start | bytes 1548296 | tf_op jit(solution)/shard_map/ppermute | solution.py:20
  2.9 0.6 pad_add_fusion.here_ref.base_ref
  3.6 22.6 %split_columns.1 = (bf16[64,1792]{1,0:T(8,128)(2,1)}, bf16[64,1792]{1,0:T(8,128)(2,1)}, bf16[64,1792]{1,0:T(8,128)(2,1)}) custom-call(s32[2]{0:T(128)} %pad_add_fusion.here_ref.base_ref, bf16[64,7168]{1,0:T(8,128)(2,1)} %prompts_ref.1), custom_call_target="tpu_custom_call" | custom-call | tf_op jit(solution)/shard_map/split_columns/pallas_call | solution.py:50
  26.2 1.6 %collective-permute-start = (bf16[64,1792]{1,0:T(8,128)(2,1)}, bf16[64,1792]{1,0:T(8,128)(2,1)S(1)}, u32[]{:S(2)}, u32[]{:S(2)}) collective-permute-start(bf16[64,1792]{1,0:T(8,128)(2,1)} %get-tuple-element.17), channel_id=1, source_target_pairs={{0,4},{4,0},{8,12},{12,8},{1,5},{5,1},{9,13},{13,9},{2,6},{6,2},{1... | collective-permute-start | bytes 688136 | tf_op jit(solution)/shard_map/ppermute | solution.py:20
  27.8 2.6 %collective-permute-start.1 = (bf16[64,1792]{1,0:T(8,128)(2,1)}, bf16[64,1792]{1,0:T(8,128)(2,1)S(1)}, u32[]{:S(2)}, u32[]{:S(2)}) collective-permute-start(bf16[64,1792]{1,0:T(8,128)(2,1)} %get-tuple-element.18), channel_id=1, source_target_pairs={{0,8},{4,12},{8,0},{12,4},{1,9},{5,13},{9,1},{13,5},{2,10},{6,14},... | collective-permute-start | bytes 688136 | tf_op jit(solution)/shard_map/ppermute | solution.py:20
  30.7 0.8 eq.86
  31.4 0.7 convert_element_type.60
  32.3 0.9 slice.10
  33.4 0.6 gather_fusion.1
  34.0 0.6 gather_fusion.2
  34.6 0.6 gather_fusion
  35.4 0.7 convert_element_type.69
  36.5 0.6 gather_fusion.3
  37.1 1.4 %fusion.42 = (s32[8]{0:T(128)}, s32[8]{0:T(128)S(1)}) fusion(s32[16]{0:T(128)} %param.19, s32[8]{0:T(128)S(1)} %iota_add_fusion, s32[16]{0:T(128)} %param.18), kind=kLoop, calls=%fused_computation.68 | loop fusion | flops 624 | bytes 224 | tf_op jit(solution)/shard_map/reduce_sum | solution.py:353
  39.0 0.7 broadcast_select_fusion
  39.6 0.7 fusion.38
  40.3 3.0 %fusion.10 = bf16[32,8,2,512]{3,1,2,0:T(8,128)(2,1)S(1)} fusion(bf16[32,128,512]{2,1,0:T(8,128)(2,1)} %param.23, bf16[8,2,32,128]{3,2,1,0:T(8,128)(2,1)S(1)} %slice-done), kind=kOutput, calls=%fused_computation.12 | convolution fusion | flops 67371008 | bytes 4849664 | tf_op jit(solution)/shard_map/sthn,hnc->hstc/dot_general | solution.py:344
  43.4 0.6 fusion.46
  44.2 0.8 fusion.7
  45.0 1.0 constant_dynamic-slice_fusion.refs_0_
  46.0 1.3 %collective-permute-done.1.refs_2_ = bf16[64,1792]{1,0:T(8,128)(2,1)S(1)} collective-permute-done((bf16[64,1792]{1,0:T(8,128)(2,1)}, bf16[64,1792]{1,0:T(8,128)(2,1)S(1)}, u32[]{:S(2)}, u32[]{:S(2)}) %collective-permute-start.1) | collective-permute-done | bytes 229408 | tf_op jit(solution)/shard_map/ppermute | solution.py:20
  47.3 2.6 %project.1 = (f32[128,576]{1,0:T(8,128)S(1)}, bf16[128,576]{1,0:T(8,128)(2,1)S(1)}, bf16[128,576]{1,0:T(8,128)(2,1)S(1)}, bf16[128,576]{1,0:T(8,128)(2,1)S(1)}) custom-call(s32[2]{0:T(128)S(1)} %copy-done.3, s32[1,256]{1,0:T(1,128)S(1)} %select_n.112.target_ref, bf16[64,1792]{1,0:T(8,128)(2,1)S(1)} %constant_dynamic-slice_fusion.refs_0_, ...), custom_call_target="tpu_custom_call" | custom-call | tf_op jit(solution)/shard_map/project/pallas_call | solution.py:89
  49.9 4.8 %collective-permute-start.6 = (bf16[128,576]{1,0:T(8,128)(2,1)S(1)}, bf16[128,576]{1,0:T(8,128)(2,1)S(1)}, u32[]{:S(2)}, u32[]{:S(2)}) collective-permute-start(bf16[128,576]{1,0:T(8,128)(2,1)S(1)} %get-tuple-element.21), channel_id=1, source_target_pairs={{0,4},{4,0},{8,12},{12,8},{1,5},{5,1},{9,13},{13,9},{2,6},{6,2},{1... | collective-permute-start | bytes 442376 | tf_op jit(solution)/shard_map/ppermute | solution.py:20
  54.7 1.1 collective-permute-start.7
  55.8 1.4 %collective-permute-start.8 = (bf16[128,576]{1,0:T(8,128)(2,1)S(1)}, bf16[128,576]{1,0:T(8,128)(2,1)S(1)}, u32[]{:S(2)}, u32[]{:S(2)}) collective-permute-start(bf16[128,576]{1,0:T(8,128)(2,1)S(1)} %get-tuple-element.23), channel_id=1, source_target_pairs={{0,12},{4,8},{8,4},{12,0},{1,13},{5,9},{9,5},{13,1},{2,14},{6,10},... | collective-permute-start | bytes 442376 | tf_op jit(solution)/shard_map/ppermute | solution.py:20
  57.2 3.4 %collective-permute-done.6.refs_1_ = bf16[128,576]{1,0:T(8,128)(2,1)S(1)} collective-permute-done((bf16[128,576]{1,0:T(8,128)(2,1)S(1)}, bf16[128,576]{1,0:T(8,128)(2,1)S(1)}, u32[]{:S(2)}, u32[]{:S(2)}) %collective-permute-start.6) | collective-permute-done | bytes 147488 | tf_op jit(solution)/shard_map/ppermute | solution.py:20
  60.6 9.1 %collective-permute-done.7.refs_2_ = bf16[128,576]{1,0:T(8,128)(2,1)S(1)} collective-permute-done((bf16[128,576]{1,0:T(8,128)(2,1)S(1)}, bf16[128,576]{1,0:T(8,128)(2,1)S(1)}, u32[]{:S(2)}, u32[]{:S(2)}) %collective-permute-start.7) | collective-permute-done | bytes 147488 | tf_op jit(solution)/shard_map/ppermute | solution.py:20
  69.9 0.6 collective-permute-start.10
  70.5 1.6 %collective-permute-start.9 = (bf16[128,576]{1,0:T(8,128)(2,1)S(1)}, bf16[128,576]{1,0:T(8,128)(2,1)S(1)}, u32[]{:S(2)}, u32[]{:S(2)}) collective-permute-start(bf16[128,576]{1,0:T(8,128)(2,1)S(1)} %finish_rows.1.refs_0_), channel_id=1, source_target_pairs={{0,1},{1,0},{2,3},{3,2},{4,5},{5,4},{6,7},{7,6},{8,9},{9,8},{10,11... | collective-permute-start | bytes 442376 | tf_op jit(solution)/shard_map/ppermute | solution.py:20
  72.4 0.8 copy.96
  73.2 1.4 %copy.88 = bf16[32,8,2,576]{3,2,1,0:T(2,128)(2,1)} copy(bf16[32,8,2,576]{3,1,2,0:T(8,128)(2,1)S(1)} %pad_maximum_fusion) | data formatting | bytes 1179648 | tf_op jit(solution)/shard_map/concatenate | solution.py:347
  74.8 1.8 %copy.99 = f32[32,8,2,512]{3,2,1,0:T(2,128)} copy(f32[32,8,2,512]{3,0,2,1:T(8,128)S(1)} %fusion.7) | data formatting | bytes 2097152 | tf_op jit(solution)/shard_map/hstj,sjc->hstc/transpose | solution.py:363
  76.6 2.0 %reshape.214.mix_ref = f32[512,512]{1,0:T(8,128)S(1)} reshape(f32[32,8,2,512]{3,2,1,0:T(2,128)} %copy.99) | data formatting | bytes 2097152 | tf_op jit(solution)/shard_map/reshape | solution.py:378
  79.0 2.1 %reshape.211.query_ref = bf16[512,576]{1,0:T(8,128)(2,1)S(1)} reshape(bf16[32,8,2,576]{3,2,1,0:T(2,128)(2,1)} %copy.88) | data formatting | bytes 1179648 | tf_op jit(solution)/shard_map/reshape | solution.py:376
  81.4 2.2 %copy-done.1 = bf16[32,512,128]{2,1,0:T(8,128)(2,1)S(1)} copy-done((bf16[32,512,128]{2,1,0:T(8,128)(2,1)S(1)}, bf16[32,512,128]{2,1,0:T(8,128)(2,1)}, u32[]{:S(2)}) %copy-start.1) | copy-done | bytes 4194328
  83.6 5.0 %attend.1.refs_0_ = bf16[16,4096]{1,0:T(8,128)(2,1)S(1)} custom-call(s32[2]{0:T(128)S(1)} %copy-done.3, bf16[512,576]{1,0:T(8,128)(2,1)S(1)} %reshape.211.query_ref, bf16[16,576]{1,0:T(8,128)(2,1)S(1)} %reshape.212.fresh_ref, s32[1,512]{1,0:T(1,128)S(1)} %bitcast.66, f32[512,1]{1,0:T(8,128)S(1)} %reshape_broadcast_in_dim.8.top_ref, ...), custom_call_target="tpu_custom_call" | custom-call | tf_op jit(solution)/shard_map/attend/pallas_call | solution.py:192
  88.6 2.4 %collective-permute-start.12 = (bf16[16,4096]{1,0:T(8,128)(2,1)S(1)}, bf16[16,4096]{1,0:T(8,128)(2,1)S(1)}, u32[]{:S(2)}, u32[]{:S(2)}) collective-permute-start(bf16[16,4096]{1,0:T(8,128)(2,1)S(1)} %attend.1.refs_0_), channel_id=1, source_target_pairs={{0,4},{4,0},{8,12},{12,8},{1,5},{5,1},{9,13},{13,9},{2,6},{6,2},{1... | collective-permute-start | bytes 393224 | tf_op jit(solution)/shard_map/ppermute | solution.py:20
  90.9 1.0 collective-permute-start.13
  92.0 1.4 %collective-permute-start.14 = (bf16[16,4096]{1,0:T(8,128)(2,1)S(1)}, bf16[16,4096]{1,0:T(8,128)(2,1)S(1)}, u32[]{:S(2)}, u32[]{:S(2)}) collective-permute-start(bf16[16,4096]{1,0:T(8,128)(2,1)S(1)} %attend.1.refs_0_), channel_id=1, source_target_pairs={{0,12},{4,8},{8,4},{12,0},{1,13},{5,9},{9,5},{13,1},{2,14},{6,10},... | collective-permute-start | bytes 393224 | tf_op jit(solution)/shard_map/ppermute | solution.py:20
  93.4 2.9 %collective-permute-done.12.refs_1_ = bf16[16,4096]{1,0:T(8,128)(2,1)S(1)} collective-permute-done((bf16[16,4096]{1,0:T(8,128)(2,1)S(1)}, bf16[16,4096]{1,0:T(8,128)(2,1)S(1)}, u32[]{:S(2)}, u32[]{:S(2)}) %collective-permute-start.12) | collective-permute-done | bytes 131104 | tf_op jit(solution)/shard_map/ppermute | solution.py:20
  96.3 7.5 %collective-permute-done.13.refs_2_ = bf16[16,4096]{1,0:T(8,128)(2,1)S(1)} collective-permute-done((bf16[16,4096]{1,0:T(8,128)(2,1)S(1)}, bf16[16,4096]{1,0:T(8,128)(2,1)S(1)}, u32[]{:S(2)}, u32[]{:S(2)}) %collective-permute-start.13) | collective-permute-done | bytes 131104 | tf_op jit(solution)/shard_map/ppermute | solution.py:20
  103.9 5.2 %copy-done = bf16[4096,1792]{1,0:T(8,128)(2,1)S(1)} copy-done((bf16[4096,1792]{1,0:T(8,128)(2,1)S(1)}, bf16[4096,1792]{1,0:T(8,128)(2,1)}, u32[]{:S(2)}) %copy-start) | copy-done | bytes 14680088
  109.0 3.2 %output_product.1 = (f32[16,1792]{1,0:T(8,128)S(1)}, bf16[16,1792]{1,0:T(8,128)(2,1)S(1)}, bf16[16,1792]{1,0:T(8,128)(2,1)S(1)}, bf16[16,1792]{1,0:T(8,128)(2,1)S(1)}) custom-call(s32[2]{0:T(128)S(1)} %copy-done.3, bf16[16,4096]{1,0:T(8,128)(2,1)S(1)} %attend.1.refs_0_, bf16[16,4096]{1,0:T(8,128)(2,1)S(1)} %collective-permute-done.12.refs_1_, ...), custom_call_target="tpu_custom_call" | custom-call | tf_op jit(solution)/shard_map/output_product/pallas_call | solution.py:230
  112.3 0.6 collective-permute-start.16
  112.9 1.3 %collective-permute-start.17 = (bf16[16,1792]{1,0:T(8,128)(2,1)S(1)}, bf16[16,1792]{1,0:T(8,128)(2,1)S(1)}, u32[]{:S(2)}, u32[]{:S(2)}) collective-permute-start(bf16[16,1792]{1,0:T(8,128)(2,1)S(1)} %get-tuple-element.27), channel_id=1, source_target_pairs={{0,1},{1,0},{2,3},{3,2},{4,5},{5,4},{6,7},{7,6},{8,9},{9,8},{10,11... | collective-permute-start | bytes 172040 | tf_op jit(solution)/shard_map/ppermute | solution.py:20
  114.2 1.7 %collective-permute-done.15 = bf16[16,1792]{1,0:T(8,128)(2,1)S(1)} collective-permute-done((bf16[16,1792]{1,0:T(8,128)(2,1)S(1)}, bf16[16,1792]{1,0:T(8,128)(2,1)S(1)}, u32[]{:S(2)}, u32[]{:S(2)}) %collective-permute-start.15) | collective-permute-done | bytes 57376 | tf_op jit(solution)/shard_map/ppermute | solution.py:20
  115.9 1.2 %collective-permute-done.16 = bf16[16,1792]{1,0:T(8,128)(2,1)S(1)} collective-permute-done((bf16[16,1792]{1,0:T(8,128)(2,1)S(1)}, bf16[16,1792]{1,0:T(8,128)(2,1)S(1)}, u32[]{:S(2)}, u32[]{:S(2)}) %collective-permute-start.16) | collective-permute-done | bytes 57376 | tf_op jit(solution)/shard_map/ppermute | solution.py:20
  117.1 0.7 add_convert_fusion
  (77 shorter events, 3.6 us)
Async XLA Ops:
  0.0 40.3 %slice-start = ((bf16[8,2,32,192]{3,2,1,0:T(8,128)(2,1)}), bf16[8,2,32,128]{3,2,1,0:T(8,128)(2,1)S(1)}, s32[]{:S(2)}) async-start(bf16[8,2,32,192]{3,2,1,0:T(8,128)(2,1)} %param.22), calls=%async_computation | async-start | bytes 262144 | tf_op jit(solution)/shard_map/slice | solution.py:345
  0.0 44.1 %collective-permute-start.4 = (bf16[448,576]{1,0:T(8,128)(2,1)}, bf16[448,576]{1,0:T(8,128)(2,1)S(1)}, u32[]{:S(2)}, u32[]{:S(2)}) collective-permute-start(bf16[448,576]{1,0:T(8,128)(2,1)} %refs_4_.2), channel_id=1, source_target_pairs={{0,2},{1,3},{2,0},{3,1},{4,6},{5,7},{6,4},{7,5},{8,10},{9,11},{10,... | collective-permute-start | bytes 1548296 | tf_op jit(solution)/shard_map/ppermute | solution.py:20
  2.9 44.3 %collective-permute-start.3 = (bf16[448,576]{1,0:T(8,128)(2,1)}, bf16[448,576]{1,0:T(8,128)(2,1)S(1)}, u32[]{:S(2)}, u32[]{:S(2)}) collective-permute-start(bf16[448,576]{1,0:T(8,128)(2,1)} %refs_4_.2), channel_id=1, source_target_pairs={{0,1},{1,0},{2,3},{3,2},{4,5},{5,4},{6,7},{7,6},{8,9},{9,8},{10,11... | collective-permute-start | bytes 1548296 | tf_op jit(solution)/shard_map/ppermute | solution.py:20
  26.2 19.8 %collective-permute-start = (bf16[64,1792]{1,0:T(8,128)(2,1)}, bf16[64,1792]{1,0:T(8,128)(2,1)S(1)}, u32[]{:S(2)}, u32[]{:S(2)}) collective-permute-start(bf16[64,1792]{1,0:T(8,128)(2,1)} %get-tuple-element.17), channel_id=1, source_target_pairs={{0,4},{4,0},{8,12},{12,8},{1,5},{5,1},{9,13},{13,9},{2,6},{6,2},{1... | collective-permute-start | bytes 688136 | tf_op jit(solution)/shard_map/ppermute | solution.py:20
  27.8 19.4 %collective-permute-start.1 = (bf16[64,1792]{1,0:T(8,128)(2,1)}, bf16[64,1792]{1,0:T(8,128)(2,1)S(1)}, u32[]{:S(2)}, u32[]{:S(2)}) collective-permute-start(bf16[64,1792]{1,0:T(8,128)(2,1)} %get-tuple-element.18), channel_id=1, source_target_pairs={{0,8},{4,12},{8,0},{12,4},{1,9},{5,13},{9,1},{13,5},{2,10},{6,14},... | collective-permute-start | bytes 688136 | tf_op jit(solution)/shard_map/ppermute | solution.py:20
  30.4 16.8 %collective-permute-start.2 = (bf16[64,1792]{1,0:T(8,128)(2,1)}, bf16[64,1792]{1,0:T(8,128)(2,1)S(1)}, u32[]{:S(2)}, u32[]{:S(2)}) collective-permute-start(bf16[64,1792]{1,0:T(8,128)(2,1)} %get-tuple-element.19), channel_id=1, source_target_pairs={{0,12},{4,8},{8,4},{12,0},{1,13},{5,9},{9,5},{13,1},{2,14},{6,10},... | collective-permute-start | bytes 688136 | tf_op jit(solution)/shard_map/ppermute | solution.py:20
  40.3 3.1 %copy-start.5 = (bf16[8,256,576]{1,2,0:T(8,128)(2,1)S(1)}, bf16[8,256,576]{1,2,0:T(8,128)(2,1)}, u32[]{:S(2)}) copy-start(bf16[8,256,576]{1,2,0:T(8,128)(2,1)} %param.20) | copy-start | bytes 7077892
  44.1 3.2 %copy-start.2 = (bf16[448,576]{1,0:T(8,128)(2,1)S(1)}, bf16[448,576]{1,0:T(8,128)(2,1)}, u32[]{:S(2)}) copy-start(bf16[448,576]{1,0:T(8,128)(2,1)} %refs_4_.2) | copy-start | bytes 1548292
  44.1 3.2 %copy-start.3 = (s32[2]{0:T(128)S(1)}, s32[2]{0:T(128)}, u32[]{:S(2)}) copy-start(s32[2]{0:T(128)} %pad_add_fusion.here_ref.base_ref) | copy-start | bytes 28
  44.1 3.1 %collective-permute-start.5 = (bf16[448,576]{1,0:T(8,128)(2,1)S(1)}, bf16[448,576]{1,0:T(8,128)(2,1)S(1)}, u32[]{:S(2)}, u32[]{:S(2)}) collective-permute-start(bf16[448,576]{1,0:T(8,128)(2,1)S(1)} %collective-permute-done.4.refs_6_), channel_id=1, source_target_pairs={{0,1},{1,0},{2,3},{3,2},{4,5},{5,4},{6,7},{7,6},{8,9},{9,8},{10,11... | collective-permute-start | bytes 1548296 | tf_op jit(solution)/shard_map/ppermute | solution.py:20
  45.0 12.2 %copy-start.10 = (s32[8]{0:T(128)S(1)}, s32[8]{0:T(128)}, u32[]{:S(2)}) copy-start(s32[8]{0:T(128)} %get-tuple-element.30) | copy-start | bytes 100
  45.0 24.7 %copy-start.4 = (f32[512]{0:T(512)S(1)}, f32[512]{0:T(512)}, u32[]{:S(2)}) copy-start(f32[512]{0:T(512)} %param.16) | copy-start | bytes 6148
  49.9 24.7 %copy-start.7 = (s32[4,4,64]{2,1,0:T(4,128)S(1)}, s32[4,4,64]{2,1,0:T(4,128)}, u32[]{:S(2)}) copy-start(s32[4,4,64]{2,1,0:T(4,128)} %fusion.38) | copy-start | bytes 12292
  49.9 24.8 %copy-start.8 = (s32[4,4,64]{2,1,0:T(4,128)S(1)}, s32[4,4,64]{2,1,0:T(4,128)}, u32[]{:S(2)}) copy-start(s32[4,4,64]{2,1,0:T(4,128)} %broadcast_select_fusion) | copy-start | bytes 12292
  49.9 10.7 %collective-permute-start.6 = (bf16[128,576]{1,0:T(8,128)(2,1)S(1)}, bf16[128,576]{1,0:T(8,128)(2,1)S(1)}, u32[]{:S(2)}, u32[]{:S(2)}) collective-permute-start(bf16[128,576]{1,0:T(8,128)(2,1)S(1)} %get-tuple-element.21), channel_id=1, source_target_pairs={{0,4},{4,0},{8,12},{12,8},{1,5},{5,1},{9,13},{13,9},{2,6},{6,2},{1... | collective-permute-start | bytes 442376 | tf_op jit(solution)/shard_map/ppermute | solution.py:20
  54.7 15.0 %collective-permute-start.7 = (bf16[128,576]{1,0:T(8,128)(2,1)S(1)}, bf16[128,576]{1,0:T(8,128)(2,1)S(1)}, u32[]{:S(2)}, u32[]{:S(2)}) collective-permute-start(bf16[128,576]{1,0:T(8,128)(2,1)S(1)} %get-tuple-element.22), channel_id=1, source_target_pairs={{0,8},{4,12},{8,0},{12,4},{1,9},{5,13},{9,1},{13,5},{2,10},{6,14},... | collective-permute-start | bytes 442376 | tf_op jit(solution)/shard_map/ppermute | solution.py:20
  55.8 13.9 %collective-permute-start.8 = (bf16[128,576]{1,0:T(8,128)(2,1)S(1)}, bf16[128,576]{1,0:T(8,128)(2,1)S(1)}, u32[]{:S(2)}, u32[]{:S(2)}) collective-permute-start(bf16[128,576]{1,0:T(8,128)(2,1)S(1)} %get-tuple-element.23), channel_id=1, source_target_pairs={{0,12},{4,8},{8,4},{12,0},{1,13},{5,9},{9,5},{13,1},{2,14},{6,10},... | collective-permute-start | bytes 442376 | tf_op jit(solution)/shard_map/ppermute | solution.py:20
  69.9 11.4 %collective-permute-start.10 = (bf16[128,576]{1,0:T(8,128)(2,1)S(1)}, bf16[128,576]{1,0:T(8,128)(2,1)S(1)}, u32[]{:S(2)}, u32[]{:S(2)}) collective-permute-start(bf16[128,576]{1,0:T(8,128)(2,1)S(1)} %finish_rows.1.refs_0_), channel_id=1, source_target_pairs={{0,2},{1,3},{2,0},{3,1},{4,6},{5,7},{6,4},{7,5},{8,10},{9,11},{10,... | collective-permute-start | bytes 442376 | tf_op jit(solution)/shard_map/ppermute | solution.py:20
  70.5 10.8 %collective-permute-start.11 = (bf16[128,576]{1,0:T(8,128)(2,1)S(1)}, bf16[128,576]{1,0:T(8,128)(2,1)S(1)}, u32[]{:S(2)}, u32[]{:S(2)}) collective-permute-start(bf16[128,576]{1,0:T(8,128)(2,1)S(1)} %finish_rows.1.refs_0_), channel_id=1, source_target_pairs={{0,3},{1,2},{2,1},{3,0},{4,7},{5,6},{6,5},{7,4},{8,11},{9,10},{10,... | collective-permute-start | bytes 442376 | tf_op jit(solution)/shard_map/ppermute | solution.py:20
  70.5 10.8 %collective-permute-start.9 = (bf16[128,576]{1,0:T(8,128)(2,1)S(1)}, bf16[128,576]{1,0:T(8,128)(2,1)S(1)}, u32[]{:S(2)}, u32[]{:S(2)}) collective-permute-start(bf16[128,576]{1,0:T(8,128)(2,1)S(1)} %finish_rows.1.refs_0_), channel_id=1, source_target_pairs={{0,1},{1,0},{2,3},{3,2},{4,5},{5,4},{6,7},{7,6},{8,9},{9,8},{10,11... | collective-permute-start | bytes 442376 | tf_op jit(solution)/shard_map/ppermute | solution.py:20
  74.8 4.0 %copy-start.6 = (f32[32,8,2]{2,1,0:T(8,128)S(1)}, f32[32,8,2]{2,1,0:T(8,128)}, u32[]{:S(2)}) copy-start(f32[32,8,2]{2,1,0:T(8,128)} %copy.96) | copy-start | bytes 6148
  76.6 4.6 %copy-start.9 = (bf16[8,2,576]{2,1,0:T(2,128)(2,1)S(1)}, bf16[8,2,576]{2,1,0:T(2,128)(2,1)}, u32[]{:S(2)}) copy-start(bf16[8,2,576]{2,1,0:T(2,128)(2,1)} %param.21) | copy-start | bytes 55300
  81.4 2.2 %copy-start.1 = (bf16[32,512,128]{2,1,0:T(8,128)(2,1)S(1)}, bf16[32,512,128]{2,1,0:T(8,128)(2,1)}, u32[]{:S(2)}) copy-start(bf16[32,512,128]{2,1,0:T(8,128)(2,1)} %value_ref.1) | copy-start | bytes 12582916
  88.6 7.8 %collective-permute-start.12 = (bf16[16,4096]{1,0:T(8,128)(2,1)S(1)}, bf16[16,4096]{1,0:T(8,128)(2,1)S(1)}, u32[]{:S(2)}, u32[]{:S(2)}) collective-permute-start(bf16[16,4096]{1,0:T(8,128)(2,1)S(1)} %attend.1.refs_0_), channel_id=1, source_target_pairs={{0,4},{4,0},{8,12},{12,8},{1,5},{5,1},{9,13},{13,9},{2,6},{6,2},{1... | collective-permute-start | bytes 393224 | tf_op jit(solution)/shard_map/ppermute | solution.py:20
  90.9 12.9 %collective-permute-start.13 = (bf16[16,4096]{1,0:T(8,128)(2,1)S(1)}, bf16[16,4096]{1,0:T(8,128)(2,1)S(1)}, u32[]{:S(2)}, u32[]{:S(2)}) collective-permute-start(bf16[16,4096]{1,0:T(8,128)(2,1)S(1)} %attend.1.refs_0_), channel_id=1, source_target_pairs={{0,8},{4,12},{8,0},{12,4},{1,9},{5,13},{9,1},{13,5},{2,10},{6,14},... | collective-permute-start | bytes 393224 | tf_op jit(solution)/shard_map/ppermute | solution.py:20
  92.0 11.9 %collective-permute-start.14 = (bf16[16,4096]{1,0:T(8,128)(2,1)S(1)}, bf16[16,4096]{1,0:T(8,128)(2,1)S(1)}, u32[]{:S(2)}, u32[]{:S(2)}) collective-permute-start(bf16[16,4096]{1,0:T(8,128)(2,1)S(1)} %attend.1.refs_0_), channel_id=1, source_target_pairs={{0,12},{4,8},{8,4},{12,0},{1,13},{5,9},{9,5},{13,1},{2,14},{6,10},... | collective-permute-start | bytes 393224 | tf_op jit(solution)/shard_map/ppermute | solution.py:20
  103.9 5.2 %copy-start = (bf16[4096,1792]{1,0:T(8,128)(2,1)S(1)}, bf16[4096,1792]{1,0:T(8,128)(2,1)}, u32[]{:S(2)}) copy-start(bf16[4096,1792]{1,0:T(8,128)(2,1)} %refs_4_.3) | copy-start | bytes 44040196
  112.3 3.7 %collective-permute-start.15 = (bf16[16,1792]{1,0:T(8,128)(2,1)S(1)}, bf16[16,1792]{1,0:T(8,128)(2,1)S(1)}, u32[]{:S(2)}, u32[]{:S(2)}) collective-permute-start(bf16[16,1792]{1,0:T(8,128)(2,1)S(1)} %get-tuple-element.25), channel_id=1, source_target_pairs={{0,3},{1,2},{2,1},{3,0},{4,7},{5,6},{6,5},{7,4},{8,11},{9,10},{10,... | collective-permute-start | bytes 172040 | tf_op jit(solution)/shard_map/ppermute | solution.py:20
  112.3 4.8 %collective-permute-start.16 = (bf16[16,1792]{1,0:T(8,128)(2,1)S(1)}, bf16[16,1792]{1,0:T(8,128)(2,1)S(1)}, u32[]{:S(2)}, u32[]{:S(2)}) collective-permute-start(bf16[16,1792]{1,0:T(8,128)(2,1)S(1)} %get-tuple-element.26), channel_id=1, source_target_pairs={{0,2},{1,3},{2,0},{3,1},{4,6},{5,7},{6,4},{7,5},{8,10},{9,11},{10,... | collective-permute-start | bytes 172040 | tf_op jit(solution)/shard_map/ppermute | solution.py:20
  112.9 4.2 %collective-permute-start.17 = (bf16[16,1792]{1,0:T(8,128)(2,1)S(1)}, bf16[16,1792]{1,0:T(8,128)(2,1)S(1)}, u32[]{:S(2)}, u32[]{:S(2)}) collective-permute-start(bf16[16,1792]{1,0:T(8,128)(2,1)S(1)} %get-tuple-element.27), channel_id=1, source_target_pairs={{0,1},{1,0},{2,3},{3,2},{4,5},{5,4},{6,7},{7,6},{8,9},{9,8},{10,11... | collective-permute-start | bytes 172040 | tf_op jit(solution)/shard_map/ppermute | solution.py:20

commit v3 on v2

v3 whole, which is shorter than its diff:
```python
import functools

import jax
import jax.numpy as jnp
from jax import lax
from jax.experimental import pallas as pl
from jax.experimental.pallas import tpu as pltpu
from jax.sharding import PartitionSpec as P

masked_score = -1e30
bf16, f32 = jnp.bfloat16, jnp.float32
in_vmem = pl.BlockSpec(memory_space=pltpu.VMEM)
in_smem = pl.BlockSpec(memory_space=pltpu.SMEM)
anywhere = pl.BlockSpec(memory_space=pl.ANY)
mib = 1024 * 1024
prepare_mib = 10


def swap(value, axis, step):
    count = lax.axis_size(axis)
    return lax.ppermute(value, axis, [(i, i ^ step) for i in range(count)])


def pick(pieces, index):
    out = pieces[0]
    for k in range(1, len(pieces)):
        out = jnp.where(index == k, pieces[k], out)
    return out


def lane_tiles(width):
    return [slice(n, min(n + 128, width)) for n in range(0, width, 128)]


def split_kernel(slab, prompts_ref, *refs):
    my_dev = lax.axis_index("dev")
    out_refs, sems = refs[:-1], refs[-1]
    copies = []
    for k in range(len(out_refs))[::-1]:
        first = pl.multiple_of((my_dev ^ k) * slab, 128)
        copies.append(
            pltpu.make_async_copy(prompts_ref.at[:, pl.ds(first, slab)], out_refs[k], sems.at[k])
        )
    for copy in copies:
        copy.start()
    for copy in copies:
        copy.wait()


def split_columns(prompts, count):
    rows, width = prompts.shape
    slab = width // count
    if slab % 128:
        columns = [prompts[:, k * slab : (k + 1) * slab] for k in range(count)]
        my_dev = lax.axis_index("dev")
        return [pick(columns, my_dev ^ k) for k in range(count)]
    return pl.pallas_call(
        functools.partial(split_kernel, slab),
        out_shape=[jax.ShapeDtypeStruct((rows, slab), prompts.dtype)] * count,
        in_specs=[anywhere],
        out_specs=[in_vmem] * count,
        scratch_shapes=[pltpu.SemaphoreType.DMA((count,))],
        compiler_params=pltpu.CompilerParams(vmem_limit_bytes=8 * mib),
        name="split_columns",
    )(prompts)


def fill_tables(
    dev_count, side_count, bucket, cap_slots, length_ref, slot_ref, request_ref, inverse_ref,
    target_ref, cos_ref, sin_ref, spot_ref, to_ref, place_ref, local_ref, position_ref,
):
    my_dev, my_side = lax.axis_index("dev"), lax.axis_index("side")
    requests = request_ref[...]
    lane_rows, lanes = requests.shape
    tok_rows = bucket * dev_count // 2
    per_row = lanes // tok_rows
    group_rows = dev_count * bucket
    before = lax.broadcasted_iota(jnp.int32, (lanes, lanes), 0)
    after = lax.broadcasted_iota(jnp.int32, (lanes, lanes), 1)
    below = jnp.where(before < after, 1.0, 0.0)
    near = jnp.where((before < after) & (before // tok_rows == after // tok_rows), 1.0, 0.0)
    scan = jnp.concatenate([below, jnp.ones_like(below)], axis=1).astype(bf16)
    lower = lax.broadcasted_iota(jnp.int32, (lane_rows, lane_rows), 0)
    upper = lax.broadcasted_iota(jnp.int32, (lane_rows, lane_rows), 1)
    rows_before = jnp.where(upper < lower, 1.0, 0.0)
    position = jnp.zeros(requests.shape, f32)
    slot = jnp.zeros(requests.shape, jnp.int32)
    for q in range(slot_ref.shape[0]):
        hit = requests == q
        ranks = jnp.dot(
            jnp.where(hit, 1.0, 0.0).astype(bf16), scan, preferred_element_type=f32
        )
        earlier = jnp.dot(rows_before, ranks[:, lanes:], preferred_element_type=f32)
        start = length_ref[q].astype(f32)
        position = jnp.where(hit, ranks[:, :lanes] + earlier + start, position)
        slot = jnp.where(hit, slot_ref[q], slot)
    group = lax.div(slot, cap_slots)
    rank = jnp.zeros(requests.shape, f32)
    for g in range(dev_count):
        hit = group == g
        ranks = jnp.dot(
            jnp.where(hit, 1.0, 0.0).astype(bf16), near.astype(bf16), preferred_element_type=f32
        )
        rank = jnp.where(hit, ranks, rank)
    block = lax.broadcasted_iota(jnp.int32, requests.shape, 0) * per_row + lax.div(
        lax.broadcasted_iota(jnp.int32, requests.shape, 1), tok_rows
    )
    place = lax.div(block, side_count) * bucket + rank.astype(jnp.int32)
    to_ref[...] = (group ^ my_dev) * group_rows + place
    place_ref[...] = jnp.where(group == my_dev, place, -1)
    local_ref[...] = (slot - my_dev * cap_slots + 1).astype(f32)
    position_ref[...] = position
    lane_block = lax.div(lax.broadcasted_iota(jnp.int32, (1, lanes), 1), tok_rows)
    ids = lax.broadcasted_iota(jnp.int32, (group_rows, 1), 0)

    def find(dev, side):
        held = dev * side_count + side
        return pl.ds(lax.div(held, per_row), 1), lane_block == lax.rem(held, per_row)

    for k in range(dev_count):
        row, inside = find(my_dev ^ k, my_side)
        target_ref[:, k * lanes : (k + 1) * lanes] = jnp.where(inside, to_ref[row, :], -1)
    found = jnp.zeros((group_rows, lanes), f32)
    for d in range(dev_count):
        row, inside = find(d, my_side)
        found = jnp.where((place_ref[row, :] == ids) & inside, position_ref[row, :], found)
    angles = jnp.sum(found, axis=1, keepdims=True) * inverse_ref[...]
    cos_ref[...] = jnp.cos(angles)
    sin_ref[...] = jnp.sin(angles)
    for k in range(side_count):
        total = jnp.zeros((8, group_rows), f32)
        for d in range(dev_count):
            row, inside = find(d, my_side ^ k)
            chosen = jnp.where((place_ref[row, :] == ids) & inside, 1.0, 0.0).astype(bf16)
            values = jnp.broadcast_to(local_ref[row, :], (8, lanes)).astype(bf16)
            total = total + lax.dot_general(
                values, chosen, (((1,), (1,)), ((), ())), preferred_element_type=f32
            )
        spot_ref[:, k * group_rows : (k + 1) * group_rows] = total[:1].astype(jnp.int32)


def prepare_kernel(
    scale, steps, layout, length_ref, slot_ref, request_ref, inverse_ref, query_ref, absorb_ref,
    cache_ref, value_hbm, out_hbm, full_ref, top_ref, sum_ref, mix_ref, live_ref, target_ref,
    cos_ref, sin_ref, spot_ref, value_ref, out_ref, plain, full, to_ref, place_ref, local_ref,
    position_ref, sems,
):
    copies = [pltpu.make_async_copy(value_hbm, value_ref, sems.at[0])]
    parts = sems.shape[0] - 1
    rows = out_hbm.shape[0] // parts
    for n in range(parts):
        part = pl.ds(n * rows, rows)
        copies.append(pltpu.make_async_copy(out_hbm.at[part], out_ref.at[part], sems.at[n + 1]))
    for copy in copies:
        copy.start()
    slots, _, context = cache_ref.shape
    heads, nope, lat_width = absorb_ref.shape
    per_head = slots * steps
    fill_tables(
        *layout, slots, length_ref, slot_ref, request_ref, inverse_ref, target_ref, cos_ref,
        sin_ref, spot_ref, to_ref, place_ref, local_ref, position_ref,
    )
    first_slot = lax.axis_index("dev") * slots
    lengths = []
    for s in range(slots):
        length = jnp.int32(0)
        for q in range(slot_ref.shape[0]):
            length = jnp.where(slot_ref[q] == first_slot + s, length_ref[q], length)
        lengths.append(length)
    slot_of = lax.div(lax.broadcasted_iota(jnp.int32, live_ref.shape, 0), steps)
    live = jnp.zeros(live_ref.shape, f32)
    for s in range(slots):
        live = jnp.where((slot_of == s) & (lengths[s] > 0), 1.0, live)
    live_ref[...] = live
    for n, here in enumerate(lane_tiles(query_ref.shape[1])):
        plain[n, :, : here.stop - here.start] = query_ref[:, here].astype(f32)
    wide = lane_tiles(full_ref.shape[1])
    for h in range(heads):
        there = pl.ds(h, per_head, stride=heads)
        query = plain[0, there, :].astype(bf16)
        latent = jnp.dot(query, absorb_ref[h], preferred_element_type=f32).astype(bf16).astype(f32)
        here = slice(h * per_head, (h + 1) * per_head)
        for n, lanes in enumerate(lane_tiles(lat_width)):
            full[n, here, :] = latent[:, lanes]
        full[len(wide) - 1, here, :] = plain[1, there, :]
    for n, lanes in enumerate(wide):
        full_ref[:, lanes] = full[n, :, : lanes.stop - lanes.start].astype(bf16)
    key = lax.broadcasted_iota(jnp.int32, (1, context), 1)
    for s in range(slots):
        theres = [pl.ds(s * steps + t, heads, stride=per_head) for t in range(steps)]
        query = jnp.concatenate(
            [
                jnp.concatenate([full[n, there, :] for there in theres], axis=0)[
                    :, : lanes.stop - lanes.start
                ].astype(bf16)
                for n, lanes in enumerate(wide)
            ],
            axis=1,
        )
        rows = cache_ref[s]
        score = jnp.dot(query, rows, preferred_element_type=f32)
        score = jnp.where(key < lengths[s], score * scale, masked_score)
        top = jnp.max(score, axis=1, keepdims=True)
        weight = jnp.exp(score - top)
        total = jnp.sum(weight, axis=1, keepdims=True)
        mix = lax.dot_general(
            weight.astype(bf16), rows[:lat_width, :], (((1,), (1,)), ((), ())),
            preferred_element_type=f32,
        )
        lanes = top_ref.shape[1]
        for t in range(steps):
            there = theres[t]
            here = slice(t * heads, (t + 1) * heads)
            top_ref[there, :] = jnp.broadcast_to(top[here], (heads, lanes))
            sum_ref[there, :] = jnp.broadcast_to(total[here], (heads, lanes))
            for n, part in enumerate(lane_tiles(lat_width)):
                mix_ref[n, there, :] = mix[here, part]
    for copy in copies:
        copy.wait()


def prepare(
    scale, dev_count, side_count, bucket, lengths, request_slot, requests, inverse, queries,
    absorb, cache, value, out_weight,
):
    slots, steps, heads, width = queries.shape
    kv_width = cache.shape[1]
    lat_width = absorb.shape[2]
    rows = slots * steps * heads
    group_rows = dev_count * bucket
    parts = 8
    lanes = requests.shape[1]
    half = inverse.shape[1]
    shapes = [
        ((rows, kv_width), bf16), ((rows, 128), f32), ((rows, 128), f32),
        ((lat_width // 128, rows, 128), f32), ((slots * steps, 128), f32),
        ((1, dev_count * lanes), jnp.int32), ((group_rows, half), f32), ((group_rows, half), f32),
        ((1, side_count * group_rows), jnp.int32), (value.shape, bf16), (out_weight.shape, bf16),
    ]
    return pl.pallas_call(
        functools.partial(prepare_kernel, scale, steps, (dev_count, side_count, bucket)),
        out_shape=[jax.ShapeDtypeStruct(*shape) for shape in shapes],
        in_specs=[in_smem] * 2 + [in_vmem] * 5 + [anywhere] * 2,
        out_specs=[in_vmem] * len(shapes),
        scratch_shapes=[
            pltpu.VMEM((len(lane_tiles(width)), rows, 128), f32),
            pltpu.VMEM((len(lane_tiles(kv_width)), rows, 128), f32),
            pltpu.VMEM(requests.shape, jnp.int32),
            pltpu.VMEM(requests.shape, jnp.int32),
            pltpu.VMEM(requests.shape, f32),
            pltpu.VMEM(requests.shape, f32),
            pltpu.SemaphoreType.DMA((parts + 1,)),
        ],
        compiler_params=pltpu.CompilerParams(vmem_limit_bytes=prepare_mib * mib),
        cost_estimate=pl.CostEstimate(
            flops=4 * 10**9, bytes_accessed=28 * 10**6, transcendentals=10**5
        ),
        name="prepare",
    )(lengths, request_slot, requests, inverse, queries.reshape(rows, width), absorb, cache, value,
      out_weight)


def project_kernel(dev_count, side_count, target_ref, *refs):
    my_side = lax.axis_index("side")
    x_refs = refs[:dev_count]
    weight_refs = refs[dev_count : dev_count + side_count]
    out_refs = refs[dev_count + side_count : -2]
    slab_weight, rows = refs[-2:]
    shard = weight_refs[0].shape[0]
    tok_rows = x_refs[0].shape[0]
    if side_count > 1:
        for k in range(side_count):
            first = pl.multiple_of((my_side ^ k) * shard, 16)
            slab_weight[pl.ds(first, shard), :] = weight_refs[k][...]
    copies = target_ref.shape[1] // (dev_count * tok_rows)
    for k in range(dev_count):
        part = jnp.dot(
            x_refs[k][...], slab_weight[...] if side_count > 1 else weight_refs[0][...],
            preferred_element_type=f32,
        ).astype(bf16)
        for n in range(k * copies, (k + 1) * copies):
            rows[n * tok_rows : (n + 1) * tok_rows, :] = part
    group_rows = out_refs[0].shape[0]
    target = target_ref[...]
    for j in range(dev_count):
        ids = lax.broadcasted_iota(jnp.int32, (group_rows, target.shape[1]), 0) + j * group_rows
        route = jnp.where(ids == target, 1.0, 0.0).astype(bf16)
        out_refs[j][...] = jnp.dot(
            route, rows[...], preferred_element_type=f32
        ).astype(out_refs[j].dtype)


def project(x_pieces, weights, target, group_rows):
    dev_count, width = len(x_pieces), weights[0].shape[1]
    tok_rows, slab = x_pieces[0].shape
    return pl.pallas_call(
        functools.partial(project_kernel, dev_count, len(weights)),
        out_shape=[
            jax.ShapeDtypeStruct((group_rows, width), f32 if j == 0 else bf16)
            for j in range(dev_count)
        ],
        in_specs=[in_vmem] * (1 + dev_count + len(weights)),
        out_specs=[in_vmem] * dev_count,
        scratch_shapes=[
            pltpu.VMEM((slab, width), bf16),
            pltpu.VMEM((target.shape[1], width), bf16),
        ],
        compiler_params=pltpu.CompilerParams(vmem_limit_bytes=10 * mib),
        name="project",
    )(target, *x_pieces, *weights)


def finish_kernel(gain_ref, cos_ref, sin_ref, *refs):
    parts, out_ref = refs[:-1], refs[-1]
    lat_width = gain_ref.shape[1]
    half = cos_ref.shape[1]
    total = parts[0][...].astype(f32)
    for part in parts[1:]:
        total = total + part[...].astype(f32)
    latent = total[:, :lat_width]
    spread = jnp.mean(latent * latent, axis=1, keepdims=True)
    out_ref[:, :lat_width] = (latent * lax.rsqrt(spread + 1e-06) * gain_ref[...]).astype(bf16)
    first = total[:, lat_width : lat_width + half]
    second = total[:, lat_width + half :]
    cosine, sine = cos_ref[...], sin_ref[...]
    turned = jnp.concatenate(
        [first * cosine - second * sine, second * cosine + first * sine], axis=1
    )
    out_ref[:, lat_width:] = turned.astype(bf16)


def finish(parts, gain, cosine, sine):
    return pl.pallas_call(
        finish_kernel,
        out_shape=jax.ShapeDtypeStruct(parts[0].shape, bf16),
        in_specs=[in_vmem] * (3 + len(parts)),
        out_specs=in_vmem,
        compiler_params=pltpu.CompilerParams(vmem_limit_bytes=8 * mib),
        name="finish_rows",
    )(gain, cosine, sine, *parts)


def attend_kernel(
    scale, cap_slots, steps, part, parts, query_ref, fresh_ref, slot_ref, top_ref,
    sum_ref, mix_ref, live_ref, value_ref, *refs
):
    pieces, out_ref, keys = refs[:-2], refs[-2], refs[-1]
    lat_width = mix_ref.shape[0] * mix_ref.shape[2]
    per_head = cap_slots * steps
    rows = query_ref.shape[0] // parts
    heads = rows // per_head
    mine = slice(part * rows, (part + 1) * rows)
    piece_rows = pieces[0].shape[0]
    for n, piece in enumerate(pieces):
        keys[n * piece_rows : (n + 1) * piece_rows, :] = piece[...]
    contract = (((1,), (1,)), ((), ()))
    row = lax.broadcasted_iota(jnp.int32, (rows, 1), 0)
    row_slot = (row // steps) % cap_slots
    key = lax.broadcasted_iota(jnp.int32, (1, per_head), 1)
    see_fresh = (key // steps == row_slot) & (key % steps <= row % steps)
    query = query_ref[mine, :]
    fresh = lax.dot_general(query, fresh_ref[...], contract, preferred_element_type=f32)
    fresh = jnp.where(see_fresh, fresh * scale, masked_score)
    score = lax.dot_general(query, keys[...], contract, preferred_element_type=f32)
    score = jnp.where(
        slot_ref[...] == row_slot + 1, score * scale, masked_score
    )
    top_held = top_ref[mine, :1]
    top = jnp.maximum(
        jnp.maximum(top_held, jnp.max(fresh, axis=1, keepdims=True)),
        jnp.max(score, axis=1, keepdims=True),
    )
    held = jnp.exp(top_held - top)
    weight_fresh = jnp.exp(fresh - top)
    weight = jnp.exp(score - top)
    total = (
        sum_ref[mine, :1] * held
        + jnp.sum(weight_fresh, axis=1, keepdims=True)
        + jnp.sum(weight, axis=1, keepdims=True)
    )
    mix = jnp.dot(
        weight_fresh.astype(bf16), fresh_ref[:, :lat_width], preferred_element_type=f32
    ) + jnp.dot(weight.astype(bf16), keys[:, :lat_width], preferred_element_type=f32)
    mix_held = jnp.concatenate([mix_ref[n, mine, :] for n in range(mix_ref.shape[0])], axis=1)
    latent = ((mix_held * held + mix) / total).astype(bf16)
    live = live_ref[:, :1]
    width = value_ref.shape[2]
    for h in range(0, heads, 2):
        head = part * heads + h
        pair = jnp.concatenate([value_ref[head], value_ref[head + 1]], axis=1)
        both = jnp.dot(
            latent[h * per_head : (h + 2) * per_head, :], pair, preferred_element_type=f32
        )
        out_ref[:, h * width : (h + 1) * width] = (both[:per_head, :width] * live).astype(bf16)
        out_ref[:, (h + 1) * width : (h + 2) * width] = (both[per_head:, width:] * live).astype(bf16)


def attend(scale, query, fresh, row_slot, top, total, mix, live, value, pieces, cap_slots,
           part, parts):
    heads, _, width = value.shape
    steps = fresh.shape[0] // cap_slots
    part_heads = heads // parts
    return pl.pallas_call(
        functools.partial(attend_kernel, scale, cap_slots, steps, part, parts),
        out_shape=jax.ShapeDtypeStruct((cap_slots * steps, part_heads * width), bf16),
        in_specs=[in_vmem] * (8 + len(pieces)),
        out_specs=in_vmem,
        scratch_shapes=[pltpu.VMEM((len(pieces) * pieces[0].shape[0], query.shape[1]), bf16)],
        compiler_params=pltpu.CompilerParams(vmem_limit_bytes=10 * mib),
        name="attend",
    )(query, fresh, row_slot, top, total, mix, live, value, *pieces)


def output_kernel(dev_count, side_count, part, parts, *refs):
    my_dev, my_side = lax.axis_index("dev"), lax.axis_index("side")
    head_refs = refs[:dev_count]
    weight_ref = refs[dev_count]
    earlier_ref = refs[dev_count + 1] if part else None
    out_refs = refs[dev_count + 1 + (part > 0) : -1]
    held = refs[-1]
    rows, depth = head_refs[0].shape
    per_side = dev_count // side_count
    for j in range(dev_count):
        group = my_dev ^ j
        place = (lax.div(group, per_side) ^ my_side) * per_side + lax.rem(group, per_side)
        held[pl.ds(pl.multiple_of(place * rows, 16), rows), :] = head_refs[j][...]
    columns = weight_ref.shape[1]
    tile = 256 if columns % 256 == 0 else columns
    side_rows = rows * per_side
    for n in range(columns // tile):
        here = slice(n * tile, (n + 1) * tile)
        product = jnp.dot(
            held[...], weight_ref[part * depth : (part + 1) * depth, here],
            preferred_element_type=f32,
        )
        if part:
            product = product + earlier_ref[:, here]
        if part + 1 < parts:
            out_refs[0][:, here] = product
        else:
            for k in range(side_count):
                out_refs[k][:, here] = product[k * side_rows : (k + 1) * side_rows, :].astype(
                    out_refs[k].dtype
                )


def output_product(head_pieces, weight, side_count, earlier, part, parts):
    dev_count = len(head_pieces)
    rows, depth = head_pieces[0].shape
    columns = weight.shape[1]
    side_rows = rows * dev_count // side_count
    if part + 1 < parts:
        shapes = [((rows * dev_count, columns), f32)]
    else:
        shapes = [((side_rows, columns), f32 if k == 0 else bf16) for k in range(side_count)]
    earlier = [] if earlier is None else [earlier]
    return pl.pallas_call(
        functools.partial(output_kernel, dev_count, side_count, part, parts),
        out_shape=[jax.ShapeDtypeStruct(*shape) for shape in shapes],
        in_specs=[in_vmem] * (dev_count + 1 + len(earlier)),
        out_specs=[in_vmem] * len(shapes),
        scratch_shapes=[pltpu.VMEM((dev_count * rows, depth), bf16)],
        compiler_params=pltpu.CompilerParams(vmem_limit_bytes=10 * mib),
        name="output_product",
    )(*head_pieces, weight, *earlier)


def on_device(
    prompts,
    latent_weight,
    latent_gain,
    row_request,
    context_len,
    request_slot,
    latent_cache,
    new_latent,
    queries,
    key_absorb,
    value_absorb,
    out_weight,
):
    dev_count = lax.axis_size("dev")
    side_count = lax.axis_size("side")
    tok_rows, model_width = prompts.shape
    shard_rows, kv_width = latent_weight.shape
    lat_width = latent_gain.shape[0]
    head_count, nope_width, _ = key_absorb.shape
    rope_width = kv_width - lat_width
    cap_slots, ctx_len, _ = latent_cache.shape
    step_count = new_latent.shape[1]
    bucket_rows = 2 * tok_rows // dev_count
    group_rows = dev_count * bucket_rows
    slab = model_width // dev_count

    x_pieces = list(split_columns(prompts, dev_count))
    for k in sorted(range(1, dev_count), reverse=True):
        x_pieces[k] = swap(x_pieces[k], "dev", k)

    weights = [None] * side_count
    for k in range(0, side_count, 2):
        weights[k] = swap(latent_weight, "side", k) if k else latent_weight
    for k in range(0, side_count, 2):
        weights[k + 1] = swap(weights[k], "side", 1)
    if shard_rows % 16:
        my_side = lax.axis_index("side")
        held = jnp.zeros((side_count, shard_rows, kv_width), bf16)
        for k in range(side_count):
            held = lax.dynamic_update_slice(held, weights[k][None], (my_side ^ k, 0, 0))
        weights = [held.reshape(slab, kv_width)]

    score_scale = queries.shape[-1] ** (-0.5)
    half = rope_width // 2
    inverse = 1.0 / 10000.0 ** (jnp.arange(half, dtype=f32) * (2.0 / rope_width))
    fresh, lengths = lax.optimization_barrier((new_latent.reshape(-1, kv_width), context_len))
    (
        query_full, top_held, sum_held, mix_held, live, target, cosine, sine, row_slot,
        value_here, out_here,
    ) = prepare(
        score_scale, dev_count, side_count, bucket_rows, lengths, request_slot,
        row_request.reshape(-1, 128), inverse.reshape(1, -1), queries, key_absorb,
        jnp.swapaxes(latent_cache, 1, 2), value_absorb, out_weight,
    )

    routed = project(x_pieces, weights, target, group_rows)
    parts = [routed[0]] + [None] * (dev_count - 1)
    for k in sorted(range(1, dev_count), reverse=True):
        parts[k] = swap(routed[k], "dev", k)
    latent_rows = finish(parts, latent_gain.reshape(1, -1), cosine, sine)
    pieces = [latent_rows] + [swap(latent_rows, "side", k) for k in range(1, side_count)]
    product, parts = None, 2
    for part in range(parts):
        head_out = attend(
            score_scale, query_full, fresh, row_slot, top_held,
            sum_held, mix_held, live, value_here, pieces, cap_slots, part, parts,
        )
        heads = [head_out] + [None] * (dev_count - 1)
        for k in sorted(range(1, dev_count), reverse=True):
            heads[k] = swap(head_out, "dev", k)
        products = output_product(heads, out_here, side_count, product, part, parts)
        product = products[0]
    result = products[0]
    for k in sorted(range(1, side_count), reverse=True):
        result = result + swap(products[k], "side", k).astype(f32)
    return result.astype(bf16)


def solution(mesh):
    placed = (
        P(("rep", "dev", "side"), None),
        P(("dev", "side"), None),
        P(),
        P("rep"),
        P("rep"),
        P("rep"),
        P(("rep", "dev"), None, None),
        P(("rep", "dev"), None, None),
        P(("rep", "dev"), None, "side", None),
        P("side", None, None),
        P("side", None, None),
        P("side", "dev"),
    )
    return jax.shard_map(
        on_device, mesh=mesh, in_specs=placed, out_specs=P(("rep", "side"), "dev"), check_vma=False
    )
```

time: 118 us -> 97.3 us (0.82)
  Pallas kernels: 33.6 us -> 19.4 us
  waiting for transfers between devices: 27.2 us -> 41.2 us
  local copies, waits for them, and re-layouts: 21.4 us -> 10.9 us
  other arithmetic: 6.63 us -> 0.67 us
  matrix products: 4.82 us -> 0 us
    pallas_call x1, Pallas kernels: 22.6 us -> 0.19 us  [split_columns(): pl.pallas_call(functools.partial(split_kernel, slab), out_shape=[jax.Shap...]
    ppermute x18 -> x21, waiting for transfers between devices: 27.2 us -> 41.2 us  [swap(): return lax.ppermute(value, axis, [(i, i ^ step) for i in range(count)])]
    pallas_call x2 -> x5, Pallas kernels: 8.17 us -> 16.7 us  [the longest x1 11.3 us: prepare(): pl.pallas_call(functools.partial(prepare_kernel, scale, steps, (dev_count...]
    dot_general x6 -> x0, matrix products: 4.82 us -> none  [the longest x1 2.98 us: on_device(): jnp.einsum('sthn,hnc->hstc', queries[..., :nope_width], key_absorb, prefe...]
    reshape x3 -> x0, local copies, waits for them, and re-layouts: 4.16 us -> none  [the longest x1 2.14 us: on_device(): query_full.reshape(row_count, kv_width)]
    unnamed x23 -> x20, local copies, waits for them, and re-layouts: 7.49 us -> 10.2 us
    gather x4 -> x0, local copies, waits for them, and re-layouts: 2.27 us -> none  [the longest x3 1.71 us: on_device(): jnp.take(table.reshape(dev_count, side_count, tok_rows), side_order, axis=1)]
    reduce_sum x4 -> x0, other arithmetic: 1.87 us -> none  [the longest x1 1.36 us: on_device(): occupied = (jnp.sum(slot_hit, axis=1) > 0).astype(f32)]
  transfers between devices with their start and end apart: 18 -> 21, of which waited for: 7 -> 10; matrix products, arithmetic and copies ran while one was open for 21% -> 1% of each run, Pallas kernels for 19% -> 15%
where the time goes in v3:
time: 97.3 us; the launch traced here: 96.9 us
  waiting for transfers between devices  41.2 us (42%)
  starting transfers between devices  24.6 us (25%)
  Pallas kernels  19.4 us (20%)
  local copies, waits for them, and re-layouts  10.9 us (11%)
    ppermute x21, waiting for transfers between devices, swap(): return lax.ppermute(value, axis, [(i, i ^ step) for i in range(count)])  41.2 us
    ppermute x21, starting transfers between devices, swap(): return lax.ppermute(value, axis, [(i, i ^ step) for i in range(count)])  24.6 us
    pallas_call x1, Pallas kernels, prepare(): pl.pallas_call(functools.partial(prepare_kernel, scale, steps, (dev_count...  11.3 us
    unnamed x20, local copies, waits for them, and re-layouts  10.2 us
    pallas_call x2, Pallas kernels, output_product(): pl.pallas_call(functools.partial(output_kernel, dev_count, side_count, pa...  2.77 us
    pallas_call x2, Pallas kernels, attend(): pl.pallas_call(functools.partial(attend_kernel, scale, cap_slots, steps,...  2.66 us
    pallas_call x1, Pallas kernels, project(): pl.pallas_call(functools.partial(project_kernel, dev_count, len(weights))...  2.22 us
  transfers between devices with their start and end apart: 21, of which 10 were waited for; matrix products, arithmetic and copies ran while one was open for 1% of the time, Pallas kernels for 15%

profile of v3, /device:TPU:0, one launch (start us, length us, event | category | flops | bytes accessed | tf_op | source)
XLA Modules:
  0.0 96.9 jit_solution(4775393801643717009)
XLA Ops:
  0.0 2.9 %collective-permute-start.4 = (bf16[448,576]{1,0:T(8,128)(2,1)}, bf16[448,576]{1,0:T(8,128)(2,1)S(1)}, u32[]{:S(2)}, u32[]{:S(2)}) collective-permute-start(bf16[448,576]{1,0:T(8,128)(2,1)} %refs_4_.1), channel_id=1, source_target_pairs={{0,2},{1,3},{2,0},{3,1},{4,6},{5,7},{6,4},{7,5},{8,10},{9,11},{10,... | collective-permute-start | bytes 1548296 | tf_op jit(solution)/shard_map/ppermute | solution.py:21
  2.9 0.0 collective-permute-start.3
  2.9 13.2 %collective-permute-done.4.refs_6_ = bf16[448,576]{1,0:T(8,128)(2,1)S(1)} collective-permute-done((bf16[448,576]{1,0:T(8,128)(2,1)}, bf16[448,576]{1,0:T(8,128)(2,1)S(1)}, u32[]{:S(2)}, u32[]{:S(2)}) %collective-permute-start.4) | collective-permute-done | bytes 516128 | tf_op jit(solution)/shard_map/ppermute | solution.py:21
  16.1 1.2 %copy-done.3 = bf16[64,7168]{1,0:T(8,128)(2,1)S(1)} copy-done((bf16[64,7168]{1,0:T(8,128)(2,1)S(1)}, bf16[64,7168]{1,0:T(8,128)(2,1)}, u32[]{:S(2)}) %copy-start.3) | copy-done | bytes 917528
  17.3 0.2 split_columns.1
  17.5 1.9 %collective-permute-start = (bf16[64,1792]{1,0:T(8,128)(2,1)S(1)}, bf16[64,1792]{1,0:T(8,128)(2,1)S(1)}, u32[]{:S(2)}, u32[]{:S(2)}) collective-permute-start(bf16[64,1792]{1,0:T(8,128)(2,1)S(1)} %get-tuple-element.43), channel_id=1, source_target_pairs={{0,4},{4,0},{8,12},{12,8},{1,5},{5,1},{9,13},{13,9},{2,6},{6,2},{1... | collective-permute-start | bytes 688136 | tf_op jit(solution)/shard_map/ppermute | solution.py:21
  19.4 2.6 %collective-permute-start.1 = (bf16[64,1792]{1,0:T(8,128)(2,1)S(1)}, bf16[64,1792]{1,0:T(8,128)(2,1)S(1)}, u32[]{:S(2)}, u32[]{:S(2)}) collective-permute-start(bf16[64,1792]{1,0:T(8,128)(2,1)S(1)} %get-tuple-element.44), channel_id=1, source_target_pairs={{0,8},{4,12},{8,0},{12,4},{1,9},{5,13},{9,1},{13,5},{2,10},{6,14},... | collective-permute-start | bytes 688136 | tf_op jit(solution)/shard_map/ppermute | solution.py:21
  22.0 0.8 reshape.26.fresh_ref
  22.8 0.0 copy-start
  22.8 2.2 %copy-done = bf16[32,128,512]{2,1,0:T(8,128)(2,1)S(1)} copy-done((bf16[32,128,512]{2,1,0:T(8,128)(2,1)S(1)}, bf16[32,128,512]{2,1,0:T(8,128)(2,1)}, u32[]{:S(2)}) %copy-start) | copy-done | bytes 4194328
  25.0 2.2 %copy-done.1 = bf16[32,512,128]{2,1,0:T(8,128)(2,1)S(1)} copy-done((bf16[32,512,128]{2,1,0:T(8,128)(2,1)S(1)}, bf16[32,512,128]{2,1,0:T(8,128)(2,1)}, u32[]{:S(2)}) %copy-start.1) | copy-done | bytes 4194328
  27.1 1.7 %copy-done.2 = bf16[8,256,576]{1,2,0:T(8,128)(2,1)S(1)} copy-done((bf16[8,256,576]{1,2,0:T(8,128)(2,1)S(1)}, bf16[8,256,576]{1,2,0:T(8,128)(2,1)}, u32[]{:S(2)}) %copy-start.2) | copy-done | bytes 2359320
  28.8 0.9 copy-done.5
  29.8 0.7 copy-done.6
  30.4 0.7 copy-done.8
  31.1 0.7 copy-done.9
  31.8 11.3 %prepare.1 = (bf16[512,576]{1,0:T(8,128)(2,1)S(1)}, f32[512,128]{1,0:T(8,128)S(1)}, f32[512,128]{1,0:T(8,128)S(1)}, f32[4,512,128]{2,1,0:T(8,128)S(1)}, f32[16,1...) custom-call(s32[16]{0:T(128)S(1)} %copy-done.8, ...), custom_call_target="tpu_custom_call" | custom-call | flops 4000000000 | bytes 28000000 | tf_op jit(solution)/shard_map/prepare/pallas_call | solution.py:240
  43.1 2.2 %project.1 = (f32[128,576]{1,0:T(8,128)S(1)}, bf16[128,576]{1,0:T(8,128)(2,1)S(1)}, bf16[128,576]{1,0:T(8,128)(2,1)S(1)}, bf16[128,576]{1,0:T(8,128)(2,1)S(1)}) custom-call(s32[1,512]{1,0:T(1,128)S(1)} %get-tuple-element.41.target_ref, bf16[64,1792]{1,0:T(8,128)(2,1)S(1)} %get-tuple-element.42.refs_0_, bf16[64,1792]{1,0:T(8,128)(2,1)S(1)} %collective-permute-done.refs_1_, ...), custom_call_target="tpu_custom_call" | custom-call | tf_op jit(solution)/shard_map/project/pallas_call | solution.py:296
  45.3 1.0 collective-permute-start.6
  46.3 3.5 %collective-permute-start.7 = (bf16[128,576]{1,0:T(8,128)(2,1)S(1)}, bf16[128,576]{1,0:T(8,128)(2,1)S(1)}, u32[]{:S(2)}, u32[]{:S(2)}) collective-permute-start(bf16[128,576]{1,0:T(8,128)(2,1)S(1)} %get-tuple-element.48), channel_id=1, source_target_pairs={{0,8},{4,12},{8,0},{12,4},{1,9},{5,13},{9,1},{13,5},{2,10},{6,14},... | collective-permute-start | bytes 442376 | tf_op jit(solution)/shard_map/ppermute | solution.py:21
  49.8 0.0 collective-permute-start.8
  49.8 4.3 %collective-permute-done.6.refs_1_ = bf16[128,576]{1,0:T(8,128)(2,1)S(1)} collective-permute-done((bf16[128,576]{1,0:T(8,128)(2,1)S(1)}, bf16[128,576]{1,0:T(8,128)(2,1)S(1)}, u32[]{:S(2)}, u32[]{:S(2)}) %collective-permute-start.6) | collective-permute-done | bytes 147488 | tf_op jit(solution)/shard_map/ppermute | solution.py:21
  54.1 7.8 %collective-permute-done.7.refs_2_ = bf16[128,576]{1,0:T(8,128)(2,1)S(1)} collective-permute-done((bf16[128,576]{1,0:T(8,128)(2,1)S(1)}, bf16[128,576]{1,0:T(8,128)(2,1)S(1)}, u32[]{:S(2)}, u32[]{:S(2)}) %collective-permute-start.7) | collective-permute-done | bytes 147488 | tf_op jit(solution)/shard_map/ppermute | solution.py:21
  61.9 0.3 finish_rows.1.refs_0_
  62.2 0.1 collective-permute-start.11
  62.2 1.6 %collective-permute-start.10 = (bf16[128,576]{1,0:T(8,128)(2,1)S(1)}, bf16[128,576]{1,0:T(8,128)(2,1)S(1)}, u32[]{:S(2)}, u32[]{:S(2)}) collective-permute-start(bf16[128,576]{1,0:T(8,128)(2,1)S(1)} %finish_rows.1.refs_0_), channel_id=1, source_target_pairs={{0,2},{1,3},{2,0},{3,1},{4,6},{5,7},{6,4},{7,5},{8,10},{9,11},{10,... | collective-permute-start | bytes 442376 | tf_op jit(solution)/shard_map/ppermute | solution.py:21
  63.8 0.3 collective-permute-start.9
  64.1 4.6 %collective-permute-done.11.refs_3_ = bf16[128,576]{1,0:T(8,128)(2,1)S(1)} collective-permute-done((bf16[128,576]{1,0:T(8,128)(2,1)S(1)}, bf16[128,576]{1,0:T(8,128)(2,1)S(1)}, u32[]{:S(2)}, u32[]{:S(2)}) %collective-permute-start.11) | collective-permute-done | bytes 147488 | tf_op jit(solution)/shard_map/ppermute | solution.py:21
  68.7 3.6 %collective-permute-done.10.refs_2_ = bf16[128,576]{1,0:T(8,128)(2,1)S(1)} collective-permute-done((bf16[128,576]{1,0:T(8,128)(2,1)S(1)}, bf16[128,576]{1,0:T(8,128)(2,1)S(1)}, u32[]{:S(2)}, u32[]{:S(2)}) %collective-permute-start.10) | collective-permute-done | bytes 147488 | tf_op jit(solution)/shard_map/ppermute | solution.py:21
  72.2 1.3 %attend.3.refs_0_ = bf16[16,2048]{1,0:T(8,128)(2,1)S(1)} custom-call(bf16[512,576]{1,0:T(8,128)(2,1)S(1)} %get-tuple-element.31.query_ref, bf16[16,576]{1,0:T(8,128)(2,1)S(1)} %reshape.26.fresh_ref, s32[1,512]{1,0:T(1,128)S(1)} %get-tuple-element.33.slot_ref, f32[512,128]{1,0:T(8,128)S(1)} %get-tuple-element.34.top_ref, ...), custom_call_target="tpu_custom_call" | custom-call | tf_op jit(solution)/shard_map/attend/pallas_call | solution.py:403
  73.6 2.4 %collective-permute-start.17 = (bf16[16,2048]{1,0:T(8,128)(2,1)S(1)}, bf16[16,2048]{1,0:T(8,128)(2,1)S(1)}, u32[]{:S(2)}, u32[]{:S(2)}) collective-permute-start(bf16[16,2048]{1,0:T(8,128)(2,1)S(1)} %attend.3.refs_0_), channel_id=1, source_target_pairs={{0,12},{4,8},{8,4},{12,0},{1,13},{5,9},{9,5},{13,1},{2,14},{6,10},... | collective-permute-start | bytes 196616 | tf_op jit(solution)/shard_map/ppermute | solution.py:21
  76.0 1.9 %collective-permute-start.16 = (bf16[16,2048]{1,0:T(8,128)(2,1)S(1)}, bf16[16,2048]{1,0:T(8,128)(2,1)S(1)}, u32[]{:S(2)}, u32[]{:S(2)}) collective-permute-start(bf16[16,2048]{1,0:T(8,128)(2,1)S(1)} %attend.3.refs_0_), channel_id=1, source_target_pairs={{0,8},{4,12},{8,0},{12,4},{1,9},{5,13},{9,1},{13,5},{2,10},{6,14},... | collective-permute-start | bytes 196616 | tf_op jit(solution)/shard_map/ppermute | solution.py:21
  77.9 0.2 collective-permute-start.15
  78.0 1.3 %attend.2.refs_0_ = bf16[16,2048]{1,0:T(8,128)(2,1)S(1)} custom-call(bf16[512,576]{1,0:T(8,128)(2,1)S(1)} %get-tuple-element.31.query_ref, bf16[16,576]{1,0:T(8,128)(2,1)S(1)} %reshape.26.fresh_ref, s32[1,512]{1,0:T(1,128)S(1)} %get-tuple-element.33.slot_ref, f32[512,128]{1,0:T(8,128)S(1)} %get-tuple-element.34.top_ref, ...), custom_call_target="tpu_custom_call" | custom-call | tf_op jit(solution)/shard_map/attend/pallas_call | solution.py:403
  79.4 2.4 %collective-permute-start.14 = (bf16[16,2048]{1,0:T(8,128)(2,1)S(1)}, bf16[16,2048]{1,0:T(8,128)(2,1)S(1)}, u32[]{:S(2)}, u32[]{:S(2)}) collective-permute-start(bf16[16,2048]{1,0:T(8,128)(2,1)S(1)} %attend.2.refs_0_), channel_id=1, source_target_pairs={{0,12},{4,8},{8,4},{12,0},{1,13},{5,9},{9,5},{13,1},{2,14},{6,10},... | collective-permute-start | bytes 196616 | tf_op jit(solution)/shard_map/ppermute | solution.py:21
  81.8 1.0 %collective-permute-start.13 = (bf16[16,2048]{1,0:T(8,128)(2,1)S(1)}, bf16[16,2048]{1,0:T(8,128)(2,1)S(1)}, u32[]{:S(2)}, u32[]{:S(2)}) collective-permute-start(bf16[16,2048]{1,0:T(8,128)(2,1)S(1)} %attend.2.refs_0_), channel_id=1, source_target_pairs={{0,8},{4,12},{8,0},{12,4},{1,9},{5,13},{9,1},{13,5},{2,10},{6,14},... | collective-permute-start | bytes 196616 | tf_op jit(solution)/shard_map/ppermute | solution.py:21
  82.8 1.1 %collective-permute-start.12 = (bf16[16,2048]{1,0:T(8,128)(2,1)S(1)}, bf16[16,2048]{1,0:T(8,128)(2,1)S(1)}, u32[]{:S(2)}, u32[]{:S(2)}) collective-permute-start(bf16[16,2048]{1,0:T(8,128)(2,1)S(1)} %attend.2.refs_0_), channel_id=1, source_target_pairs={{0,4},{4,0},{8,12},{12,8},{1,5},{5,1},{9,13},{13,9},{2,6},{6,2},{1... | collective-permute-start | bytes 196616 | tf_op jit(solution)/shard_map/ppermute | solution.py:21
  83.8 0.8 collective-permute-done.16.refs_2_
  84.7 1.4 %output_product.2.refs_5_ = f32[64,1792]{1,0:T(8,128)S(1)} custom-call(bf16[16,2048]{1,0:T(8,128)(2,1)S(1)} %attend.3.refs_0_, bf16[16,2048]{1,0:T(8,128)(2,1)S(1)} %collective-permute-done.15.refs_1_, bf16[16,2048]{1,0:T(8,128)(2,1)S(1)} %collective-permute-done.16.refs_2_, bf16[16,2048]{1,0:T(8,128)(2,1)S(1)} %collective-permute-done.17.refs_3_, ...), custom_call_target="tpu_custom_call" | custom-call | tf_op jit(solution)/shard_map/output_product/pallas_call | solution.py:457
  86.0 0.1 collective-permute-done.14.refs_3_
  86.2 3.1 %collective-permute-done.13.refs_2_ = bf16[16,2048]{1,0:T(8,128)(2,1)S(1)} collective-permute-done((bf16[16,2048]{1,0:T(8,128)(2,1)S(1)}, bf16[16,2048]{1,0:T(8,128)(2,1)S(1)}, u32[]{:S(2)}, u32[]{:S(2)}) %collective-permute-start.13) | collective-permute-done | bytes 65568 | tf_op jit(solution)/shard_map/ppermute | solution.py:21
  89.3 1.4 %output_product.3 = (f32[16,1792]{1,0:T(8,128)S(1)}, bf16[16,1792]{1,0:T(8,128)(2,1)S(1)}, bf16[16,1792]{1,0:T(8,128)(2,1)S(1)}, bf16[16,1792]{1,0:T(8,128)(2,1)S(1)}) custom-call(bf16[16,2048]{1,0:T(8,128)(2,1)S(1)} %attend.2.refs_0_, bf16[16,2048]{1,0:T(8,128)(2,1)S(1)} %collective-permute-done.12.refs_1_, ...), custom_call_target="tpu_custom_call" | custom-call | tf_op jit(solution)/shard_map/output_product/pallas_call | solution.py:457
  90.7 0.1 collective-permute-start.18
  90.8 1.5 %collective-permute-start.19 = (bf16[16,1792]{1,0:T(8,128)(2,1)S(1)}, bf16[16,1792]{1,0:T(8,128)(2,1)S(1)}, u32[]{:S(2)}, u32[]{:S(2)}) collective-permute-start(bf16[16,1792]{1,0:T(8,128)(2,1)S(1)} %get-tuple-element.53), channel_id=1, source_target_pairs={{0,2},{1,3},{2,0},{3,1},{4,6},{5,7},{6,4},{7,5},{8,10},{9,11},{10,... | collective-permute-start | bytes 172040 | tf_op jit(solution)/shard_map/ppermute | solution.py:21
  92.3 0.4 collective-permute-start.20
  92.7 2.3 %collective-permute-done.18 = bf16[16,1792]{1,0:T(8,128)(2,1)S(1)} collective-permute-done((bf16[16,1792]{1,0:T(8,128)(2,1)S(1)}, bf16[16,1792]{1,0:T(8,128)(2,1)S(1)}, u32[]{:S(2)}, u32[]{:S(2)}) %collective-permute-start.18) | collective-permute-done | bytes 57376 | tf_op jit(solution)/shard_map/ppermute | solution.py:21
  95.0 1.3 %collective-permute-done.19 = bf16[16,1792]{1,0:T(8,128)(2,1)S(1)} collective-permute-done((bf16[16,1792]{1,0:T(8,128)(2,1)S(1)}, bf16[16,1792]{1,0:T(8,128)(2,1)S(1)}, u32[]{:S(2)}, u32[]{:S(2)}) %collective-permute-start.19) | collective-permute-done | bytes 57376 | tf_op jit(solution)/shard_map/ppermute | solution.py:21
  96.3 0.7 add_convert_fusion
  (25 shorter events, 0.1 us)
Async XLA Ops:
  0.0 16.1 %collective-permute-start.4 = (bf16[448,576]{1,0:T(8,128)(2,1)}, bf16[448,576]{1,0:T(8,128)(2,1)S(1)}, u32[]{:S(2)}, u32[]{:S(2)}) collective-permute-start(bf16[448,576]{1,0:T(8,128)(2,1)} %refs_4_.1), channel_id=1, source_target_pairs={{0,2},{1,3},{2,0},{3,1},{4,6},{5,7},{6,4},{7,5},{8,10},{9,11},{10,... | collective-permute-start | bytes 1548296 | tf_op jit(solution)/shard_map/ppermute | solution.py:21
  2.9 40.1 %collective-permute-start.3 = (bf16[448,576]{1,0:T(8,128)(2,1)}, bf16[448,576]{1,0:T(8,128)(2,1)S(1)}, u32[]{:S(2)}, u32[]{:S(2)}) collective-permute-start(bf16[448,576]{1,0:T(8,128)(2,1)} %refs_4_.1), channel_id=1, source_target_pairs={{0,1},{1,0},{2,3},{3,2},{4,5},{5,4},{6,7},{7,6},{8,9},{9,8},{10,11... | collective-permute-start | bytes 1548296 | tf_op jit(solution)/shard_map/ppermute | solution.py:21
  16.1 27.0 %collective-permute-start.5 = (bf16[448,576]{1,0:T(8,128)(2,1)S(1)}, bf16[448,576]{1,0:T(8,128)(2,1)S(1)}, u32[]{:S(2)}, u32[]{:S(2)}) collective-permute-start(bf16[448,576]{1,0:T(8,128)(2,1)S(1)} %collective-permute-done.4.refs_6_), channel_id=1, source_target_pairs={{0,1},{1,0},{2,3},{3,2},{4,5},{5,4},{6,7},{7,6},{8,9},{9,8},{10,11... | collective-permute-start | bytes 1548296 | tf_op jit(solution)/shard_map/ppermute | solution.py:21
  16.1 1.2 %copy-start.3 = (bf16[64,7168]{1,0:T(8,128)(2,1)S(1)}, bf16[64,7168]{1,0:T(8,128)(2,1)}, u32[]{:S(2)}) copy-start(bf16[64,7168]{1,0:T(8,128)(2,1)} %prompts_ref.1) | copy-start | bytes 2752516
  17.5 25.5 %collective-permute-start = (bf16[64,1792]{1,0:T(8,128)(2,1)S(1)}, bf16[64,1792]{1,0:T(8,128)(2,1)S(1)}, u32[]{:S(2)}, u32[]{:S(2)}) collective-permute-start(bf16[64,1792]{1,0:T(8,128)(2,1)S(1)} %get-tuple-element.43), channel_id=1, source_target_pairs={{0,4},{4,0},{8,12},{12,8},{1,5},{5,1},{9,13},{13,9},{2,6},{6,2},{1... | collective-permute-start | bytes 688136 | tf_op jit(solution)/shard_map/ppermute | solution.py:21
  19.4 23.7 %collective-permute-start.1 = (bf16[64,1792]{1,0:T(8,128)(2,1)S(1)}, bf16[64,1792]{1,0:T(8,128)(2,1)S(1)}, u32[]{:S(2)}, u32[]{:S(2)}) collective-permute-start(bf16[64,1792]{1,0:T(8,128)(2,1)S(1)} %get-tuple-element.44), channel_id=1, source_target_pairs={{0,8},{4,12},{8,0},{12,4},{1,9},{5,13},{9,1},{13,5},{2,10},{6,14},... | collective-permute-start | bytes 688136 | tf_op jit(solution)/shard_map/ppermute | solution.py:21
  22.0 21.1 %collective-permute-start.2 = (bf16[64,1792]{1,0:T(8,128)(2,1)S(1)}, bf16[64,1792]{1,0:T(8,128)(2,1)S(1)}, u32[]{:S(2)}, u32[]{:S(2)}) collective-permute-start(bf16[64,1792]{1,0:T(8,128)(2,1)S(1)} %get-tuple-element.45), channel_id=1, source_target_pairs={{0,12},{4,8},{8,4},{12,0},{1,13},{5,9},{9,5},{13,1},{2,14},{6,10},... | collective-permute-start | bytes 688136 | tf_op jit(solution)/shard_map/ppermute | solution.py:21
  22.8 2.2 %copy-start = (bf16[32,128,512]{2,1,0:T(8,128)(2,1)S(1)}, bf16[32,128,512]{2,1,0:T(8,128)(2,1)}, u32[]{:S(2)}) copy-start(bf16[32,128,512]{2,1,0:T(8,128)(2,1)} %absorb_ref.1) | copy-start | bytes 12582916
  25.0 2.2 %copy-start.1 = (bf16[32,512,128]{2,1,0:T(8,128)(2,1)S(1)}, bf16[32,512,128]{2,1,0:T(8,128)(2,1)}, u32[]{:S(2)}) copy-start(bf16[32,512,128]{2,1,0:T(8,128)(2,1)} %value_hbm.1) | copy-start | bytes 12582916
  27.1 1.7 %copy-start.2 = (bf16[8,256,576]{1,2,0:T(8,128)(2,1)S(1)}, bf16[8,256,576]{1,2,0:T(8,128)(2,1)}, u32[]{:S(2)}) copy-start(bf16[8,256,576]{1,2,0:T(8,128)(2,1)} %param.18) | copy-start | bytes 7077892
  28.8 0.9 copy-start.5
  29.8 0.7 copy-start.6
  30.4 0.7 copy-start.8
  31.1 0.7 copy-start.9
  31.8 11.3 %copy-start.4 = (bf16[448,576]{1,0:T(8,128)(2,1)S(1)}, bf16[448,576]{1,0:T(8,128)(2,1)}, u32[]{:S(2)}) copy-start(bf16[448,576]{1,0:T(8,128)(2,1)} %refs_4_.1) | copy-start | bytes 1548292
  31.8 30.1 %copy-start.7 = (f32[512]{0:T(512)S(1)}, f32[512]{0:T(512)}, u32[]{:S(2)}) copy-start(f32[512]{0:T(512)} %param.14) | copy-start | bytes 6148
  45.3 8.8 %collective-permute-start.6 = (bf16[128,576]{1,0:T(8,128)(2,1)S(1)}, bf16[128,576]{1,0:T(8,128)(2,1)S(1)}, u32[]{:S(2)}, u32[]{:S(2)}) collective-permute-start(bf16[128,576]{1,0:T(8,128)(2,1)S(1)} %get-tuple-element.47), channel_id=1, source_target_pairs={{0,4},{4,0},{8,12},{12,8},{1,5},{5,1},{9,13},{13,9},{2,6},{6,2},{1... | collective-permute-start | bytes 442376 | tf_op jit(solution)/shard_map/ppermute | solution.py:21
  46.3 15.6 %collective-permute-start.7 = (bf16[128,576]{1,0:T(8,128)(2,1)S(1)}, bf16[128,576]{1,0:T(8,128)(2,1)S(1)}, u32[]{:S(2)}, u32[]{:S(2)}) collective-permute-start(bf16[128,576]{1,0:T(8,128)(2,1)S(1)} %get-tuple-element.48), channel_id=1, source_target_pairs={{0,8},{4,12},{8,0},{12,4},{1,9},{5,13},{9,1},{13,5},{2,10},{6,14},... | collective-permute-start | bytes 442376 | tf_op jit(solution)/shard_map/ppermute | solution.py:21
  49.8 12.1 %collective-permute-start.8 = (bf16[128,576]{1,0:T(8,128)(2,1)S(1)}, bf16[128,576]{1,0:T(8,128)(2,1)S(1)}, u32[]{:S(2)}, u32[]{:S(2)}) collective-permute-start(bf16[128,576]{1,0:T(8,128)(2,1)S(1)} %get-tuple-element.49), channel_id=1, source_target_pairs={{0,12},{4,8},{8,4},{12,0},{1,13},{5,9},{9,5},{13,1},{2,14},{6,10},... | collective-permute-start | bytes 442376 | tf_op jit(solution)/shard_map/ppermute | solution.py:21
  62.2 6.5 %collective-permute-start.11 = (bf16[128,576]{1,0:T(8,128)(2,1)S(1)}, bf16[128,576]{1,0:T(8,128)(2,1)S(1)}, u32[]{:S(2)}, u32[]{:S(2)}) collective-permute-start(bf16[128,576]{1,0:T(8,128)(2,1)S(1)} %finish_rows.1.refs_0_), channel_id=1, source_target_pairs={{0,3},{1,2},{2,1},{3,0},{4,7},{5,6},{6,5},{7,4},{8,11},{9,10},{10,... | collective-permute-start | bytes 442376 | tf_op jit(solution)/shard_map/ppermute | solution.py:21
  62.2 10.0 %collective-permute-start.10 = (bf16[128,576]{1,0:T(8,128)(2,1)S(1)}, bf16[128,576]{1,0:T(8,128)(2,1)S(1)}, u32[]{:S(2)}, u32[]{:S(2)}) collective-permute-start(bf16[128,576]{1,0:T(8,128)(2,1)S(1)} %finish_rows.1.refs_0_), channel_id=1, source_target_pairs={{0,2},{1,3},{2,0},{3,1},{4,6},{5,7},{6,4},{7,5},{8,10},{9,11},{10,... | collective-permute-start | bytes 442376 | tf_op jit(solution)/shard_map/ppermute | solution.py:21
  63.8 8.4 %collective-permute-start.9 = (bf16[128,576]{1,0:T(8,128)(2,1)S(1)}, bf16[128,576]{1,0:T(8,128)(2,1)S(1)}, u32[]{:S(2)}, u32[]{:S(2)}) collective-permute-start(bf16[128,576]{1,0:T(8,128)(2,1)S(1)} %finish_rows.1.refs_0_), channel_id=1, source_target_pairs={{0,1},{1,0},{2,3},{3,2},{4,5},{5,4},{6,7},{7,6},{8,9},{9,8},{10,11... | collective-permute-start | bytes 442376 | tf_op jit(solution)/shard_map/ppermute | solution.py:21
  73.6 9.2 %collective-permute-start.17 = (bf16[16,2048]{1,0:T(8,128)(2,1)S(1)}, bf16[16,2048]{1,0:T(8,128)(2,1)S(1)}, u32[]{:S(2)}, u32[]{:S(2)}) collective-permute-start(bf16[16,2048]{1,0:T(8,128)(2,1)S(1)} %attend.3.refs_0_), channel_id=1, source_target_pairs={{0,12},{4,8},{8,4},{12,0},{1,13},{5,9},{9,5},{13,1},{2,14},{6,10},... | collective-permute-start | bytes 196616 | tf_op jit(solution)/shard_map/ppermute | solution.py:21
  76.0 8.6 %collective-permute-start.16 = (bf16[16,2048]{1,0:T(8,128)(2,1)S(1)}, bf16[16,2048]{1,0:T(8,128)(2,1)S(1)}, u32[]{:S(2)}, u32[]{:S(2)}) collective-permute-start(bf16[16,2048]{1,0:T(8,128)(2,1)S(1)} %attend.3.refs_0_), channel_id=1, source_target_pairs={{0,8},{4,12},{8,0},{12,4},{1,9},{5,13},{9,1},{13,5},{2,10},{6,14},... | collective-permute-start | bytes 196616 | tf_op jit(solution)/shard_map/ppermute | solution.py:21
  77.9 6.8 %collective-permute-start.15 = (bf16[16,2048]{1,0:T(8,128)(2,1)S(1)}, bf16[16,2048]{1,0:T(8,128)(2,1)S(1)}, u32[]{:S(2)}, u32[]{:S(2)}) collective-permute-start(bf16[16,2048]{1,0:T(8,128)(2,1)S(1)} %attend.3.refs_0_), channel_id=1, source_target_pairs={{0,4},{4,0},{8,12},{12,8},{1,5},{5,1},{9,13},{13,9},{2,6},{6,2},{1... | collective-permute-start | bytes 196616 | tf_op jit(solution)/shard_map/ppermute | solution.py:21
  79.4 6.8 %collective-permute-start.14 = (bf16[16,2048]{1,0:T(8,128)(2,1)S(1)}, bf16[16,2048]{1,0:T(8,128)(2,1)S(1)}, u32[]{:S(2)}, u32[]{:S(2)}) collective-permute-start(bf16[16,2048]{1,0:T(8,128)(2,1)S(1)} %attend.2.refs_0_), channel_id=1, source_target_pairs={{0,12},{4,8},{8,4},{12,0},{1,13},{5,9},{9,5},{13,1},{2,14},{6,10},... | collective-permute-start | bytes 196616 | tf_op jit(solution)/shard_map/ppermute | solution.py:21
  81.8 7.5 %collective-permute-start.13 = (bf16[16,2048]{1,0:T(8,128)(2,1)S(1)}, bf16[16,2048]{1,0:T(8,128)(2,1)S(1)}, u32[]{:S(2)}, u32[]{:S(2)}) collective-permute-start(bf16[16,2048]{1,0:T(8,128)(2,1)S(1)} %attend.2.refs_0_), channel_id=1, source_target_pairs={{0,8},{4,12},{8,0},{12,4},{1,9},{5,13},{9,1},{13,5},{2,10},{6,14},... | collective-permute-start | bytes 196616 | tf_op jit(solution)/shard_map/ppermute | solution.py:21
  82.8 6.6 %collective-permute-start.12 = (bf16[16,2048]{1,0:T(8,128)(2,1)S(1)}, bf16[16,2048]{1,0:T(8,128)(2,1)S(1)}, u32[]{:S(2)}, u32[]{:S(2)}) collective-permute-start(bf16[16,2048]{1,0:T(8,128)(2,1)S(1)} %attend.2.refs_0_), channel_id=1, source_target_pairs={{0,4},{4,0},{8,12},{12,8},{1,5},{5,1},{9,13},{13,9},{2,6},{6,2},{1... | collective-permute-start | bytes 196616 | tf_op jit(solution)/shard_map/ppermute | solution.py:21
  90.7 4.2 %collective-permute-start.18 = (bf16[16,1792]{1,0:T(8,128)(2,1)S(1)}, bf16[16,1792]{1,0:T(8,128)(2,1)S(1)}, u32[]{:S(2)}, u32[]{:S(2)}) collective-permute-start(bf16[16,1792]{1,0:T(8,128)(2,1)S(1)} %get-tuple-element.52), channel_id=1, source_target_pairs={{0,3},{1,2},{2,1},{3,0},{4,7},{5,6},{6,5},{7,4},{8,11},{9,10},{10,... | collective-permute-start | bytes 172040 | tf_op jit(solution)/shard_map/ppermute | solution.py:21
  90.8 5.4 %collective-permute-start.19 = (bf16[16,1792]{1,0:T(8,128)(2,1)S(1)}, bf16[16,1792]{1,0:T(8,128)(2,1)S(1)}, u32[]{:S(2)}, u32[]{:S(2)}) collective-permute-start(bf16[16,1792]{1,0:T(8,128)(2,1)S(1)} %get-tuple-element.53), channel_id=1, source_target_pairs={{0,2},{1,3},{2,0},{3,1},{4,6},{5,7},{6,4},{7,5},{8,10},{9,11},{10,... | collective-permute-start | bytes 172040 | tf_op jit(solution)/shard_map/ppermute | solution.py:21
  92.3 4.0 %collective-permute-start.20 = (bf16[16,1792]{1,0:T(8,128)(2,1)S(1)}, bf16[16,1792]{1,0:T(8,128)(2,1)S(1)}, u32[]{:S(2)}, u32[]{:S(2)}) collective-permute-start(bf16[16,1792]{1,0:T(8,128)(2,1)S(1)} %get-tuple-element.54), channel_id=1, source_target_pairs={{0,1},{1,0},{2,3},{3,2},{4,5},{5,4},{6,7},{7,6},{8,9},{9,8},{10,11... | collective-permute-start | bytes 172040 | tf_op jit(solution)/shard_map/ppermute | solution.py:21

commit v4 on v3

--- a/solution.py
+++ b/solution.py
@@ -11,9 +11,9 @@
 bf16, f32 = jnp.bfloat16, jnp.float32
 in_vmem = pl.BlockSpec(memory_space=pltpu.VMEM)
 in_smem = pl.BlockSpec(memory_space=pltpu.SMEM)
-anywhere = pl.BlockSpec(memory_space=pl.ANY)
+in_hbm = pl.BlockSpec(memory_space=pltpu.HBM)
 mib = 1024 * 1024
-prepare_mib = 10
+prepare_mib = 16
 
 
 def swap(value, axis, step):
@@ -57,7 +57,7 @@
     return pl.pallas_call(
         functools.partial(split_kernel, slab),
         out_shape=[jax.ShapeDtypeStruct((rows, slab), prompts.dtype)] * count,
-        in_specs=[anywhere],
+        in_specs=[in_hbm],
         out_specs=[in_vmem] * count,
         scratch_shapes=[pltpu.SemaphoreType.DMA((count,))],
         compiler_params=pltpu.CompilerParams(vmem_limit_bytes=8 * mib),
@@ -140,19 +140,26 @@
 
 
 def prepare_kernel(
-    scale, steps, layout, length_ref, slot_ref, request_ref, inverse_ref, query_ref, absorb_ref,
-    cache_ref, value_hbm, out_hbm, full_ref, top_ref, sum_ref, mix_ref, live_ref, target_ref,
-    cos_ref, sin_ref, spot_ref, value_ref, out_ref, plain, full, to_ref, place_ref, local_ref,
-    position_ref, sems,
+    scale, steps, layout, inverse_ref, length_hbm, slot_hbm, request_hbm, query_hbm, absorb_hbm,
+    cache_hbm, value_hbm, out_hbm, full_ref, top_ref, sum_ref, mix_ref, live_ref, target_ref,
+    cos_ref, sin_ref, spot_ref, value_ref, out_ref, length_ref, slot_ref, request_ref, query_ref,
+    absorb_ref, cache_ref, plain, full, to_ref, place_ref, local_ref, position_ref, sems,
 ):
-    copies = [pltpu.make_async_copy(value_hbm, value_ref, sems.at[0])]
-    parts = sems.shape[0] - 1
+    pairs = [
+        (length_hbm, length_ref), (slot_hbm, slot_ref), (request_hbm, request_ref),
+        (query_hbm, query_ref), (absorb_hbm, absorb_ref), (cache_hbm, cache_ref),
+        (value_hbm, value_ref),
+    ]
+    parts = sems.shape[0] - len(pairs)
     rows = out_hbm.shape[0] // parts
     for n in range(parts):
         part = pl.ds(n * rows, rows)
-        copies.append(pltpu.make_async_copy(out_hbm.at[part], out_ref.at[part], sems.at[n + 1]))
+        pairs.append((out_hbm.at[part], out_ref.at[part]))
+    copies = [pltpu.make_async_copy(*pair, sems.at[n]) for n, pair in enumerate(pairs)]
     for copy in copies:
         copy.start()
+    for copy in copies[:3]:
+        copy.wait()
     slots, _, context = cache_ref.shape
     heads, nope, lat_width = absorb_ref.shape
     per_head = slots * steps
@@ -172,6 +179,8 @@
     for s in range(slots):
         live = jnp.where((slot_of == s) & (lengths[s] > 0), 1.0, live)
     live_ref[...] = live
+    copies[3].wait()
+    copies[4].wait()
     for n, here in enumerate(lane_tiles(query_ref.shape[1])):
         plain[n, :, : here.stop - here.start] = query_ref[:, here].astype(f32)
     wide = lane_tiles(full_ref.shape[1])
@@ -186,6 +195,7 @@
     for n, lanes in enumerate(wide):
         full_ref[:, lanes] = full[n, :, : lanes.stop - lanes.start].astype(bf16)
     key = lax.broadcasted_iota(jnp.int32, (1, context), 1)
+    copies[5].wait()
     for s in range(slots):
         theres = [pl.ds(s * steps + t, heads, stride=per_head) for t in range(steps)]
         query = jnp.concatenate(
@@ -215,7 +225,7 @@
             sum_ref[there, :] = jnp.broadcast_to(total[here], (heads, lanes))
             for n, part in enumerate(lane_tiles(lat_width)):
                 mix_ref[n, there, :] = mix[here, part]
-    for copy in copies:
+    for copy in copies[6:]:
         copy.wait()
 
 
@@ -240,23 +250,29 @@
     return pl.pallas_call(
         functools.partial(prepare_kernel, scale, steps, (dev_count, side_count, bucket)),
         out_shape=[jax.ShapeDtypeStruct(*shape) for shape in shapes],
-        in_specs=[in_smem] * 2 + [in_vmem] * 5 + [anywhere] * 2,
+        in_specs=[in_vmem] + [in_hbm] * 8,
         out_specs=[in_vmem] * len(shapes),
         scratch_shapes=[
+            pltpu.SMEM(lengths.shape, lengths.dtype),
+            pltpu.SMEM(request_slot.shape, request_slot.dtype),
+            pltpu.VMEM(requests.shape, requests.dtype),
+            pltpu.VMEM((rows, width), queries.dtype),
+            pltpu.VMEM(absorb.shape, absorb.dtype),
+            pltpu.VMEM(cache.shape, cache.dtype),
             pltpu.VMEM((len(lane_tiles(width)), rows, 128), f32),
             pltpu.VMEM((len(lane_tiles(kv_width)), rows, 128), f32),
             pltpu.VMEM(requests.shape, jnp.int32),
             pltpu.VMEM(requests.shape, jnp.int32),
             pltpu.VMEM(requests.shape, f32),
             pltpu.VMEM(requests.shape, f32),
-            pltpu.SemaphoreType.DMA((parts + 1,)),
+            pltpu.SemaphoreType.DMA((parts + 7,)),
         ],
         compiler_params=pltpu.CompilerParams(vmem_limit_bytes=prepare_mib * mib),
         cost_estimate=pl.CostEstimate(
             flops=4 * 10**9, bytes_accessed=28 * 10**6, transcendentals=10**5
         ),
         name="prepare",
-    )(lengths, request_slot, requests, inverse, queries.reshape(rows, width), absorb, cache, value,
+    )(inverse, lengths, request_slot, requests, queries.reshape(rows, width), absorb, cache, value,
       out_weight)
 
 
@@ -264,22 +280,22 @@
     my_side = lax.axis_index("side")
     x_refs = refs[:dev_count]
     weight_refs = refs[dev_count : dev_count + side_count]
-    out_refs = refs[dev_count + side_count : -2]
-    slab_weight, rows = refs[-2:]
+    out_refs = refs[dev_count + side_count : -3]
+    x_rows, slab_weight, rows = refs[-3:]
     shard = weight_refs[0].shape[0]
     tok_rows = x_refs[0].shape[0]
     if side_count > 1:
         for k in range(side_count):
             first = pl.multiple_of((my_side ^ k) * shard, 16)
             slab_weight[pl.ds(first, shard), :] = weight_refs[k][...]
+    for k in range(dev_count):
+        x_rows[k * tok_rows : (k + 1) * tok_rows, :] = x_refs[k][...]
+    slab = slab_weight[...] if side_count > 1 else weight_refs[0][...]
+    raw = jnp.dot(x_rows[...], slab, preferred_element_type=f32).astype(bf16)
     copies = target_ref.shape[1] // (dev_count * tok_rows)
     for k in range(dev_count):
-        part = jnp.dot(
-            x_refs[k][...], slab_weight[...] if side_count > 1 else weight_refs[0][...],
-            preferred_element_type=f32,
-        ).astype(bf16)
         for n in range(k * copies, (k + 1) * copies):
-            rows[n * tok_rows : (n + 1) * tok_rows, :] = part
+            rows[n * tok_rows : (n + 1) * tok_rows, :] = raw[k * tok_rows : (k + 1) * tok_rows, :]
     group_rows = out_refs[0].shape[0]
     target = target_ref[...]
     for j in range(dev_count):
@@ -302,6 +318,7 @@
         in_specs=[in_vmem] * (1 + dev_count + len(weights)),
         out_specs=[in_vmem] * dev_count,
         scratch_shapes=[
+            pltpu.VMEM((dev_count * tok_rows, slab), bf16),
             pltpu.VMEM((slab, width), bf16),
             pltpu.VMEM((target.shape[1], width), bf16),
         ],
@@ -493,25 +510,20 @@
     slab = model_width // dev_count
 
     x_pieces = list(split_columns(prompts, dev_count))
-    for k in sorted(range(1, dev_count), reverse=True):
+    weights = [latent_weight] + [None] * (side_count - 1)
+    for k in sorted(range(2, dev_count), reverse=True):
         x_pieces[k] = swap(x_pieces[k], "dev", k)
-
-    weights = [None] * side_count
-    for k in range(0, side_count, 2):
-        weights[k] = swap(latent_weight, "side", k) if k else latent_weight
-    for k in range(0, side_count, 2):
-        weights[k + 1] = swap(weights[k], "side", 1)
-    if shard_rows % 16:
-        my_side = lax.axis_index("side")
-        held = jnp.zeros((side_count, shard_rows, kv_width), bf16)
-        for k in range(side_count):
-            held = lax.dynamic_update_slice(held, weights[k][None], (my_side ^ k, 0, 0))
-        weights = [held.reshape(slab, kv_width)]
+    for k in range(1, side_count):
+        weights[k] = swap(latent_weight, "side", k)
+    x_pieces[1], weights[1] = lax.optimization_barrier((x_pieces[1], weights[1]))
+    x_pieces[1] = swap(x_pieces[1], "dev", 1)
 
     score_scale = queries.shape[-1] ** (-0.5)
     half = rope_width // 2
     inverse = 1.0 / 10000.0 ** (jnp.arange(half, dtype=f32) * (2.0 / rope_width))
-    fresh, lengths = lax.optimization_barrier((new_latent.reshape(-1, kv_width), context_len))
+    fresh, lengths, x_pieces[0] = lax.optimization_barrier(
+        (new_latent.reshape(-1, kv_width), context_len, x_pieces[0])
+    )
     (
         query_full, top_held, sum_held, mix_held, live, target, cosine, sine, row_slot,
         value_here, out_here,
@@ -520,6 +532,13 @@
         row_request.reshape(-1, 128), inverse.reshape(1, -1), queries, key_absorb,
         jnp.swapaxes(latent_cache, 1, 2), value_absorb, out_weight,
     )
+
+    if shard_rows % 16:
+        my_side = lax.axis_index("side")
+        held = jnp.zeros((side_count, shard_rows, kv_width), bf16)
+        for k in range(side_count):
+            held = lax.dynamic_update_slice(held, weights[k][None], (my_side ^ k, 0, 0))
+        weights = [held.reshape(slab, kv_width)]
 
     routed = project(x_pieces, weights, target, group_rows)
     parts = [routed[0]] + [None] * (dev_count - 1)

time: 97.3 us -> 82.6 us (0.85)
  waiting for transfers between devices: 41.2 us -> 31.1 us
  Pallas kernels: 19.4 us -> 14.3 us
    ppermute x21, waiting for transfers between devices: 41.2 us -> 31.1 us  [swap(): return lax.ppermute(value, axis, [(i, i ^ step) for i in range(count)])]
    pallas_call x1, Pallas kernels: 11.3 us -> 6.87 us  [prepare(): pl.pallas_call(functools.partial(prepare_kernel, scale, steps, (dev_count...]
  transfers between devices with their start and end apart: 21 -> 21, of which waited for: 10 -> 10; matrix products, arithmetic and copies ran while one was open for 1% -> 1% of each run, Pallas kernels for 15% -> 12%
where the time goes in v4:
time: 82.6 us; the launch traced here: 82.2 us
  waiting for transfers between devices  31.1 us (38%)
  starting transfers between devices  25.1 us (30%)
  Pallas kernels  14.3 us (17%)
  local copies, waits for them, and re-layouts  10.9 us (13%)
    ppermute x21, waiting for transfers between devices, swap(): return lax.ppermute(value, axis, [(i, i ^ step) for i in range(count)])  31.1 us
    ppermute x21, starting transfers between devices, swap(): return lax.ppermute(value, axis, [(i, i ^ step) for i in range(count)])  25.1 us
    unnamed x20, local copies, waits for them, and re-layouts  10.2 us
    pallas_call x1, Pallas kernels, prepare(): pl.pallas_call(functools.partial(prepare_kernel, scale, steps, (dev_count...  6.87 us
    pallas_call x2, Pallas kernels, output_product(): pl.pallas_call(functools.partial(output_kernel, dev_count, side_count, pa...  2.77 us
    pallas_call x2, Pallas kernels, attend(): pl.pallas_call(functools.partial(attend_kernel, scale, cap_slots, steps,...  2.66 us
  transfers between devices with their start and end apart: 21, of which 10 were waited for; matrix products, arithmetic and copies ran while one was open for 1% of the time, Pallas kernels for 12%

profile of v4, /device:TPU:0, one launch (start us, length us, event | category | flops | bytes accessed | tf_op | source)
XLA Modules:
  0.0 82.2 jit_solution(12838508882499140292)
XLA Ops:
  0.0 0.5 collective-permute-start
  0.5 2.5 %collective-permute-start.4 = (bf16[448,576]{1,0:T(8,128)(2,1)}, bf16[448,576]{1,0:T(8,128)(2,1)S(1)}, u32[]{:S(2)}, u32[]{:S(2)}) collective-permute-start(bf16[448,576]{1,0:T(8,128)(2,1)} %refs_4_.1), channel_id=1, source_target_pairs={{0,2},{1,3},{2,0},{3,1},{4,6},{5,7},{6,4},{7,5},{8,10},{9,11},{10,... | collective-permute-start | bytes 1548296 | tf_op jit(solution)/shard_map/ppermute | solution.py:21
  2.9 0.1 collective-permute-start.5
  3.1 1.2 %copy-done.3 = bf16[64,7168]{1,0:T(8,128)(2,1)S(1)} copy-done((bf16[64,7168]{1,0:T(8,128)(2,1)S(1)}, bf16[64,7168]{1,0:T(8,128)(2,1)}, u32[]{:S(2)}) %copy-start.3) | copy-done | bytes 917528
  4.3 0.2 split_columns.1
  4.5 2.9 %collective-permute-start.2 = (bf16[64,1792]{1,0:T(8,128)(2,1)S(1)}, bf16[64,1792]{1,0:T(8,128)(2,1)S(1)}, u32[]{:S(2)}, u32[]{:S(2)}) collective-permute-start(bf16[64,1792]{1,0:T(8,128)(2,1)S(1)} %get-tuple-element.49), channel_id=1, source_target_pairs={{0,8},{4,12},{8,0},{12,4},{1,9},{5,13},{9,1},{13,5},{2,10},{6,14},... | collective-permute-start | bytes 688136 | tf_op jit(solution)/shard_map/ppermute | solution.py:21
  7.3 1.3 %collective-permute-start.3 = (bf16[64,1792]{1,0:T(8,128)(2,1)S(1)}, bf16[64,1792]{1,0:T(8,128)(2,1)S(1)}, u32[]{:S(2)}, u32[]{:S(2)}) collective-permute-start(bf16[64,1792]{1,0:T(8,128)(2,1)S(1)} %get-tuple-element.50), channel_id=1, source_target_pairs={{0,12},{4,8},{8,4},{12,0},{1,13},{5,9},{9,5},{13,1},{2,14},{6,10},... | collective-permute-start | bytes 688136 | tf_op jit(solution)/shard_map/ppermute | solution.py:21
  8.7 0.8 reshape.26.fresh_ref
  9.5 0.3 collective-permute-start.1
  9.8 2.2 %copy-done = bf16[32,128,512]{2,1,0:T(8,128)(2,1)S(1)} copy-done((bf16[32,128,512]{2,1,0:T(8,128)(2,1)S(1)}, bf16[32,128,512]{2,1,0:T(8,128)(2,1)}, u32[]{:S(2)}) %copy-start) | copy-done | bytes 4194328
  12.0 2.2 %copy-done.1 = bf16[32,512,128]{2,1,0:T(8,128)(2,1)S(1)} copy-done((bf16[32,512,128]{2,1,0:T(8,128)(2,1)S(1)}, bf16[32,512,128]{2,1,0:T(8,128)(2,1)}, u32[]{:S(2)}) %copy-start.1) | copy-done | bytes 4194328
  14.1 1.7 %copy-done.2 = bf16[8,256,576]{1,2,0:T(8,128)(2,1)S(1)} copy-done((bf16[8,256,576]{1,2,0:T(8,128)(2,1)S(1)}, bf16[8,256,576]{1,2,0:T(8,128)(2,1)}, u32[]{:S(2)}) %copy-start.2) | copy-done | bytes 2359320
  15.8 0.9 %copy-done.5 = bf16[8,2,32,192]{3,2,1,0:T(8,128)(2,1)S(1)} copy-done((bf16[8,2,32,192]{3,2,1,0:T(8,128)(2,1)S(1)}, bf16[8,2,32,192]{3,2,1,0:T(8,128)(2,1)}, u32[]{:S(2)}) %copy-start.5) | copy-done | bytes 196632
  16.8 0.7 copy-done.6
  17.4 0.7 copy-done.8
  18.1 0.7 copy-done.9
  18.8 6.9 %prepare.1 = (bf16[512,576]{1,0:T(8,128)(2,1)S(1)}, f32[512,128]{1,0:T(8,128)S(1)}, f32[512,128]{1,0:T(8,128)S(1)}, f32[4,512,128]{2,1,0:T(8,128)S(1)}, f32[16,1...) custom-call(f32[1,32]{1,0:T(1,128)S(1)} %negate_power_fusion.inverse, ...), custom_call_target="tpu_custom_call" | custom-call | flops 4000000000 | bytes 28000000 | tf_op jit(solution)/shard_map/prepare/pallas_call | solution.py:250
  25.7 3.2 %collective-permute-done.5.refs_7_ = bf16[448,576]{1,0:T(8,128)(2,1)S(1)} collective-permute-done((bf16[448,576]{1,0:T(8,128)(2,1)}, bf16[448,576]{1,0:T(8,128)(2,1)S(1)}, u32[]{:S(2)}, u32[]{:S(2)}) %collective-permute-start.5) | collective-permute-done | bytes 516128 | tf_op jit(solution)/shard_map/ppermute | solution.py:21
  28.9 1.6 %project.1 = (f32[128,576]{1,0:T(8,128)S(1)}, bf16[128,576]{1,0:T(8,128)(2,1)S(1)}, bf16[128,576]{1,0:T(8,128)(2,1)S(1)}, bf16[128,576]{1,0:T(8,128)(2,1)S(1)}) custom-call(s32[1,512]{1,0:T(1,128)S(1)} %get-tuple-element.45.target_ref, bf16[64,1792]{1,0:T(8,128)(2,1)S(1)} %get-tuple-element.46.refs_0_, bf16[64,1792]{1,0:T(8,128)(2,1)S(1)} %collective-permute-done.1.refs_1_, ...), custom_call_target="tpu_custom_call" | custom-call | tf_op jit(solution)/shard_map/project/pallas_call | solution.py:312
  30.5 1.7 %collective-permute-start.6 = (bf16[128,576]{1,0:T(8,128)(2,1)S(1)}, bf16[128,576]{1,0:T(8,128)(2,1)S(1)}, u32[]{:S(2)}, u32[]{:S(2)}) collective-permute-start(bf16[128,576]{1,0:T(8,128)(2,1)S(1)} %get-tuple-element.53), channel_id=1, source_target_pairs={{0,4},{4,0},{8,12},{12,8},{1,5},{5,1},{9,13},{13,9},{2,6},{6,2},{1... | collective-permute-start | bytes 442376 | tf_op jit(solution)/shard_map/ppermute | solution.py:21
  32.2 2.6 %collective-permute-start.7 = (bf16[128,576]{1,0:T(8,128)(2,1)S(1)}, bf16[128,576]{1,0:T(8,128)(2,1)S(1)}, u32[]{:S(2)}, u32[]{:S(2)}) collective-permute-start(bf16[128,576]{1,0:T(8,128)(2,1)S(1)} %get-tuple-element.54), channel_id=1, source_target_pairs={{0,8},{4,12},{8,0},{12,4},{1,9},{5,13},{9,1},{13,5},{2,10},{6,14},... | collective-permute-start | bytes 442376 | tf_op jit(solution)/shard_map/ppermute | solution.py:21
  34.8 0.2 collective-permute-start.8
  35.0 4.7 %collective-permute-done.6.refs_1_ = bf16[128,576]{1,0:T(8,128)(2,1)S(1)} collective-permute-done((bf16[128,576]{1,0:T(8,128)(2,1)S(1)}, bf16[128,576]{1,0:T(8,128)(2,1)S(1)}, u32[]{:S(2)}, u32[]{:S(2)}) %collective-permute-start.6) | collective-permute-done | bytes 147488 | tf_op jit(solution)/shard_map/ppermute | solution.py:21
  39.7 7.5 %collective-permute-done.7.refs_2_ = bf16[128,576]{1,0:T(8,128)(2,1)S(1)} collective-permute-done((bf16[128,576]{1,0:T(8,128)(2,1)S(1)}, bf16[128,576]{1,0:T(8,128)(2,1)S(1)}, u32[]{:S(2)}, u32[]{:S(2)}) %collective-permute-start.7) | collective-permute-done | bytes 147488 | tf_op jit(solution)/shard_map/ppermute | solution.py:21
  47.2 0.3 finish_rows.1.refs_0_
  47.5 0.1 collective-permute-start.11
  47.6 1.6 %collective-permute-start.10 = (bf16[128,576]{1,0:T(8,128)(2,1)S(1)}, bf16[128,576]{1,0:T(8,128)(2,1)S(1)}, u32[]{:S(2)}, u32[]{:S(2)}) collective-permute-start(bf16[128,576]{1,0:T(8,128)(2,1)S(1)} %finish_rows.1.refs_0_), channel_id=1, source_target_pairs={{0,2},{1,3},{2,0},{3,1},{4,6},{5,7},{6,4},{7,5},{8,10},{9,11},{10,... | collective-permute-start | bytes 442376 | tf_op jit(solution)/shard_map/ppermute | solution.py:21
  49.1 0.3 collective-permute-start.9
  49.4 4.6 %collective-permute-done.11.refs_3_ = bf16[128,576]{1,0:T(8,128)(2,1)S(1)} collective-permute-done((bf16[128,576]{1,0:T(8,128)(2,1)S(1)}, bf16[128,576]{1,0:T(8,128)(2,1)S(1)}, u32[]{:S(2)}, u32[]{:S(2)}) %collective-permute-start.11) | collective-permute-done | bytes 147488 | tf_op jit(solution)/shard_map/ppermute | solution.py:21
  54.0 3.6 %collective-permute-done.10.refs_2_ = bf16[128,576]{1,0:T(8,128)(2,1)S(1)} collective-permute-done((bf16[128,576]{1,0:T(8,128)(2,1)S(1)}, bf16[128,576]{1,0:T(8,128)(2,1)S(1)}, u32[]{:S(2)}, u32[]{:S(2)}) %collective-permute-start.10) | collective-permute-done | bytes 147488 | tf_op jit(solution)/shard_map/ppermute | solution.py:21
  57.6 1.3 %attend.3.refs_0_ = bf16[16,2048]{1,0:T(8,128)(2,1)S(1)} custom-call(bf16[512,576]{1,0:T(8,128)(2,1)S(1)} %get-tuple-element.35.query_ref, bf16[16,576]{1,0:T(8,128)(2,1)S(1)} %reshape.26.fresh_ref, s32[1,512]{1,0:T(1,128)S(1)} %get-tuple-element.37.slot_ref, f32[512,128]{1,0:T(8,128)S(1)} %get-tuple-element.38.top_ref, ...), custom_call_target="tpu_custom_call" | custom-call | tf_op jit(solution)/shard_map/attend/pallas_call | solution.py:420
  58.9 2.5 %collective-permute-start.17 = (bf16[16,2048]{1,0:T(8,128)(2,1)S(1)}, bf16[16,2048]{1,0:T(8,128)(2,1)S(1)}, u32[]{:S(2)}, u32[]{:S(2)}) collective-permute-start(bf16[16,2048]{1,0:T(8,128)(2,1)S(1)} %attend.3.refs_0_), channel_id=1, source_target_pairs={{0,12},{4,8},{8,4},{12,0},{1,13},{5,9},{9,5},{13,1},{2,14},{6,10},... | collective-permute-start | bytes 196616 | tf_op jit(solution)/shard_map/ppermute | solution.py:21
  61.4 2.1 %collective-permute-start.16 = (bf16[16,2048]{1,0:T(8,128)(2,1)S(1)}, bf16[16,2048]{1,0:T(8,128)(2,1)S(1)}, u32[]{:S(2)}, u32[]{:S(2)}) collective-permute-start(bf16[16,2048]{1,0:T(8,128)(2,1)S(1)} %attend.3.refs_0_), channel_id=1, source_target_pairs={{0,8},{4,12},{8,0},{12,4},{1,9},{5,13},{9,1},{13,5},{2,10},{6,14},... | collective-permute-start | bytes 196616 | tf_op jit(solution)/shard_map/ppermute | solution.py:21
  63.5 0.1 collective-permute-start.15
  63.6 1.3 %attend.2.refs_0_ = bf16[16,2048]{1,0:T(8,128)(2,1)S(1)} custom-call(bf16[512,576]{1,0:T(8,128)(2,1)S(1)} %get-tuple-element.35.query_ref, bf16[16,576]{1,0:T(8,128)(2,1)S(1)} %reshape.26.fresh_ref, s32[1,512]{1,0:T(1,128)S(1)} %get-tuple-element.37.slot_ref, f32[512,128]{1,0:T(8,128)S(1)} %get-tuple-element.38.top_ref, ...), custom_call_target="tpu_custom_call" | custom-call | tf_op jit(solution)/shard_map/attend/pallas_call | solution.py:420
  64.9 2.4 %collective-permute-start.14 = (bf16[16,2048]{1,0:T(8,128)(2,1)S(1)}, bf16[16,2048]{1,0:T(8,128)(2,1)S(1)}, u32[]{:S(2)}, u32[]{:S(2)}) collective-permute-start(bf16[16,2048]{1,0:T(8,128)(2,1)S(1)} %attend.2.refs_0_), channel_id=1, source_target_pairs={{0,12},{4,8},{8,4},{12,0},{1,13},{5,9},{9,5},{13,1},{2,14},{6,10},... | collective-permute-start | bytes 196616 | tf_op jit(solution)/shard_map/ppermute | solution.py:21
  67.4 1.0 %collective-permute-start.13 = (bf16[16,2048]{1,0:T(8,128)(2,1)S(1)}, bf16[16,2048]{1,0:T(8,128)(2,1)S(1)}, u32[]{:S(2)}, u32[]{:S(2)}) collective-permute-start(bf16[16,2048]{1,0:T(8,128)(2,1)S(1)} %attend.2.refs_0_), channel_id=1, source_target_pairs={{0,8},{4,12},{8,0},{12,4},{1,9},{5,13},{9,1},{13,5},{2,10},{6,14},... | collective-permute-start | bytes 196616 | tf_op jit(solution)/shard_map/ppermute | solution.py:21
  68.4 1.0 %collective-permute-start.12 = (bf16[16,2048]{1,0:T(8,128)(2,1)S(1)}, bf16[16,2048]{1,0:T(8,128)(2,1)S(1)}, u32[]{:S(2)}, u32[]{:S(2)}) collective-permute-start(bf16[16,2048]{1,0:T(8,128)(2,1)S(1)} %attend.2.refs_0_), channel_id=1, source_target_pairs={{0,4},{4,0},{8,12},{12,8},{1,5},{5,1},{9,13},{13,9},{2,6},{6,2},{1... | collective-permute-start | bytes 196616 | tf_op jit(solution)/shard_map/ppermute | solution.py:21
  69.4 0.7 collective-permute-done.16.refs_2_
  70.0 1.4 %output_product.2.refs_5_ = f32[64,1792]{1,0:T(8,128)S(1)} custom-call(bf16[16,2048]{1,0:T(8,128)(2,1)S(1)} %attend.3.refs_0_, bf16[16,2048]{1,0:T(8,128)(2,1)S(1)} %collective-permute-done.15.refs_1_, bf16[16,2048]{1,0:T(8,128)(2,1)S(1)} %collective-permute-done.16.refs_2_, bf16[16,2048]{1,0:T(8,128)(2,1)S(1)} %collective-permute-done.17.refs_3_, ...), custom_call_target="tpu_custom_call" | custom-call | tf_op jit(solution)/shard_map/output_product/pallas_call | solution.py:474
  71.4 0.4 collective-permute-done.14.refs_3_
  71.8 2.9 %collective-permute-done.13.refs_2_ = bf16[16,2048]{1,0:T(8,128)(2,1)S(1)} collective-permute-done((bf16[16,2048]{1,0:T(8,128)(2,1)S(1)}, bf16[16,2048]{1,0:T(8,128)(2,1)S(1)}, u32[]{:S(2)}, u32[]{:S(2)}) %collective-permute-start.13) | collective-permute-done | bytes 65568 | tf_op jit(solution)/shard_map/ppermute | solution.py:21
  74.7 1.4 %output_product.3 = (f32[16,1792]{1,0:T(8,128)S(1)}, bf16[16,1792]{1,0:T(8,128)(2,1)S(1)}, bf16[16,1792]{1,0:T(8,128)(2,1)S(1)}, bf16[16,1792]{1,0:T(8,128)(2,1)S(1)}) custom-call(bf16[16,2048]{1,0:T(8,128)(2,1)S(1)} %attend.2.refs_0_, bf16[16,2048]{1,0:T(8,128)(2,1)S(1)} %collective-permute-done.12.refs_1_, ...), custom_call_target="tpu_custom_call" | custom-call | tf_op jit(solution)/shard_map/output_product/pallas_call | solution.py:474
  76.1 1.4 %collective-permute-start.19 = (bf16[16,1792]{1,0:T(8,128)(2,1)S(1)}, bf16[16,1792]{1,0:T(8,128)(2,1)S(1)}, u32[]{:S(2)}, u32[]{:S(2)}) collective-permute-start(bf16[16,1792]{1,0:T(8,128)(2,1)S(1)} %get-tuple-element.59), channel_id=1, source_target_pairs={{0,2},{1,3},{2,0},{3,1},{4,6},{5,7},{6,4},{7,5},{8,10},{9,11},{10,... | collective-permute-start | bytes 172040 | tf_op jit(solution)/shard_map/ppermute | solution.py:21
  77.6 0.4 collective-permute-start.20
  78.0 2.4 %collective-permute-done.18 = bf16[16,1792]{1,0:T(8,128)(2,1)S(1)} collective-permute-done((bf16[16,1792]{1,0:T(8,128)(2,1)S(1)}, bf16[16,1792]{1,0:T(8,128)(2,1)S(1)}, u32[]{:S(2)}, u32[]{:S(2)}) %collective-permute-start.18) | collective-permute-done | bytes 57376 | tf_op jit(solution)/shard_map/ppermute | solution.py:21
  80.3 1.2 %collective-permute-done.19 = bf16[16,1792]{1,0:T(8,128)(2,1)S(1)} collective-permute-done((bf16[16,1792]{1,0:T(8,128)(2,1)S(1)}, bf16[16,1792]{1,0:T(8,128)(2,1)S(1)}, u32[]{:S(2)}, u32[]{:S(2)}) %collective-permute-start.19) | collective-permute-done | bytes 57376 | tf_op jit(solution)/shard_map/ppermute | solution.py:21
  81.5 0.7 add_convert_fusion
  (25 shorter events, 0.1 us)
Async XLA Ops:
  0.0 9.5 %collective-permute-start = (bf16[448,576]{1,0:T(8,128)(2,1)}, bf16[448,576]{1,0:T(8,128)(2,1)S(1)}, u32[]{:S(2)}, u32[]{:S(2)}) collective-permute-start(bf16[448,576]{1,0:T(8,128)(2,1)} %refs_4_.1), channel_id=1, source_target_pairs={{0,1},{1,0},{2,3},{3,2},{4,5},{5,4},{6,7},{7,6},{8,9},{9,8},{10,11... | collective-permute-start | bytes 1548296 | tf_op jit(solution)/shard_map/ppermute | solution.py:21
  0.5 25.2 %collective-permute-start.4 = (bf16[448,576]{1,0:T(8,128)(2,1)}, bf16[448,576]{1,0:T(8,128)(2,1)S(1)}, u32[]{:S(2)}, u32[]{:S(2)}) collective-permute-start(bf16[448,576]{1,0:T(8,128)(2,1)} %refs_4_.1), channel_id=1, source_target_pairs={{0,2},{1,3},{2,0},{3,1},{4,6},{5,7},{6,4},{7,5},{8,10},{9,11},{10,... | collective-permute-start | bytes 1548296 | tf_op jit(solution)/shard_map/ppermute | solution.py:21
  2.9 26.0 %collective-permute-start.5 = (bf16[448,576]{1,0:T(8,128)(2,1)}, bf16[448,576]{1,0:T(8,128)(2,1)S(1)}, u32[]{:S(2)}, u32[]{:S(2)}) collective-permute-start(bf16[448,576]{1,0:T(8,128)(2,1)} %refs_4_.1), channel_id=1, source_target_pairs={{0,3},{1,2},{2,1},{3,0},{4,7},{5,6},{6,5},{7,4},{8,11},{9,10},{10,... | collective-permute-start | bytes 1548296 | tf_op jit(solution)/shard_map/ppermute | solution.py:21
  3.1 1.2 %copy-start.3 = (bf16[64,7168]{1,0:T(8,128)(2,1)S(1)}, bf16[64,7168]{1,0:T(8,128)(2,1)}, u32[]{:S(2)}) copy-start(bf16[64,7168]{1,0:T(8,128)(2,1)} %prompts_ref.1) | copy-start | bytes 2752516
  4.5 21.2 %collective-permute-start.2 = (bf16[64,1792]{1,0:T(8,128)(2,1)S(1)}, bf16[64,1792]{1,0:T(8,128)(2,1)S(1)}, u32[]{:S(2)}, u32[]{:S(2)}) collective-permute-start(bf16[64,1792]{1,0:T(8,128)(2,1)S(1)} %get-tuple-element.49), channel_id=1, source_target_pairs={{0,8},{4,12},{8,0},{12,4},{1,9},{5,13},{9,1},{13,5},{2,10},{6,14},... | collective-permute-start | bytes 688136 | tf_op jit(solution)/shard_map/ppermute | solution.py:21
  7.3 18.3 %collective-permute-start.3 = (bf16[64,1792]{1,0:T(8,128)(2,1)S(1)}, bf16[64,1792]{1,0:T(8,128)(2,1)S(1)}, u32[]{:S(2)}, u32[]{:S(2)}) collective-permute-start(bf16[64,1792]{1,0:T(8,128)(2,1)S(1)} %get-tuple-element.50), channel_id=1, source_target_pairs={{0,12},{4,8},{8,4},{12,0},{1,13},{5,9},{9,5},{13,1},{2,14},{6,10},... | collective-permute-start | bytes 688136 | tf_op jit(solution)/shard_map/ppermute | solution.py:21
  9.5 19.4 %collective-permute-start.1 = (bf16[64,1792]{1,0:T(8,128)(2,1)S(1)}, bf16[64,1792]{1,0:T(8,128)(2,1)S(1)}, u32[]{:S(2)}, u32[]{:S(2)}) collective-permute-start(bf16[64,1792]{1,0:T(8,128)(2,1)S(1)} %get-tuple-element.48), channel_id=1, source_target_pairs={{0,4},{4,0},{8,12},{12,8},{1,5},{5,1},{9,13},{13,9},{2,6},{6,2},{1... | collective-permute-start | bytes 688136 | tf_op jit(solution)/shard_map/ppermute | solution.py:21
  9.8 2.2 %copy-start = (bf16[32,128,512]{2,1,0:T(8,128)(2,1)S(1)}, bf16[32,128,512]{2,1,0:T(8,128)(2,1)}, u32[]{:S(2)}) copy-start(bf16[32,128,512]{2,1,0:T(8,128)(2,1)} %absorb_hbm.1) | copy-start | bytes 12582916
  12.0 2.2 %copy-start.1 = (bf16[32,512,128]{2,1,0:T(8,128)(2,1)S(1)}, bf16[32,512,128]{2,1,0:T(8,128)(2,1)}, u32[]{:S(2)}) copy-start(bf16[32,512,128]{2,1,0:T(8,128)(2,1)} %value_hbm.1) | copy-start | bytes 12582916
  14.1 1.7 %copy-start.2 = (bf16[8,256,576]{1,2,0:T(8,128)(2,1)S(1)}, bf16[8,256,576]{1,2,0:T(8,128)(2,1)}, u32[]{:S(2)}) copy-start(bf16[8,256,576]{1,2,0:T(8,128)(2,1)} %param.18) | copy-start | bytes 7077892
  15.8 0.9 %copy-start.5 = (bf16[8,2,32,192]{3,2,1,0:T(8,128)(2,1)S(1)}, bf16[8,2,32,192]{3,2,1,0:T(8,128)(2,1)}, u32[]{:S(2)}) copy-start(bf16[8,2,32,192]{3,2,1,0:T(8,128)(2,1)} %param.20) | copy-start | bytes 589828
  16.8 0.7 copy-start.6
  17.4 0.7 copy-start.8
  18.1 0.7 copy-start.9
  18.8 10.1 %copy-start.4 = (bf16[448,576]{1,0:T(8,128)(2,1)S(1)}, bf16[448,576]{1,0:T(8,128)(2,1)}, u32[]{:S(2)}) copy-start(bf16[448,576]{1,0:T(8,128)(2,1)} %refs_4_.1) | copy-start | bytes 1548292
  18.8 28.4 %copy-start.7 = (f32[512]{0:T(512)S(1)}, f32[512]{0:T(512)}, u32[]{:S(2)}) copy-start(f32[512]{0:T(512)} %param.14) | copy-start | bytes 6148
  30.5 9.2 %collective-permute-start.6 = (bf16[128,576]{1,0:T(8,128)(2,1)S(1)}, bf16[128,576]{1,0:T(8,128)(2,1)S(1)}, u32[]{:S(2)}, u32[]{:S(2)}) collective-permute-start(bf16[128,576]{1,0:T(8,128)(2,1)S(1)} %get-tuple-element.53), channel_id=1, source_target_pairs={{0,4},{4,0},{8,12},{12,8},{1,5},{5,1},{9,13},{13,9},{2,6},{6,2},{1... | collective-permute-start | bytes 442376 | tf_op jit(solution)/shard_map/ppermute | solution.py:21
  32.2 15.0 %collective-permute-start.7 = (bf16[128,576]{1,0:T(8,128)(2,1)S(1)}, bf16[128,576]{1,0:T(8,128)(2,1)S(1)}, u32[]{:S(2)}, u32[]{:S(2)}) collective-permute-start(bf16[128,576]{1,0:T(8,128)(2,1)S(1)} %get-tuple-element.54), channel_id=1, source_target_pairs={{0,8},{4,12},{8,0},{12,4},{1,9},{5,13},{9,1},{13,5},{2,10},{6,14},... | collective-permute-start | bytes 442376 | tf_op jit(solution)/shard_map/ppermute | solution.py:21
  34.8 12.4 %collective-permute-start.8 = (bf16[128,576]{1,0:T(8,128)(2,1)S(1)}, bf16[128,576]{1,0:T(8,128)(2,1)S(1)}, u32[]{:S(2)}, u32[]{:S(2)}) collective-permute-start(bf16[128,576]{1,0:T(8,128)(2,1)S(1)} %get-tuple-element.55), channel_id=1, source_target_pairs={{0,12},{4,8},{8,4},{12,0},{1,13},{5,9},{9,5},{13,1},{2,14},{6,10},... | collective-permute-start | bytes 442376 | tf_op jit(solution)/shard_map/ppermute | solution.py:21
  47.5 6.5 %collective-permute-start.11 = (bf16[128,576]{1,0:T(8,128)(2,1)S(1)}, bf16[128,576]{1,0:T(8,128)(2,1)S(1)}, u32[]{:S(2)}, u32[]{:S(2)}) collective-permute-start(bf16[128,576]{1,0:T(8,128)(2,1)S(1)} %finish_rows.1.refs_0_), channel_id=1, source_target_pairs={{0,3},{1,2},{2,1},{3,0},{4,7},{5,6},{6,5},{7,4},{8,11},{9,10},{10,... | collective-permute-start | bytes 442376 | tf_op jit(solution)/shard_map/ppermute | solution.py:21
  47.6 10.0 %collective-permute-start.10 = (bf16[128,576]{1,0:T(8,128)(2,1)S(1)}, bf16[128,576]{1,0:T(8,128)(2,1)S(1)}, u32[]{:S(2)}, u32[]{:S(2)}) collective-permute-start(bf16[128,576]{1,0:T(8,128)(2,1)S(1)} %finish_rows.1.refs_0_), channel_id=1, source_target_pairs={{0,2},{1,3},{2,0},{3,1},{4,6},{5,7},{6,4},{7,5},{8,10},{9,11},{10,... | collective-permute-start | bytes 442376 | tf_op jit(solution)/shard_map/ppermute | solution.py:21
  49.1 8.4 %collective-permute-start.9 = (bf16[128,576]{1,0:T(8,128)(2,1)S(1)}, bf16[128,576]{1,0:T(8,128)(2,1)S(1)}, u32[]{:S(2)}, u32[]{:S(2)}) collective-permute-start(bf16[128,576]{1,0:T(8,128)(2,1)S(1)} %finish_rows.1.refs_0_), channel_id=1, source_target_pairs={{0,1},{1,0},{2,3},{3,2},{4,5},{5,4},{6,7},{7,6},{8,9},{9,8},{10,11... | collective-permute-start | bytes 442376 | tf_op jit(solution)/shard_map/ppermute | solution.py:21
  58.9 9.5 %collective-permute-start.17 = (bf16[16,2048]{1,0:T(8,128)(2,1)S(1)}, bf16[16,2048]{1,0:T(8,128)(2,1)S(1)}, u32[]{:S(2)}, u32[]{:S(2)}) collective-permute-start(bf16[16,2048]{1,0:T(8,128)(2,1)S(1)} %attend.3.refs_0_), channel_id=1, source_target_pairs={{0,12},{4,8},{8,4},{12,0},{1,13},{5,9},{9,5},{13,1},{2,14},{6,10},... | collective-permute-start | bytes 196616 | tf_op jit(solution)/shard_map/ppermute | solution.py:21
  61.4 8.6 %collective-permute-start.16 = (bf16[16,2048]{1,0:T(8,128)(2,1)S(1)}, bf16[16,2048]{1,0:T(8,128)(2,1)S(1)}, u32[]{:S(2)}, u32[]{:S(2)}) collective-permute-start(bf16[16,2048]{1,0:T(8,128)(2,1)S(1)} %attend.3.refs_0_), channel_id=1, source_target_pairs={{0,8},{4,12},{8,0},{12,4},{1,9},{5,13},{9,1},{13,5},{2,10},{6,14},... | collective-permute-start | bytes 196616 | tf_op jit(solution)/shard_map/ppermute | solution.py:21
  63.5 6.5 %collective-permute-start.15 = (bf16[16,2048]{1,0:T(8,128)(2,1)S(1)}, bf16[16,2048]{1,0:T(8,128)(2,1)S(1)}, u32[]{:S(2)}, u32[]{:S(2)}) collective-permute-start(bf16[16,2048]{1,0:T(8,128)(2,1)S(1)} %attend.3.refs_0_), channel_id=1, source_target_pairs={{0,4},{4,0},{8,12},{12,8},{1,5},{5,1},{9,13},{13,9},{2,6},{6,2},{1... | collective-permute-start | bytes 196616 | tf_op jit(solution)/shard_map/ppermute | solution.py:21
  64.9 6.9 %collective-permute-start.14 = (bf16[16,2048]{1,0:T(8,128)(2,1)S(1)}, bf16[16,2048]{1,0:T(8,128)(2,1)S(1)}, u32[]{:S(2)}, u32[]{:S(2)}) collective-permute-start(bf16[16,2048]{1,0:T(8,128)(2,1)S(1)} %attend.2.refs_0_), channel_id=1, source_target_pairs={{0,12},{4,8},{8,4},{12,0},{1,13},{5,9},{9,5},{13,1},{2,14},{6,10},... | collective-permute-start | bytes 196616 | tf_op jit(solution)/shard_map/ppermute | solution.py:21
  67.4 7.3 %collective-permute-start.13 = (bf16[16,2048]{1,0:T(8,128)(2,1)S(1)}, bf16[16,2048]{1,0:T(8,128)(2,1)S(1)}, u32[]{:S(2)}, u32[]{:S(2)}) collective-permute-start(bf16[16,2048]{1,0:T(8,128)(2,1)S(1)} %attend.2.refs_0_), channel_id=1, source_target_pairs={{0,8},{4,12},{8,0},{12,4},{1,9},{5,13},{9,1},{13,5},{2,10},{6,14},... | collective-permute-start | bytes 196616 | tf_op jit(solution)/shard_map/ppermute | solution.py:21
  68.4 6.3 %collective-permute-start.12 = (bf16[16,2048]{1,0:T(8,128)(2,1)S(1)}, bf16[16,2048]{1,0:T(8,128)(2,1)S(1)}, u32[]{:S(2)}, u32[]{:S(2)}) collective-permute-start(bf16[16,2048]{1,0:T(8,128)(2,1)S(1)} %attend.2.refs_0_), channel_id=1, source_target_pairs={{0,4},{4,0},{8,12},{12,8},{1,5},{5,1},{9,13},{13,9},{2,6},{6,2},{1... | collective-permute-start | bytes 196616 | tf_op jit(solution)/shard_map/ppermute | solution.py:21
  76.1 4.3 %collective-permute-start.18 = (bf16[16,1792]{1,0:T(8,128)(2,1)S(1)}, bf16[16,1792]{1,0:T(8,128)(2,1)S(1)}, u32[]{:S(2)}, u32[]{:S(2)}) collective-permute-start(bf16[16,1792]{1,0:T(8,128)(2,1)S(1)} %get-tuple-element.58), channel_id=1, source_target_pairs={{0,3},{1,2},{2,1},{3,0},{4,7},{5,6},{6,5},{7,4},{8,11},{9,10},{10,... | collective-permute-start | bytes 172040 | tf_op jit(solution)/shard_map/ppermute | solution.py:21
  76.1 5.4 %collective-permute-start.19 = (bf16[16,1792]{1,0:T(8,128)(2,1)S(1)}, bf16[16,1792]{1,0:T(8,128)(2,1)S(1)}, u32[]{:S(2)}, u32[]{:S(2)}) collective-permute-start(bf16[16,1792]{1,0:T(8,128)(2,1)S(1)} %get-tuple-element.59), channel_id=1, source_target_pairs={{0,2},{1,3},{2,0},{3,1},{4,6},{5,7},{6,4},{7,5},{8,10},{9,11},{10,... | collective-permute-start | bytes 172040 | tf_op jit(solution)/shard_map/ppermute | solution.py:21
  77.6 4.0 %collective-permute-start.20 = (bf16[16,1792]{1,0:T(8,128)(2,1)S(1)}, bf16[16,1792]{1,0:T(8,128)(2,1)S(1)}, u32[]{:S(2)}, u32[]{:S(2)}) collective-permute-start(bf16[16,1792]{1,0:T(8,128)(2,1)S(1)} %get-tuple-element.60), channel_id=1, source_target_pairs={{0,1},{1,0},{2,3},{3,2},{4,5},{5,4},{6,7},{7,6},{8,9},{9,8},{10,11... | collective-permute-start | bytes 172040 | tf_op jit(solution)/shard_map/ppermute | solution.py:21

commit v5 on v4

--- a/solution.py
+++ b/solution.py
@@ -30,6 +30,49 @@
 
 def lane_tiles(width):
     return [slice(n, min(n + 128, width)) for n in range(0, width, 128)]
+
+
+def packed_rows(rows, width):
+    return rows * (width // 128) + rows // 2
+
+
+def pack(value):
+    rows, width = value.shape
+    full = width // 128
+    rest = value[:, full * 128 :]
+    parts = [value[:, n * 128 : (n + 1) * 128] for n in range(full)]
+    return parts + [jnp.concatenate([rest[: rows // 2], rest[rows // 2 :]], axis=1)]
+
+
+def store_packed(ref, value):
+    first = 0
+    for part in pack(value):
+        ref[first : first + part.shape[0], :] = part.astype(ref.dtype)
+        first += part.shape[0]
+
+
+def load_packed(ref, rows):
+    full = ref.shape[0] // rows
+    tiles = [ref[n * rows : (n + 1) * rows, :] for n in range(full)]
+    rest = ref[full * rows :, :]
+    return tiles, jnp.concatenate([rest[:, :64], rest[:, 64:]], axis=0)
+
+
+def pack_kernel(value_ref, out_ref):
+    store_packed(out_ref, value_ref[...])
+
+
+def pack_weight(weight):
+    rows, width = weight.shape
+    return pl.pallas_call(
+        pack_kernel,
+        out_shape=jax.ShapeDtypeStruct((packed_rows(rows, width), 128), weight.dtype),
+        in_specs=[in_vmem],
+        out_specs=in_vmem,
+        compiler_params=pltpu.CompilerParams(vmem_limit_bytes=8 * mib),
+        cost_estimate=pl.CostEstimate(flops=10**10, bytes_accessed=10**6, transcendentals=0),
+        name="pack_weight",
+    )(weight)
 
 
 def split_kernel(slab, prompts_ref, *refs):
@@ -61,6 +104,9 @@
         out_specs=[in_vmem] * count,
         scratch_shapes=[pltpu.SemaphoreType.DMA((count,))],
         compiler_params=pltpu.CompilerParams(vmem_limit_bytes=8 * mib),
+        cost_estimate=pl.CostEstimate(
+            flops=10**10, bytes_accessed=4 * 10**7, transcendentals=0
+        ),
         name="split_columns",
     )(prompts)
 
@@ -282,12 +328,16 @@
     weight_refs = refs[dev_count : dev_count + side_count]
     out_refs = refs[dev_count + side_count : -3]
     x_rows, slab_weight, rows = refs[-3:]
-    shard = weight_refs[0].shape[0]
     tok_rows = x_refs[0].shape[0]
+    full = slab_weight.shape[1] // 128
     if side_count > 1:
+        shard = slab_weight.shape[0] // side_count
         for k in range(side_count):
             first = pl.multiple_of((my_side ^ k) * shard, 16)
-            slab_weight[pl.ds(first, shard), :] = weight_refs[k][...]
+            tiles, rest = load_packed(weight_refs[k], shard)
+            for n, tile in enumerate(tiles):
+                slab_weight[pl.ds(first, shard), n * 128 : (n + 1) * 128] = tile
+            slab_weight[pl.ds(first, shard), full * 128 :] = rest
     for k in range(dev_count):
         x_rows[k * tok_rows : (k + 1) * tok_rows, :] = x_refs[k][...]
     slab = slab_weight[...] if side_count > 1 else weight_refs[0][...]
@@ -296,23 +346,24 @@
     for k in range(dev_count):
         for n in range(k * copies, (k + 1) * copies):
             rows[n * tok_rows : (n + 1) * tok_rows, :] = raw[k * tok_rows : (k + 1) * tok_rows, :]
-    group_rows = out_refs[0].shape[0]
     target = target_ref[...]
-    for j in range(dev_count):
-        ids = lax.broadcasted_iota(jnp.int32, (group_rows, target.shape[1]), 0) + j * group_rows
-        route = jnp.where(ids == target, 1.0, 0.0).astype(bf16)
-        out_refs[j][...] = jnp.dot(
-            route, rows[...], preferred_element_type=f32
-        ).astype(out_refs[j].dtype)
-
-
-def project(x_pieces, weights, target, group_rows):
-    dev_count, width = len(x_pieces), weights[0].shape[1]
+    group_rows = 2 * tok_rows
+    step = max(1, min(dev_count, 512 // group_rows))
+    for j in range(0, dev_count, step):
+        ids = lax.broadcasted_iota(jnp.int32, (step * group_rows, target.shape[1]), 0)
+        route = jnp.where(ids + j * group_rows == target, 1.0, 0.0).astype(bf16)
+        placed = jnp.dot(route, rows[...], preferred_element_type=f32)
+        for n in range(step):
+            store_packed(out_refs[j + n], placed[n * group_rows : (n + 1) * group_rows])
+
+
+def project(x_pieces, weights, target, width):
+    dev_count = len(x_pieces)
     tok_rows, slab = x_pieces[0].shape
     return pl.pallas_call(
         functools.partial(project_kernel, dev_count, len(weights)),
         out_shape=[
-            jax.ShapeDtypeStruct((group_rows, width), f32 if j == 0 else bf16)
+            jax.ShapeDtypeStruct((packed_rows(2 * tok_rows, width), 128), f32 if j == 0 else bf16)
             for j in range(dev_count)
         ],
         in_specs=[in_vmem] * (1 + dev_count + len(weights)),
@@ -322,28 +373,29 @@
             pltpu.VMEM((slab, width), bf16),
             pltpu.VMEM((target.shape[1], width), bf16),
         ],
-        compiler_params=pltpu.CompilerParams(vmem_limit_bytes=10 * mib),
+        compiler_params=pltpu.CompilerParams(vmem_limit_bytes=20 * mib),
         name="project",
     )(target, *x_pieces, *weights)
 
 
 def finish_kernel(gain_ref, cos_ref, sin_ref, *refs):
     parts, out_ref = refs[:-1], refs[-1]
-    lat_width = gain_ref.shape[1]
-    half = cos_ref.shape[1]
+    rows, half = cos_ref.shape
     total = parts[0][...].astype(f32)
     for part in parts[1:]:
         total = total + part[...].astype(f32)
-    latent = total[:, :lat_width]
+    tiles, rest = load_packed(total, rows)
+    latent = jnp.concatenate(tiles, axis=1)
     spread = jnp.mean(latent * latent, axis=1, keepdims=True)
-    out_ref[:, :lat_width] = (latent * lax.rsqrt(spread + 1e-06) * gain_ref[...]).astype(bf16)
-    first = total[:, lat_width : lat_width + half]
-    second = total[:, lat_width + half :]
+    latent = latent * lax.rsqrt(spread + 1e-06) * gain_ref[...]
+    first, second = rest[:, :half], rest[:, half:]
     cosine, sine = cos_ref[...], sin_ref[...]
-    turned = jnp.concatenate(
-        [first * cosine - second * sine, second * cosine + first * sine], axis=1
-    )
-    out_ref[:, lat_width:] = turned.astype(bf16)
+    store_packed(
+        out_ref,
+        jnp.concatenate(
+            [latent, first * cosine - second * sine, second * cosine + first * sine], axis=1
+        ),
+    )
 
 
 def finish(parts, gain, cosine, sine):
@@ -367,9 +419,13 @@
     rows = query_ref.shape[0] // parts
     heads = rows // per_head
     mine = slice(part * rows, (part + 1) * rows)
-    piece_rows = pieces[0].shape[0]
+    piece_rows = keys.shape[0] // len(pieces)
     for n, piece in enumerate(pieces):
-        keys[n * piece_rows : (n + 1) * piece_rows, :] = piece[...]
+        tiles, rest = load_packed(piece, piece_rows)
+        there = slice(n * piece_rows, (n + 1) * piece_rows)
+        for j, tile in enumerate(tiles):
+            keys[there, j * 128 : (j + 1) * 128] = tile
+        keys[there, lat_width:] = rest
     contract = (((1,), (1,)), ((), ()))
     row = lax.broadcasted_iota(jnp.int32, (rows, 1), 0)
     row_slot = (row // steps) % cap_slots
@@ -422,7 +478,7 @@
         out_shape=jax.ShapeDtypeStruct((cap_slots * steps, part_heads * width), bf16),
         in_specs=[in_vmem] * (8 + len(pieces)),
         out_specs=in_vmem,
-        scratch_shapes=[pltpu.VMEM((len(pieces) * pieces[0].shape[0], query.shape[1]), bf16)],
+        scratch_shapes=[pltpu.VMEM((row_slot.shape[1], query.shape[1]), bf16)],
         compiler_params=pltpu.CompilerParams(vmem_limit_bytes=10 * mib),
         name="attend",
     )(query, fresh, row_slot, top, total, mix, live, value, *pieces)
@@ -510,11 +566,12 @@
     slab = model_width // dev_count
 
     x_pieces = list(split_columns(prompts, dev_count))
-    weights = [latent_weight] + [None] * (side_count - 1)
+    packs = shard_rows % 32 == 0
+    weights = [pack_weight(latent_weight) if packs else latent_weight] + [None] * (side_count - 1)
     for k in sorted(range(2, dev_count), reverse=True):
         x_pieces[k] = swap(x_pieces[k], "dev", k)
     for k in range(1, side_count):
-        weights[k] = swap(latent_weight, "side", k)
+        weights[k] = swap(weights[0], "side", k)
     x_pieces[1], weights[1] = lax.optimization_barrier((x_pieces[1], weights[1]))
     x_pieces[1] = swap(x_pieces[1], "dev", 1)
 
@@ -533,14 +590,14 @@
         jnp.swapaxes(latent_cache, 1, 2), value_absorb, out_weight,
     )
 
-    if shard_rows % 16:
+    if not packs:
         my_side = lax.axis_index("side")
         held = jnp.zeros((side_count, shard_rows, kv_width), bf16)
         for k in range(side_count):
             held = lax.dynamic_update_slice(held, weights[k][None], (my_side ^ k, 0, 0))
         weights = [held.reshape(slab, kv_width)]
 
-    routed = project(x_pieces, weights, target, group_rows)
+    routed = project(x_pieces, weights, target, kv_width)
     parts = [routed[0]] + [None] * (dev_count - 1)
     for k in sorted(range(1, dev_count), reverse=True):
         parts[k] = swap(routed[k], "dev", k)

time: 82.6 us -> 82 us (level)
  local copies, waits for them, and re-layouts: 10.9 us -> 7.25 us
  starting transfers between devices: 25.1 us -> 28.3 us
  waiting for transfers between devices: 31.1 us -> 28.4 us
  Pallas kernels: 14.3 us -> 16.9 us
    ppermute x21, starting transfers between devices: 25.1 us -> 28.3 us  [swap(): return lax.ppermute(value, axis, [(i, i ^ step) for i in range(count)])]
    unnamed x20 -> x28, local copies, waits for them, and re-layouts: 10.2 us -> 7.22 us
    ppermute x21, waiting for transfers between devices: 31.1 us -> 28.4 us  [swap(): return lax.ppermute(value, axis, [(i, i ^ step) for i in range(count)])]
    pallas_call x1, Pallas kernels: 1.59 us -> 3.3 us  [project(): pl.pallas_call(functools.partial(project_kernel, dev_count, len(weights))...]
  transfers between devices with their start and end apart: 21 -> 21, of which waited for: 10 -> 10; matrix products, arithmetic and copies ran while one was open for 1% -> 0% of each run, Pallas kernels for 12% -> 13%
where the time goes in v5:
time: 82 us; the launch traced here: 81.7 us
  waiting for transfers between devices  28.4 us (35%)
  starting transfers between devices  28.3 us (35%)
  Pallas kernels  16.9 us (21%)
  local copies, waits for them, and re-layouts  7.25 us (9%)
    ppermute x21, waiting for transfers between devices, swap(): return lax.ppermute(value, axis, [(i, i ^ step) for i in range(count)])  28.4 us
    ppermute x21, starting transfers between devices, swap(): return lax.ppermute(value, axis, [(i, i ^ step) for i in range(count)])  28.3 us
    unnamed x28, local copies, waits for them, and re-layouts  7.22 us
    pallas_call x1, Pallas kernels, prepare(): pl.pallas_call(functools.partial(prepare_kernel, scale, steps, (dev_count...  6.87 us
    pallas_call x1, Pallas kernels, project(): pl.pallas_call(functools.partial(project_kernel, dev_count, len(weights))...  3.3 us
    pallas_call x2, Pallas kernels, output_product(): pl.pallas_call(functools.partial(output_kernel, dev_count, side_count, pa...  2.77 us
    pallas_call x2, Pallas kernels, attend(): pl.pallas_call(functools.partial(attend_kernel, scale, cap_slots, steps,...  2.67 us
  transfers between devices with their start and end apart: 21, of which 10 were waited for; matrix products, arithmetic and copies ran while one was open for 0% of the time, Pallas kernels for 13%

profile of v5, /device:TPU:0, one launch (start us, length us, event | category | flops | bytes accessed | tf_op | source)
XLA Modules:
  0.0 81.7 jit_solution(14846837532716582496)
XLA Ops:
  0.0 1.1 %copy-done.11 = bf16[448,576]{1,0:T(8,128)(2,1)S(1)} copy-done((bf16[448,576]{1,0:T(8,128)(2,1)S(1)}, bf16[448,576]{1,0:T(8,128)(2,1)}, u32[]{:S(2)}) %copy-start.11) | copy-done | bytes 516120
  1.1 0.1 pack_weight.1.refs_4_
  1.2 0.0 copy-start.13
  1.3 0.0 copy-start.8
  1.3 2.4 %collective-permute-start.5 = (bf16[2016,128]{1,0:T(8,128)(2,1)S(1)}, bf16[2016,128]{1,0:T(8,128)(2,1)S(1)}, u32[]{:S(2)}, u32[]{:S(2)}) collective-permute-start(bf16[2016,128]{1,0:T(8,128)(2,1)S(1)} %pack_weight.1.refs_4_), channel_id=1, source_target_pairs={{0,3},{1,2},{2,1},{3,0},{4,7},{5,6},{6,5},{7,4},{8,11},{9,10},{10,... | collective-permute-start | bytes 1548296 | tf_op jit(solution)/shard_map/ppermute | solution.py:21
  3.7 0.6 collective-permute-start.4
  4.4 0.0 collective-permute-start
  4.4 1.0 %split_columns.1 = (bf16[64,1792]{1,0:T(8,128)(2,1)S(1)}, bf16[64,1792]{1,0:T(8,128)(2,1)S(1)}, bf16[64,1792]{1,0:T(8,128)(2,1)}, bf16[64,1792]{1,0:T(8,128)(2,1)}) custom-call(bf16[64,7168]{1,0:T(8,128)(2,1)S(1)} %copy-done.10), custom_call_target="tpu_custom_call" | custom-call | flops 10000000000 | bytes 40000000 | tf_op jit(solution)/shard_map/split_columns/pallas_call | solution.py:100
  5.4 0.7 copy-done.4
  6.1 2.8 %collective-permute-start.2 = (bf16[64,1792]{1,0:T(8,128)(2,1)}, bf16[64,1792]{1,0:T(8,128)(2,1)}, u32[]{:S(2)}, u32[]{:S(2)}) collective-permute-start(bf16[64,1792]{1,0:T(8,128)(2,1)} %get-tuple-element.49), channel_id=1, source_target_pairs={{0,8},{4,12},{8,0},{12,4},{1,9},{5,13},{9,1},{13,5},{2,10},{6,14},... | collective-permute-start | bytes 688136 | tf_op jit(solution)/shard_map/ppermute | solution.py:21
  9.0 1.7 %collective-permute-start.3 = (bf16[64,1792]{1,0:T(8,128)(2,1)}, bf16[64,1792]{1,0:T(8,128)(2,1)}, u32[]{:S(2)}, u32[]{:S(2)}) collective-permute-start(bf16[64,1792]{1,0:T(8,128)(2,1)} %get-tuple-element.50), channel_id=1, source_target_pairs={{0,12},{4,8},{8,4},{12,0},{1,13},{5,9},{9,5},{13,1},{2,14},{6,10},... | collective-permute-start | bytes 688136 | tf_op jit(solution)/shard_map/ppermute | solution.py:21
  10.7 0.1 collective-permute-start.1
  10.8 2.2 %copy-done = bf16[32,128,512]{2,1,0:T(8,128)(2,1)S(1)} copy-done((bf16[32,128,512]{2,1,0:T(8,128)(2,1)S(1)}, bf16[32,128,512]{2,1,0:T(8,128)(2,1)}, u32[]{:S(2)}) %copy-start) | copy-done | bytes 4194328
  13.0 2.2 %copy-done.1 = bf16[32,512,128]{2,1,0:T(8,128)(2,1)S(1)} copy-done((bf16[32,512,128]{2,1,0:T(8,128)(2,1)S(1)}, bf16[32,512,128]{2,1,0:T(8,128)(2,1)}, u32[]{:S(2)}) %copy-start.1) | copy-done | bytes 4194328
  15.2 0.9 %copy-done.3 = bf16[8,2,32,192]{3,2,1,0:T(8,128)(2,1)S(1)} copy-done((bf16[8,2,32,192]{3,2,1,0:T(8,128)(2,1)S(1)}, bf16[8,2,32,192]{3,2,1,0:T(8,128)(2,1)}, u32[]{:S(2)}) %copy-start.3) | copy-done | bytes 196632
  16.2 6.9 %prepare.1 = (bf16[512,576]{1,0:T(8,128)(2,1)S(1)}, f32[512,128]{1,0:T(8,128)S(1)}, f32[512,128]{1,0:T(8,128)S(1)}, f32[4,512,128]{2,1,0:T(8,128)S(1)}, f32[16,1...) custom-call(f32[1,32]{1,0:T(1,128)S(1)} %negate_power_fusion.inverse, ...), custom_call_target="tpu_custom_call" | custom-call | flops 4000000000 | bytes 28000000 | tf_op jit(solution)/shard_map/prepare/pallas_call | solution.py:296
  23.0 2.6 %collective-permute-done.2.refs_2_ = bf16[64,1792]{1,0:T(8,128)(2,1)} collective-permute-done((bf16[64,1792]{1,0:T(8,128)(2,1)}, bf16[64,1792]{1,0:T(8,128)(2,1)}, u32[]{:S(2)}, u32[]{:S(2)}) %collective-permute-start.2) | collective-permute-done | bytes 229408 | tf_op jit(solution)/shard_map/ppermute | solution.py:21
  25.6 1.6 %collective-permute-done.4.refs_6_ = bf16[2016,128]{1,0:T(8,128)(2,1)} collective-permute-done((bf16[2016,128]{1,0:T(8,128)(2,1)S(1)}, bf16[2016,128]{1,0:T(8,128)(2,1)}, u32[]{:S(2)}, u32[]{:S(2)}) %collective-permute-start.4) | collective-permute-done | bytes 516128 | tf_op jit(solution)/shard_map/ppermute | solution.py:21
  27.2 3.3 %project.1 = (f32[576,128]{1,0:T(8,128)S(1)}, bf16[576,128]{1,0:T(8,128)(2,1)S(1)}, bf16[576,128]{1,0:T(8,128)(2,1)S(1)}, bf16[576,128]{1,0:T(8,128)(2,1)S(1)}) custom-call(s32[1,512]{1,0:T(1,128)S(1)} %get-tuple-element.45.target_ref, bf16[64,1792]{1,0:T(8,128)(2,1)S(1)} %copy-done.5, bf16[64,1792]{1,0:T(8,128)(2,1)S(1)} %collective-permute-done.1.refs_1_, ...), custom_call_target="tpu_custom_call" | custom-call | tf_op jit(solution)/shard_map/project/pallas_call | solution.py:363
  30.5 3.7 %collective-permute-start.6 = (bf16[576,128]{1,0:T(8,128)(2,1)S(1)}, bf16[576,128]{1,0:T(8,128)(2,1)S(1)}, u32[]{:S(2)}, u32[]{:S(2)}) collective-permute-start(bf16[576,128]{1,0:T(8,128)(2,1)S(1)} %get-tuple-element.53), channel_id=1, source_target_pairs={{0,4},{4,0},{8,12},{12,8},{1,5},{5,1},{9,13},{13,9},{2,6},{6,2},{1... | collective-permute-start | bytes 442376 | tf_op jit(solution)/shard_map/ppermute | solution.py:21
  34.2 2.0 %collective-permute-start.7 = (bf16[576,128]{1,0:T(8,128)(2,1)S(1)}, bf16[576,128]{1,0:T(8,128)(2,1)S(1)}, u32[]{:S(2)}, u32[]{:S(2)}) collective-permute-start(bf16[576,128]{1,0:T(8,128)(2,1)S(1)} %get-tuple-element.54), channel_id=1, source_target_pairs={{0,8},{4,12},{8,0},{12,4},{1,9},{5,13},{9,1},{13,5},{2,10},{6,14},... | collective-permute-start | bytes 442376 | tf_op jit(solution)/shard_map/ppermute | solution.py:21
  36.2 1.4 %collective-permute-start.8 = (bf16[576,128]{1,0:T(8,128)(2,1)S(1)}, bf16[576,128]{1,0:T(8,128)(2,1)S(1)}, u32[]{:S(2)}, u32[]{:S(2)}) collective-permute-start(bf16[576,128]{1,0:T(8,128)(2,1)S(1)} %get-tuple-element.55), channel_id=1, source_target_pairs={{0,12},{4,8},{8,4},{12,0},{1,13},{5,9},{9,5},{13,1},{2,14},{6,10},... | collective-permute-start | bytes 442376 | tf_op jit(solution)/shard_map/ppermute | solution.py:21
  37.6 3.3 %collective-permute-done.6.refs_1_ = bf16[576,128]{1,0:T(8,128)(2,1)S(1)} collective-permute-done((bf16[576,128]{1,0:T(8,128)(2,1)S(1)}, bf16[576,128]{1,0:T(8,128)(2,1)S(1)}, u32[]{:S(2)}, u32[]{:S(2)}) %collective-permute-start.6) | collective-permute-done | bytes 147488 | tf_op jit(solution)/shard_map/ppermute | solution.py:21
  40.9 7.1 %collective-permute-done.7.refs_2_ = bf16[576,128]{1,0:T(8,128)(2,1)S(1)} collective-permute-done((bf16[576,128]{1,0:T(8,128)(2,1)S(1)}, bf16[576,128]{1,0:T(8,128)(2,1)S(1)}, u32[]{:S(2)}, u32[]{:S(2)}) %collective-permute-start.7) | collective-permute-done | bytes 147488 | tf_op jit(solution)/shard_map/ppermute | solution.py:21
  48.0 0.3 finish_rows.1.refs_0_
  48.2 0.1 collective-permute-start.11
  48.3 1.4 %collective-permute-start.10 = (bf16[576,128]{1,0:T(8,128)(2,1)S(1)}, bf16[576,128]{1,0:T(8,128)(2,1)S(1)}, u32[]{:S(2)}, u32[]{:S(2)}) collective-permute-start(bf16[576,128]{1,0:T(8,128)(2,1)S(1)} %finish_rows.1.refs_0_), channel_id=1, source_target_pairs={{0,2},{1,3},{2,0},{3,1},{4,6},{5,7},{6,4},{7,5},{8,10},{9,11},{10,... | collective-permute-start | bytes 442376 | tf_op jit(solution)/shard_map/ppermute | solution.py:21
  49.8 0.4 collective-permute-start.9
  50.2 4.3 %collective-permute-done.11.refs_3_ = bf16[576,128]{1,0:T(8,128)(2,1)S(1)} collective-permute-done((bf16[576,128]{1,0:T(8,128)(2,1)S(1)}, bf16[576,128]{1,0:T(8,128)(2,1)S(1)}, u32[]{:S(2)}, u32[]{:S(2)}) %collective-permute-start.11) | collective-permute-done | bytes 147488 | tf_op jit(solution)/shard_map/ppermute | solution.py:21
  54.5 3.0 %collective-permute-done.10.refs_2_ = bf16[576,128]{1,0:T(8,128)(2,1)S(1)} collective-permute-done((bf16[576,128]{1,0:T(8,128)(2,1)S(1)}, bf16[576,128]{1,0:T(8,128)(2,1)S(1)}, u32[]{:S(2)}, u32[]{:S(2)}) %collective-permute-start.10) | collective-permute-done | bytes 147488 | tf_op jit(solution)/shard_map/ppermute | solution.py:21
  57.5 1.3 %attend.3.refs_0_ = bf16[16,2048]{1,0:T(8,128)(2,1)S(1)} custom-call(bf16[512,576]{1,0:T(8,128)(2,1)S(1)} %get-tuple-element.35.query_ref, bf16[16,576]{1,0:T(8,128)(2,1)S(1)} %reshape.26.fresh_ref, s32[1,512]{1,0:T(1,128)S(1)} %get-tuple-element.37.slot_ref, f32[512,128]{1,0:T(8,128)S(1)} %get-tuple-element.38.top_ref, ...), custom_call_target="tpu_custom_call" | custom-call | tf_op jit(solution)/shard_map/attend/pallas_call | solution.py:476
  58.8 3.0 %collective-permute-start.17 = (bf16[16,2048]{1,0:T(8,128)(2,1)S(1)}, bf16[16,2048]{1,0:T(8,128)(2,1)S(1)}, u32[]{:S(2)}, u32[]{:S(2)}) collective-permute-start(bf16[16,2048]{1,0:T(8,128)(2,1)S(1)} %attend.3.refs_0_), channel_id=1, source_target_pairs={{0,12},{4,8},{8,4},{12,0},{1,13},{5,9},{9,5},{13,1},{2,14},{6,10},... | collective-permute-start | bytes 196616 | tf_op jit(solution)/shard_map/ppermute | solution.py:21
  61.9 1.7 %collective-permute-start.16 = (bf16[16,2048]{1,0:T(8,128)(2,1)S(1)}, bf16[16,2048]{1,0:T(8,128)(2,1)S(1)}, u32[]{:S(2)}, u32[]{:S(2)}) collective-permute-start(bf16[16,2048]{1,0:T(8,128)(2,1)S(1)} %attend.3.refs_0_), channel_id=1, source_target_pairs={{0,8},{4,12},{8,0},{12,4},{1,9},{5,13},{9,1},{13,5},{2,10},{6,14},... | collective-permute-start | bytes 196616 | tf_op jit(solution)/shard_map/ppermute | solution.py:21
  63.6 0.5 collective-permute-start.15
  64.0 1.3 %attend.2.refs_0_ = bf16[16,2048]{1,0:T(8,128)(2,1)S(1)} custom-call(bf16[512,576]{1,0:T(8,128)(2,1)S(1)} %get-tuple-element.35.query_ref, bf16[16,576]{1,0:T(8,128)(2,1)S(1)} %reshape.26.fresh_ref, s32[1,512]{1,0:T(1,128)S(1)} %get-tuple-element.37.slot_ref, f32[512,128]{1,0:T(8,128)S(1)} %get-tuple-element.38.top_ref, ...), custom_call_target="tpu_custom_call" | custom-call | tf_op jit(solution)/shard_map/attend/pallas_call | solution.py:476
  65.4 2.4 %collective-permute-start.14 = (bf16[16,2048]{1,0:T(8,128)(2,1)S(1)}, bf16[16,2048]{1,0:T(8,128)(2,1)S(1)}, u32[]{:S(2)}, u32[]{:S(2)}) collective-permute-start(bf16[16,2048]{1,0:T(8,128)(2,1)S(1)} %attend.2.refs_0_), channel_id=1, source_target_pairs={{0,12},{4,8},{8,4},{12,0},{1,13},{5,9},{9,5},{13,1},{2,14},{6,10},... | collective-permute-start | bytes 196616 | tf_op jit(solution)/shard_map/ppermute | solution.py:21
  67.8 0.6 collective-permute-start.13
  68.5 1.4 %collective-permute-start.12 = (bf16[16,2048]{1,0:T(8,128)(2,1)S(1)}, bf16[16,2048]{1,0:T(8,128)(2,1)S(1)}, u32[]{:S(2)}, u32[]{:S(2)}) collective-permute-start(bf16[16,2048]{1,0:T(8,128)(2,1)S(1)} %attend.2.refs_0_), channel_id=1, source_target_pairs={{0,4},{4,0},{8,12},{12,8},{1,5},{5,1},{9,13},{13,9},{2,6},{6,2},{1... | collective-permute-start | bytes 196616 | tf_op jit(solution)/shard_map/ppermute | solution.py:21
  69.9 1.4 %output_product.2.refs_5_ = f32[64,1792]{1,0:T(8,128)S(1)} custom-call(bf16[16,2048]{1,0:T(8,128)(2,1)S(1)} %attend.3.refs_0_, bf16[16,2048]{1,0:T(8,128)(2,1)S(1)} %collective-permute-done.15.refs_1_, bf16[16,2048]{1,0:T(8,128)(2,1)S(1)} %collective-permute-done.16.refs_2_, bf16[16,2048]{1,0:T(8,128)(2,1)S(1)} %collective-permute-done.17.refs_3_, ...), custom_call_target="tpu_custom_call" | custom-call | tf_op jit(solution)/shard_map/output_product/pallas_call | solution.py:530
  71.2 0.9 %collective-permute-done.14.refs_3_ = bf16[16,2048]{1,0:T(8,128)(2,1)S(1)} collective-permute-done((bf16[16,2048]{1,0:T(8,128)(2,1)S(1)}, bf16[16,2048]{1,0:T(8,128)(2,1)S(1)}, u32[]{:S(2)}, u32[]{:S(2)}) %collective-permute-start.14) | collective-permute-done | bytes 65568 | tf_op jit(solution)/shard_map/ppermute | solution.py:21
  72.2 2.6 %collective-permute-done.13.refs_2_ = bf16[16,2048]{1,0:T(8,128)(2,1)S(1)} collective-permute-done((bf16[16,2048]{1,0:T(8,128)(2,1)S(1)}, bf16[16,2048]{1,0:T(8,128)(2,1)S(1)}, u32[]{:S(2)}, u32[]{:S(2)}) %collective-permute-start.13) | collective-permute-done | bytes 65568 | tf_op jit(solution)/shard_map/ppermute | solution.py:21
  74.8 1.4 %output_product.3 = (f32[16,1792]{1,0:T(8,128)S(1)}, bf16[16,1792]{1,0:T(8,128)(2,1)S(1)}, bf16[16,1792]{1,0:T(8,128)(2,1)S(1)}, bf16[16,1792]{1,0:T(8,128)(2,1)S(1)}) custom-call(bf16[16,2048]{1,0:T(8,128)(2,1)S(1)} %attend.2.refs_0_, bf16[16,2048]{1,0:T(8,128)(2,1)S(1)} %collective-permute-done.12.refs_1_, ...), custom_call_target="tpu_custom_call" | custom-call | tf_op jit(solution)/shard_map/output_product/pallas_call | solution.py:530
  76.2 0.1 collective-permute-start.18
  76.3 1.1 %collective-permute-start.19 = (bf16[16,1792]{1,0:T(8,128)(2,1)S(1)}, bf16[16,1792]{1,0:T(8,128)(2,1)S(1)}, u32[]{:S(2)}, u32[]{:S(2)}) collective-permute-start(bf16[16,1792]{1,0:T(8,128)(2,1)S(1)} %get-tuple-element.59), channel_id=1, source_target_pairs={{0,2},{1,3},{2,0},{3,1},{4,6},{5,7},{6,4},{7,5},{8,10},{9,11},{10,... | collective-permute-start | bytes 172040 | tf_op jit(solution)/shard_map/ppermute | solution.py:21
  77.4 0.7 collective-permute-start.20
  78.1 2.4 %collective-permute-done.18 = bf16[16,1792]{1,0:T(8,128)(2,1)S(1)} collective-permute-done((bf16[16,1792]{1,0:T(8,128)(2,1)S(1)}, bf16[16,1792]{1,0:T(8,128)(2,1)S(1)}, u32[]{:S(2)}, u32[]{:S(2)}) %collective-permute-start.18) | collective-permute-done | bytes 57376 | tf_op jit(solution)/shard_map/ppermute | solution.py:21
  80.5 0.6 collective-permute-done.19
  81.1 0.7 add_convert_fusion
  (34 shorter events, 0.1 us)
Async XLA Ops:
  0.0 4.4 %copy-start.10 = (bf16[64,7168]{1,0:T(8,128)(2,1)S(1)}, bf16[64,7168]{1,0:T(8,128)(2,1)}, u32[]{:S(2)}) copy-start(bf16[64,7168]{1,0:T(8,128)(2,1)} %prompts_ref.1) | copy-start | bytes 2752516
  0.0 1.1 %copy-start.11 = (bf16[448,576]{1,0:T(8,128)(2,1)S(1)}, bf16[448,576]{1,0:T(8,128)(2,1)}, u32[]{:S(2)}) copy-start(bf16[448,576]{1,0:T(8,128)(2,1)} %value_ref.1) | copy-start | bytes 1548292
  1.2 9.4 %copy-start.13 = (bf16[8,2,576]{2,1,0:T(2,128)(2,1)S(1)}, bf16[8,2,576]{2,1,0:T(2,128)(2,1)}, u32[]{:S(2)}) copy-start(bf16[8,2,576]{2,1,0:T(2,128)(2,1)} %param.19) | copy-start | bytes 55300
  1.2 9.6 %copy-start.2 = (bf16[8,256,576]{1,2,0:T(8,128)(2,1)S(1)}, bf16[8,256,576]{1,2,0:T(8,128)(2,1)}, u32[]{:S(2)}) copy-start(bf16[8,256,576]{1,2,0:T(8,128)(2,1)} %param.18) | copy-start | bytes 7077892
  1.3 9.6 %copy-start.6 = (s32[1024]{0:T(1024)S(1)}, s32[1024]{0:T(1024)}, u32[]{:S(2)}) copy-start(s32[1024]{0:T(1024)} %param.15) | copy-start | bytes 12292
  1.3 9.6 %copy-start.8 = (s32[16]{0:T(128)S(1)}, s32[16]{0:T(128)}, u32[]{:S(2)}) copy-start(s32[16]{0:T(128)} %length_hbm) | copy-start | bytes 196
  1.3 9.5 %copy-start.9 = (s32[16]{0:T(128)S(1)}, s32[16]{0:T(128)}, u32[]{:S(2)}) copy-start(s32[16]{0:T(128)} %slot_hbm.1) | copy-start | bytes 196
  1.3 24.3 %collective-permute-start.5 = (bf16[2016,128]{1,0:T(8,128)(2,1)S(1)}, bf16[2016,128]{1,0:T(8,128)(2,1)S(1)}, u32[]{:S(2)}, u32[]{:S(2)}) collective-permute-start(bf16[2016,128]{1,0:T(8,128)(2,1)S(1)} %pack_weight.1.refs_4_), channel_id=1, source_target_pairs={{0,3},{1,2},{2,1},{3,0},{4,7},{5,6},{6,5},{7,4},{8,11},{9,10},{10,... | collective-permute-start | bytes 1548296 | tf_op jit(solution)/shard_map/ppermute | solution.py:21
  3.7 23.5 %collective-permute-start.4 = (bf16[2016,128]{1,0:T(8,128)(2,1)S(1)}, bf16[2016,128]{1,0:T(8,128)(2,1)}, u32[]{:S(2)}, u32[]{:S(2)}) collective-permute-start(bf16[2016,128]{1,0:T(8,128)(2,1)S(1)} %pack_weight.1.refs_4_), channel_id=1, source_target_pairs={{0,2},{1,3},{2,0},{3,1},{4,6},{5,7},{6,4},{7,5},{8,10},{9,11},{10,... | collective-permute-start | bytes 1548296 | tf_op jit(solution)/shard_map/ppermute | solution.py:21
  4.4 6.3 %collective-permute-start = (bf16[2016,128]{1,0:T(8,128)(2,1)S(1)}, bf16[2016,128]{1,0:T(8,128)(2,1)}, u32[]{:S(2)}, u32[]{:S(2)}) collective-permute-start(bf16[2016,128]{1,0:T(8,128)(2,1)S(1)} %pack_weight.1.refs_4_), channel_id=1, source_target_pairs={{0,1},{1,0},{2,3},{3,2},{4,5},{5,4},{6,7},{7,6},{8,9},{9,8},{10,11... | collective-permute-start | bytes 1548296 | tf_op jit(solution)/shard_map/ppermute | solution.py:21
  5.4 0.7 copy-start.4
  6.1 2.8 %copy-start.12 = (bf16[64,1792]{1,0:T(8,128)(2,1)}, bf16[64,1792]{1,0:T(8,128)(2,1)S(1)}, u32[]{:S(2)}) copy-start(bf16[64,1792]{1,0:T(8,128)(2,1)S(1)} %get-tuple-element.48) | copy-start | bytes 688132
  6.1 19.5 %collective-permute-start.2 = (bf16[64,1792]{1,0:T(8,128)(2,1)}, bf16[64,1792]{1,0:T(8,128)(2,1)}, u32[]{:S(2)}, u32[]{:S(2)}) collective-permute-start(bf16[64,1792]{1,0:T(8,128)(2,1)} %get-tuple-element.49), channel_id=1, source_target_pairs={{0,8},{4,12},{8,0},{12,4},{1,9},{5,13},{9,1},{13,5},{2,10},{6,14},... | collective-permute-start | bytes 688136 | tf_op jit(solution)/shard_map/ppermute | solution.py:21
  9.0 16.7 %collective-permute-start.3 = (bf16[64,1792]{1,0:T(8,128)(2,1)}, bf16[64,1792]{1,0:T(8,128)(2,1)}, u32[]{:S(2)}, u32[]{:S(2)}) collective-permute-start(bf16[64,1792]{1,0:T(8,128)(2,1)} %get-tuple-element.50), channel_id=1, source_target_pairs={{0,12},{4,8},{8,4},{12,0},{1,13},{5,9},{9,5},{13,1},{2,14},{6,10},... | collective-permute-start | bytes 688136 | tf_op jit(solution)/shard_map/ppermute | solution.py:21
  10.7 16.5 %collective-permute-start.1 = (bf16[64,1792]{1,0:T(8,128)(2,1)}, bf16[64,1792]{1,0:T(8,128)(2,1)S(1)}, u32[]{:S(2)}, u32[]{:S(2)}) collective-permute-start(bf16[64,1792]{1,0:T(8,128)(2,1)} %copy-done.12), channel_id=1, source_target_pairs={{0,4},{4,0},{8,12},{12,8},{1,5},{5,1},{9,13},{13,9},{2,6},{6,2},{1... | collective-permute-start | bytes 688136 | tf_op jit(solution)/shard_map/ppermute | solution.py:21
  10.8 2.2 %copy-start = (bf16[32,128,512]{2,1,0:T(8,128)(2,1)S(1)}, bf16[32,128,512]{2,1,0:T(8,128)(2,1)}, u32[]{:S(2)}) copy-start(bf16[32,128,512]{2,1,0:T(8,128)(2,1)} %absorb_hbm.1) | copy-start | bytes 12582916
  13.0 2.2 %copy-start.1 = (bf16[32,512,128]{2,1,0:T(8,128)(2,1)S(1)}, bf16[32,512,128]{2,1,0:T(8,128)(2,1)}, u32[]{:S(2)}) copy-start(bf16[32,512,128]{2,1,0:T(8,128)(2,1)} %value_hbm.1) | copy-start | bytes 12582916
  15.2 0.9 %copy-start.3 = (bf16[8,2,32,192]{3,2,1,0:T(8,128)(2,1)S(1)}, bf16[8,2,32,192]{3,2,1,0:T(8,128)(2,1)}, u32[]{:S(2)}) copy-start(bf16[8,2,32,192]{3,2,1,0:T(8,128)(2,1)} %param.20) | copy-start | bytes 589828
  16.2 11.0 %copy-start.5 = (bf16[64,1792]{1,0:T(8,128)(2,1)S(1)}, bf16[64,1792]{1,0:T(8,128)(2,1)}, u32[]{:S(2)}) copy-start(bf16[64,1792]{1,0:T(8,128)(2,1)} %copy-done.4) | copy-start | bytes 688132
  16.2 31.8 %copy-start.7 = (f32[512]{0:T(512)S(1)}, f32[512]{0:T(512)}, u32[]{:S(2)}) copy-start(f32[512]{0:T(512)} %param.14) | copy-start | bytes 6148
  30.5 10.4 %collective-permute-start.6 = (bf16[576,128]{1,0:T(8,128)(2,1)S(1)}, bf16[576,128]{1,0:T(8,128)(2,1)S(1)}, u32[]{:S(2)}, u32[]{:S(2)}) collective-permute-start(bf16[576,128]{1,0:T(8,128)(2,1)S(1)} %get-tuple-element.53), channel_id=1, source_target_pairs={{0,4},{4,0},{8,12},{12,8},{1,5},{5,1},{9,13},{13,9},{2,6},{6,2},{1... | collective-permute-start | bytes 442376 | tf_op jit(solution)/shard_map/ppermute | solution.py:21
  34.2 13.8 %collective-permute-start.7 = (bf16[576,128]{1,0:T(8,128)(2,1)S(1)}, bf16[576,128]{1,0:T(8,128)(2,1)S(1)}, u32[]{:S(2)}, u32[]{:S(2)}) collective-permute-start(bf16[576,128]{1,0:T(8,128)(2,1)S(1)} %get-tuple-element.54), channel_id=1, source_target_pairs={{0,8},{4,12},{8,0},{12,4},{1,9},{5,13},{9,1},{13,5},{2,10},{6,14},... | collective-permute-start | bytes 442376 | tf_op jit(solution)/shard_map/ppermute | solution.py:21
  36.2 11.8 %collective-permute-start.8 = (bf16[576,128]{1,0:T(8,128)(2,1)S(1)}, bf16[576,128]{1,0:T(8,128)(2,1)S(1)}, u32[]{:S(2)}, u32[]{:S(2)}) collective-permute-start(bf16[576,128]{1,0:T(8,128)(2,1)S(1)} %get-tuple-element.55), channel_id=1, source_target_pairs={{0,12},{4,8},{8,4},{12,0},{1,13},{5,9},{9,5},{13,1},{2,14},{6,10},... | collective-permute-start | bytes 442376 | tf_op jit(solution)/shard_map/ppermute | solution.py:21
  48.2 6.2 %collective-permute-start.11 = (bf16[576,128]{1,0:T(8,128)(2,1)S(1)}, bf16[576,128]{1,0:T(8,128)(2,1)S(1)}, u32[]{:S(2)}, u32[]{:S(2)}) collective-permute-start(bf16[576,128]{1,0:T(8,128)(2,1)S(1)} %finish_rows.1.refs_0_), channel_id=1, source_target_pairs={{0,3},{1,2},{2,1},{3,0},{4,7},{5,6},{6,5},{7,4},{8,11},{9,10},{10,... | collective-permute-start | bytes 442376 | tf_op jit(solution)/shard_map/ppermute | solution.py:21
  48.3 9.2 %collective-permute-start.10 = (bf16[576,128]{1,0:T(8,128)(2,1)S(1)}, bf16[576,128]{1,0:T(8,128)(2,1)S(1)}, u32[]{:S(2)}, u32[]{:S(2)}) collective-permute-start(bf16[576,128]{1,0:T(8,128)(2,1)S(1)} %finish_rows.1.refs_0_), channel_id=1, source_target_pairs={{0,2},{1,3},{2,0},{3,1},{4,6},{5,7},{6,4},{7,5},{8,10},{9,11},{10,... | collective-permute-start | bytes 442376 | tf_op jit(solution)/shard_map/ppermute | solution.py:21
  49.8 7.7 %collective-permute-start.9 = (bf16[576,128]{1,0:T(8,128)(2,1)S(1)}, bf16[576,128]{1,0:T(8,128)(2,1)S(1)}, u32[]{:S(2)}, u32[]{:S(2)}) collective-permute-start(bf16[576,128]{1,0:T(8,128)(2,1)S(1)} %finish_rows.1.refs_0_), channel_id=1, source_target_pairs={{0,1},{1,0},{2,3},{3,2},{4,5},{5,4},{6,7},{7,6},{8,9},{9,8},{10,11... | collective-permute-start | bytes 442376 | tf_op jit(solution)/shard_map/ppermute | solution.py:21
  58.8 9.6 %collective-permute-start.17 = (bf16[16,2048]{1,0:T(8,128)(2,1)S(1)}, bf16[16,2048]{1,0:T(8,128)(2,1)S(1)}, u32[]{:S(2)}, u32[]{:S(2)}) collective-permute-start(bf16[16,2048]{1,0:T(8,128)(2,1)S(1)} %attend.3.refs_0_), channel_id=1, source_target_pairs={{0,12},{4,8},{8,4},{12,0},{1,13},{5,9},{9,5},{13,1},{2,14},{6,10},... | collective-permute-start | bytes 196616 | tf_op jit(solution)/shard_map/ppermute | solution.py:21
  61.9 8.0 %collective-permute-start.16 = (bf16[16,2048]{1,0:T(8,128)(2,1)S(1)}, bf16[16,2048]{1,0:T(8,128)(2,1)S(1)}, u32[]{:S(2)}, u32[]{:S(2)}) collective-permute-start(bf16[16,2048]{1,0:T(8,128)(2,1)S(1)} %attend.3.refs_0_), channel_id=1, source_target_pairs={{0,8},{4,12},{8,0},{12,4},{1,9},{5,13},{9,1},{13,5},{2,10},{6,14},... | collective-permute-start | bytes 196616 | tf_op jit(solution)/shard_map/ppermute | solution.py:21
  63.6 6.3 %collective-permute-start.15 = (bf16[16,2048]{1,0:T(8,128)(2,1)S(1)}, bf16[16,2048]{1,0:T(8,128)(2,1)S(1)}, u32[]{:S(2)}, u32[]{:S(2)}) collective-permute-start(bf16[16,2048]{1,0:T(8,128)(2,1)S(1)} %attend.3.refs_0_), channel_id=1, source_target_pairs={{0,4},{4,0},{8,12},{12,8},{1,5},{5,1},{9,13},{13,9},{2,6},{6,2},{1... | collective-permute-start | bytes 196616 | tf_op jit(solution)/shard_map/ppermute | solution.py:21
  65.4 6.8 %collective-permute-start.14 = (bf16[16,2048]{1,0:T(8,128)(2,1)S(1)}, bf16[16,2048]{1,0:T(8,128)(2,1)S(1)}, u32[]{:S(2)}, u32[]{:S(2)}) collective-permute-start(bf16[16,2048]{1,0:T(8,128)(2,1)S(1)} %attend.2.refs_0_), channel_id=1, source_target_pairs={{0,12},{4,8},{8,4},{12,0},{1,13},{5,9},{9,5},{13,1},{2,14},{6,10},... | collective-permute-start | bytes 196616 | tf_op jit(solution)/shard_map/ppermute | solution.py:21
  67.8 7.0 %collective-permute-start.13 = (bf16[16,2048]{1,0:T(8,128)(2,1)S(1)}, bf16[16,2048]{1,0:T(8,128)(2,1)S(1)}, u32[]{:S(2)}, u32[]{:S(2)}) collective-permute-start(bf16[16,2048]{1,0:T(8,128)(2,1)S(1)} %attend.2.refs_0_), channel_id=1, source_target_pairs={{0,8},{4,12},{8,0},{12,4},{1,9},{5,13},{9,1},{13,5},{2,10},{6,14},... | collective-permute-start | bytes 196616 | tf_op jit(solution)/shard_map/ppermute | solution.py:21
  68.5 6.3 %collective-permute-start.12 = (bf16[16,2048]{1,0:T(8,128)(2,1)S(1)}, bf16[16,2048]{1,0:T(8,128)(2,1)S(1)}, u32[]{:S(2)}, u32[]{:S(2)}) collective-permute-start(bf16[16,2048]{1,0:T(8,128)(2,1)S(1)} %attend.2.refs_0_), channel_id=1, source_target_pairs={{0,4},{4,0},{8,12},{12,8},{1,5},{5,1},{9,13},{13,9},{2,6},{6,2},{1... | collective-permute-start | bytes 196616 | tf_op jit(solution)/shard_map/ppermute | solution.py:21
  76.2 4.3 %collective-permute-start.18 = (bf16[16,1792]{1,0:T(8,128)(2,1)S(1)}, bf16[16,1792]{1,0:T(8,128)(2,1)S(1)}, u32[]{:S(2)}, u32[]{:S(2)}) collective-permute-start(bf16[16,1792]{1,0:T(8,128)(2,1)S(1)} %get-tuple-element.58), channel_id=1, source_target_pairs={{0,3},{1,2},{2,1},{3,0},{4,7},{5,6},{6,5},{7,4},{8,11},{9,10},{10,... | collective-permute-start | bytes 172040 | tf_op jit(solution)/shard_map/ppermute | solution.py:21
  76.3 4.8 %collective-permute-start.19 = (bf16[16,1792]{1,0:T(8,128)(2,1)S(1)}, bf16[16,1792]{1,0:T(8,128)(2,1)S(1)}, u32[]{:S(2)}, u32[]{:S(2)}) collective-permute-start(bf16[16,1792]{1,0:T(8,128)(2,1)S(1)} %get-tuple-element.59), channel_id=1, source_target_pairs={{0,2},{1,3},{2,0},{3,1},{4,6},{5,7},{6,4},{7,5},{8,10},{9,11},{10,... | collective-permute-start | bytes 172040 | tf_op jit(solution)/shard_map/ppermute | solution.py:21
  77.4 3.7 %collective-permute-start.20 = (bf16[16,1792]{1,0:T(8,128)(2,1)S(1)}, bf16[16,1792]{1,0:T(8,128)(2,1)S(1)}, u32[]{:S(2)}, u32[]{:S(2)}) collective-permute-start(bf16[16,1792]{1,0:T(8,128)(2,1)S(1)} %get-tuple-element.60), channel_id=1, source_target_pairs={{0,1},{1,0},{2,3},{3,2},{4,5},{5,4},{6,7},{7,6},{8,9},{9,8},{10,11... | collective-permute-start | bytes 172040 | tf_op jit(solution)/shard_map/ppermute | solution.py:21

commit v6 on v5

--- a/solution.py
+++ b/solution.py
@@ -120,7 +120,9 @@
     lane_rows, lanes = requests.shape
     tok_rows = bucket * dev_count // 2
     per_row = lanes // tok_rows
-    group_rows = dev_count * bucket
+    half_bucket = bucket // 2
+    half_rows = dev_count * half_bucket
+    group_rows = 2 * half_rows
     before = lax.broadcasted_iota(jnp.int32, (lanes, lanes), 0)
     after = lax.broadcasted_iota(jnp.int32, (lanes, lanes), 1)
     below = jnp.where(before < after, 1.0, 0.0)
@@ -151,8 +153,11 @@
     block = lax.broadcasted_iota(jnp.int32, requests.shape, 0) * per_row + lax.div(
         lax.broadcasted_iota(jnp.int32, requests.shape, 1), tok_rows
     )
-    place = lax.div(block, side_count) * bucket + rank.astype(jnp.int32)
-    to_ref[...] = (group ^ my_dev) * group_rows + place
+    rank = rank.astype(jnp.int32)
+    which = lax.div(rank, half_bucket)
+    place = lax.div(block, side_count) * half_bucket + lax.rem(rank, half_bucket)
+    to_ref[...] = (which * dev_count + (group ^ my_dev)) * half_rows + place
+    place = which * half_rows + place
     place_ref[...] = jnp.where(group == my_dev, place, -1)
     local_ref[...] = (slot - my_dev * cap_slots + 1).astype(f32)
     position_ref[...] = position
@@ -163,9 +168,16 @@
         held = dev * side_count + side
         return pl.ds(lax.div(held, per_row), 1), lane_block == lax.rem(held, per_row)
 
+    targets = []
     for k in range(dev_count):
-        row, inside = find(my_dev ^ k, my_side)
-        target_ref[:, k * lanes : (k + 1) * lanes] = jnp.where(inside, to_ref[row, :], -1)
+        held = (my_dev ^ k) * side_count + my_side
+        row = jnp.broadcast_to(to_ref[pl.ds(lax.div(held, per_row), 1), :], (8, lanes))
+        start = lax.rem(lanes - tok_rows * lax.rem(held, per_row), lanes)
+        targets.append(pltpu.roll(row, start, 1)[:1, :tok_rows])
+    for k in range(0, dev_count, per_row):
+        target_ref[:, k * tok_rows : k * tok_rows + lanes] = jnp.concatenate(
+            targets[k : k + per_row], axis=1
+        )
     found = jnp.zeros((group_rows, lanes), f32)
     for d in range(dev_count):
         row, inside = find(d, my_side)
@@ -187,14 +199,14 @@
 
 def prepare_kernel(
     scale, steps, layout, inverse_ref, length_hbm, slot_hbm, request_hbm, query_hbm, absorb_hbm,
-    cache_hbm, value_hbm, out_hbm, full_ref, top_ref, sum_ref, mix_ref, live_ref, target_ref,
+    cache_hbm, fresh_hbm, value_hbm, out_hbm, full_ref, top_ref, sum_ref, mix_ref, live_ref, target_ref,
     cos_ref, sin_ref, spot_ref, value_ref, out_ref, length_ref, slot_ref, request_ref, query_ref,
-    absorb_ref, cache_ref, plain, full, to_ref, place_ref, local_ref, position_ref, sems,
+    absorb_ref, cache_ref, fresh_ref, plain, full, to_ref, place_ref, local_ref, position_ref, sems,
 ):
     pairs = [
         (length_hbm, length_ref), (slot_hbm, slot_ref), (request_hbm, request_ref),
         (query_hbm, query_ref), (absorb_hbm, absorb_ref), (cache_hbm, cache_ref),
-        (value_hbm, value_ref),
+        (fresh_hbm, fresh_ref), (value_hbm, value_ref),
     ]
     parts = sems.shape[0] - len(pairs)
     rows = out_hbm.shape[0] // parts
@@ -242,6 +254,9 @@
         full_ref[:, lanes] = full[n, :, : lanes.stop - lanes.start].astype(bf16)
     key = lax.broadcasted_iota(jnp.int32, (1, context), 1)
     copies[5].wait()
+    copies[6].wait()
+    late = lax.broadcasted_iota(jnp.int32, (steps * heads, steps), 1)
+    late = late > lax.div(lax.broadcasted_iota(jnp.int32, (steps * heads, steps), 0), heads)
     for s in range(slots):
         theres = [pl.ds(s * steps + t, heads, stride=per_head) for t in range(steps)]
         query = jnp.concatenate(
@@ -256,13 +271,25 @@
         rows = cache_ref[s]
         score = jnp.dot(query, rows, preferred_element_type=f32)
         score = jnp.where(key < lengths[s], score * scale, masked_score)
-        top = jnp.max(score, axis=1, keepdims=True)
+        fresh = fresh_ref[s]
+        new = lax.dot_general(
+            query, fresh, (((1,), (1,)), ((), ())), preferred_element_type=f32
+        )
+        new = jnp.where(late, masked_score, new * scale)
+        top = jnp.maximum(
+            jnp.max(score, axis=1, keepdims=True), jnp.max(new, axis=1, keepdims=True)
+        )
         weight = jnp.exp(score - top)
-        total = jnp.sum(weight, axis=1, keepdims=True)
+        new = jnp.exp(new - top)
+        total = jnp.sum(weight, axis=1, keepdims=True) + jnp.sum(new, axis=1, keepdims=True)
         mix = lax.dot_general(
             weight.astype(bf16), rows[:lat_width, :], (((1,), (1,)), ((), ())),
             preferred_element_type=f32,
         )
+        for u in range(steps):
+            mix = mix + new[:, u : u + 1].astype(bf16).astype(f32) * fresh[
+                u : u + 1, :lat_width
+            ].astype(f32)
         lanes = top_ref.shape[1]
         for t in range(steps):
             there = theres[t]
@@ -271,13 +298,13 @@
             sum_ref[there, :] = jnp.broadcast_to(total[here], (heads, lanes))
             for n, part in enumerate(lane_tiles(lat_width)):
                 mix_ref[n, there, :] = mix[here, part]
-    for copy in copies[6:]:
+    for copy in copies[7:]:
         copy.wait()
 
 
 def prepare(
     scale, dev_count, side_count, bucket, lengths, request_slot, requests, inverse, queries,
-    absorb, cache, value, out_weight,
+    absorb, cache, fresh, value, out_weight,
 ):
     slots, steps, heads, width = queries.shape
     kv_width = cache.shape[1]
@@ -290,13 +317,13 @@
     shapes = [
         ((rows, kv_width), bf16), ((rows, 128), f32), ((rows, 128), f32),
         ((lat_width // 128, rows, 128), f32), ((slots * steps, 128), f32),
-        ((1, dev_count * lanes), jnp.int32), ((group_rows, half), f32), ((group_rows, half), f32),
+        ((1, group_rows // 2 * dev_count), jnp.int32), ((group_rows, half), f32), ((group_rows, half), f32),
         ((1, side_count * group_rows), jnp.int32), (value.shape, bf16), (out_weight.shape, bf16),
     ]
     return pl.pallas_call(
         functools.partial(prepare_kernel, scale, steps, (dev_count, side_count, bucket)),
         out_shape=[jax.ShapeDtypeStruct(*shape) for shape in shapes],
-        in_specs=[in_vmem] + [in_hbm] * 8,
+        in_specs=[in_vmem] + [in_hbm] * 9,
         out_specs=[in_vmem] * len(shapes),
         scratch_shapes=[
             pltpu.SMEM(lengths.shape, lengths.dtype),
@@ -305,21 +332,22 @@
             pltpu.VMEM((rows, width), queries.dtype),
             pltpu.VMEM(absorb.shape, absorb.dtype),
             pltpu.VMEM(cache.shape, cache.dtype),
+            pltpu.VMEM(fresh.shape, fresh.dtype),
             pltpu.VMEM((len(lane_tiles(width)), rows, 128), f32),
             pltpu.VMEM((len(lane_tiles(kv_width)), rows, 128), f32),
             pltpu.VMEM(requests.shape, jnp.int32),
             pltpu.VMEM(requests.shape, jnp.int32),
             pltpu.VMEM(requests.shape, f32),
             pltpu.VMEM(requests.shape, f32),
-            pltpu.SemaphoreType.DMA((parts + 7,)),
+            pltpu.SemaphoreType.DMA((parts + 8,)),
         ],
         compiler_params=pltpu.CompilerParams(vmem_limit_bytes=prepare_mib * mib),
         cost_estimate=pl.CostEstimate(
             flops=4 * 10**9, bytes_accessed=28 * 10**6, transcendentals=10**5
         ),
         name="prepare",
-    )(inverse, lengths, request_slot, requests, queries.reshape(rows, width), absorb, cache, value,
-      out_weight)
+    )(inverse, lengths, request_slot, requests, queries.reshape(rows, width), absorb, cache, fresh,
+      value, out_weight)
 
 
 def project_kernel(dev_count, side_count, target_ref, *refs):
@@ -342,19 +370,13 @@
         x_rows[k * tok_rows : (k + 1) * tok_rows, :] = x_refs[k][...]
     slab = slab_weight[...] if side_count > 1 else weight_refs[0][...]
     raw = jnp.dot(x_rows[...], slab, preferred_element_type=f32).astype(bf16)
-    copies = target_ref.shape[1] // (dev_count * tok_rows)
-    for k in range(dev_count):
-        for n in range(k * copies, (k + 1) * copies):
-            rows[n * tok_rows : (n + 1) * tok_rows, :] = raw[k * tok_rows : (k + 1) * tok_rows, :]
+    rows[...] = raw
     target = target_ref[...]
-    group_rows = 2 * tok_rows
-    step = max(1, min(dev_count, 512 // group_rows))
-    for j in range(0, dev_count, step):
-        ids = lax.broadcasted_iota(jnp.int32, (step * group_rows, target.shape[1]), 0)
-        route = jnp.where(ids + j * group_rows == target, 1.0, 0.0).astype(bf16)
-        placed = jnp.dot(route, rows[...], preferred_element_type=f32)
-        for n in range(step):
-            store_packed(out_refs[j + n], placed[n * group_rows : (n + 1) * group_rows])
+    half_rows = tok_rows
+    for j in range(2 * dev_count):
+        ids = lax.broadcasted_iota(jnp.int32, (half_rows, target.shape[1]), 0)
+        route = jnp.where(ids + j * half_rows == target, 1.0, 0.0).astype(bf16)
+        store_packed(out_refs[j], jnp.dot(route, rows[...], preferred_element_type=f32))
 
 
 def project(x_pieces, weights, target, width):
@@ -363,11 +385,13 @@
     return pl.pallas_call(
         functools.partial(project_kernel, dev_count, len(weights)),
         out_shape=[
-            jax.ShapeDtypeStruct((packed_rows(2 * tok_rows, width), 128), f32 if j == 0 else bf16)
-            for j in range(dev_count)
+            jax.ShapeDtypeStruct(
+                (packed_rows(tok_rows, width), 128), f32 if j % dev_count == 0 else bf16
+            )
+            for j in range(2 * dev_count)
         ],
         in_specs=[in_vmem] * (1 + dev_count + len(weights)),
-        out_specs=[in_vmem] * dev_count,
+        out_specs=[in_vmem] * (2 * dev_count),
         scratch_shapes=[
             pltpu.VMEM((dev_count * tok_rows, slab), bf16),
             pltpu.VMEM((slab, width), bf16),
@@ -378,9 +402,10 @@
     )(target, *x_pieces, *weights)
 
 
-def finish_kernel(gain_ref, cos_ref, sin_ref, *refs):
+def finish_kernel(which, gain_ref, cos_ref, sin_ref, *refs):
     parts, out_ref = refs[:-1], refs[-1]
-    rows, half = cos_ref.shape
+    rows, half = cos_ref.shape[0] // 2, cos_ref.shape[1]
+    mine = slice(which * rows, (which + 1) * rows)
     total = parts[0][...].astype(f32)
     for part in parts[1:]:
         total = total + part[...].astype(f32)
@@ -389,7 +414,7 @@
     spread = jnp.mean(latent * latent, axis=1, keepdims=True)
     latent = latent * lax.rsqrt(spread + 1e-06) * gain_ref[...]
     first, second = rest[:, :half], rest[:, half:]
-    cosine, sine = cos_ref[...], sin_ref[...]
+    cosine, sine = cos_ref[mine, :], sin_ref[mine, :]
     store_packed(
         out_ref,
         jnp.concatenate(
@@ -398,9 +423,9 @@
     )
 
 
-def finish(parts, gain, cosine, sine):
+def finish(parts, gain, cosine, sine, which):
     return pl.pallas_call(
-        finish_kernel,
+        functools.partial(finish_kernel, which),
         out_shape=jax.ShapeDtypeStruct(parts[0].shape, bf16),
         in_specs=[in_vmem] * (3 + len(parts)),
         out_specs=in_vmem,
@@ -410,7 +435,7 @@
 
 
 def attend_kernel(
-    scale, cap_slots, steps, part, parts, query_ref, fresh_ref, slot_ref, top_ref,
+    scale, cap_slots, steps, part, parts, query_ref, slot_ref, top_ref,
     sum_ref, mix_ref, live_ref, value_ref, *refs
 ):
     pieces, out_ref, keys = refs[:-2], refs[-2], refs[-1]
@@ -419,41 +444,29 @@
     rows = query_ref.shape[0] // parts
     heads = rows // per_head
     mine = slice(part * rows, (part + 1) * rows)
+    sides = len(pieces) // 2
     piece_rows = keys.shape[0] // len(pieces)
     for n, piece in enumerate(pieces):
         tiles, rest = load_packed(piece, piece_rows)
-        there = slice(n * piece_rows, (n + 1) * piece_rows)
+        place = (n % sides) * 2 + n // sides
+        there = slice(place * piece_rows, (place + 1) * piece_rows)
         for j, tile in enumerate(tiles):
             keys[there, j * 128 : (j + 1) * 128] = tile
         keys[there, lat_width:] = rest
     contract = (((1,), (1,)), ((), ()))
     row = lax.broadcasted_iota(jnp.int32, (rows, 1), 0)
     row_slot = (row // steps) % cap_slots
-    key = lax.broadcasted_iota(jnp.int32, (1, per_head), 1)
-    see_fresh = (key // steps == row_slot) & (key % steps <= row % steps)
     query = query_ref[mine, :]
-    fresh = lax.dot_general(query, fresh_ref[...], contract, preferred_element_type=f32)
-    fresh = jnp.where(see_fresh, fresh * scale, masked_score)
     score = lax.dot_general(query, keys[...], contract, preferred_element_type=f32)
     score = jnp.where(
         slot_ref[...] == row_slot + 1, score * scale, masked_score
     )
     top_held = top_ref[mine, :1]
-    top = jnp.maximum(
-        jnp.maximum(top_held, jnp.max(fresh, axis=1, keepdims=True)),
-        jnp.max(score, axis=1, keepdims=True),
-    )
+    top = jnp.maximum(top_held, jnp.max(score, axis=1, keepdims=True))
     held = jnp.exp(top_held - top)
-    weight_fresh = jnp.exp(fresh - top)
     weight = jnp.exp(score - top)
-    total = (
-        sum_ref[mine, :1] * held
-        + jnp.sum(weight_fresh, axis=1, keepdims=True)
-        + jnp.sum(weight, axis=1, keepdims=True)
-    )
-    mix = jnp.dot(
-        weight_fresh.astype(bf16), fresh_ref[:, :lat_width], preferred_element_type=f32
-    ) + jnp.dot(weight.astype(bf16), keys[:, :lat_width], preferred_element_type=f32)
+    total = sum_ref[mine, :1] * held + jnp.sum(weight, axis=1, keepdims=True)
+    mix = jnp.dot(weight.astype(bf16), keys[:, :lat_width], preferred_element_type=f32)
     mix_held = jnp.concatenate([mix_ref[n, mine, :] for n in range(mix_ref.shape[0])], axis=1)
     latent = ((mix_held * held + mix) / total).astype(bf16)
     live = live_ref[:, :1]
@@ -468,20 +481,19 @@
         out_ref[:, (h + 1) * width : (h + 2) * width] = (both[per_head:, width:] * live).astype(bf16)
 
 
-def attend(scale, query, fresh, row_slot, top, total, mix, live, value, pieces, cap_slots,
-           part, parts):
+def attend(scale, query, row_slot, top, total, mix, live, value, pieces, cap_slots, steps, part,
+           parts):
     heads, _, width = value.shape
-    steps = fresh.shape[0] // cap_slots
     part_heads = heads // parts
     return pl.pallas_call(
         functools.partial(attend_kernel, scale, cap_slots, steps, part, parts),
         out_shape=jax.ShapeDtypeStruct((cap_slots * steps, part_heads * width), bf16),
-        in_specs=[in_vmem] * (8 + len(pieces)),
+        in_specs=[in_vmem] * (7 + len(pieces)),
         out_specs=in_vmem,
         scratch_shapes=[pltpu.VMEM((row_slot.shape[1], query.shape[1]), bf16)],
         compiler_params=pltpu.CompilerParams(vmem_limit_bytes=10 * mib),
         name="attend",
-    )(query, fresh, row_slot, top, total, mix, live, value, *pieces)
+    )(query, row_slot, top, total, mix, live, value, *pieces)
 
 
 def output_kernel(dev_count, side_count, part, parts, *refs):
@@ -578,16 +590,14 @@
     score_scale = queries.shape[-1] ** (-0.5)
     half = rope_width // 2
     inverse = 1.0 / 10000.0 ** (jnp.arange(half, dtype=f32) * (2.0 / rope_width))
-    fresh, lengths, x_pieces[0] = lax.optimization_barrier(
-        (new_latent.reshape(-1, kv_width), context_len, x_pieces[0])
-    )
+    lengths, x_pieces[0] = lax.optimization_barrier((context_len, x_pieces[0]))
     (
         query_full, top_held, sum_held, mix_held, live, target, cosine, sine, row_slot,
         value_here, out_here,
     ) = prepare(
         score_scale, dev_count, side_count, bucket_rows, lengths, request_slot,
         row_request.reshape(-1, 128), inverse.reshape(1, -1), queries, key_absorb,
-        jnp.swapaxes(latent_cache, 1, 2), value_absorb, out_weight,
+        jnp.swapaxes(latent_cache, 1, 2), new_latent, value_absorb, out_weight,
     )
 
     if not packs:
@@ -598,16 +608,18 @@
         weights = [held.reshape(slab, kv_width)]
 
     routed = project(x_pieces, weights, target, kv_width)
-    parts = [routed[0]] + [None] * (dev_count - 1)
-    for k in sorted(range(1, dev_count), reverse=True):
-        parts[k] = swap(routed[k], "dev", k)
-    latent_rows = finish(parts, latent_gain.reshape(1, -1), cosine, sine)
-    pieces = [latent_rows] + [swap(latent_rows, "side", k) for k in range(1, side_count)]
+    pieces = []
+    for which in range(2):
+        half = list(routed[which * dev_count : (which + 1) * dev_count])
+        for k in sorted(range(1, dev_count), reverse=True):
+            half[k] = swap(half[k], "dev", k)
+        latent_rows = finish(half, latent_gain.reshape(1, -1), cosine, sine, which)
+        pieces += [latent_rows] + [swap(latent_rows, "side", k) for k in range(1, side_count)]
     product, parts = None, 2
     for part in range(parts):
         head_out = attend(
-            score_scale, query_full, fresh, row_slot, top_held,
-            sum_held, mix_held, live, value_here, pieces, cap_slots, part, parts,
+            score_scale, query_full, row_slot, top_held, sum_held, mix_held, live, value_here,
+            pieces, cap_slots, step_count, part, parts,
         )
         heads = [head_out] + [None] * (dev_count - 1)
         for k in sorted(range(1, dev_count), reverse=True):

time: 82 us -> 77.8 us (0.949)
  local copies, waits for them, and re-layouts: 7.25 us -> 1.2 us
  starting transfers between devices: 28.3 us -> 32.1 us
  Pallas kernels: 16.9 us -> 15.8 us
    unnamed x28 -> x22, local copies, waits for them, and re-layouts: 7.22 us -> 1.2 us
    ppermute x21 -> x27, starting transfers between devices: 28.3 us -> 32.1 us  [swap(): return lax.ppermute(value, axis, [(i, i ^ step) for i in range(count)])]
    pallas_call x1, Pallas kernels: 3.3 us -> 1.96 us  [project(): pl.pallas_call(functools.partial(project_kernel, dev_count, len(weights))...]
    ppermute x21 -> x27, waiting for transfers between devices: 28.4 us -> 27.8 us  [swap(): return lax.ppermute(value, axis, [(i, i ^ step) for i in range(count)])]
  transfers between devices with their start and end apart: 21 -> 27, of which waited for: 10 -> 11; matrix products, arithmetic and copies ran while one was open for 0% -> 0% of each run, Pallas kernels for 13% -> 14%
where the time goes in v6:
time: 77.8 us; the launch traced here: 77.7 us
  starting transfers between devices  32.1 us (41%)
  waiting for transfers between devices  27.8 us (36%)
  Pallas kernels  15.8 us (20%)
  local copies, waits for them, and re-layouts  1.2 us (2%)
    ppermute x27, starting transfers between devices, swap(): return lax.ppermute(value, axis, [(i, i ^ step) for i in range(count)])  32.1 us
    ppermute x27, waiting for transfers between devices, swap(): return lax.ppermute(value, axis, [(i, i ^ step) for i in range(count)])  27.8 us
    pallas_call x1, Pallas kernels, prepare(): pl.pallas_call(functools.partial(prepare_kernel, scale, steps, (dev_count...  7.61 us
    pallas_call x2, Pallas kernels, output_product(): pl.pallas_call(functools.partial(output_kernel, dev_count, side_count, pa...  2.84 us
    pallas_call x2, Pallas kernels, attend(): pl.pallas_call(functools.partial(attend_kernel, scale, cap_slots, steps,...  2.65 us
    pallas_call x1, Pallas kernels, project(): pl.pallas_call(functools.partial(project_kernel, dev_count, len(weights))...  1.96 us
  transfers between devices with their start and end apart: 27, of which 11 were waited for; matrix products, arithmetic and copies ran while one was open for 0% of the time, Pallas kernels for 14%

profile of v6, /device:TPU:0, one launch (start us, length us, event | category | flops | bytes accessed | tf_op | source)
XLA Modules:
  0.0 77.7 jit_solution(13035102458053474981)
XLA Ops:
  0.0 1.1 %copy-done.10 = bf16[448,576]{1,0:T(8,128)(2,1)S(1)} copy-done((bf16[448,576]{1,0:T(8,128)(2,1)S(1)}, bf16[448,576]{1,0:T(8,128)(2,1)}, u32[]{:S(2)}) %copy-start.10) | copy-done | bytes 516120
  1.1 0.1 pack_weight.1.refs_4_
  1.3 2.4 %collective-permute-start.5 = (bf16[2016,128]{1,0:T(8,128)(2,1)S(1)}, bf16[2016,128]{1,0:T(8,128)(2,1)S(1)}, u32[]{:S(2)}, u32[]{:S(2)}) collective-permute-start(bf16[2016,128]{1,0:T(8,128)(2,1)S(1)} %pack_weight.1.refs_4_), channel_id=1, source_target_pairs={{0,3},{1,2},{2,1},{3,0},{4,7},{5,6},{6,5},{7,4},{8,11},{9,10},{10,... | collective-permute-start | bytes 1548296 | tf_op jit(solution)/shard_map/ppermute | solution.py:21
  3.8 0.6 collective-permute-start.4
  4.5 0.2 split_columns.1
  4.7 2.9 %collective-permute-start.2 = (bf16[64,1792]{1,0:T(8,128)(2,1)S(1)}, bf16[64,1792]{1,0:T(8,128)(2,1)S(1)}, u32[]{:S(2)}, u32[]{:S(2)}) collective-permute-start(bf16[64,1792]{1,0:T(8,128)(2,1)S(1)} %get-tuple-element.51), channel_id=1, source_target_pairs={{0,8},{4,12},{8,0},{12,4},{1,9},{5,13},{9,1},{13,5},{2,10},{6,14},... | collective-permute-start | bytes 688136 | tf_op jit(solution)/shard_map/ppermute | solution.py:21
  7.6 1.3 %collective-permute-start.3 = (bf16[64,1792]{1,0:T(8,128)(2,1)S(1)}, bf16[64,1792]{1,0:T(8,128)(2,1)S(1)}, u32[]{:S(2)}, u32[]{:S(2)}) collective-permute-start(bf16[64,1792]{1,0:T(8,128)(2,1)S(1)} %get-tuple-element.52), channel_id=1, source_target_pairs={{0,12},{4,8},{8,4},{12,0},{1,13},{5,9},{9,5},{13,1},{2,14},{6,10},... | collective-permute-start | bytes 688136 | tf_op jit(solution)/shard_map/ppermute | solution.py:21
  8.9 0.3 collective-permute-start.1
  9.3 7.6 %prepare.1 = (bf16[512,576]{1,0:T(8,128)(2,1)S(1)}, f32[512,128]{1,0:T(8,128)S(1)}, f32[512,128]{1,0:T(8,128)S(1)}, f32[4,512,128]{2,1,0:T(8,128)S(1)}, f32[16,1...) custom-call(f32[1,32]{1,0:T(1,128)S(1)} %negate_power_fusion.inverse, ...), custom_call_target="tpu_custom_call" | custom-call | flops 4000000000 | bytes 28000000 | tf_op jit(solution)/shard_map/prepare/pallas_call | solution.py:323
  16.9 7.0 %collective-permute-done.2.refs_2_ = bf16[64,1792]{1,0:T(8,128)(2,1)S(1)} collective-permute-done((bf16[64,1792]{1,0:T(8,128)(2,1)S(1)}, bf16[64,1792]{1,0:T(8,128)(2,1)S(1)}, u32[]{:S(2)}, u32[]{:S(2)}) %collective-permute-start.2) | collective-permute-done | bytes 229408 | tf_op jit(solution)/shard_map/ppermute | solution.py:21
  23.9 3.2 %collective-permute-done.4.refs_6_ = bf16[2016,128]{1,0:T(8,128)(2,1)S(1)} collective-permute-done((bf16[2016,128]{1,0:T(8,128)(2,1)S(1)}, bf16[2016,128]{1,0:T(8,128)(2,1)S(1)}, u32[]{:S(2)}, u32[]{:S(2)}) %collective-permute-start.4) | collective-permute-done | bytes 516128 | tf_op jit(solution)/shard_map/ppermute | solution.py:21
  27.1 2.0 %project.1 = (f32[288,128]{1,0:T(8,128)S(1)}, bf16[288,128]{1,0:T(8,128)(2,1)S(1)}, bf16[288,128]{1,0:T(8,128)(2,1)S(1)}, bf16[288,128]{1,0:T(8,128)(2,1)S(1)}, ...) custom-call(s32[1,256]{1,0:T(1,128)S(1)} %get-tuple-element.47.targe, ...), custom_call_target="tpu_custom_call" | custom-call | tf_op jit(solution)/shard_map/project/pallas_call | solution.py:385
  29.1 2.4 %collective-permute-start.6 = (bf16[288,128]{1,0:T(8,128)(2,1)S(1)}, bf16[288,128]{1,0:T(8,128)(2,1)S(1)}, u32[]{:S(2)}, u32[]{:S(2)}) collective-permute-start(bf16[288,128]{1,0:T(8,128)(2,1)S(1)} %get-tuple-element.55), channel_id=1, source_target_pairs={{0,4},{4,0},{8,12},{12,8},{1,5},{5,1},{9,13},{13,9},{2,6},{6,2},{1... | collective-permute-start | bytes 221192 | tf_op jit(solution)/shard_map/ppermute | solution.py:21
  31.5 2.6 %collective-permute-start.7 = (bf16[288,128]{1,0:T(8,128)(2,1)S(1)}, bf16[288,128]{1,0:T(8,128)(2,1)S(1)}, u32[]{:S(2)}, u32[]{:S(2)}) collective-permute-start(bf16[288,128]{1,0:T(8,128)(2,1)S(1)} %get-tuple-element.56), channel_id=1, source_target_pairs={{0,8},{4,12},{8,0},{12,4},{1,9},{5,13},{9,1},{13,5},{2,10},{6,14},... | collective-permute-start | bytes 221192 | tf_op jit(solution)/shard_map/ppermute | solution.py:21
  34.1 0.3 collective-permute-start.8
  34.4 0.6 collective-permute-start.12
  35.0 3.5 %collective-permute-start.13 = (bf16[288,128]{1,0:T(8,128)(2,1)S(1)}, bf16[288,128]{1,0:T(8,128)(2,1)S(1)}, u32[]{:S(2)}, u32[]{:S(2)}) collective-permute-start(bf16[288,128]{1,0:T(8,128)(2,1)S(1)} %get-tuple-element.60), channel_id=1, source_target_pairs={{0,8},{4,12},{8,0},{12,4},{1,9},{5,13},{9,1},{13,5},{2,10},{6,14},... | collective-permute-start | bytes 221192 | tf_op jit(solution)/shard_map/ppermute | solution.py:21
  38.5 0.3 collective-permute-start.14
  38.8 0.7 collective-permute-done.7.refs_2_
  39.5 1.6 %collective-permute-done.8.refs_3_ = bf16[288,128]{1,0:T(8,128)(2,1)S(1)} collective-permute-done((bf16[288,128]{1,0:T(8,128)(2,1)S(1)}, bf16[288,128]{1,0:T(8,128)(2,1)S(1)}, u32[]{:S(2)}, u32[]{:S(2)}) %collective-permute-start.8) | collective-permute-done | bytes 73760 | tf_op jit(solution)/shard_map/ppermute | solution.py:21
  41.1 0.2 finish_rows.2.refs_0_
  41.4 0.1 collective-permute-start.11
  41.4 1.6 %collective-permute-start.10 = (bf16[288,128]{1,0:T(8,128)(2,1)S(1)}, bf16[288,128]{1,0:T(8,128)(2,1)S(1)}, u32[]{:S(2)}, u32[]{:S(2)}) collective-permute-start(bf16[288,128]{1,0:T(8,128)(2,1)S(1)} %finish_rows.2.refs_0_), channel_id=1, source_target_pairs={{0,2},{1,3},{2,0},{3,1},{4,6},{5,7},{6,4},{7,5},{8,10},{9,11},{10,... | collective-permute-start | bytes 221192 | tf_op jit(solution)/shard_map/ppermute | solution.py:21
  43.0 0.2 collective-permute-start.9
  43.3 3.3 %collective-permute-done.13.refs_2_ = bf16[288,128]{1,0:T(8,128)(2,1)S(1)} collective-permute-done((bf16[288,128]{1,0:T(8,128)(2,1)S(1)}, bf16[288,128]{1,0:T(8,128)(2,1)S(1)}, u32[]{:S(2)}, u32[]{:S(2)}) %collective-permute-start.13) | collective-permute-done | bytes 73760 | tf_op jit(solution)/shard_map/ppermute | solution.py:21
  46.6 0.2 finish_rows.3.refs_4_
  46.8 0.1 collective-permute-start.17
  47.0 1.5 %collective-permute-start.16 = (bf16[288,128]{1,0:T(8,128)(2,1)S(1)}, bf16[288,128]{1,0:T(8,128)(2,1)S(1)}, u32[]{:S(2)}, u32[]{:S(2)}) collective-permute-start(bf16[288,128]{1,0:T(8,128)(2,1)S(1)} %finish_rows.3.refs_4_), channel_id=1, source_target_pairs={{0,2},{1,3},{2,0},{3,1},{4,6},{5,7},{6,4},{7,5},{8,10},{9,11},{10,... | collective-permute-start | bytes 221192 | tf_op jit(solution)/shard_map/ppermute | solution.py:21
  48.5 0.3 collective-permute-start.15
  48.8 2.7 %collective-permute-done.17.refs_7_ = bf16[288,128]{1,0:T(8,128)(2,1)S(1)} collective-permute-done((bf16[288,128]{1,0:T(8,128)(2,1)S(1)}, bf16[288,128]{1,0:T(8,128)(2,1)S(1)}, u32[]{:S(2)}, u32[]{:S(2)}) %collective-permute-start.17) | collective-permute-done | bytes 73760 | tf_op jit(solution)/shard_map/ppermute | solution.py:21
  51.4 1.6 %collective-permute-done.16.refs_6_ = bf16[288,128]{1,0:T(8,128)(2,1)S(1)} collective-permute-done((bf16[288,128]{1,0:T(8,128)(2,1)S(1)}, bf16[288,128]{1,0:T(8,128)(2,1)S(1)}, u32[]{:S(2)}, u32[]{:S(2)}) %collective-permute-start.16) | collective-permute-done | bytes 73760 | tf_op jit(solution)/shard_map/ppermute | solution.py:21
  53.1 1.3 %attend.3.refs_0_ = bf16[16,2048]{1,0:T(8,128)(2,1)S(1)} custom-call(bf16[512,576]{1,0:T(8,128)(2,1)S(1)} %get-tuple-element.38.query_ref, s32[1,512]{1,0:T(1,128)S(1)} %get-tuple-element.39.slot_ref, f32[512,128]{1,0:T(8,128)S(1)} %get-tuple-element.40.top_ref, f32[512,128]{1,0:T(8,128)S(1)} %get-tuple-element.41.sum_ref, ...), custom_call_target="tpu_custom_call" | custom-call | tf_op jit(solution)/shard_map/attend/pallas_call | solution.py:488
  54.4 2.9 %collective-permute-start.23 = (bf16[16,2048]{1,0:T(8,128)(2,1)S(1)}, bf16[16,2048]{1,0:T(8,128)(2,1)S(1)}, u32[]{:S(2)}, u32[]{:S(2)}) collective-permute-start(bf16[16,2048]{1,0:T(8,128)(2,1)S(1)} %attend.3.refs_0_), channel_id=1, source_target_pairs={{0,12},{4,8},{8,4},{12,0},{1,13},{5,9},{9,5},{13,1},{2,14},{6,10},... | collective-permute-start | bytes 196616 | tf_op jit(solution)/shard_map/ppermute | solution.py:21
  57.3 0.8 collective-permute-start.22
  58.1 0.8 %collective-permute-start.21 = (bf16[16,2048]{1,0:T(8,128)(2,1)S(1)}, bf16[16,2048]{1,0:T(8,128)(2,1)S(1)}, u32[]{:S(2)}, u32[]{:S(2)}) collective-permute-start(bf16[16,2048]{1,0:T(8,128)(2,1)S(1)} %attend.3.refs_0_), channel_id=1, source_target_pairs={{0,4},{4,0},{8,12},{12,8},{1,5},{5,1},{9,13},{13,9},{2,6},{6,2},{1... | collective-permute-start | bytes 196616 | tf_op jit(solution)/shard_map/ppermute | solution.py:21
  58.8 1.3 %attend.2.refs_0_ = bf16[16,2048]{1,0:T(8,128)(2,1)S(1)} custom-call(bf16[512,576]{1,0:T(8,128)(2,1)S(1)} %get-tuple-element.38.query_ref, s32[1,512]{1,0:T(1,128)S(1)} %get-tuple-element.39.slot_ref, f32[512,128]{1,0:T(8,128)S(1)} %get-tuple-element.40.top_ref, f32[512,128]{1,0:T(8,128)S(1)} %get-tuple-element.41.sum_ref, ...), custom_call_target="tpu_custom_call" | custom-call | tf_op jit(solution)/shard_map/attend/pallas_call | solution.py:488
  60.2 2.9 %collective-permute-start.20 = (bf16[16,2048]{1,0:T(8,128)(2,1)S(1)}, bf16[16,2048]{1,0:T(8,128)(2,1)S(1)}, u32[]{:S(2)}, u32[]{:S(2)}) collective-permute-start(bf16[16,2048]{1,0:T(8,128)(2,1)S(1)} %attend.2.refs_0_), channel_id=1, source_target_pairs={{0,12},{4,8},{8,4},{12,0},{1,13},{5,9},{9,5},{13,1},{2,14},{6,10},... | collective-permute-start | bytes 196616 | tf_op jit(solution)/shard_map/ppermute | solution.py:21
  63.1 1.5 %collective-permute-start.18 = (bf16[16,2048]{1,0:T(8,128)(2,1)S(1)}, bf16[16,2048]{1,0:T(8,128)(2,1)S(1)}, u32[]{:S(2)}, u32[]{:S(2)}) collective-permute-start(bf16[16,2048]{1,0:T(8,128)(2,1)S(1)} %attend.2.refs_0_), channel_id=1, source_target_pairs={{0,4},{4,0},{8,12},{12,8},{1,5},{5,1},{9,13},{13,9},{2,6},{6,2},{1... | collective-permute-start | bytes 196616 | tf_op jit(solution)/shard_map/ppermute | solution.py:21
  64.6 2.1 %collective-permute-done.22.refs_2_ = bf16[16,2048]{1,0:T(8,128)(2,1)S(1)} collective-permute-done((bf16[16,2048]{1,0:T(8,128)(2,1)S(1)}, bf16[16,2048]{1,0:T(8,128)(2,1)S(1)}, u32[]{:S(2)}, u32[]{:S(2)}) %collective-permute-start.22) | collective-permute-done | bytes 65568 | tf_op jit(solution)/shard_map/ppermute | solution.py:21
  66.7 1.4 %output_product.2.refs_5_ = f32[64,1792]{1,0:T(8,128)S(1)} custom-call(bf16[16,2048]{1,0:T(8,128)(2,1)S(1)} %attend.3.refs_0_, bf16[16,2048]{1,0:T(8,128)(2,1)S(1)} %collective-permute-done.21.refs_1_, bf16[16,2048]{1,0:T(8,128)(2,1)S(1)} %collective-permute-done.22.refs_2_, bf16[16,2048]{1,0:T(8,128)(2,1)S(1)} %collective-permute-done.23.refs_3_, ...), custom_call_target="tpu_custom_call" | custom-call | tf_op jit(solution)/shard_map/output_product/pallas_call | solution.py:542
  68.2 1.9 %collective-permute-done.19.refs_2_ = bf16[16,2048]{1,0:T(8,128)(2,1)S(1)} collective-permute-done((bf16[16,2048]{1,0:T(8,128)(2,1)S(1)}, bf16[16,2048]{1,0:T(8,128)(2,1)S(1)}, u32[]{:S(2)}, u32[]{:S(2)}) %collective-permute-start.19) | collective-permute-done | bytes 65568 | tf_op jit(solution)/shard_map/ppermute | solution.py:21
  70.1 1.4 %output_product.3 = (f32[16,1792]{1,0:T(8,128)S(1)}, bf16[16,1792]{1,0:T(8,128)(2,1)S(1)}, bf16[16,1792]{1,0:T(8,128)(2,1)S(1)}, bf16[16,1792]{1,0:T(8,128)(2,1)S(1)}) custom-call(bf16[16,2048]{1,0:T(8,128)(2,1)S(1)} %attend.2.refs_0_, bf16[16,2048]{1,0:T(8,128)(2,1)S(1)} %collective-permute-done.18.refs_1_, ...), custom_call_target="tpu_custom_call" | custom-call | tf_op jit(solution)/shard_map/output_product/pallas_call | solution.py:542
  71.5 0.3 collective-permute-start.24
  71.9 1.3 %collective-permute-start.25 = (bf16[16,1792]{1,0:T(8,128)(2,1)S(1)}, bf16[16,1792]{1,0:T(8,128)(2,1)S(1)}, u32[]{:S(2)}, u32[]{:S(2)}) collective-permute-start(bf16[16,1792]{1,0:T(8,128)(2,1)S(1)} %get-tuple-element.65), channel_id=1, source_target_pairs={{0,2},{1,3},{2,0},{3,1},{4,6},{5,7},{6,4},{7,5},{8,10},{9,11},{10,... | collective-permute-start | bytes 172040 | tf_op jit(solution)/shard_map/ppermute | solution.py:21
  73.2 0.3 collective-permute-start.26
  73.5 2.2 %collective-permute-done.24 = bf16[16,1792]{1,0:T(8,128)(2,1)S(1)} collective-permute-done((bf16[16,1792]{1,0:T(8,128)(2,1)S(1)}, bf16[16,1792]{1,0:T(8,128)(2,1)S(1)}, u32[]{:S(2)}, u32[]{:S(2)}) %collective-permute-start.24) | collective-permute-done | bytes 57376 | tf_op jit(solution)/shard_map/ppermute | solution.py:21
  75.7 1.4 %collective-permute-done.25 = bf16[16,1792]{1,0:T(8,128)(2,1)S(1)} collective-permute-done((bf16[16,1792]{1,0:T(8,128)(2,1)S(1)}, bf16[16,1792]{1,0:T(8,128)(2,1)S(1)}, u32[]{:S(2)}, u32[]{:S(2)}) %collective-permute-start.25) | collective-permute-done | bytes 57376 | tf_op jit(solution)/shard_map/ppermute | solution.py:21
  77.0 0.7 add_convert_fusion
  (40 shorter events, 0.2 us)
Async XLA Ops:
  0.0 4.5 %copy-start.9 = (bf16[64,7168]{1,0:T(8,128)(2,1)S(1)}, bf16[64,7168]{1,0:T(8,128)(2,1)}, u32[]{:S(2)}) copy-start(bf16[64,7168]{1,0:T(8,128)(2,1)} %prompts_ref.1) | copy-start | bytes 2752516
  0.0 1.1 %copy-start.10 = (bf16[448,576]{1,0:T(8,128)(2,1)S(1)}, bf16[448,576]{1,0:T(8,128)(2,1)}, u32[]{:S(2)}) copy-start(bf16[448,576]{1,0:T(8,128)(2,1)} %value_ref.1) | copy-start | bytes 1548292
  1.2 8.0 %copy-start = (bf16[32,128,512]{2,1,0:T(8,128)(2,1)S(1)}, bf16[32,128,512]{2,1,0:T(8,128)(2,1)}, u32[]{:S(2)}) copy-start(bf16[32,128,512]{2,1,0:T(8,128)(2,1)} %absorb_hbm.1) | copy-start | bytes 12582916
  1.2 8.0 %copy-start.1 = (bf16[32,512,128]{2,1,0:T(8,128)(2,1)S(1)}, bf16[32,512,128]{2,1,0:T(8,128)(2,1)}, u32[]{:S(2)}) copy-start(bf16[32,512,128]{2,1,0:T(8,128)(2,1)} %value_hbm.1) | copy-start | bytes 12582916
  1.3 8.0 %copy-start.2 = (bf16[8,256,576]{1,2,0:T(8,128)(2,1)S(1)}, bf16[8,256,576]{1,2,0:T(8,128)(2,1)}, u32[]{:S(2)}) copy-start(bf16[8,256,576]{1,2,0:T(8,128)(2,1)} %param.18) | copy-start | bytes 7077892
  1.3 8.0 %copy-start.3 = (bf16[8,2,32,192]{3,2,1,0:T(8,128)(2,1)S(1)}, bf16[8,2,32,192]{3,2,1,0:T(8,128)(2,1)}, u32[]{:S(2)}) copy-start(bf16[8,2,32,192]{3,2,1,0:T(8,128)(2,1)} %param.20) | copy-start | bytes 589828
  1.3 8.0 %copy-start.4 = (bf16[8,2,576]{2,1,0:T(2,128)(2,1)S(1)}, bf16[8,2,576]{2,1,0:T(2,128)(2,1)}, u32[]{:S(2)}) copy-start(bf16[8,2,576]{2,1,0:T(2,128)(2,1)} %fresh_hbm.1) | copy-start | bytes 55300
  1.3 8.0 %copy-start.6 = (s32[1024]{0:T(1024)S(1)}, s32[1024]{0:T(1024)}, u32[]{:S(2)}) copy-start(s32[1024]{0:T(1024)} %param.15) | copy-start | bytes 12292
  1.3 8.0 %copy-start.7 = (s32[16]{0:T(128)S(1)}, s32[16]{0:T(128)}, u32[]{:S(2)}) copy-start(s32[16]{0:T(128)} %length_hbm) | copy-start | bytes 196
  1.3 8.0 %copy-start.8 = (s32[16]{0:T(128)S(1)}, s32[16]{0:T(128)}, u32[]{:S(2)}) copy-start(s32[16]{0:T(128)} %slot_hbm.1) | copy-start | bytes 196
  1.3 22.6 %collective-permute-start.5 = (bf16[2016,128]{1,0:T(8,128)(2,1)S(1)}, bf16[2016,128]{1,0:T(8,128)(2,1)S(1)}, u32[]{:S(2)}, u32[]{:S(2)}) collective-permute-start(bf16[2016,128]{1,0:T(8,128)(2,1)S(1)} %pack_weight.1.refs_4_), channel_id=1, source_target_pairs={{0,3},{1,2},{2,1},{3,0},{4,7},{5,6},{6,5},{7,4},{8,11},{9,10},{10,... | collective-permute-start | bytes 1548296 | tf_op jit(solution)/shard_map/ppermute | solution.py:21
  3.8 23.4 %collective-permute-start.4 = (bf16[2016,128]{1,0:T(8,128)(2,1)S(1)}, bf16[2016,128]{1,0:T(8,128)(2,1)S(1)}, u32[]{:S(2)}, u32[]{:S(2)}) collective-permute-start(bf16[2016,128]{1,0:T(8,128)(2,1)S(1)} %pack_weight.1.refs_4_), channel_id=1, source_target_pairs={{0,2},{1,3},{2,0},{3,1},{4,6},{5,7},{6,4},{7,5},{8,10},{9,11},{10,... | collective-permute-start | bytes 1548296 | tf_op jit(solution)/shard_map/ppermute | solution.py:21
  4.4 4.5 %collective-permute-start = (bf16[2016,128]{1,0:T(8,128)(2,1)S(1)}, bf16[2016,128]{1,0:T(8,128)(2,1)S(1)}, u32[]{:S(2)}, u32[]{:S(2)}) collective-permute-start(bf16[2016,128]{1,0:T(8,128)(2,1)S(1)} %pack_weight.1.refs_4_), channel_id=1, source_target_pairs={{0,1},{1,0},{2,3},{3,2},{4,5},{5,4},{6,7},{7,6},{8,9},{9,8},{10,11... | collective-permute-start | bytes 1548296 | tf_op jit(solution)/shard_map/ppermute | solution.py:21
  4.7 19.2 %collective-permute-start.2 = (bf16[64,1792]{1,0:T(8,128)(2,1)S(1)}, bf16[64,1792]{1,0:T(8,128)(2,1)S(1)}, u32[]{:S(2)}, u32[]{:S(2)}) collective-permute-start(bf16[64,1792]{1,0:T(8,128)(2,1)S(1)} %get-tuple-element.51), channel_id=1, source_target_pairs={{0,8},{4,12},{8,0},{12,4},{1,9},{5,13},{9,1},{13,5},{2,10},{6,14},... | collective-permute-start | bytes 688136 | tf_op jit(solution)/shard_map/ppermute | solution.py:21
  7.6 16.3 %collective-permute-start.3 = (bf16[64,1792]{1,0:T(8,128)(2,1)S(1)}, bf16[64,1792]{1,0:T(8,128)(2,1)S(1)}, u32[]{:S(2)}, u32[]{:S(2)}) collective-permute-start(bf16[64,1792]{1,0:T(8,128)(2,1)S(1)} %get-tuple-element.52), channel_id=1, source_target_pairs={{0,12},{4,8},{8,4},{12,0},{1,13},{5,9},{9,5},{13,1},{2,14},{6,10},... | collective-permute-start | bytes 688136 | tf_op jit(solution)/shard_map/ppermute | solution.py:21
  8.9 18.2 %collective-permute-start.1 = (bf16[64,1792]{1,0:T(8,128)(2,1)S(1)}, bf16[64,1792]{1,0:T(8,128)(2,1)S(1)}, u32[]{:S(2)}, u32[]{:S(2)}) collective-permute-start(bf16[64,1792]{1,0:T(8,128)(2,1)S(1)} %get-tuple-element.50), channel_id=1, source_target_pairs={{0,4},{4,0},{8,12},{12,8},{1,5},{5,1},{9,13},{13,9},{2,6},{6,2},{1... | collective-permute-start | bytes 688136 | tf_op jit(solution)/shard_map/ppermute | solution.py:21
  9.3 31.9 %copy-start.5 = (f32[512]{0:T(512)S(1)}, f32[512]{0:T(512)}, u32[]{:S(2)}) copy-start(f32[512]{0:T(512)} %param.14) | copy-start | bytes 6148
  29.1 9.4 %collective-permute-start.6 = (bf16[288,128]{1,0:T(8,128)(2,1)S(1)}, bf16[288,128]{1,0:T(8,128)(2,1)S(1)}, u32[]{:S(2)}, u32[]{:S(2)}) collective-permute-start(bf16[288,128]{1,0:T(8,128)(2,1)S(1)} %get-tuple-element.55), channel_id=1, source_target_pairs={{0,4},{4,0},{8,12},{12,8},{1,5},{5,1},{9,13},{13,9},{2,6},{6,2},{1... | collective-permute-start | bytes 221192 | tf_op jit(solution)/shard_map/ppermute | solution.py:21
  31.5 8.0 %collective-permute-start.7 = (bf16[288,128]{1,0:T(8,128)(2,1)S(1)}, bf16[288,128]{1,0:T(8,128)(2,1)S(1)}, u32[]{:S(2)}, u32[]{:S(2)}) collective-permute-start(bf16[288,128]{1,0:T(8,128)(2,1)S(1)} %get-tuple-element.56), channel_id=1, source_target_pairs={{0,8},{4,12},{8,0},{12,4},{1,9},{5,13},{9,1},{13,5},{2,10},{6,14},... | collective-permute-start | bytes 221192 | tf_op jit(solution)/shard_map/ppermute | solution.py:21
  34.1 7.1 %collective-permute-start.8 = (bf16[288,128]{1,0:T(8,128)(2,1)S(1)}, bf16[288,128]{1,0:T(8,128)(2,1)S(1)}, u32[]{:S(2)}, u32[]{:S(2)}) collective-permute-start(bf16[288,128]{1,0:T(8,128)(2,1)S(1)} %get-tuple-element.57), channel_id=1, source_target_pairs={{0,12},{4,8},{8,4},{12,0},{1,13},{5,9},{9,5},{13,1},{2,14},{6,10},... | collective-permute-start | bytes 221192 | tf_op jit(solution)/shard_map/ppermute | solution.py:21
  34.4 8.6 %collective-permute-start.12 = (bf16[288,128]{1,0:T(8,128)(2,1)S(1)}, bf16[288,128]{1,0:T(8,128)(2,1)S(1)}, u32[]{:S(2)}, u32[]{:S(2)}) collective-permute-start(bf16[288,128]{1,0:T(8,128)(2,1)S(1)} %get-tuple-element.59), channel_id=1, source_target_pairs={{0,4},{4,0},{8,12},{12,8},{1,5},{5,1},{9,13},{13,9},{2,6},{6,2},{1... | collective-permute-start | bytes 221192 | tf_op jit(solution)/shard_map/ppermute | solution.py:21
  35.0 11.6 %collective-permute-start.13 = (bf16[288,128]{1,0:T(8,128)(2,1)S(1)}, bf16[288,128]{1,0:T(8,128)(2,1)S(1)}, u32[]{:S(2)}, u32[]{:S(2)}) collective-permute-start(bf16[288,128]{1,0:T(8,128)(2,1)S(1)} %get-tuple-element.60), channel_id=1, source_target_pairs={{0,8},{4,12},{8,0},{12,4},{1,9},{5,13},{9,1},{13,5},{2,10},{6,14},... | collective-permute-start | bytes 221192 | tf_op jit(solution)/shard_map/ppermute | solution.py:21
  38.5 8.1 %collective-permute-start.14 = (bf16[288,128]{1,0:T(8,128)(2,1)S(1)}, bf16[288,128]{1,0:T(8,128)(2,1)S(1)}, u32[]{:S(2)}, u32[]{:S(2)}) collective-permute-start(bf16[288,128]{1,0:T(8,128)(2,1)S(1)} %get-tuple-element.61), channel_id=1, source_target_pairs={{0,12},{4,8},{8,4},{12,0},{1,13},{5,9},{9,5},{13,1},{2,14},{6,10},... | collective-permute-start | bytes 221192 | tf_op jit(solution)/shard_map/ppermute | solution.py:21
  41.4 7.1 %collective-permute-start.11 = (bf16[288,128]{1,0:T(8,128)(2,1)S(1)}, bf16[288,128]{1,0:T(8,128)(2,1)S(1)}, u32[]{:S(2)}, u32[]{:S(2)}) collective-permute-start(bf16[288,128]{1,0:T(8,128)(2,1)S(1)} %finish_rows.2.refs_0_), channel_id=1, source_target_pairs={{0,3},{1,2},{2,1},{3,0},{4,7},{5,6},{6,5},{7,4},{8,11},{9,10},{10,... | collective-permute-start | bytes 221192 | tf_op jit(solution)/shard_map/ppermute | solution.py:21
  41.4 7.3 %collective-permute-start.10 = (bf16[288,128]{1,0:T(8,128)(2,1)S(1)}, bf16[288,128]{1,0:T(8,128)(2,1)S(1)}, u32[]{:S(2)}, u32[]{:S(2)}) collective-permute-start(bf16[288,128]{1,0:T(8,128)(2,1)S(1)} %finish_rows.2.refs_0_), channel_id=1, source_target_pairs={{0,2},{1,3},{2,0},{3,1},{4,6},{5,7},{6,4},{7,5},{8,10},{9,11},{10,... | collective-permute-start | bytes 221192 | tf_op jit(solution)/shard_map/ppermute | solution.py:21
  43.0 5.7 %collective-permute-start.9 = (bf16[288,128]{1,0:T(8,128)(2,1)S(1)}, bf16[288,128]{1,0:T(8,128)(2,1)S(1)}, u32[]{:S(2)}, u32[]{:S(2)}) collective-permute-start(bf16[288,128]{1,0:T(8,128)(2,1)S(1)} %finish_rows.2.refs_0_), channel_id=1, source_target_pairs={{0,1},{1,0},{2,3},{3,2},{4,5},{5,4},{6,7},{7,6},{8,9},{9,8},{10,11... | collective-permute-start | bytes 221192 | tf_op jit(solution)/shard_map/ppermute | solution.py:21
  46.8 4.6 %collective-permute-start.17 = (bf16[288,128]{1,0:T(8,128)(2,1)S(1)}, bf16[288,128]{1,0:T(8,128)(2,1)S(1)}, u32[]{:S(2)}, u32[]{:S(2)}) collective-permute-start(bf16[288,128]{1,0:T(8,128)(2,1)S(1)} %finish_rows.3.refs_4_), channel_id=1, source_target_pairs={{0,3},{1,2},{2,1},{3,0},{4,7},{5,6},{6,5},{7,4},{8,11},{9,10},{10,... | collective-permute-start | bytes 221192 | tf_op jit(solution)/shard_map/ppermute | solution.py:21
  47.0 6.1 %collective-permute-start.16 = (bf16[288,128]{1,0:T(8,128)(2,1)S(1)}, bf16[288,128]{1,0:T(8,128)(2,1)S(1)}, u32[]{:S(2)}, u32[]{:S(2)}) collective-permute-start(bf16[288,128]{1,0:T(8,128)(2,1)S(1)} %finish_rows.3.refs_4_), channel_id=1, source_target_pairs={{0,2},{1,3},{2,0},{3,1},{4,6},{5,7},{6,4},{7,5},{8,10},{9,11},{10,... | collective-permute-start | bytes 221192 | tf_op jit(solution)/shard_map/ppermute | solution.py:21
  48.5 4.6 %collective-permute-start.15 = (bf16[288,128]{1,0:T(8,128)(2,1)S(1)}, bf16[288,128]{1,0:T(8,128)(2,1)S(1)}, u32[]{:S(2)}, u32[]{:S(2)}) collective-permute-start(bf16[288,128]{1,0:T(8,128)(2,1)S(1)} %finish_rows.3.refs_4_), channel_id=1, source_target_pairs={{0,1},{1,0},{2,3},{3,2},{4,5},{5,4},{6,7},{7,6},{8,9},{9,8},{10,11... | collective-permute-start | bytes 221192 | tf_op jit(solution)/shard_map/ppermute | solution.py:21
  54.4 8.7 %collective-permute-start.23 = (bf16[16,2048]{1,0:T(8,128)(2,1)S(1)}, bf16[16,2048]{1,0:T(8,128)(2,1)S(1)}, u32[]{:S(2)}, u32[]{:S(2)}) collective-permute-start(bf16[16,2048]{1,0:T(8,128)(2,1)S(1)} %attend.3.refs_0_), channel_id=1, source_target_pairs={{0,12},{4,8},{8,4},{12,0},{1,13},{5,9},{9,5},{13,1},{2,14},{6,10},... | collective-permute-start | bytes 196616 | tf_op jit(solution)/shard_map/ppermute | solution.py:21
  57.3 9.4 %collective-permute-start.22 = (bf16[16,2048]{1,0:T(8,128)(2,1)S(1)}, bf16[16,2048]{1,0:T(8,128)(2,1)S(1)}, u32[]{:S(2)}, u32[]{:S(2)}) collective-permute-start(bf16[16,2048]{1,0:T(8,128)(2,1)S(1)} %attend.3.refs_0_), channel_id=1, source_target_pairs={{0,8},{4,12},{8,0},{12,4},{1,9},{5,13},{9,1},{13,5},{2,10},{6,14},... | collective-permute-start | bytes 196616 | tf_op jit(solution)/shard_map/ppermute | solution.py:21
  58.1 8.7 %collective-permute-start.21 = (bf16[16,2048]{1,0:T(8,128)(2,1)S(1)}, bf16[16,2048]{1,0:T(8,128)(2,1)S(1)}, u32[]{:S(2)}, u32[]{:S(2)}) collective-permute-start(bf16[16,2048]{1,0:T(8,128)(2,1)S(1)} %attend.3.refs_0_), channel_id=1, source_target_pairs={{0,4},{4,0},{8,12},{12,8},{1,5},{5,1},{9,13},{13,9},{2,6},{6,2},{1... | collective-permute-start | bytes 196616 | tf_op jit(solution)/shard_map/ppermute | solution.py:21
  60.2 8.0 %collective-permute-start.20 = (bf16[16,2048]{1,0:T(8,128)(2,1)S(1)}, bf16[16,2048]{1,0:T(8,128)(2,1)S(1)}, u32[]{:S(2)}, u32[]{:S(2)}) collective-permute-start(bf16[16,2048]{1,0:T(8,128)(2,1)S(1)} %attend.2.refs_0_), channel_id=1, source_target_pairs={{0,12},{4,8},{8,4},{12,0},{1,13},{5,9},{9,5},{13,1},{2,14},{6,10},... | collective-permute-start | bytes 196616 | tf_op jit(solution)/shard_map/ppermute | solution.py:21
  63.1 7.0 %collective-permute-start.19 = (bf16[16,2048]{1,0:T(8,128)(2,1)S(1)}, bf16[16,2048]{1,0:T(8,128)(2,1)S(1)}, u32[]{:S(2)}, u32[]{:S(2)}) collective-permute-start(bf16[16,2048]{1,0:T(8,128)(2,1)S(1)} %attend.2.refs_0_), channel_id=1, source_target_pairs={{0,8},{4,12},{8,0},{12,4},{1,9},{5,13},{9,1},{13,5},{2,10},{6,14},... | collective-permute-start | bytes 196616 | tf_op jit(solution)/shard_map/ppermute | solution.py:21
  63.1 7.0 %collective-permute-start.18 = (bf16[16,2048]{1,0:T(8,128)(2,1)S(1)}, bf16[16,2048]{1,0:T(8,128)(2,1)S(1)}, u32[]{:S(2)}, u32[]{:S(2)}) collective-permute-start(bf16[16,2048]{1,0:T(8,128)(2,1)S(1)} %attend.2.refs_0_), channel_id=1, source_target_pairs={{0,4},{4,0},{8,12},{12,8},{1,5},{5,1},{9,13},{13,9},{2,6},{6,2},{1... | collective-permute-start | bytes 196616 | tf_op jit(solution)/shard_map/ppermute | solution.py:21
  71.5 4.1 %collective-permute-start.24 = (bf16[16,1792]{1,0:T(8,128)(2,1)S(1)}, bf16[16,1792]{1,0:T(8,128)(2,1)S(1)}, u32[]{:S(2)}, u32[]{:S(2)}) collective-permute-start(bf16[16,1792]{1,0:T(8,128)(2,1)S(1)} %get-tuple-element.64), channel_id=1, source_target_pairs={{0,3},{1,2},{2,1},{3,0},{4,7},{5,6},{6,5},{7,4},{8,11},{9,10},{10,... | collective-permute-start | bytes 172040 | tf_op jit(solution)/shard_map/ppermute | solution.py:21
  71.9 5.2 %collective-permute-start.25 = (bf16[16,1792]{1,0:T(8,128)(2,1)S(1)}, bf16[16,1792]{1,0:T(8,128)(2,1)S(1)}, u32[]{:S(2)}, u32[]{:S(2)}) collective-permute-start(bf16[16,1792]{1,0:T(8,128)(2,1)S(1)} %get-tuple-element.65), channel_id=1, source_target_pairs={{0,2},{1,3},{2,0},{3,1},{4,6},{5,7},{6,4},{7,5},{8,10},{9,11},{10,... | collective-permute-start | bytes 172040 | tf_op jit(solution)/shard_map/ppermute | solution.py:21
  73.2 3.9 %collective-permute-start.26 = (bf16[16,1792]{1,0:T(8,128)(2,1)S(1)}, bf16[16,1792]{1,0:T(8,128)(2,1)S(1)}, u32[]{:S(2)}, u32[]{:S(2)}) collective-permute-start(bf16[16,1792]{1,0:T(8,128)(2,1)S(1)} %get-tuple-element.66), channel_id=1, source_target_pairs={{0,1},{1,0},{2,3},{3,2},{4,5},{5,4},{6,7},{7,6},{8,9},{9,8},{10,11... | collective-permute-start | bytes 172040 | tf_op jit(solution)/shard_map/ppermute | solution.py:21

commit v7 on v6

--- a/solution.py
+++ b/solution.py
@@ -373,10 +373,13 @@
     rows[...] = raw
     target = target_ref[...]
     half_rows = tok_rows
-    for j in range(2 * dev_count):
-        ids = lax.broadcasted_iota(jnp.int32, (half_rows, target.shape[1]), 0)
+    step = min(4, 2 * dev_count)
+    for j in range(0, 2 * dev_count, step):
+        ids = lax.broadcasted_iota(jnp.int32, (step * half_rows, target.shape[1]), 0)
         route = jnp.where(ids + j * half_rows == target, 1.0, 0.0).astype(bf16)
-        store_packed(out_refs[j], jnp.dot(route, rows[...], preferred_element_type=f32))
+        placed = jnp.dot(route, rows[...], preferred_element_type=f32)
+        for n in range(step):
+            store_packed(out_refs[j + n], placed[n * half_rows : (n + 1) * half_rows])
 
 
 def project(x_pieces, weights, target, width):
@@ -435,15 +438,14 @@
 
 
 def attend_kernel(
-    scale, cap_slots, steps, part, parts, query_ref, slot_ref, top_ref,
+    scale, cap_slots, steps, first_head, heads, query_ref, slot_ref, top_ref,
     sum_ref, mix_ref, live_ref, value_ref, *refs
 ):
     pieces, out_ref, keys = refs[:-2], refs[-2], refs[-1]
     lat_width = mix_ref.shape[0] * mix_ref.shape[2]
     per_head = cap_slots * steps
-    rows = query_ref.shape[0] // parts
-    heads = rows // per_head
-    mine = slice(part * rows, (part + 1) * rows)
+    rows = heads * per_head
+    mine = slice(first_head * per_head, first_head * per_head + rows)
     sides = len(pieces) // 2
     piece_rows = keys.shape[0] // len(pieces)
     for n, piece in enumerate(pieces):
@@ -472,7 +474,7 @@
     live = live_ref[:, :1]
     width = value_ref.shape[2]
     for h in range(0, heads, 2):
-        head = part * heads + h
+        head = first_head + h
         pair = jnp.concatenate([value_ref[head], value_ref[head + 1]], axis=1)
         both = jnp.dot(
             latent[h * per_head : (h + 2) * per_head, :], pair, preferred_element_type=f32
@@ -481,13 +483,12 @@
         out_ref[:, (h + 1) * width : (h + 2) * width] = (both[per_head:, width:] * live).astype(bf16)
 
 
-def attend(scale, query, row_slot, top, total, mix, live, value, pieces, cap_slots, steps, part,
-           parts):
-    heads, _, width = value.shape
-    part_heads = heads // parts
+def attend(scale, query, row_slot, top, total, mix, live, value, pieces, cap_slots, steps,
+           first_head, heads):
+    width = value.shape[2]
     return pl.pallas_call(
-        functools.partial(attend_kernel, scale, cap_slots, steps, part, parts),
-        out_shape=jax.ShapeDtypeStruct((cap_slots * steps, part_heads * width), bf16),
+        functools.partial(attend_kernel, scale, cap_slots, steps, first_head, heads),
+        out_shape=jax.ShapeDtypeStruct((cap_slots * steps, heads * width), bf16),
         in_specs=[in_vmem] * (7 + len(pieces)),
         out_specs=in_vmem,
         scratch_shapes=[pltpu.VMEM((row_slot.shape[1], query.shape[1]), bf16)],
@@ -496,12 +497,12 @@
     )(query, row_slot, top, total, mix, live, value, *pieces)
 
 
-def output_kernel(dev_count, side_count, part, parts, *refs):
+def output_kernel(dev_count, side_count, start, last, *refs):
     my_dev, my_side = lax.axis_index("dev"), lax.axis_index("side")
     head_refs = refs[:dev_count]
     weight_ref = refs[dev_count]
-    earlier_ref = refs[dev_count + 1] if part else None
-    out_refs = refs[dev_count + 1 + (part > 0) : -1]
+    earlier_ref = refs[dev_count + 1] if start else None
+    out_refs = refs[dev_count + 1 + (start > 0) : -1]
     held = refs[-1]
     rows, depth = head_refs[0].shape
     per_side = dev_count // side_count
@@ -515,12 +516,12 @@
     for n in range(columns // tile):
         here = slice(n * tile, (n + 1) * tile)
         product = jnp.dot(
-            held[...], weight_ref[part * depth : (part + 1) * depth, here],
+            held[...], weight_ref[start : start + depth, here],
             preferred_element_type=f32,
         )
-        if part:
+        if start:
             product = product + earlier_ref[:, here]
-        if part + 1 < parts:
+        if not last:
             out_refs[0][:, here] = product
         else:
             for k in range(side_count):
@@ -529,18 +530,18 @@
                 )
 
 
-def output_product(head_pieces, weight, side_count, earlier, part, parts):
+def output_product(head_pieces, weight, side_count, earlier, start, last):
     dev_count = len(head_pieces)
     rows, depth = head_pieces[0].shape
     columns = weight.shape[1]
     side_rows = rows * dev_count // side_count
-    if part + 1 < parts:
+    if not last:
         shapes = [((rows * dev_count, columns), f32)]
     else:
         shapes = [((side_rows, columns), f32 if k == 0 else bf16) for k in range(side_count)]
     earlier = [] if earlier is None else [earlier]
     return pl.pallas_call(
-        functools.partial(output_kernel, dev_count, side_count, part, parts),
+        functools.partial(output_kernel, dev_count, side_count, start, last),
         out_shape=[jax.ShapeDtypeStruct(*shape) for shape in shapes],
         in_specs=[in_vmem] * (dev_count + 1 + len(earlier)),
         out_specs=[in_vmem] * len(shapes),
@@ -569,7 +570,7 @@
     tok_rows, model_width = prompts.shape
     shard_rows, kv_width = latent_weight.shape
     lat_width = latent_gain.shape[0]
-    head_count, nope_width, _ = key_absorb.shape
+    nope_width = value_absorb.shape[2]
     rope_width = kv_width - lat_width
     cap_slots, ctx_len, _ = latent_cache.shape
     step_count = new_latent.shape[1]
@@ -613,18 +614,21 @@
         half = list(routed[which * dev_count : (which + 1) * dev_count])
         for k in sorted(range(1, dev_count), reverse=True):
             half[k] = swap(half[k], "dev", k)
-        latent_rows = finish(half, latent_gain.reshape(1, -1), cosine, sine, which)
+        latent_rows = finish(half[:1] + half[:0:-1], latent_gain.reshape(1, -1), cosine, sine, which)
         pieces += [latent_rows] + [swap(latent_rows, "side", k) for k in range(1, side_count)]
-    product, parts = None, 2
-    for part in range(parts):
+    product, first_head, head_count = None, 0, value_absorb.shape[0]
+    for part_heads in (head_count * 3 // 4, head_count // 4):
         head_out = attend(
             score_scale, query_full, row_slot, top_held, sum_held, mix_held, live, value_here,
-            pieces, cap_slots, step_count, part, parts,
+            pieces, cap_slots, step_count, first_head, part_heads,
         )
         heads = [head_out] + [None] * (dev_count - 1)
         for k in sorted(range(1, dev_count), reverse=True):
             heads[k] = swap(head_out, "dev", k)
-        products = output_product(heads, out_here, side_count, product, part, parts)
+        start, first_head = first_head * nope_width, first_head + part_heads
+        products = output_product(
+            heads, out_here, side_count, product, start, first_head == head_count
+        )
         product = products[0]
     result = products[0]
     for k in sorted(range(1, side_count), reverse=True):

time: 77.8 us -> 76 us (0.977)
  waiting for transfers between devices: 27.8 us -> 24.7 us
  starting transfers between devices: 32.1 us -> 33.4 us
    ppermute x27, waiting for transfers between devices: 27.8 us -> 24.7 us  [swap(): return lax.ppermute(value, axis, [(i, i ^ step) for i in range(count)])]
    ppermute x27, starting transfers between devices: 32.1 us -> 33.4 us  [swap(): return lax.ppermute(value, axis, [(i, i ^ step) for i in range(count)])]
  transfers between devices with their start and end apart: 27 -> 27, of which waited for: 11 -> 11; matrix products, arithmetic and copies ran while one was open for 0% -> 0% of each run, Pallas kernels for 14% -> 15%
where the time goes in v7:
time: 76 us; the launch traced here: 75.8 us
  starting transfers between devices  33.4 us (44%)
  waiting for transfers between devices  24.7 us (32%)
  Pallas kernels  15.6 us (21%)
  local copies, waits for them, and re-layouts  1.2 us (2%)
    ppermute x27, starting transfers between devices, swap(): return lax.ppermute(value, axis, [(i, i ^ step) for i in range(count)])  33.4 us
    ppermute x27, waiting for transfers between devices, swap(): return lax.ppermute(value, axis, [(i, i ^ step) for i in range(count)])  24.7 us
    pallas_call x1, Pallas kernels, prepare(): pl.pallas_call(functools.partial(prepare_kernel, scale, steps, (dev_count...  7.61 us
    pallas_call x2, Pallas kernels, output_product(): pl.pallas_call(functools.partial(output_kernel, dev_count, side_count, st...  2.84 us
    pallas_call x2, Pallas kernels, attend(): pl.pallas_call(functools.partial(attend_kernel, scale, cap_slots, steps,...  2.77 us
    pallas_call x1, Pallas kernels, project(): pl.pallas_call(functools.partial(project_kernel, dev_count, len(weights))...  1.69 us
  transfers between devices with their start and end apart: 27, of which 11 were waited for; matrix products, arithmetic and copies ran while one was open for 0% of the time, Pallas kernels for 15%

profile of v7, /device:TPU:0, one launch (start us, length us, event | category | flops | bytes accessed | tf_op | source)
XLA Modules:
  0.0 75.8 jit_solution(12547519610099380541)
XLA Ops:
  0.0 1.1 %copy-done.10 = bf16[448,576]{1,0:T(8,128)(2,1)S(1)} copy-done((bf16[448,576]{1,0:T(8,128)(2,1)S(1)}, bf16[448,576]{1,0:T(8,128)(2,1)}, u32[]{:S(2)}) %copy-start.10) | copy-done | bytes 516120
  1.1 0.1 pack_weight.1.refs_4_
  1.2 0.0 copy-start.1
  1.3 0.0 copy-start.2
  1.3 2.4 %collective-permute-start.5 = (bf16[2016,128]{1,0:T(8,128)(2,1)S(1)}, bf16[2016,128]{1,0:T(8,128)(2,1)S(1)}, u32[]{:S(2)}, u32[]{:S(2)}) collective-permute-start(bf16[2016,128]{1,0:T(8,128)(2,1)S(1)} %pack_weight.1.refs_4_), channel_id=1, source_target_pairs={{0,3},{1,2},{2,1},{3,0},{4,7},{5,6},{6,5},{7,4},{8,11},{9,10},{10,... | collective-permute-start | bytes 1548296 | tf_op jit(solution)/shard_map/ppermute | solution.py:21
  3.8 0.6 collective-permute-start.4
  4.4 0.0 collective-permute-start
  4.5 0.2 split_columns.1
  4.7 2.9 %collective-permute-start.2 = (bf16[64,1792]{1,0:T(8,128)(2,1)S(1)}, bf16[64,1792]{1,0:T(8,128)(2,1)S(1)}, u32[]{:S(2)}, u32[]{:S(2)}) collective-permute-start(bf16[64,1792]{1,0:T(8,128)(2,1)S(1)} %get-tuple-element.51), channel_id=1, source_target_pairs={{0,8},{4,12},{8,0},{12,4},{1,9},{5,13},{9,1},{13,5},{2,10},{6,14},... | collective-permute-start | bytes 688136 | tf_op jit(solution)/shard_map/ppermute | solution.py:21
  7.6 1.3 %collective-permute-start.3 = (bf16[64,1792]{1,0:T(8,128)(2,1)S(1)}, bf16[64,1792]{1,0:T(8,128)(2,1)S(1)}, u32[]{:S(2)}, u32[]{:S(2)}) collective-permute-start(bf16[64,1792]{1,0:T(8,128)(2,1)S(1)} %get-tuple-element.52), channel_id=1, source_target_pairs={{0,12},{4,8},{8,4},{12,0},{1,13},{5,9},{9,5},{13,1},{2,14},{6,10},... | collective-permute-start | bytes 688136 | tf_op jit(solution)/shard_map/ppermute | solution.py:21
  8.9 0.3 collective-permute-start.1
  9.3 7.6 %prepare.1 = (bf16[512,576]{1,0:T(8,128)(2,1)S(1)}, f32[512,128]{1,0:T(8,128)S(1)}, f32[512,128]{1,0:T(8,128)S(1)}, f32[4,512,128]{2,1,0:T(8,128)S(1)}, f32[16,1...) custom-call(f32[1,32]{1,0:T(1,128)S(1)} %negate_power_fusion.inverse, ...), custom_call_target="tpu_custom_call" | custom-call | flops 4000000000 | bytes 28000000 | tf_op jit(solution)/shard_map/prepare/pallas_call | solution.py:323
  16.9 7.0 %collective-permute-done.2.refs_2_ = bf16[64,1792]{1,0:T(8,128)(2,1)S(1)} collective-permute-done((bf16[64,1792]{1,0:T(8,128)(2,1)S(1)}, bf16[64,1792]{1,0:T(8,128)(2,1)S(1)}, u32[]{:S(2)}, u32[]{:S(2)}) %collective-permute-start.2) | collective-permute-done | bytes 229408 | tf_op jit(solution)/shard_map/ppermute | solution.py:21
  23.9 3.2 %collective-permute-done.4.refs_6_ = bf16[2016,128]{1,0:T(8,128)(2,1)S(1)} collective-permute-done((bf16[2016,128]{1,0:T(8,128)(2,1)S(1)}, bf16[2016,128]{1,0:T(8,128)(2,1)S(1)}, u32[]{:S(2)}, u32[]{:S(2)}) %collective-permute-start.4) | collective-permute-done | bytes 516128 | tf_op jit(solution)/shard_map/ppermute | solution.py:21
  27.1 1.7 %project.1 = (f32[288,128]{1,0:T(8,128)S(1)}, bf16[288,128]{1,0:T(8,128)(2,1)S(1)}, bf16[288,128]{1,0:T(8,128)(2,1)S(1)}, bf16[288,128]{1,0:T(8,128)(2,1)S(1)}, ...) custom-call(s32[1,256]{1,0:T(1,128)S(1)} %get-tuple-element.47.targe, ...), custom_call_target="tpu_custom_call" | custom-call | tf_op jit(solution)/shard_map/project/pallas_call | solution.py:388
  28.8 4.5 %collective-permute-start.6 = (bf16[288,128]{1,0:T(8,128)(2,1)S(1)}, bf16[288,128]{1,0:T(8,128)(2,1)S(1)}, u32[]{:S(2)}, u32[]{:S(2)}) collective-permute-start(bf16[288,128]{1,0:T(8,128)(2,1)S(1)} %get-tuple-element.55), channel_id=1, source_target_pairs={{0,12},{4,8},{8,4},{12,0},{1,13},{5,9},{9,5},{13,1},{2,14},{6,10},... | collective-permute-start | bytes 221192 | tf_op jit(solution)/shard_map/ppermute | solution.py:21
  33.3 0.6 collective-permute-start.8
  34.0 3.7 %collective-permute-start.12 = (bf16[288,128]{1,0:T(8,128)(2,1)S(1)}, bf16[288,128]{1,0:T(8,128)(2,1)S(1)}, u32[]{:S(2)}, u32[]{:S(2)}) collective-permute-start(bf16[288,128]{1,0:T(8,128)(2,1)S(1)} %get-tuple-element.59), channel_id=1, source_target_pairs={{0,12},{4,8},{8,4},{12,0},{1,13},{5,9},{9,5},{13,1},{2,14},{6,10},... | collective-permute-start | bytes 221192 | tf_op jit(solution)/shard_map/ppermute | solution.py:21
  37.7 2.5 %collective-permute-start.14 = (bf16[288,128]{1,0:T(8,128)(2,1)S(1)}, bf16[288,128]{1,0:T(8,128)(2,1)S(1)}, u32[]{:S(2)}, u32[]{:S(2)}) collective-permute-start(bf16[288,128]{1,0:T(8,128)(2,1)S(1)} %get-tuple-element.61), channel_id=1, source_target_pairs={{0,4},{4,0},{8,12},{12,8},{1,5},{5,1},{9,13},{13,9},{2,6},{6,2},{1... | collective-permute-start | bytes 221192 | tf_op jit(solution)/shard_map/ppermute | solution.py:21
  40.2 3.5 %collective-permute-done.7.refs_2_ = bf16[288,128]{1,0:T(8,128)(2,1)S(1)} collective-permute-done((bf16[288,128]{1,0:T(8,128)(2,1)S(1)}, bf16[288,128]{1,0:T(8,128)(2,1)S(1)}, u32[]{:S(2)}, u32[]{:S(2)}) %collective-permute-start.7) | collective-permute-done | bytes 73760 | tf_op jit(solution)/shard_map/ppermute | solution.py:21
  43.7 0.2 finish_rows.2.refs_0_
  43.9 0.1 collective-permute-start.11
  44.0 1.6 %collective-permute-start.10 = (bf16[288,128]{1,0:T(8,128)(2,1)S(1)}, bf16[288,128]{1,0:T(8,128)(2,1)S(1)}, u32[]{:S(2)}, u32[]{:S(2)}) collective-permute-start(bf16[288,128]{1,0:T(8,128)(2,1)S(1)} %finish_rows.2.refs_0_), channel_id=1, source_target_pairs={{0,2},{1,3},{2,0},{3,1},{4,6},{5,7},{6,4},{7,5},{8,10},{9,11},{10,... | collective-permute-start | bytes 221192 | tf_op jit(solution)/shard_map/ppermute | solution.py:21
  45.6 0.3 collective-permute-start.9
  45.9 0.4 collective-permute-done.13.refs_2_
  46.3 0.2 finish_rows.3.refs_4_
  46.5 0.7 collective-permute-start.17
  47.3 0.8 %collective-permute-start.16 = (bf16[288,128]{1,0:T(8,128)(2,1)S(1)}, bf16[288,128]{1,0:T(8,128)(2,1)S(1)}, u32[]{:S(2)}, u32[]{:S(2)}) collective-permute-start(bf16[288,128]{1,0:T(8,128)(2,1)S(1)} %finish_rows.3.refs_4_), channel_id=1, source_target_pairs={{0,2},{1,3},{2,0},{3,1},{4,6},{5,7},{6,4},{7,5},{8,10},{9,11},{10,... | collective-permute-start | bytes 221192 | tf_op jit(solution)/shard_map/ppermute | solution.py:21
  48.0 0.5 collective-permute-done.11.refs_3_
  48.5 0.1 collective-permute-start.15
  48.6 1.5 %collective-permute-done.10.refs_2_ = bf16[288,128]{1,0:T(8,128)(2,1)S(1)} collective-permute-done((bf16[288,128]{1,0:T(8,128)(2,1)S(1)}, bf16[288,128]{1,0:T(8,128)(2,1)S(1)}, u32[]{:S(2)}, u32[]{:S(2)}) %collective-permute-start.10) | collective-permute-done | bytes 73760 | tf_op jit(solution)/shard_map/ppermute | solution.py:21
  50.2 1.5 %collective-permute-done.17.refs_7_ = bf16[288,128]{1,0:T(8,128)(2,1)S(1)} collective-permute-done((bf16[288,128]{1,0:T(8,128)(2,1)S(1)}, bf16[288,128]{1,0:T(8,128)(2,1)S(1)}, u32[]{:S(2)}, u32[]{:S(2)}) %collective-permute-start.17) | collective-permute-done | bytes 73760 | tf_op jit(solution)/shard_map/ppermute | solution.py:21
  51.7 1.6 %collective-permute-done.16.refs_6_ = bf16[288,128]{1,0:T(8,128)(2,1)S(1)} collective-permute-done((bf16[288,128]{1,0:T(8,128)(2,1)S(1)}, bf16[288,128]{1,0:T(8,128)(2,1)S(1)}, u32[]{:S(2)}, u32[]{:S(2)}) %collective-permute-start.16) | collective-permute-done | bytes 73760 | tf_op jit(solution)/shard_map/ppermute | solution.py:21
  53.3 1.8 %attend.3.refs_0_ = bf16[16,3072]{1,0:T(8,128)(2,1)S(1)} custom-call(bf16[512,576]{1,0:T(8,128)(2,1)S(1)} %get-tuple-element.38.query_ref, s32[1,512]{1,0:T(1,128)S(1)} %get-tuple-element.39.slot_ref, f32[512,128]{1,0:T(8,128)S(1)} %get-tuple-element.40.top_ref, f32[512,128]{1,0:T(8,128)S(1)} %get-tuple-element.41.sum_ref, ...), custom_call_target="tpu_custom_call" | custom-call | tf_op jit(solution)/shard_map/attend/pallas_call | solution.py:489
  55.1 2.9 %collective-permute-start.23 = (bf16[16,3072]{1,0:T(8,128)(2,1)S(1)}, bf16[16,3072]{1,0:T(8,128)(2,1)S(1)}, u32[]{:S(2)}, u32[]{:S(2)}) collective-permute-start(bf16[16,3072]{1,0:T(8,128)(2,1)S(1)} %attend.3.refs_0_), channel_id=1, source_target_pairs={{0,12},{4,8},{8,4},{12,0},{1,13},{5,9},{9,5},{13,1},{2,14},{6,10},... | collective-permute-start | bytes 294920 | tf_op jit(solution)/shard_map/ppermute | solution.py:21
  58.0 1.5 %collective-permute-start.21 = (bf16[16,3072]{1,0:T(8,128)(2,1)S(1)}, bf16[16,3072]{1,0:T(8,128)(2,1)S(1)}, u32[]{:S(2)}, u32[]{:S(2)}) collective-permute-start(bf16[16,3072]{1,0:T(8,128)(2,1)S(1)} %attend.3.refs_0_), channel_id=1, source_target_pairs={{0,4},{4,0},{8,12},{12,8},{1,5},{5,1},{9,13},{13,9},{2,6},{6,2},{1... | collective-permute-start | bytes 294920 | tf_op jit(solution)/shard_map/ppermute | solution.py:21
  59.5 1.0 %attend.2.refs_0_ = bf16[16,1024]{1,0:T(8,128)(2,1)S(1)} custom-call(bf16[512,576]{1,0:T(8,128)(2,1)S(1)} %get-tuple-element.38.query_ref, s32[1,512]{1,0:T(1,128)S(1)} %get-tuple-element.39.slot_ref, f32[512,128]{1,0:T(8,128)S(1)} %get-tuple-element.40.top_ref, f32[512,128]{1,0:T(8,128)S(1)} %get-tuple-element.41.sum_ref, ...), custom_call_target="tpu_custom_call" | custom-call | tf_op jit(solution)/shard_map/attend/pallas_call | solution.py:489
  60.6 2.9 %collective-permute-start.20 = (bf16[16,1024]{1,0:T(8,128)(2,1)S(1)}, bf16[16,1024]{1,0:T(8,128)(2,1)S(1)}, u32[]{:S(2)}, u32[]{:S(2)}) collective-permute-start(bf16[16,1024]{1,0:T(8,128)(2,1)S(1)} %attend.2.refs_0_), channel_id=1, source_target_pairs={{0,12},{4,8},{8,4},{12,0},{1,13},{5,9},{9,5},{13,1},{2,14},{6,10},... | collective-permute-start | bytes 98312 | tf_op jit(solution)/shard_map/ppermute | solution.py:21
  63.5 1.5 %collective-permute-start.18 = (bf16[16,1024]{1,0:T(8,128)(2,1)S(1)}, bf16[16,1024]{1,0:T(8,128)(2,1)S(1)}, u32[]{:S(2)}, u32[]{:S(2)}) collective-permute-start(bf16[16,1024]{1,0:T(8,128)(2,1)S(1)} %attend.2.refs_0_), channel_id=1, source_target_pairs={{0,4},{4,0},{8,12},{12,8},{1,5},{5,1},{9,13},{13,9},{2,6},{6,2},{1... | collective-permute-start | bytes 98312 | tf_op jit(solution)/shard_map/ppermute | solution.py:21
  65.0 2.4 %collective-permute-done.22.refs_2_ = bf16[16,3072]{1,0:T(8,128)(2,1)S(1)} collective-permute-done((bf16[16,3072]{1,0:T(8,128)(2,1)S(1)}, bf16[16,3072]{1,0:T(8,128)(2,1)S(1)}, u32[]{:S(2)}, u32[]{:S(2)}) %collective-permute-start.22) | collective-permute-done | bytes 98336 | tf_op jit(solution)/shard_map/ppermute | solution.py:21
  67.4 2.1 %output_product.2.refs_5_ = f32[64,1792]{1,0:T(8,128)S(1)} custom-call(bf16[16,3072]{1,0:T(8,128)(2,1)S(1)} %attend.3.refs_0_, bf16[16,3072]{1,0:T(8,128)(2,1)S(1)} %collective-permute-done.21.refs_1_, bf16[16,3072]{1,0:T(8,128)(2,1)S(1)} %collective-permute-done.22.refs_2_, bf16[16,3072]{1,0:T(8,128)(2,1)S(1)} %collective-permute-done.23.refs_3_, ...), custom_call_target="tpu_custom_call" | custom-call | tf_op jit(solution)/shard_map/output_product/pallas_call | solution.py:543
  69.5 0.8 %output_product.3 = (f32[16,1792]{1,0:T(8,128)S(1)}, bf16[16,1792]{1,0:T(8,128)(2,1)S(1)}, bf16[16,1792]{1,0:T(8,128)(2,1)S(1)}, bf16[16,1792]{1,0:T(8,128)(2,1)S(1)}) custom-call(bf16[16,1024]{1,0:T(8,128)(2,1)S(1)} %attend.2.refs_0_, bf16[16,1024]{1,0:T(8,128)(2,1)S(1)} %collective-permute-done.18.refs_1_, ...), custom_call_target="tpu_custom_call" | custom-call | tf_op jit(solution)/shard_map/output_product/pallas_call | solution.py:543
  70.3 0.1 collective-permute-start.24
  70.4 0.9 %collective-permute-start.25 = (bf16[16,1792]{1,0:T(8,128)(2,1)S(1)}, bf16[16,1792]{1,0:T(8,128)(2,1)S(1)}, u32[]{:S(2)}, u32[]{:S(2)}) collective-permute-start(bf16[16,1792]{1,0:T(8,128)(2,1)S(1)} %get-tuple-element.65), channel_id=1, source_target_pairs={{0,2},{1,3},{2,0},{3,1},{4,6},{5,7},{6,4},{7,5},{8,10},{9,11},{10,... | collective-permute-start | bytes 172040 | tf_op jit(solution)/shard_map/ppermute | solution.py:21
  71.2 1.0 %collective-permute-start.26 = (bf16[16,1792]{1,0:T(8,128)(2,1)S(1)}, bf16[16,1792]{1,0:T(8,128)(2,1)S(1)}, u32[]{:S(2)}, u32[]{:S(2)}) collective-permute-start(bf16[16,1792]{1,0:T(8,128)(2,1)S(1)} %get-tuple-element.66), channel_id=1, source_target_pairs={{0,1},{1,0},{2,3},{3,2},{4,5},{5,4},{6,7},{7,6},{8,9},{9,8},{10,11... | collective-permute-start | bytes 172040 | tf_op jit(solution)/shard_map/ppermute | solution.py:21
  72.2 1.8 %collective-permute-done.24 = bf16[16,1792]{1,0:T(8,128)(2,1)S(1)} collective-permute-done((bf16[16,1792]{1,0:T(8,128)(2,1)S(1)}, bf16[16,1792]{1,0:T(8,128)(2,1)S(1)}, u32[]{:S(2)}, u32[]{:S(2)}) %collective-permute-start.24) | collective-permute-done | bytes 57376 | tf_op jit(solution)/shard_map/ppermute | solution.py:21
  74.1 1.1 %collective-permute-done.25 = bf16[16,1792]{1,0:T(8,128)(2,1)S(1)} collective-permute-done((bf16[16,1792]{1,0:T(8,128)(2,1)S(1)}, bf16[16,1792]{1,0:T(8,128)(2,1)S(1)}, u32[]{:S(2)}, u32[]{:S(2)}) %collective-permute-start.25) | collective-permute-done | bytes 57376 | tf_op jit(solution)/shard_map/ppermute | solution.py:21
  75.2 0.7 add_convert_fusion
  (40 shorter events, 0.1 us)
Async XLA Ops:
  0.0 4.5 %copy-start.9 = (bf16[64,7168]{1,0:T(8,128)(2,1)S(1)}, bf16[64,7168]{1,0:T(8,128)(2,1)}, u32[]{:S(2)}) copy-start(bf16[64,7168]{1,0:T(8,128)(2,1)} %prompts_ref.1) | copy-start | bytes 2752516
  0.0 1.1 %copy-start.10 = (bf16[448,576]{1,0:T(8,128)(2,1)S(1)}, bf16[448,576]{1,0:T(8,128)(2,1)}, u32[]{:S(2)}) copy-start(bf16[448,576]{1,0:T(8,128)(2,1)} %value_ref.1) | copy-start | bytes 1548292
  1.2 8.0 %copy-start = (bf16[32,128,512]{2,1,0:T(8,128)(2,1)S(1)}, bf16[32,128,512]{2,1,0:T(8,128)(2,1)}, u32[]{:S(2)}) copy-start(bf16[32,128,512]{2,1,0:T(8,128)(2,1)} %absorb_hbm.1) | copy-start | bytes 12582916
  1.2 8.0 %copy-start.1 = (bf16[32,512,128]{2,1,0:T(8,128)(2,1)S(1)}, bf16[32,512,128]{2,1,0:T(8,128)(2,1)}, u32[]{:S(2)}) copy-start(bf16[32,512,128]{2,1,0:T(8,128)(2,1)} %value_hbm.1) | copy-start | bytes 12582916
  1.3 8.0 %copy-start.2 = (bf16[8,256,576]{1,2,0:T(8,128)(2,1)S(1)}, bf16[8,256,576]{1,2,0:T(8,128)(2,1)}, u32[]{:S(2)}) copy-start(bf16[8,256,576]{1,2,0:T(8,128)(2,1)} %param.18) | copy-start | bytes 7077892
  1.3 8.0 %copy-start.3 = (bf16[8,2,32,192]{3,2,1,0:T(8,128)(2,1)S(1)}, bf16[8,2,32,192]{3,2,1,0:T(8,128)(2,1)}, u32[]{:S(2)}) copy-start(bf16[8,2,32,192]{3,2,1,0:T(8,128)(2,1)} %param.20) | copy-start | bytes 589828
  1.3 8.0 %copy-start.4 = (bf16[8,2,576]{2,1,0:T(2,128)(2,1)S(1)}, bf16[8,2,576]{2,1,0:T(2,128)(2,1)}, u32[]{:S(2)}) copy-start(bf16[8,2,576]{2,1,0:T(2,128)(2,1)} %fresh_hbm.1) | copy-start | bytes 55300
  1.3 8.0 %copy-start.6 = (s32[1024]{0:T(1024)S(1)}, s32[1024]{0:T(1024)}, u32[]{:S(2)}) copy-start(s32[1024]{0:T(1024)} %param.15) | copy-start | bytes 12292
  1.3 8.0 %copy-start.7 = (s32[16]{0:T(128)S(1)}, s32[16]{0:T(128)}, u32[]{:S(2)}) copy-start(s32[16]{0:T(128)} %length_hbm) | copy-start | bytes 196
  1.3 8.0 %copy-start.8 = (s32[16]{0:T(128)S(1)}, s32[16]{0:T(128)}, u32[]{:S(2)}) copy-start(s32[16]{0:T(128)} %slot_hbm.1) | copy-start | bytes 196
  1.3 22.6 %collective-permute-start.5 = (bf16[2016,128]{1,0:T(8,128)(2,1)S(1)}, bf16[2016,128]{1,0:T(8,128)(2,1)S(1)}, u32[]{:S(2)}, u32[]{:S(2)}) collective-permute-start(bf16[2016,128]{1,0:T(8,128)(2,1)S(1)} %pack_weight.1.refs_4_), channel_id=1, source_target_pairs={{0,3},{1,2},{2,1},{3,0},{4,7},{5,6},{6,5},{7,4},{8,11},{9,10},{10,... | collective-permute-start | bytes 1548296 | tf_op jit(solution)/shard_map/ppermute | solution.py:21
  3.8 23.4 %collective-permute-start.4 = (bf16[2016,128]{1,0:T(8,128)(2,1)S(1)}, bf16[2016,128]{1,0:T(8,128)(2,1)S(1)}, u32[]{:S(2)}, u32[]{:S(2)}) collective-permute-start(bf16[2016,128]{1,0:T(8,128)(2,1)S(1)} %pack_weight.1.refs_4_), channel_id=1, source_target_pairs={{0,2},{1,3},{2,0},{3,1},{4,6},{5,7},{6,4},{7,5},{8,10},{9,11},{10,... | collective-permute-start | bytes 1548296 | tf_op jit(solution)/shard_map/ppermute | solution.py:21
  4.4 4.5 %collective-permute-start = (bf16[2016,128]{1,0:T(8,128)(2,1)S(1)}, bf16[2016,128]{1,0:T(8,128)(2,1)S(1)}, u32[]{:S(2)}, u32[]{:S(2)}) collective-permute-start(bf16[2016,128]{1,0:T(8,128)(2,1)S(1)} %pack_weight.1.refs_4_), channel_id=1, source_target_pairs={{0,1},{1,0},{2,3},{3,2},{4,5},{5,4},{6,7},{7,6},{8,9},{9,8},{10,11... | collective-permute-start | bytes 1548296 | tf_op jit(solution)/shard_map/ppermute | solution.py:21
  4.7 19.2 %collective-permute-start.2 = (bf16[64,1792]{1,0:T(8,128)(2,1)S(1)}, bf16[64,1792]{1,0:T(8,128)(2,1)S(1)}, u32[]{:S(2)}, u32[]{:S(2)}) collective-permute-start(bf16[64,1792]{1,0:T(8,128)(2,1)S(1)} %get-tuple-element.51), channel_id=1, source_target_pairs={{0,8},{4,12},{8,0},{12,4},{1,9},{5,13},{9,1},{13,5},{2,10},{6,14},... | collective-permute-start | bytes 688136 | tf_op jit(solution)/shard_map/ppermute | solution.py:21
  7.6 16.3 %collective-permute-start.3 = (bf16[64,1792]{1,0:T(8,128)(2,1)S(1)}, bf16[64,1792]{1,0:T(8,128)(2,1)S(1)}, u32[]{:S(2)}, u32[]{:S(2)}) collective-permute-start(bf16[64,1792]{1,0:T(8,128)(2,1)S(1)} %get-tuple-element.52), channel_id=1, source_target_pairs={{0,12},{4,8},{8,4},{12,0},{1,13},{5,9},{9,5},{13,1},{2,14},{6,10},... | collective-permute-start | bytes 688136 | tf_op jit(solution)/shard_map/ppermute | solution.py:21
  8.9 18.2 %collective-permute-start.1 = (bf16[64,1792]{1,0:T(8,128)(2,1)S(1)}, bf16[64,1792]{1,0:T(8,128)(2,1)S(1)}, u32[]{:S(2)}, u32[]{:S(2)}) collective-permute-start(bf16[64,1792]{1,0:T(8,128)(2,1)S(1)} %get-tuple-element.50), channel_id=1, source_target_pairs={{0,4},{4,0},{8,12},{12,8},{1,5},{5,1},{9,13},{13,9},{2,6},{6,2},{1... | collective-permute-start | bytes 688136 | tf_op jit(solution)/shard_map/ppermute | solution.py:21
  9.3 34.4 %copy-start.5 = (f32[512]{0:T(512)S(1)}, f32[512]{0:T(512)}, u32[]{:S(2)}) copy-start(f32[512]{0:T(512)} %param.14) | copy-start | bytes 6148
  28.8 8.9 %collective-permute-start.6 = (bf16[288,128]{1,0:T(8,128)(2,1)S(1)}, bf16[288,128]{1,0:T(8,128)(2,1)S(1)}, u32[]{:S(2)}, u32[]{:S(2)}) collective-permute-start(bf16[288,128]{1,0:T(8,128)(2,1)S(1)} %get-tuple-element.55), channel_id=1, source_target_pairs={{0,12},{4,8},{8,4},{12,0},{1,13},{5,9},{9,5},{13,1},{2,14},{6,10},... | collective-permute-start | bytes 221192 | tf_op jit(solution)/shard_map/ppermute | solution.py:21
  33.3 10.4 %collective-permute-start.7 = (bf16[288,128]{1,0:T(8,128)(2,1)S(1)}, bf16[288,128]{1,0:T(8,128)(2,1)S(1)}, u32[]{:S(2)}, u32[]{:S(2)}) collective-permute-start(bf16[288,128]{1,0:T(8,128)(2,1)S(1)} %get-tuple-element.56), channel_id=1, source_target_pairs={{0,8},{4,12},{8,0},{12,4},{1,9},{5,13},{9,1},{13,5},{2,10},{6,14},... | collective-permute-start | bytes 221192 | tf_op jit(solution)/shard_map/ppermute | solution.py:21
  33.3 10.4 %collective-permute-start.8 = (bf16[288,128]{1,0:T(8,128)(2,1)S(1)}, bf16[288,128]{1,0:T(8,128)(2,1)S(1)}, u32[]{:S(2)}, u32[]{:S(2)}) collective-permute-start(bf16[288,128]{1,0:T(8,128)(2,1)S(1)} %get-tuple-element.57), channel_id=1, source_target_pairs={{0,4},{4,0},{8,12},{12,8},{1,5},{5,1},{9,13},{13,9},{2,6},{6,2},{1... | collective-permute-start | bytes 221192 | tf_op jit(solution)/shard_map/ppermute | solution.py:21
  34.0 11.6 %collective-permute-start.12 = (bf16[288,128]{1,0:T(8,128)(2,1)S(1)}, bf16[288,128]{1,0:T(8,128)(2,1)S(1)}, u32[]{:S(2)}, u32[]{:S(2)}) collective-permute-start(bf16[288,128]{1,0:T(8,128)(2,1)S(1)} %get-tuple-element.59), channel_id=1, source_target_pairs={{0,12},{4,8},{8,4},{12,0},{1,13},{5,9},{9,5},{13,1},{2,14},{6,10},... | collective-permute-start | bytes 221192 | tf_op jit(solution)/shard_map/ppermute | solution.py:21
  37.7 8.6 %collective-permute-start.13 = (bf16[288,128]{1,0:T(8,128)(2,1)S(1)}, bf16[288,128]{1,0:T(8,128)(2,1)S(1)}, u32[]{:S(2)}, u32[]{:S(2)}) collective-permute-start(bf16[288,128]{1,0:T(8,128)(2,1)S(1)} %get-tuple-element.60), channel_id=1, source_target_pairs={{0,8},{4,12},{8,0},{12,4},{1,9},{5,13},{9,1},{13,5},{2,10},{6,14},... | collective-permute-start | bytes 221192 | tf_op jit(solution)/shard_map/ppermute | solution.py:21
  37.7 8.6 %collective-permute-start.14 = (bf16[288,128]{1,0:T(8,128)(2,1)S(1)}, bf16[288,128]{1,0:T(8,128)(2,1)S(1)}, u32[]{:S(2)}, u32[]{:S(2)}) collective-permute-start(bf16[288,128]{1,0:T(8,128)(2,1)S(1)} %get-tuple-element.61), channel_id=1, source_target_pairs={{0,4},{4,0},{8,12},{12,8},{1,5},{5,1},{9,13},{13,9},{2,6},{6,2},{1... | collective-permute-start | bytes 221192 | tf_op jit(solution)/shard_map/ppermute | solution.py:21
  43.9 4.6 %collective-permute-start.11 = (bf16[288,128]{1,0:T(8,128)(2,1)S(1)}, bf16[288,128]{1,0:T(8,128)(2,1)S(1)}, u32[]{:S(2)}, u32[]{:S(2)}) collective-permute-start(bf16[288,128]{1,0:T(8,128)(2,1)S(1)} %finish_rows.2.refs_0_), channel_id=1, source_target_pairs={{0,3},{1,2},{2,1},{3,0},{4,7},{5,6},{6,5},{7,4},{8,11},{9,10},{10,... | collective-permute-start | bytes 221192 | tf_op jit(solution)/shard_map/ppermute | solution.py:21
  44.0 6.2 %collective-permute-start.10 = (bf16[288,128]{1,0:T(8,128)(2,1)S(1)}, bf16[288,128]{1,0:T(8,128)(2,1)S(1)}, u32[]{:S(2)}, u32[]{:S(2)}) collective-permute-start(bf16[288,128]{1,0:T(8,128)(2,1)S(1)} %finish_rows.2.refs_0_), channel_id=1, source_target_pairs={{0,2},{1,3},{2,0},{3,1},{4,6},{5,7},{6,4},{7,5},{8,10},{9,11},{10,... | collective-permute-start | bytes 221192 | tf_op jit(solution)/shard_map/ppermute | solution.py:21
  45.6 4.6 %collective-permute-start.9 = (bf16[288,128]{1,0:T(8,128)(2,1)S(1)}, bf16[288,128]{1,0:T(8,128)(2,1)S(1)}, u32[]{:S(2)}, u32[]{:S(2)}) collective-permute-start(bf16[288,128]{1,0:T(8,128)(2,1)S(1)} %finish_rows.2.refs_0_), channel_id=1, source_target_pairs={{0,1},{1,0},{2,3},{3,2},{4,5},{5,4},{6,7},{7,6},{8,9},{9,8},{10,11... | collective-permute-start | bytes 221192 | tf_op jit(solution)/shard_map/ppermute | solution.py:21
  46.5 5.2 %collective-permute-start.17 = (bf16[288,128]{1,0:T(8,128)(2,1)S(1)}, bf16[288,128]{1,0:T(8,128)(2,1)S(1)}, u32[]{:S(2)}, u32[]{:S(2)}) collective-permute-start(bf16[288,128]{1,0:T(8,128)(2,1)S(1)} %finish_rows.3.refs_4_), channel_id=1, source_target_pairs={{0,3},{1,2},{2,1},{3,0},{4,7},{5,6},{6,5},{7,4},{8,11},{9,10},{10,... | collective-permute-start | bytes 221192 | tf_op jit(solution)/shard_map/ppermute | solution.py:21
  47.3 6.1 %collective-permute-start.16 = (bf16[288,128]{1,0:T(8,128)(2,1)S(1)}, bf16[288,128]{1,0:T(8,128)(2,1)S(1)}, u32[]{:S(2)}, u32[]{:S(2)}) collective-permute-start(bf16[288,128]{1,0:T(8,128)(2,1)S(1)} %finish_rows.3.refs_4_), channel_id=1, source_target_pairs={{0,2},{1,3},{2,0},{3,1},{4,6},{5,7},{6,4},{7,5},{8,10},{9,11},{10,... | collective-permute-start | bytes 221192 | tf_op jit(solution)/shard_map/ppermute | solution.py:21
  48.5 4.8 %collective-permute-start.15 = (bf16[288,128]{1,0:T(8,128)(2,1)S(1)}, bf16[288,128]{1,0:T(8,128)(2,1)S(1)}, u32[]{:S(2)}, u32[]{:S(2)}) collective-permute-start(bf16[288,128]{1,0:T(8,128)(2,1)S(1)} %finish_rows.3.refs_4_), channel_id=1, source_target_pairs={{0,1},{1,0},{2,3},{3,2},{4,5},{5,4},{6,7},{7,6},{8,9},{9,8},{10,11... | collective-permute-start | bytes 221192 | tf_op jit(solution)/shard_map/ppermute | solution.py:21
  55.1 8.4 %collective-permute-start.23 = (bf16[16,3072]{1,0:T(8,128)(2,1)S(1)}, bf16[16,3072]{1,0:T(8,128)(2,1)S(1)}, u32[]{:S(2)}, u32[]{:S(2)}) collective-permute-start(bf16[16,3072]{1,0:T(8,128)(2,1)S(1)} %attend.3.refs_0_), channel_id=1, source_target_pairs={{0,12},{4,8},{8,4},{12,0},{1,13},{5,9},{9,5},{13,1},{2,14},{6,10},... | collective-permute-start | bytes 294920 | tf_op jit(solution)/shard_map/ppermute | solution.py:21
  58.0 9.4 %collective-permute-start.22 = (bf16[16,3072]{1,0:T(8,128)(2,1)S(1)}, bf16[16,3072]{1,0:T(8,128)(2,1)S(1)}, u32[]{:S(2)}, u32[]{:S(2)}) collective-permute-start(bf16[16,3072]{1,0:T(8,128)(2,1)S(1)} %attend.3.refs_0_), channel_id=1, source_target_pairs={{0,8},{4,12},{8,0},{12,4},{1,9},{5,13},{9,1},{13,5},{2,10},{6,14},... | collective-permute-start | bytes 294920 | tf_op jit(solution)/shard_map/ppermute | solution.py:21
  58.0 9.4 %collective-permute-start.21 = (bf16[16,3072]{1,0:T(8,128)(2,1)S(1)}, bf16[16,3072]{1,0:T(8,128)(2,1)S(1)}, u32[]{:S(2)}, u32[]{:S(2)}) collective-permute-start(bf16[16,3072]{1,0:T(8,128)(2,1)S(1)} %attend.3.refs_0_), channel_id=1, source_target_pairs={{0,4},{4,0},{8,12},{12,8},{1,5},{5,1},{9,13},{13,9},{2,6},{6,2},{1... | collective-permute-start | bytes 294920 | tf_op jit(solution)/shard_map/ppermute | solution.py:21
  60.6 8.9 %collective-permute-start.20 = (bf16[16,1024]{1,0:T(8,128)(2,1)S(1)}, bf16[16,1024]{1,0:T(8,128)(2,1)S(1)}, u32[]{:S(2)}, u32[]{:S(2)}) collective-permute-start(bf16[16,1024]{1,0:T(8,128)(2,1)S(1)} %attend.2.refs_0_), channel_id=1, source_target_pairs={{0,12},{4,8},{8,4},{12,0},{1,13},{5,9},{9,5},{13,1},{2,14},{6,10},... | collective-permute-start | bytes 98312 | tf_op jit(solution)/shard_map/ppermute | solution.py:21
  63.5 6.0 %collective-permute-start.19 = (bf16[16,1024]{1,0:T(8,128)(2,1)S(1)}, bf16[16,1024]{1,0:T(8,128)(2,1)S(1)}, u32[]{:S(2)}, u32[]{:S(2)}) collective-permute-start(bf16[16,1024]{1,0:T(8,128)(2,1)S(1)} %attend.2.refs_0_), channel_id=1, source_target_pairs={{0,8},{4,12},{8,0},{12,4},{1,9},{5,13},{9,1},{13,5},{2,10},{6,14},... | collective-permute-start | bytes 98312 | tf_op jit(solution)/shard_map/ppermute | solution.py:21
  63.5 6.0 %collective-permute-start.18 = (bf16[16,1024]{1,0:T(8,128)(2,1)S(1)}, bf16[16,1024]{1,0:T(8,128)(2,1)S(1)}, u32[]{:S(2)}, u32[]{:S(2)}) collective-permute-start(bf16[16,1024]{1,0:T(8,128)(2,1)S(1)} %attend.2.refs_0_), channel_id=1, source_target_pairs={{0,4},{4,0},{8,12},{12,8},{1,5},{5,1},{9,13},{13,9},{2,6},{6,2},{1... | collective-permute-start | bytes 98312 | tf_op jit(solution)/shard_map/ppermute | solution.py:21
  70.3 3.8 %collective-permute-start.24 = (bf16[16,1792]{1,0:T(8,128)(2,1)S(1)}, bf16[16,1792]{1,0:T(8,128)(2,1)S(1)}, u32[]{:S(2)}, u32[]{:S(2)}) collective-permute-start(bf16[16,1792]{1,0:T(8,128)(2,1)S(1)} %get-tuple-element.64), channel_id=1, source_target_pairs={{0,3},{1,2},{2,1},{3,0},{4,7},{5,6},{6,5},{7,4},{8,11},{9,10},{10,... | collective-permute-start | bytes 172040 | tf_op jit(solution)/shard_map/ppermute | solution.py:21
  70.4 4.8 %collective-permute-start.25 = (bf16[16,1792]{1,0:T(8,128)(2,1)S(1)}, bf16[16,1792]{1,0:T(8,128)(2,1)S(1)}, u32[]{:S(2)}, u32[]{:S(2)}) collective-permute-start(bf16[16,1792]{1,0:T(8,128)(2,1)S(1)} %get-tuple-element.65), channel_id=1, source_target_pairs={{0,2},{1,3},{2,0},{3,1},{4,6},{5,7},{6,4},{7,5},{8,10},{9,11},{10,... | collective-permute-start | bytes 172040 | tf_op jit(solution)/shard_map/ppermute | solution.py:21
  71.2 3.9 %collective-permute-start.26 = (bf16[16,1792]{1,0:T(8,128)(2,1)S(1)}, bf16[16,1792]{1,0:T(8,128)(2,1)S(1)}, u32[]{:S(2)}, u32[]{:S(2)}) collective-permute-start(bf16[16,1792]{1,0:T(8,128)(2,1)S(1)} %get-tuple-element.66), channel_id=1, source_target_pairs={{0,1},{1,0},{2,3},{3,2},{4,5},{5,4},{6,7},{7,6},{8,9},{9,8},{10,11... | collective-permute-start | bytes 172040 | tf_op jit(solution)/shard_map/ppermute | solution.py:21

commit v8 on v7

--- a/solution.py
+++ b/solution.py
@@ -350,13 +350,33 @@
       value, out_weight)
 
 
-def project_kernel(dev_count, side_count, target_ref, *refs):
+def stack_kernel(*refs):
+    out_ref = refs[-1]
+    rows = refs[0].shape[0]
+    for n, ref in enumerate(refs[:-1]):
+        k = (len(refs) - 1 - n) % (len(refs) - 1)
+        out_ref[k * rows : (k + 1) * rows, :] = ref[...]
+
+
+def stack_rows(pieces):
+    rows, width = pieces[0].shape
+    return pl.pallas_call(
+        stack_kernel,
+        out_shape=jax.ShapeDtypeStruct((len(pieces) * rows, width), bf16),
+        in_specs=[in_vmem] * len(pieces),
+        out_specs=in_vmem,
+        compiler_params=pltpu.CompilerParams(vmem_limit_bytes=8 * mib),
+        cost_estimate=pl.CostEstimate(flops=2 * 10**10, bytes_accessed=10**6, transcendentals=0),
+        name="stack_rows",
+    )(pieces[0], *pieces[:0:-1])
+
+
+def project_kernel(dev_count, side_count, target_ref, x_ref, *refs):
     my_side = lax.axis_index("side")
-    x_refs = refs[:dev_count]
-    weight_refs = refs[dev_count : dev_count + side_count]
-    out_refs = refs[dev_count + side_count : -3]
-    x_rows, slab_weight, rows = refs[-3:]
-    tok_rows = x_refs[0].shape[0]
+    weight_refs = refs[:side_count]
+    out_refs = refs[side_count:-2]
+    slab_weight, rows = refs[-2:]
+    tok_rows = x_ref.shape[0] // dev_count
     full = slab_weight.shape[1] // 128
     if side_count > 1:
         shard = slab_weight.shape[0] // side_count
@@ -366,10 +386,8 @@
             for n, tile in enumerate(tiles):
                 slab_weight[pl.ds(first, shard), n * 128 : (n + 1) * 128] = tile
             slab_weight[pl.ds(first, shard), full * 128 :] = rest
-    for k in range(dev_count):
-        x_rows[k * tok_rows : (k + 1) * tok_rows, :] = x_refs[k][...]
     slab = slab_weight[...] if side_count > 1 else weight_refs[0][...]
-    raw = jnp.dot(x_rows[...], slab, preferred_element_type=f32).astype(bf16)
+    raw = jnp.dot(x_ref[...], slab, preferred_element_type=f32).astype(bf16)
     rows[...] = raw
     target = target_ref[...]
     half_rows = tok_rows
@@ -382,9 +400,8 @@
             store_packed(out_refs[j + n], placed[n * half_rows : (n + 1) * half_rows])
 
 
-def project(x_pieces, weights, target, width):
-    dev_count = len(x_pieces)
-    tok_rows, slab = x_pieces[0].shape
+def project(x_rows, weights, target, width, dev_count):
+    tok_rows, slab = x_rows.shape[0] // dev_count, x_rows.shape[1]
     return pl.pallas_call(
         functools.partial(project_kernel, dev_count, len(weights)),
         out_shape=[
@@ -393,16 +410,15 @@
             )
             for j in range(2 * dev_count)
         ],
-        in_specs=[in_vmem] * (1 + dev_count + len(weights)),
+        in_specs=[in_vmem] * (2 + len(weights)),
         out_specs=[in_vmem] * (2 * dev_count),
         scratch_shapes=[
-            pltpu.VMEM((dev_count * tok_rows, slab), bf16),
             pltpu.VMEM((slab, width), bf16),
             pltpu.VMEM((target.shape[1], width), bf16),
         ],
         compiler_params=pltpu.CompilerParams(vmem_limit_bytes=20 * mib),
         name="project",
-    )(target, *x_pieces, *weights)
+    )(target, x_rows, *weights)
 
 
 def finish_kernel(which, gain_ref, cos_ref, sin_ref, *refs):
@@ -581,12 +597,10 @@
     x_pieces = list(split_columns(prompts, dev_count))
     packs = shard_rows % 32 == 0
     weights = [pack_weight(latent_weight) if packs else latent_weight] + [None] * (side_count - 1)
-    for k in sorted(range(2, dev_count), reverse=True):
+    for k in range(2, side_count, 2):
+        weights[k] = swap(weights[0], "side", k)
+    for k in sorted(range(1, dev_count), reverse=True):
         x_pieces[k] = swap(x_pieces[k], "dev", k)
-    for k in range(1, side_count):
-        weights[k] = swap(weights[0], "side", k)
-    x_pieces[1], weights[1] = lax.optimization_barrier((x_pieces[1], weights[1]))
-    x_pieces[1] = swap(x_pieces[1], "dev", 1)
 
     score_scale = queries.shape[-1] ** (-0.5)
     half = rope_width // 2
@@ -601,6 +615,9 @@
         jnp.swapaxes(latent_cache, 1, 2), new_latent, value_absorb, out_weight,
     )
 
+    weights[0::2], top_held = lax.optimization_barrier((weights[0::2], top_held))
+    for k in range(0, side_count, 2):
+        weights[k + 1] = swap(weights[k], "side", 1)
     if not packs:
         my_side = lax.axis_index("side")
         held = jnp.zeros((side_count, shard_rows, kv_width), bf16)
@@ -608,7 +625,7 @@
             held = lax.dynamic_update_slice(held, weights[k][None], (my_side ^ k, 0, 0))
         weights = [held.reshape(slab, kv_width)]
 
-    routed = project(x_pieces, weights, target, kv_width)
+    routed = project(stack_rows(x_pieces), weights, target, kv_width, dev_count)
     pieces = []
     for which in range(2):
         half = list(routed[which * dev_count : (which + 1) * dev_count])

time: 76 us -> 72.2 us (0.950)
  starting transfers between devices: 33.4 us -> 31.2 us
  waiting for transfers between devices: 24.7 us -> 23 us
    ppermute x27, starting transfers between devices: 33.4 us -> 31.2 us  [swap(): return lax.ppermute(value, axis, [(i, i ^ step) for i in range(count)])]
    ppermute x27, waiting for transfers between devices: 24.7 us -> 23 us  [swap(): return lax.ppermute(value, axis, [(i, i ^ step) for i in range(count)])]
  transfers between devices with their start and end apart: 27 -> 27, of which waited for: 11 -> 11; matrix products, arithmetic and copies ran while one was open for 0% -> 0% of each run, Pallas kernels for 15% -> 16%
where the time goes in v8:
time: 72.2 us; the launch traced here: 72.1 us
  starting transfers between devices  31.2 us (43%)
  waiting for transfers between devices  23 us (32%)
  Pallas kernels  15.7 us (22%)
  local copies, waits for them, and re-layouts  1.2 us (2%)
    ppermute x27, starting transfers between devices, swap(): return lax.ppermute(value, axis, [(i, i ^ step) for i in range(count)])  31.2 us
    ppermute x27, waiting for transfers between devices, swap(): return lax.ppermute(value, axis, [(i, i ^ step) for i in range(count)])  23 us
    pallas_call x1, Pallas kernels, prepare(): pl.pallas_call(functools.partial(prepare_kernel, scale, steps, (dev_count...  7.6 us
    pallas_call x2, Pallas kernels, output_product(): pl.pallas_call(functools.partial(output_kernel, dev_count, side_count, st...  2.84 us
    pallas_call x2, Pallas kernels, attend(): pl.pallas_call(functools.partial(attend_kernel, scale, cap_slots, steps,...  2.77 us
    pallas_call x1, Pallas kernels, project(): pl.pallas_call(functools.partial(project_kernel, dev_count, len(weights))...  1.7 us
  transfers between devices with their start and end apart: 27, of which 11 were waited for; matrix products, arithmetic and copies ran while one was open for 0% of the time, Pallas kernels for 16%

profile of v8, /device:TPU:0, one launch (start us, length us, event | category | flops | bytes accessed | tf_op | source)
XLA Modules:
  0.0 72.1 jit_solution(13461170290268457757)
XLA Ops:
  0.0 1.1 %copy-done.10 = bf16[448,576]{1,0:T(8,128)(2,1)S(1)} copy-done((bf16[448,576]{1,0:T(8,128)(2,1)S(1)}, bf16[448,576]{1,0:T(8,128)(2,1)}, u32[]{:S(2)}) %copy-start.10) | copy-done | bytes 516120
  1.1 0.1 pack_weight.1.refs_0_
  1.3 0.0 copy-start.2
  1.3 3.0 %collective-permute-start = (bf16[2016,128]{1,0:T(8,128)(2,1)S(1)}, bf16[2016,128]{1,0:T(8,128)(2,1)S(1)}, u32[]{:S(2)}, u32[]{:S(2)}) collective-permute-start(bf16[2016,128]{1,0:T(8,128)(2,1)S(1)} %pack_weight.1.refs_0_), channel_id=1, source_target_pairs={{0,2},{1,3},{2,0},{3,1},{4,6},{5,7},{6,4},{7,5},{8,10},{9,11},{10,... | collective-permute-start | bytes 1548296 | tf_op jit(solution)/shard_map/ppermute | solution.py:21
  4.3 0.2 split_columns.1
  4.5 3.7 %collective-permute-start.1 = (bf16[64,1792]{1,0:T(8,128)(2,1)S(1)}, bf16[64,1792]{1,0:T(8,128)(2,1)S(1)}, u32[]{:S(2)}, u32[]{:S(2)}) collective-permute-start(bf16[64,1792]{1,0:T(8,128)(2,1)S(1)} %get-tuple-element.51), channel_id=1, source_target_pairs={{0,12},{4,8},{8,4},{12,0},{1,13},{5,9},{9,5},{13,1},{2,14},{6,10},... | collective-permute-start | bytes 688136 | tf_op jit(solution)/shard_map/ppermute | solution.py:21
  8.2 0.8 %collective-permute-start.3 = (bf16[64,1792]{1,0:T(8,128)(2,1)S(1)}, bf16[64,1792]{1,0:T(8,128)(2,1)S(1)}, u32[]{:S(2)}, u32[]{:S(2)}) collective-permute-start(bf16[64,1792]{1,0:T(8,128)(2,1)S(1)} %get-tuple-element.53), channel_id=1, source_target_pairs={{0,4},{4,0},{8,12},{12,8},{1,5},{5,1},{9,13},{13,9},{2,6},{6,2},{1... | collective-permute-start | bytes 688136 | tf_op jit(solution)/shard_map/ppermute | solution.py:21
  9.1 7.6 %prepare.1 = (bf16[512,576]{1,0:T(8,128)(2,1)S(1)}, f32[512,128]{1,0:T(8,128)S(1)}, f32[512,128]{1,0:T(8,128)S(1)}, f32[4,512,128]{2,1,0:T(8,128)S(1)}, f32[16,1...) custom-call(f32[1,32]{1,0:T(1,128)S(1)} %negate_power_fusion.inverse, ...), custom_call_target="tpu_custom_call" | custom-call | flops 4000000000 | bytes 28000000 | tf_op jit(solution)/shard_map/prepare/pallas_call | solution.py:323
  16.7 0.1 collective-permute-start.4
  16.8 0.5 collective-permute-start.5
  17.3 10.1 %collective-permute-done.2.refs_2_ = bf16[64,1792]{1,0:T(8,128)(2,1)S(1)} collective-permute-done((bf16[64,1792]{1,0:T(8,128)(2,1)S(1)}, bf16[64,1792]{1,0:T(8,128)(2,1)S(1)}, u32[]{:S(2)}, u32[]{:S(2)}) %collective-permute-start.2) | collective-permute-done | bytes 229408 | tf_op jit(solution)/shard_map/ppermute | solution.py:21
  27.4 0.1 stack_rows.1.x_ref
  27.5 1.7 %project.1 = (f32[288,128]{1,0:T(8,128)S(1)}, bf16[288,128]{1,0:T(8,128)(2,1)S(1)}, bf16[288,128]{1,0:T(8,128)(2,1)S(1)}, bf16[288,128]{1,0:T(8,128)(2,1)S(1)}, ...) custom-call(s32[1,256]{1,0:T(1,128)S(1)} %get-tuple-element.49.targe, ...), custom_call_target="tpu_custom_call" | custom-call | tf_op jit(solution)/shard_map/project/pallas_call | solution.py:405
  29.2 2.5 %collective-permute-start.6 = (bf16[288,128]{1,0:T(8,128)(2,1)S(1)}, bf16[288,128]{1,0:T(8,128)(2,1)S(1)}, u32[]{:S(2)}, u32[]{:S(2)}) collective-permute-start(bf16[288,128]{1,0:T(8,128)(2,1)S(1)} %get-tuple-element.57), channel_id=1, source_target_pairs={{0,12},{4,8},{8,4},{12,0},{1,13},{5,9},{9,5},{13,1},{2,14},{6,10},... | collective-permute-start | bytes 221192 | tf_op jit(solution)/shard_map/ppermute | solution.py:21
  31.8 1.9 %collective-permute-start.8 = (bf16[288,128]{1,0:T(8,128)(2,1)S(1)}, bf16[288,128]{1,0:T(8,128)(2,1)S(1)}, u32[]{:S(2)}, u32[]{:S(2)}) collective-permute-start(bf16[288,128]{1,0:T(8,128)(2,1)S(1)} %get-tuple-element.59), channel_id=1, source_target_pairs={{0,4},{4,0},{8,12},{12,8},{1,5},{5,1},{9,13},{13,9},{2,6},{6,2},{1... | collective-permute-start | bytes 221192 | tf_op jit(solution)/shard_map/ppermute | solution.py:21
  33.7 2.5 %collective-permute-start.12 = (bf16[288,128]{1,0:T(8,128)(2,1)S(1)}, bf16[288,128]{1,0:T(8,128)(2,1)S(1)}, u32[]{:S(2)}, u32[]{:S(2)}) collective-permute-start(bf16[288,128]{1,0:T(8,128)(2,1)S(1)} %get-tuple-element.61), channel_id=1, source_target_pairs={{0,12},{4,8},{8,4},{12,0},{1,13},{5,9},{9,5},{13,1},{2,14},{6,10},... | collective-permute-start | bytes 221192 | tf_op jit(solution)/shard_map/ppermute | solution.py:21
  36.1 1.9 %collective-permute-start.14 = (bf16[288,128]{1,0:T(8,128)(2,1)S(1)}, bf16[288,128]{1,0:T(8,128)(2,1)S(1)}, u32[]{:S(2)}, u32[]{:S(2)}) collective-permute-start(bf16[288,128]{1,0:T(8,128)(2,1)S(1)} %get-tuple-element.63), channel_id=1, source_target_pairs={{0,4},{4,0},{8,12},{12,8},{1,5},{5,1},{9,13},{13,9},{2,6},{6,2},{1... | collective-permute-start | bytes 221192 | tf_op jit(solution)/shard_map/ppermute | solution.py:21
  38.1 2.9 %collective-permute-done.7.refs_2_ = bf16[288,128]{1,0:T(8,128)(2,1)S(1)} collective-permute-done((bf16[288,128]{1,0:T(8,128)(2,1)S(1)}, bf16[288,128]{1,0:T(8,128)(2,1)S(1)}, u32[]{:S(2)}, u32[]{:S(2)}) %collective-permute-start.7) | collective-permute-done | bytes 73760 | tf_op jit(solution)/shard_map/ppermute | solution.py:21
  41.0 0.2 finish_rows.2.refs_0_
  41.2 0.1 collective-permute-start.11
  41.3 0.6 collective-permute-start.10
  41.9 1.3 %collective-permute-start.9 = (bf16[288,128]{1,0:T(8,128)(2,1)S(1)}, bf16[288,128]{1,0:T(8,128)(2,1)S(1)}, u32[]{:S(2)}, u32[]{:S(2)}) collective-permute-start(bf16[288,128]{1,0:T(8,128)(2,1)S(1)} %finish_rows.2.refs_0_), channel_id=1, source_target_pairs={{0,1},{1,0},{2,3},{3,2},{4,5},{5,4},{6,7},{7,6},{8,9},{9,8},{10,11... | collective-permute-start | bytes 221192 | tf_op jit(solution)/shard_map/ppermute | solution.py:21
  43.1 0.7 collective-permute-done.13.refs_2_
  43.8 0.2 finish_rows.3.refs_4_
  44.1 0.1 collective-permute-start.17
  44.1 0.9 %collective-permute-start.16 = (bf16[288,128]{1,0:T(8,128)(2,1)S(1)}, bf16[288,128]{1,0:T(8,128)(2,1)S(1)}, u32[]{:S(2)}, u32[]{:S(2)}) collective-permute-start(bf16[288,128]{1,0:T(8,128)(2,1)S(1)} %finish_rows.3.refs_4_), channel_id=1, source_target_pairs={{0,2},{1,3},{2,0},{3,1},{4,6},{5,7},{6,4},{7,5},{8,10},{9,11},{10,... | collective-permute-start | bytes 221192 | tf_op jit(solution)/shard_map/ppermute | solution.py:21
  45.1 0.2 collective-permute-done.11.refs_3_
  45.2 0.7 %collective-permute-start.15 = (bf16[288,128]{1,0:T(8,128)(2,1)S(1)}, bf16[288,128]{1,0:T(8,128)(2,1)S(1)}, u32[]{:S(2)}, u32[]{:S(2)}) collective-permute-start(bf16[288,128]{1,0:T(8,128)(2,1)S(1)} %finish_rows.3.refs_4_), channel_id=1, source_target_pairs={{0,1},{1,0},{2,3},{3,2},{4,5},{5,4},{6,7},{7,6},{8,9},{9,8},{10,11... | collective-permute-start | bytes 221192 | tf_op jit(solution)/shard_map/ppermute | solution.py:21
  46.0 0.5 collective-permute-done.10.refs_2_
  46.5 2.2 %collective-permute-done.17.refs_7_ = bf16[288,128]{1,0:T(8,128)(2,1)S(1)} collective-permute-done((bf16[288,128]{1,0:T(8,128)(2,1)S(1)}, bf16[288,128]{1,0:T(8,128)(2,1)S(1)}, u32[]{:S(2)}, u32[]{:S(2)}) %collective-permute-start.17) | collective-permute-done | bytes 73760 | tf_op jit(solution)/shard_map/ppermute | solution.py:21
  48.6 0.8 %collective-permute-done.16.refs_6_ = bf16[288,128]{1,0:T(8,128)(2,1)S(1)} collective-permute-done((bf16[288,128]{1,0:T(8,128)(2,1)S(1)}, bf16[288,128]{1,0:T(8,128)(2,1)S(1)}, u32[]{:S(2)}, u32[]{:S(2)}) %collective-permute-start.16) | collective-permute-done | bytes 73760 | tf_op jit(solution)/shard_map/ppermute | solution.py:21
  49.4 1.8 %attend.3.refs_0_ = bf16[16,3072]{1,0:T(8,128)(2,1)S(1)} custom-call(bf16[512,576]{1,0:T(8,128)(2,1)S(1)} %get-tuple-element.39.query_ref, s32[1,512]{1,0:T(1,128)S(1)} %get-tuple-element.40.slot_ref, f32[512,128]{1,0:T(8,128)S(1)} %get-tuple-element.42.top_ref, f32[512,128]{1,0:T(8,128)S(1)} %get-tuple-element.43.sum_ref, ...), custom_call_target="tpu_custom_call" | custom-call | tf_op jit(solution)/shard_map/attend/pallas_call | solution.py:505
  51.2 2.0 %collective-permute-start.23 = (bf16[16,3072]{1,0:T(8,128)(2,1)S(1)}, bf16[16,3072]{1,0:T(8,128)(2,1)S(1)}, u32[]{:S(2)}, u32[]{:S(2)}) collective-permute-start(bf16[16,3072]{1,0:T(8,128)(2,1)S(1)} %attend.3.refs_0_), channel_id=1, source_target_pairs={{0,12},{4,8},{8,4},{12,0},{1,13},{5,9},{9,5},{13,1},{2,14},{6,10},... | collective-permute-start | bytes 294920 | tf_op jit(solution)/shard_map/ppermute | solution.py:21
  53.1 0.2 collective-permute-start.22
  53.4 2.3 %collective-permute-start.21 = (bf16[16,3072]{1,0:T(8,128)(2,1)S(1)}, bf16[16,3072]{1,0:T(8,128)(2,1)S(1)}, u32[]{:S(2)}, u32[]{:S(2)}) collective-permute-start(bf16[16,3072]{1,0:T(8,128)(2,1)S(1)} %attend.3.refs_0_), channel_id=1, source_target_pairs={{0,4},{4,0},{8,12},{12,8},{1,5},{5,1},{9,13},{13,9},{2,6},{6,2},{1... | collective-permute-start | bytes 294920 | tf_op jit(solution)/shard_map/ppermute | solution.py:21
  55.6 1.0 %attend.2.refs_0_ = bf16[16,1024]{1,0:T(8,128)(2,1)S(1)} custom-call(bf16[512,576]{1,0:T(8,128)(2,1)S(1)} %get-tuple-element.39.query_ref, s32[1,512]{1,0:T(1,128)S(1)} %get-tuple-element.40.slot_ref, f32[512,128]{1,0:T(8,128)S(1)} %get-tuple-element.42.top_ref, f32[512,128]{1,0:T(8,128)S(1)} %get-tuple-element.43.sum_ref, ...), custom_call_target="tpu_custom_call" | custom-call | tf_op jit(solution)/shard_map/attend/pallas_call | solution.py:505
  56.7 2.0 %collective-permute-start.20 = (bf16[16,1024]{1,0:T(8,128)(2,1)S(1)}, bf16[16,1024]{1,0:T(8,128)(2,1)S(1)}, u32[]{:S(2)}, u32[]{:S(2)}) collective-permute-start(bf16[16,1024]{1,0:T(8,128)(2,1)S(1)} %attend.2.refs_0_), channel_id=1, source_target_pairs={{0,12},{4,8},{8,4},{12,0},{1,13},{5,9},{9,5},{13,1},{2,14},{6,10},... | collective-permute-start | bytes 98312 | tf_op jit(solution)/shard_map/ppermute | solution.py:21
  58.6 0.2 collective-permute-done.23.refs_3_
  58.8 2.3 %collective-permute-start.18 = (bf16[16,1024]{1,0:T(8,128)(2,1)S(1)}, bf16[16,1024]{1,0:T(8,128)(2,1)S(1)}, u32[]{:S(2)}, u32[]{:S(2)}) collective-permute-start(bf16[16,1024]{1,0:T(8,128)(2,1)S(1)} %attend.2.refs_0_), channel_id=1, source_target_pairs={{0,4},{4,0},{8,12},{12,8},{1,5},{5,1},{9,13},{13,9},{2,6},{6,2},{1... | collective-permute-start | bytes 98312 | tf_op jit(solution)/shard_map/ppermute | solution.py:21
  61.1 1.9 %collective-permute-done.22.refs_2_ = bf16[16,3072]{1,0:T(8,128)(2,1)S(1)} collective-permute-done((bf16[16,3072]{1,0:T(8,128)(2,1)S(1)}, bf16[16,3072]{1,0:T(8,128)(2,1)S(1)}, u32[]{:S(2)}, u32[]{:S(2)}) %collective-permute-start.22) | collective-permute-done | bytes 98336 | tf_op jit(solution)/shard_map/ppermute | solution.py:21
  63.0 2.1 %output_product.2.refs_5_ = f32[64,1792]{1,0:T(8,128)S(1)} custom-call(bf16[16,3072]{1,0:T(8,128)(2,1)S(1)} %attend.3.refs_0_, bf16[16,3072]{1,0:T(8,128)(2,1)S(1)} %collective-permute-done.21.refs_1_, bf16[16,3072]{1,0:T(8,128)(2,1)S(1)} %collective-permute-done.22.refs_2_, bf16[16,3072]{1,0:T(8,128)(2,1)S(1)} %collective-permute-done.23.refs_3_, ...), custom_call_target="tpu_custom_call" | custom-call | tf_op jit(solution)/shard_map/output_product/pallas_call | solution.py:559
  65.1 0.8 %output_product.3 = (f32[16,1792]{1,0:T(8,128)S(1)}, bf16[16,1792]{1,0:T(8,128)(2,1)S(1)}, bf16[16,1792]{1,0:T(8,128)(2,1)S(1)}, bf16[16,1792]{1,0:T(8,128)(2,1)S(1)}) custom-call(bf16[16,1024]{1,0:T(8,128)(2,1)S(1)} %attend.2.refs_0_, bf16[16,1024]{1,0:T(8,128)(2,1)S(1)} %collective-permute-done.18.refs_1_, ...), custom_call_target="tpu_custom_call" | custom-call | tf_op jit(solution)/shard_map/output_product/pallas_call | solution.py:559
  65.9 1.1 %collective-permute-start.24 = (bf16[16,1792]{1,0:T(8,128)(2,1)S(1)}, bf16[16,1792]{1,0:T(8,128)(2,1)S(1)}, u32[]{:S(2)}, u32[]{:S(2)}) collective-permute-start(bf16[16,1792]{1,0:T(8,128)(2,1)S(1)} %get-tuple-element.66), channel_id=1, source_target_pairs={{0,3},{1,2},{2,1},{3,0},{4,7},{5,6},{6,5},{7,4},{8,11},{9,10},{10,... | collective-permute-start | bytes 172040 | tf_op jit(solution)/shard_map/ppermute | solution.py:21
  67.0 0.7 collective-permute-start.25
  67.7 0.2 collective-permute-start.26
  67.8 2.1 %collective-permute-done.24 = bf16[16,1792]{1,0:T(8,128)(2,1)S(1)} collective-permute-done((bf16[16,1792]{1,0:T(8,128)(2,1)S(1)}, bf16[16,1792]{1,0:T(8,128)(2,1)S(1)}, u32[]{:S(2)}, u32[]{:S(2)}) %collective-permute-start.24) | collective-permute-done | bytes 57376 | tf_op jit(solution)/shard_map/ppermute | solution.py:21
  69.9 1.5 %collective-permute-done.25 = bf16[16,1792]{1,0:T(8,128)(2,1)S(1)} collective-permute-done((bf16[16,1792]{1,0:T(8,128)(2,1)S(1)}, bf16[16,1792]{1,0:T(8,128)(2,1)S(1)}, u32[]{:S(2)}, u32[]{:S(2)}) %collective-permute-start.25) | collective-permute-done | bytes 57376 | tf_op jit(solution)/shard_map/ppermute | solution.py:21
  71.4 0.7 add_convert_fusion
  (41 shorter events, 0.1 us)
Async XLA Ops:
  0.0 4.3 %copy-start.9 = (bf16[64,7168]{1,0:T(8,128)(2,1)S(1)}, bf16[64,7168]{1,0:T(8,128)(2,1)}, u32[]{:S(2)}) copy-start(bf16[64,7168]{1,0:T(8,128)(2,1)} %prompts_ref.1) | copy-start | bytes 2752516
  0.0 1.1 %copy-start.10 = (bf16[448,576]{1,0:T(8,128)(2,1)S(1)}, bf16[448,576]{1,0:T(8,128)(2,1)}, u32[]{:S(2)}) copy-start(bf16[448,576]{1,0:T(8,128)(2,1)} %value_ref.1) | copy-start | bytes 1548292
  1.2 7.8 %copy-start = (bf16[32,128,512]{2,1,0:T(8,128)(2,1)S(1)}, bf16[32,128,512]{2,1,0:T(8,128)(2,1)}, u32[]{:S(2)}) copy-start(bf16[32,128,512]{2,1,0:T(8,128)(2,1)} %absorb_hbm.1) | copy-start | bytes 12582916
  1.2 7.8 %copy-start.1 = (bf16[32,512,128]{2,1,0:T(8,128)(2,1)S(1)}, bf16[32,512,128]{2,1,0:T(8,128)(2,1)}, u32[]{:S(2)}) copy-start(bf16[32,512,128]{2,1,0:T(8,128)(2,1)} %value_hbm.1) | copy-start | bytes 12582916
  1.3 7.8 %copy-start.2 = (bf16[8,256,576]{1,2,0:T(8,128)(2,1)S(1)}, bf16[8,256,576]{1,2,0:T(8,128)(2,1)}, u32[]{:S(2)}) copy-start(bf16[8,256,576]{1,2,0:T(8,128)(2,1)} %param.18) | copy-start | bytes 7077892
  1.3 7.8 %copy-start.3 = (bf16[8,2,32,192]{3,2,1,0:T(8,128)(2,1)S(1)}, bf16[8,2,32,192]{3,2,1,0:T(8,128)(2,1)}, u32[]{:S(2)}) copy-start(bf16[8,2,32,192]{3,2,1,0:T(8,128)(2,1)} %param.20) | copy-start | bytes 589828
  1.3 7.8 %copy-start.4 = (bf16[8,2,576]{2,1,0:T(2,128)(2,1)S(1)}, bf16[8,2,576]{2,1,0:T(2,128)(2,1)}, u32[]{:S(2)}) copy-start(bf16[8,2,576]{2,1,0:T(2,128)(2,1)} %fresh_hbm.1) | copy-start | bytes 55300
  1.3 7.8 %copy-start.6 = (s32[1024]{0:T(1024)S(1)}, s32[1024]{0:T(1024)}, u32[]{:S(2)}) copy-start(s32[1024]{0:T(1024)} %param.15) | copy-start | bytes 12292
  1.3 7.8 %copy-start.7 = (s32[16]{0:T(128)S(1)}, s32[16]{0:T(128)}, u32[]{:S(2)}) copy-start(s32[16]{0:T(128)} %length_hbm) | copy-start | bytes 196
  1.3 7.7 %copy-start.8 = (s32[16]{0:T(128)S(1)}, s32[16]{0:T(128)}, u32[]{:S(2)}) copy-start(s32[16]{0:T(128)} %slot_hbm.1) | copy-start | bytes 196
  1.3 15.4 %collective-permute-start = (bf16[2016,128]{1,0:T(8,128)(2,1)S(1)}, bf16[2016,128]{1,0:T(8,128)(2,1)S(1)}, u32[]{:S(2)}, u32[]{:S(2)}) collective-permute-start(bf16[2016,128]{1,0:T(8,128)(2,1)S(1)} %pack_weight.1.refs_0_), channel_id=1, source_target_pairs={{0,2},{1,3},{2,0},{3,1},{4,6},{5,7},{6,4},{7,5},{8,10},{9,11},{10,... | collective-permute-start | bytes 1548296 | tf_op jit(solution)/shard_map/ppermute | solution.py:21
  4.5 12.8 %collective-permute-start.1 = (bf16[64,1792]{1,0:T(8,128)(2,1)S(1)}, bf16[64,1792]{1,0:T(8,128)(2,1)S(1)}, u32[]{:S(2)}, u32[]{:S(2)}) collective-permute-start(bf16[64,1792]{1,0:T(8,128)(2,1)S(1)} %get-tuple-element.51), channel_id=1, source_target_pairs={{0,12},{4,8},{8,4},{12,0},{1,13},{5,9},{9,5},{13,1},{2,14},{6,10},... | collective-permute-start | bytes 688136 | tf_op jit(solution)/shard_map/ppermute | solution.py:21
  8.2 19.2 %collective-permute-start.2 = (bf16[64,1792]{1,0:T(8,128)(2,1)S(1)}, bf16[64,1792]{1,0:T(8,128)(2,1)S(1)}, u32[]{:S(2)}, u32[]{:S(2)}) collective-permute-start(bf16[64,1792]{1,0:T(8,128)(2,1)S(1)} %get-tuple-element.52), channel_id=1, source_target_pairs={{0,8},{4,12},{8,0},{12,4},{1,9},{5,13},{9,1},{13,5},{2,10},{6,14},... | collective-permute-start | bytes 688136 | tf_op jit(solution)/shard_map/ppermute | solution.py:21
  8.2 19.2 %collective-permute-start.3 = (bf16[64,1792]{1,0:T(8,128)(2,1)S(1)}, bf16[64,1792]{1,0:T(8,128)(2,1)S(1)}, u32[]{:S(2)}, u32[]{:S(2)}) collective-permute-start(bf16[64,1792]{1,0:T(8,128)(2,1)S(1)} %get-tuple-element.53), channel_id=1, source_target_pairs={{0,4},{4,0},{8,12},{12,8},{1,5},{5,1},{9,13},{13,9},{2,6},{6,2},{1... | collective-permute-start | bytes 688136 | tf_op jit(solution)/shard_map/ppermute | solution.py:21
  16.7 24.3 %copy-start.5 = (f32[512]{0:T(512)S(1)}, f32[512]{0:T(512)}, u32[]{:S(2)}) copy-start(f32[512]{0:T(512)} %param.14) | copy-start | bytes 6148
  16.7 10.8 %collective-permute-start.4 = (bf16[2016,128]{1,0:T(8,128)(2,1)S(1)}, bf16[2016,128]{1,0:T(8,128)(2,1)S(1)}, u32[]{:S(2)}, u32[]{:S(2)}) collective-permute-start(bf16[2016,128]{1,0:T(8,128)(2,1)S(1)} %pack_weight.1.refs_0_), channel_id=1, source_target_pairs={{0,1},{1,0},{2,3},{3,2},{4,5},{5,4},{6,7},{7,6},{8,9},{9,8},{10,11... | collective-permute-start | bytes 1548296 | tf_op jit(solution)/shard_map/ppermute | solution.py:21
  16.8 10.7 %collective-permute-start.5 = (bf16[2016,128]{1,0:T(8,128)(2,1)S(1)}, bf16[2016,128]{1,0:T(8,128)(2,1)S(1)}, u32[]{:S(2)}, u32[]{:S(2)}) collective-permute-start(bf16[2016,128]{1,0:T(8,128)(2,1)S(1)} %collective-permute-done.refs_2_), channel_id=1, source_target_pairs={{0,1},{1,0},{2,3},{3,2},{4,5},{5,4},{6,7},{7,6},{8,9},{9,8},{10,11... | collective-permute-start | bytes 1548296 | tf_op jit(solution)/shard_map/ppermute | solution.py:21
  29.2 6.9 %collective-permute-start.6 = (bf16[288,128]{1,0:T(8,128)(2,1)S(1)}, bf16[288,128]{1,0:T(8,128)(2,1)S(1)}, u32[]{:S(2)}, u32[]{:S(2)}) collective-permute-start(bf16[288,128]{1,0:T(8,128)(2,1)S(1)} %get-tuple-element.57), channel_id=1, source_target_pairs={{0,12},{4,8},{8,4},{12,0},{1,13},{5,9},{9,5},{13,1},{2,14},{6,10},... | collective-permute-start | bytes 221192 | tf_op jit(solution)/shard_map/ppermute | solution.py:21
  31.8 9.2 %collective-permute-start.7 = (bf16[288,128]{1,0:T(8,128)(2,1)S(1)}, bf16[288,128]{1,0:T(8,128)(2,1)S(1)}, u32[]{:S(2)}, u32[]{:S(2)}) collective-permute-start(bf16[288,128]{1,0:T(8,128)(2,1)S(1)} %get-tuple-element.58), channel_id=1, source_target_pairs={{0,8},{4,12},{8,0},{12,4},{1,9},{5,13},{9,1},{13,5},{2,10},{6,14},... | collective-permute-start | bytes 221192 | tf_op jit(solution)/shard_map/ppermute | solution.py:21
  31.8 9.2 %collective-permute-start.8 = (bf16[288,128]{1,0:T(8,128)(2,1)S(1)}, bf16[288,128]{1,0:T(8,128)(2,1)S(1)}, u32[]{:S(2)}, u32[]{:S(2)}) collective-permute-start(bf16[288,128]{1,0:T(8,128)(2,1)S(1)} %get-tuple-element.59), channel_id=1, source_target_pairs={{0,4},{4,0},{8,12},{12,8},{1,5},{5,1},{9,13},{13,9},{2,6},{6,2},{1... | collective-permute-start | bytes 221192 | tf_op jit(solution)/shard_map/ppermute | solution.py:21
  33.7 8.2 %collective-permute-start.12 = (bf16[288,128]{1,0:T(8,128)(2,1)S(1)}, bf16[288,128]{1,0:T(8,128)(2,1)S(1)}, u32[]{:S(2)}, u32[]{:S(2)}) collective-permute-start(bf16[288,128]{1,0:T(8,128)(2,1)S(1)} %get-tuple-element.61), channel_id=1, source_target_pairs={{0,12},{4,8},{8,4},{12,0},{1,13},{5,9},{9,5},{13,1},{2,14},{6,10},... | collective-permute-start | bytes 221192 | tf_op jit(solution)/shard_map/ppermute | solution.py:21
  36.1 7.7 %collective-permute-start.13 = (bf16[288,128]{1,0:T(8,128)(2,1)S(1)}, bf16[288,128]{1,0:T(8,128)(2,1)S(1)}, u32[]{:S(2)}, u32[]{:S(2)}) collective-permute-start(bf16[288,128]{1,0:T(8,128)(2,1)S(1)} %get-tuple-element.62), channel_id=1, source_target_pairs={{0,8},{4,12},{8,0},{12,4},{1,9},{5,13},{9,1},{13,5},{2,10},{6,14},... | collective-permute-start | bytes 221192 | tf_op jit(solution)/shard_map/ppermute | solution.py:21
  36.1 7.7 %collective-permute-start.14 = (bf16[288,128]{1,0:T(8,128)(2,1)S(1)}, bf16[288,128]{1,0:T(8,128)(2,1)S(1)}, u32[]{:S(2)}, u32[]{:S(2)}) collective-permute-start(bf16[288,128]{1,0:T(8,128)(2,1)S(1)} %get-tuple-element.63), channel_id=1, source_target_pairs={{0,4},{4,0},{8,12},{12,8},{1,5},{5,1},{9,13},{13,9},{2,6},{6,2},{1... | collective-permute-start | bytes 221192 | tf_op jit(solution)/shard_map/ppermute | solution.py:21
  41.2 4.0 %collective-permute-start.11 = (bf16[288,128]{1,0:T(8,128)(2,1)S(1)}, bf16[288,128]{1,0:T(8,128)(2,1)S(1)}, u32[]{:S(2)}, u32[]{:S(2)}) collective-permute-start(bf16[288,128]{1,0:T(8,128)(2,1)S(1)} %finish_rows.2.refs_0_), channel_id=1, source_target_pairs={{0,3},{1,2},{2,1},{3,0},{4,7},{5,6},{6,5},{7,4},{8,11},{9,10},{10,... | collective-permute-start | bytes 221192 | tf_op jit(solution)/shard_map/ppermute | solution.py:21
  41.3 5.2 %collective-permute-start.10 = (bf16[288,128]{1,0:T(8,128)(2,1)S(1)}, bf16[288,128]{1,0:T(8,128)(2,1)S(1)}, u32[]{:S(2)}, u32[]{:S(2)}) collective-permute-start(bf16[288,128]{1,0:T(8,128)(2,1)S(1)} %finish_rows.2.refs_0_), channel_id=1, source_target_pairs={{0,2},{1,3},{2,0},{3,1},{4,6},{5,7},{6,4},{7,5},{8,10},{9,11},{10,... | collective-permute-start | bytes 221192 | tf_op jit(solution)/shard_map/ppermute | solution.py:21
  41.9 4.6 %collective-permute-start.9 = (bf16[288,128]{1,0:T(8,128)(2,1)S(1)}, bf16[288,128]{1,0:T(8,128)(2,1)S(1)}, u32[]{:S(2)}, u32[]{:S(2)}) collective-permute-start(bf16[288,128]{1,0:T(8,128)(2,1)S(1)} %finish_rows.2.refs_0_), channel_id=1, source_target_pairs={{0,1},{1,0},{2,3},{3,2},{4,5},{5,4},{6,7},{7,6},{8,9},{9,8},{10,11... | collective-permute-start | bytes 221192 | tf_op jit(solution)/shard_map/ppermute | solution.py:21
  44.1 4.5 %collective-permute-start.17 = (bf16[288,128]{1,0:T(8,128)(2,1)S(1)}, bf16[288,128]{1,0:T(8,128)(2,1)S(1)}, u32[]{:S(2)}, u32[]{:S(2)}) collective-permute-start(bf16[288,128]{1,0:T(8,128)(2,1)S(1)} %finish_rows.3.refs_4_), channel_id=1, source_target_pairs={{0,3},{1,2},{2,1},{3,0},{4,7},{5,6},{6,5},{7,4},{8,11},{9,10},{10,... | collective-permute-start | bytes 221192 | tf_op jit(solution)/shard_map/ppermute | solution.py:21
  44.1 5.3 %collective-permute-start.16 = (bf16[288,128]{1,0:T(8,128)(2,1)S(1)}, bf16[288,128]{1,0:T(8,128)(2,1)S(1)}, u32[]{:S(2)}, u32[]{:S(2)}) collective-permute-start(bf16[288,128]{1,0:T(8,128)(2,1)S(1)} %finish_rows.3.refs_4_), channel_id=1, source_target_pairs={{0,2},{1,3},{2,0},{3,1},{4,6},{5,7},{6,4},{7,5},{8,10},{9,11},{10,... | collective-permute-start | bytes 221192 | tf_op jit(solution)/shard_map/ppermute | solution.py:21
  45.2 4.2 %collective-permute-start.15 = (bf16[288,128]{1,0:T(8,128)(2,1)S(1)}, bf16[288,128]{1,0:T(8,128)(2,1)S(1)}, u32[]{:S(2)}, u32[]{:S(2)}) collective-permute-start(bf16[288,128]{1,0:T(8,128)(2,1)S(1)} %finish_rows.3.refs_4_), channel_id=1, source_target_pairs={{0,1},{1,0},{2,3},{3,2},{4,5},{5,4},{6,7},{7,6},{8,9},{9,8},{10,11... | collective-permute-start | bytes 221192 | tf_op jit(solution)/shard_map/ppermute | solution.py:21
  51.2 7.6 %collective-permute-start.23 = (bf16[16,3072]{1,0:T(8,128)(2,1)S(1)}, bf16[16,3072]{1,0:T(8,128)(2,1)S(1)}, u32[]{:S(2)}, u32[]{:S(2)}) collective-permute-start(bf16[16,3072]{1,0:T(8,128)(2,1)S(1)} %attend.3.refs_0_), channel_id=1, source_target_pairs={{0,12},{4,8},{8,4},{12,0},{1,13},{5,9},{9,5},{13,1},{2,14},{6,10},... | collective-permute-start | bytes 294920 | tf_op jit(solution)/shard_map/ppermute | solution.py:21
  53.1 9.9 %collective-permute-start.22 = (bf16[16,3072]{1,0:T(8,128)(2,1)S(1)}, bf16[16,3072]{1,0:T(8,128)(2,1)S(1)}, u32[]{:S(2)}, u32[]{:S(2)}) collective-permute-start(bf16[16,3072]{1,0:T(8,128)(2,1)S(1)} %attend.3.refs_0_), channel_id=1, source_target_pairs={{0,8},{4,12},{8,0},{12,4},{1,9},{5,13},{9,1},{13,5},{2,10},{6,14},... | collective-permute-start | bytes 294920 | tf_op jit(solution)/shard_map/ppermute | solution.py:21
  53.4 9.7 %collective-permute-start.21 = (bf16[16,3072]{1,0:T(8,128)(2,1)S(1)}, bf16[16,3072]{1,0:T(8,128)(2,1)S(1)}, u32[]{:S(2)}, u32[]{:S(2)}) collective-permute-start(bf16[16,3072]{1,0:T(8,128)(2,1)S(1)} %attend.3.refs_0_), channel_id=1, source_target_pairs={{0,4},{4,0},{8,12},{12,8},{1,5},{5,1},{9,13},{13,9},{2,6},{6,2},{1... | collective-permute-start | bytes 294920 | tf_op jit(solution)/shard_map/ppermute | solution.py:21
  56.7 8.4 %collective-permute-start.20 = (bf16[16,1024]{1,0:T(8,128)(2,1)S(1)}, bf16[16,1024]{1,0:T(8,128)(2,1)S(1)}, u32[]{:S(2)}, u32[]{:S(2)}) collective-permute-start(bf16[16,1024]{1,0:T(8,128)(2,1)S(1)} %attend.2.refs_0_), channel_id=1, source_target_pairs={{0,12},{4,8},{8,4},{12,0},{1,13},{5,9},{9,5},{13,1},{2,14},{6,10},... | collective-permute-start | bytes 98312 | tf_op jit(solution)/shard_map/ppermute | solution.py:21
  58.6 6.5 %collective-permute-start.19 = (bf16[16,1024]{1,0:T(8,128)(2,1)S(1)}, bf16[16,1024]{1,0:T(8,128)(2,1)S(1)}, u32[]{:S(2)}, u32[]{:S(2)}) collective-permute-start(bf16[16,1024]{1,0:T(8,128)(2,1)S(1)} %attend.2.refs_0_), channel_id=1, source_target_pairs={{0,8},{4,12},{8,0},{12,4},{1,9},{5,13},{9,1},{13,5},{2,10},{6,14},... | collective-permute-start | bytes 98312 | tf_op jit(solution)/shard_map/ppermute | solution.py:21
  58.8 6.3 %collective-permute-start.18 = (bf16[16,1024]{1,0:T(8,128)(2,1)S(1)}, bf16[16,1024]{1,0:T(8,128)(2,1)S(1)}, u32[]{:S(2)}, u32[]{:S(2)}) collective-permute-start(bf16[16,1024]{1,0:T(8,128)(2,1)S(1)} %attend.2.refs_0_), channel_id=1, source_target_pairs={{0,4},{4,0},{8,12},{12,8},{1,5},{5,1},{9,13},{13,9},{2,6},{6,2},{1... | collective-permute-start | bytes 98312 | tf_op jit(solution)/shard_map/ppermute | solution.py:21
  65.9 4.0 %collective-permute-start.24 = (bf16[16,1792]{1,0:T(8,128)(2,1)S(1)}, bf16[16,1792]{1,0:T(8,128)(2,1)S(1)}, u32[]{:S(2)}, u32[]{:S(2)}) collective-permute-start(bf16[16,1792]{1,0:T(8,128)(2,1)S(1)} %get-tuple-element.66), channel_id=1, source_target_pairs={{0,3},{1,2},{2,1},{3,0},{4,7},{5,6},{6,5},{7,4},{8,11},{9,10},{10,... | collective-permute-start | bytes 172040 | tf_op jit(solution)/shard_map/ppermute | solution.py:21
  67.0 4.4 %collective-permute-start.25 = (bf16[16,1792]{1,0:T(8,128)(2,1)S(1)}, bf16[16,1792]{1,0:T(8,128)(2,1)S(1)}, u32[]{:S(2)}, u32[]{:S(2)}) collective-permute-start(bf16[16,1792]{1,0:T(8,128)(2,1)S(1)} %get-tuple-element.67), channel_id=1, source_target_pairs={{0,2},{1,3},{2,0},{3,1},{4,6},{5,7},{6,4},{7,5},{8,10},{9,11},{10,... | collective-permute-start | bytes 172040 | tf_op jit(solution)/shard_map/ppermute | solution.py:21
  67.7 3.7 %collective-permute-start.26 = (bf16[16,1792]{1,0:T(8,128)(2,1)S(1)}, bf16[16,1792]{1,0:T(8,128)(2,1)S(1)}, u32[]{:S(2)}, u32[]{:S(2)}) collective-permute-start(bf16[16,1792]{1,0:T(8,128)(2,1)S(1)} %get-tuple-element.68), channel_id=1, source_target_pairs={{0,1},{1,0},{2,3},{3,2},{4,5},{5,4},{6,7},{7,6},{8,9},{9,8},{10,11... | collective-permute-start | bytes 172040 | tf_op jit(solution)/shard_map/ppermute | solution.py:21

commit v9 on v8

--- a/solution.py
+++ b/solution.py
@@ -343,7 +343,7 @@
         ],
         compiler_params=pltpu.CompilerParams(vmem_limit_bytes=prepare_mib * mib),
         cost_estimate=pl.CostEstimate(
-            flops=4 * 10**9, bytes_accessed=28 * 10**6, transcendentals=10**5
+            flops=4 * 10**10, bytes_accessed=28 * 10**6, transcendentals=10**5
         ),
         name="prepare",
     )(inverse, lengths, request_slot, requests, queries.reshape(rows, width), absorb, cache, fresh,
@@ -453,32 +453,32 @@
     )(gain, cosine, sine, *parts)
 
 
-def attend_kernel(
-    scale, cap_slots, steps, first_head, heads, query_ref, slot_ref, top_ref,
-    sum_ref, mix_ref, live_ref, value_ref, *refs
-):
-    pieces, out_ref, keys = refs[:-2], refs[-2], refs[-1]
-    lat_width = mix_ref.shape[0] * mix_ref.shape[2]
-    per_head = cap_slots * steps
-    rows = heads * per_head
-    mine = slice(first_head * per_head, first_head * per_head + rows)
-    sides = len(pieces) // 2
-    piece_rows = keys.shape[0] // len(pieces)
+def take_keys(keys, pieces, lat_width):
+    rows = keys.shape[0] // len(pieces)
     for n, piece in enumerate(pieces):
-        tiles, rest = load_packed(piece, piece_rows)
-        place = (n % sides) * 2 + n // sides
-        there = slice(place * piece_rows, (place + 1) * piece_rows)
+        tiles, rest = load_packed(piece, rows)
+        there = slice(n * rows, (n + 1) * rows)
         for j, tile in enumerate(tiles):
             keys[there, j * 128 : (j + 1) * 128] = tile
         keys[there, lat_width:] = rest
-    contract = (((1,), (1,)), ((), ()))
-    row = lax.broadcasted_iota(jnp.int32, (rows, 1), 0)
+
+
+def merge(layout, which, mine, query_ref, slot_ref, top_ref, sum_ref, mix_ref, keys):
+    scale, cap_slots, steps, half_rows = layout
+    lat_width = mix_ref.shape[0] * mix_ref.shape[2]
+    row = lax.broadcasted_iota(jnp.int32, (mine.stop - mine.start, 1), 0)
     row_slot = (row // steps) % cap_slots
     query = query_ref[mine, :]
-    score = lax.dot_general(query, keys[...], contract, preferred_element_type=f32)
-    score = jnp.where(
-        slot_ref[...] == row_slot + 1, score * scale, masked_score
-    )
+    score = lax.dot_general(
+        query, keys[...], (((1,), (1,)), ((), ())), preferred_element_type=f32
+    )
+    count = slot_ref.shape[1]
+    part = half_rows
+    slots = jnp.concatenate(
+        [slot_ref[:, n + which * part : n + (which + 1) * part] for n in range(0, count, 2 * part)],
+        axis=1,
+    )
+    score = jnp.where(slots == row_slot + 1, score * scale, masked_score)
     top_held = top_ref[mine, :1]
     top = jnp.maximum(top_held, jnp.max(score, axis=1, keepdims=True))
     held = jnp.exp(top_held - top)
@@ -486,7 +486,50 @@
     total = sum_ref[mine, :1] * held + jnp.sum(weight, axis=1, keepdims=True)
     mix = jnp.dot(weight.astype(bf16), keys[:, :lat_width], preferred_element_type=f32)
     mix_held = jnp.concatenate([mix_ref[n, mine, :] for n in range(mix_ref.shape[0])], axis=1)
-    latent = ((mix_held * held + mix) / total).astype(bf16)
+    return top, total, mix_held * held + mix
+
+
+def absorb_kernel(layout, which, query_ref, slot_ref, top_ref, sum_ref, mix_ref, *refs):
+    pieces, (new_top, new_sum, new_mix, keys) = refs[:-4], refs[-4:]
+    take_keys(keys, pieces, mix_ref.shape[0] * mix_ref.shape[2])
+    rows, lanes = top_ref.shape
+    step = rows // 2
+    for first in range(0, rows, step):
+        mine = slice(first, first + step)
+        top, total, mix = merge(
+            layout, which, mine, query_ref, slot_ref, top_ref, sum_ref, mix_ref, keys
+        )
+        new_top[mine, :] = jnp.broadcast_to(top, (step, lanes))
+        new_sum[mine, :] = jnp.broadcast_to(total, (step, lanes))
+        for n, part in enumerate(lane_tiles(mix.shape[1])):
+            new_mix[n, mine, :] = mix[:, part]
+
+
+def absorb(layout, which, query, row_slot, top, total, mix, pieces):
+    return pl.pallas_call(
+        functools.partial(absorb_kernel, layout, which),
+        out_shape=[jax.ShapeDtypeStruct(x.shape, f32) for x in (top, total, mix)],
+        in_specs=[in_vmem] * (5 + len(pieces)),
+        out_specs=[in_vmem] * 3,
+        scratch_shapes=[pltpu.VMEM((row_slot.shape[1] // 2, query.shape[1]), bf16)],
+        compiler_params=pltpu.CompilerParams(vmem_limit_bytes=10 * mib),
+        cost_estimate=pl.CostEstimate(flops=2 * 10**9, bytes_accessed=10**6, transcendentals=0),
+        name="absorb",
+    )(query, row_slot, top, total, mix, *pieces)
+
+
+def attend_kernel(
+    layout, which, first_head, heads, query_ref, slot_ref, top_ref, sum_ref, mix_ref, live_ref,
+    value_ref, *refs
+):
+    pieces, out_ref, keys = refs[:-2], refs[-2], refs[-1]
+    per_head = layout[1] * layout[2]
+    take_keys(keys, pieces, mix_ref.shape[0] * mix_ref.shape[2])
+    mine = slice(first_head * per_head, (first_head + heads) * per_head)
+    _, total, mix = merge(
+        layout, which, mine, query_ref, slot_ref, top_ref, sum_ref, mix_ref, keys
+    )
+    latent = (mix / total).astype(bf16)
     live = live_ref[:, :1]
     width = value_ref.shape[2]
     for h in range(0, heads, 2):
@@ -499,15 +542,13 @@
         out_ref[:, (h + 1) * width : (h + 2) * width] = (both[per_head:, width:] * live).astype(bf16)
 
 
-def attend(scale, query, row_slot, top, total, mix, live, value, pieces, cap_slots, steps,
-           first_head, heads):
-    width = value.shape[2]
-    return pl.pallas_call(
-        functools.partial(attend_kernel, scale, cap_slots, steps, first_head, heads),
-        out_shape=jax.ShapeDtypeStruct((cap_slots * steps, heads * width), bf16),
+def attend(layout, which, query, row_slot, top, total, mix, live, value, pieces, first_head, heads):
+    return pl.pallas_call(
+        functools.partial(attend_kernel, layout, which, first_head, heads),
+        out_shape=jax.ShapeDtypeStruct((live.shape[0], heads * value.shape[2]), bf16),
         in_specs=[in_vmem] * (7 + len(pieces)),
         out_specs=in_vmem,
-        scratch_shapes=[pltpu.VMEM((row_slot.shape[1], query.shape[1]), bf16)],
+        scratch_shapes=[pltpu.VMEM((row_slot.shape[1] // 2, query.shape[1]), bf16)],
         compiler_params=pltpu.CompilerParams(vmem_limit_bytes=10 * mib),
         name="attend",
     )(query, row_slot, top, total, mix, live, value, *pieces)
@@ -596,7 +637,8 @@
 
     x_pieces = list(split_columns(prompts, dev_count))
     packs = shard_rows % 32 == 0
-    weights = [pack_weight(latent_weight) if packs else latent_weight] + [None] * (side_count - 1)
+    x_pieces[0], own_weight = lax.optimization_barrier((x_pieces[0], latent_weight))
+    weights = [pack_weight(own_weight) if packs else own_weight] + [None] * (side_count - 1)
     for k in range(2, side_count, 2):
         weights[k] = swap(weights[0], "side", k)
     for k in sorted(range(1, dev_count), reverse=True):
@@ -626,18 +668,21 @@
         weights = [held.reshape(slab, kv_width)]
 
     routed = project(stack_rows(x_pieces), weights, target, kv_width, dev_count)
-    pieces = []
+    layout = (score_scale, cap_slots, step_count, group_rows // 2)
+    state = top_held, sum_held, mix_held
     for which in range(2):
         half = list(routed[which * dev_count : (which + 1) * dev_count])
         for k in sorted(range(1, dev_count), reverse=True):
             half[k] = swap(half[k], "dev", k)
         latent_rows = finish(half[:1] + half[:0:-1], latent_gain.reshape(1, -1), cosine, sine, which)
-        pieces += [latent_rows] + [swap(latent_rows, "side", k) for k in range(1, side_count)]
+        pieces = [latent_rows] + [swap(latent_rows, "side", k) for k in range(1, side_count)]
+        if which == 0:
+            state = absorb(layout, which, query_full, row_slot, *state, pieces)
     product, first_head, head_count = None, 0, value_absorb.shape[0]
     for part_heads in (head_count * 3 // 4, head_count // 4):
         head_out = attend(
-            score_scale, query_full, row_slot, top_held, sum_held, mix_held, live, value_here,
-            pieces, cap_slots, step_count, first_head, part_heads,
+            layout, 1, query_full, row_slot, *state, live, value_here, pieces, first_head,
+            part_heads,
         )
         heads = [head_out] + [None] * (dev_count - 1)
         for k in sorted(range(1, dev_count), reverse=True):

time: 72.2 us -> 71.4 us (0.989)
  waiting for transfers between devices: 23 us -> 18.4 us
  local copies, waits for them, and re-layouts: 1.2 us -> 3.49 us
  Pallas kernels: 15.7 us -> 17.1 us
    ppermute x27, waiting for transfers between devices: 23 us -> 18.4 us  [swap(): return lax.ppermute(value, axis, [(i, i ^ step) for i in range(count)])]
    unnamed x22, local copies, waits for them, and re-layouts: 1.2 us -> 3.49 us
    pallas_call x2 -> x3, Pallas kernels: 2.77 us -> 4.15 us  [the longest x2 2.71 us: attend(): pl.pallas_call(functools.partial(attend_kernel, layout, which, first_head...]
  transfers between devices with their start and end apart: 27 -> 27, of which waited for: 11 -> 9; matrix products, arithmetic and copies ran while one was open for 0% -> 0% of each run, Pallas kernels for 16% -> 18%
where the time goes in v9:
time: 71.4 us; the launch traced here: 71.3 us
  starting transfers between devices  31.4 us (44%)
  waiting for transfers between devices  18.4 us (26%)
  Pallas kernels  17.1 us (24%)
  local copies, waits for them, and re-layouts  3.49 us (5%)
    ppermute x27, starting transfers between devices, swap(): return lax.ppermute(value, axis, [(i, i ^ step) for i in range(count)])  31.4 us
    ppermute x27, waiting for transfers between devices, swap(): return lax.ppermute(value, axis, [(i, i ^ step) for i in range(count)])  18.4 us
    pallas_call x1, Pallas kernels, prepare(): pl.pallas_call(functools.partial(prepare_kernel, scale, steps, (dev_count...  7.61 us
    unnamed x22, local copies, waits for them, and re-layouts  3.49 us
    pallas_call x2, Pallas kernels, output_product(): pl.pallas_call(functools.partial(output_kernel, dev_count, side_count, st...  2.84 us
    pallas_call x2, Pallas kernels, attend(): pl.pallas_call(functools.partial(attend_kernel, layout, which, first_head...  2.71 us
    pallas_call x1, Pallas kernels, project(): pl.pallas_call(functools.partial(project_kernel, dev_count, len(weights))...  1.7 us
    pallas_call x1, Pallas kernels, absorb(): pl.pallas_call(functools.partial(absorb_kernel, layout, which), out_shape...  1.44 us
  transfers between devices with their start and end apart: 27, of which 9 were waited for; matrix products, arithmetic and copies ran while one was open for 0% of the time, Pallas kernels for 18%

profile of v9, /device:TPU:0, one launch (start us, length us, event | category | flops | bytes accessed | tf_op | source)
XLA Modules:
  0.0 71.3 jit_solution(9471132340561788972)
XLA Ops:
  0.0 1.2 %copy-done.4 = bf16[64,7168]{1,0:T(8,128)(2,1)S(1)} copy-done((bf16[64,7168]{1,0:T(8,128)(2,1)S(1)}, bf16[64,7168]{1,0:T(8,128)(2,1)}, u32[]{:S(2)}) %copy-start.4) | copy-done | bytes 917528
  1.2 0.2 split_columns.1
  1.4 5.1 %collective-permute-start.1 = (bf16[64,1792]{1,0:T(8,128)(2,1)S(1)}, bf16[64,1792]{1,0:T(8,128)(2,1)S(1)}, u32[]{:S(2)}, u32[]{:S(2)}) collective-permute-start(bf16[64,1792]{1,0:T(8,128)(2,1)S(1)} %get-tuple-element.56), channel_id=1, source_target_pairs={{0,12},{4,8},{8,4},{12,0},{1,13},{5,9},{9,5},{13,1},{2,14},{6,10},... | collective-permute-start | bytes 688136 | tf_op jit(solution)/shard_map/ppermute | solution.py:21
  6.5 0.6 collective-permute-start.3
  7.2 0.1 pack_weight.1.refs_0_
  7.3 1.7 %collective-permute-start = (bf16[2016,128]{1,0:T(8,128)(2,1)S(1)}, bf16[2016,128]{1,0:T(8,128)(2,1)S(1)}, u32[]{:S(2)}, u32[]{:S(2)}) collective-permute-start(bf16[2016,128]{1,0:T(8,128)(2,1)S(1)} %pack_weight.1.refs_0_), channel_id=1, source_target_pairs={{0,2},{1,3},{2,0},{3,1},{4,6},{5,7},{6,4},{7,5},{8,10},{9,11},{10,... | collective-permute-start | bytes 1548296 | tf_op jit(solution)/shard_map/ppermute | solution.py:21
  9.0 0.3 copy-done.1
  9.3 1.3 %copy-done.2 = bf16[32,512,128]{2,1,0:T(8,128)(2,1)S(1)} copy-done((bf16[32,512,128]{2,1,0:T(8,128)(2,1)S(1)}, bf16[32,512,128]{2,1,0:T(8,128)(2,1)}, u32[]{:S(2)}) %copy-start.2) | copy-done | bytes 4194328
  10.6 0.7 copy-done.3
  11.3 7.6 %prepare.1 = (bf16[512,576]{1,0:T(8,128)(2,1)S(1)}, f32[512,128]{1,0:T(8,128)S(1)}, f32[512,128]{1,0:T(8,128)S(1)}, f32[4,512,128]{2,1,0:T(8,128)S(1)}, f32[16,1...) custom-call(f32[1,32]{1,0:T(1,128)S(1)} %negate_power_fusion.inverse, ...), custom_call_target="tpu_custom_call" | custom-call | flops 40000000000 | bytes 28000000 | tf_op jit(solution)/shard_map/prepare/pallas_call | solution.py:323
  18.9 1.4 %collective-permute-done.refs_2_ = bf16[2016,128]{1,0:T(8,128)(2,1)S(1)} collective-permute-done((bf16[2016,128]{1,0:T(8,128)(2,1)S(1)}, bf16[2016,128]{1,0:T(8,128)(2,1)S(1)}, u32[]{:S(2)}, u32[]{:S(2)}) %collective-permute-start) | collective-permute-done | bytes 516128 | tf_op jit(solution)/shard_map/ppermute | solution.py:21
  20.3 0.5 collective-permute-start.5
  20.8 5.2 %collective-permute-done.2.refs_2_ = bf16[64,1792]{1,0:T(8,128)(2,1)S(1)} collective-permute-done((bf16[64,1792]{1,0:T(8,128)(2,1)S(1)}, bf16[64,1792]{1,0:T(8,128)(2,1)S(1)}, u32[]{:S(2)}, u32[]{:S(2)}) %collective-permute-start.2) | collective-permute-done | bytes 229408 | tf_op jit(solution)/shard_map/ppermute | solution.py:21
  26.0 0.1 stack_rows.1.x_ref
  26.1 1.7 %project.1 = (f32[288,128]{1,0:T(8,128)S(1)}, bf16[288,128]{1,0:T(8,128)(2,1)S(1)}, bf16[288,128]{1,0:T(8,128)(2,1)S(1)}, bf16[288,128]{1,0:T(8,128)(2,1)S(1)}, ...) custom-call(s32[1,256]{1,0:T(1,128)S(1)} %get-tuple-element.54.targe, ...), custom_call_target="tpu_custom_call" | custom-call | tf_op jit(solution)/shard_map/project/pallas_call | solution.py:405
  27.8 2.5 %collective-permute-start.6 = (bf16[288,128]{1,0:T(8,128)(2,1)S(1)}, bf16[288,128]{1,0:T(8,128)(2,1)S(1)}, u32[]{:S(2)}, u32[]{:S(2)}) collective-permute-start(bf16[288,128]{1,0:T(8,128)(2,1)S(1)} %get-tuple-element.62), channel_id=1, source_target_pairs={{0,12},{4,8},{8,4},{12,0},{1,13},{5,9},{9,5},{13,1},{2,14},{6,10},... | collective-permute-start | bytes 221192 | tf_op jit(solution)/shard_map/ppermute | solution.py:21
  30.3 1.9 %collective-permute-start.8 = (bf16[288,128]{1,0:T(8,128)(2,1)S(1)}, bf16[288,128]{1,0:T(8,128)(2,1)S(1)}, u32[]{:S(2)}, u32[]{:S(2)}) collective-permute-start(bf16[288,128]{1,0:T(8,128)(2,1)S(1)} %get-tuple-element.64), channel_id=1, source_target_pairs={{0,4},{4,0},{8,12},{12,8},{1,5},{5,1},{9,13},{13,9},{2,6},{6,2},{1... | collective-permute-start | bytes 221192 | tf_op jit(solution)/shard_map/ppermute | solution.py:21
  32.2 2.5 %collective-permute-start.12 = (bf16[288,128]{1,0:T(8,128)(2,1)S(1)}, bf16[288,128]{1,0:T(8,128)(2,1)S(1)}, u32[]{:S(2)}, u32[]{:S(2)}) collective-permute-start(bf16[288,128]{1,0:T(8,128)(2,1)S(1)} %get-tuple-element.71), channel_id=1, source_target_pairs={{0,12},{4,8},{8,4},{12,0},{1,13},{5,9},{9,5},{13,1},{2,14},{6,10},... | collective-permute-start | bytes 221192 | tf_op jit(solution)/shard_map/ppermute | solution.py:21
  34.7 1.9 %collective-permute-start.14 = (bf16[288,128]{1,0:T(8,128)(2,1)S(1)}, bf16[288,128]{1,0:T(8,128)(2,1)S(1)}, u32[]{:S(2)}, u32[]{:S(2)}) collective-permute-start(bf16[288,128]{1,0:T(8,128)(2,1)S(1)} %get-tuple-element.73), channel_id=1, source_target_pairs={{0,4},{4,0},{8,12},{12,8},{1,5},{5,1},{9,13},{13,9},{2,6},{6,2},{1... | collective-permute-start | bytes 221192 | tf_op jit(solution)/shard_map/ppermute | solution.py:21
  36.6 2.7 %collective-permute-done.7.refs_2_ = bf16[288,128]{1,0:T(8,128)(2,1)S(1)} collective-permute-done((bf16[288,128]{1,0:T(8,128)(2,1)S(1)}, bf16[288,128]{1,0:T(8,128)(2,1)S(1)}, u32[]{:S(2)}, u32[]{:S(2)}) %collective-permute-start.7) | collective-permute-done | bytes 73760 | tf_op jit(solution)/shard_map/ppermute | solution.py:21
  39.4 0.2 finish_rows.2.refs_0_
  39.6 0.1 collective-permute-start.11
  39.6 1.6 %collective-permute-start.10 = (bf16[288,128]{1,0:T(8,128)(2,1)S(1)}, bf16[288,128]{1,0:T(8,128)(2,1)S(1)}, u32[]{:S(2)}, u32[]{:S(2)}) collective-permute-start(bf16[288,128]{1,0:T(8,128)(2,1)S(1)} %finish_rows.2.refs_0_), channel_id=1, source_target_pairs={{0,2},{1,3},{2,0},{3,1},{4,6},{5,7},{6,4},{7,5},{8,10},{9,11},{10,... | collective-permute-start | bytes 221192 | tf_op jit(solution)/shard_map/ppermute | solution.py:21
  41.2 0.3 collective-permute-start.9
  41.5 0.9 %collective-permute-done.13.refs_2_ = bf16[288,128]{1,0:T(8,128)(2,1)S(1)} collective-permute-done((bf16[288,128]{1,0:T(8,128)(2,1)S(1)}, bf16[288,128]{1,0:T(8,128)(2,1)S(1)}, u32[]{:S(2)}, u32[]{:S(2)}) %collective-permute-start.13) | collective-permute-done | bytes 73760 | tf_op jit(solution)/shard_map/ppermute | solution.py:21
  42.5 0.2 finish_rows.3.refs_0_
  42.7 0.2 collective-permute-start.17
  42.9 1.4 %collective-permute-start.16 = (bf16[288,128]{1,0:T(8,128)(2,1)S(1)}, bf16[288,128]{1,0:T(8,128)(2,1)S(1)}, u32[]{:S(2)}, u32[]{:S(2)}) collective-permute-start(bf16[288,128]{1,0:T(8,128)(2,1)S(1)} %finish_rows.3.refs_0_), channel_id=1, source_target_pairs={{0,2},{1,3},{2,0},{3,1},{4,6},{5,7},{6,4},{7,5},{8,10},{9,11},{10,... | collective-permute-start | bytes 221192 | tf_op jit(solution)/shard_map/ppermute | solution.py:21
  44.3 0.3 collective-permute-start.15
  44.6 1.2 %collective-permute-done.10.refs_2_ = bf16[288,128]{1,0:T(8,128)(2,1)S(1)} collective-permute-done((bf16[288,128]{1,0:T(8,128)(2,1)S(1)}, bf16[288,128]{1,0:T(8,128)(2,1)S(1)}, u32[]{:S(2)}, u32[]{:S(2)}) %collective-permute-start.10) | collective-permute-done | bytes 73760 | tf_op jit(solution)/shard_map/ppermute | solution.py:21
  45.8 1.4 %absorb.1 = (f32[512,128]{1,0:T(8,128)S(1)}, f32[512,128]{1,0:T(8,128)S(1)}, f32[4,512,128]{2,1,0:T(8,128)S(1)}) custom-call(bf16[512,576]{1,0:T(8,128)(2,1)S(1)} %get-tuple-element.45.query_ref, s32[1,512]{1,0:T(1,128)S(1)} %get-tuple-element.46.slot_ref, f32[512,128]{1,0:T(8,128)S(1)} %get-tuple-element.49.top_ref, ...), custom_call_target="tpu_custom_call" | custom-call | flops 2000000000 | bytes 1000000 | tf_op jit(solution)/shard_map/absorb/pallas_call | solution.py:509
  47.3 0.0 collective-permute-done.17.refs_3_
  47.3 1.6 %collective-permute-done.16.refs_2_ = bf16[288,128]{1,0:T(8,128)(2,1)S(1)} collective-permute-done((bf16[288,128]{1,0:T(8,128)(2,1)S(1)}, bf16[288,128]{1,0:T(8,128)(2,1)S(1)}, u32[]{:S(2)}, u32[]{:S(2)}) %collective-permute-start.16) | collective-permute-done | bytes 73760 | tf_op jit(solution)/shard_map/ppermute | solution.py:21
  48.9 1.7 %attend.3.refs_0_ = bf16[16,3072]{1,0:T(8,128)(2,1)S(1)} custom-call(bf16[512,576]{1,0:T(8,128)(2,1)S(1)} %get-tuple-element.45.query_ref, s32[1,512]{1,0:T(1,128)S(1)} %get-tuple-element.46.slot_ref, f32[512,128]{1,0:T(8,128)S(1)} %get-tuple-element.65.top_ref, f32[512,128]{1,0:T(8,128)S(1)} %get-tuple-element.66.sum_ref, ...), custom_call_target="tpu_custom_call" | custom-call | tf_op jit(solution)/shard_map/attend/pallas_call | solution.py:546
  50.7 2.3 %collective-permute-start.23 = (bf16[16,3072]{1,0:T(8,128)(2,1)S(1)}, bf16[16,3072]{1,0:T(8,128)(2,1)S(1)}, u32[]{:S(2)}, u32[]{:S(2)}) collective-permute-start(bf16[16,3072]{1,0:T(8,128)(2,1)S(1)} %attend.3.refs_0_), channel_id=1, source_target_pairs={{0,12},{4,8},{8,4},{12,0},{1,13},{5,9},{9,5},{13,1},{2,14},{6,10},... | collective-permute-start | bytes 294920 | tf_op jit(solution)/shard_map/ppermute | solution.py:21
  53.0 2.2 %collective-permute-start.21 = (bf16[16,3072]{1,0:T(8,128)(2,1)S(1)}, bf16[16,3072]{1,0:T(8,128)(2,1)S(1)}, u32[]{:S(2)}, u32[]{:S(2)}) collective-permute-start(bf16[16,3072]{1,0:T(8,128)(2,1)S(1)} %attend.3.refs_0_), channel_id=1, source_target_pairs={{0,4},{4,0},{8,12},{12,8},{1,5},{5,1},{9,13},{13,9},{2,6},{6,2},{1... | collective-permute-start | bytes 294920 | tf_op jit(solution)/shard_map/ppermute | solution.py:21
  55.1 1.0 %attend.2.refs_0_ = bf16[16,1024]{1,0:T(8,128)(2,1)S(1)} custom-call(bf16[512,576]{1,0:T(8,128)(2,1)S(1)} %get-tuple-element.45.query_ref, s32[1,512]{1,0:T(1,128)S(1)} %get-tuple-element.46.slot_ref, f32[512,128]{1,0:T(8,128)S(1)} %get-tuple-element.65.top_ref, f32[512,128]{1,0:T(8,128)S(1)} %get-tuple-element.66.sum_ref, ...), custom_call_target="tpu_custom_call" | custom-call | tf_op jit(solution)/shard_map/attend/pallas_call | solution.py:546
  56.1 2.3 %collective-permute-start.20 = (bf16[16,1024]{1,0:T(8,128)(2,1)S(1)}, bf16[16,1024]{1,0:T(8,128)(2,1)S(1)}, u32[]{:S(2)}, u32[]{:S(2)}) collective-permute-start(bf16[16,1024]{1,0:T(8,128)(2,1)S(1)} %attend.2.refs_0_), channel_id=1, source_target_pairs={{0,12},{4,8},{8,4},{12,0},{1,13},{5,9},{9,5},{13,1},{2,14},{6,10},... | collective-permute-start | bytes 98312 | tf_op jit(solution)/shard_map/ppermute | solution.py:21
  58.4 2.2 %collective-permute-start.18 = (bf16[16,1024]{1,0:T(8,128)(2,1)S(1)}, bf16[16,1024]{1,0:T(8,128)(2,1)S(1)}, u32[]{:S(2)}, u32[]{:S(2)}) collective-permute-start(bf16[16,1024]{1,0:T(8,128)(2,1)S(1)} %attend.2.refs_0_), channel_id=1, source_target_pairs={{0,4},{4,0},{8,12},{12,8},{1,5},{5,1},{9,13},{13,9},{2,6},{6,2},{1... | collective-permute-start | bytes 98312 | tf_op jit(solution)/shard_map/ppermute | solution.py:21
  60.6 1.8 %collective-permute-done.22.refs_2_ = bf16[16,3072]{1,0:T(8,128)(2,1)S(1)} collective-permute-done((bf16[16,3072]{1,0:T(8,128)(2,1)S(1)}, bf16[16,3072]{1,0:T(8,128)(2,1)S(1)}, u32[]{:S(2)}, u32[]{:S(2)}) %collective-permute-start.22) | collective-permute-done | bytes 98336 | tf_op jit(solution)/shard_map/ppermute | solution.py:21
  62.3 2.1 %output_product.2.refs_5_ = f32[64,1792]{1,0:T(8,128)S(1)} custom-call(bf16[16,3072]{1,0:T(8,128)(2,1)S(1)} %attend.3.refs_0_, bf16[16,3072]{1,0:T(8,128)(2,1)S(1)} %collective-permute-done.21.refs_1_, bf16[16,3072]{1,0:T(8,128)(2,1)S(1)} %collective-permute-done.22.refs_2_, bf16[16,3072]{1,0:T(8,128)(2,1)S(1)} %collective-permute-done.23.refs_3_, ...), custom_call_target="tpu_custom_call" | custom-call | tf_op jit(solution)/shard_map/output_product/pallas_call | solution.py:600
  64.4 0.8 %output_product.3 = (f32[16,1792]{1,0:T(8,128)S(1)}, bf16[16,1792]{1,0:T(8,128)(2,1)S(1)}, bf16[16,1792]{1,0:T(8,128)(2,1)S(1)}, bf16[16,1792]{1,0:T(8,128)(2,1)S(1)}) custom-call(bf16[16,1024]{1,0:T(8,128)(2,1)S(1)} %attend.2.refs_0_, bf16[16,1024]{1,0:T(8,128)(2,1)S(1)} %collective-permute-done.18.refs_1_, ...), custom_call_target="tpu_custom_call" | custom-call | tf_op jit(solution)/shard_map/output_product/pallas_call | solution.py:600
  65.2 0.6 collective-permute-start.24
  65.9 1.1 %collective-permute-start.25 = (bf16[16,1792]{1,0:T(8,128)(2,1)S(1)}, bf16[16,1792]{1,0:T(8,128)(2,1)S(1)}, u32[]{:S(2)}, u32[]{:S(2)}) collective-permute-start(bf16[16,1792]{1,0:T(8,128)(2,1)S(1)} %get-tuple-element.77), channel_id=1, source_target_pairs={{0,2},{1,3},{2,0},{3,1},{4,6},{5,7},{6,4},{7,5},{8,10},{9,11},{10,... | collective-permute-start | bytes 172040 | tf_op jit(solution)/shard_map/ppermute | solution.py:21
  67.0 0.2 collective-permute-start.26
  67.1 2.2 %collective-permute-done.24 = bf16[16,1792]{1,0:T(8,128)(2,1)S(1)} collective-permute-done((bf16[16,1792]{1,0:T(8,128)(2,1)S(1)}, bf16[16,1792]{1,0:T(8,128)(2,1)S(1)}, u32[]{:S(2)}, u32[]{:S(2)}) %collective-permute-start.24) | collective-permute-done | bytes 57376 | tf_op jit(solution)/shard_map/ppermute | solution.py:21
  69.3 1.3 %collective-permute-done.25 = bf16[16,1792]{1,0:T(8,128)(2,1)S(1)} collective-permute-done((bf16[16,1792]{1,0:T(8,128)(2,1)S(1)}, bf16[16,1792]{1,0:T(8,128)(2,1)S(1)}, u32[]{:S(2)}, u32[]{:S(2)}) %collective-permute-start.25) | collective-permute-done | bytes 57376 | tf_op jit(solution)/shard_map/ppermute | solution.py:21
  70.6 0.7 add_convert_fusion
  (42 shorter events, 0.1 us)
Async XLA Ops:
  0.0 1.2 %copy-start.4 = (bf16[64,7168]{1,0:T(8,128)(2,1)S(1)}, bf16[64,7168]{1,0:T(8,128)(2,1)}, u32[]{:S(2)}) copy-start(bf16[64,7168]{1,0:T(8,128)(2,1)} %prompts_ref.1) | copy-start | bytes 2752516
  1.2 6.0 %copy-start.5 = (bf16[448,576]{1,0:T(8,128)(2,1)S(1)}, bf16[448,576]{1,0:T(8,128)(2,1)}, u32[]{:S(2)}) copy-start(bf16[448,576]{1,0:T(8,128)(2,1)} %value_ref) | copy-start | bytes 1548292
  1.4 19.4 %collective-permute-start.1 = (bf16[64,1792]{1,0:T(8,128)(2,1)S(1)}, bf16[64,1792]{1,0:T(8,128)(2,1)S(1)}, u32[]{:S(2)}, u32[]{:S(2)}) collective-permute-start(bf16[64,1792]{1,0:T(8,128)(2,1)S(1)} %get-tuple-element.56), channel_id=1, source_target_pairs={{0,12},{4,8},{8,4},{12,0},{1,13},{5,9},{9,5},{13,1},{2,14},{6,10},... | collective-permute-start | bytes 688136 | tf_op jit(solution)/shard_map/ppermute | solution.py:21
  6.5 19.5 %collective-permute-start.2 = (bf16[64,1792]{1,0:T(8,128)(2,1)S(1)}, bf16[64,1792]{1,0:T(8,128)(2,1)S(1)}, u32[]{:S(2)}, u32[]{:S(2)}) collective-permute-start(bf16[64,1792]{1,0:T(8,128)(2,1)S(1)} %get-tuple-element.57), channel_id=1, source_target_pairs={{0,8},{4,12},{8,0},{12,4},{1,9},{5,13},{9,1},{13,5},{2,10},{6,14},... | collective-permute-start | bytes 688136 | tf_op jit(solution)/shard_map/ppermute | solution.py:21
  6.5 19.5 %collective-permute-start.3 = (bf16[64,1792]{1,0:T(8,128)(2,1)S(1)}, bf16[64,1792]{1,0:T(8,128)(2,1)S(1)}, u32[]{:S(2)}, u32[]{:S(2)}) collective-permute-start(bf16[64,1792]{1,0:T(8,128)(2,1)S(1)} %get-tuple-element.58), channel_id=1, source_target_pairs={{0,4},{4,0},{8,12},{12,8},{1,5},{5,1},{9,13},{13,9},{2,6},{6,2},{1... | collective-permute-start | bytes 688136 | tf_op jit(solution)/shard_map/ppermute | solution.py:21
  7.1 2.2 %copy-start.1 = (bf16[32,128,512]{2,1,0:T(8,128)(2,1)S(1)}, bf16[32,128,512]{2,1,0:T(8,128)(2,1)}, u32[]{:S(2)}) copy-start(bf16[32,128,512]{2,1,0:T(8,128)(2,1)} %absorb_hbm.1) | copy-start | bytes 12582916
  7.1 3.5 %copy-start.2 = (bf16[32,512,128]{2,1,0:T(8,128)(2,1)S(1)}, bf16[32,512,128]{2,1,0:T(8,128)(2,1)}, u32[]{:S(2)}) copy-start(bf16[32,512,128]{2,1,0:T(8,128)(2,1)} %value_hbm.1) | copy-start | bytes 12582916
  7.1 4.1 %copy-start.3 = (bf16[8,256,576]{1,2,0:T(8,128)(2,1)S(1)}, bf16[8,256,576]{1,2,0:T(8,128)(2,1)}, u32[]{:S(2)}) copy-start(bf16[8,256,576]{1,2,0:T(8,128)(2,1)} %param.18) | copy-start | bytes 7077892
  7.2 4.1 %copy-start.6 = (bf16[8,2,32,192]{3,2,1,0:T(8,128)(2,1)S(1)}, bf16[8,2,32,192]{3,2,1,0:T(8,128)(2,1)}, u32[]{:S(2)}) copy-start(bf16[8,2,32,192]{3,2,1,0:T(8,128)(2,1)} %param.20) | copy-start | bytes 589828
  7.2 4.1 %copy-start.7 = (bf16[8,2,576]{2,1,0:T(2,128)(2,1)S(1)}, bf16[8,2,576]{2,1,0:T(2,128)(2,1)}, u32[]{:S(2)}) copy-start(bf16[8,2,576]{2,1,0:T(2,128)(2,1)} %fresh_hbm.1) | copy-start | bytes 55300
  7.2 4.1 %copy-start.8 = (s32[1024]{0:T(1024)S(1)}, s32[1024]{0:T(1024)}, u32[]{:S(2)}) copy-start(s32[1024]{0:T(1024)} %param.15) | copy-start | bytes 12292
  7.2 4.1 %copy-start.9 = (s32[16]{0:T(128)S(1)}, s32[16]{0:T(128)}, u32[]{:S(2)}) copy-start(s32[16]{0:T(128)} %length_hbm) | copy-start | bytes 196
  7.2 4.1 %copy-start.10 = (s32[16]{0:T(128)S(1)}, s32[16]{0:T(128)}, u32[]{:S(2)}) copy-start(s32[16]{0:T(128)} %slot_hbm.1) | copy-start | bytes 196
  7.3 13.0 %collective-permute-start = (bf16[2016,128]{1,0:T(8,128)(2,1)S(1)}, bf16[2016,128]{1,0:T(8,128)(2,1)S(1)}, u32[]{:S(2)}, u32[]{:S(2)}) collective-permute-start(bf16[2016,128]{1,0:T(8,128)(2,1)S(1)} %pack_weight.1.refs_0_), channel_id=1, source_target_pairs={{0,2},{1,3},{2,0},{3,1},{4,6},{5,7},{6,4},{7,5},{8,10},{9,11},{10,... | collective-permute-start | bytes 1548296 | tf_op jit(solution)/shard_map/ppermute | solution.py:21
  20.3 19.1 %copy-start = (f32[512]{0:T(512)S(1)}, f32[512]{0:T(512)}, u32[]{:S(2)}) copy-start(f32[512]{0:T(512)} %param.14) | copy-start | bytes 6148
  20.3 5.8 %collective-permute-start.4 = (bf16[2016,128]{1,0:T(8,128)(2,1)S(1)}, bf16[2016,128]{1,0:T(8,128)(2,1)S(1)}, u32[]{:S(2)}, u32[]{:S(2)}) collective-permute-start(bf16[2016,128]{1,0:T(8,128)(2,1)S(1)} %pack_weight.1.refs_0_), channel_id=1, source_target_pairs={{0,1},{1,0},{2,3},{3,2},{4,5},{5,4},{6,7},{7,6},{8,9},{9,8},{10,11... | collective-permute-start | bytes 1548296 | tf_op jit(solution)/shard_map/ppermute | solution.py:21
  20.3 5.8 %collective-permute-start.5 = (bf16[2016,128]{1,0:T(8,128)(2,1)S(1)}, bf16[2016,128]{1,0:T(8,128)(2,1)S(1)}, u32[]{:S(2)}, u32[]{:S(2)}) collective-permute-start(bf16[2016,128]{1,0:T(8,128)(2,1)S(1)} %collective-permute-done.refs_2_), channel_id=1, source_target_pairs={{0,1},{1,0},{2,3},{3,2},{4,5},{5,4},{6,7},{7,6},{8,9},{9,8},{10,11... | collective-permute-start | bytes 1548296 | tf_op jit(solution)/shard_map/ppermute | solution.py:21
  27.8 6.9 %collective-permute-start.6 = (bf16[288,128]{1,0:T(8,128)(2,1)S(1)}, bf16[288,128]{1,0:T(8,128)(2,1)S(1)}, u32[]{:S(2)}, u32[]{:S(2)}) collective-permute-start(bf16[288,128]{1,0:T(8,128)(2,1)S(1)} %get-tuple-element.62), channel_id=1, source_target_pairs={{0,12},{4,8},{8,4},{12,0},{1,13},{5,9},{9,5},{13,1},{2,14},{6,10},... | collective-permute-start | bytes 221192 | tf_op jit(solution)/shard_map/ppermute | solution.py:21
  30.3 9.0 %collective-permute-start.7 = (bf16[288,128]{1,0:T(8,128)(2,1)S(1)}, bf16[288,128]{1,0:T(8,128)(2,1)S(1)}, u32[]{:S(2)}, u32[]{:S(2)}) collective-permute-start(bf16[288,128]{1,0:T(8,128)(2,1)S(1)} %get-tuple-element.63), channel_id=1, source_target_pairs={{0,8},{4,12},{8,0},{12,4},{1,9},{5,13},{9,1},{13,5},{2,10},{6,14},... | collective-permute-start | bytes 221192 | tf_op jit(solution)/shard_map/ppermute | solution.py:21
  30.3 9.0 %collective-permute-start.8 = (bf16[288,128]{1,0:T(8,128)(2,1)S(1)}, bf16[288,128]{1,0:T(8,128)(2,1)S(1)}, u32[]{:S(2)}, u32[]{:S(2)}) collective-permute-start(bf16[288,128]{1,0:T(8,128)(2,1)S(1)} %get-tuple-element.64), channel_id=1, source_target_pairs={{0,4},{4,0},{8,12},{12,8},{1,5},{5,1},{9,13},{13,9},{2,6},{6,2},{1... | collective-permute-start | bytes 221192 | tf_op jit(solution)/shard_map/ppermute | solution.py:21
  32.2 9.0 %collective-permute-start.12 = (bf16[288,128]{1,0:T(8,128)(2,1)S(1)}, bf16[288,128]{1,0:T(8,128)(2,1)S(1)}, u32[]{:S(2)}, u32[]{:S(2)}) collective-permute-start(bf16[288,128]{1,0:T(8,128)(2,1)S(1)} %get-tuple-element.71), channel_id=1, source_target_pairs={{0,12},{4,8},{8,4},{12,0},{1,13},{5,9},{9,5},{13,1},{2,14},{6,10},... | collective-permute-start | bytes 221192 | tf_op jit(solution)/shard_map/ppermute | solution.py:21
  34.7 7.7 %collective-permute-start.13 = (bf16[288,128]{1,0:T(8,128)(2,1)S(1)}, bf16[288,128]{1,0:T(8,128)(2,1)S(1)}, u32[]{:S(2)}, u32[]{:S(2)}) collective-permute-start(bf16[288,128]{1,0:T(8,128)(2,1)S(1)} %get-tuple-element.72), channel_id=1, source_target_pairs={{0,8},{4,12},{8,0},{12,4},{1,9},{5,13},{9,1},{13,5},{2,10},{6,14},... | collective-permute-start | bytes 221192 | tf_op jit(solution)/shard_map/ppermute | solution.py:21
  34.7 7.7 %collective-permute-start.14 = (bf16[288,128]{1,0:T(8,128)(2,1)S(1)}, bf16[288,128]{1,0:T(8,128)(2,1)S(1)}, u32[]{:S(2)}, u32[]{:S(2)}) collective-permute-start(bf16[288,128]{1,0:T(8,128)(2,1)S(1)} %get-tuple-element.73), channel_id=1, source_target_pairs={{0,4},{4,0},{8,12},{12,8},{1,5},{5,1},{9,13},{13,9},{2,6},{6,2},{1... | collective-permute-start | bytes 221192 | tf_op jit(solution)/shard_map/ppermute | solution.py:21
  39.6 4.7 %collective-permute-start.11 = (bf16[288,128]{1,0:T(8,128)(2,1)S(1)}, bf16[288,128]{1,0:T(8,128)(2,1)S(1)}, u32[]{:S(2)}, u32[]{:S(2)}) collective-permute-start(bf16[288,128]{1,0:T(8,128)(2,1)S(1)} %finish_rows.2.refs_0_), channel_id=1, source_target_pairs={{0,3},{1,2},{2,1},{3,0},{4,7},{5,6},{6,5},{7,4},{8,11},{9,10},{10,... | collective-permute-start | bytes 221192 | tf_op jit(solution)/shard_map/ppermute | solution.py:21
  39.6 6.2 %collective-permute-start.10 = (bf16[288,128]{1,0:T(8,128)(2,1)S(1)}, bf16[288,128]{1,0:T(8,128)(2,1)S(1)}, u32[]{:S(2)}, u32[]{:S(2)}) collective-permute-start(bf16[288,128]{1,0:T(8,128)(2,1)S(1)} %finish_rows.2.refs_0_), channel_id=1, source_target_pairs={{0,2},{1,3},{2,0},{3,1},{4,6},{5,7},{6,4},{7,5},{8,10},{9,11},{10,... | collective-permute-start | bytes 221192 | tf_op jit(solution)/shard_map/ppermute | solution.py:21
  41.2 4.6 %collective-permute-start.9 = (bf16[288,128]{1,0:T(8,128)(2,1)S(1)}, bf16[288,128]{1,0:T(8,128)(2,1)S(1)}, u32[]{:S(2)}, u32[]{:S(2)}) collective-permute-start(bf16[288,128]{1,0:T(8,128)(2,1)S(1)} %finish_rows.2.refs_0_), channel_id=1, source_target_pairs={{0,1},{1,0},{2,3},{3,2},{4,5},{5,4},{6,7},{7,6},{8,9},{9,8},{10,11... | collective-permute-start | bytes 221192 | tf_op jit(solution)/shard_map/ppermute | solution.py:21
  42.7 4.6 %collective-permute-start.17 = (bf16[288,128]{1,0:T(8,128)(2,1)S(1)}, bf16[288,128]{1,0:T(8,128)(2,1)S(1)}, u32[]{:S(2)}, u32[]{:S(2)}) collective-permute-start(bf16[288,128]{1,0:T(8,128)(2,1)S(1)} %finish_rows.3.refs_0_), channel_id=1, source_target_pairs={{0,3},{1,2},{2,1},{3,0},{4,7},{5,6},{6,5},{7,4},{8,11},{9,10},{10,... | collective-permute-start | bytes 221192 | tf_op jit(solution)/shard_map/ppermute | solution.py:21
  42.9 6.0 %collective-permute-start.16 = (bf16[288,128]{1,0:T(8,128)(2,1)S(1)}, bf16[288,128]{1,0:T(8,128)(2,1)S(1)}, u32[]{:S(2)}, u32[]{:S(2)}) collective-permute-start(bf16[288,128]{1,0:T(8,128)(2,1)S(1)} %finish_rows.3.refs_0_), channel_id=1, source_target_pairs={{0,2},{1,3},{2,0},{3,1},{4,6},{5,7},{6,4},{7,5},{8,10},{9,11},{10,... | collective-permute-start | bytes 221192 | tf_op jit(solution)/shard_map/ppermute | solution.py:21
  44.3 4.6 %collective-permute-start.15 = (bf16[288,128]{1,0:T(8,128)(2,1)S(1)}, bf16[288,128]{1,0:T(8,128)(2,1)S(1)}, u32[]{:S(2)}, u32[]{:S(2)}) collective-permute-start(bf16[288,128]{1,0:T(8,128)(2,1)S(1)} %finish_rows.3.refs_0_), channel_id=1, source_target_pairs={{0,1},{1,0},{2,3},{3,2},{4,5},{5,4},{6,7},{7,6},{8,9},{9,8},{10,11... | collective-permute-start | bytes 221192 | tf_op jit(solution)/shard_map/ppermute | solution.py:21
  50.7 7.7 %collective-permute-start.23 = (bf16[16,3072]{1,0:T(8,128)(2,1)S(1)}, bf16[16,3072]{1,0:T(8,128)(2,1)S(1)}, u32[]{:S(2)}, u32[]{:S(2)}) collective-permute-start(bf16[16,3072]{1,0:T(8,128)(2,1)S(1)} %attend.3.refs_0_), channel_id=1, source_target_pairs={{0,12},{4,8},{8,4},{12,0},{1,13},{5,9},{9,5},{13,1},{2,14},{6,10},... | collective-permute-start | bytes 294920 | tf_op jit(solution)/shard_map/ppermute | solution.py:21
  53.0 9.3 %collective-permute-start.22 = (bf16[16,3072]{1,0:T(8,128)(2,1)S(1)}, bf16[16,3072]{1,0:T(8,128)(2,1)S(1)}, u32[]{:S(2)}, u32[]{:S(2)}) collective-permute-start(bf16[16,3072]{1,0:T(8,128)(2,1)S(1)} %attend.3.refs_0_), channel_id=1, source_target_pairs={{0,8},{4,12},{8,0},{12,4},{1,9},{5,13},{9,1},{13,5},{2,10},{6,14},... | collective-permute-start | bytes 294920 | tf_op jit(solution)/shard_map/ppermute | solution.py:21
  53.0 9.3 %collective-permute-start.21 = (bf16[16,3072]{1,0:T(8,128)(2,1)S(1)}, bf16[16,3072]{1,0:T(8,128)(2,1)S(1)}, u32[]{:S(2)}, u32[]{:S(2)}) collective-permute-start(bf16[16,3072]{1,0:T(8,128)(2,1)S(1)} %attend.3.refs_0_), channel_id=1, source_target_pairs={{0,4},{4,0},{8,12},{12,8},{1,5},{5,1},{9,13},{13,9},{2,6},{6,2},{1... | collective-permute-start | bytes 294920 | tf_op jit(solution)/shard_map/ppermute | solution.py:21
  56.1 8.3 %collective-permute-start.20 = (bf16[16,1024]{1,0:T(8,128)(2,1)S(1)}, bf16[16,1024]{1,0:T(8,128)(2,1)S(1)}, u32[]{:S(2)}, u32[]{:S(2)}) collective-permute-start(bf16[16,1024]{1,0:T(8,128)(2,1)S(1)} %attend.2.refs_0_), channel_id=1, source_target_pairs={{0,12},{4,8},{8,4},{12,0},{1,13},{5,9},{9,5},{13,1},{2,14},{6,10},... | collective-permute-start | bytes 98312 | tf_op jit(solution)/shard_map/ppermute | solution.py:21
  58.4 6.0 %collective-permute-start.19 = (bf16[16,1024]{1,0:T(8,128)(2,1)S(1)}, bf16[16,1024]{1,0:T(8,128)(2,1)S(1)}, u32[]{:S(2)}, u32[]{:S(2)}) collective-permute-start(bf16[16,1024]{1,0:T(8,128)(2,1)S(1)} %attend.2.refs_0_), channel_id=1, source_target_pairs={{0,8},{4,12},{8,0},{12,4},{1,9},{5,13},{9,1},{13,5},{2,10},{6,14},... | collective-permute-start | bytes 98312 | tf_op jit(solution)/shard_map/ppermute | solution.py:21
  58.4 6.0 %collective-permute-start.18 = (bf16[16,1024]{1,0:T(8,128)(2,1)S(1)}, bf16[16,1024]{1,0:T(8,128)(2,1)S(1)}, u32[]{:S(2)}, u32[]{:S(2)}) collective-permute-start(bf16[16,1024]{1,0:T(8,128)(2,1)S(1)} %attend.2.refs_0_), channel_id=1, source_target_pairs={{0,4},{4,0},{8,12},{12,8},{1,5},{5,1},{9,13},{13,9},{2,6},{6,2},{1... | collective-permute-start | bytes 98312 | tf_op jit(solution)/shard_map/ppermute | solution.py:21
  65.2 4.1 %collective-permute-start.24 = (bf16[16,1792]{1,0:T(8,128)(2,1)S(1)}, bf16[16,1792]{1,0:T(8,128)(2,1)S(1)}, u32[]{:S(2)}, u32[]{:S(2)}) collective-permute-start(bf16[16,1792]{1,0:T(8,128)(2,1)S(1)} %get-tuple-element.76), channel_id=1, source_target_pairs={{0,3},{1,2},{2,1},{3,0},{4,7},{5,6},{6,5},{7,4},{8,11},{9,10},{10,... | collective-permute-start | bytes 172040 | tf_op jit(solution)/shard_map/ppermute | solution.py:21
  65.9 4.7 %collective-permute-start.25 = (bf16[16,1792]{1,0:T(8,128)(2,1)S(1)}, bf16[16,1792]{1,0:T(8,128)(2,1)S(1)}, u32[]{:S(2)}, u32[]{:S(2)}) collective-permute-start(bf16[16,1792]{1,0:T(8,128)(2,1)S(1)} %get-tuple-element.77), channel_id=1, source_target_pairs={{0,2},{1,3},{2,0},{3,1},{4,6},{5,7},{6,4},{7,5},{8,10},{9,11},{10,... | collective-permute-start | bytes 172040 | tf_op jit(solution)/shard_map/ppermute | solution.py:21
  67.0 3.6 %collective-permute-start.26 = (bf16[16,1792]{1,0:T(8,128)(2,1)S(1)}, bf16[16,1792]{1,0:T(8,128)(2,1)S(1)}, u32[]{:S(2)}, u32[]{:S(2)}) collective-permute-start(bf16[16,1792]{1,0:T(8,128)(2,1)S(1)} %get-tuple-element.78), channel_id=1, source_target_pairs={{0,1},{1,0},{2,3},{3,2},{4,5},{5,4},{6,7},{7,6},{8,9},{9,8},{10,11... | collective-permute-start | bytes 172040 | tf_op jit(solution)/shard_map/ppermute | solution.py:21

commit v10 on v9

--- a/solution.py
+++ b/solution.py
@@ -108,7 +108,7 @@
             flops=10**10, bytes_accessed=4 * 10**7, transcendentals=0
         ),
         name="split_columns",
-    )(prompts)
+    )(pltpu.with_memory_space_constraint(prompts, pltpu.HBM))
 
 
 def fill_tables(
@@ -532,14 +532,10 @@
     latent = (mix / total).astype(bf16)
     live = live_ref[:, :1]
     width = value_ref.shape[2]
-    for h in range(0, heads, 2):
-        head = first_head + h
-        pair = jnp.concatenate([value_ref[head], value_ref[head + 1]], axis=1)
-        both = jnp.dot(
-            latent[h * per_head : (h + 2) * per_head, :], pair, preferred_element_type=f32
-        )
-        out_ref[:, h * width : (h + 1) * width] = (both[:per_head, :width] * live).astype(bf16)
-        out_ref[:, (h + 1) * width : (h + 2) * width] = (both[per_head:, width:] * live).astype(bf16)
+    for h in range(heads):
+        mixed = latent[h * per_head : (h + 1) * per_head, :]
+        value = jnp.dot(mixed, value_ref[first_head + h], preferred_element_type=f32) * live
+        out_ref[:, h * width : (h + 1) * width] = value.astype(bf16)
 
 
 def attend(layout, which, query, row_slot, top, total, mix, live, value, pieces, first_head, heads):
@@ -679,14 +675,17 @@
         if which == 0:
             state = absorb(layout, which, query_full, row_slot, *state, pieces)
     product, first_head, head_count = None, 0, value_absorb.shape[0]
-    for part_heads in (head_count * 3 // 4, head_count // 4):
+    for part_heads in (head_count * 5 // 8, head_count * 3 // 8):
         head_out = attend(
             layout, 1, query_full, row_slot, *state, live, value_here, pieces, first_head,
             part_heads,
         )
         heads = [head_out] + [None] * (dev_count - 1)
         for k in sorted(range(1, dev_count), reverse=True):
-            heads[k] = swap(head_out, "dev", k)
+            if k == 1 or k % 2 == 0:
+                heads[k] = swap(head_out, "dev", k)
+        for k in range(3, dev_count, 2):
+            heads[k] = swap(heads[k - 1], "dev", 1)
         start, first_head = first_head * nope_width, first_head + part_heads
         products = output_product(
             heads, out_here, side_count, product, start, first_head == head_count

time: 71.4 us -> 70.9 us (level)
  starting transfers between devices: 31.4 us -> 28.1 us
  waiting for transfers between devices: 18.4 us -> 21.6 us
  local copies, waits for them, and re-layouts: 3.49 us -> 2.31 us
  Pallas kernels: 17.1 us -> 18 us
    ppermute x27, starting transfers between devices: 31.4 us -> 28.1 us  [swap(): return lax.ppermute(value, axis, [(i, i ^ step) for i in range(count)])]
    ppermute x27, waiting for transfers between devices: 18.4 us -> 21.6 us  [swap(): return lax.ppermute(value, axis, [(i, i ^ step) for i in range(count)])]
    unnamed x22 -> x20, local copies, waits for them, and re-layouts: 3.49 us -> 2.31 us
    pallas_call x1, Pallas kernels: 0.19 us -> 1.36 us  [split_columns(): pl.pallas_call(functools.partial(split_kernel, slab), out_shape=[jax.Shap...]
  transfers between devices with their start and end apart: 27 -> 27, of which waited for: 9 -> 12; matrix products, arithmetic and copies ran while one was open for 0% -> 0% of each run, Pallas kernels for 18% -> 18%
where the time goes in v10:
time: 70.9 us; the launch traced here: 70.8 us
  starting transfers between devices  28.1 us (40%)
  waiting for transfers between devices  21.6 us (30%)
  Pallas kernels  18 us (25%)
  local copies, waits for them, and re-layouts  2.31 us (3%)
    ppermute x27, starting transfers between devices, swap(): return lax.ppermute(value, axis, [(i, i ^ step) for i in range(count)])  28.1 us
    ppermute x27, waiting for transfers between devices, swap(): return lax.ppermute(value, axis, [(i, i ^ step) for i in range(count)])  21.6 us
    pallas_call x1, Pallas kernels, prepare(): pl.pallas_call(functools.partial(prepare_kernel, scale, steps, (dev_count...  7.61 us
    pallas_call x2, Pallas kernels, output_product(): pl.pallas_call(functools.partial(output_kernel, dev_count, side_count, st...  2.79 us
    pallas_call x2, Pallas kernels, attend(): pl.pallas_call(functools.partial(attend_kernel, layout, which, first_head...  2.49 us
    unnamed x20, local copies, waits for them, and re-layouts  2.31 us
    pallas_call x1, Pallas kernels, project(): pl.pallas_call(functools.partial(project_kernel, dev_count, len(weights))...  1.7 us
    pallas_call x1, Pallas kernels, absorb(): pl.pallas_call(functools.partial(absorb_kernel, layout, which), out_shape...  1.44 us
  transfers between devices with their start and end apart: 27, of which 12 were waited for; matrix products, arithmetic and copies ran while one was open for 0% of the time, Pallas kernels for 18%

profile of v10, /device:TPU:0, one launch (start us, length us, event | category | flops | bytes accessed | tf_op | source)
XLA Modules:
  0.0 70.8 jit_solution(5200156633679898991)
XLA Ops:
  0.0 1.4 %split_columns.1 = (bf16[64,1792]{1,0:T(8,128)(2,1)S(1)}, bf16[64,1792]{1,0:T(8,128)(2,1)S(1)}, bf16[64,1792]{1,0:T(8,128)(2,1)S(1)}, bf16[64,1792]{1,0:T(8,128)(2,1)S(1)}) custom-call(bf16[64,7168]{1,0:T(8,128)(2,1)} %prompts_ref.1), custom_call_target="tpu_custom_call" | custom-call | flops 10000000000 | bytes 40000000 | tf_op jit(solution)/shard_map/split_columns/pallas_call | solution.py:100
  1.4 5.1 %collective-permute-start.1 = (bf16[64,1792]{1,0:T(8,128)(2,1)S(1)}, bf16[64,1792]{1,0:T(8,128)(2,1)S(1)}, u32[]{:S(2)}, u32[]{:S(2)}) collective-permute-start(bf16[64,1792]{1,0:T(8,128)(2,1)S(1)} %get-tuple-element.56), channel_id=1, source_target_pairs={{0,12},{4,8},{8,4},{12,0},{1,13},{5,9},{9,5},{13,1},{2,14},{6,10},... | collective-permute-start | bytes 688136 | tf_op jit(solution)/shard_map/ppermute | solution.py:21
  6.5 0.6 collective-permute-start.3
  7.2 0.1 pack_weight.1.refs_0_
  7.3 1.7 %collective-permute-start = (bf16[2016,128]{1,0:T(8,128)(2,1)S(1)}, bf16[2016,128]{1,0:T(8,128)(2,1)S(1)}, u32[]{:S(2)}, u32[]{:S(2)}) collective-permute-start(bf16[2016,128]{1,0:T(8,128)(2,1)S(1)} %pack_weight.1.refs_0_), channel_id=1, source_target_pairs={{0,2},{1,3},{2,0},{3,1},{4,6},{5,7},{6,4},{7,5},{8,10},{9,11},{10,... | collective-permute-start | bytes 1548296 | tf_op jit(solution)/shard_map/ppermute | solution.py:21
  9.0 0.3 copy-done.1
  9.3 1.3 %copy-done.2 = bf16[32,512,128]{2,1,0:T(8,128)(2,1)S(1)} copy-done((bf16[32,512,128]{2,1,0:T(8,128)(2,1)S(1)}, bf16[32,512,128]{2,1,0:T(8,128)(2,1)}, u32[]{:S(2)}) %copy-start.2) | copy-done | bytes 4194328
  10.6 0.7 copy-done.3
  11.3 7.6 %prepare.1 = (bf16[512,576]{1,0:T(8,128)(2,1)S(1)}, f32[512,128]{1,0:T(8,128)S(1)}, f32[512,128]{1,0:T(8,128)S(1)}, f32[4,512,128]{2,1,0:T(8,128)S(1)}, f32[16,1...) custom-call(f32[1,32]{1,0:T(1,128)S(1)} %negate_power_fusion.inverse, ...), custom_call_target="tpu_custom_call" | custom-call | flops 40000000000 | bytes 28000000 | tf_op jit(solution)/shard_map/prepare/pallas_call | solution.py:323
  18.9 1.4 %collective-permute-done.refs_2_ = bf16[2016,128]{1,0:T(8,128)(2,1)S(1)} collective-permute-done((bf16[2016,128]{1,0:T(8,128)(2,1)S(1)}, bf16[2016,128]{1,0:T(8,128)(2,1)S(1)}, u32[]{:S(2)}, u32[]{:S(2)}) %collective-permute-start) | collective-permute-done | bytes 516128 | tf_op jit(solution)/shard_map/ppermute | solution.py:21
  20.3 0.5 collective-permute-start.5
  20.8 5.2 %collective-permute-done.2.refs_2_ = bf16[64,1792]{1,0:T(8,128)(2,1)S(1)} collective-permute-done((bf16[64,1792]{1,0:T(8,128)(2,1)S(1)}, bf16[64,1792]{1,0:T(8,128)(2,1)S(1)}, u32[]{:S(2)}, u32[]{:S(2)}) %collective-permute-start.2) | collective-permute-done | bytes 229408 | tf_op jit(solution)/shard_map/ppermute | solution.py:21
  26.0 0.1 stack_rows.1.x_ref
  26.1 1.7 %project.1 = (f32[288,128]{1,0:T(8,128)S(1)}, bf16[288,128]{1,0:T(8,128)(2,1)S(1)}, bf16[288,128]{1,0:T(8,128)(2,1)S(1)}, bf16[288,128]{1,0:T(8,128)(2,1)S(1)}, ...) custom-call(s32[1,256]{1,0:T(1,128)S(1)} %get-tuple-element.54.targe, ...), custom_call_target="tpu_custom_call" | custom-call | tf_op jit(solution)/shard_map/project/pallas_call | solution.py:405
  27.8 2.5 %collective-permute-start.6 = (bf16[288,128]{1,0:T(8,128)(2,1)S(1)}, bf16[288,128]{1,0:T(8,128)(2,1)S(1)}, u32[]{:S(2)}, u32[]{:S(2)}) collective-permute-start(bf16[288,128]{1,0:T(8,128)(2,1)S(1)} %get-tuple-element.62), channel_id=1, source_target_pairs={{0,12},{4,8},{8,4},{12,0},{1,13},{5,9},{9,5},{13,1},{2,14},{6,10},... | collective-permute-start | bytes 221192 | tf_op jit(solution)/shard_map/ppermute | solution.py:21
  30.3 1.9 %collective-permute-start.8 = (bf16[288,128]{1,0:T(8,128)(2,1)S(1)}, bf16[288,128]{1,0:T(8,128)(2,1)S(1)}, u32[]{:S(2)}, u32[]{:S(2)}) collective-permute-start(bf16[288,128]{1,0:T(8,128)(2,1)S(1)} %get-tuple-element.64), channel_id=1, source_target_pairs={{0,4},{4,0},{8,12},{12,8},{1,5},{5,1},{9,13},{13,9},{2,6},{6,2},{1... | collective-permute-start | bytes 221192 | tf_op jit(solution)/shard_map/ppermute | solution.py:21
  32.2 2.5 %collective-permute-start.12 = (bf16[288,128]{1,0:T(8,128)(2,1)S(1)}, bf16[288,128]{1,0:T(8,128)(2,1)S(1)}, u32[]{:S(2)}, u32[]{:S(2)}) collective-permute-start(bf16[288,128]{1,0:T(8,128)(2,1)S(1)} %get-tuple-element.71), channel_id=1, source_target_pairs={{0,12},{4,8},{8,4},{12,0},{1,13},{5,9},{9,5},{13,1},{2,14},{6,10},... | collective-permute-start | bytes 221192 | tf_op jit(solution)/shard_map/ppermute | solution.py:21
  34.7 1.9 %collective-permute-start.14 = (bf16[288,128]{1,0:T(8,128)(2,1)S(1)}, bf16[288,128]{1,0:T(8,128)(2,1)S(1)}, u32[]{:S(2)}, u32[]{:S(2)}) collective-permute-start(bf16[288,128]{1,0:T(8,128)(2,1)S(1)} %get-tuple-element.73), channel_id=1, source_target_pairs={{0,4},{4,0},{8,12},{12,8},{1,5},{5,1},{9,13},{13,9},{2,6},{6,2},{1... | collective-permute-start | bytes 221192 | tf_op jit(solution)/shard_map/ppermute | solution.py:21
  36.6 2.7 %collective-permute-done.7.refs_2_ = bf16[288,128]{1,0:T(8,128)(2,1)S(1)} collective-permute-done((bf16[288,128]{1,0:T(8,128)(2,1)S(1)}, bf16[288,128]{1,0:T(8,128)(2,1)S(1)}, u32[]{:S(2)}, u32[]{:S(2)}) %collective-permute-start.7) | collective-permute-done | bytes 73760 | tf_op jit(solution)/shard_map/ppermute | solution.py:21
  39.4 0.2 finish_rows.2.refs_0_
  39.7 1.5 %collective-permute-start.10 = (bf16[288,128]{1,0:T(8,128)(2,1)S(1)}, bf16[288,128]{1,0:T(8,128)(2,1)S(1)}, u32[]{:S(2)}, u32[]{:S(2)}) collective-permute-start(bf16[288,128]{1,0:T(8,128)(2,1)S(1)} %finish_rows.2.refs_0_), channel_id=1, source_target_pairs={{0,2},{1,3},{2,0},{3,1},{4,6},{5,7},{6,4},{7,5},{8,10},{9,11},{10,... | collective-permute-start | bytes 221192 | tf_op jit(solution)/shard_map/ppermute | solution.py:21
  41.2 0.3 collective-permute-start.9
  41.5 0.9 %collective-permute-done.13.refs_2_ = bf16[288,128]{1,0:T(8,128)(2,1)S(1)} collective-permute-done((bf16[288,128]{1,0:T(8,128)(2,1)S(1)}, bf16[288,128]{1,0:T(8,128)(2,1)S(1)}, u32[]{:S(2)}, u32[]{:S(2)}) %collective-permute-start.13) | collective-permute-done | bytes 73760 | tf_op jit(solution)/shard_map/ppermute | solution.py:21
  42.4 0.2 finish_rows.3.refs_0_
  42.7 0.2 collective-permute-start.17
  42.9 1.4 %collective-permute-start.16 = (bf16[288,128]{1,0:T(8,128)(2,1)S(1)}, bf16[288,128]{1,0:T(8,128)(2,1)S(1)}, u32[]{:S(2)}, u32[]{:S(2)}) collective-permute-start(bf16[288,128]{1,0:T(8,128)(2,1)S(1)} %finish_rows.3.refs_0_), channel_id=1, source_target_pairs={{0,2},{1,3},{2,0},{3,1},{4,6},{5,7},{6,4},{7,5},{8,10},{9,11},{10,... | collective-permute-start | bytes 221192 | tf_op jit(solution)/shard_map/ppermute | solution.py:21
  44.3 0.3 collective-permute-start.15
  44.6 1.2 %collective-permute-done.10.refs_2_ = bf16[288,128]{1,0:T(8,128)(2,1)S(1)} collective-permute-done((bf16[288,128]{1,0:T(8,128)(2,1)S(1)}, bf16[288,128]{1,0:T(8,128)(2,1)S(1)}, u32[]{:S(2)}, u32[]{:S(2)}) %collective-permute-start.10) | collective-permute-done | bytes 73760 | tf_op jit(solution)/shard_map/ppermute | solution.py:21
  45.8 1.4 %absorb.1 = (f32[512,128]{1,0:T(8,128)S(1)}, f32[512,128]{1,0:T(8,128)S(1)}, f32[4,512,128]{2,1,0:T(8,128)S(1)}) custom-call(bf16[512,576]{1,0:T(8,128)(2,1)S(1)} %get-tuple-element.45.query_ref, s32[1,512]{1,0:T(1,128)S(1)} %get-tuple-element.46.slot_ref, f32[512,128]{1,0:T(8,128)S(1)} %get-tuple-element.49.top_ref, ...), custom_call_target="tpu_custom_call" | custom-call | flops 2000000000 | bytes 1000000 | tf_op jit(solution)/shard_map/absorb/pallas_call | solution.py:509
  47.3 0.1 collective-permute-done.17.refs_3_
  47.3 1.6 %collective-permute-done.16.refs_2_ = bf16[288,128]{1,0:T(8,128)(2,1)S(1)} collective-permute-done((bf16[288,128]{1,0:T(8,128)(2,1)S(1)}, bf16[288,128]{1,0:T(8,128)(2,1)S(1)}, u32[]{:S(2)}, u32[]{:S(2)}) %collective-permute-start.16) | collective-permute-done | bytes 73760 | tf_op jit(solution)/shard_map/ppermute | solution.py:21
  49.0 1.3 %attend.3.refs_0_ = bf16[16,2560]{1,0:T(8,128)(2,1)S(1)} custom-call(bf16[512,576]{1,0:T(8,128)(2,1)S(1)} %get-tuple-element.45.query_ref, s32[1,512]{1,0:T(1,128)S(1)} %get-tuple-element.46.slot_ref, f32[512,128]{1,0:T(8,128)S(1)} %get-tuple-element.65.top_ref, f32[512,128]{1,0:T(8,128)S(1)} %get-tuple-element.66.sum_ref, ...), custom_call_target="tpu_custom_call" | custom-call | tf_op jit(solution)/shard_map/attend/pallas_call | solution.py:542
  50.3 0.5 collective-permute-start.22
  50.8 1.1 %attend.2.refs_0_ = bf16[16,1536]{1,0:T(8,128)(2,1)S(1)} custom-call(bf16[512,576]{1,0:T(8,128)(2,1)S(1)} %get-tuple-element.45.query_ref, s32[1,512]{1,0:T(1,128)S(1)} %get-tuple-element.46.slot_ref, f32[512,128]{1,0:T(8,128)S(1)} %get-tuple-element.65.top_ref, f32[512,128]{1,0:T(8,128)S(1)} %get-tuple-element.66.sum_ref, ...), custom_call_target="tpu_custom_call" | custom-call | tf_op jit(solution)/shard_map/attend/pallas_call | solution.py:542
  52.0 2.5 %collective-permute-start.19 = (bf16[16,1536]{1,0:T(8,128)(2,1)S(1)}, bf16[16,1536]{1,0:T(8,128)(2,1)S(1)}, u32[]{:S(2)}, u32[]{:S(2)}) collective-permute-start(bf16[16,1536]{1,0:T(8,128)(2,1)S(1)} %attend.2.refs_0_), channel_id=1, source_target_pairs={{0,8},{4,12},{8,0},{12,4},{1,9},{5,13},{9,1},{13,5},{2,10},{6,14},... | collective-permute-start | bytes 147464 | tf_op jit(solution)/shard_map/ppermute | solution.py:21
  54.5 2.7 %collective-permute-done.22.refs_2_ = bf16[16,2560]{1,0:T(8,128)(2,1)S(1)} collective-permute-done((bf16[16,2560]{1,0:T(8,128)(2,1)S(1)}, bf16[16,2560]{1,0:T(8,128)(2,1)S(1)}, u32[]{:S(2)}, u32[]{:S(2)}) %collective-permute-start.22) | collective-permute-done | bytes 81952 | tf_op jit(solution)/shard_map/ppermute | solution.py:21
  57.1 2.0 %collective-permute-start.18 = (bf16[16,1536]{1,0:T(8,128)(2,1)S(1)}, bf16[16,1536]{1,0:T(8,128)(2,1)S(1)}, u32[]{:S(2)}, u32[]{:S(2)}) collective-permute-start(bf16[16,1536]{1,0:T(8,128)(2,1)S(1)} %attend.2.refs_0_), channel_id=1, source_target_pairs={{0,4},{4,0},{8,12},{12,8},{1,5},{5,1},{9,13},{13,9},{2,6},{6,2},{1... | collective-permute-start | bytes 147464 | tf_op jit(solution)/shard_map/ppermute | solution.py:21
  59.2 0.5 collective-permute-start.20
  59.6 0.3 collective-permute-done.21.refs_1_
  59.9 2.5 %collective-permute-done.23.refs_3_ = bf16[16,2560]{1,0:T(8,128)(2,1)S(1)} collective-permute-done((bf16[16,2560]{1,0:T(8,128)(2,1)S(1)}, bf16[16,2560]{1,0:T(8,128)(2,1)S(1)}, u32[]{:S(2)}, u32[]{:S(2)}) %collective-permute-start.23) | collective-permute-done | bytes 81952 | tf_op jit(solution)/shard_map/ppermute | solution.py:21
  62.4 1.7 %output_product.2.refs_5_ = f32[64,1792]{1,0:T(8,128)S(1)} custom-call(bf16[16,2560]{1,0:T(8,128)(2,1)S(1)} %attend.3.refs_0_, bf16[16,2560]{1,0:T(8,128)(2,1)S(1)} %collective-permute-done.21.refs_1_, bf16[16,2560]{1,0:T(8,128)(2,1)S(1)} %collective-permute-done.22.refs_2_, bf16[16,2560]{1,0:T(8,128)(2,1)S(1)} %collective-permute-done.23.refs_3_, ...), custom_call_target="tpu_custom_call" | custom-call | tf_op jit(solution)/shard_map/output_product/pallas_call | solution.py:596
  64.2 1.1 %output_product.3 = (f32[16,1792]{1,0:T(8,128)S(1)}, bf16[16,1792]{1,0:T(8,128)(2,1)S(1)}, bf16[16,1792]{1,0:T(8,128)(2,1)S(1)}, bf16[16,1792]{1,0:T(8,128)(2,1)S(1)}) custom-call(bf16[16,1536]{1,0:T(8,128)(2,1)S(1)} %attend.2.refs_0_, bf16[16,1536]{1,0:T(8,128)(2,1)S(1)} %collective-permute-done.18.refs_1_, ...), custom_call_target="tpu_custom_call" | custom-call | tf_op jit(solution)/shard_map/output_product/pallas_call | solution.py:596
  65.3 0.1 collective-permute-start.24
  65.3 0.9 %collective-permute-start.25 = (bf16[16,1792]{1,0:T(8,128)(2,1)S(1)}, bf16[16,1792]{1,0:T(8,128)(2,1)S(1)}, u32[]{:S(2)}, u32[]{:S(2)}) collective-permute-start(bf16[16,1792]{1,0:T(8,128)(2,1)S(1)} %get-tuple-element.77), channel_id=1, source_target_pairs={{0,2},{1,3},{2,0},{3,1},{4,6},{5,7},{6,4},{7,5},{8,10},{9,11},{10,... | collective-permute-start | bytes 172040 | tf_op jit(solution)/shard_map/ppermute | solution.py:21
  66.3 0.9 %collective-permute-start.26 = (bf16[16,1792]{1,0:T(8,128)(2,1)S(1)}, bf16[16,1792]{1,0:T(8,128)(2,1)S(1)}, u32[]{:S(2)}, u32[]{:S(2)}) collective-permute-start(bf16[16,1792]{1,0:T(8,128)(2,1)S(1)} %get-tuple-element.78), channel_id=1, source_target_pairs={{0,1},{1,0},{2,3},{3,2},{4,5},{5,4},{6,7},{7,6},{8,9},{9,8},{10,11... | collective-permute-start | bytes 172040 | tf_op jit(solution)/shard_map/ppermute | solution.py:21
  67.2 1.8 %collective-permute-done.24 = bf16[16,1792]{1,0:T(8,128)(2,1)S(1)} collective-permute-done((bf16[16,1792]{1,0:T(8,128)(2,1)S(1)}, bf16[16,1792]{1,0:T(8,128)(2,1)S(1)}, u32[]{:S(2)}, u32[]{:S(2)}) %collective-permute-start.24) | collective-permute-done | bytes 57376 | tf_op jit(solution)/shard_map/ppermute | solution.py:21
  69.0 1.2 %collective-permute-done.25 = bf16[16,1792]{1,0:T(8,128)(2,1)S(1)} collective-permute-done((bf16[16,1792]{1,0:T(8,128)(2,1)S(1)}, bf16[16,1792]{1,0:T(8,128)(2,1)S(1)}, u32[]{:S(2)}, u32[]{:S(2)}) %collective-permute-start.25) | collective-permute-done | bytes 57376 | tf_op jit(solution)/shard_map/ppermute | solution.py:21
  70.1 0.7 add_convert_fusion
  (40 shorter events, 0.2 us)
Async XLA Ops:
  0.0 7.1 %copy-start.4 = (bf16[448,576]{1,0:T(8,128)(2,1)S(1)}, bf16[448,576]{1,0:T(8,128)(2,1)}, u32[]{:S(2)}) copy-start(bf16[448,576]{1,0:T(8,128)(2,1)} %value_ref) | copy-start | bytes 1548292
  1.4 19.4 %collective-permute-start.1 = (bf16[64,1792]{1,0:T(8,128)(2,1)S(1)}, bf16[64,1792]{1,0:T(8,128)(2,1)S(1)}, u32[]{:S(2)}, u32[]{:S(2)}) collective-permute-start(bf16[64,1792]{1,0:T(8,128)(2,1)S(1)} %get-tuple-element.56), channel_id=1, source_target_pairs={{0,12},{4,8},{8,4},{12,0},{1,13},{5,9},{9,5},{13,1},{2,14},{6,10},... | collective-permute-start | bytes 688136 | tf_op jit(solution)/shard_map/ppermute | solution.py:21
  6.5 19.5 %collective-permute-start.2 = (bf16[64,1792]{1,0:T(8,128)(2,1)S(1)}, bf16[64,1792]{1,0:T(8,128)(2,1)S(1)}, u32[]{:S(2)}, u32[]{:S(2)}) collective-permute-start(bf16[64,1792]{1,0:T(8,128)(2,1)S(1)} %get-tuple-element.57), channel_id=1, source_target_pairs={{0,8},{4,12},{8,0},{12,4},{1,9},{5,13},{9,1},{13,5},{2,10},{6,14},... | collective-permute-start | bytes 688136 | tf_op jit(solution)/shard_map/ppermute | solution.py:21
  6.5 19.5 %collective-permute-start.3 = (bf16[64,1792]{1,0:T(8,128)(2,1)S(1)}, bf16[64,1792]{1,0:T(8,128)(2,1)S(1)}, u32[]{:S(2)}, u32[]{:S(2)}) collective-permute-start(bf16[64,1792]{1,0:T(8,128)(2,1)S(1)} %get-tuple-element.58), channel_id=1, source_target_pairs={{0,4},{4,0},{8,12},{12,8},{1,5},{5,1},{9,13},{13,9},{2,6},{6,2},{1... | collective-permute-start | bytes 688136 | tf_op jit(solution)/shard_map/ppermute | solution.py:21
  7.1 2.2 %copy-start.1 = (bf16[32,128,512]{2,1,0:T(8,128)(2,1)S(1)}, bf16[32,128,512]{2,1,0:T(8,128)(2,1)}, u32[]{:S(2)}) copy-start(bf16[32,128,512]{2,1,0:T(8,128)(2,1)} %absorb_hbm.1) | copy-start | bytes 12582916
  7.1 3.5 %copy-start.2 = (bf16[32,512,128]{2,1,0:T(8,128)(2,1)S(1)}, bf16[32,512,128]{2,1,0:T(8,128)(2,1)}, u32[]{:S(2)}) copy-start(bf16[32,512,128]{2,1,0:T(8,128)(2,1)} %value_hbm.1) | copy-start | bytes 12582916
  7.1 4.1 %copy-start.3 = (bf16[8,256,576]{1,2,0:T(8,128)(2,1)S(1)}, bf16[8,256,576]{1,2,0:T(8,128)(2,1)}, u32[]{:S(2)}) copy-start(bf16[8,256,576]{1,2,0:T(8,128)(2,1)} %param.18) | copy-start | bytes 7077892
  7.1 4.1 %copy-start.5 = (bf16[8,2,32,192]{3,2,1,0:T(8,128)(2,1)S(1)}, bf16[8,2,32,192]{3,2,1,0:T(8,128)(2,1)}, u32[]{:S(2)}) copy-start(bf16[8,2,32,192]{3,2,1,0:T(8,128)(2,1)} %param.20) | copy-start | bytes 589828
  7.2 4.1 %copy-start.6 = (bf16[8,2,576]{2,1,0:T(2,128)(2,1)S(1)}, bf16[8,2,576]{2,1,0:T(2,128)(2,1)}, u32[]{:S(2)}) copy-start(bf16[8,2,576]{2,1,0:T(2,128)(2,1)} %fresh_hbm.1) | copy-start | bytes 55300
  7.2 4.1 %copy-start.7 = (s32[1024]{0:T(1024)S(1)}, s32[1024]{0:T(1024)}, u32[]{:S(2)}) copy-start(s32[1024]{0:T(1024)} %param.15) | copy-start | bytes 12292
  7.2 4.1 %copy-start.8 = (s32[16]{0:T(128)S(1)}, s32[16]{0:T(128)}, u32[]{:S(2)}) copy-start(s32[16]{0:T(128)} %length_hbm) | copy-start | bytes 196
  7.2 4.1 %copy-start.9 = (s32[16]{0:T(128)S(1)}, s32[16]{0:T(128)}, u32[]{:S(2)}) copy-start(s32[16]{0:T(128)} %slot_hbm.1) | copy-start | bytes 196
  7.3 13.0 %collective-permute-start = (bf16[2016,128]{1,0:T(8,128)(2,1)S(1)}, bf16[2016,128]{1,0:T(8,128)(2,1)S(1)}, u32[]{:S(2)}, u32[]{:S(2)}) collective-permute-start(bf16[2016,128]{1,0:T(8,128)(2,1)S(1)} %pack_weight.1.refs_0_), channel_id=1, source_target_pairs={{0,2},{1,3},{2,0},{3,1},{4,6},{5,7},{6,4},{7,5},{8,10},{9,11},{10,... | collective-permute-start | bytes 1548296 | tf_op jit(solution)/shard_map/ppermute | solution.py:21
  20.3 19.1 %copy-start = (f32[512]{0:T(512)S(1)}, f32[512]{0:T(512)}, u32[]{:S(2)}) copy-start(f32[512]{0:T(512)} %param.14) | copy-start | bytes 6148
  20.3 5.8 %collective-permute-start.4 = (bf16[2016,128]{1,0:T(8,128)(2,1)S(1)}, bf16[2016,128]{1,0:T(8,128)(2,1)S(1)}, u32[]{:S(2)}, u32[]{:S(2)}) collective-permute-start(bf16[2016,128]{1,0:T(8,128)(2,1)S(1)} %pack_weight.1.refs_0_), channel_id=1, source_target_pairs={{0,1},{1,0},{2,3},{3,2},{4,5},{5,4},{6,7},{7,6},{8,9},{9,8},{10,11... | collective-permute-start | bytes 1548296 | tf_op jit(solution)/shard_map/ppermute | solution.py:21
  20.3 5.8 %collective-permute-start.5 = (bf16[2016,128]{1,0:T(8,128)(2,1)S(1)}, bf16[2016,128]{1,0:T(8,128)(2,1)S(1)}, u32[]{:S(2)}, u32[]{:S(2)}) collective-permute-start(bf16[2016,128]{1,0:T(8,128)(2,1)S(1)} %collective-permute-done.refs_2_), channel_id=1, source_target_pairs={{0,1},{1,0},{2,3},{3,2},{4,5},{5,4},{6,7},{7,6},{8,9},{9,8},{10,11... | collective-permute-start | bytes 1548296 | tf_op jit(solution)/shard_map/ppermute | solution.py:21
  27.8 6.9 %collective-permute-start.6 = (bf16[288,128]{1,0:T(8,128)(2,1)S(1)}, bf16[288,128]{1,0:T(8,128)(2,1)S(1)}, u32[]{:S(2)}, u32[]{:S(2)}) collective-permute-start(bf16[288,128]{1,0:T(8,128)(2,1)S(1)} %get-tuple-element.62), channel_id=1, source_target_pairs={{0,12},{4,8},{8,4},{12,0},{1,13},{5,9},{9,5},{13,1},{2,14},{6,10},... | collective-permute-start | bytes 221192 | tf_op jit(solution)/shard_map/ppermute | solution.py:21
  30.3 9.0 %collective-permute-start.7 = (bf16[288,128]{1,0:T(8,128)(2,1)S(1)}, bf16[288,128]{1,0:T(8,128)(2,1)S(1)}, u32[]{:S(2)}, u32[]{:S(2)}) collective-permute-start(bf16[288,128]{1,0:T(8,128)(2,1)S(1)} %get-tuple-element.63), channel_id=1, source_target_pairs={{0,8},{4,12},{8,0},{12,4},{1,9},{5,13},{9,1},{13,5},{2,10},{6,14},... | collective-permute-start | bytes 221192 | tf_op jit(solution)/shard_map/ppermute | solution.py:21
  30.3 9.0 %collective-permute-start.8 = (bf16[288,128]{1,0:T(8,128)(2,1)S(1)}, bf16[288,128]{1,0:T(8,128)(2,1)S(1)}, u32[]{:S(2)}, u32[]{:S(2)}) collective-permute-start(bf16[288,128]{1,0:T(8,128)(2,1)S(1)} %get-tuple-element.64), channel_id=1, source_target_pairs={{0,4},{4,0},{8,12},{12,8},{1,5},{5,1},{9,13},{13,9},{2,6},{6,2},{1... | collective-permute-start | bytes 221192 | tf_op jit(solution)/shard_map/ppermute | solution.py:21
  32.2 9.0 %collective-permute-start.12 = (bf16[288,128]{1,0:T(8,128)(2,1)S(1)}, bf16[288,128]{1,0:T(8,128)(2,1)S(1)}, u32[]{:S(2)}, u32[]{:S(2)}) collective-permute-start(bf16[288,128]{1,0:T(8,128)(2,1)S(1)} %get-tuple-element.71), channel_id=1, source_target_pairs={{0,12},{4,8},{8,4},{12,0},{1,13},{5,9},{9,5},{13,1},{2,14},{6,10},... | collective-permute-start | bytes 221192 | tf_op jit(solution)/shard_map/ppermute | solution.py:21
  34.7 7.7 %collective-permute-start.13 = (bf16[288,128]{1,0:T(8,128)(2,1)S(1)}, bf16[288,128]{1,0:T(8,128)(2,1)S(1)}, u32[]{:S(2)}, u32[]{:S(2)}) collective-permute-start(bf16[288,128]{1,0:T(8,128)(2,1)S(1)} %get-tuple-element.72), channel_id=1, source_target_pairs={{0,8},{4,12},{8,0},{12,4},{1,9},{5,13},{9,1},{13,5},{2,10},{6,14},... | collective-permute-start | bytes 221192 | tf_op jit(solution)/shard_map/ppermute | solution.py:21
  34.7 7.7 %collective-permute-start.14 = (bf16[288,128]{1,0:T(8,128)(2,1)S(1)}, bf16[288,128]{1,0:T(8,128)(2,1)S(1)}, u32[]{:S(2)}, u32[]{:S(2)}) collective-permute-start(bf16[288,128]{1,0:T(8,128)(2,1)S(1)} %get-tuple-element.73), channel_id=1, source_target_pairs={{0,4},{4,0},{8,12},{12,8},{1,5},{5,1},{9,13},{13,9},{2,6},{6,2},{1... | collective-permute-start | bytes 221192 | tf_op jit(solution)/shard_map/ppermute | solution.py:21
  39.6 4.7 %collective-permute-start.11 = (bf16[288,128]{1,0:T(8,128)(2,1)S(1)}, bf16[288,128]{1,0:T(8,128)(2,1)S(1)}, u32[]{:S(2)}, u32[]{:S(2)}) collective-permute-start(bf16[288,128]{1,0:T(8,128)(2,1)S(1)} %finish_rows.2.refs_0_), channel_id=1, source_target_pairs={{0,3},{1,2},{2,1},{3,0},{4,7},{5,6},{6,5},{7,4},{8,11},{9,10},{10,... | collective-permute-start | bytes 221192 | tf_op jit(solution)/shard_map/ppermute | solution.py:21
  39.7 6.2 %collective-permute-start.10 = (bf16[288,128]{1,0:T(8,128)(2,1)S(1)}, bf16[288,128]{1,0:T(8,128)(2,1)S(1)}, u32[]{:S(2)}, u32[]{:S(2)}) collective-permute-start(bf16[288,128]{1,0:T(8,128)(2,1)S(1)} %finish_rows.2.refs_0_), channel_id=1, source_target_pairs={{0,2},{1,3},{2,0},{3,1},{4,6},{5,7},{6,4},{7,5},{8,10},{9,11},{10,... | collective-permute-start | bytes 221192 | tf_op jit(solution)/shard_map/ppermute | solution.py:21
  41.2 4.6 %collective-permute-start.9 = (bf16[288,128]{1,0:T(8,128)(2,1)S(1)}, bf16[288,128]{1,0:T(8,128)(2,1)S(1)}, u32[]{:S(2)}, u32[]{:S(2)}) collective-permute-start(bf16[288,128]{1,0:T(8,128)(2,1)S(1)} %finish_rows.2.refs_0_), channel_id=1, source_target_pairs={{0,1},{1,0},{2,3},{3,2},{4,5},{5,4},{6,7},{7,6},{8,9},{9,8},{10,11... | collective-permute-start | bytes 221192 | tf_op jit(solution)/shard_map/ppermute | solution.py:21
  42.7 4.7 %collective-permute-start.17 = (bf16[288,128]{1,0:T(8,128)(2,1)S(1)}, bf16[288,128]{1,0:T(8,128)(2,1)S(1)}, u32[]{:S(2)}, u32[]{:S(2)}) collective-permute-start(bf16[288,128]{1,0:T(8,128)(2,1)S(1)} %finish_rows.3.refs_0_), channel_id=1, source_target_pairs={{0,3},{1,2},{2,1},{3,0},{4,7},{5,6},{6,5},{7,4},{8,11},{9,10},{10,... | collective-permute-start | bytes 221192 | tf_op jit(solution)/shard_map/ppermute | solution.py:21
  42.9 6.1 %collective-permute-start.16 = (bf16[288,128]{1,0:T(8,128)(2,1)S(1)}, bf16[288,128]{1,0:T(8,128)(2,1)S(1)}, u32[]{:S(2)}, u32[]{:S(2)}) collective-permute-start(bf16[288,128]{1,0:T(8,128)(2,1)S(1)} %finish_rows.3.refs_0_), channel_id=1, source_target_pairs={{0,2},{1,3},{2,0},{3,1},{4,6},{5,7},{6,4},{7,5},{8,10},{9,11},{10,... | collective-permute-start | bytes 221192 | tf_op jit(solution)/shard_map/ppermute | solution.py:21
  44.3 4.7 %collective-permute-start.15 = (bf16[288,128]{1,0:T(8,128)(2,1)S(1)}, bf16[288,128]{1,0:T(8,128)(2,1)S(1)}, u32[]{:S(2)}, u32[]{:S(2)}) collective-permute-start(bf16[288,128]{1,0:T(8,128)(2,1)S(1)} %finish_rows.3.refs_0_), channel_id=1, source_target_pairs={{0,1},{1,0},{2,3},{3,2},{4,5},{5,4},{6,7},{7,6},{8,9},{9,8},{10,11... | collective-permute-start | bytes 221192 | tf_op jit(solution)/shard_map/ppermute | solution.py:21
  50.3 6.8 %collective-permute-start.22 = (bf16[16,2560]{1,0:T(8,128)(2,1)S(1)}, bf16[16,2560]{1,0:T(8,128)(2,1)S(1)}, u32[]{:S(2)}, u32[]{:S(2)}) collective-permute-start(bf16[16,2560]{1,0:T(8,128)(2,1)S(1)} %attend.3.refs_0_), channel_id=1, source_target_pairs={{0,8},{4,12},{8,0},{12,4},{1,9},{5,13},{9,1},{13,5},{2,10},{6,14},... | collective-permute-start | bytes 245768 | tf_op jit(solution)/shard_map/ppermute | solution.py:21
  52.0 7.2 %collective-permute-start.19 = (bf16[16,1536]{1,0:T(8,128)(2,1)S(1)}, bf16[16,1536]{1,0:T(8,128)(2,1)S(1)}, u32[]{:S(2)}, u32[]{:S(2)}) collective-permute-start(bf16[16,1536]{1,0:T(8,128)(2,1)S(1)} %attend.2.refs_0_), channel_id=1, source_target_pairs={{0,8},{4,12},{8,0},{12,4},{1,9},{5,13},{9,1},{13,5},{2,10},{6,14},... | collective-permute-start | bytes 147464 | tf_op jit(solution)/shard_map/ppermute | solution.py:21
  54.5 5.5 %collective-permute-start.21 = (bf16[16,2560]{1,0:T(8,128)(2,1)S(1)}, bf16[16,2560]{1,0:T(8,128)(2,1)S(1)}, u32[]{:S(2)}, u32[]{:S(2)}) collective-permute-start(bf16[16,2560]{1,0:T(8,128)(2,1)S(1)} %attend.3.refs_0_), channel_id=1, source_target_pairs={{0,4},{4,0},{8,12},{12,8},{1,5},{5,1},{9,13},{13,9},{2,6},{6,2},{1... | collective-permute-start | bytes 245768 | tf_op jit(solution)/shard_map/ppermute | solution.py:21
  57.1 5.3 %collective-permute-start.23 = (bf16[16,2560]{1,0:T(8,128)(2,1)S(1)}, bf16[16,2560]{1,0:T(8,128)(2,1)S(1)}, u32[]{:S(2)}, u32[]{:S(2)}) collective-permute-start(bf16[16,2560]{1,0:T(8,128)(2,1)S(1)} %collective-permute-done.22.refs_2_), channel_id=1, source_target_pairs={{0,4},{4,0},{8,12},{12,8},{1,5},{5,1},{9,13},{13,9},{2,6},{6,2},{1... | collective-permute-start | bytes 245768 | tf_op jit(solution)/shard_map/ppermute | solution.py:21
  57.1 7.0 %collective-permute-start.18 = (bf16[16,1536]{1,0:T(8,128)(2,1)S(1)}, bf16[16,1536]{1,0:T(8,128)(2,1)S(1)}, u32[]{:S(2)}, u32[]{:S(2)}) collective-permute-start(bf16[16,1536]{1,0:T(8,128)(2,1)S(1)} %attend.2.refs_0_), channel_id=1, source_target_pairs={{0,4},{4,0},{8,12},{12,8},{1,5},{5,1},{9,13},{13,9},{2,6},{6,2},{1... | collective-permute-start | bytes 147464 | tf_op jit(solution)/shard_map/ppermute | solution.py:21
  59.2 5.0 %collective-permute-start.20 = (bf16[16,1536]{1,0:T(8,128)(2,1)S(1)}, bf16[16,1536]{1,0:T(8,128)(2,1)S(1)}, u32[]{:S(2)}, u32[]{:S(2)}) collective-permute-start(bf16[16,1536]{1,0:T(8,128)(2,1)S(1)} %collective-permute-done.19.refs_2_), channel_id=1, source_target_pairs={{0,4},{4,0},{8,12},{12,8},{1,5},{5,1},{9,13},{13,9},{2,6},{6,2},{1... | collective-permute-start | bytes 147464 | tf_op jit(solution)/shard_map/ppermute | solution.py:21
  65.3 3.7 %collective-permute-start.24 = (bf16[16,1792]{1,0:T(8,128)(2,1)S(1)}, bf16[16,1792]{1,0:T(8,128)(2,1)S(1)}, u32[]{:S(2)}, u32[]{:S(2)}) collective-permute-start(bf16[16,1792]{1,0:T(8,128)(2,1)S(1)} %get-tuple-element.76), channel_id=1, source_target_pairs={{0,3},{1,2},{2,1},{3,0},{4,7},{5,6},{6,5},{7,4},{8,11},{9,10},{10,... | collective-permute-start | bytes 172040 | tf_op jit(solution)/shard_map/ppermute | solution.py:21
  65.3 4.8 %collective-permute-start.25 = (bf16[16,1792]{1,0:T(8,128)(2,1)S(1)}, bf16[16,1792]{1,0:T(8,128)(2,1)S(1)}, u32[]{:S(2)}, u32[]{:S(2)}) collective-permute-start(bf16[16,1792]{1,0:T(8,128)(2,1)S(1)} %get-tuple-element.77), channel_id=1, source_target_pairs={{0,2},{1,3},{2,0},{3,1},{4,6},{5,7},{6,4},{7,5},{8,10},{9,11},{10,... | collective-permute-start | bytes 172040 | tf_op jit(solution)/shard_map/ppermute | solution.py:21
  66.3 3.9 %collective-permute-start.26 = (bf16[16,1792]{1,0:T(8,128)(2,1)S(1)}, bf16[16,1792]{1,0:T(8,128)(2,1)S(1)}, u32[]{:S(2)}, u32[]{:S(2)}) collective-permute-start(bf16[16,1792]{1,0:T(8,128)(2,1)S(1)} %get-tuple-element.78), channel_id=1, source_target_pairs={{0,1},{1,0},{2,3},{3,2},{4,5},{5,4},{6,7},{7,6},{8,9},{9,8},{10,11... | collective-permute-start | bytes 172040 | tf_op jit(solution)/shard_map/ppermute | solution.py:21

commit v11 on v10

--- a/solution.py
+++ b/solution.py
@@ -674,21 +674,31 @@
         pieces = [latent_rows] + [swap(latent_rows, "side", k) for k in range(1, side_count)]
         if which == 0:
             state = absorb(layout, which, query_full, row_slot, *state, pieces)
-    product, first_head, head_count = None, 0, value_absorb.shape[0]
-    for part_heads in (head_count * 5 // 8, head_count * 3 // 8):
+    head_count = value_absorb.shape[0]
+    near = head_count * 7 // 16
+    bounds = ((0, near), (near, head_count - near))
+    gathered = []
+    for first_head, part_heads in bounds:
         head_out = attend(
             layout, 1, query_full, row_slot, *state, live, value_here, pieces, first_head,
             part_heads,
         )
+        by_way = [] if first_head else list(range(3, dev_count, 2))
         heads = [head_out] + [None] * (dev_count - 1)
         for k in sorted(range(1, dev_count), reverse=True):
-            if k == 1 or k % 2 == 0:
+            if k not in by_way:
                 heads[k] = swap(head_out, "dev", k)
-        for k in range(3, dev_count, 2):
-            heads[k] = swap(heads[k - 1], "dev", 1)
-        start, first_head = first_head * nope_width, first_head + part_heads
+        gathered.append(heads)
+    gathered[1][0], gathered[0][2::2] = lax.optimization_barrier(
+        (gathered[1][0], gathered[0][2::2])
+    )
+    for k in range(3, dev_count, 2):
+        gathered[0][k] = swap(gathered[0][k - 1], "dev", 1)
+    product = None
+    for heads, (first_head, part_heads) in zip(gathered, bounds):
         products = output_product(
-            heads, out_here, side_count, product, start, first_head == head_count
+            heads, out_here, side_count, product, first_head * nope_width,
+            first_head + part_heads == head_count,
         )
         product = products[0]
     result = products[0]

time: 70.9 us -> 72.4 us (1.021)
  starting transfers between devices: 28.1 us -> 29.5 us
    ppermute x27, starting transfers between devices: 28.1 us -> 29.5 us  [swap(): return lax.ppermute(value, axis, [(i, i ^ step) for i in range(count)])]
  transfers between devices with their start and end apart: 27 -> 27, of which waited for: 12 -> 11; matrix products, arithmetic and copies ran while one was open for 0% -> 0% of each run, Pallas kernels for 18% -> 17%
where the time goes in v11:
time: 72.4 us; the launch traced here: 72.3 us
  starting transfers between devices  29.5 us (41%)
  waiting for transfers between devices  21.6 us (30%)
  Pallas kernels  18 us (25%)
  local copies, waits for them, and re-layouts  2.31 us (3%)
    ppermute x27, starting transfers between devices, swap(): return lax.ppermute(value, axis, [(i, i ^ step) for i in range(count)])  29.5 us
    ppermute x27, waiting for transfers between devices, swap(): return lax.ppermute(value, axis, [(i, i ^ step) for i in range(count)])  21.6 us
    pallas_call x1, Pallas kernels, prepare(): pl.pallas_call(functools.partial(prepare_kernel, scale, steps, (dev_count...  7.61 us
    pallas_call x2, Pallas kernels, output_product(): pl.pallas_call(functools.partial(output_kernel, dev_count, side_count, st...  2.83 us
    pallas_call x2, Pallas kernels, attend(): pl.pallas_call(functools.partial(attend_kernel, layout, which, first_head...  2.48 us
    unnamed x20, local copies, waits for them, and re-layouts  2.31 us
    pallas_call x1, Pallas kernels, project(): pl.pallas_call(functools.partial(project_kernel, dev_count, len(weights))...  1.7 us
  transfers between devices with their start and end apart: 27, of which 11 were waited for; matrix products, arithmetic and copies ran while one was open for 0% of the time, Pallas kernels for 17%

profile of v11, /device:TPU:0, one launch (start us, length us, event | category | flops | bytes accessed | tf_op | source)
XLA Modules:
  0.0 72.3 jit_solution(2639550103184966788)
XLA Ops:
  0.0 1.4 %split_columns.1 = (bf16[64,1792]{1,0:T(8,128)(2,1)S(1)}, bf16[64,1792]{1,0:T(8,128)(2,1)S(1)}, bf16[64,1792]{1,0:T(8,128)(2,1)S(1)}, bf16[64,1792]{1,0:T(8,128)(2,1)S(1)}) custom-call(bf16[64,7168]{1,0:T(8,128)(2,1)} %prompts_ref.1), custom_call_target="tpu_custom_call" | custom-call | flops 10000000000 | bytes 40000000 | tf_op jit(solution)/shard_map/split_columns/pallas_call | solution.py:100
  1.4 5.1 %collective-permute-start.1 = (bf16[64,1792]{1,0:T(8,128)(2,1)S(1)}, bf16[64,1792]{1,0:T(8,128)(2,1)S(1)}, u32[]{:S(2)}, u32[]{:S(2)}) collective-permute-start(bf16[64,1792]{1,0:T(8,128)(2,1)S(1)} %get-tuple-element.58), channel_id=1, source_target_pairs={{0,12},{4,8},{8,4},{12,0},{1,13},{5,9},{9,5},{13,1},{2,14},{6,10},... | collective-permute-start | bytes 688136 | tf_op jit(solution)/shard_map/ppermute | solution.py:21
  6.5 0.6 collective-permute-start.3
  7.2 0.1 pack_weight.1.refs_0_
  7.3 1.7 %collective-permute-start = (bf16[2016,128]{1,0:T(8,128)(2,1)S(1)}, bf16[2016,128]{1,0:T(8,128)(2,1)S(1)}, u32[]{:S(2)}, u32[]{:S(2)}) collective-permute-start(bf16[2016,128]{1,0:T(8,128)(2,1)S(1)} %pack_weight.1.refs_0_), channel_id=1, source_target_pairs={{0,2},{1,3},{2,0},{3,1},{4,6},{5,7},{6,4},{7,5},{8,10},{9,11},{10,... | collective-permute-start | bytes 1548296 | tf_op jit(solution)/shard_map/ppermute | solution.py:21
  9.0 0.3 copy-done.1
  9.3 1.3 %copy-done.2 = bf16[32,512,128]{2,1,0:T(8,128)(2,1)S(1)} copy-done((bf16[32,512,128]{2,1,0:T(8,128)(2,1)S(1)}, bf16[32,512,128]{2,1,0:T(8,128)(2,1)}, u32[]{:S(2)}) %copy-start.2) | copy-done | bytes 4194328
  10.6 0.7 copy-done.3
  11.3 7.6 %prepare.1 = (bf16[512,576]{1,0:T(8,128)(2,1)S(1)}, f32[512,128]{1,0:T(8,128)S(1)}, f32[512,128]{1,0:T(8,128)S(1)}, f32[4,512,128]{2,1,0:T(8,128)S(1)}, f32[16,1...) custom-call(f32[1,32]{1,0:T(1,128)S(1)} %negate_power_fusion.inverse, ...), custom_call_target="tpu_custom_call" | custom-call | flops 40000000000 | bytes 28000000 | tf_op jit(solution)/shard_map/prepare/pallas_call | solution.py:323
  18.9 1.4 %collective-permute-done.refs_2_ = bf16[2016,128]{1,0:T(8,128)(2,1)S(1)} collective-permute-done((bf16[2016,128]{1,0:T(8,128)(2,1)S(1)}, bf16[2016,128]{1,0:T(8,128)(2,1)S(1)}, u32[]{:S(2)}, u32[]{:S(2)}) %collective-permute-start) | collective-permute-done | bytes 516128 | tf_op jit(solution)/shard_map/ppermute | solution.py:21
  20.3 0.5 collective-permute-start.5
  20.8 5.2 %collective-permute-done.2.refs_2_ = bf16[64,1792]{1,0:T(8,128)(2,1)S(1)} collective-permute-done((bf16[64,1792]{1,0:T(8,128)(2,1)S(1)}, bf16[64,1792]{1,0:T(8,128)(2,1)S(1)}, u32[]{:S(2)}, u32[]{:S(2)}) %collective-permute-start.2) | collective-permute-done | bytes 229408 | tf_op jit(solution)/shard_map/ppermute | solution.py:21
  26.1 1.7 %project.1 = (f32[288,128]{1,0:T(8,128)S(1)}, bf16[288,128]{1,0:T(8,128)(2,1)S(1)}, bf16[288,128]{1,0:T(8,128)(2,1)S(1)}, bf16[288,128]{1,0:T(8,128)(2,1)S(1)}, ...) custom-call(s32[1,256]{1,0:T(1,128)S(1)} %get-tuple-element.56.targe, ...), custom_call_target="tpu_custom_call" | custom-call | tf_op jit(solution)/shard_map/project/pallas_call | solution.py:405
  27.8 2.5 %collective-permute-start.6 = (bf16[288,128]{1,0:T(8,128)(2,1)S(1)}, bf16[288,128]{1,0:T(8,128)(2,1)S(1)}, u32[]{:S(2)}, u32[]{:S(2)}) collective-permute-start(bf16[288,128]{1,0:T(8,128)(2,1)S(1)} %get-tuple-element.64), channel_id=1, source_target_pairs={{0,12},{4,8},{8,4},{12,0},{1,13},{5,9},{9,5},{13,1},{2,14},{6,10},... | collective-permute-start | bytes 221192 | tf_op jit(solution)/shard_map/ppermute | solution.py:21
  30.3 1.9 %collective-permute-start.8 = (bf16[288,128]{1,0:T(8,128)(2,1)S(1)}, bf16[288,128]{1,0:T(8,128)(2,1)S(1)}, u32[]{:S(2)}, u32[]{:S(2)}) collective-permute-start(bf16[288,128]{1,0:T(8,128)(2,1)S(1)} %get-tuple-element.66), channel_id=1, source_target_pairs={{0,4},{4,0},{8,12},{12,8},{1,5},{5,1},{9,13},{13,9},{2,6},{6,2},{1... | collective-permute-start | bytes 221192 | tf_op jit(solution)/shard_map/ppermute | solution.py:21
  32.2 2.5 %collective-permute-start.12 = (bf16[288,128]{1,0:T(8,128)(2,1)S(1)}, bf16[288,128]{1,0:T(8,128)(2,1)S(1)}, u32[]{:S(2)}, u32[]{:S(2)}) collective-permute-start(bf16[288,128]{1,0:T(8,128)(2,1)S(1)} %get-tuple-element.73), channel_id=1, source_target_pairs={{0,12},{4,8},{8,4},{12,0},{1,13},{5,9},{9,5},{13,1},{2,14},{6,10},... | collective-permute-start | bytes 221192 | tf_op jit(solution)/shard_map/ppermute | solution.py:21
  34.7 1.9 %collective-permute-start.14 = (bf16[288,128]{1,0:T(8,128)(2,1)S(1)}, bf16[288,128]{1,0:T(8,128)(2,1)S(1)}, u32[]{:S(2)}, u32[]{:S(2)}) collective-permute-start(bf16[288,128]{1,0:T(8,128)(2,1)S(1)} %get-tuple-element.75), channel_id=1, source_target_pairs={{0,4},{4,0},{8,12},{12,8},{1,5},{5,1},{9,13},{13,9},{2,6},{6,2},{1... | collective-permute-start | bytes 221192 | tf_op jit(solution)/shard_map/ppermute | solution.py:21
  36.6 2.7 %collective-permute-done.7.refs_2_ = bf16[288,128]{1,0:T(8,128)(2,1)S(1)} collective-permute-done((bf16[288,128]{1,0:T(8,128)(2,1)S(1)}, bf16[288,128]{1,0:T(8,128)(2,1)S(1)}, u32[]{:S(2)}, u32[]{:S(2)}) %collective-permute-start.7) | collective-permute-done | bytes 73760 | tf_op jit(solution)/shard_map/ppermute | solution.py:21
  39.4 0.2 finish_rows.2.refs_0_
  39.7 1.5 %collective-permute-start.10 = (bf16[288,128]{1,0:T(8,128)(2,1)S(1)}, bf16[288,128]{1,0:T(8,128)(2,1)S(1)}, u32[]{:S(2)}, u32[]{:S(2)}) collective-permute-start(bf16[288,128]{1,0:T(8,128)(2,1)S(1)} %finish_rows.2.refs_0_), channel_id=1, source_target_pairs={{0,2},{1,3},{2,0},{3,1},{4,6},{5,7},{6,4},{7,5},{8,10},{9,11},{10,... | collective-permute-start | bytes 221192 | tf_op jit(solution)/shard_map/ppermute | solution.py:21
  41.2 0.3 collective-permute-start.9
  41.5 0.9 %collective-permute-done.13.refs_2_ = bf16[288,128]{1,0:T(8,128)(2,1)S(1)} collective-permute-done((bf16[288,128]{1,0:T(8,128)(2,1)S(1)}, bf16[288,128]{1,0:T(8,128)(2,1)S(1)}, u32[]{:S(2)}, u32[]{:S(2)}) %collective-permute-start.13) | collective-permute-done | bytes 73760 | tf_op jit(solution)/shard_map/ppermute | solution.py:21
  42.4 0.2 finish_rows.3.refs_0_
  42.7 0.2 collective-permute-start.17
  42.9 1.4 %collective-permute-start.16 = (bf16[288,128]{1,0:T(8,128)(2,1)S(1)}, bf16[288,128]{1,0:T(8,128)(2,1)S(1)}, u32[]{:S(2)}, u32[]{:S(2)}) collective-permute-start(bf16[288,128]{1,0:T(8,128)(2,1)S(1)} %finish_rows.3.refs_0_), channel_id=1, source_target_pairs={{0,2},{1,3},{2,0},{3,1},{4,6},{5,7},{6,4},{7,5},{8,10},{9,11},{10,... | collective-permute-start | bytes 221192 | tf_op jit(solution)/shard_map/ppermute | solution.py:21
  44.3 0.3 collective-permute-start.15
  44.6 1.2 %collective-permute-done.10.refs_2_ = bf16[288,128]{1,0:T(8,128)(2,1)S(1)} collective-permute-done((bf16[288,128]{1,0:T(8,128)(2,1)S(1)}, bf16[288,128]{1,0:T(8,128)(2,1)S(1)}, u32[]{:S(2)}, u32[]{:S(2)}) %collective-permute-start.10) | collective-permute-done | bytes 73760 | tf_op jit(solution)/shard_map/ppermute | solution.py:21
  45.8 1.4 %absorb.1 = (f32[512,128]{1,0:T(8,128)S(1)}, f32[512,128]{1,0:T(8,128)S(1)}, f32[4,512,128]{2,1,0:T(8,128)S(1)}) custom-call(bf16[512,576]{1,0:T(8,128)(2,1)S(1)} %get-tuple-element.47.query_ref, s32[1,512]{1,0:T(1,128)S(1)} %get-tuple-element.48.slot_ref, f32[512,128]{1,0:T(8,128)S(1)} %get-tuple-element.51.top_ref, ...), custom_call_target="tpu_custom_call" | custom-call | flops 2000000000 | bytes 1000000 | tf_op jit(solution)/shard_map/absorb/pallas_call | solution.py:509
  47.3 0.1 collective-permute-done.17.refs_3_
  47.3 1.6 %collective-permute-done.16.refs_2_ = bf16[288,128]{1,0:T(8,128)(2,1)S(1)} collective-permute-done((bf16[288,128]{1,0:T(8,128)(2,1)S(1)}, bf16[288,128]{1,0:T(8,128)(2,1)S(1)}, u32[]{:S(2)}, u32[]{:S(2)}) %collective-permute-start.16) | collective-permute-done | bytes 73760 | tf_op jit(solution)/shard_map/ppermute | solution.py:21
  49.0 1.2 %attend.3.refs_0_ = bf16[16,1792]{1,0:T(8,128)(2,1)S(1)} custom-call(bf16[512,576]{1,0:T(8,128)(2,1)S(1)} %get-tuple-element.47.query_ref, s32[1,512]{1,0:T(1,128)S(1)} %get-tuple-element.48.slot_ref, f32[512,128]{1,0:T(8,128)S(1)} %get-tuple-element.67.top_ref, f32[512,128]{1,0:T(8,128)S(1)} %get-tuple-element.68.sum_ref, ...), custom_call_target="tpu_custom_call" | custom-call | tf_op jit(solution)/shard_map/attend/pallas_call | solution.py:542
  50.2 0.5 collective-permute-start.18
  50.7 1.3 %attend.2.refs_0_ = bf16[16,2304]{1,0:T(8,128)(2,1)S(1)} custom-call(bf16[512,576]{1,0:T(8,128)(2,1)S(1)} %get-tuple-element.47.query_ref, s32[1,512]{1,0:T(1,128)S(1)} %get-tuple-element.48.slot_ref, f32[512,128]{1,0:T(8,128)S(1)} %get-tuple-element.67.top_ref, f32[512,128]{1,0:T(8,128)S(1)} %get-tuple-element.68.sum_ref, ...), custom_call_target="tpu_custom_call" | custom-call | tf_op jit(solution)/shard_map/attend/pallas_call | solution.py:542
  52.0 1.8 %collective-permute-start.21 = (bf16[16,2304]{1,0:T(8,128)(2,1)S(1)}, bf16[16,2304]{1,0:T(8,128)(2,1)S(1)}, u32[]{:S(2)}, u32[]{:S(2)}) collective-permute-start(bf16[16,2304]{1,0:T(8,128)(2,1)S(1)} %attend.2.refs_0_), channel_id=1, source_target_pairs={{0,12},{4,8},{8,4},{12,0},{1,13},{5,9},{9,5},{13,1},{2,14},{6,10},... | collective-permute-start | bytes 221192 | tf_op jit(solution)/shard_map/ppermute | solution.py:21
  53.7 2.0 %collective-permute-start.20 = (bf16[16,2304]{1,0:T(8,128)(2,1)S(1)}, bf16[16,2304]{1,0:T(8,128)(2,1)S(1)}, u32[]{:S(2)}, u32[]{:S(2)}) collective-permute-start(bf16[16,2304]{1,0:T(8,128)(2,1)S(1)} %attend.2.refs_0_), channel_id=1, source_target_pairs={{0,8},{4,12},{8,0},{12,4},{1,9},{5,13},{9,1},{13,5},{2,10},{6,14},... | collective-permute-start | bytes 221192 | tf_op jit(solution)/shard_map/ppermute | solution.py:21
  55.7 0.6 collective-permute-start.19
  56.4 1.4 %collective-permute-start.22 = (bf16[16,1792]{1,0:T(8,128)(2,1)S(1)}, bf16[16,1792]{1,0:T(8,128)(2,1)S(1)}, u32[]{:S(2)}, u32[]{:S(2)}) collective-permute-start(bf16[16,1792]{1,0:T(8,128)(2,1)S(1)} %attend.3.refs_0_), channel_id=1, source_target_pairs={{0,4},{4,0},{8,12},{12,8},{1,5},{5,1},{9,13},{13,9},{2,6},{6,2},{1... | collective-permute-start | bytes 172040 | tf_op jit(solution)/shard_map/ppermute | solution.py:21
  57.8 0.6 collective-permute-start.23
  58.4 4.8 %collective-permute-done.22.refs_1_ = bf16[16,1792]{1,0:T(8,128)(2,1)S(1)} collective-permute-done((bf16[16,1792]{1,0:T(8,128)(2,1)S(1)}, bf16[16,1792]{1,0:T(8,128)(2,1)S(1)}, u32[]{:S(2)}, u32[]{:S(2)}) %collective-permute-start.22) | collective-permute-done | bytes 57376 | tf_op jit(solution)/shard_map/ppermute | solution.py:21
  63.3 0.6 collective-permute-done.23.refs_3_
  63.9 1.2 %output_product.2.refs_5_ = f32[64,1792]{1,0:T(8,128)S(1)} custom-call(bf16[16,1792]{1,0:T(8,128)(2,1)S(1)} %attend.3.refs_0_, bf16[16,1792]{1,0:T(8,128)(2,1)S(1)} %collective-permute-done.22.refs_1_, bf16[16,1792]{1,0:T(8,128)(2,1)S(1)} %collective-permute-done.18.refs_2_, bf16[16,1792]{1,0:T(8,128)(2,1)S(1)} %collective-permute-done.23.refs_3_, ...), custom_call_target="tpu_custom_call" | custom-call | tf_op jit(solution)/shard_map/output_product/pallas_call | solution.py:596
  65.2 1.6 %output_product.3 = (f32[16,1792]{1,0:T(8,128)S(1)}, bf16[16,1792]{1,0:T(8,128)(2,1)S(1)}, bf16[16,1792]{1,0:T(8,128)(2,1)S(1)}, bf16[16,1792]{1,0:T(8,128)(2,1)S(1)}) custom-call(bf16[16,2304]{1,0:T(8,128)(2,1)S(1)} %attend.2.refs_0_, bf16[16,2304]{1,0:T(8,128)(2,1)S(1)} %collective-permute-done.19.refs_1_, ...), custom_call_target="tpu_custom_call" | custom-call | tf_op jit(solution)/shard_map/output_product/pallas_call | solution.py:596
  66.7 0.1 collective-permute-start.24
  66.8 0.9 %collective-permute-start.25 = (bf16[16,1792]{1,0:T(8,128)(2,1)S(1)}, bf16[16,1792]{1,0:T(8,128)(2,1)S(1)}, u32[]{:S(2)}, u32[]{:S(2)}) collective-permute-start(bf16[16,1792]{1,0:T(8,128)(2,1)S(1)} %get-tuple-element.81), channel_id=1, source_target_pairs={{0,2},{1,3},{2,0},{3,1},{4,6},{5,7},{6,4},{7,5},{8,10},{9,11},{10,... | collective-permute-start | bytes 172040 | tf_op jit(solution)/shard_map/ppermute | solution.py:21
  67.8 0.9 %collective-permute-start.26 = (bf16[16,1792]{1,0:T(8,128)(2,1)S(1)}, bf16[16,1792]{1,0:T(8,128)(2,1)S(1)}, u32[]{:S(2)}, u32[]{:S(2)}) collective-permute-start(bf16[16,1792]{1,0:T(8,128)(2,1)S(1)} %get-tuple-element.82), channel_id=1, source_target_pairs={{0,1},{1,0},{2,3},{3,2},{4,5},{5,4},{6,7},{7,6},{8,9},{9,8},{10,11... | collective-permute-start | bytes 172040 | tf_op jit(solution)/shard_map/ppermute | solution.py:21
  68.7 1.9 %collective-permute-done.24 = bf16[16,1792]{1,0:T(8,128)(2,1)S(1)} collective-permute-done((bf16[16,1792]{1,0:T(8,128)(2,1)S(1)}, bf16[16,1792]{1,0:T(8,128)(2,1)S(1)}, u32[]{:S(2)}, u32[]{:S(2)}) %collective-permute-start.24) | collective-permute-done | bytes 57376 | tf_op jit(solution)/shard_map/ppermute | solution.py:21
  70.5 1.1 %collective-permute-done.25 = bf16[16,1792]{1,0:T(8,128)(2,1)S(1)} collective-permute-done((bf16[16,1792]{1,0:T(8,128)(2,1)S(1)}, bf16[16,1792]{1,0:T(8,128)(2,1)S(1)}, u32[]{:S(2)}, u32[]{:S(2)}) %collective-permute-start.25) | collective-permute-done | bytes 57376 | tf_op jit(solution)/shard_map/ppermute | solution.py:21
  71.6 0.7 add_convert_fusion
  (40 shorter events, 0.2 us)
Async XLA Ops:
  0.0 7.1 %copy-start.4 = (bf16[448,576]{1,0:T(8,128)(2,1)S(1)}, bf16[448,576]{1,0:T(8,128)(2,1)}, u32[]{:S(2)}) copy-start(bf16[448,576]{1,0:T(8,128)(2,1)} %value_ref) | copy-start | bytes 1548292
  1.4 19.4 %collective-permute-start.1 = (bf16[64,1792]{1,0:T(8,128)(2,1)S(1)}, bf16[64,1792]{1,0:T(8,128)(2,1)S(1)}, u32[]{:S(2)}, u32[]{:S(2)}) collective-permute-start(bf16[64,1792]{1,0:T(8,128)(2,1)S(1)} %get-tuple-element.58), channel_id=1, source_target_pairs={{0,12},{4,8},{8,4},{12,0},{1,13},{5,9},{9,5},{13,1},{2,14},{6,10},... | collective-permute-start | bytes 688136 | tf_op jit(solution)/shard_map/ppermute | solution.py:21
  6.5 19.5 %collective-permute-start.2 = (bf16[64,1792]{1,0:T(8,128)(2,1)S(1)}, bf16[64,1792]{1,0:T(8,128)(2,1)S(1)}, u32[]{:S(2)}, u32[]{:S(2)}) collective-permute-start(bf16[64,1792]{1,0:T(8,128)(2,1)S(1)} %get-tuple-element.59), channel_id=1, source_target_pairs={{0,8},{4,12},{8,0},{12,4},{1,9},{5,13},{9,1},{13,5},{2,10},{6,14},... | collective-permute-start | bytes 688136 | tf_op jit(solution)/shard_map/ppermute | solution.py:21
  6.5 19.5 %collective-permute-start.3 = (bf16[64,1792]{1,0:T(8,128)(2,1)S(1)}, bf16[64,1792]{1,0:T(8,128)(2,1)S(1)}, u32[]{:S(2)}, u32[]{:S(2)}) collective-permute-start(bf16[64,1792]{1,0:T(8,128)(2,1)S(1)} %get-tuple-element.60), channel_id=1, source_target_pairs={{0,4},{4,0},{8,12},{12,8},{1,5},{5,1},{9,13},{13,9},{2,6},{6,2},{1... | collective-permute-start | bytes 688136 | tf_op jit(solution)/shard_map/ppermute | solution.py:21
  7.1 2.2 %copy-start.1 = (bf16[32,128,512]{2,1,0:T(8,128)(2,1)S(1)}, bf16[32,128,512]{2,1,0:T(8,128)(2,1)}, u32[]{:S(2)}) copy-start(bf16[32,128,512]{2,1,0:T(8,128)(2,1)} %absorb_hbm.1) | copy-start | bytes 12582916
  7.1 3.5 %copy-start.2 = (bf16[32,512,128]{2,1,0:T(8,128)(2,1)S(1)}, bf16[32,512,128]{2,1,0:T(8,128)(2,1)}, u32[]{:S(2)}) copy-start(bf16[32,512,128]{2,1,0:T(8,128)(2,1)} %value_hbm.1) | copy-start | bytes 12582916
  7.1 4.1 %copy-start.3 = (bf16[8,256,576]{1,2,0:T(8,128)(2,1)S(1)}, bf16[8,256,576]{1,2,0:T(8,128)(2,1)}, u32[]{:S(2)}) copy-start(bf16[8,256,576]{1,2,0:T(8,128)(2,1)} %param.18) | copy-start | bytes 7077892
  7.1 4.1 %copy-start.5 = (bf16[8,2,32,192]{3,2,1,0:T(8,128)(2,1)S(1)}, bf16[8,2,32,192]{3,2,1,0:T(8,128)(2,1)}, u32[]{:S(2)}) copy-start(bf16[8,2,32,192]{3,2,1,0:T(8,128)(2,1)} %param.20) | copy-start | bytes 589828
  7.2 4.1 %copy-start.6 = (bf16[8,2,576]{2,1,0:T(2,128)(2,1)S(1)}, bf16[8,2,576]{2,1,0:T(2,128)(2,1)}, u32[]{:S(2)}) copy-start(bf16[8,2,576]{2,1,0:T(2,128)(2,1)} %fresh_hbm.1) | copy-start | bytes 55300
  7.2 4.1 %copy-start.7 = (s32[1024]{0:T(1024)S(1)}, s32[1024]{0:T(1024)}, u32[]{:S(2)}) copy-start(s32[1024]{0:T(1024)} %param.15) | copy-start | bytes 12292
  7.2 4.1 %copy-start.8 = (s32[16]{0:T(128)S(1)}, s32[16]{0:T(128)}, u32[]{:S(2)}) copy-start(s32[16]{0:T(128)} %length_hbm) | copy-start | bytes 196
  7.2 4.1 %copy-start.9 = (s32[16]{0:T(128)S(1)}, s32[16]{0:T(128)}, u32[]{:S(2)}) copy-start(s32[16]{0:T(128)} %slot_hbm.1) | copy-start | bytes 196
  7.3 13.0 %collective-permute-start = (bf16[2016,128]{1,0:T(8,128)(2,1)S(1)}, bf16[2016,128]{1,0:T(8,128)(2,1)S(1)}, u32[]{:S(2)}, u32[]{:S(2)}) collective-permute-start(bf16[2016,128]{1,0:T(8,128)(2,1)S(1)} %pack_weight.1.refs_0_), channel_id=1, source_target_pairs={{0,2},{1,3},{2,0},{3,1},{4,6},{5,7},{6,4},{7,5},{8,10},{9,11},{10,... | collective-permute-start | bytes 1548296 | tf_op jit(solution)/shard_map/ppermute | solution.py:21
  20.3 19.1 %copy-start = (f32[512]{0:T(512)S(1)}, f32[512]{0:T(512)}, u32[]{:S(2)}) copy-start(f32[512]{0:T(512)} %param.14) | copy-start | bytes 6148
  20.3 5.8 %collective-permute-start.4 = (bf16[2016,128]{1,0:T(8,128)(2,1)S(1)}, bf16[2016,128]{1,0:T(8,128)(2,1)S(1)}, u32[]{:S(2)}, u32[]{:S(2)}) collective-permute-start(bf16[2016,128]{1,0:T(8,128)(2,1)S(1)} %pack_weight.1.refs_0_), channel_id=1, source_target_pairs={{0,1},{1,0},{2,3},{3,2},{4,5},{5,4},{6,7},{7,6},{8,9},{9,8},{10,11... | collective-permute-start | bytes 1548296 | tf_op jit(solution)/shard_map/ppermute | solution.py:21
  20.3 5.8 %collective-permute-start.5 = (bf16[2016,128]{1,0:T(8,128)(2,1)S(1)}, bf16[2016,128]{1,0:T(8,128)(2,1)S(1)}, u32[]{:S(2)}, u32[]{:S(2)}) collective-permute-start(bf16[2016,128]{1,0:T(8,128)(2,1)S(1)} %collective-permute-done.refs_2_), channel_id=1, source_target_pairs={{0,1},{1,0},{2,3},{3,2},{4,5},{5,4},{6,7},{7,6},{8,9},{9,8},{10,11... | collective-permute-start | bytes 1548296 | tf_op jit(solution)/shard_map/ppermute | solution.py:21
  27.8 6.9 %collective-permute-start.6 = (bf16[288,128]{1,0:T(8,128)(2,1)S(1)}, bf16[288,128]{1,0:T(8,128)(2,1)S(1)}, u32[]{:S(2)}, u32[]{:S(2)}) collective-permute-start(bf16[288,128]{1,0:T(8,128)(2,1)S(1)} %get-tuple-element.64), channel_id=1, source_target_pairs={{0,12},{4,8},{8,4},{12,0},{1,13},{5,9},{9,5},{13,1},{2,14},{6,10},... | collective-permute-start | bytes 221192 | tf_op jit(solution)/shard_map/ppermute | solution.py:21
  30.3 9.0 %collective-permute-start.7 = (bf16[288,128]{1,0:T(8,128)(2,1)S(1)}, bf16[288,128]{1,0:T(8,128)(2,1)S(1)}, u32[]{:S(2)}, u32[]{:S(2)}) collective-permute-start(bf16[288,128]{1,0:T(8,128)(2,1)S(1)} %get-tuple-element.65), channel_id=1, source_target_pairs={{0,8},{4,12},{8,0},{12,4},{1,9},{5,13},{9,1},{13,5},{2,10},{6,14},... | collective-permute-start | bytes 221192 | tf_op jit(solution)/shard_map/ppermute | solution.py:21
  30.3 9.0 %collective-permute-start.8 = (bf16[288,128]{1,0:T(8,128)(2,1)S(1)}, bf16[288,128]{1,0:T(8,128)(2,1)S(1)}, u32[]{:S(2)}, u32[]{:S(2)}) collective-permute-start(bf16[288,128]{1,0:T(8,128)(2,1)S(1)} %get-tuple-element.66), channel_id=1, source_target_pairs={{0,4},{4,0},{8,12},{12,8},{1,5},{5,1},{9,13},{13,9},{2,6},{6,2},{1... | collective-permute-start | bytes 221192 | tf_op jit(solution)/shard_map/ppermute | solution.py:21
  32.2 9.0 %collective-permute-start.12 = (bf16[288,128]{1,0:T(8,128)(2,1)S(1)}, bf16[288,128]{1,0:T(8,128)(2,1)S(1)}, u32[]{:S(2)}, u32[]{:S(2)}) collective-permute-start(bf16[288,128]{1,0:T(8,128)(2,1)S(1)} %get-tuple-element.73), channel_id=1, source_target_pairs={{0,12},{4,8},{8,4},{12,0},{1,13},{5,9},{9,5},{13,1},{2,14},{6,10},... | collective-permute-start | bytes 221192 | tf_op jit(solution)/shard_map/ppermute | solution.py:21
  34.7 7.7 %collective-permute-start.13 = (bf16[288,128]{1,0:T(8,128)(2,1)S(1)}, bf16[288,128]{1,0:T(8,128)(2,1)S(1)}, u32[]{:S(2)}, u32[]{:S(2)}) collective-permute-start(bf16[288,128]{1,0:T(8,128)(2,1)S(1)} %get-tuple-element.74), channel_id=1, source_target_pairs={{0,8},{4,12},{8,0},{12,4},{1,9},{5,13},{9,1},{13,5},{2,10},{6,14},... | collective-permute-start | bytes 221192 | tf_op jit(solution)/shard_map/ppermute | solution.py:21
  34.7 7.7 %collective-permute-start.14 = (bf16[288,128]{1,0:T(8,128)(2,1)S(1)}, bf16[288,128]{1,0:T(8,128)(2,1)S(1)}, u32[]{:S(2)}, u32[]{:S(2)}) collective-permute-start(bf16[288,128]{1,0:T(8,128)(2,1)S(1)} %get-tuple-element.75), channel_id=1, source_target_pairs={{0,4},{4,0},{8,12},{12,8},{1,5},{5,1},{9,13},{13,9},{2,6},{6,2},{1... | collective-permute-start | bytes 221192 | tf_op jit(solution)/shard_map/ppermute | solution.py:21
  39.6 4.7 %collective-permute-start.11 = (bf16[288,128]{1,0:T(8,128)(2,1)S(1)}, bf16[288,128]{1,0:T(8,128)(2,1)S(1)}, u32[]{:S(2)}, u32[]{:S(2)}) collective-permute-start(bf16[288,128]{1,0:T(8,128)(2,1)S(1)} %finish_rows.2.refs_0_), channel_id=1, source_target_pairs={{0,3},{1,2},{2,1},{3,0},{4,7},{5,6},{6,5},{7,4},{8,11},{9,10},{10,... | collective-permute-start | bytes 221192 | tf_op jit(solution)/shard_map/ppermute | solution.py:21
  39.7 6.2 %collective-permute-start.10 = (bf16[288,128]{1,0:T(8,128)(2,1)S(1)}, bf16[288,128]{1,0:T(8,128)(2,1)S(1)}, u32[]{:S(2)}, u32[]{:S(2)}) collective-permute-start(bf16[288,128]{1,0:T(8,128)(2,1)S(1)} %finish_rows.2.refs_0_), channel_id=1, source_target_pairs={{0,2},{1,3},{2,0},{3,1},{4,6},{5,7},{6,4},{7,5},{8,10},{9,11},{10,... | collective-permute-start | bytes 221192 | tf_op jit(solution)/shard_map/ppermute | solution.py:21
  41.2 4.6 %collective-permute-start.9 = (bf16[288,128]{1,0:T(8,128)(2,1)S(1)}, bf16[288,128]{1,0:T(8,128)(2,1)S(1)}, u32[]{:S(2)}, u32[]{:S(2)}) collective-permute-start(bf16[288,128]{1,0:T(8,128)(2,1)S(1)} %finish_rows.2.refs_0_), channel_id=1, source_target_pairs={{0,1},{1,0},{2,3},{3,2},{4,5},{5,4},{6,7},{7,6},{8,9},{9,8},{10,11... | collective-permute-start | bytes 221192 | tf_op jit(solution)/shard_map/ppermute | solution.py:21
  42.7 4.7 %collective-permute-start.17 = (bf16[288,128]{1,0:T(8,128)(2,1)S(1)}, bf16[288,128]{1,0:T(8,128)(2,1)S(1)}, u32[]{:S(2)}, u32[]{:S(2)}) collective-permute-start(bf16[288,128]{1,0:T(8,128)(2,1)S(1)} %finish_rows.3.refs_0_), channel_id=1, source_target_pairs={{0,3},{1,2},{2,1},{3,0},{4,7},{5,6},{6,5},{7,4},{8,11},{9,10},{10,... | collective-permute-start | bytes 221192 | tf_op jit(solution)/shard_map/ppermute | solution.py:21
  42.9 6.1 %collective-permute-start.16 = (bf16[288,128]{1,0:T(8,128)(2,1)S(1)}, bf16[288,128]{1,0:T(8,128)(2,1)S(1)}, u32[]{:S(2)}, u32[]{:S(2)}) collective-permute-start(bf16[288,128]{1,0:T(8,128)(2,1)S(1)} %finish_rows.3.refs_0_), channel_id=1, source_target_pairs={{0,2},{1,3},{2,0},{3,1},{4,6},{5,7},{6,4},{7,5},{8,10},{9,11},{10,... | collective-permute-start | bytes 221192 | tf_op jit(solution)/shard_map/ppermute | solution.py:21
  44.3 4.7 %collective-permute-start.15 = (bf16[288,128]{1,0:T(8,128)(2,1)S(1)}, bf16[288,128]{1,0:T(8,128)(2,1)S(1)}, u32[]{:S(2)}, u32[]{:S(2)}) collective-permute-start(bf16[288,128]{1,0:T(8,128)(2,1)S(1)} %finish_rows.3.refs_0_), channel_id=1, source_target_pairs={{0,1},{1,0},{2,3},{3,2},{4,5},{5,4},{6,7},{7,6},{8,9},{9,8},{10,11... | collective-permute-start | bytes 221192 | tf_op jit(solution)/shard_map/ppermute | solution.py:21
  50.2 7.6 %collective-permute-start.18 = (bf16[16,1792]{1,0:T(8,128)(2,1)S(1)}, bf16[16,1792]{1,0:T(8,128)(2,1)S(1)}, u32[]{:S(2)}, u32[]{:S(2)}) collective-permute-start(bf16[16,1792]{1,0:T(8,128)(2,1)S(1)} %attend.3.refs_0_), channel_id=1, source_target_pairs={{0,8},{4,12},{8,0},{12,4},{1,9},{5,13},{9,1},{13,5},{2,10},{6,14},... | collective-permute-start | bytes 172040 | tf_op jit(solution)/shard_map/ppermute | solution.py:21
  52.0 13.2 %collective-permute-start.21 = (bf16[16,2304]{1,0:T(8,128)(2,1)S(1)}, bf16[16,2304]{1,0:T(8,128)(2,1)S(1)}, u32[]{:S(2)}, u32[]{:S(2)}) collective-permute-start(bf16[16,2304]{1,0:T(8,128)(2,1)S(1)} %attend.2.refs_0_), channel_id=1, source_target_pairs={{0,12},{4,8},{8,4},{12,0},{1,13},{5,9},{9,5},{13,1},{2,14},{6,10},... | collective-permute-start | bytes 221192 | tf_op jit(solution)/shard_map/ppermute | solution.py:21
  53.7 11.4 %collective-permute-start.20 = (bf16[16,2304]{1,0:T(8,128)(2,1)S(1)}, bf16[16,2304]{1,0:T(8,128)(2,1)S(1)}, u32[]{:S(2)}, u32[]{:S(2)}) collective-permute-start(bf16[16,2304]{1,0:T(8,128)(2,1)S(1)} %attend.2.refs_0_), channel_id=1, source_target_pairs={{0,8},{4,12},{8,0},{12,4},{1,9},{5,13},{9,1},{13,5},{2,10},{6,14},... | collective-permute-start | bytes 221192 | tf_op jit(solution)/shard_map/ppermute | solution.py:21
  55.7 9.4 %collective-permute-start.19 = (bf16[16,2304]{1,0:T(8,128)(2,1)S(1)}, bf16[16,2304]{1,0:T(8,128)(2,1)S(1)}, u32[]{:S(2)}, u32[]{:S(2)}) collective-permute-start(bf16[16,2304]{1,0:T(8,128)(2,1)S(1)} %attend.2.refs_0_), channel_id=1, source_target_pairs={{0,4},{4,0},{8,12},{12,8},{1,5},{5,1},{9,13},{13,9},{2,6},{6,2},{1... | collective-permute-start | bytes 221192 | tf_op jit(solution)/shard_map/ppermute | solution.py:21
  56.4 6.9 %collective-permute-start.22 = (bf16[16,1792]{1,0:T(8,128)(2,1)S(1)}, bf16[16,1792]{1,0:T(8,128)(2,1)S(1)}, u32[]{:S(2)}, u32[]{:S(2)}) collective-permute-start(bf16[16,1792]{1,0:T(8,128)(2,1)S(1)} %attend.3.refs_0_), channel_id=1, source_target_pairs={{0,4},{4,0},{8,12},{12,8},{1,5},{5,1},{9,13},{13,9},{2,6},{6,2},{1... | collective-permute-start | bytes 172040 | tf_op jit(solution)/shard_map/ppermute | solution.py:21
  57.8 6.1 %collective-permute-start.23 = (bf16[16,1792]{1,0:T(8,128)(2,1)S(1)}, bf16[16,1792]{1,0:T(8,128)(2,1)S(1)}, u32[]{:S(2)}, u32[]{:S(2)}) collective-permute-start(bf16[16,1792]{1,0:T(8,128)(2,1)S(1)} %collective-permute-done.18.refs_2_), channel_id=1, source_target_pairs={{0,4},{4,0},{8,12},{12,8},{1,5},{5,1},{9,13},{13,9},{2,6},{6,2},{1... | collective-permute-start | bytes 172040 | tf_op jit(solution)/shard_map/ppermute | solution.py:21
  66.7 3.8 %collective-permute-start.24 = (bf16[16,1792]{1,0:T(8,128)(2,1)S(1)}, bf16[16,1792]{1,0:T(8,128)(2,1)S(1)}, u32[]{:S(2)}, u32[]{:S(2)}) collective-permute-start(bf16[16,1792]{1,0:T(8,128)(2,1)S(1)} %get-tuple-element.80), channel_id=1, source_target_pairs={{0,3},{1,2},{2,1},{3,0},{4,7},{5,6},{6,5},{7,4},{8,11},{9,10},{10,... | collective-permute-start | bytes 172040 | tf_op jit(solution)/shard_map/ppermute | solution.py:21
  66.8 4.8 %collective-permute-start.25 = (bf16[16,1792]{1,0:T(8,128)(2,1)S(1)}, bf16[16,1792]{1,0:T(8,128)(2,1)S(1)}, u32[]{:S(2)}, u32[]{:S(2)}) collective-permute-start(bf16[16,1792]{1,0:T(8,128)(2,1)S(1)} %get-tuple-element.81), channel_id=1, source_target_pairs={{0,2},{1,3},{2,0},{3,1},{4,6},{5,7},{6,4},{7,5},{8,10},{9,11},{10,... | collective-permute-start | bytes 172040 | tf_op jit(solution)/shard_map/ppermute | solution.py:21
  67.8 3.9 %collective-permute-start.26 = (bf16[16,1792]{1,0:T(8,128)(2,1)S(1)}, bf16[16,1792]{1,0:T(8,128)(2,1)S(1)}, u32[]{:S(2)}, u32[]{:S(2)}) collective-permute-start(bf16[16,1792]{1,0:T(8,128)(2,1)S(1)} %get-tuple-element.82), channel_id=1, source_target_pairs={{0,1},{1,0},{2,3},{3,2},{4,5},{5,4},{6,7},{7,6},{8,9},{9,8},{10,11... | collective-permute-start | bytes 172040 | tf_op jit(solution)/shard_map/ppermute | solution.py:21

commit v12 on v10

--- a/solution.py
+++ b/solution.py
@@ -453,9 +453,13 @@
     )(gain, cosine, sine, *parts)
 
 
+def piece_order(count):
+    return [0, 1, *range(3, count, 2), *range(2, count, 2)]
+
+
 def take_keys(keys, pieces, lat_width):
     rows = keys.shape[0] // len(pieces)
-    for n, piece in enumerate(pieces):
+    for n, piece in zip(piece_order(len(pieces)), pieces):
         tiles, rest = load_packed(piece, rows)
         there = slice(n * rows, (n + 1) * rows)
         for j, tile in enumerate(tiles):
@@ -671,21 +675,20 @@
         for k in sorted(range(1, dev_count), reverse=True):
             half[k] = swap(half[k], "dev", k)
         latent_rows = finish(half[:1] + half[:0:-1], latent_gain.reshape(1, -1), cosine, sine, which)
-        pieces = [latent_rows] + [swap(latent_rows, "side", k) for k in range(1, side_count)]
+        pieces = [
+            swap(latent_rows, "side", k) if k else latent_rows for k in piece_order(side_count)
+        ]
         if which == 0:
             state = absorb(layout, which, query_full, row_slot, *state, pieces)
     product, first_head, head_count = None, 0, value_absorb.shape[0]
-    for part_heads in (head_count * 5 // 8, head_count * 3 // 8):
+    for part_heads in (head_count * 3 // 4, head_count // 4):
         head_out = attend(
             layout, 1, query_full, row_slot, *state, live, value_here, pieces, first_head,
             part_heads,
         )
         heads = [head_out] + [None] * (dev_count - 1)
         for k in sorted(range(1, dev_count), reverse=True):
-            if k == 1 or k % 2 == 0:
-                heads[k] = swap(head_out, "dev", k)
-        for k in range(3, dev_count, 2):
-            heads[k] = swap(heads[k - 1], "dev", 1)
+            heads[k] = swap(head_out, "dev", k)
         start, first_head = first_head * nope_width, first_head + part_heads
         products = output_product(
             heads, out_here, side_count, product, start, first_head == head_count

time: 70.9 us -> 71.4 us (level)
  starting transfers between devices: 28.1 us -> 32 us
  waiting for transfers between devices: 21.6 us -> 17.9 us
    ppermute x27, starting transfers between devices: 28.1 us -> 32 us  [swap(): return lax.ppermute(value, axis, [(i, i ^ step) for i in range(count)])]
    ppermute x27, waiting for transfers between devices: 21.6 us -> 17.9 us  [swap(): return lax.ppermute(value, axis, [(i, i ^ step) for i in range(count)])]
  transfers between devices with their start and end apart: 27 -> 27, of which waited for: 12 -> 10; matrix products, arithmetic and copies ran while one was open for 0% -> 0% of each run, Pallas kernels for 18% -> 18%
where the time goes in v12:
time: 71.4 us; the launch traced here: 71.2 us
  starting transfers between devices  32 us (45%)
  Pallas kernels  18.2 us (25%)
  waiting for transfers between devices  17.9 us (25%)
  local copies, waits for them, and re-layouts  2.31 us (3%)
    ppermute x27, starting transfers between devices, swap(): return lax.ppermute(value, axis, [(i, i ^ step) for i in range(count)])  32 us
    ppermute x27, waiting for transfers between devices, swap(): return lax.ppermute(value, axis, [(i, i ^ step) for i in range(count)])  17.9 us
    pallas_call x1, Pallas kernels, prepare(): pl.pallas_call(functools.partial(prepare_kernel, scale, steps, (dev_count...  7.61 us
    pallas_call x2, Pallas kernels, output_product(): pl.pallas_call(functools.partial(output_kernel, dev_count, side_count, st...  2.84 us
    pallas_call x2, Pallas kernels, attend(): pl.pallas_call(functools.partial(attend_kernel, layout, which, first_head...  2.69 us
    unnamed x20, local copies, waits for them, and re-layouts  2.31 us
    pallas_call x1, Pallas kernels, project(): pl.pallas_call(functools.partial(project_kernel, dev_count, len(weights))...  1.7 us
    pallas_call x1, Pallas kernels, absorb(): pl.pallas_call(functools.partial(absorb_kernel, layout, which), out_shape...  1.44 us
  transfers between devices with their start and end apart: 27, of which 10 were waited for; matrix products, arithmetic and copies ran while one was open for 0% of the time, Pallas kernels for 18%

profile of v12, /device:TPU:0, one launch (start us, length us, event | category | flops | bytes accessed | tf_op | source)
XLA Modules:
  0.0 71.2 jit_solution(16377789620062810498)
XLA Ops:
  0.0 1.4 %split_columns.1 = (bf16[64,1792]{1,0:T(8,128)(2,1)S(1)}, bf16[64,1792]{1,0:T(8,128)(2,1)S(1)}, bf16[64,1792]{1,0:T(8,128)(2,1)S(1)}, bf16[64,1792]{1,0:T(8,128)(2,1)S(1)}) custom-call(bf16[64,7168]{1,0:T(8,128)(2,1)} %prompts_ref.1), custom_call_target="tpu_custom_call" | custom-call | flops 10000000000 | bytes 40000000 | tf_op jit(solution)/shard_map/split_columns/pallas_call | solution.py:100
  1.4 5.1 %collective-permute-start.1 = (bf16[64,1792]{1,0:T(8,128)(2,1)S(1)}, bf16[64,1792]{1,0:T(8,128)(2,1)S(1)}, u32[]{:S(2)}, u32[]{:S(2)}) collective-permute-start(bf16[64,1792]{1,0:T(8,128)(2,1)S(1)} %get-tuple-element.56), channel_id=1, source_target_pairs={{0,12},{4,8},{8,4},{12,0},{1,13},{5,9},{9,5},{13,1},{2,14},{6,10},... | collective-permute-start | bytes 688136 | tf_op jit(solution)/shard_map/ppermute | solution.py:21
  6.5 0.6 collective-permute-start.3
  7.1 0.0 copy-start.5
  7.2 0.0 copy-start.6
  7.2 0.0 copy-start.7
  7.2 0.1 pack_weight.1.refs_0_
  7.3 1.7 %collective-permute-start = (bf16[2016,128]{1,0:T(8,128)(2,1)S(1)}, bf16[2016,128]{1,0:T(8,128)(2,1)S(1)}, u32[]{:S(2)}, u32[]{:S(2)}) collective-permute-start(bf16[2016,128]{1,0:T(8,128)(2,1)S(1)} %pack_weight.1.refs_0_), channel_id=1, source_target_pairs={{0,2},{1,3},{2,0},{3,1},{4,6},{5,7},{6,4},{7,5},{8,10},{9,11},{10,... | collective-permute-start | bytes 1548296 | tf_op jit(solution)/shard_map/ppermute | solution.py:21
  9.0 0.3 copy-done.1
  9.3 1.3 %copy-done.2 = bf16[32,512,128]{2,1,0:T(8,128)(2,1)S(1)} copy-done((bf16[32,512,128]{2,1,0:T(8,128)(2,1)S(1)}, bf16[32,512,128]{2,1,0:T(8,128)(2,1)}, u32[]{:S(2)}) %copy-start.2) | copy-done | bytes 4194328
  10.6 0.7 copy-done.3
  11.3 7.6 %prepare.1 = (bf16[512,576]{1,0:T(8,128)(2,1)S(1)}, f32[512,128]{1,0:T(8,128)S(1)}, f32[512,128]{1,0:T(8,128)S(1)}, f32[4,512,128]{2,1,0:T(8,128)S(1)}, f32[16,1...) custom-call(f32[1,32]{1,0:T(1,128)S(1)} %negate_power_fusion.inverse, ...), custom_call_target="tpu_custom_call" | custom-call | flops 40000000000 | bytes 28000000 | tf_op jit(solution)/shard_map/prepare/pallas_call | solution.py:323
  18.9 1.4 %collective-permute-done.refs_2_ = bf16[2016,128]{1,0:T(8,128)(2,1)S(1)} collective-permute-done((bf16[2016,128]{1,0:T(8,128)(2,1)S(1)}, bf16[2016,128]{1,0:T(8,128)(2,1)S(1)}, u32[]{:S(2)}, u32[]{:S(2)}) %collective-permute-start) | collective-permute-done | bytes 516128 | tf_op jit(solution)/shard_map/ppermute | solution.py:21
  20.3 0.5 collective-permute-start.5
  20.8 5.2 %collective-permute-done.2.refs_2_ = bf16[64,1792]{1,0:T(8,128)(2,1)S(1)} collective-permute-done((bf16[64,1792]{1,0:T(8,128)(2,1)S(1)}, bf16[64,1792]{1,0:T(8,128)(2,1)S(1)}, u32[]{:S(2)}, u32[]{:S(2)}) %collective-permute-start.2) | collective-permute-done | bytes 229408 | tf_op jit(solution)/shard_map/ppermute | solution.py:21
  26.0 0.1 stack_rows.1.x_ref
  26.1 1.7 %project.1 = (f32[288,128]{1,0:T(8,128)S(1)}, bf16[288,128]{1,0:T(8,128)(2,1)S(1)}, bf16[288,128]{1,0:T(8,128)(2,1)S(1)}, bf16[288,128]{1,0:T(8,128)(2,1)S(1)}, ...) custom-call(s32[1,256]{1,0:T(1,128)S(1)} %get-tuple-element.54.targe, ...), custom_call_target="tpu_custom_call" | custom-call | tf_op jit(solution)/shard_map/project/pallas_call | solution.py:405
  27.8 2.5 %collective-permute-start.6 = (bf16[288,128]{1,0:T(8,128)(2,1)S(1)}, bf16[288,128]{1,0:T(8,128)(2,1)S(1)}, u32[]{:S(2)}, u32[]{:S(2)}) collective-permute-start(bf16[288,128]{1,0:T(8,128)(2,1)S(1)} %get-tuple-element.62), channel_id=1, source_target_pairs={{0,12},{4,8},{8,4},{12,0},{1,13},{5,9},{9,5},{13,1},{2,14},{6,10},... | collective-permute-start | bytes 221192 | tf_op jit(solution)/shard_map/ppermute | solution.py:21
  30.3 1.9 %collective-permute-start.8 = (bf16[288,128]{1,0:T(8,128)(2,1)S(1)}, bf16[288,128]{1,0:T(8,128)(2,1)S(1)}, u32[]{:S(2)}, u32[]{:S(2)}) collective-permute-start(bf16[288,128]{1,0:T(8,128)(2,1)S(1)} %get-tuple-element.64), channel_id=1, source_target_pairs={{0,4},{4,0},{8,12},{12,8},{1,5},{5,1},{9,13},{13,9},{2,6},{6,2},{1... | collective-permute-start | bytes 221192 | tf_op jit(solution)/shard_map/ppermute | solution.py:21
  32.2 2.5 %collective-permute-start.12 = (bf16[288,128]{1,0:T(8,128)(2,1)S(1)}, bf16[288,128]{1,0:T(8,128)(2,1)S(1)}, u32[]{:S(2)}, u32[]{:S(2)}) collective-permute-start(bf16[288,128]{1,0:T(8,128)(2,1)S(1)} %get-tuple-element.71), channel_id=1, source_target_pairs={{0,12},{4,8},{8,4},{12,0},{1,13},{5,9},{9,5},{13,1},{2,14},{6,10},... | collective-permute-start | bytes 221192 | tf_op jit(solution)/shard_map/ppermute | solution.py:21
  34.7 1.9 %collective-permute-start.14 = (bf16[288,128]{1,0:T(8,128)(2,1)S(1)}, bf16[288,128]{1,0:T(8,128)(2,1)S(1)}, u32[]{:S(2)}, u32[]{:S(2)}) collective-permute-start(bf16[288,128]{1,0:T(8,128)(2,1)S(1)} %get-tuple-element.73), channel_id=1, source_target_pairs={{0,4},{4,0},{8,12},{12,8},{1,5},{5,1},{9,13},{13,9},{2,6},{6,2},{1... | collective-permute-start | bytes 221192 | tf_op jit(solution)/shard_map/ppermute | solution.py:21
  36.6 2.7 %collective-permute-done.7.refs_2_ = bf16[288,128]{1,0:T(8,128)(2,1)S(1)} collective-permute-done((bf16[288,128]{1,0:T(8,128)(2,1)S(1)}, bf16[288,128]{1,0:T(8,128)(2,1)S(1)}, u32[]{:S(2)}, u32[]{:S(2)}) %collective-permute-start.7) | collective-permute-done | bytes 73760 | tf_op jit(solution)/shard_map/ppermute | solution.py:21
  39.4 0.2 finish_rows.2.refs_0_
  39.6 1.5 %collective-permute-start.11 = (bf16[288,128]{1,0:T(8,128)(2,1)S(1)}, bf16[288,128]{1,0:T(8,128)(2,1)S(1)}, u32[]{:S(2)}, u32[]{:S(2)}) collective-permute-start(bf16[288,128]{1,0:T(8,128)(2,1)S(1)} %finish_rows.2.refs_0_), channel_id=1, source_target_pairs={{0,2},{1,3},{2,0},{3,1},{4,6},{5,7},{6,4},{7,5},{8,10},{9,11},{10,... | collective-permute-start | bytes 221192 | tf_op jit(solution)/shard_map/ppermute | solution.py:21
  41.1 0.7 collective-permute-start.9
  41.8 0.7 collective-permute-done.13.refs_2_
  42.4 0.2 finish_rows.3.refs_0_
  42.7 1.5 %collective-permute-start.17 = (bf16[288,128]{1,0:T(8,128)(2,1)S(1)}, bf16[288,128]{1,0:T(8,128)(2,1)S(1)}, u32[]{:S(2)}, u32[]{:S(2)}) collective-permute-start(bf16[288,128]{1,0:T(8,128)(2,1)S(1)} %finish_rows.3.refs_0_), channel_id=1, source_target_pairs={{0,2},{1,3},{2,0},{3,1},{4,6},{5,7},{6,4},{7,5},{8,10},{9,11},{10,... | collective-permute-start | bytes 221192 | tf_op jit(solution)/shard_map/ppermute | solution.py:21
  44.2 0.6 collective-permute-start.15
  44.9 0.7 collective-permute-done.10.refs_2_
  45.6 1.4 %absorb.1 = (f32[512,128]{1,0:T(8,128)S(1)}, f32[512,128]{1,0:T(8,128)S(1)}, f32[4,512,128]{2,1,0:T(8,128)S(1)}) custom-call(bf16[512,576]{1,0:T(8,128)(2,1)S(1)} %get-tuple-element.45.query_ref, s32[1,512]{1,0:T(1,128)S(1)} %get-tuple-element.46.slot_ref, f32[512,128]{1,0:T(8,128)S(1)} %get-tuple-element.49.top_ref, ...), custom_call_target="tpu_custom_call" | custom-call | flops 2000000000 | bytes 1000000 | tf_op jit(solution)/shard_map/absorb/pallas_call | solution.py:513
  47.0 0.1 collective-permute-done.17.refs_3_
  47.2 1.6 %collective-permute-done.16.refs_2_ = bf16[288,128]{1,0:T(8,128)(2,1)S(1)} collective-permute-done((bf16[288,128]{1,0:T(8,128)(2,1)S(1)}, bf16[288,128]{1,0:T(8,128)(2,1)S(1)}, u32[]{:S(2)}, u32[]{:S(2)}) %collective-permute-start.16) | collective-permute-done | bytes 73760 | tf_op jit(solution)/shard_map/ppermute | solution.py:21
  48.7 1.7 %attend.3.refs_0_ = bf16[16,3072]{1,0:T(8,128)(2,1)S(1)} custom-call(bf16[512,576]{1,0:T(8,128)(2,1)S(1)} %get-tuple-element.45.query_ref, s32[1,512]{1,0:T(1,128)S(1)} %get-tuple-element.46.slot_ref, f32[512,128]{1,0:T(8,128)S(1)} %get-tuple-element.65.top_ref, f32[512,128]{1,0:T(8,128)S(1)} %get-tuple-element.66.sum_ref, ...), custom_call_target="tpu_custom_call" | custom-call | tf_op jit(solution)/shard_map/attend/pallas_call | solution.py:546
  50.4 2.2 %collective-permute-start.23 = (bf16[16,3072]{1,0:T(8,128)(2,1)S(1)}, bf16[16,3072]{1,0:T(8,128)(2,1)S(1)}, u32[]{:S(2)}, u32[]{:S(2)}) collective-permute-start(bf16[16,3072]{1,0:T(8,128)(2,1)S(1)} %attend.3.refs_0_), channel_id=1, source_target_pairs={{0,12},{4,8},{8,4},{12,0},{1,13},{5,9},{9,5},{13,1},{2,14},{6,10},... | collective-permute-start | bytes 294920 | tf_op jit(solution)/shard_map/ppermute | solution.py:21
  52.7 2.2 %collective-permute-start.21 = (bf16[16,3072]{1,0:T(8,128)(2,1)S(1)}, bf16[16,3072]{1,0:T(8,128)(2,1)S(1)}, u32[]{:S(2)}, u32[]{:S(2)}) collective-permute-start(bf16[16,3072]{1,0:T(8,128)(2,1)S(1)} %attend.3.refs_0_), channel_id=1, source_target_pairs={{0,4},{4,0},{8,12},{12,8},{1,5},{5,1},{9,13},{13,9},{2,6},{6,2},{1... | collective-permute-start | bytes 294920 | tf_op jit(solution)/shard_map/ppermute | solution.py:21
  54.8 1.0 %attend.2.refs_0_ = bf16[16,1024]{1,0:T(8,128)(2,1)S(1)} custom-call(bf16[512,576]{1,0:T(8,128)(2,1)S(1)} %get-tuple-element.45.query_ref, s32[1,512]{1,0:T(1,128)S(1)} %get-tuple-element.46.slot_ref, f32[512,128]{1,0:T(8,128)S(1)} %get-tuple-element.65.top_ref, f32[512,128]{1,0:T(8,128)S(1)} %get-tuple-element.66.sum_ref, ...), custom_call_target="tpu_custom_call" | custom-call | tf_op jit(solution)/shard_map/attend/pallas_call | solution.py:546
  55.9 2.2 %collective-permute-start.20 = (bf16[16,1024]{1,0:T(8,128)(2,1)S(1)}, bf16[16,1024]{1,0:T(8,128)(2,1)S(1)}, u32[]{:S(2)}, u32[]{:S(2)}) collective-permute-start(bf16[16,1024]{1,0:T(8,128)(2,1)S(1)} %attend.2.refs_0_), channel_id=1, source_target_pairs={{0,12},{4,8},{8,4},{12,0},{1,13},{5,9},{9,5},{13,1},{2,14},{6,10},... | collective-permute-start | bytes 98312 | tf_op jit(solution)/shard_map/ppermute | solution.py:21
  58.1 2.2 %collective-permute-start.18 = (bf16[16,1024]{1,0:T(8,128)(2,1)S(1)}, bf16[16,1024]{1,0:T(8,128)(2,1)S(1)}, u32[]{:S(2)}, u32[]{:S(2)}) collective-permute-start(bf16[16,1024]{1,0:T(8,128)(2,1)S(1)} %attend.2.refs_0_), channel_id=1, source_target_pairs={{0,4},{4,0},{8,12},{12,8},{1,5},{5,1},{9,13},{13,9},{2,6},{6,2},{1... | collective-permute-start | bytes 98312 | tf_op jit(solution)/shard_map/ppermute | solution.py:21
  60.3 1.7 %collective-permute-done.22.refs_2_ = bf16[16,3072]{1,0:T(8,128)(2,1)S(1)} collective-permute-done((bf16[16,3072]{1,0:T(8,128)(2,1)S(1)}, bf16[16,3072]{1,0:T(8,128)(2,1)S(1)}, u32[]{:S(2)}, u32[]{:S(2)}) %collective-permute-start.22) | collective-permute-done | bytes 98336 | tf_op jit(solution)/shard_map/ppermute | solution.py:21
  62.0 2.1 %output_product.2.refs_5_ = f32[64,1792]{1,0:T(8,128)S(1)} custom-call(bf16[16,3072]{1,0:T(8,128)(2,1)S(1)} %attend.3.refs_0_, bf16[16,3072]{1,0:T(8,128)(2,1)S(1)} %collective-permute-done.21.refs_1_, bf16[16,3072]{1,0:T(8,128)(2,1)S(1)} %collective-permute-done.22.refs_2_, bf16[16,3072]{1,0:T(8,128)(2,1)S(1)} %collective-permute-done.23.refs_3_, ...), custom_call_target="tpu_custom_call" | custom-call | tf_op jit(solution)/shard_map/output_product/pallas_call | solution.py:600
  64.1 0.8 %output_product.3 = (f32[16,1792]{1,0:T(8,128)S(1)}, bf16[16,1792]{1,0:T(8,128)(2,1)S(1)}, bf16[16,1792]{1,0:T(8,128)(2,1)S(1)}, bf16[16,1792]{1,0:T(8,128)(2,1)S(1)}) custom-call(bf16[16,1024]{1,0:T(8,128)(2,1)S(1)} %attend.2.refs_0_, bf16[16,1024]{1,0:T(8,128)(2,1)S(1)} %collective-permute-done.18.refs_1_, ...), custom_call_target="tpu_custom_call" | custom-call | tf_op jit(solution)/shard_map/output_product/pallas_call | solution.py:600
  64.9 0.9 %collective-permute-start.24 = (bf16[16,1792]{1,0:T(8,128)(2,1)S(1)}, bf16[16,1792]{1,0:T(8,128)(2,1)S(1)}, u32[]{:S(2)}, u32[]{:S(2)}) collective-permute-start(bf16[16,1792]{1,0:T(8,128)(2,1)S(1)} %get-tuple-element.76), channel_id=1, source_target_pairs={{0,3},{1,2},{2,1},{3,0},{4,7},{5,6},{6,5},{7,4},{8,11},{9,10},{10,... | collective-permute-start | bytes 172040 | tf_op jit(solution)/shard_map/ppermute | solution.py:21
  65.8 0.9 %collective-permute-start.25 = (bf16[16,1792]{1,0:T(8,128)(2,1)S(1)}, bf16[16,1792]{1,0:T(8,128)(2,1)S(1)}, u32[]{:S(2)}, u32[]{:S(2)}) collective-permute-start(bf16[16,1792]{1,0:T(8,128)(2,1)S(1)} %get-tuple-element.77), channel_id=1, source_target_pairs={{0,2},{1,3},{2,0},{3,1},{4,6},{5,7},{6,4},{7,5},{8,10},{9,11},{10,... | collective-permute-start | bytes 172040 | tf_op jit(solution)/shard_map/ppermute | solution.py:21
  66.7 0.2 collective-permute-start.26
  66.8 2.2 %collective-permute-done.24 = bf16[16,1792]{1,0:T(8,128)(2,1)S(1)} collective-permute-done((bf16[16,1792]{1,0:T(8,128)(2,1)S(1)}, bf16[16,1792]{1,0:T(8,128)(2,1)S(1)}, u32[]{:S(2)}, u32[]{:S(2)}) %collective-permute-start.24) | collective-permute-done | bytes 57376 | tf_op jit(solution)/shard_map/ppermute | solution.py:21
  69.0 1.5 %collective-permute-done.25 = bf16[16,1792]{1,0:T(8,128)(2,1)S(1)} collective-permute-done((bf16[16,1792]{1,0:T(8,128)(2,1)S(1)}, bf16[16,1792]{1,0:T(8,128)(2,1)S(1)}, u32[]{:S(2)}, u32[]{:S(2)}) %collective-permute-start.25) | collective-permute-done | bytes 57376 | tf_op jit(solution)/shard_map/ppermute | solution.py:21
  70.6 0.7 add_convert_fusion
  (40 shorter events, 0.1 us)
Async XLA Ops:
  0.0 7.1 %copy-start.4 = (bf16[448,576]{1,0:T(8,128)(2,1)S(1)}, bf16[448,576]{1,0:T(8,128)(2,1)}, u32[]{:S(2)}) copy-start(bf16[448,576]{1,0:T(8,128)(2,1)} %value_ref) | copy-start | bytes 1548292
  1.4 19.4 %collective-permute-start.1 = (bf16[64,1792]{1,0:T(8,128)(2,1)S(1)}, bf16[64,1792]{1,0:T(8,128)(2,1)S(1)}, u32[]{:S(2)}, u32[]{:S(2)}) collective-permute-start(bf16[64,1792]{1,0:T(8,128)(2,1)S(1)} %get-tuple-element.56), channel_id=1, source_target_pairs={{0,12},{4,8},{8,4},{12,0},{1,13},{5,9},{9,5},{13,1},{2,14},{6,10},... | collective-permute-start | bytes 688136 | tf_op jit(solution)/shard_map/ppermute | solution.py:21
  6.5 19.5 %collective-permute-start.2 = (bf16[64,1792]{1,0:T(8,128)(2,1)S(1)}, bf16[64,1792]{1,0:T(8,128)(2,1)S(1)}, u32[]{:S(2)}, u32[]{:S(2)}) collective-permute-start(bf16[64,1792]{1,0:T(8,128)(2,1)S(1)} %get-tuple-element.57), channel_id=1, source_target_pairs={{0,8},{4,12},{8,0},{12,4},{1,9},{5,13},{9,1},{13,5},{2,10},{6,14},... | collective-permute-start | bytes 688136 | tf_op jit(solution)/shard_map/ppermute | solution.py:21
  6.5 19.5 %collective-permute-start.3 = (bf16[64,1792]{1,0:T(8,128)(2,1)S(1)}, bf16[64,1792]{1,0:T(8,128)(2,1)S(1)}, u32[]{:S(2)}, u32[]{:S(2)}) collective-permute-start(bf16[64,1792]{1,0:T(8,128)(2,1)S(1)} %get-tuple-element.58), channel_id=1, source_target_pairs={{0,4},{4,0},{8,12},{12,8},{1,5},{5,1},{9,13},{13,9},{2,6},{6,2},{1... | collective-permute-start | bytes 688136 | tf_op jit(solution)/shard_map/ppermute | solution.py:21
  7.1 2.2 %copy-start.1 = (bf16[32,128,512]{2,1,0:T(8,128)(2,1)S(1)}, bf16[32,128,512]{2,1,0:T(8,128)(2,1)}, u32[]{:S(2)}) copy-start(bf16[32,128,512]{2,1,0:T(8,128)(2,1)} %absorb_hbm.1) | copy-start | bytes 12582916
  7.1 3.5 %copy-start.2 = (bf16[32,512,128]{2,1,0:T(8,128)(2,1)S(1)}, bf16[32,512,128]{2,1,0:T(8,128)(2,1)}, u32[]{:S(2)}) copy-start(bf16[32,512,128]{2,1,0:T(8,128)(2,1)} %value_hbm.1) | copy-start | bytes 12582916
  7.1 4.1 %copy-start.3 = (bf16[8,256,576]{1,2,0:T(8,128)(2,1)S(1)}, bf16[8,256,576]{1,2,0:T(8,128)(2,1)}, u32[]{:S(2)}) copy-start(bf16[8,256,576]{1,2,0:T(8,128)(2,1)} %param.18) | copy-start | bytes 7077892
  7.1 4.1 %copy-start.5 = (bf16[8,2,32,192]{3,2,1,0:T(8,128)(2,1)S(1)}, bf16[8,2,32,192]{3,2,1,0:T(8,128)(2,1)}, u32[]{:S(2)}) copy-start(bf16[8,2,32,192]{3,2,1,0:T(8,128)(2,1)} %param.20) | copy-start | bytes 589828
  7.2 4.1 %copy-start.6 = (bf16[8,2,576]{2,1,0:T(2,128)(2,1)S(1)}, bf16[8,2,576]{2,1,0:T(2,128)(2,1)}, u32[]{:S(2)}) copy-start(bf16[8,2,576]{2,1,0:T(2,128)(2,1)} %fresh_hbm.1) | copy-start | bytes 55300
  7.2 4.1 %copy-start.7 = (s32[1024]{0:T(1024)S(1)}, s32[1024]{0:T(1024)}, u32[]{:S(2)}) copy-start(s32[1024]{0:T(1024)} %param.15) | copy-start | bytes 12292
  7.2 4.1 %copy-start.8 = (s32[16]{0:T(128)S(1)}, s32[16]{0:T(128)}, u32[]{:S(2)}) copy-start(s32[16]{0:T(128)} %length_hbm) | copy-start | bytes 196
  7.2 4.1 %copy-start.9 = (s32[16]{0:T(128)S(1)}, s32[16]{0:T(128)}, u32[]{:S(2)}) copy-start(s32[16]{0:T(128)} %slot_hbm.1) | copy-start | bytes 196
  7.3 13.0 %collective-permute-start = (bf16[2016,128]{1,0:T(8,128)(2,1)S(1)}, bf16[2016,128]{1,0:T(8,128)(2,1)S(1)}, u32[]{:S(2)}, u32[]{:S(2)}) collective-permute-start(bf16[2016,128]{1,0:T(8,128)(2,1)S(1)} %pack_weight.1.refs_0_), channel_id=1, source_target_pairs={{0,2},{1,3},{2,0},{3,1},{4,6},{5,7},{6,4},{7,5},{8,10},{9,11},{10,... | collective-permute-start | bytes 1548296 | tf_op jit(solution)/shard_map/ppermute | solution.py:21
  20.3 19.1 %copy-start = (f32[512]{0:T(512)S(1)}, f32[512]{0:T(512)}, u32[]{:S(2)}) copy-start(f32[512]{0:T(512)} %param.14) | copy-start | bytes 6148
  20.3 5.8 %collective-permute-start.4 = (bf16[2016,128]{1,0:T(8,128)(2,1)S(1)}, bf16[2016,128]{1,0:T(8,128)(2,1)S(1)}, u32[]{:S(2)}, u32[]{:S(2)}) collective-permute-start(bf16[2016,128]{1,0:T(8,128)(2,1)S(1)} %pack_weight.1.refs_0_), channel_id=1, source_target_pairs={{0,1},{1,0},{2,3},{3,2},{4,5},{5,4},{6,7},{7,6},{8,9},{9,8},{10,11... | collective-permute-start | bytes 1548296 | tf_op jit(solution)/shard_map/ppermute | solution.py:21
  20.3 5.8 %collective-permute-start.5 = (bf16[2016,128]{1,0:T(8,128)(2,1)S(1)}, bf16[2016,128]{1,0:T(8,128)(2,1)S(1)}, u32[]{:S(2)}, u32[]{:S(2)}) collective-permute-start(bf16[2016,128]{1,0:T(8,128)(2,1)S(1)} %collective-permute-done.refs_2_), channel_id=1, source_target_pairs={{0,1},{1,0},{2,3},{3,2},{4,5},{5,4},{6,7},{7,6},{8,9},{9,8},{10,11... | collective-permute-start | bytes 1548296 | tf_op jit(solution)/shard_map/ppermute | solution.py:21
  27.8 6.9 %collective-permute-start.6 = (bf16[288,128]{1,0:T(8,128)(2,1)S(1)}, bf16[288,128]{1,0:T(8,128)(2,1)S(1)}, u32[]{:S(2)}, u32[]{:S(2)}) collective-permute-start(bf16[288,128]{1,0:T(8,128)(2,1)S(1)} %get-tuple-element.62), channel_id=1, source_target_pairs={{0,12},{4,8},{8,4},{12,0},{1,13},{5,9},{9,5},{13,1},{2,14},{6,10},... | collective-permute-start | bytes 221192 | tf_op jit(solution)/shard_map/ppermute | solution.py:21
  30.3 9.0 %collective-permute-start.7 = (bf16[288,128]{1,0:T(8,128)(2,1)S(1)}, bf16[288,128]{1,0:T(8,128)(2,1)S(1)}, u32[]{:S(2)}, u32[]{:S(2)}) collective-permute-start(bf16[288,128]{1,0:T(8,128)(2,1)S(1)} %get-tuple-element.63), channel_id=1, source_target_pairs={{0,8},{4,12},{8,0},{12,4},{1,9},{5,13},{9,1},{13,5},{2,10},{6,14},... | collective-permute-start | bytes 221192 | tf_op jit(solution)/shard_map/ppermute | solution.py:21
  30.3 9.0 %collective-permute-start.8 = (bf16[288,128]{1,0:T(8,128)(2,1)S(1)}, bf16[288,128]{1,0:T(8,128)(2,1)S(1)}, u32[]{:S(2)}, u32[]{:S(2)}) collective-permute-start(bf16[288,128]{1,0:T(8,128)(2,1)S(1)} %get-tuple-element.64), channel_id=1, source_target_pairs={{0,4},{4,0},{8,12},{12,8},{1,5},{5,1},{9,13},{13,9},{2,6},{6,2},{1... | collective-permute-start | bytes 221192 | tf_op jit(solution)/shard_map/ppermute | solution.py:21
  32.2 8.9 %collective-permute-start.12 = (bf16[288,128]{1,0:T(8,128)(2,1)S(1)}, bf16[288,128]{1,0:T(8,128)(2,1)S(1)}, u32[]{:S(2)}, u32[]{:S(2)}) collective-permute-start(bf16[288,128]{1,0:T(8,128)(2,1)S(1)} %get-tuple-element.71), channel_id=1, source_target_pairs={{0,12},{4,8},{8,4},{12,0},{1,13},{5,9},{9,5},{13,1},{2,14},{6,10},... | collective-permute-start | bytes 221192 | tf_op jit(solution)/shard_map/ppermute | solution.py:21
  34.7 7.7 %collective-permute-start.13 = (bf16[288,128]{1,0:T(8,128)(2,1)S(1)}, bf16[288,128]{1,0:T(8,128)(2,1)S(1)}, u32[]{:S(2)}, u32[]{:S(2)}) collective-permute-start(bf16[288,128]{1,0:T(8,128)(2,1)S(1)} %get-tuple-element.72), channel_id=1, source_target_pairs={{0,8},{4,12},{8,0},{12,4},{1,9},{5,13},{9,1},{13,5},{2,10},{6,14},... | collective-permute-start | bytes 221192 | tf_op jit(solution)/shard_map/ppermute | solution.py:21
  34.7 7.7 %collective-permute-start.14 = (bf16[288,128]{1,0:T(8,128)(2,1)S(1)}, bf16[288,128]{1,0:T(8,128)(2,1)S(1)}, u32[]{:S(2)}, u32[]{:S(2)}) collective-permute-start(bf16[288,128]{1,0:T(8,128)(2,1)S(1)} %get-tuple-element.73), channel_id=1, source_target_pairs={{0,4},{4,0},{8,12},{12,8},{1,5},{5,1},{9,13},{13,9},{2,6},{6,2},{1... | collective-permute-start | bytes 221192 | tf_op jit(solution)/shard_map/ppermute | solution.py:21
  39.6 4.6 %collective-permute-start.11 = (bf16[288,128]{1,0:T(8,128)(2,1)S(1)}, bf16[288,128]{1,0:T(8,128)(2,1)S(1)}, u32[]{:S(2)}, u32[]{:S(2)}) collective-permute-start(bf16[288,128]{1,0:T(8,128)(2,1)S(1)} %finish_rows.2.refs_0_), channel_id=1, source_target_pairs={{0,2},{1,3},{2,0},{3,1},{4,6},{5,7},{6,4},{7,5},{8,10},{9,11},{10,... | collective-permute-start | bytes 221192 | tf_op jit(solution)/shard_map/ppermute | solution.py:21
  41.1 4.5 %collective-permute-start.10 = (bf16[288,128]{1,0:T(8,128)(2,1)S(1)}, bf16[288,128]{1,0:T(8,128)(2,1)S(1)}, u32[]{:S(2)}, u32[]{:S(2)}) collective-permute-start(bf16[288,128]{1,0:T(8,128)(2,1)S(1)} %finish_rows.2.refs_0_), channel_id=1, source_target_pairs={{0,3},{1,2},{2,1},{3,0},{4,7},{5,6},{6,5},{7,4},{8,11},{9,10},{10,... | collective-permute-start | bytes 221192 | tf_op jit(solution)/shard_map/ppermute | solution.py:21
  41.1 4.4 %collective-permute-start.9 = (bf16[288,128]{1,0:T(8,128)(2,1)S(1)}, bf16[288,128]{1,0:T(8,128)(2,1)S(1)}, u32[]{:S(2)}, u32[]{:S(2)}) collective-permute-start(bf16[288,128]{1,0:T(8,128)(2,1)S(1)} %finish_rows.2.refs_0_), channel_id=1, source_target_pairs={{0,1},{1,0},{2,3},{3,2},{4,5},{5,4},{6,7},{7,6},{8,9},{9,8},{10,11... | collective-permute-start | bytes 221192 | tf_op jit(solution)/shard_map/ppermute | solution.py:21
  42.7 4.5 %collective-permute-start.17 = (bf16[288,128]{1,0:T(8,128)(2,1)S(1)}, bf16[288,128]{1,0:T(8,128)(2,1)S(1)}, u32[]{:S(2)}, u32[]{:S(2)}) collective-permute-start(bf16[288,128]{1,0:T(8,128)(2,1)S(1)} %finish_rows.3.refs_0_), channel_id=1, source_target_pairs={{0,2},{1,3},{2,0},{3,1},{4,6},{5,7},{6,4},{7,5},{8,10},{9,11},{10,... | collective-permute-start | bytes 221192 | tf_op jit(solution)/shard_map/ppermute | solution.py:21
  44.2 4.5 %collective-permute-start.16 = (bf16[288,128]{1,0:T(8,128)(2,1)S(1)}, bf16[288,128]{1,0:T(8,128)(2,1)S(1)}, u32[]{:S(2)}, u32[]{:S(2)}) collective-permute-start(bf16[288,128]{1,0:T(8,128)(2,1)S(1)} %finish_rows.3.refs_0_), channel_id=1, source_target_pairs={{0,3},{1,2},{2,1},{3,0},{4,7},{5,6},{6,5},{7,4},{8,11},{9,10},{10,... | collective-permute-start | bytes 221192 | tf_op jit(solution)/shard_map/ppermute | solution.py:21
  44.2 4.5 %collective-permute-start.15 = (bf16[288,128]{1,0:T(8,128)(2,1)S(1)}, bf16[288,128]{1,0:T(8,128)(2,1)S(1)}, u32[]{:S(2)}, u32[]{:S(2)}) collective-permute-start(bf16[288,128]{1,0:T(8,128)(2,1)S(1)} %finish_rows.3.refs_0_), channel_id=1, source_target_pairs={{0,1},{1,0},{2,3},{3,2},{4,5},{5,4},{6,7},{7,6},{8,9},{9,8},{10,11... | collective-permute-start | bytes 221192 | tf_op jit(solution)/shard_map/ppermute | solution.py:21
  50.4 7.7 %collective-permute-start.23 = (bf16[16,3072]{1,0:T(8,128)(2,1)S(1)}, bf16[16,3072]{1,0:T(8,128)(2,1)S(1)}, u32[]{:S(2)}, u32[]{:S(2)}) collective-permute-start(bf16[16,3072]{1,0:T(8,128)(2,1)S(1)} %attend.3.refs_0_), channel_id=1, source_target_pairs={{0,12},{4,8},{8,4},{12,0},{1,13},{5,9},{9,5},{13,1},{2,14},{6,10},... | collective-permute-start | bytes 294920 | tf_op jit(solution)/shard_map/ppermute | solution.py:21
  52.7 9.4 %collective-permute-start.22 = (bf16[16,3072]{1,0:T(8,128)(2,1)S(1)}, bf16[16,3072]{1,0:T(8,128)(2,1)S(1)}, u32[]{:S(2)}, u32[]{:S(2)}) collective-permute-start(bf16[16,3072]{1,0:T(8,128)(2,1)S(1)} %attend.3.refs_0_), channel_id=1, source_target_pairs={{0,8},{4,12},{8,0},{12,4},{1,9},{5,13},{9,1},{13,5},{2,10},{6,14},... | collective-permute-start | bytes 294920 | tf_op jit(solution)/shard_map/ppermute | solution.py:21
  52.7 9.4 %collective-permute-start.21 = (bf16[16,3072]{1,0:T(8,128)(2,1)S(1)}, bf16[16,3072]{1,0:T(8,128)(2,1)S(1)}, u32[]{:S(2)}, u32[]{:S(2)}) collective-permute-start(bf16[16,3072]{1,0:T(8,128)(2,1)S(1)} %attend.3.refs_0_), channel_id=1, source_target_pairs={{0,4},{4,0},{8,12},{12,8},{1,5},{5,1},{9,13},{13,9},{2,6},{6,2},{1... | collective-permute-start | bytes 294920 | tf_op jit(solution)/shard_map/ppermute | solution.py:21
  55.9 8.2 %collective-permute-start.20 = (bf16[16,1024]{1,0:T(8,128)(2,1)S(1)}, bf16[16,1024]{1,0:T(8,128)(2,1)S(1)}, u32[]{:S(2)}, u32[]{:S(2)}) collective-permute-start(bf16[16,1024]{1,0:T(8,128)(2,1)S(1)} %attend.2.refs_0_), channel_id=1, source_target_pairs={{0,12},{4,8},{8,4},{12,0},{1,13},{5,9},{9,5},{13,1},{2,14},{6,10},... | collective-permute-start | bytes 98312 | tf_op jit(solution)/shard_map/ppermute | solution.py:21
  58.1 6.0 %collective-permute-start.19 = (bf16[16,1024]{1,0:T(8,128)(2,1)S(1)}, bf16[16,1024]{1,0:T(8,128)(2,1)S(1)}, u32[]{:S(2)}, u32[]{:S(2)}) collective-permute-start(bf16[16,1024]{1,0:T(8,128)(2,1)S(1)} %attend.2.refs_0_), channel_id=1, source_target_pairs={{0,8},{4,12},{8,0},{12,4},{1,9},{5,13},{9,1},{13,5},{2,10},{6,14},... | collective-permute-start | bytes 98312 | tf_op jit(solution)/shard_map/ppermute | solution.py:21
  58.1 6.0 %collective-permute-start.18 = (bf16[16,1024]{1,0:T(8,128)(2,1)S(1)}, bf16[16,1024]{1,0:T(8,128)(2,1)S(1)}, u32[]{:S(2)}, u32[]{:S(2)}) collective-permute-start(bf16[16,1024]{1,0:T(8,128)(2,1)S(1)} %attend.2.refs_0_), channel_id=1, source_target_pairs={{0,4},{4,0},{8,12},{12,8},{1,5},{5,1},{9,13},{13,9},{2,6},{6,2},{1... | collective-permute-start | bytes 98312 | tf_op jit(solution)/shard_map/ppermute | solution.py:21
  64.9 4.1 %collective-permute-start.24 = (bf16[16,1792]{1,0:T(8,128)(2,1)S(1)}, bf16[16,1792]{1,0:T(8,128)(2,1)S(1)}, u32[]{:S(2)}, u32[]{:S(2)}) collective-permute-start(bf16[16,1792]{1,0:T(8,128)(2,1)S(1)} %get-tuple-element.76), channel_id=1, source_target_pairs={{0,3},{1,2},{2,1},{3,0},{4,7},{5,6},{6,5},{7,4},{8,11},{9,10},{10,... | collective-permute-start | bytes 172040 | tf_op jit(solution)/shard_map/ppermute | solution.py:21
  65.8 4.8 %collective-permute-start.25 = (bf16[16,1792]{1,0:T(8,128)(2,1)S(1)}, bf16[16,1792]{1,0:T(8,128)(2,1)S(1)}, u32[]{:S(2)}, u32[]{:S(2)}) collective-permute-start(bf16[16,1792]{1,0:T(8,128)(2,1)S(1)} %get-tuple-element.77), channel_id=1, source_target_pairs={{0,2},{1,3},{2,0},{3,1},{4,6},{5,7},{6,4},{7,5},{8,10},{9,11},{10,... | collective-permute-start | bytes 172040 | tf_op jit(solution)/shard_map/ppermute | solution.py:21
  66.7 3.9 %collective-permute-start.26 = (bf16[16,1792]{1,0:T(8,128)(2,1)S(1)}, bf16[16,1792]{1,0:T(8,128)(2,1)S(1)}, u32[]{:S(2)}, u32[]{:S(2)}) collective-permute-start(bf16[16,1792]{1,0:T(8,128)(2,1)S(1)} %get-tuple-element.78), channel_id=1, source_target_pairs={{0,1},{1,0},{2,3},{3,2},{4,5},{5,4},{6,7},{7,6},{8,9},{9,8},{10,11... | collective-permute-start | bytes 172040 | tf_op jit(solution)/shard_map/ppermute | solution.py:21

commit v13 on v12

--- a/solution.py
+++ b/solution.py
@@ -681,14 +681,17 @@
         if which == 0:
             state = absorb(layout, which, query_full, row_slot, *state, pieces)
     product, first_head, head_count = None, 0, value_absorb.shape[0]
-    for part_heads in (head_count * 3 // 4, head_count // 4):
+    for part_heads in (head_count * 9 // 16, head_count * 7 // 16):
         head_out = attend(
             layout, 1, query_full, row_slot, *state, live, value_here, pieces, first_head,
             part_heads,
         )
         heads = [head_out] + [None] * (dev_count - 1)
         for k in sorted(range(1, dev_count), reverse=True):
-            heads[k] = swap(head_out, "dev", k)
+            if k == 1 or k % 2 == 0:
+                heads[k] = swap(head_out, "dev", k)
+        for k in range(3, dev_count, 2):
+            heads[k] = swap(heads[k - 1], "dev", 1)
         start, first_head = first_head * nope_width, first_head + part_heads
         products = output_product(
             heads, out_here, side_count, product, start, first_head == head_count

time: 71.4 us -> 70.4 us (0.986)
  starting transfers between devices: 32 us -> 29.1 us
  waiting for transfers between devices: 17.9 us -> 20.1 us
    ppermute x27, starting transfers between devices: 32 us -> 29.1 us  [swap(): return lax.ppermute(value, axis, [(i, i ^ step) for i in range(count)])]
    ppermute x27, waiting for transfers between devices: 17.9 us -> 20.1 us  [swap(): return lax.ppermute(value, axis, [(i, i ^ step) for i in range(count)])]
  transfers between devices with their start and end apart: 27 -> 27, of which waited for: 10 -> 11; matrix products, arithmetic and copies ran while one was open for 0% -> 0% of each run, Pallas kernels for 18% -> 18%
where the time goes in v13:
time: 70.4 us; the launch traced here: 70.3 us
  starting transfers between devices  29.1 us (41%)
  waiting for transfers between devices  20.1 us (29%)
  Pallas kernels  18 us (26%)
  local copies, waits for them, and re-layouts  2.31 us (3%)
    ppermute x27, starting transfers between devices, swap(): return lax.ppermute(value, axis, [(i, i ^ step) for i in range(count)])  29.1 us
    ppermute x27, waiting for transfers between devices, swap(): return lax.ppermute(value, axis, [(i, i ^ step) for i in range(count)])  20.1 us
    pallas_call x1, Pallas kernels, prepare(): pl.pallas_call(functools.partial(prepare_kernel, scale, steps, (dev_count...  7.61 us
    pallas_call x2, Pallas kernels, output_product(): pl.pallas_call(functools.partial(output_kernel, dev_count, side_count, st...  2.81 us
    pallas_call x2, Pallas kernels, attend(): pl.pallas_call(functools.partial(attend_kernel, layout, which, first_head...  2.48 us
    unnamed x20, local copies, waits for them, and re-layouts  2.31 us
    pallas_call x1, Pallas kernels, project(): pl.pallas_call(functools.partial(project_kernel, dev_count, len(weights))...  1.7 us
    pallas_call x1, Pallas kernels, absorb(): pl.pallas_call(functools.partial(absorb_kernel, layout, which), out_shape...  1.44 us
  transfers between devices with their start and end apart: 27, of which 11 were waited for; matrix products, arithmetic and copies ran while one was open for 0% of the time, Pallas kernels for 18%

profile of v13, /device:TPU:0, one launch (start us, length us, event | category | flops | bytes accessed | tf_op | source)
XLA Modules:
  0.0 70.3 jit_solution(4250412549637124813)
XLA Ops:
  0.0 1.4 %split_columns.1 = (bf16[64,1792]{1,0:T(8,128)(2,1)S(1)}, bf16[64,1792]{1,0:T(8,128)(2,1)S(1)}, bf16[64,1792]{1,0:T(8,128)(2,1)S(1)}, bf16[64,1792]{1,0:T(8,128)(2,1)S(1)}) custom-call(bf16[64,7168]{1,0:T(8,128)(2,1)} %prompts_ref.1), custom_call_target="tpu_custom_call" | custom-call | flops 10000000000 | bytes 40000000 | tf_op jit(solution)/shard_map/split_columns/pallas_call | solution.py:100
  1.4 5.1 %collective-permute-start.1 = (bf16[64,1792]{1,0:T(8,128)(2,1)S(1)}, bf16[64,1792]{1,0:T(8,128)(2,1)S(1)}, u32[]{:S(2)}, u32[]{:S(2)}) collective-permute-start(bf16[64,1792]{1,0:T(8,128)(2,1)S(1)} %get-tuple-element.56), channel_id=1, source_target_pairs={{0,12},{4,8},{8,4},{12,0},{1,13},{5,9},{9,5},{13,1},{2,14},{6,10},... | collective-permute-start | bytes 688136 | tf_op jit(solution)/shard_map/ppermute | solution.py:21
  6.5 0.6 collective-permute-start.3
  7.2 0.1 pack_weight.1.refs_0_
  7.3 1.7 %collective-permute-start = (bf16[2016,128]{1,0:T(8,128)(2,1)S(1)}, bf16[2016,128]{1,0:T(8,128)(2,1)S(1)}, u32[]{:S(2)}, u32[]{:S(2)}) collective-permute-start(bf16[2016,128]{1,0:T(8,128)(2,1)S(1)} %pack_weight.1.refs_0_), channel_id=1, source_target_pairs={{0,2},{1,3},{2,0},{3,1},{4,6},{5,7},{6,4},{7,5},{8,10},{9,11},{10,... | collective-permute-start | bytes 1548296 | tf_op jit(solution)/shard_map/ppermute | solution.py:21
  9.0 0.3 copy-done.1
  9.3 1.3 %copy-done.2 = bf16[32,512,128]{2,1,0:T(8,128)(2,1)S(1)} copy-done((bf16[32,512,128]{2,1,0:T(8,128)(2,1)S(1)}, bf16[32,512,128]{2,1,0:T(8,128)(2,1)}, u32[]{:S(2)}) %copy-start.2) | copy-done | bytes 4194328
  10.6 0.7 copy-done.3
  11.3 7.6 %prepare.1 = (bf16[512,576]{1,0:T(8,128)(2,1)S(1)}, f32[512,128]{1,0:T(8,128)S(1)}, f32[512,128]{1,0:T(8,128)S(1)}, f32[4,512,128]{2,1,0:T(8,128)S(1)}, f32[16,1...) custom-call(f32[1,32]{1,0:T(1,128)S(1)} %negate_power_fusion.inverse, ...), custom_call_target="tpu_custom_call" | custom-call | flops 40000000000 | bytes 28000000 | tf_op jit(solution)/shard_map/prepare/pallas_call | solution.py:323
  18.9 1.4 %collective-permute-done.refs_2_ = bf16[2016,128]{1,0:T(8,128)(2,1)S(1)} collective-permute-done((bf16[2016,128]{1,0:T(8,128)(2,1)S(1)}, bf16[2016,128]{1,0:T(8,128)(2,1)S(1)}, u32[]{:S(2)}, u32[]{:S(2)}) %collective-permute-start) | collective-permute-done | bytes 516128 | tf_op jit(solution)/shard_map/ppermute | solution.py:21
  20.3 0.5 collective-permute-start.5
  20.8 5.2 %collective-permute-done.2.refs_2_ = bf16[64,1792]{1,0:T(8,128)(2,1)S(1)} collective-permute-done((bf16[64,1792]{1,0:T(8,128)(2,1)S(1)}, bf16[64,1792]{1,0:T(8,128)(2,1)S(1)}, u32[]{:S(2)}, u32[]{:S(2)}) %collective-permute-start.2) | collective-permute-done | bytes 229408 | tf_op jit(solution)/shard_map/ppermute | solution.py:21
  26.0 0.1 stack_rows.1.x_ref
  26.1 1.7 %project.1 = (f32[288,128]{1,0:T(8,128)S(1)}, bf16[288,128]{1,0:T(8,128)(2,1)S(1)}, bf16[288,128]{1,0:T(8,128)(2,1)S(1)}, bf16[288,128]{1,0:T(8,128)(2,1)S(1)}, ...) custom-call(s32[1,256]{1,0:T(1,128)S(1)} %get-tuple-element.54.targe, ...), custom_call_target="tpu_custom_call" | custom-call | tf_op jit(solution)/shard_map/project/pallas_call | solution.py:405
  27.8 2.5 %collective-permute-start.6 = (bf16[288,128]{1,0:T(8,128)(2,1)S(1)}, bf16[288,128]{1,0:T(8,128)(2,1)S(1)}, u32[]{:S(2)}, u32[]{:S(2)}) collective-permute-start(bf16[288,128]{1,0:T(8,128)(2,1)S(1)} %get-tuple-element.62), channel_id=1, source_target_pairs={{0,12},{4,8},{8,4},{12,0},{1,13},{5,9},{9,5},{13,1},{2,14},{6,10},... | collective-permute-start | bytes 221192 | tf_op jit(solution)/shard_map/ppermute | solution.py:21
  30.3 1.9 %collective-permute-start.8 = (bf16[288,128]{1,0:T(8,128)(2,1)S(1)}, bf16[288,128]{1,0:T(8,128)(2,1)S(1)}, u32[]{:S(2)}, u32[]{:S(2)}) collective-permute-start(bf16[288,128]{1,0:T(8,128)(2,1)S(1)} %get-tuple-element.64), channel_id=1, source_target_pairs={{0,4},{4,0},{8,12},{12,8},{1,5},{5,1},{9,13},{13,9},{2,6},{6,2},{1... | collective-permute-start | bytes 221192 | tf_op jit(solution)/shard_map/ppermute | solution.py:21
  32.2 2.5 %collective-permute-start.12 = (bf16[288,128]{1,0:T(8,128)(2,1)S(1)}, bf16[288,128]{1,0:T(8,128)(2,1)S(1)}, u32[]{:S(2)}, u32[]{:S(2)}) collective-permute-start(bf16[288,128]{1,0:T(8,128)(2,1)S(1)} %get-tuple-element.71), channel_id=1, source_target_pairs={{0,12},{4,8},{8,4},{12,0},{1,13},{5,9},{9,5},{13,1},{2,14},{6,10},... | collective-permute-start | bytes 221192 | tf_op jit(solution)/shard_map/ppermute | solution.py:21
  34.7 1.9 %collective-permute-start.14 = (bf16[288,128]{1,0:T(8,128)(2,1)S(1)}, bf16[288,128]{1,0:T(8,128)(2,1)S(1)}, u32[]{:S(2)}, u32[]{:S(2)}) collective-permute-start(bf16[288,128]{1,0:T(8,128)(2,1)S(1)} %get-tuple-element.73), channel_id=1, source_target_pairs={{0,4},{4,0},{8,12},{12,8},{1,5},{5,1},{9,13},{13,9},{2,6},{6,2},{1... | collective-permute-start | bytes 221192 | tf_op jit(solution)/shard_map/ppermute | solution.py:21
  36.6 2.7 %collective-permute-done.7.refs_2_ = bf16[288,128]{1,0:T(8,128)(2,1)S(1)} collective-permute-done((bf16[288,128]{1,0:T(8,128)(2,1)S(1)}, bf16[288,128]{1,0:T(8,128)(2,1)S(1)}, u32[]{:S(2)}, u32[]{:S(2)}) %collective-permute-start.7) | collective-permute-done | bytes 73760 | tf_op jit(solution)/shard_map/ppermute | solution.py:21
  39.4 0.2 finish_rows.2.refs_0_
  39.6 1.5 %collective-permute-start.11 = (bf16[288,128]{1,0:T(8,128)(2,1)S(1)}, bf16[288,128]{1,0:T(8,128)(2,1)S(1)}, u32[]{:S(2)}, u32[]{:S(2)}) collective-permute-start(bf16[288,128]{1,0:T(8,128)(2,1)S(1)} %finish_rows.2.refs_0_), channel_id=1, source_target_pairs={{0,2},{1,3},{2,0},{3,1},{4,6},{5,7},{6,4},{7,5},{8,10},{9,11},{10,... | collective-permute-start | bytes 221192 | tf_op jit(solution)/shard_map/ppermute | solution.py:21
  41.1 0.7 collective-permute-start.9
  41.8 0.7 collective-permute-done.13.refs_2_
  42.4 0.2 finish_rows.3.refs_0_
  42.7 1.5 %collective-permute-start.17 = (bf16[288,128]{1,0:T(8,128)(2,1)S(1)}, bf16[288,128]{1,0:T(8,128)(2,1)S(1)}, u32[]{:S(2)}, u32[]{:S(2)}) collective-permute-start(bf16[288,128]{1,0:T(8,128)(2,1)S(1)} %finish_rows.3.refs_0_), channel_id=1, source_target_pairs={{0,2},{1,3},{2,0},{3,1},{4,6},{5,7},{6,4},{7,5},{8,10},{9,11},{10,... | collective-permute-start | bytes 221192 | tf_op jit(solution)/shard_map/ppermute | solution.py:21
  44.2 0.6 collective-permute-start.15
  44.9 0.7 %collective-permute-done.10.refs_2_ = bf16[288,128]{1,0:T(8,128)(2,1)S(1)} collective-permute-done((bf16[288,128]{1,0:T(8,128)(2,1)S(1)}, bf16[288,128]{1,0:T(8,128)(2,1)S(1)}, u32[]{:S(2)}, u32[]{:S(2)}) %collective-permute-start.10) | collective-permute-done | bytes 73760 | tf_op jit(solution)/shard_map/ppermute | solution.py:21
  45.6 1.4 %absorb.1 = (f32[512,128]{1,0:T(8,128)S(1)}, f32[512,128]{1,0:T(8,128)S(1)}, f32[4,512,128]{2,1,0:T(8,128)S(1)}) custom-call(bf16[512,576]{1,0:T(8,128)(2,1)S(1)} %get-tuple-element.45.query_ref, s32[1,512]{1,0:T(1,128)S(1)} %get-tuple-element.46.slot_ref, f32[512,128]{1,0:T(8,128)S(1)} %get-tuple-element.49.top_ref, ...), custom_call_target="tpu_custom_call" | custom-call | flops 2000000000 | bytes 1000000 | tf_op jit(solution)/shard_map/absorb/pallas_call | solution.py:513
  47.0 0.1 collective-permute-done.17.refs_3_
  47.2 1.6 %collective-permute-done.16.refs_2_ = bf16[288,128]{1,0:T(8,128)(2,1)S(1)} collective-permute-done((bf16[288,128]{1,0:T(8,128)(2,1)S(1)}, bf16[288,128]{1,0:T(8,128)(2,1)S(1)}, u32[]{:S(2)}, u32[]{:S(2)}) %collective-permute-start.16) | collective-permute-done | bytes 73760 | tf_op jit(solution)/shard_map/ppermute | solution.py:21
  48.7 1.3 %attend.3.refs_0_ = bf16[16,2304]{1,0:T(8,128)(2,1)S(1)} custom-call(bf16[512,576]{1,0:T(8,128)(2,1)S(1)} %get-tuple-element.45.query_ref, s32[1,512]{1,0:T(1,128)S(1)} %get-tuple-element.46.slot_ref, f32[512,128]{1,0:T(8,128)S(1)} %get-tuple-element.65.top_ref, f32[512,128]{1,0:T(8,128)S(1)} %get-tuple-element.66.sum_ref, ...), custom_call_target="tpu_custom_call" | custom-call | tf_op jit(solution)/shard_map/attend/pallas_call | solution.py:546
  50.0 0.6 collective-permute-start.22
  50.7 1.2 %attend.2.refs_0_ = bf16[16,1792]{1,0:T(8,128)(2,1)S(1)} custom-call(bf16[512,576]{1,0:T(8,128)(2,1)S(1)} %get-tuple-element.45.query_ref, s32[1,512]{1,0:T(1,128)S(1)} %get-tuple-element.46.slot_ref, f32[512,128]{1,0:T(8,128)S(1)} %get-tuple-element.65.top_ref, f32[512,128]{1,0:T(8,128)S(1)} %get-tuple-element.66.sum_ref, ...), custom_call_target="tpu_custom_call" | custom-call | tf_op jit(solution)/shard_map/attend/pallas_call | solution.py:546
  51.8 2.4 %collective-permute-start.19 = (bf16[16,1792]{1,0:T(8,128)(2,1)S(1)}, bf16[16,1792]{1,0:T(8,128)(2,1)S(1)}, u32[]{:S(2)}, u32[]{:S(2)}) collective-permute-start(bf16[16,1792]{1,0:T(8,128)(2,1)S(1)} %attend.2.refs_0_), channel_id=1, source_target_pairs={{0,8},{4,12},{8,0},{12,4},{1,9},{5,13},{9,1},{13,5},{2,10},{6,14},... | collective-permute-start | bytes 172040 | tf_op jit(solution)/shard_map/ppermute | solution.py:21
  54.2 2.1 %collective-permute-done.22.refs_2_ = bf16[16,2304]{1,0:T(8,128)(2,1)S(1)} collective-permute-done((bf16[16,2304]{1,0:T(8,128)(2,1)S(1)}, bf16[16,2304]{1,0:T(8,128)(2,1)S(1)}, u32[]{:S(2)}, u32[]{:S(2)}) %collective-permute-start.22) | collective-permute-done | bytes 73760 | tf_op jit(solution)/shard_map/ppermute | solution.py:21
  56.4 2.0 %collective-permute-start.18 = (bf16[16,1792]{1,0:T(8,128)(2,1)S(1)}, bf16[16,1792]{1,0:T(8,128)(2,1)S(1)}, u32[]{:S(2)}, u32[]{:S(2)}) collective-permute-start(bf16[16,1792]{1,0:T(8,128)(2,1)S(1)} %attend.2.refs_0_), channel_id=1, source_target_pairs={{0,4},{4,0},{8,12},{12,8},{1,5},{5,1},{9,13},{13,9},{2,6},{6,2},{1... | collective-permute-start | bytes 172040 | tf_op jit(solution)/shard_map/ppermute | solution.py:21
  58.4 0.9 %collective-permute-start.20 = (bf16[16,1792]{1,0:T(8,128)(2,1)S(1)}, bf16[16,1792]{1,0:T(8,128)(2,1)S(1)}, u32[]{:S(2)}, u32[]{:S(2)}) collective-permute-start(bf16[16,1792]{1,0:T(8,128)(2,1)S(1)} %collective-permute-done.19.refs_2_), channel_id=1, source_target_pairs={{0,4},{4,0},{8,12},{12,8},{1,5},{5,1},{9,13},{13,9},{2,6},{6,2},{1... | collective-permute-start | bytes 172040 | tf_op jit(solution)/shard_map/ppermute | solution.py:21
  59.3 2.2 %collective-permute-done.23.refs_3_ = bf16[16,2304]{1,0:T(8,128)(2,1)S(1)} collective-permute-done((bf16[16,2304]{1,0:T(8,128)(2,1)S(1)}, bf16[16,2304]{1,0:T(8,128)(2,1)S(1)}, u32[]{:S(2)}, u32[]{:S(2)}) %collective-permute-start.23) | collective-permute-done | bytes 73760 | tf_op jit(solution)/shard_map/ppermute | solution.py:21
  61.5 1.6 %output_product.2.refs_5_ = f32[64,1792]{1,0:T(8,128)S(1)} custom-call(bf16[16,2304]{1,0:T(8,128)(2,1)S(1)} %attend.3.refs_0_, bf16[16,2304]{1,0:T(8,128)(2,1)S(1)} %collective-permute-done.21.refs_1_, bf16[16,2304]{1,0:T(8,128)(2,1)S(1)} %collective-permute-done.22.refs_2_, bf16[16,2304]{1,0:T(8,128)(2,1)S(1)} %collective-permute-done.23.refs_3_, ...), custom_call_target="tpu_custom_call" | custom-call | tf_op jit(solution)/shard_map/output_product/pallas_call | solution.py:600
  63.1 0.0 collective-permute-done.18.refs_1_
  63.1 0.0 collective-permute-done.20.refs_3_
  63.1 1.3 %output_product.3 = (f32[16,1792]{1,0:T(8,128)S(1)}, bf16[16,1792]{1,0:T(8,128)(2,1)S(1)}, bf16[16,1792]{1,0:T(8,128)(2,1)S(1)}, bf16[16,1792]{1,0:T(8,128)(2,1)S(1)}) custom-call(bf16[16,1792]{1,0:T(8,128)(2,1)S(1)} %attend.2.refs_0_, bf16[16,1792]{1,0:T(8,128)(2,1)S(1)} %collective-permute-done.18.refs_1_, ...), custom_call_target="tpu_custom_call" | custom-call | tf_op jit(solution)/shard_map/output_product/pallas_call | solution.py:600
  64.4 0.5 collective-permute-start.24
  64.9 0.9 %collective-permute-start.25 = (bf16[16,1792]{1,0:T(8,128)(2,1)S(1)}, bf16[16,1792]{1,0:T(8,128)(2,1)S(1)}, u32[]{:S(2)}, u32[]{:S(2)}) collective-permute-start(bf16[16,1792]{1,0:T(8,128)(2,1)S(1)} %get-tuple-element.77), channel_id=1, source_target_pairs={{0,2},{1,3},{2,0},{3,1},{4,6},{5,7},{6,4},{7,5},{8,10},{9,11},{10,... | collective-permute-start | bytes 172040 | tf_op jit(solution)/shard_map/ppermute | solution.py:21
  65.8 0.5 collective-permute-start.26
  66.3 2.3 %collective-permute-done.24 = bf16[16,1792]{1,0:T(8,128)(2,1)S(1)} collective-permute-done((bf16[16,1792]{1,0:T(8,128)(2,1)S(1)}, bf16[16,1792]{1,0:T(8,128)(2,1)S(1)}, u32[]{:S(2)}, u32[]{:S(2)}) %collective-permute-start.24) | collective-permute-done | bytes 57376 | tf_op jit(solution)/shard_map/ppermute | solution.py:21
  68.6 1.1 %collective-permute-done.25 = bf16[16,1792]{1,0:T(8,128)(2,1)S(1)} collective-permute-done((bf16[16,1792]{1,0:T(8,128)(2,1)S(1)}, bf16[16,1792]{1,0:T(8,128)(2,1)S(1)}, u32[]{:S(2)}, u32[]{:S(2)}) %collective-permute-start.25) | collective-permute-done | bytes 57376 | tf_op jit(solution)/shard_map/ppermute | solution.py:21
  69.6 0.7 add_convert_fusion
  (40 shorter events, 0.1 us)
Async XLA Ops:
  0.0 7.1 %copy-start.4 = (bf16[448,576]{1,0:T(8,128)(2,1)S(1)}, bf16[448,576]{1,0:T(8,128)(2,1)}, u32[]{:S(2)}) copy-start(bf16[448,576]{1,0:T(8,128)(2,1)} %value_ref) | copy-start | bytes 1548292
  1.4 19.4 %collective-permute-start.1 = (bf16[64,1792]{1,0:T(8,128)(2,1)S(1)}, bf16[64,1792]{1,0:T(8,128)(2,1)S(1)}, u32[]{:S(2)}, u32[]{:S(2)}) collective-permute-start(bf16[64,1792]{1,0:T(8,128)(2,1)S(1)} %get-tuple-element.56), channel_id=1, source_target_pairs={{0,12},{4,8},{8,4},{12,0},{1,13},{5,9},{9,5},{13,1},{2,14},{6,10},... | collective-permute-start | bytes 688136 | tf_op jit(solution)/shard_map/ppermute | solution.py:21
  6.5 19.5 %collective-permute-start.2 = (bf16[64,1792]{1,0:T(8,128)(2,1)S(1)}, bf16[64,1792]{1,0:T(8,128)(2,1)S(1)}, u32[]{:S(2)}, u32[]{:S(2)}) collective-permute-start(bf16[64,1792]{1,0:T(8,128)(2,1)S(1)} %get-tuple-element.57), channel_id=1, source_target_pairs={{0,8},{4,12},{8,0},{12,4},{1,9},{5,13},{9,1},{13,5},{2,10},{6,14},... | collective-permute-start | bytes 688136 | tf_op jit(solution)/shard_map/ppermute | solution.py:21
  6.5 19.5 %collective-permute-start.3 = (bf16[64,1792]{1,0:T(8,128)(2,1)S(1)}, bf16[64,1792]{1,0:T(8,128)(2,1)S(1)}, u32[]{:S(2)}, u32[]{:S(2)}) collective-permute-start(bf16[64,1792]{1,0:T(8,128)(2,1)S(1)} %get-tuple-element.58), channel_id=1, source_target_pairs={{0,4},{4,0},{8,12},{12,8},{1,5},{5,1},{9,13},{13,9},{2,6},{6,2},{1... | collective-permute-start | bytes 688136 | tf_op jit(solution)/shard_map/ppermute | solution.py:21
  7.1 2.2 %copy-start.1 = (bf16[32,128,512]{2,1,0:T(8,128)(2,1)S(1)}, bf16[32,128,512]{2,1,0:T(8,128)(2,1)}, u32[]{:S(2)}) copy-start(bf16[32,128,512]{2,1,0:T(8,128)(2,1)} %absorb_hbm.1) | copy-start | bytes 12582916
  7.1 3.5 %copy-start.2 = (bf16[32,512,128]{2,1,0:T(8,128)(2,1)S(1)}, bf16[32,512,128]{2,1,0:T(8,128)(2,1)}, u32[]{:S(2)}) copy-start(bf16[32,512,128]{2,1,0:T(8,128)(2,1)} %value_hbm.1) | copy-start | bytes 12582916
  7.1 4.1 %copy-start.3 = (bf16[8,256,576]{1,2,0:T(8,128)(2,1)S(1)}, bf16[8,256,576]{1,2,0:T(8,128)(2,1)}, u32[]{:S(2)}) copy-start(bf16[8,256,576]{1,2,0:T(8,128)(2,1)} %param.18) | copy-start | bytes 7077892
  7.1 4.1 %copy-start.5 = (bf16[8,2,32,192]{3,2,1,0:T(8,128)(2,1)S(1)}, bf16[8,2,32,192]{3,2,1,0:T(8,128)(2,1)}, u32[]{:S(2)}) copy-start(bf16[8,2,32,192]{3,2,1,0:T(8,128)(2,1)} %param.20) | copy-start | bytes 589828
  7.2 4.1 %copy-start.6 = (bf16[8,2,576]{2,1,0:T(2,128)(2,1)S(1)}, bf16[8,2,576]{2,1,0:T(2,128)(2,1)}, u32[]{:S(2)}) copy-start(bf16[8,2,576]{2,1,0:T(2,128)(2,1)} %fresh_hbm.1) | copy-start | bytes 55300
  7.2 4.1 %copy-start.7 = (s32[1024]{0:T(1024)S(1)}, s32[1024]{0:T(1024)}, u32[]{:S(2)}) copy-start(s32[1024]{0:T(1024)} %param.15) | copy-start | bytes 12292
  7.2 4.1 %copy-start.8 = (s32[16]{0:T(128)S(1)}, s32[16]{0:T(128)}, u32[]{:S(2)}) copy-start(s32[16]{0:T(128)} %length_hbm) | copy-start | bytes 196
  7.2 4.1 %copy-start.9 = (s32[16]{0:T(128)S(1)}, s32[16]{0:T(128)}, u32[]{:S(2)}) copy-start(s32[16]{0:T(128)} %slot_hbm.1) | copy-start | bytes 196
  7.3 13.0 %collective-permute-start = (bf16[2016,128]{1,0:T(8,128)(2,1)S(1)}, bf16[2016,128]{1,0:T(8,128)(2,1)S(1)}, u32[]{:S(2)}, u32[]{:S(2)}) collective-permute-start(bf16[2016,128]{1,0:T(8,128)(2,1)S(1)} %pack_weight.1.refs_0_), channel_id=1, source_target_pairs={{0,2},{1,3},{2,0},{3,1},{4,6},{5,7},{6,4},{7,5},{8,10},{9,11},{10,... | collective-permute-start | bytes 1548296 | tf_op jit(solution)/shard_map/ppermute | solution.py:21
  20.3 19.1 %copy-start = (f32[512]{0:T(512)S(1)}, f32[512]{0:T(512)}, u32[]{:S(2)}) copy-start(f32[512]{0:T(512)} %param.14) | copy-start | bytes 6148
  20.3 5.8 %collective-permute-start.4 = (bf16[2016,128]{1,0:T(8,128)(2,1)S(1)}, bf16[2016,128]{1,0:T(8,128)(2,1)S(1)}, u32[]{:S(2)}, u32[]{:S(2)}) collective-permute-start(bf16[2016,128]{1,0:T(8,128)(2,1)S(1)} %pack_weight.1.refs_0_), channel_id=1, source_target_pairs={{0,1},{1,0},{2,3},{3,2},{4,5},{5,4},{6,7},{7,6},{8,9},{9,8},{10,11... | collective-permute-start | bytes 1548296 | tf_op jit(solution)/shard_map/ppermute | solution.py:21
  20.3 5.8 %collective-permute-start.5 = (bf16[2016,128]{1,0:T(8,128)(2,1)S(1)}, bf16[2016,128]{1,0:T(8,128)(2,1)S(1)}, u32[]{:S(2)}, u32[]{:S(2)}) collective-permute-start(bf16[2016,128]{1,0:T(8,128)(2,1)S(1)} %collective-permute-done.refs_2_), channel_id=1, source_target_pairs={{0,1},{1,0},{2,3},{3,2},{4,5},{5,4},{6,7},{7,6},{8,9},{9,8},{10,11... | collective-permute-start | bytes 1548296 | tf_op jit(solution)/shard_map/ppermute | solution.py:21
  27.8 6.9 %collective-permute-start.6 = (bf16[288,128]{1,0:T(8,128)(2,1)S(1)}, bf16[288,128]{1,0:T(8,128)(2,1)S(1)}, u32[]{:S(2)}, u32[]{:S(2)}) collective-permute-start(bf16[288,128]{1,0:T(8,128)(2,1)S(1)} %get-tuple-element.62), channel_id=1, source_target_pairs={{0,12},{4,8},{8,4},{12,0},{1,13},{5,9},{9,5},{13,1},{2,14},{6,10},... | collective-permute-start | bytes 221192 | tf_op jit(solution)/shard_map/ppermute | solution.py:21
  30.3 9.0 %collective-permute-start.7 = (bf16[288,128]{1,0:T(8,128)(2,1)S(1)}, bf16[288,128]{1,0:T(8,128)(2,1)S(1)}, u32[]{:S(2)}, u32[]{:S(2)}) collective-permute-start(bf16[288,128]{1,0:T(8,128)(2,1)S(1)} %get-tuple-element.63), channel_id=1, source_target_pairs={{0,8},{4,12},{8,0},{12,4},{1,9},{5,13},{9,1},{13,5},{2,10},{6,14},... | collective-permute-start | bytes 221192 | tf_op jit(solution)/shard_map/ppermute | solution.py:21
  30.3 9.0 %collective-permute-start.8 = (bf16[288,128]{1,0:T(8,128)(2,1)S(1)}, bf16[288,128]{1,0:T(8,128)(2,1)S(1)}, u32[]{:S(2)}, u32[]{:S(2)}) collective-permute-start(bf16[288,128]{1,0:T(8,128)(2,1)S(1)} %get-tuple-element.64), channel_id=1, source_target_pairs={{0,4},{4,0},{8,12},{12,8},{1,5},{5,1},{9,13},{13,9},{2,6},{6,2},{1... | collective-permute-start | bytes 221192 | tf_op jit(solution)/shard_map/ppermute | solution.py:21
  32.2 8.9 %collective-permute-start.12 = (bf16[288,128]{1,0:T(8,128)(2,1)S(1)}, bf16[288,128]{1,0:T(8,128)(2,1)S(1)}, u32[]{:S(2)}, u32[]{:S(2)}) collective-permute-start(bf16[288,128]{1,0:T(8,128)(2,1)S(1)} %get-tuple-element.71), channel_id=1, source_target_pairs={{0,12},{4,8},{8,4},{12,0},{1,13},{5,9},{9,5},{13,1},{2,14},{6,10},... | collective-permute-start | bytes 221192 | tf_op jit(solution)/shard_map/ppermute | solution.py:21
  34.7 7.7 %collective-permute-start.13 = (bf16[288,128]{1,0:T(8,128)(2,1)S(1)}, bf16[288,128]{1,0:T(8,128)(2,1)S(1)}, u32[]{:S(2)}, u32[]{:S(2)}) collective-permute-start(bf16[288,128]{1,0:T(8,128)(2,1)S(1)} %get-tuple-element.72), channel_id=1, source_target_pairs={{0,8},{4,12},{8,0},{12,4},{1,9},{5,13},{9,1},{13,5},{2,10},{6,14},... | collective-permute-start | bytes 221192 | tf_op jit(solution)/shard_map/ppermute | solution.py:21
  34.7 7.7 %collective-permute-start.14 = (bf16[288,128]{1,0:T(8,128)(2,1)S(1)}, bf16[288,128]{1,0:T(8,128)(2,1)S(1)}, u32[]{:S(2)}, u32[]{:S(2)}) collective-permute-start(bf16[288,128]{1,0:T(8,128)(2,1)S(1)} %get-tuple-element.73), channel_id=1, source_target_pairs={{0,4},{4,0},{8,12},{12,8},{1,5},{5,1},{9,13},{13,9},{2,6},{6,2},{1... | collective-permute-start | bytes 221192 | tf_op jit(solution)/shard_map/ppermute | solution.py:21
  39.6 4.6 %collective-permute-start.11 = (bf16[288,128]{1,0:T(8,128)(2,1)S(1)}, bf16[288,128]{1,0:T(8,128)(2,1)S(1)}, u32[]{:S(2)}, u32[]{:S(2)}) collective-permute-start(bf16[288,128]{1,0:T(8,128)(2,1)S(1)} %finish_rows.2.refs_0_), channel_id=1, source_target_pairs={{0,2},{1,3},{2,0},{3,1},{4,6},{5,7},{6,4},{7,5},{8,10},{9,11},{10,... | collective-permute-start | bytes 221192 | tf_op jit(solution)/shard_map/ppermute | solution.py:21
  41.1 4.5 %collective-permute-start.10 = (bf16[288,128]{1,0:T(8,128)(2,1)S(1)}, bf16[288,128]{1,0:T(8,128)(2,1)S(1)}, u32[]{:S(2)}, u32[]{:S(2)}) collective-permute-start(bf16[288,128]{1,0:T(8,128)(2,1)S(1)} %finish_rows.2.refs_0_), channel_id=1, source_target_pairs={{0,3},{1,2},{2,1},{3,0},{4,7},{5,6},{6,5},{7,4},{8,11},{9,10},{10,... | collective-permute-start | bytes 221192 | tf_op jit(solution)/shard_map/ppermute | solution.py:21
  41.1 4.4 %collective-permute-start.9 = (bf16[288,128]{1,0:T(8,128)(2,1)S(1)}, bf16[288,128]{1,0:T(8,128)(2,1)S(1)}, u32[]{:S(2)}, u32[]{:S(2)}) collective-permute-start(bf16[288,128]{1,0:T(8,128)(2,1)S(1)} %finish_rows.2.refs_0_), channel_id=1, source_target_pairs={{0,1},{1,0},{2,3},{3,2},{4,5},{5,4},{6,7},{7,6},{8,9},{9,8},{10,11... | collective-permute-start | bytes 221192 | tf_op jit(solution)/shard_map/ppermute | solution.py:21
  42.7 4.5 %collective-permute-start.17 = (bf16[288,128]{1,0:T(8,128)(2,1)S(1)}, bf16[288,128]{1,0:T(8,128)(2,1)S(1)}, u32[]{:S(2)}, u32[]{:S(2)}) collective-permute-start(bf16[288,128]{1,0:T(8,128)(2,1)S(1)} %finish_rows.3.refs_0_), channel_id=1, source_target_pairs={{0,2},{1,3},{2,0},{3,1},{4,6},{5,7},{6,4},{7,5},{8,10},{9,11},{10,... | collective-permute-start | bytes 221192 | tf_op jit(solution)/shard_map/ppermute | solution.py:21
  44.2 4.5 %collective-permute-start.16 = (bf16[288,128]{1,0:T(8,128)(2,1)S(1)}, bf16[288,128]{1,0:T(8,128)(2,1)S(1)}, u32[]{:S(2)}, u32[]{:S(2)}) collective-permute-start(bf16[288,128]{1,0:T(8,128)(2,1)S(1)} %finish_rows.3.refs_0_), channel_id=1, source_target_pairs={{0,3},{1,2},{2,1},{3,0},{4,7},{5,6},{6,5},{7,4},{8,11},{9,10},{10,... | collective-permute-start | bytes 221192 | tf_op jit(solution)/shard_map/ppermute | solution.py:21
  44.2 4.5 %collective-permute-start.15 = (bf16[288,128]{1,0:T(8,128)(2,1)S(1)}, bf16[288,128]{1,0:T(8,128)(2,1)S(1)}, u32[]{:S(2)}, u32[]{:S(2)}) collective-permute-start(bf16[288,128]{1,0:T(8,128)(2,1)S(1)} %finish_rows.3.refs_0_), channel_id=1, source_target_pairs={{0,1},{1,0},{2,3},{3,2},{4,5},{5,4},{6,7},{7,6},{8,9},{9,8},{10,11... | collective-permute-start | bytes 221192 | tf_op jit(solution)/shard_map/ppermute | solution.py:21
  50.0 6.3 %collective-permute-start.22 = (bf16[16,2304]{1,0:T(8,128)(2,1)S(1)}, bf16[16,2304]{1,0:T(8,128)(2,1)S(1)}, u32[]{:S(2)}, u32[]{:S(2)}) collective-permute-start(bf16[16,2304]{1,0:T(8,128)(2,1)S(1)} %attend.3.refs_0_), channel_id=1, source_target_pairs={{0,8},{4,12},{8,0},{12,4},{1,9},{5,13},{9,1},{13,5},{2,10},{6,14},... | collective-permute-start | bytes 221192 | tf_op jit(solution)/shard_map/ppermute | solution.py:21
  51.8 6.5 %collective-permute-start.19 = (bf16[16,1792]{1,0:T(8,128)(2,1)S(1)}, bf16[16,1792]{1,0:T(8,128)(2,1)S(1)}, u32[]{:S(2)}, u32[]{:S(2)}) collective-permute-start(bf16[16,1792]{1,0:T(8,128)(2,1)S(1)} %attend.2.refs_0_), channel_id=1, source_target_pairs={{0,8},{4,12},{8,0},{12,4},{1,9},{5,13},{9,1},{13,5},{2,10},{6,14},... | collective-permute-start | bytes 172040 | tf_op jit(solution)/shard_map/ppermute | solution.py:21
  54.2 5.1 %collective-permute-start.21 = (bf16[16,2304]{1,0:T(8,128)(2,1)S(1)}, bf16[16,2304]{1,0:T(8,128)(2,1)S(1)}, u32[]{:S(2)}, u32[]{:S(2)}) collective-permute-start(bf16[16,2304]{1,0:T(8,128)(2,1)S(1)} %attend.3.refs_0_), channel_id=1, source_target_pairs={{0,4},{4,0},{8,12},{12,8},{1,5},{5,1},{9,13},{13,9},{2,6},{6,2},{1... | collective-permute-start | bytes 221192 | tf_op jit(solution)/shard_map/ppermute | solution.py:21
  56.4 5.1 %collective-permute-start.23 = (bf16[16,2304]{1,0:T(8,128)(2,1)S(1)}, bf16[16,2304]{1,0:T(8,128)(2,1)S(1)}, u32[]{:S(2)}, u32[]{:S(2)}) collective-permute-start(bf16[16,2304]{1,0:T(8,128)(2,1)S(1)} %collective-permute-done.22.refs_2_), channel_id=1, source_target_pairs={{0,4},{4,0},{8,12},{12,8},{1,5},{5,1},{9,13},{13,9},{2,6},{6,2},{1... | collective-permute-start | bytes 221192 | tf_op jit(solution)/shard_map/ppermute | solution.py:21
  56.4 6.7 %collective-permute-start.18 = (bf16[16,1792]{1,0:T(8,128)(2,1)S(1)}, bf16[16,1792]{1,0:T(8,128)(2,1)S(1)}, u32[]{:S(2)}, u32[]{:S(2)}) collective-permute-start(bf16[16,1792]{1,0:T(8,128)(2,1)S(1)} %attend.2.refs_0_), channel_id=1, source_target_pairs={{0,4},{4,0},{8,12},{12,8},{1,5},{5,1},{9,13},{13,9},{2,6},{6,2},{1... | collective-permute-start | bytes 172040 | tf_op jit(solution)/shard_map/ppermute | solution.py:21
  58.4 4.7 %collective-permute-start.20 = (bf16[16,1792]{1,0:T(8,128)(2,1)S(1)}, bf16[16,1792]{1,0:T(8,128)(2,1)S(1)}, u32[]{:S(2)}, u32[]{:S(2)}) collective-permute-start(bf16[16,1792]{1,0:T(8,128)(2,1)S(1)} %collective-permute-done.19.refs_2_), channel_id=1, source_target_pairs={{0,4},{4,0},{8,12},{12,8},{1,5},{5,1},{9,13},{13,9},{2,6},{6,2},{1... | collective-permute-start | bytes 172040 | tf_op jit(solution)/shard_map/ppermute | solution.py:21
  64.4 4.2 %collective-permute-start.24 = (bf16[16,1792]{1,0:T(8,128)(2,1)S(1)}, bf16[16,1792]{1,0:T(8,128)(2,1)S(1)}, u32[]{:S(2)}, u32[]{:S(2)}) collective-permute-start(bf16[16,1792]{1,0:T(8,128)(2,1)S(1)} %get-tuple-element.76), channel_id=1, source_target_pairs={{0,3},{1,2},{2,1},{3,0},{4,7},{5,6},{6,5},{7,4},{8,11},{9,10},{10,... | collective-permute-start | bytes 172040 | tf_op jit(solution)/shard_map/ppermute | solution.py:21
  64.9 4.8 %collective-permute-start.25 = (bf16[16,1792]{1,0:T(8,128)(2,1)S(1)}, bf16[16,1792]{1,0:T(8,128)(2,1)S(1)}, u32[]{:S(2)}, u32[]{:S(2)}) collective-permute-start(bf16[16,1792]{1,0:T(8,128)(2,1)S(1)} %get-tuple-element.77), channel_id=1, source_target_pairs={{0,2},{1,3},{2,0},{3,1},{4,6},{5,7},{6,4},{7,5},{8,10},{9,11},{10,... | collective-permute-start | bytes 172040 | tf_op jit(solution)/shard_map/ppermute | solution.py:21
  65.8 3.8 %collective-permute-start.26 = (bf16[16,1792]{1,0:T(8,128)(2,1)S(1)}, bf16[16,1792]{1,0:T(8,128)(2,1)S(1)}, u32[]{:S(2)}, u32[]{:S(2)}) collective-permute-start(bf16[16,1792]{1,0:T(8,128)(2,1)S(1)} %get-tuple-element.78), channel_id=1, source_target_pairs={{0,1},{1,0},{2,3},{3,2},{4,5},{5,4},{6,7},{7,6},{8,9},{9,8},{10,11... | collective-permute-start | bytes 172040 | tf_op jit(solution)/shard_map/ppermute | solution.py:21

commit v14 on v13

--- a/solution.py
+++ b/solution.py
@@ -374,8 +374,7 @@
 def project_kernel(dev_count, side_count, target_ref, x_ref, *refs):
     my_side = lax.axis_index("side")
     weight_refs = refs[:side_count]
-    out_refs = refs[side_count:-2]
-    slab_weight, rows = refs[-2:]
+    out_refs, slab_weight = refs[side_count:-1], refs[-1]
     tok_rows = x_ref.shape[0] // dev_count
     full = slab_weight.shape[1] // 128
     if side_count > 1:
@@ -388,14 +387,13 @@
             slab_weight[pl.ds(first, shard), full * 128 :] = rest
     slab = slab_weight[...] if side_count > 1 else weight_refs[0][...]
     raw = jnp.dot(x_ref[...], slab, preferred_element_type=f32).astype(bf16)
-    rows[...] = raw
     target = target_ref[...]
     half_rows = tok_rows
     step = min(4, 2 * dev_count)
     for j in range(0, 2 * dev_count, step):
         ids = lax.broadcasted_iota(jnp.int32, (step * half_rows, target.shape[1]), 0)
         route = jnp.where(ids + j * half_rows == target, 1.0, 0.0).astype(bf16)
-        placed = jnp.dot(route, rows[...], preferred_element_type=f32)
+        placed = jnp.dot(route, raw, preferred_element_type=f32)
         for n in range(step):
             store_packed(out_refs[j + n], placed[n * half_rows : (n + 1) * half_rows])
 
@@ -414,7 +412,6 @@
         out_specs=[in_vmem] * (2 * dev_count),
         scratch_shapes=[
             pltpu.VMEM((slab, width), bf16),
-            pltpu.VMEM((target.shape[1], width), bf16),
         ],
         compiler_params=pltpu.CompilerParams(vmem_limit_bytes=20 * mib),
         name="project",
@@ -698,7 +695,7 @@
         )
         product = products[0]
     result = products[0]
-    for k in sorted(range(1, side_count), reverse=True):
+    for k in piece_order(side_count)[:0:-1]:
         result = result + swap(products[k], "side", k).astype(f32)
     return result.astype(bf16)
 

time: 70.4 us -> 70.6 us (level)
  no operation moved by 1% of the time
where the time goes in v14:
time: 70.6 us; the launch traced here: 70.5 us
  starting transfers between devices  29.3 us (42%)
  waiting for transfers between devices  20.1 us (28%)
  Pallas kernels  18 us (25%)
  local copies, waits for them, and re-layouts  2.31 us (3%)
    ppermute x27, starting transfers between devices, swap(): return lax.ppermute(value, axis, [(i, i ^ step) for i in range(count)])  29.3 us
    ppermute x27, waiting for transfers between devices, swap(): return lax.ppermute(value, axis, [(i, i ^ step) for i in range(count)])  20.1 us
    pallas_call x1, Pallas kernels, prepare(): pl.pallas_call(functools.partial(prepare_kernel, scale, steps, (dev_count...  7.61 us
    pallas_call x2, Pallas kernels, output_product(): pl.pallas_call(functools.partial(output_kernel, dev_count, side_count, st...  2.82 us
    pallas_call x2, Pallas kernels, attend(): pl.pallas_call(functools.partial(attend_kernel, layout, which, first_head...  2.48 us
    unnamed x20, local copies, waits for them, and re-layouts  2.31 us
    pallas_call x1, Pallas kernels, project(): pl.pallas_call(functools.partial(project_kernel, dev_count, len(weights))...  1.68 us
    pallas_call x1, Pallas kernels, absorb(): pl.pallas_call(functools.partial(absorb_kernel, layout, which), out_shape...  1.44 us
  transfers between devices with their start and end apart: 27, of which 11 were waited for; matrix products, arithmetic and copies ran while one was open for 0% of the time, Pallas kernels for 18%

profile of v14, /device:TPU:0, one launch (start us, length us, event | category | flops | bytes accessed | tf_op | source)
XLA Modules:
  0.0 70.5 jit_solution(16802265390839570654)
XLA Ops:
  0.0 1.4 %split_columns.1 = (bf16[64,1792]{1,0:T(8,128)(2,1)S(1)}, bf16[64,1792]{1,0:T(8,128)(2,1)S(1)}, bf16[64,1792]{1,0:T(8,128)(2,1)S(1)}, bf16[64,1792]{1,0:T(8,128)(2,1)S(1)}) custom-call(bf16[64,7168]{1,0:T(8,128)(2,1)} %prompts_ref.1), custom_call_target="tpu_custom_call" | custom-call | flops 10000000000 | bytes 40000000 | tf_op jit(solution)/shard_map/split_columns/pallas_call | solution.py:100
  1.4 5.1 %collective-permute-start.1 = (bf16[64,1792]{1,0:T(8,128)(2,1)S(1)}, bf16[64,1792]{1,0:T(8,128)(2,1)S(1)}, u32[]{:S(2)}, u32[]{:S(2)}) collective-permute-start(bf16[64,1792]{1,0:T(8,128)(2,1)S(1)} %get-tuple-element.56), channel_id=1, source_target_pairs={{0,12},{4,8},{8,4},{12,0},{1,13},{5,9},{9,5},{13,1},{2,14},{6,10},... | collective-permute-start | bytes 688136 | tf_op jit(solution)/shard_map/ppermute | solution.py:21
  6.5 0.6 collective-permute-start.3
  7.1 0.0 copy-start.5
  7.2 0.1 pack_weight.1.refs_0_
  7.3 1.7 %collective-permute-start = (bf16[2016,128]{1,0:T(8,128)(2,1)S(1)}, bf16[2016,128]{1,0:T(8,128)(2,1)S(1)}, u32[]{:S(2)}, u32[]{:S(2)}) collective-permute-start(bf16[2016,128]{1,0:T(8,128)(2,1)S(1)} %pack_weight.1.refs_0_), channel_id=1, source_target_pairs={{0,2},{1,3},{2,0},{3,1},{4,6},{5,7},{6,4},{7,5},{8,10},{9,11},{10,... | collective-permute-start | bytes 1548296 | tf_op jit(solution)/shard_map/ppermute | solution.py:21
  9.0 0.3 copy-done.1
  9.3 1.3 %copy-done.2 = bf16[32,512,128]{2,1,0:T(8,128)(2,1)S(1)} copy-done((bf16[32,512,128]{2,1,0:T(8,128)(2,1)S(1)}, bf16[32,512,128]{2,1,0:T(8,128)(2,1)}, u32[]{:S(2)}) %copy-start.2) | copy-done | bytes 4194328
  10.6 0.7 copy-done.3
  11.3 7.6 %prepare.1 = (bf16[512,576]{1,0:T(8,128)(2,1)S(1)}, f32[512,128]{1,0:T(8,128)S(1)}, f32[512,128]{1,0:T(8,128)S(1)}, f32[4,512,128]{2,1,0:T(8,128)S(1)}, f32[16,1...) custom-call(f32[1,32]{1,0:T(1,128)S(1)} %negate_power_fusion.inverse, ...), custom_call_target="tpu_custom_call" | custom-call | flops 40000000000 | bytes 28000000 | tf_op jit(solution)/shard_map/prepare/pallas_call | solution.py:323
  18.9 1.4 %collective-permute-done.refs_2_ = bf16[2016,128]{1,0:T(8,128)(2,1)S(1)} collective-permute-done((bf16[2016,128]{1,0:T(8,128)(2,1)S(1)}, bf16[2016,128]{1,0:T(8,128)(2,1)S(1)}, u32[]{:S(2)}, u32[]{:S(2)}) %collective-permute-start) | collective-permute-done | bytes 516128 | tf_op jit(solution)/shard_map/ppermute | solution.py:21
  20.3 0.5 collective-permute-start.5
  20.8 5.2 %collective-permute-done.2.refs_2_ = bf16[64,1792]{1,0:T(8,128)(2,1)S(1)} collective-permute-done((bf16[64,1792]{1,0:T(8,128)(2,1)S(1)}, bf16[64,1792]{1,0:T(8,128)(2,1)S(1)}, u32[]{:S(2)}, u32[]{:S(2)}) %collective-permute-start.2) | collective-permute-done | bytes 229408 | tf_op jit(solution)/shard_map/ppermute | solution.py:21
  26.0 0.1 stack_rows.1.x_ref
  26.1 1.7 %project.1 = (f32[288,128]{1,0:T(8,128)S(1)}, bf16[288,128]{1,0:T(8,128)(2,1)S(1)}, bf16[288,128]{1,0:T(8,128)(2,1)S(1)}, bf16[288,128]{1,0:T(8,128)(2,1)S(1)}, ...) custom-call(s32[1,256]{1,0:T(1,128)S(1)} %get-tuple-element.54.targe, ...), custom_call_target="tpu_custom_call" | custom-call | tf_op jit(solution)/shard_map/project/pallas_call | solution.py:403
  27.8 2.5 %collective-permute-start.6 = (bf16[288,128]{1,0:T(8,128)(2,1)S(1)}, bf16[288,128]{1,0:T(8,128)(2,1)S(1)}, u32[]{:S(2)}, u32[]{:S(2)}) collective-permute-start(bf16[288,128]{1,0:T(8,128)(2,1)S(1)} %get-tuple-element.62), channel_id=1, source_target_pairs={{0,12},{4,8},{8,4},{12,0},{1,13},{5,9},{9,5},{13,1},{2,14},{6,10},... | collective-permute-start | bytes 221192 | tf_op jit(solution)/shard_map/ppermute | solution.py:21
  30.3 1.9 %collective-permute-start.8 = (bf16[288,128]{1,0:T(8,128)(2,1)S(1)}, bf16[288,128]{1,0:T(8,128)(2,1)S(1)}, u32[]{:S(2)}, u32[]{:S(2)}) collective-permute-start(bf16[288,128]{1,0:T(8,128)(2,1)S(1)} %get-tuple-element.64), channel_id=1, source_target_pairs={{0,4},{4,0},{8,12},{12,8},{1,5},{5,1},{9,13},{13,9},{2,6},{6,2},{1... | collective-permute-start | bytes 221192 | tf_op jit(solution)/shard_map/ppermute | solution.py:21
  32.2 2.5 %collective-permute-start.12 = (bf16[288,128]{1,0:T(8,128)(2,1)S(1)}, bf16[288,128]{1,0:T(8,128)(2,1)S(1)}, u32[]{:S(2)}, u32[]{:S(2)}) collective-permute-start(bf16[288,128]{1,0:T(8,128)(2,1)S(1)} %get-tuple-element.71), channel_id=1, source_target_pairs={{0,12},{4,8},{8,4},{12,0},{1,13},{5,9},{9,5},{13,1},{2,14},{6,10},... | collective-permute-start | bytes 221192 | tf_op jit(solution)/shard_map/ppermute | solution.py:21
  34.7 1.9 %collective-permute-start.14 = (bf16[288,128]{1,0:T(8,128)(2,1)S(1)}, bf16[288,128]{1,0:T(8,128)(2,1)S(1)}, u32[]{:S(2)}, u32[]{:S(2)}) collective-permute-start(bf16[288,128]{1,0:T(8,128)(2,1)S(1)} %get-tuple-element.73), channel_id=1, source_target_pairs={{0,4},{4,0},{8,12},{12,8},{1,5},{5,1},{9,13},{13,9},{2,6},{6,2},{1... | collective-permute-start | bytes 221192 | tf_op jit(solution)/shard_map/ppermute | solution.py:21
  36.6 2.7 %collective-permute-done.7.refs_2_ = bf16[288,128]{1,0:T(8,128)(2,1)S(1)} collective-permute-done((bf16[288,128]{1,0:T(8,128)(2,1)S(1)}, bf16[288,128]{1,0:T(8,128)(2,1)S(1)}, u32[]{:S(2)}, u32[]{:S(2)}) %collective-permute-start.7) | collective-permute-done | bytes 73760 | tf_op jit(solution)/shard_map/ppermute | solution.py:21
  39.3 0.2 finish_rows.2.refs_0_
  39.6 1.5 %collective-permute-start.11 = (bf16[288,128]{1,0:T(8,128)(2,1)S(1)}, bf16[288,128]{1,0:T(8,128)(2,1)S(1)}, u32[]{:S(2)}, u32[]{:S(2)}) collective-permute-start(bf16[288,128]{1,0:T(8,128)(2,1)S(1)} %finish_rows.2.refs_0_), channel_id=1, source_target_pairs={{0,2},{1,3},{2,0},{3,1},{4,6},{5,7},{6,4},{7,5},{8,10},{9,11},{10,... | collective-permute-start | bytes 221192 | tf_op jit(solution)/shard_map/ppermute | solution.py:21
  41.1 0.6 collective-permute-start.9
  41.8 0.7 collective-permute-done.13.refs_2_
  42.4 0.2 finish_rows.3.refs_0_
  42.6 1.5 %collective-permute-start.17 = (bf16[288,128]{1,0:T(8,128)(2,1)S(1)}, bf16[288,128]{1,0:T(8,128)(2,1)S(1)}, u32[]{:S(2)}, u32[]{:S(2)}) collective-permute-start(bf16[288,128]{1,0:T(8,128)(2,1)S(1)} %finish_rows.3.refs_0_), channel_id=1, source_target_pairs={{0,2},{1,3},{2,0},{3,1},{4,6},{5,7},{6,4},{7,5},{8,10},{9,11},{10,... | collective-permute-start | bytes 221192 | tf_op jit(solution)/shard_map/ppermute | solution.py:21
  44.2 0.6 collective-permute-start.15
  44.8 0.7 collective-permute-done.10.refs_2_
  45.5 1.4 %absorb.1 = (f32[512,128]{1,0:T(8,128)S(1)}, f32[512,128]{1,0:T(8,128)S(1)}, f32[4,512,128]{2,1,0:T(8,128)S(1)}) custom-call(bf16[512,576]{1,0:T(8,128)(2,1)S(1)} %get-tuple-element.45.query_ref, s32[1,512]{1,0:T(1,128)S(1)} %get-tuple-element.46.slot_ref, f32[512,128]{1,0:T(8,128)S(1)} %get-tuple-element.49.top_ref, ...), custom_call_target="tpu_custom_call" | custom-call | flops 2000000000 | bytes 1000000 | tf_op jit(solution)/shard_map/absorb/pallas_call | solution.py:510
  47.0 0.1 collective-permute-done.17.refs_3_
  47.1 1.6 %collective-permute-done.16.refs_2_ = bf16[288,128]{1,0:T(8,128)(2,1)S(1)} collective-permute-done((bf16[288,128]{1,0:T(8,128)(2,1)S(1)}, bf16[288,128]{1,0:T(8,128)(2,1)S(1)}, u32[]{:S(2)}, u32[]{:S(2)}) %collective-permute-start.16) | collective-permute-done | bytes 73760 | tf_op jit(solution)/shard_map/ppermute | solution.py:21
  48.7 1.3 %attend.3.refs_0_ = bf16[16,2304]{1,0:T(8,128)(2,1)S(1)} custom-call(bf16[512,576]{1,0:T(8,128)(2,1)S(1)} %get-tuple-element.45.query_ref, s32[1,512]{1,0:T(1,128)S(1)} %get-tuple-element.46.slot_ref, f32[512,128]{1,0:T(8,128)S(1)} %get-tuple-element.65.top_ref, f32[512,128]{1,0:T(8,128)S(1)} %get-tuple-element.66.sum_ref, ...), custom_call_target="tpu_custom_call" | custom-call | tf_op jit(solution)/shard_map/attend/pallas_call | solution.py:543
  50.0 0.6 collective-permute-start.22
  50.6 1.2 %attend.2.refs_0_ = bf16[16,1792]{1,0:T(8,128)(2,1)S(1)} custom-call(bf16[512,576]{1,0:T(8,128)(2,1)S(1)} %get-tuple-element.45.query_ref, s32[1,512]{1,0:T(1,128)S(1)} %get-tuple-element.46.slot_ref, f32[512,128]{1,0:T(8,128)S(1)} %get-tuple-element.65.top_ref, f32[512,128]{1,0:T(8,128)S(1)} %get-tuple-element.66.sum_ref, ...), custom_call_target="tpu_custom_call" | custom-call | tf_op jit(solution)/shard_map/attend/pallas_call | solution.py:543
  51.8 2.4 %collective-permute-start.19 = (bf16[16,1792]{1,0:T(8,128)(2,1)S(1)}, bf16[16,1792]{1,0:T(8,128)(2,1)S(1)}, u32[]{:S(2)}, u32[]{:S(2)}) collective-permute-start(bf16[16,1792]{1,0:T(8,128)(2,1)S(1)} %attend.2.refs_0_), channel_id=1, source_target_pairs={{0,8},{4,12},{8,0},{12,4},{1,9},{5,13},{9,1},{13,5},{2,10},{6,14},... | collective-permute-start | bytes 172040 | tf_op jit(solution)/shard_map/ppermute | solution.py:21
  54.2 2.2 %collective-permute-done.22.refs_2_ = bf16[16,2304]{1,0:T(8,128)(2,1)S(1)} collective-permute-done((bf16[16,2304]{1,0:T(8,128)(2,1)S(1)}, bf16[16,2304]{1,0:T(8,128)(2,1)S(1)}, u32[]{:S(2)}, u32[]{:S(2)}) %collective-permute-start.22) | collective-permute-done | bytes 73760 | tf_op jit(solution)/shard_map/ppermute | solution.py:21
  56.3 2.0 %collective-permute-start.18 = (bf16[16,1792]{1,0:T(8,128)(2,1)S(1)}, bf16[16,1792]{1,0:T(8,128)(2,1)S(1)}, u32[]{:S(2)}, u32[]{:S(2)}) collective-permute-start(bf16[16,1792]{1,0:T(8,128)(2,1)S(1)} %attend.2.refs_0_), channel_id=1, source_target_pairs={{0,4},{4,0},{8,12},{12,8},{1,5},{5,1},{9,13},{13,9},{2,6},{6,2},{1... | collective-permute-start | bytes 172040 | tf_op jit(solution)/shard_map/ppermute | solution.py:21
  58.4 0.9 %collective-permute-start.20 = (bf16[16,1792]{1,0:T(8,128)(2,1)S(1)}, bf16[16,1792]{1,0:T(8,128)(2,1)S(1)}, u32[]{:S(2)}, u32[]{:S(2)}) collective-permute-start(bf16[16,1792]{1,0:T(8,128)(2,1)S(1)} %collective-permute-done.19.refs_2_), channel_id=1, source_target_pairs={{0,4},{4,0},{8,12},{12,8},{1,5},{5,1},{9,13},{13,9},{2,6},{6,2},{1... | collective-permute-start | bytes 172040 | tf_op jit(solution)/shard_map/ppermute | solution.py:21
  59.3 2.2 %collective-permute-done.23.refs_3_ = bf16[16,2304]{1,0:T(8,128)(2,1)S(1)} collective-permute-done((bf16[16,2304]{1,0:T(8,128)(2,1)S(1)}, bf16[16,2304]{1,0:T(8,128)(2,1)S(1)}, u32[]{:S(2)}, u32[]{:S(2)}) %collective-permute-start.23) | collective-permute-done | bytes 73760 | tf_op jit(solution)/shard_map/ppermute | solution.py:21
  61.5 1.6 %output_product.2.refs_5_ = f32[64,1792]{1,0:T(8,128)S(1)} custom-call(bf16[16,2304]{1,0:T(8,128)(2,1)S(1)} %attend.3.refs_0_, bf16[16,2304]{1,0:T(8,128)(2,1)S(1)} %collective-permute-done.21.refs_1_, bf16[16,2304]{1,0:T(8,128)(2,1)S(1)} %collective-permute-done.22.refs_2_, bf16[16,2304]{1,0:T(8,128)(2,1)S(1)} %collective-permute-done.23.refs_3_, ...), custom_call_target="tpu_custom_call" | custom-call | tf_op jit(solution)/shard_map/output_product/pallas_call | solution.py:597
  63.0 0.0 collective-permute-done.18.refs_1_
  63.1 0.0 collective-permute-done.20.refs_3_
  63.1 1.3 %output_product.3 = (f32[16,1792]{1,0:T(8,128)S(1)}, bf16[16,1792]{1,0:T(8,128)(2,1)S(1)}, bf16[16,1792]{1,0:T(8,128)(2,1)S(1)}, bf16[16,1792]{1,0:T(8,128)(2,1)S(1)}) custom-call(bf16[16,1792]{1,0:T(8,128)(2,1)S(1)} %attend.2.refs_0_, bf16[16,1792]{1,0:T(8,128)(2,1)S(1)} %collective-permute-done.18.refs_1_, ...), custom_call_target="tpu_custom_call" | custom-call | tf_op jit(solution)/shard_map/output_product/pallas_call | solution.py:597
  64.4 1.3 %collective-permute-start.24 = (bf16[16,1792]{1,0:T(8,128)(2,1)S(1)}, bf16[16,1792]{1,0:T(8,128)(2,1)S(1)}, u32[]{:S(2)}, u32[]{:S(2)}) collective-permute-start(bf16[16,1792]{1,0:T(8,128)(2,1)S(1)} %get-tuple-element.76), channel_id=1, source_target_pairs={{0,2},{1,3},{2,0},{3,1},{4,6},{5,7},{6,4},{7,5},{8,10},{9,11},{10,... | collective-permute-start | bytes 172040 | tf_op jit(solution)/shard_map/ppermute | solution.py:21
  65.7 0.9 %collective-permute-start.26 = (bf16[16,1792]{1,0:T(8,128)(2,1)S(1)}, bf16[16,1792]{1,0:T(8,128)(2,1)S(1)}, u32[]{:S(2)}, u32[]{:S(2)}) collective-permute-start(bf16[16,1792]{1,0:T(8,128)(2,1)S(1)} %get-tuple-element.78), channel_id=1, source_target_pairs={{0,1},{1,0},{2,3},{3,2},{4,5},{5,4},{6,7},{7,6},{8,9},{9,8},{10,11... | collective-permute-start | bytes 172040 | tf_op jit(solution)/shard_map/ppermute | solution.py:21
  66.6 2.0 %collective-permute-done.24 = bf16[16,1792]{1,0:T(8,128)(2,1)S(1)} collective-permute-done((bf16[16,1792]{1,0:T(8,128)(2,1)S(1)}, bf16[16,1792]{1,0:T(8,128)(2,1)S(1)}, u32[]{:S(2)}, u32[]{:S(2)}) %collective-permute-start.24) | collective-permute-done | bytes 57376 | tf_op jit(solution)/shard_map/ppermute | solution.py:21
  68.6 1.2 %collective-permute-done.25 = bf16[16,1792]{1,0:T(8,128)(2,1)S(1)} collective-permute-done((bf16[16,1792]{1,0:T(8,128)(2,1)S(1)}, bf16[16,1792]{1,0:T(8,128)(2,1)S(1)}, u32[]{:S(2)}, u32[]{:S(2)}) %collective-permute-start.25) | collective-permute-done | bytes 57376 | tf_op jit(solution)/shard_map/ppermute | solution.py:21
  69.8 0.7 add_convert_fusion
  (40 shorter events, 0.1 us)
Async XLA Ops:
  0.0 7.1 %copy-start.4 = (bf16[448,576]{1,0:T(8,128)(2,1)S(1)}, bf16[448,576]{1,0:T(8,128)(2,1)}, u32[]{:S(2)}) copy-start(bf16[448,576]{1,0:T(8,128)(2,1)} %value_ref) | copy-start | bytes 1548292
  1.4 19.4 %collective-permute-start.1 = (bf16[64,1792]{1,0:T(8,128)(2,1)S(1)}, bf16[64,1792]{1,0:T(8,128)(2,1)S(1)}, u32[]{:S(2)}, u32[]{:S(2)}) collective-permute-start(bf16[64,1792]{1,0:T(8,128)(2,1)S(1)} %get-tuple-element.56), channel_id=1, source_target_pairs={{0,12},{4,8},{8,4},{12,0},{1,13},{5,9},{9,5},{13,1},{2,14},{6,10},... | collective-permute-start | bytes 688136 | tf_op jit(solution)/shard_map/ppermute | solution.py:21
  6.5 19.5 %collective-permute-start.2 = (bf16[64,1792]{1,0:T(8,128)(2,1)S(1)}, bf16[64,1792]{1,0:T(8,128)(2,1)S(1)}, u32[]{:S(2)}, u32[]{:S(2)}) collective-permute-start(bf16[64,1792]{1,0:T(8,128)(2,1)S(1)} %get-tuple-element.57), channel_id=1, source_target_pairs={{0,8},{4,12},{8,0},{12,4},{1,9},{5,13},{9,1},{13,5},{2,10},{6,14},... | collective-permute-start | bytes 688136 | tf_op jit(solution)/shard_map/ppermute | solution.py:21
  6.5 19.5 %collective-permute-start.3 = (bf16[64,1792]{1,0:T(8,128)(2,1)S(1)}, bf16[64,1792]{1,0:T(8,128)(2,1)S(1)}, u32[]{:S(2)}, u32[]{:S(2)}) collective-permute-start(bf16[64,1792]{1,0:T(8,128)(2,1)S(1)} %get-tuple-element.58), channel_id=1, source_target_pairs={{0,4},{4,0},{8,12},{12,8},{1,5},{5,1},{9,13},{13,9},{2,6},{6,2},{1... | collective-permute-start | bytes 688136 | tf_op jit(solution)/shard_map/ppermute | solution.py:21
  7.1 2.2 %copy-start.1 = (bf16[32,128,512]{2,1,0:T(8,128)(2,1)S(1)}, bf16[32,128,512]{2,1,0:T(8,128)(2,1)}, u32[]{:S(2)}) copy-start(bf16[32,128,512]{2,1,0:T(8,128)(2,1)} %absorb_hbm.1) | copy-start | bytes 12582916
  7.1 3.5 %copy-start.2 = (bf16[32,512,128]{2,1,0:T(8,128)(2,1)S(1)}, bf16[32,512,128]{2,1,0:T(8,128)(2,1)}, u32[]{:S(2)}) copy-start(bf16[32,512,128]{2,1,0:T(8,128)(2,1)} %value_hbm.1) | copy-start | bytes 12582916
  7.1 4.1 %copy-start.3 = (bf16[8,256,576]{1,2,0:T(8,128)(2,1)S(1)}, bf16[8,256,576]{1,2,0:T(8,128)(2,1)}, u32[]{:S(2)}) copy-start(bf16[8,256,576]{1,2,0:T(8,128)(2,1)} %param.18) | copy-start | bytes 7077892
  7.1 4.1 %copy-start.5 = (bf16[8,2,32,192]{3,2,1,0:T(8,128)(2,1)S(1)}, bf16[8,2,32,192]{3,2,1,0:T(8,128)(2,1)}, u32[]{:S(2)}) copy-start(bf16[8,2,32,192]{3,2,1,0:T(8,128)(2,1)} %param.20) | copy-start | bytes 589828
  7.2 4.1 %copy-start.6 = (bf16[8,2,576]{2,1,0:T(2,128)(2,1)S(1)}, bf16[8,2,576]{2,1,0:T(2,128)(2,1)}, u32[]{:S(2)}) copy-start(bf16[8,2,576]{2,1,0:T(2,128)(2,1)} %fresh_hbm.1) | copy-start | bytes 55300
  7.2 4.1 %copy-start.7 = (s32[1024]{0:T(1024)S(1)}, s32[1024]{0:T(1024)}, u32[]{:S(2)}) copy-start(s32[1024]{0:T(1024)} %param.15) | copy-start | bytes 12292
  7.2 4.1 %copy-start.8 = (s32[16]{0:T(128)S(1)}, s32[16]{0:T(128)}, u32[]{:S(2)}) copy-start(s32[16]{0:T(128)} %length_hbm) | copy-start | bytes 196
  7.2 4.1 %copy-start.9 = (s32[16]{0:T(128)S(1)}, s32[16]{0:T(128)}, u32[]{:S(2)}) copy-start(s32[16]{0:T(128)} %slot_hbm.1) | copy-start | bytes 196
  7.3 13.0 %collective-permute-start = (bf16[2016,128]{1,0:T(8,128)(2,1)S(1)}, bf16[2016,128]{1,0:T(8,128)(2,1)S(1)}, u32[]{:S(2)}, u32[]{:S(2)}) collective-permute-start(bf16[2016,128]{1,0:T(8,128)(2,1)S(1)} %pack_weight.1.refs_0_), channel_id=1, source_target_pairs={{0,2},{1,3},{2,0},{3,1},{4,6},{5,7},{6,4},{7,5},{8,10},{9,11},{10,... | collective-permute-start | bytes 1548296 | tf_op jit(solution)/shard_map/ppermute | solution.py:21
  20.3 19.0 %copy-start = (f32[512]{0:T(512)S(1)}, f32[512]{0:T(512)}, u32[]{:S(2)}) copy-start(f32[512]{0:T(512)} %param.14) | copy-start | bytes 6148
  20.3 5.8 %collective-permute-start.4 = (bf16[2016,128]{1,0:T(8,128)(2,1)S(1)}, bf16[2016,128]{1,0:T(8,128)(2,1)S(1)}, u32[]{:S(2)}, u32[]{:S(2)}) collective-permute-start(bf16[2016,128]{1,0:T(8,128)(2,1)S(1)} %pack_weight.1.refs_0_), channel_id=1, source_target_pairs={{0,1},{1,0},{2,3},{3,2},{4,5},{5,4},{6,7},{7,6},{8,9},{9,8},{10,11... | collective-permute-start | bytes 1548296 | tf_op jit(solution)/shard_map/ppermute | solution.py:21
  20.3 5.8 %collective-permute-start.5 = (bf16[2016,128]{1,0:T(8,128)(2,1)S(1)}, bf16[2016,128]{1,0:T(8,128)(2,1)S(1)}, u32[]{:S(2)}, u32[]{:S(2)}) collective-permute-start(bf16[2016,128]{1,0:T(8,128)(2,1)S(1)} %collective-permute-done.refs_2_), channel_id=1, source_target_pairs={{0,1},{1,0},{2,3},{3,2},{4,5},{5,4},{6,7},{7,6},{8,9},{9,8},{10,11... | collective-permute-start | bytes 1548296 | tf_op jit(solution)/shard_map/ppermute | solution.py:21
  27.8 6.9 %collective-permute-start.6 = (bf16[288,128]{1,0:T(8,128)(2,1)S(1)}, bf16[288,128]{1,0:T(8,128)(2,1)S(1)}, u32[]{:S(2)}, u32[]{:S(2)}) collective-permute-start(bf16[288,128]{1,0:T(8,128)(2,1)S(1)} %get-tuple-element.62), channel_id=1, source_target_pairs={{0,12},{4,8},{8,4},{12,0},{1,13},{5,9},{9,5},{13,1},{2,14},{6,10},... | collective-permute-start | bytes 221192 | tf_op jit(solution)/shard_map/ppermute | solution.py:21
  30.3 9.0 %collective-permute-start.7 = (bf16[288,128]{1,0:T(8,128)(2,1)S(1)}, bf16[288,128]{1,0:T(8,128)(2,1)S(1)}, u32[]{:S(2)}, u32[]{:S(2)}) collective-permute-start(bf16[288,128]{1,0:T(8,128)(2,1)S(1)} %get-tuple-element.63), channel_id=1, source_target_pairs={{0,8},{4,12},{8,0},{12,4},{1,9},{5,13},{9,1},{13,5},{2,10},{6,14},... | collective-permute-start | bytes 221192 | tf_op jit(solution)/shard_map/ppermute | solution.py:21
  30.3 9.0 %collective-permute-start.8 = (bf16[288,128]{1,0:T(8,128)(2,1)S(1)}, bf16[288,128]{1,0:T(8,128)(2,1)S(1)}, u32[]{:S(2)}, u32[]{:S(2)}) collective-permute-start(bf16[288,128]{1,0:T(8,128)(2,1)S(1)} %get-tuple-element.64), channel_id=1, source_target_pairs={{0,4},{4,0},{8,12},{12,8},{1,5},{5,1},{9,13},{13,9},{2,6},{6,2},{1... | collective-permute-start | bytes 221192 | tf_op jit(solution)/shard_map/ppermute | solution.py:21
  32.2 8.9 %collective-permute-start.12 = (bf16[288,128]{1,0:T(8,128)(2,1)S(1)}, bf16[288,128]{1,0:T(8,128)(2,1)S(1)}, u32[]{:S(2)}, u32[]{:S(2)}) collective-permute-start(bf16[288,128]{1,0:T(8,128)(2,1)S(1)} %get-tuple-element.71), channel_id=1, source_target_pairs={{0,12},{4,8},{8,4},{12,0},{1,13},{5,9},{9,5},{13,1},{2,14},{6,10},... | collective-permute-start | bytes 221192 | tf_op jit(solution)/shard_map/ppermute | solution.py:21
  34.7 7.7 %collective-permute-start.13 = (bf16[288,128]{1,0:T(8,128)(2,1)S(1)}, bf16[288,128]{1,0:T(8,128)(2,1)S(1)}, u32[]{:S(2)}, u32[]{:S(2)}) collective-permute-start(bf16[288,128]{1,0:T(8,128)(2,1)S(1)} %get-tuple-element.72), channel_id=1, source_target_pairs={{0,8},{4,12},{8,0},{12,4},{1,9},{5,13},{9,1},{13,5},{2,10},{6,14},... | collective-permute-start | bytes 221192 | tf_op jit(solution)/shard_map/ppermute | solution.py:21
  34.7 7.7 %collective-permute-start.14 = (bf16[288,128]{1,0:T(8,128)(2,1)S(1)}, bf16[288,128]{1,0:T(8,128)(2,1)S(1)}, u32[]{:S(2)}, u32[]{:S(2)}) collective-permute-start(bf16[288,128]{1,0:T(8,128)(2,1)S(1)} %get-tuple-element.73), channel_id=1, source_target_pairs={{0,4},{4,0},{8,12},{12,8},{1,5},{5,1},{9,13},{13,9},{2,6},{6,2},{1... | collective-permute-start | bytes 221192 | tf_op jit(solution)/shard_map/ppermute | solution.py:21
  39.6 4.6 %collective-permute-start.11 = (bf16[288,128]{1,0:T(8,128)(2,1)S(1)}, bf16[288,128]{1,0:T(8,128)(2,1)S(1)}, u32[]{:S(2)}, u32[]{:S(2)}) collective-permute-start(bf16[288,128]{1,0:T(8,128)(2,1)S(1)} %finish_rows.2.refs_0_), channel_id=1, source_target_pairs={{0,2},{1,3},{2,0},{3,1},{4,6},{5,7},{6,4},{7,5},{8,10},{9,11},{10,... | collective-permute-start | bytes 221192 | tf_op jit(solution)/shard_map/ppermute | solution.py:21
  41.1 4.4 %collective-permute-start.10 = (bf16[288,128]{1,0:T(8,128)(2,1)S(1)}, bf16[288,128]{1,0:T(8,128)(2,1)S(1)}, u32[]{:S(2)}, u32[]{:S(2)}) collective-permute-start(bf16[288,128]{1,0:T(8,128)(2,1)S(1)} %finish_rows.2.refs_0_), channel_id=1, source_target_pairs={{0,3},{1,2},{2,1},{3,0},{4,7},{5,6},{6,5},{7,4},{8,11},{9,10},{10,... | collective-permute-start | bytes 221192 | tf_op jit(solution)/shard_map/ppermute | solution.py:21
  41.1 4.4 %collective-permute-start.9 = (bf16[288,128]{1,0:T(8,128)(2,1)S(1)}, bf16[288,128]{1,0:T(8,128)(2,1)S(1)}, u32[]{:S(2)}, u32[]{:S(2)}) collective-permute-start(bf16[288,128]{1,0:T(8,128)(2,1)S(1)} %finish_rows.2.refs_0_), channel_id=1, source_target_pairs={{0,1},{1,0},{2,3},{3,2},{4,5},{5,4},{6,7},{7,6},{8,9},{9,8},{10,11... | collective-permute-start | bytes 221192 | tf_op jit(solution)/shard_map/ppermute | solution.py:21
  42.6 4.5 %collective-permute-start.17 = (bf16[288,128]{1,0:T(8,128)(2,1)S(1)}, bf16[288,128]{1,0:T(8,128)(2,1)S(1)}, u32[]{:S(2)}, u32[]{:S(2)}) collective-permute-start(bf16[288,128]{1,0:T(8,128)(2,1)S(1)} %finish_rows.3.refs_0_), channel_id=1, source_target_pairs={{0,2},{1,3},{2,0},{3,1},{4,6},{5,7},{6,4},{7,5},{8,10},{9,11},{10,... | collective-permute-start | bytes 221192 | tf_op jit(solution)/shard_map/ppermute | solution.py:21
  44.2 4.5 %collective-permute-start.16 = (bf16[288,128]{1,0:T(8,128)(2,1)S(1)}, bf16[288,128]{1,0:T(8,128)(2,1)S(1)}, u32[]{:S(2)}, u32[]{:S(2)}) collective-permute-start(bf16[288,128]{1,0:T(8,128)(2,1)S(1)} %finish_rows.3.refs_0_), channel_id=1, source_target_pairs={{0,3},{1,2},{2,1},{3,0},{4,7},{5,6},{6,5},{7,4},{8,11},{9,10},{10,... | collective-permute-start | bytes 221192 | tf_op jit(solution)/shard_map/ppermute | solution.py:21
  44.2 4.5 %collective-permute-start.15 = (bf16[288,128]{1,0:T(8,128)(2,1)S(1)}, bf16[288,128]{1,0:T(8,128)(2,1)S(1)}, u32[]{:S(2)}, u32[]{:S(2)}) collective-permute-start(bf16[288,128]{1,0:T(8,128)(2,1)S(1)} %finish_rows.3.refs_0_), channel_id=1, source_target_pairs={{0,1},{1,0},{2,3},{3,2},{4,5},{5,4},{6,7},{7,6},{8,9},{9,8},{10,11... | collective-permute-start | bytes 221192 | tf_op jit(solution)/shard_map/ppermute | solution.py:21
  50.0 6.3 %collective-permute-start.22 = (bf16[16,2304]{1,0:T(8,128)(2,1)S(1)}, bf16[16,2304]{1,0:T(8,128)(2,1)S(1)}, u32[]{:S(2)}, u32[]{:S(2)}) collective-permute-start(bf16[16,2304]{1,0:T(8,128)(2,1)S(1)} %attend.3.refs_0_), channel_id=1, source_target_pairs={{0,8},{4,12},{8,0},{12,4},{1,9},{5,13},{9,1},{13,5},{2,10},{6,14},... | collective-permute-start | bytes 221192 | tf_op jit(solution)/shard_map/ppermute | solution.py:21
  51.8 6.6 %collective-permute-start.19 = (bf16[16,1792]{1,0:T(8,128)(2,1)S(1)}, bf16[16,1792]{1,0:T(8,128)(2,1)S(1)}, u32[]{:S(2)}, u32[]{:S(2)}) collective-permute-start(bf16[16,1792]{1,0:T(8,128)(2,1)S(1)} %attend.2.refs_0_), channel_id=1, source_target_pairs={{0,8},{4,12},{8,0},{12,4},{1,9},{5,13},{9,1},{13,5},{2,10},{6,14},... | collective-permute-start | bytes 172040 | tf_op jit(solution)/shard_map/ppermute | solution.py:21
  54.2 5.1 %collective-permute-start.21 = (bf16[16,2304]{1,0:T(8,128)(2,1)S(1)}, bf16[16,2304]{1,0:T(8,128)(2,1)S(1)}, u32[]{:S(2)}, u32[]{:S(2)}) collective-permute-start(bf16[16,2304]{1,0:T(8,128)(2,1)S(1)} %attend.3.refs_0_), channel_id=1, source_target_pairs={{0,4},{4,0},{8,12},{12,8},{1,5},{5,1},{9,13},{13,9},{2,6},{6,2},{1... | collective-permute-start | bytes 221192 | tf_op jit(solution)/shard_map/ppermute | solution.py:21
  56.3 5.1 %collective-permute-start.23 = (bf16[16,2304]{1,0:T(8,128)(2,1)S(1)}, bf16[16,2304]{1,0:T(8,128)(2,1)S(1)}, u32[]{:S(2)}, u32[]{:S(2)}) collective-permute-start(bf16[16,2304]{1,0:T(8,128)(2,1)S(1)} %collective-permute-done.22.refs_2_), channel_id=1, source_target_pairs={{0,4},{4,0},{8,12},{12,8},{1,5},{5,1},{9,13},{13,9},{2,6},{6,2},{1... | collective-permute-start | bytes 221192 | tf_op jit(solution)/shard_map/ppermute | solution.py:21
  56.3 6.7 %collective-permute-start.18 = (bf16[16,1792]{1,0:T(8,128)(2,1)S(1)}, bf16[16,1792]{1,0:T(8,128)(2,1)S(1)}, u32[]{:S(2)}, u32[]{:S(2)}) collective-permute-start(bf16[16,1792]{1,0:T(8,128)(2,1)S(1)} %attend.2.refs_0_), channel_id=1, source_target_pairs={{0,4},{4,0},{8,12},{12,8},{1,5},{5,1},{9,13},{13,9},{2,6},{6,2},{1... | collective-permute-start | bytes 172040 | tf_op jit(solution)/shard_map/ppermute | solution.py:21
  58.4 4.7 %collective-permute-start.20 = (bf16[16,1792]{1,0:T(8,128)(2,1)S(1)}, bf16[16,1792]{1,0:T(8,128)(2,1)S(1)}, u32[]{:S(2)}, u32[]{:S(2)}) collective-permute-start(bf16[16,1792]{1,0:T(8,128)(2,1)S(1)} %collective-permute-done.19.refs_2_), channel_id=1, source_target_pairs={{0,4},{4,0},{8,12},{12,8},{1,5},{5,1},{9,13},{13,9},{2,6},{6,2},{1... | collective-permute-start | bytes 172040 | tf_op jit(solution)/shard_map/ppermute | solution.py:21
  64.4 4.2 %collective-permute-start.24 = (bf16[16,1792]{1,0:T(8,128)(2,1)S(1)}, bf16[16,1792]{1,0:T(8,128)(2,1)S(1)}, u32[]{:S(2)}, u32[]{:S(2)}) collective-permute-start(bf16[16,1792]{1,0:T(8,128)(2,1)S(1)} %get-tuple-element.76), channel_id=1, source_target_pairs={{0,2},{1,3},{2,0},{3,1},{4,6},{5,7},{6,4},{7,5},{8,10},{9,11},{10,... | collective-permute-start | bytes 172040 | tf_op jit(solution)/shard_map/ppermute | solution.py:21
  65.7 4.1 %collective-permute-start.25 = (bf16[16,1792]{1,0:T(8,128)(2,1)S(1)}, bf16[16,1792]{1,0:T(8,128)(2,1)S(1)}, u32[]{:S(2)}, u32[]{:S(2)}) collective-permute-start(bf16[16,1792]{1,0:T(8,128)(2,1)S(1)} %get-tuple-element.77), channel_id=1, source_target_pairs={{0,3},{1,2},{2,1},{3,0},{4,7},{5,6},{6,5},{7,4},{8,11},{9,10},{10,... | collective-permute-start | bytes 172040 | tf_op jit(solution)/shard_map/ppermute | solution.py:21
  65.7 4.1 %collective-permute-start.26 = (bf16[16,1792]{1,0:T(8,128)(2,1)S(1)}, bf16[16,1792]{1,0:T(8,128)(2,1)S(1)}, u32[]{:S(2)}, u32[]{:S(2)}) collective-permute-start(bf16[16,1792]{1,0:T(8,128)(2,1)S(1)} %get-tuple-element.78), channel_id=1, source_target_pairs={{0,1},{1,0},{2,3},{3,2},{4,5},{5,4},{6,7},{7,6},{8,9},{9,8},{10,11... | collective-permute-start | bytes 172040 | tf_op jit(solution)/shard_map/ppermute | solution.py:21

commit v15 on v13

--- a/solution.py
+++ b/solution.py
@@ -681,7 +681,7 @@
         if which == 0:
             state = absorb(layout, which, query_full, row_slot, *state, pieces)
     product, first_head, head_count = None, 0, value_absorb.shape[0]
-    for part_heads in (head_count * 9 // 16, head_count * 7 // 16):
+    for part_heads in (head_count // 2, head_count // 2):
         head_out = attend(
             layout, 1, query_full, row_slot, *state, live, value_here, pieces, first_head,
             part_heads,

time: 70.4 us -> 70.3 us (level)
  transfers between devices with their start and end apart: 27 -> 27, of which waited for: 11 -> 12; matrix products, arithmetic and copies ran while one was open for 0% -> 0% of each run, Pallas kernels for 18% -> 17%
where the time goes in v15:
time: 70.3 us; the launch traced here: 70.2 us
  starting transfers between devices  29.5 us (42%)
  waiting for transfers between devices  19.7 us (28%)
  Pallas kernels  17.9 us (25%)
  local copies, waits for them, and re-layouts  2.31 us (3%)
    ppermute x27, starting transfers between devices, swap(): return lax.ppermute(value, axis, [(i, i ^ step) for i in range(count)])  29.5 us
    ppermute x27, waiting for transfers between devices, swap(): return lax.ppermute(value, axis, [(i, i ^ step) for i in range(count)])  19.7 us
    pallas_call x1, Pallas kernels, prepare(): pl.pallas_call(functools.partial(prepare_kernel, scale, steps, (dev_count...  7.61 us
    pallas_call x2, Pallas kernels, output_product(): pl.pallas_call(functools.partial(output_kernel, dev_count, side_count, st...  2.84 us
    pallas_call x2, Pallas kernels, attend(): pl.pallas_call(functools.partial(attend_kernel, layout, which, first_head...  2.36 us
    unnamed x20, local copies, waits for them, and re-layouts  2.31 us
    pallas_call x1, Pallas kernels, project(): pl.pallas_call(functools.partial(project_kernel, dev_count, len(weights))...  1.7 us
    pallas_call x1, Pallas kernels, absorb(): pl.pallas_call(functools.partial(absorb_kernel, layout, which), out_shape...  1.44 us
  transfers between devices with their start and end apart: 27, of which 12 were waited for; matrix products, arithmetic and copies ran while one was open for 0% of the time, Pallas kernels for 17%

profile of v15, /device:TPU:0, one launch (start us, length us, event | category | flops | bytes accessed | tf_op | source)
XLA Modules:
  0.0 70.2 jit_solution(5206990628163691728)
XLA Ops:
  0.0 1.4 %split_columns.1 = (bf16[64,1792]{1,0:T(8,128)(2,1)S(1)}, bf16[64,1792]{1,0:T(8,128)(2,1)S(1)}, bf16[64,1792]{1,0:T(8,128)(2,1)S(1)}, bf16[64,1792]{1,0:T(8,128)(2,1)S(1)}) custom-call(bf16[64,7168]{1,0:T(8,128)(2,1)} %prompts_ref.1), custom_call_target="tpu_custom_call" | custom-call | flops 10000000000 | bytes 40000000 | tf_op jit(solution)/shard_map/split_columns/pallas_call | solution.py:100
  1.4 5.1 %collective-permute-start.1 = (bf16[64,1792]{1,0:T(8,128)(2,1)S(1)}, bf16[64,1792]{1,0:T(8,128)(2,1)S(1)}, u32[]{:S(2)}, u32[]{:S(2)}) collective-permute-start(bf16[64,1792]{1,0:T(8,128)(2,1)S(1)} %get-tuple-element.56), channel_id=1, source_target_pairs={{0,12},{4,8},{8,4},{12,0},{1,13},{5,9},{9,5},{13,1},{2,14},{6,10},... | collective-permute-start | bytes 688136 | tf_op jit(solution)/shard_map/ppermute | solution.py:21
  6.5 0.6 collective-permute-start.3
  7.2 0.1 pack_weight.1.refs_0_
  7.3 1.7 %collective-permute-start = (bf16[2016,128]{1,0:T(8,128)(2,1)S(1)}, bf16[2016,128]{1,0:T(8,128)(2,1)S(1)}, u32[]{:S(2)}, u32[]{:S(2)}) collective-permute-start(bf16[2016,128]{1,0:T(8,128)(2,1)S(1)} %pack_weight.1.refs_0_), channel_id=1, source_target_pairs={{0,2},{1,3},{2,0},{3,1},{4,6},{5,7},{6,4},{7,5},{8,10},{9,11},{10,... | collective-permute-start | bytes 1548296 | tf_op jit(solution)/shard_map/ppermute | solution.py:21
  9.0 0.3 copy-done.1
  9.3 1.3 %copy-done.2 = bf16[32,512,128]{2,1,0:T(8,128)(2,1)S(1)} copy-done((bf16[32,512,128]{2,1,0:T(8,128)(2,1)S(1)}, bf16[32,512,128]{2,1,0:T(8,128)(2,1)}, u32[]{:S(2)}) %copy-start.2) | copy-done | bytes 4194328
  10.6 0.7 copy-done.3
  11.3 7.6 %prepare.1 = (bf16[512,576]{1,0:T(8,128)(2,1)S(1)}, f32[512,128]{1,0:T(8,128)S(1)}, f32[512,128]{1,0:T(8,128)S(1)}, f32[4,512,128]{2,1,0:T(8,128)S(1)}, f32[16,1...) custom-call(f32[1,32]{1,0:T(1,128)S(1)} %negate_power_fusion.inverse, ...), custom_call_target="tpu_custom_call" | custom-call | flops 40000000000 | bytes 28000000 | tf_op jit(solution)/shard_map/prepare/pallas_call | solution.py:323
  18.9 1.4 %collective-permute-done.refs_2_ = bf16[2016,128]{1,0:T(8,128)(2,1)S(1)} collective-permute-done((bf16[2016,128]{1,0:T(8,128)(2,1)S(1)}, bf16[2016,128]{1,0:T(8,128)(2,1)S(1)}, u32[]{:S(2)}, u32[]{:S(2)}) %collective-permute-start) | collective-permute-done | bytes 516128 | tf_op jit(solution)/shard_map/ppermute | solution.py:21
  20.3 0.5 collective-permute-start.5
  20.8 5.2 %collective-permute-done.2.refs_2_ = bf16[64,1792]{1,0:T(8,128)(2,1)S(1)} collective-permute-done((bf16[64,1792]{1,0:T(8,128)(2,1)S(1)}, bf16[64,1792]{1,0:T(8,128)(2,1)S(1)}, u32[]{:S(2)}, u32[]{:S(2)}) %collective-permute-start.2) | collective-permute-done | bytes 229408 | tf_op jit(solution)/shard_map/ppermute | solution.py:21
  26.0 0.1 stack_rows.1.x_ref
  26.1 1.7 %project.1 = (f32[288,128]{1,0:T(8,128)S(1)}, bf16[288,128]{1,0:T(8,128)(2,1)S(1)}, bf16[288,128]{1,0:T(8,128)(2,1)S(1)}, bf16[288,128]{1,0:T(8,128)(2,1)S(1)}, ...) custom-call(s32[1,256]{1,0:T(1,128)S(1)} %get-tuple-element.54.targe, ...), custom_call_target="tpu_custom_call" | custom-call | tf_op jit(solution)/shard_map/project/pallas_call | solution.py:405
  27.8 2.5 %collective-permute-start.6 = (bf16[288,128]{1,0:T(8,128)(2,1)S(1)}, bf16[288,128]{1,0:T(8,128)(2,1)S(1)}, u32[]{:S(2)}, u32[]{:S(2)}) collective-permute-start(bf16[288,128]{1,0:T(8,128)(2,1)S(1)} %get-tuple-element.62), channel_id=1, source_target_pairs={{0,12},{4,8},{8,4},{12,0},{1,13},{5,9},{9,5},{13,1},{2,14},{6,10},... | collective-permute-start | bytes 221192 | tf_op jit(solution)/shard_map/ppermute | solution.py:21
  30.3 1.9 %collective-permute-start.8 = (bf16[288,128]{1,0:T(8,128)(2,1)S(1)}, bf16[288,128]{1,0:T(8,128)(2,1)S(1)}, u32[]{:S(2)}, u32[]{:S(2)}) collective-permute-start(bf16[288,128]{1,0:T(8,128)(2,1)S(1)} %get-tuple-element.64), channel_id=1, source_target_pairs={{0,4},{4,0},{8,12},{12,8},{1,5},{5,1},{9,13},{13,9},{2,6},{6,2},{1... | collective-permute-start | bytes 221192 | tf_op jit(solution)/shard_map/ppermute | solution.py:21
  32.2 2.5 %collective-permute-start.12 = (bf16[288,128]{1,0:T(8,128)(2,1)S(1)}, bf16[288,128]{1,0:T(8,128)(2,1)S(1)}, u32[]{:S(2)}, u32[]{:S(2)}) collective-permute-start(bf16[288,128]{1,0:T(8,128)(2,1)S(1)} %get-tuple-element.71), channel_id=1, source_target_pairs={{0,12},{4,8},{8,4},{12,0},{1,13},{5,9},{9,5},{13,1},{2,14},{6,10},... | collective-permute-start | bytes 221192 | tf_op jit(solution)/shard_map/ppermute | solution.py:21
  34.7 1.9 %collective-permute-start.14 = (bf16[288,128]{1,0:T(8,128)(2,1)S(1)}, bf16[288,128]{1,0:T(8,128)(2,1)S(1)}, u32[]{:S(2)}, u32[]{:S(2)}) collective-permute-start(bf16[288,128]{1,0:T(8,128)(2,1)S(1)} %get-tuple-element.73), channel_id=1, source_target_pairs={{0,4},{4,0},{8,12},{12,8},{1,5},{5,1},{9,13},{13,9},{2,6},{6,2},{1... | collective-permute-start | bytes 221192 | tf_op jit(solution)/shard_map/ppermute | solution.py:21
  36.6 2.7 %collective-permute-done.7.refs_2_ = bf16[288,128]{1,0:T(8,128)(2,1)S(1)} collective-permute-done((bf16[288,128]{1,0:T(8,128)(2,1)S(1)}, bf16[288,128]{1,0:T(8,128)(2,1)S(1)}, u32[]{:S(2)}, u32[]{:S(2)}) %collective-permute-start.7) | collective-permute-done | bytes 73760 | tf_op jit(solution)/shard_map/ppermute | solution.py:21
  39.4 0.2 finish_rows.2.refs_0_
  39.6 1.5 %collective-permute-start.11 = (bf16[288,128]{1,0:T(8,128)(2,1)S(1)}, bf16[288,128]{1,0:T(8,128)(2,1)S(1)}, u32[]{:S(2)}, u32[]{:S(2)}) collective-permute-start(bf16[288,128]{1,0:T(8,128)(2,1)S(1)} %finish_rows.2.refs_0_), channel_id=1, source_target_pairs={{0,2},{1,3},{2,0},{3,1},{4,6},{5,7},{6,4},{7,5},{8,10},{9,11},{10,... | collective-permute-start | bytes 221192 | tf_op jit(solution)/shard_map/ppermute | solution.py:21
  41.1 0.7 collective-permute-start.9
  41.8 0.7 collective-permute-done.13.refs_2_
  42.4 0.2 finish_rows.3.refs_0_
  42.7 1.5 %collective-permute-start.17 = (bf16[288,128]{1,0:T(8,128)(2,1)S(1)}, bf16[288,128]{1,0:T(8,128)(2,1)S(1)}, u32[]{:S(2)}, u32[]{:S(2)}) collective-permute-start(bf16[288,128]{1,0:T(8,128)(2,1)S(1)} %finish_rows.3.refs_0_), channel_id=1, source_target_pairs={{0,2},{1,3},{2,0},{3,1},{4,6},{5,7},{6,4},{7,5},{8,10},{9,11},{10,... | collective-permute-start | bytes 221192 | tf_op jit(solution)/shard_map/ppermute | solution.py:21
  44.2 0.6 collective-permute-start.15
  44.9 0.7 %collective-permute-done.10.refs_2_ = bf16[288,128]{1,0:T(8,128)(2,1)S(1)} collective-permute-done((bf16[288,128]{1,0:T(8,128)(2,1)S(1)}, bf16[288,128]{1,0:T(8,128)(2,1)S(1)}, u32[]{:S(2)}, u32[]{:S(2)}) %collective-permute-start.10) | collective-permute-done | bytes 73760 | tf_op jit(solution)/shard_map/ppermute | solution.py:21
  45.6 1.4 %absorb.1 = (f32[512,128]{1,0:T(8,128)S(1)}, f32[512,128]{1,0:T(8,128)S(1)}, f32[4,512,128]{2,1,0:T(8,128)S(1)}) custom-call(bf16[512,576]{1,0:T(8,128)(2,1)S(1)} %get-tuple-element.45.query_ref, s32[1,512]{1,0:T(1,128)S(1)} %get-tuple-element.46.slot_ref, f32[512,128]{1,0:T(8,128)S(1)} %get-tuple-element.49.top_ref, ...), custom_call_target="tpu_custom_call" | custom-call | flops 2000000000 | bytes 1000000 | tf_op jit(solution)/shard_map/absorb/pallas_call | solution.py:513
  47.0 0.1 collective-permute-done.17.refs_3_
  47.2 1.6 %collective-permute-done.16.refs_2_ = bf16[288,128]{1,0:T(8,128)(2,1)S(1)} collective-permute-done((bf16[288,128]{1,0:T(8,128)(2,1)S(1)}, bf16[288,128]{1,0:T(8,128)(2,1)S(1)}, u32[]{:S(2)}, u32[]{:S(2)}) %collective-permute-start.16) | collective-permute-done | bytes 73760 | tf_op jit(solution)/shard_map/ppermute | solution.py:21
  48.7 1.2 %attend.3.refs_0_ = bf16[16,2048]{1,0:T(8,128)(2,1)S(1)} custom-call(bf16[512,576]{1,0:T(8,128)(2,1)S(1)} %get-tuple-element.45.query_ref, s32[1,512]{1,0:T(1,128)S(1)} %get-tuple-element.46.slot_ref, f32[512,128]{1,0:T(8,128)S(1)} %get-tuple-element.65.top_ref, f32[512,128]{1,0:T(8,128)S(1)} %get-tuple-element.66.sum_ref, ...), custom_call_target="tpu_custom_call" | custom-call | tf_op jit(solution)/shard_map/attend/pallas_call | solution.py:546
  49.9 0.6 collective-permute-start.22
  50.6 1.2 %attend.2.refs_0_ = bf16[16,2048]{1,0:T(8,128)(2,1)S(1)} custom-call(bf16[512,576]{1,0:T(8,128)(2,1)S(1)} %get-tuple-element.45.query_ref, s32[1,512]{1,0:T(1,128)S(1)} %get-tuple-element.46.slot_ref, f32[512,128]{1,0:T(8,128)S(1)} %get-tuple-element.65.top_ref, f32[512,128]{1,0:T(8,128)S(1)} %get-tuple-element.66.sum_ref, ...), custom_call_target="tpu_custom_call" | custom-call | tf_op jit(solution)/shard_map/attend/pallas_call | solution.py:546
  51.7 2.4 %collective-permute-start.19 = (bf16[16,2048]{1,0:T(8,128)(2,1)S(1)}, bf16[16,2048]{1,0:T(8,128)(2,1)S(1)}, u32[]{:S(2)}, u32[]{:S(2)}) collective-permute-start(bf16[16,2048]{1,0:T(8,128)(2,1)S(1)} %attend.2.refs_0_), channel_id=1, source_target_pairs={{0,8},{4,12},{8,0},{12,4},{1,9},{5,13},{9,1},{13,5},{2,10},{6,14},... | collective-permute-start | bytes 196616 | tf_op jit(solution)/shard_map/ppermute | solution.py:21
  54.1 1.8 %collective-permute-done.22.refs_2_ = bf16[16,2048]{1,0:T(8,128)(2,1)S(1)} collective-permute-done((bf16[16,2048]{1,0:T(8,128)(2,1)S(1)}, bf16[16,2048]{1,0:T(8,128)(2,1)S(1)}, u32[]{:S(2)}, u32[]{:S(2)}) %collective-permute-start.22) | collective-permute-done | bytes 65568 | tf_op jit(solution)/shard_map/ppermute | solution.py:21
  55.9 0.2 collective-permute-start.23
  56.1 1.8 %collective-permute-start.18 = (bf16[16,2048]{1,0:T(8,128)(2,1)S(1)}, bf16[16,2048]{1,0:T(8,128)(2,1)S(1)}, u32[]{:S(2)}, u32[]{:S(2)}) collective-permute-start(bf16[16,2048]{1,0:T(8,128)(2,1)S(1)} %attend.2.refs_0_), channel_id=1, source_target_pairs={{0,4},{4,0},{8,12},{12,8},{1,5},{5,1},{9,13},{13,9},{2,6},{6,2},{1... | collective-permute-start | bytes 196616 | tf_op jit(solution)/shard_map/ppermute | solution.py:21
  58.0 1.3 %collective-permute-start.20 = (bf16[16,2048]{1,0:T(8,128)(2,1)S(1)}, bf16[16,2048]{1,0:T(8,128)(2,1)S(1)}, u32[]{:S(2)}, u32[]{:S(2)}) collective-permute-start(bf16[16,2048]{1,0:T(8,128)(2,1)S(1)} %collective-permute-done.19.refs_2_), channel_id=1, source_target_pairs={{0,4},{4,0},{8,12},{12,8},{1,5},{5,1},{9,13},{13,9},{2,6},{6,2},{1... | collective-permute-start | bytes 196616 | tf_op jit(solution)/shard_map/ppermute | solution.py:21
  59.3 1.5 %collective-permute-done.23.refs_3_ = bf16[16,2048]{1,0:T(8,128)(2,1)S(1)} collective-permute-done((bf16[16,2048]{1,0:T(8,128)(2,1)S(1)}, bf16[16,2048]{1,0:T(8,128)(2,1)S(1)}, u32[]{:S(2)}, u32[]{:S(2)}) %collective-permute-start.23) | collective-permute-done | bytes 65568 | tf_op jit(solution)/shard_map/ppermute | solution.py:21
  60.9 1.4 %output_product.2.refs_5_ = f32[64,1792]{1,0:T(8,128)S(1)} custom-call(bf16[16,2048]{1,0:T(8,128)(2,1)S(1)} %attend.3.refs_0_, bf16[16,2048]{1,0:T(8,128)(2,1)S(1)} %collective-permute-done.21.refs_1_, bf16[16,2048]{1,0:T(8,128)(2,1)S(1)} %collective-permute-done.22.refs_2_, bf16[16,2048]{1,0:T(8,128)(2,1)S(1)} %collective-permute-done.23.refs_3_, ...), custom_call_target="tpu_custom_call" | custom-call | tf_op jit(solution)/shard_map/output_product/pallas_call | solution.py:600
  62.3 0.5 collective-permute-done.20.refs_3_
  62.9 1.4 %output_product.3 = (f32[16,1792]{1,0:T(8,128)S(1)}, bf16[16,1792]{1,0:T(8,128)(2,1)S(1)}, bf16[16,1792]{1,0:T(8,128)(2,1)S(1)}, bf16[16,1792]{1,0:T(8,128)(2,1)S(1)}) custom-call(bf16[16,2048]{1,0:T(8,128)(2,1)S(1)} %attend.2.refs_0_, bf16[16,2048]{1,0:T(8,128)(2,1)S(1)} %collective-permute-done.18.refs_1_, ...), custom_call_target="tpu_custom_call" | custom-call | tf_op jit(solution)/shard_map/output_product/pallas_call | solution.py:600
  64.3 0.3 collective-permute-start.24
  64.6 1.2 %collective-permute-start.25 = (bf16[16,1792]{1,0:T(8,128)(2,1)S(1)}, bf16[16,1792]{1,0:T(8,128)(2,1)S(1)}, u32[]{:S(2)}, u32[]{:S(2)}) collective-permute-start(bf16[16,1792]{1,0:T(8,128)(2,1)S(1)} %get-tuple-element.77), channel_id=1, source_target_pairs={{0,2},{1,3},{2,0},{3,1},{4,6},{5,7},{6,4},{7,5},{8,10},{9,11},{10,... | collective-permute-start | bytes 172040 | tf_op jit(solution)/shard_map/ppermute | solution.py:21
  65.8 0.5 collective-permute-start.26
  66.2 2.4 %collective-permute-done.24 = bf16[16,1792]{1,0:T(8,128)(2,1)S(1)} collective-permute-done((bf16[16,1792]{1,0:T(8,128)(2,1)S(1)}, bf16[16,1792]{1,0:T(8,128)(2,1)S(1)}, u32[]{:S(2)}, u32[]{:S(2)}) %collective-permute-start.24) | collective-permute-done | bytes 57376 | tf_op jit(solution)/shard_map/ppermute | solution.py:21
  68.6 1.0 %collective-permute-done.25 = bf16[16,1792]{1,0:T(8,128)(2,1)S(1)} collective-permute-done((bf16[16,1792]{1,0:T(8,128)(2,1)S(1)}, bf16[16,1792]{1,0:T(8,128)(2,1)S(1)}, u32[]{:S(2)}, u32[]{:S(2)}) %collective-permute-start.25) | collective-permute-done | bytes 57376 | tf_op jit(solution)/shard_map/ppermute | solution.py:21
  69.5 0.7 add_convert_fusion
  (40 shorter events, 0.2 us)
Async XLA Ops:
  0.0 7.1 %copy-start.4 = (bf16[448,576]{1,0:T(8,128)(2,1)S(1)}, bf16[448,576]{1,0:T(8,128)(2,1)}, u32[]{:S(2)}) copy-start(bf16[448,576]{1,0:T(8,128)(2,1)} %value_ref) | copy-start | bytes 1548292
  1.4 19.4 %collective-permute-start.1 = (bf16[64,1792]{1,0:T(8,128)(2,1)S(1)}, bf16[64,1792]{1,0:T(8,128)(2,1)S(1)}, u32[]{:S(2)}, u32[]{:S(2)}) collective-permute-start(bf16[64,1792]{1,0:T(8,128)(2,1)S(1)} %get-tuple-element.56), channel_id=1, source_target_pairs={{0,12},{4,8},{8,4},{12,0},{1,13},{5,9},{9,5},{13,1},{2,14},{6,10},... | collective-permute-start | bytes 688136 | tf_op jit(solution)/shard_map/ppermute | solution.py:21
  6.5 19.5 %collective-permute-start.2 = (bf16[64,1792]{1,0:T(8,128)(2,1)S(1)}, bf16[64,1792]{1,0:T(8,128)(2,1)S(1)}, u32[]{:S(2)}, u32[]{:S(2)}) collective-permute-start(bf16[64,1792]{1,0:T(8,128)(2,1)S(1)} %get-tuple-element.57), channel_id=1, source_target_pairs={{0,8},{4,12},{8,0},{12,4},{1,9},{5,13},{9,1},{13,5},{2,10},{6,14},... | collective-permute-start | bytes 688136 | tf_op jit(solution)/shard_map/ppermute | solution.py:21
  6.5 19.5 %collective-permute-start.3 = (bf16[64,1792]{1,0:T(8,128)(2,1)S(1)}, bf16[64,1792]{1,0:T(8,128)(2,1)S(1)}, u32[]{:S(2)}, u32[]{:S(2)}) collective-permute-start(bf16[64,1792]{1,0:T(8,128)(2,1)S(1)} %get-tuple-element.58), channel_id=1, source_target_pairs={{0,4},{4,0},{8,12},{12,8},{1,5},{5,1},{9,13},{13,9},{2,6},{6,2},{1... | collective-permute-start | bytes 688136 | tf_op jit(solution)/shard_map/ppermute | solution.py:21
  7.1 2.2 %copy-start.1 = (bf16[32,128,512]{2,1,0:T(8,128)(2,1)S(1)}, bf16[32,128,512]{2,1,0:T(8,128)(2,1)}, u32[]{:S(2)}) copy-start(bf16[32,128,512]{2,1,0:T(8,128)(2,1)} %absorb_hbm.1) | copy-start | bytes 12582916
  7.1 3.5 %copy-start.2 = (bf16[32,512,128]{2,1,0:T(8,128)(2,1)S(1)}, bf16[32,512,128]{2,1,0:T(8,128)(2,1)}, u32[]{:S(2)}) copy-start(bf16[32,512,128]{2,1,0:T(8,128)(2,1)} %value_hbm.1) | copy-start | bytes 12582916
  7.1 4.1 %copy-start.3 = (bf16[8,256,576]{1,2,0:T(8,128)(2,1)S(1)}, bf16[8,256,576]{1,2,0:T(8,128)(2,1)}, u32[]{:S(2)}) copy-start(bf16[8,256,576]{1,2,0:T(8,128)(2,1)} %param.18) | copy-start | bytes 7077892
  7.1 4.1 %copy-start.5 = (bf16[8,2,32,192]{3,2,1,0:T(8,128)(2,1)S(1)}, bf16[8,2,32,192]{3,2,1,0:T(8,128)(2,1)}, u32[]{:S(2)}) copy-start(bf16[8,2,32,192]{3,2,1,0:T(8,128)(2,1)} %param.20) | copy-start | bytes 589828
  7.2 4.1 %copy-start.6 = (bf16[8,2,576]{2,1,0:T(2,128)(2,1)S(1)}, bf16[8,2,576]{2,1,0:T(2,128)(2,1)}, u32[]{:S(2)}) copy-start(bf16[8,2,576]{2,1,0:T(2,128)(2,1)} %fresh_hbm.1) | copy-start | bytes 55300
  7.2 4.1 %copy-start.7 = (s32[1024]{0:T(1024)S(1)}, s32[1024]{0:T(1024)}, u32[]{:S(2)}) copy-start(s32[1024]{0:T(1024)} %param.15) | copy-start | bytes 12292
  7.2 4.1 %copy-start.8 = (s32[16]{0:T(128)S(1)}, s32[16]{0:T(128)}, u32[]{:S(2)}) copy-start(s32[16]{0:T(128)} %length_hbm) | copy-start | bytes 196
  7.2 4.1 %copy-start.9 = (s32[16]{0:T(128)S(1)}, s32[16]{0:T(128)}, u32[]{:S(2)}) copy-start(s32[16]{0:T(128)} %slot_hbm.1) | copy-start | bytes 196
  7.3 13.0 %collective-permute-start = (bf16[2016,128]{1,0:T(8,128)(2,1)S(1)}, bf16[2016,128]{1,0:T(8,128)(2,1)S(1)}, u32[]{:S(2)}, u32[]{:S(2)}) collective-permute-start(bf16[2016,128]{1,0:T(8,128)(2,1)S(1)} %pack_weight.1.refs_0_), channel_id=1, source_target_pairs={{0,2},{1,3},{2,0},{3,1},{4,6},{5,7},{6,4},{7,5},{8,10},{9,11},{10,... | collective-permute-start | bytes 1548296 | tf_op jit(solution)/shard_map/ppermute | solution.py:21
  20.3 19.1 %copy-start = (f32[512]{0:T(512)S(1)}, f32[512]{0:T(512)}, u32[]{:S(2)}) copy-start(f32[512]{0:T(512)} %param.14) | copy-start | bytes 6148
  20.3 5.8 %collective-permute-start.4 = (bf16[2016,128]{1,0:T(8,128)(2,1)S(1)}, bf16[2016,128]{1,0:T(8,128)(2,1)S(1)}, u32[]{:S(2)}, u32[]{:S(2)}) collective-permute-start(bf16[2016,128]{1,0:T(8,128)(2,1)S(1)} %pack_weight.1.refs_0_), channel_id=1, source_target_pairs={{0,1},{1,0},{2,3},{3,2},{4,5},{5,4},{6,7},{7,6},{8,9},{9,8},{10,11... | collective-permute-start | bytes 1548296 | tf_op jit(solution)/shard_map/ppermute | solution.py:21
  20.3 5.8 %collective-permute-start.5 = (bf16[2016,128]{1,0:T(8,128)(2,1)S(1)}, bf16[2016,128]{1,0:T(8,128)(2,1)S(1)}, u32[]{:S(2)}, u32[]{:S(2)}) collective-permute-start(bf16[2016,128]{1,0:T(8,128)(2,1)S(1)} %collective-permute-done.refs_2_), channel_id=1, source_target_pairs={{0,1},{1,0},{2,3},{3,2},{4,5},{5,4},{6,7},{7,6},{8,9},{9,8},{10,11... | collective-permute-start | bytes 1548296 | tf_op jit(solution)/shard_map/ppermute | solution.py:21
  27.8 6.9 %collective-permute-start.6 = (bf16[288,128]{1,0:T(8,128)(2,1)S(1)}, bf16[288,128]{1,0:T(8,128)(2,1)S(1)}, u32[]{:S(2)}, u32[]{:S(2)}) collective-permute-start(bf16[288,128]{1,0:T(8,128)(2,1)S(1)} %get-tuple-element.62), channel_id=1, source_target_pairs={{0,12},{4,8},{8,4},{12,0},{1,13},{5,9},{9,5},{13,1},{2,14},{6,10},... | collective-permute-start | bytes 221192 | tf_op jit(solution)/shard_map/ppermute | solution.py:21
  30.3 9.0 %collective-permute-start.7 = (bf16[288,128]{1,0:T(8,128)(2,1)S(1)}, bf16[288,128]{1,0:T(8,128)(2,1)S(1)}, u32[]{:S(2)}, u32[]{:S(2)}) collective-permute-start(bf16[288,128]{1,0:T(8,128)(2,1)S(1)} %get-tuple-element.63), channel_id=1, source_target_pairs={{0,8},{4,12},{8,0},{12,4},{1,9},{5,13},{9,1},{13,5},{2,10},{6,14},... | collective-permute-start | bytes 221192 | tf_op jit(solution)/shard_map/ppermute | solution.py:21
  30.3 9.0 %collective-permute-start.8 = (bf16[288,128]{1,0:T(8,128)(2,1)S(1)}, bf16[288,128]{1,0:T(8,128)(2,1)S(1)}, u32[]{:S(2)}, u32[]{:S(2)}) collective-permute-start(bf16[288,128]{1,0:T(8,128)(2,1)S(1)} %get-tuple-element.64), channel_id=1, source_target_pairs={{0,4},{4,0},{8,12},{12,8},{1,5},{5,1},{9,13},{13,9},{2,6},{6,2},{1... | collective-permute-start | bytes 221192 | tf_op jit(solution)/shard_map/ppermute | solution.py:21
  32.2 8.9 %collective-permute-start.12 = (bf16[288,128]{1,0:T(8,128)(2,1)S(1)}, bf16[288,128]{1,0:T(8,128)(2,1)S(1)}, u32[]{:S(2)}, u32[]{:S(2)}) collective-permute-start(bf16[288,128]{1,0:T(8,128)(2,1)S(1)} %get-tuple-element.71), channel_id=1, source_target_pairs={{0,12},{4,8},{8,4},{12,0},{1,13},{5,9},{9,5},{13,1},{2,14},{6,10},... | collective-permute-start | bytes 221192 | tf_op jit(solution)/shard_map/ppermute | solution.py:21
  34.7 7.7 %collective-permute-start.13 = (bf16[288,128]{1,0:T(8,128)(2,1)S(1)}, bf16[288,128]{1,0:T(8,128)(2,1)S(1)}, u32[]{:S(2)}, u32[]{:S(2)}) collective-permute-start(bf16[288,128]{1,0:T(8,128)(2,1)S(1)} %get-tuple-element.72), channel_id=1, source_target_pairs={{0,8},{4,12},{8,0},{12,4},{1,9},{5,13},{9,1},{13,5},{2,10},{6,14},... | collective-permute-start | bytes 221192 | tf_op jit(solution)/shard_map/ppermute | solution.py:21
  34.7 7.7 %collective-permute-start.14 = (bf16[288,128]{1,0:T(8,128)(2,1)S(1)}, bf16[288,128]{1,0:T(8,128)(2,1)S(1)}, u32[]{:S(2)}, u32[]{:S(2)}) collective-permute-start(bf16[288,128]{1,0:T(8,128)(2,1)S(1)} %get-tuple-element.73), channel_id=1, source_target_pairs={{0,4},{4,0},{8,12},{12,8},{1,5},{5,1},{9,13},{13,9},{2,6},{6,2},{1... | collective-permute-start | bytes 221192 | tf_op jit(solution)/shard_map/ppermute | solution.py:21
  39.6 4.6 %collective-permute-start.11 = (bf16[288,128]{1,0:T(8,128)(2,1)S(1)}, bf16[288,128]{1,0:T(8,128)(2,1)S(1)}, u32[]{:S(2)}, u32[]{:S(2)}) collective-permute-start(bf16[288,128]{1,0:T(8,128)(2,1)S(1)} %finish_rows.2.refs_0_), channel_id=1, source_target_pairs={{0,2},{1,3},{2,0},{3,1},{4,6},{5,7},{6,4},{7,5},{8,10},{9,11},{10,... | collective-permute-start | bytes 221192 | tf_op jit(solution)/shard_map/ppermute | solution.py:21
  41.1 4.5 %collective-permute-start.10 = (bf16[288,128]{1,0:T(8,128)(2,1)S(1)}, bf16[288,128]{1,0:T(8,128)(2,1)S(1)}, u32[]{:S(2)}, u32[]{:S(2)}) collective-permute-start(bf16[288,128]{1,0:T(8,128)(2,1)S(1)} %finish_rows.2.refs_0_), channel_id=1, source_target_pairs={{0,3},{1,2},{2,1},{3,0},{4,7},{5,6},{6,5},{7,4},{8,11},{9,10},{10,... | collective-permute-start | bytes 221192 | tf_op jit(solution)/shard_map/ppermute | solution.py:21
  41.1 4.4 %collective-permute-start.9 = (bf16[288,128]{1,0:T(8,128)(2,1)S(1)}, bf16[288,128]{1,0:T(8,128)(2,1)S(1)}, u32[]{:S(2)}, u32[]{:S(2)}) collective-permute-start(bf16[288,128]{1,0:T(8,128)(2,1)S(1)} %finish_rows.2.refs_0_), channel_id=1, source_target_pairs={{0,1},{1,0},{2,3},{3,2},{4,5},{5,4},{6,7},{7,6},{8,9},{9,8},{10,11... | collective-permute-start | bytes 221192 | tf_op jit(solution)/shard_map/ppermute | solution.py:21
  42.7 4.5 %collective-permute-start.17 = (bf16[288,128]{1,0:T(8,128)(2,1)S(1)}, bf16[288,128]{1,0:T(8,128)(2,1)S(1)}, u32[]{:S(2)}, u32[]{:S(2)}) collective-permute-start(bf16[288,128]{1,0:T(8,128)(2,1)S(1)} %finish_rows.3.refs_0_), channel_id=1, source_target_pairs={{0,2},{1,3},{2,0},{3,1},{4,6},{5,7},{6,4},{7,5},{8,10},{9,11},{10,... | collective-permute-start | bytes 221192 | tf_op jit(solution)/shard_map/ppermute | solution.py:21
  44.2 4.5 %collective-permute-start.16 = (bf16[288,128]{1,0:T(8,128)(2,1)S(1)}, bf16[288,128]{1,0:T(8,128)(2,1)S(1)}, u32[]{:S(2)}, u32[]{:S(2)}) collective-permute-start(bf16[288,128]{1,0:T(8,128)(2,1)S(1)} %finish_rows.3.refs_0_), channel_id=1, source_target_pairs={{0,3},{1,2},{2,1},{3,0},{4,7},{5,6},{6,5},{7,4},{8,11},{9,10},{10,... | collective-permute-start | bytes 221192 | tf_op jit(solution)/shard_map/ppermute | solution.py:21
  44.2 4.5 %collective-permute-start.15 = (bf16[288,128]{1,0:T(8,128)(2,1)S(1)}, bf16[288,128]{1,0:T(8,128)(2,1)S(1)}, u32[]{:S(2)}, u32[]{:S(2)}) collective-permute-start(bf16[288,128]{1,0:T(8,128)(2,1)S(1)} %finish_rows.3.refs_0_), channel_id=1, source_target_pairs={{0,1},{1,0},{2,3},{3,2},{4,5},{5,4},{6,7},{7,6},{8,9},{9,8},{10,11... | collective-permute-start | bytes 221192 | tf_op jit(solution)/shard_map/ppermute | solution.py:21
  49.9 6.0 %collective-permute-start.22 = (bf16[16,2048]{1,0:T(8,128)(2,1)S(1)}, bf16[16,2048]{1,0:T(8,128)(2,1)S(1)}, u32[]{:S(2)}, u32[]{:S(2)}) collective-permute-start(bf16[16,2048]{1,0:T(8,128)(2,1)S(1)} %attend.3.refs_0_), channel_id=1, source_target_pairs={{0,8},{4,12},{8,0},{12,4},{1,9},{5,13},{9,1},{13,5},{2,10},{6,14},... | collective-permute-start | bytes 196616 | tf_op jit(solution)/shard_map/ppermute | solution.py:21
  51.7 6.3 %collective-permute-start.19 = (bf16[16,2048]{1,0:T(8,128)(2,1)S(1)}, bf16[16,2048]{1,0:T(8,128)(2,1)S(1)}, u32[]{:S(2)}, u32[]{:S(2)}) collective-permute-start(bf16[16,2048]{1,0:T(8,128)(2,1)S(1)} %attend.2.refs_0_), channel_id=1, source_target_pairs={{0,8},{4,12},{8,0},{12,4},{1,9},{5,13},{9,1},{13,5},{2,10},{6,14},... | collective-permute-start | bytes 196616 | tf_op jit(solution)/shard_map/ppermute | solution.py:21
  54.1 5.2 %collective-permute-start.21 = (bf16[16,2048]{1,0:T(8,128)(2,1)S(1)}, bf16[16,2048]{1,0:T(8,128)(2,1)S(1)}, u32[]{:S(2)}, u32[]{:S(2)}) collective-permute-start(bf16[16,2048]{1,0:T(8,128)(2,1)S(1)} %attend.3.refs_0_), channel_id=1, source_target_pairs={{0,4},{4,0},{8,12},{12,8},{1,5},{5,1},{9,13},{13,9},{2,6},{6,2},{1... | collective-permute-start | bytes 196616 | tf_op jit(solution)/shard_map/ppermute | solution.py:21
  55.9 5.0 %collective-permute-start.23 = (bf16[16,2048]{1,0:T(8,128)(2,1)S(1)}, bf16[16,2048]{1,0:T(8,128)(2,1)S(1)}, u32[]{:S(2)}, u32[]{:S(2)}) collective-permute-start(bf16[16,2048]{1,0:T(8,128)(2,1)S(1)} %collective-permute-done.22.refs_2_), channel_id=1, source_target_pairs={{0,4},{4,0},{8,12},{12,8},{1,5},{5,1},{9,13},{13,9},{2,6},{6,2},{1... | collective-permute-start | bytes 196616 | tf_op jit(solution)/shard_map/ppermute | solution.py:21
  56.1 6.2 %collective-permute-start.18 = (bf16[16,2048]{1,0:T(8,128)(2,1)S(1)}, bf16[16,2048]{1,0:T(8,128)(2,1)S(1)}, u32[]{:S(2)}, u32[]{:S(2)}) collective-permute-start(bf16[16,2048]{1,0:T(8,128)(2,1)S(1)} %attend.2.refs_0_), channel_id=1, source_target_pairs={{0,4},{4,0},{8,12},{12,8},{1,5},{5,1},{9,13},{13,9},{2,6},{6,2},{1... | collective-permute-start | bytes 196616 | tf_op jit(solution)/shard_map/ppermute | solution.py:21
  58.0 4.9 %collective-permute-start.20 = (bf16[16,2048]{1,0:T(8,128)(2,1)S(1)}, bf16[16,2048]{1,0:T(8,128)(2,1)S(1)}, u32[]{:S(2)}, u32[]{:S(2)}) collective-permute-start(bf16[16,2048]{1,0:T(8,128)(2,1)S(1)} %collective-permute-done.19.refs_2_), channel_id=1, source_target_pairs={{0,4},{4,0},{8,12},{12,8},{1,5},{5,1},{9,13},{13,9},{2,6},{6,2},{1... | collective-permute-start | bytes 196616 | tf_op jit(solution)/shard_map/ppermute | solution.py:21
  64.3 4.3 %collective-permute-start.24 = (bf16[16,1792]{1,0:T(8,128)(2,1)S(1)}, bf16[16,1792]{1,0:T(8,128)(2,1)S(1)}, u32[]{:S(2)}, u32[]{:S(2)}) collective-permute-start(bf16[16,1792]{1,0:T(8,128)(2,1)S(1)} %get-tuple-element.76), channel_id=1, source_target_pairs={{0,3},{1,2},{2,1},{3,0},{4,7},{5,6},{6,5},{7,4},{8,11},{9,10},{10,... | collective-permute-start | bytes 172040 | tf_op jit(solution)/shard_map/ppermute | solution.py:21
  64.6 5.0 %collective-permute-start.25 = (bf16[16,1792]{1,0:T(8,128)(2,1)S(1)}, bf16[16,1792]{1,0:T(8,128)(2,1)S(1)}, u32[]{:S(2)}, u32[]{:S(2)}) collective-permute-start(bf16[16,1792]{1,0:T(8,128)(2,1)S(1)} %get-tuple-element.77), channel_id=1, source_target_pairs={{0,2},{1,3},{2,0},{3,1},{4,6},{5,7},{6,4},{7,5},{8,10},{9,11},{10,... | collective-permute-start | bytes 172040 | tf_op jit(solution)/shard_map/ppermute | solution.py:21
  65.8 3.8 %collective-permute-start.26 = (bf16[16,1792]{1,0:T(8,128)(2,1)S(1)}, bf16[16,1792]{1,0:T(8,128)(2,1)S(1)}, u32[]{:S(2)}, u32[]{:S(2)}) collective-permute-start(bf16[16,1792]{1,0:T(8,128)(2,1)S(1)} %get-tuple-element.78), channel_id=1, source_target_pairs={{0,1},{1,0},{2,3},{3,2},{4,5},{5,4},{6,7},{7,6},{8,9},{9,8},{10,11... | collective-permute-start | bytes 172040 | tf_op jit(solution)/shard_map/ppermute | solution.py:21

commit v16 on v15

--- a/solution.py
+++ b/solution.py
@@ -350,11 +350,14 @@
       value, out_weight)
 
 
+def hop_order(count):
+    return [0, *range(2, count, 2), *range(3, count, 2), 1]
+
+
 def stack_kernel(*refs):
     out_ref = refs[-1]
     rows = refs[0].shape[0]
-    for n, ref in enumerate(refs[:-1]):
-        k = (len(refs) - 1 - n) % (len(refs) - 1)
+    for k, ref in zip(hop_order(len(refs) - 1), refs[:-1]):
         out_ref[k * rows : (k + 1) * rows, :] = ref[...]
 
 
@@ -368,7 +371,7 @@
         compiler_params=pltpu.CompilerParams(vmem_limit_bytes=8 * mib),
         cost_estimate=pl.CostEstimate(flops=2 * 10**10, bytes_accessed=10**6, transcendentals=0),
         name="stack_rows",
-    )(pieces[0], *pieces[:0:-1])
+    )(*[pieces[k] for k in hop_order(len(pieces))])
 
 
 def project_kernel(dev_count, side_count, target_ref, x_ref, *refs):
@@ -674,7 +677,9 @@
         half = list(routed[which * dev_count : (which + 1) * dev_count])
         for k in sorted(range(1, dev_count), reverse=True):
             half[k] = swap(half[k], "dev", k)
-        latent_rows = finish(half[:1] + half[:0:-1], latent_gain.reshape(1, -1), cosine, sine, which)
+        latent_rows = finish(
+            [half[k] for k in hop_order(dev_count)], latent_gain.reshape(1, -1), cosine, sine, which
+        )
         pieces = [
             swap(latent_rows, "side", k) if k else latent_rows for k in piece_order(side_count)
         ]

time: 70.3 us -> 71.3 us (1.014)
  starting transfers between devices: 29.5 us -> 31.2 us
  waiting for transfers between devices: 19.7 us -> 18.8 us
    ppermute x27, starting transfers between devices: 29.5 us -> 31.2 us  [swap(): return lax.ppermute(value, axis, [(i, i ^ step) for i in range(count)])]
    ppermute x27, waiting for transfers between devices: 19.7 us -> 18.8 us  [swap(): return lax.ppermute(value, axis, [(i, i ^ step) for i in range(count)])]
  transfers between devices with their start and end apart: 27 -> 27, of which waited for: 12 -> 15; matrix products, arithmetic and copies ran while one was open for 0% -> 0% of each run, Pallas kernels for 17% -> 17%
where the time goes in v16:
time: 71.3 us; the launch traced here: 71.2 us
  starting transfers between devices  31.2 us (44%)
  waiting for transfers between devices  18.8 us (26%)
  Pallas kernels  17.9 us (25%)
  local copies, waits for them, and re-layouts  2.45 us (3%)
    ppermute x27, starting transfers between devices, swap(): return lax.ppermute(value, axis, [(i, i ^ step) for i in range(count)])  31.2 us
    ppermute x27, waiting for transfers between devices, swap(): return lax.ppermute(value, axis, [(i, i ^ step) for i in range(count)])  18.8 us
    pallas_call x1, Pallas kernels, prepare(): pl.pallas_call(functools.partial(prepare_kernel, scale, steps, (dev_count...  7.61 us
    pallas_call x2, Pallas kernels, output_product(): pl.pallas_call(functools.partial(output_kernel, dev_count, side_count, st...  2.84 us
    unnamed x20, local copies, waits for them, and re-layouts  2.45 us
    pallas_call x2, Pallas kernels, attend(): pl.pallas_call(functools.partial(attend_kernel, layout, which, first_head...  2.36 us
    pallas_call x1, Pallas kernels, project(): pl.pallas_call(functools.partial(project_kernel, dev_count, len(weights))...  1.69 us
    pallas_call x1, Pallas kernels, absorb(): pl.pallas_call(functools.partial(absorb_kernel, layout, which), out_shape...  1.44 us
  transfers between devices with their start and end apart: 27, of which 15 were waited for; matrix products, arithmetic and copies ran while one was open for 0% of the time, Pallas kernels for 17%

profile of v16, /device:TPU:0, one launch (start us, length us, event | category | flops | bytes accessed | tf_op | source)
XLA Modules:
  0.0 71.2 jit_solution(4562676212791494504)
XLA Ops:
  0.0 1.4 %split_columns.1 = (bf16[64,1792]{1,0:T(8,128)(2,1)S(1)}, bf16[64,1792]{1,0:T(8,128)(2,1)S(1)}, bf16[64,1792]{1,0:T(8,128)(2,1)S(1)}, bf16[64,1792]{1,0:T(8,128)(2,1)S(1)}) custom-call(bf16[64,7168]{1,0:T(8,128)(2,1)} %prompts_ref.1), custom_call_target="tpu_custom_call" | custom-call | flops 10000000000 | bytes 40000000 | tf_op jit(solution)/shard_map/split_columns/pallas_call | solution.py:100
  1.4 4.1 %collective-permute-start.1 = (bf16[64,1792]{1,0:T(8,128)(2,1)S(1)}, bf16[64,1792]{1,0:T(8,128)(2,1)S(1)}, u32[]{:S(2)}, u32[]{:S(2)}) collective-permute-start(bf16[64,1792]{1,0:T(8,128)(2,1)S(1)} %get-tuple-element.56), channel_id=1, source_target_pairs={{0,8},{4,12},{8,0},{12,4},{1,9},{5,13},{9,1},{13,5},{2,10},{6,14},... | collective-permute-start | bytes 688136 | tf_op jit(solution)/shard_map/ppermute | solution.py:21
  5.5 1.3 %collective-permute-start.2 = (bf16[64,1792]{1,0:T(8,128)(2,1)S(1)}, bf16[64,1792]{1,0:T(8,128)(2,1)S(1)}, u32[]{:S(2)}, u32[]{:S(2)}) collective-permute-start(bf16[64,1792]{1,0:T(8,128)(2,1)S(1)} %get-tuple-element.57), channel_id=1, source_target_pairs={{0,12},{4,8},{8,4},{12,0},{1,13},{5,9},{9,5},{13,1},{2,14},{6,10},... | collective-permute-start | bytes 688136 | tf_op jit(solution)/shard_map/ppermute | solution.py:21
  6.8 0.2 collective-permute-start.3
  7.2 1.6 %collective-permute-start = (bf16[2016,128]{1,0:T(8,128)(2,1)S(1)}, bf16[2016,128]{1,0:T(8,128)(2,1)S(1)}, u32[]{:S(2)}, u32[]{:S(2)}) collective-permute-start(bf16[2016,128]{1,0:T(8,128)(2,1)S(1)} %pack_weight.1.refs_0_), channel_id=1, source_target_pairs={{0,2},{1,3},{2,0},{3,1},{4,6},{5,7},{6,4},{7,5},{8,10},{9,11},{10,... | collective-permute-start | bytes 1548296 | tf_op jit(solution)/shard_map/ppermute | solution.py:21
  8.8 0.5 copy-done.1
  9.2 1.3 %copy-done.2 = bf16[32,512,128]{2,1,0:T(8,128)(2,1)S(1)} copy-done((bf16[32,512,128]{2,1,0:T(8,128)(2,1)S(1)}, bf16[32,512,128]{2,1,0:T(8,128)(2,1)}, u32[]{:S(2)}) %copy-start.2) | copy-done | bytes 4194328
  10.5 0.7 copy-done.3
  11.2 7.6 %prepare.1 = (bf16[512,576]{1,0:T(8,128)(2,1)S(1)}, f32[512,128]{1,0:T(8,128)S(1)}, f32[512,128]{1,0:T(8,128)S(1)}, f32[4,512,128]{2,1,0:T(8,128)S(1)}, f32[16,1...) custom-call(f32[1,32]{1,0:T(1,128)S(1)} %negate_power_fusion.inverse, ...), custom_call_target="tpu_custom_call" | custom-call | flops 40000000000 | bytes 28000000 | tf_op jit(solution)/shard_map/prepare/pallas_call | solution.py:323
  18.8 1.4 %collective-permute-done.refs_2_ = bf16[2016,128]{1,0:T(8,128)(2,1)S(1)} collective-permute-done((bf16[2016,128]{1,0:T(8,128)(2,1)S(1)}, bf16[2016,128]{1,0:T(8,128)(2,1)S(1)}, u32[]{:S(2)}, u32[]{:S(2)}) %collective-permute-start) | collective-permute-done | bytes 516128 | tf_op jit(solution)/shard_map/ppermute | solution.py:21
  20.2 0.5 collective-permute-start.5
  20.7 1.1 %collective-permute-done.1.refs_1_ = bf16[64,1792]{1,0:T(8,128)(2,1)S(1)} collective-permute-done((bf16[64,1792]{1,0:T(8,128)(2,1)S(1)}, bf16[64,1792]{1,0:T(8,128)(2,1)S(1)}, u32[]{:S(2)}, u32[]{:S(2)}) %collective-permute-start.1) | collective-permute-done | bytes 229408 | tf_op jit(solution)/shard_map/ppermute | solution.py:21
  21.8 0.5 collective-permute-done.3.refs_3_
  22.4 0.5 collective-permute-done.5.refs_3_
  22.9 1.7 %project.1 = (f32[288,128]{1,0:T(8,128)S(1)}, bf16[288,128]{1,0:T(8,128)(2,1)S(1)}, bf16[288,128]{1,0:T(8,128)(2,1)S(1)}, bf16[288,128]{1,0:T(8,128)(2,1)S(1)}, ...) custom-call(s32[1,256]{1,0:T(1,128)S(1)} %get-tuple-element.54.targe, ...), custom_call_target="tpu_custom_call" | custom-call | tf_op jit(solution)/shard_map/project/pallas_call | solution.py:408
  24.5 5.8 %collective-permute-start.6 = (bf16[288,128]{1,0:T(8,128)(2,1)S(1)}, bf16[288,128]{1,0:T(8,128)(2,1)S(1)}, u32[]{:S(2)}, u32[]{:S(2)}) collective-permute-start(bf16[288,128]{1,0:T(8,128)(2,1)S(1)} %get-tuple-element.62), channel_id=1, source_target_pairs={{0,8},{4,12},{8,0},{12,4},{1,9},{5,13},{9,1},{13,5},{2,10},{6,14},... | collective-permute-start | bytes 221192 | tf_op jit(solution)/shard_map/ppermute | solution.py:21
  30.4 0.4 collective-permute-start.7
  30.8 0.2 collective-permute-start.8
  31.0 3.7 %collective-permute-start.12 = (bf16[288,128]{1,0:T(8,128)(2,1)S(1)}, bf16[288,128]{1,0:T(8,128)(2,1)S(1)}, u32[]{:S(2)}, u32[]{:S(2)}) collective-permute-start(bf16[288,128]{1,0:T(8,128)(2,1)S(1)} %get-tuple-element.71), channel_id=1, source_target_pairs={{0,8},{4,12},{8,0},{12,4},{1,9},{5,13},{9,1},{13,5},{2,10},{6,14},... | collective-permute-start | bytes 221192 | tf_op jit(solution)/shard_map/ppermute | solution.py:21
  34.7 0.4 collective-permute-start.13
  35.2 0.3 collective-permute-done.6.refs_1_
  35.5 1.9 %collective-permute-done.7.refs_2_ = bf16[288,128]{1,0:T(8,128)(2,1)S(1)} collective-permute-done((bf16[288,128]{1,0:T(8,128)(2,1)S(1)}, bf16[288,128]{1,0:T(8,128)(2,1)S(1)}, u32[]{:S(2)}, u32[]{:S(2)}) %collective-permute-start.7) | collective-permute-done | bytes 73760 | tf_op jit(solution)/shard_map/ppermute | solution.py:21
  37.4 0.2 finish_rows.2.refs_0_
  37.6 1.6 %collective-permute-start.11 = (bf16[288,128]{1,0:T(8,128)(2,1)S(1)}, bf16[288,128]{1,0:T(8,128)(2,1)S(1)}, u32[]{:S(2)}, u32[]{:S(2)}) collective-permute-start(bf16[288,128]{1,0:T(8,128)(2,1)S(1)} %finish_rows.2.refs_0_), channel_id=1, source_target_pairs={{0,2},{1,3},{2,0},{3,1},{4,6},{5,7},{6,4},{7,5},{8,10},{9,11},{10,... | collective-permute-start | bytes 221192 | tf_op jit(solution)/shard_map/ppermute | solution.py:21
  39.2 3.4 %collective-permute-done.12.refs_1_ = bf16[288,128]{1,0:T(8,128)(2,1)S(1)} collective-permute-done((bf16[288,128]{1,0:T(8,128)(2,1)S(1)}, bf16[288,128]{1,0:T(8,128)(2,1)S(1)}, u32[]{:S(2)}, u32[]{:S(2)}) %collective-permute-start.12) | collective-permute-done | bytes 73760 | tf_op jit(solution)/shard_map/ppermute | solution.py:21
  42.6 0.2 finish_rows.3.refs_0_
  42.8 1.5 %collective-permute-start.17 = (bf16[288,128]{1,0:T(8,128)(2,1)S(1)}, bf16[288,128]{1,0:T(8,128)(2,1)S(1)}, u32[]{:S(2)}, u32[]{:S(2)}) collective-permute-start(bf16[288,128]{1,0:T(8,128)(2,1)S(1)} %finish_rows.3.refs_0_), channel_id=1, source_target_pairs={{0,2},{1,3},{2,0},{3,1},{4,6},{5,7},{6,4},{7,5},{8,10},{9,11},{10,... | collective-permute-start | bytes 221192 | tf_op jit(solution)/shard_map/ppermute | solution.py:21
  44.4 0.4 collective-permute-start.16
  44.7 0.3 collective-permute-start.15
  45.0 1.4 %absorb.1 = (f32[512,128]{1,0:T(8,128)S(1)}, f32[512,128]{1,0:T(8,128)S(1)}, f32[4,512,128]{2,1,0:T(8,128)S(1)}) custom-call(bf16[512,576]{1,0:T(8,128)(2,1)S(1)} %get-tuple-element.45.query_ref, s32[1,512]{1,0:T(1,128)S(1)} %get-tuple-element.46.slot_ref, f32[512,128]{1,0:T(8,128)S(1)} %get-tuple-element.49.top_ref, ...), custom_call_target="tpu_custom_call" | custom-call | flops 2000000000 | bytes 1000000 | tf_op jit(solution)/shard_map/absorb/pallas_call | solution.py:516
  46.5 1.3 %collective-permute-done.17.refs_3_ = bf16[288,128]{1,0:T(8,128)(2,1)S(1)} collective-permute-done((bf16[288,128]{1,0:T(8,128)(2,1)S(1)}, bf16[288,128]{1,0:T(8,128)(2,1)S(1)}, u32[]{:S(2)}, u32[]{:S(2)}) %collective-permute-start.17) | collective-permute-done | bytes 73760 | tf_op jit(solution)/shard_map/ppermute | solution.py:21
  47.8 1.2 %collective-permute-done.16.refs_2_ = bf16[288,128]{1,0:T(8,128)(2,1)S(1)} collective-permute-done((bf16[288,128]{1,0:T(8,128)(2,1)S(1)}, bf16[288,128]{1,0:T(8,128)(2,1)S(1)}, u32[]{:S(2)}, u32[]{:S(2)}) %collective-permute-start.16) | collective-permute-done | bytes 73760 | tf_op jit(solution)/shard_map/ppermute | solution.py:21
  48.9 1.2 %attend.3.refs_0_ = bf16[16,2048]{1,0:T(8,128)(2,1)S(1)} custom-call(bf16[512,576]{1,0:T(8,128)(2,1)S(1)} %get-tuple-element.45.query_ref, s32[1,512]{1,0:T(1,128)S(1)} %get-tuple-element.46.slot_ref, f32[512,128]{1,0:T(8,128)S(1)} %get-tuple-element.65.top_ref, f32[512,128]{1,0:T(8,128)S(1)} %get-tuple-element.66.sum_ref, ...), custom_call_target="tpu_custom_call" | custom-call | tf_op jit(solution)/shard_map/attend/pallas_call | solution.py:549
  50.1 1.5 %collective-permute-start.22 = (bf16[16,2048]{1,0:T(8,128)(2,1)S(1)}, bf16[16,2048]{1,0:T(8,128)(2,1)S(1)}, u32[]{:S(2)}, u32[]{:S(2)}) collective-permute-start(bf16[16,2048]{1,0:T(8,128)(2,1)S(1)} %attend.3.refs_0_), channel_id=1, source_target_pairs={{0,8},{4,12},{8,0},{12,4},{1,9},{5,13},{9,1},{13,5},{2,10},{6,14},... | collective-permute-start | bytes 196616 | tf_op jit(solution)/shard_map/ppermute | solution.py:21
  51.6 1.2 %attend.2.refs_0_ = bf16[16,2048]{1,0:T(8,128)(2,1)S(1)} custom-call(bf16[512,576]{1,0:T(8,128)(2,1)S(1)} %get-tuple-element.45.query_ref, s32[1,512]{1,0:T(1,128)S(1)} %get-tuple-element.46.slot_ref, f32[512,128]{1,0:T(8,128)S(1)} %get-tuple-element.65.top_ref, f32[512,128]{1,0:T(8,128)S(1)} %get-tuple-element.66.sum_ref, ...), custom_call_target="tpu_custom_call" | custom-call | tf_op jit(solution)/shard_map/attend/pallas_call | solution.py:549
  52.8 1.5 %collective-permute-start.19 = (bf16[16,2048]{1,0:T(8,128)(2,1)S(1)}, bf16[16,2048]{1,0:T(8,128)(2,1)S(1)}, u32[]{:S(2)}, u32[]{:S(2)}) collective-permute-start(bf16[16,2048]{1,0:T(8,128)(2,1)S(1)} %attend.2.refs_0_), channel_id=1, source_target_pairs={{0,8},{4,12},{8,0},{12,4},{1,9},{5,13},{9,1},{13,5},{2,10},{6,14},... | collective-permute-start | bytes 196616 | tf_op jit(solution)/shard_map/ppermute | solution.py:21
  54.3 1.8 %collective-permute-start.21 = (bf16[16,2048]{1,0:T(8,128)(2,1)S(1)}, bf16[16,2048]{1,0:T(8,128)(2,1)S(1)}, u32[]{:S(2)}, u32[]{:S(2)}) collective-permute-start(bf16[16,2048]{1,0:T(8,128)(2,1)S(1)} %attend.3.refs_0_), channel_id=1, source_target_pairs={{0,4},{4,0},{8,12},{12,8},{1,5},{5,1},{9,13},{13,9},{2,6},{6,2},{1... | collective-permute-start | bytes 196616 | tf_op jit(solution)/shard_map/ppermute | solution.py:21
  56.1 1.6 %collective-permute-done.22.refs_2_ = bf16[16,2048]{1,0:T(8,128)(2,1)S(1)} collective-permute-done((bf16[16,2048]{1,0:T(8,128)(2,1)S(1)}, bf16[16,2048]{1,0:T(8,128)(2,1)S(1)}, u32[]{:S(2)}, u32[]{:S(2)}) %collective-permute-start.22) | collective-permute-done | bytes 65568 | tf_op jit(solution)/shard_map/ppermute | solution.py:21
  57.7 2.0 %collective-permute-start.18 = (bf16[16,2048]{1,0:T(8,128)(2,1)S(1)}, bf16[16,2048]{1,0:T(8,128)(2,1)S(1)}, u32[]{:S(2)}, u32[]{:S(2)}) collective-permute-start(bf16[16,2048]{1,0:T(8,128)(2,1)S(1)} %attend.2.refs_0_), channel_id=1, source_target_pairs={{0,4},{4,0},{8,12},{12,8},{1,5},{5,1},{9,13},{13,9},{2,6},{6,2},{1... | collective-permute-start | bytes 196616 | tf_op jit(solution)/shard_map/ppermute | solution.py:21
  59.8 0.7 collective-permute-done.21.refs_1_
  60.4 1.5 %collective-permute-done.23.refs_3_ = bf16[16,2048]{1,0:T(8,128)(2,1)S(1)} collective-permute-done((bf16[16,2048]{1,0:T(8,128)(2,1)S(1)}, bf16[16,2048]{1,0:T(8,128)(2,1)S(1)}, u32[]{:S(2)}, u32[]{:S(2)}) %collective-permute-start.23) | collective-permute-done | bytes 65568 | tf_op jit(solution)/shard_map/ppermute | solution.py:21
  62.0 1.4 %output_product.2.refs_5_ = f32[64,1792]{1,0:T(8,128)S(1)} custom-call(bf16[16,2048]{1,0:T(8,128)(2,1)S(1)} %attend.3.refs_0_, bf16[16,2048]{1,0:T(8,128)(2,1)S(1)} %collective-permute-done.21.refs_1_, bf16[16,2048]{1,0:T(8,128)(2,1)S(1)} %collective-permute-done.22.refs_2_, bf16[16,2048]{1,0:T(8,128)(2,1)S(1)} %collective-permute-done.23.refs_3_, ...), custom_call_target="tpu_custom_call" | custom-call | tf_op jit(solution)/shard_map/output_product/pallas_call | solution.py:603
  63.4 0.7 collective-permute-done.20.refs_3_
  64.1 1.4 %output_product.3 = (f32[16,1792]{1,0:T(8,128)S(1)}, bf16[16,1792]{1,0:T(8,128)(2,1)S(1)}, bf16[16,1792]{1,0:T(8,128)(2,1)S(1)}, bf16[16,1792]{1,0:T(8,128)(2,1)S(1)}) custom-call(bf16[16,2048]{1,0:T(8,128)(2,1)S(1)} %attend.2.refs_0_, bf16[16,2048]{1,0:T(8,128)(2,1)S(1)} %collective-permute-done.18.refs_1_, ...), custom_call_target="tpu_custom_call" | custom-call | tf_op jit(solution)/shard_map/output_product/pallas_call | solution.py:603
  65.6 2.0 %collective-permute-start.25 = (bf16[16,1792]{1,0:T(8,128)(2,1)S(1)}, bf16[16,1792]{1,0:T(8,128)(2,1)S(1)}, u32[]{:S(2)}, u32[]{:S(2)}) collective-permute-start(bf16[16,1792]{1,0:T(8,128)(2,1)S(1)} %get-tuple-element.77), channel_id=1, source_target_pairs={{0,2},{1,3},{2,0},{3,1},{4,6},{5,7},{6,4},{7,5},{8,10},{9,11},{10,... | collective-permute-start | bytes 172040 | tf_op jit(solution)/shard_map/ppermute | solution.py:21
  67.7 1.7 %collective-permute-done.24 = bf16[16,1792]{1,0:T(8,128)(2,1)S(1)} collective-permute-done((bf16[16,1792]{1,0:T(8,128)(2,1)S(1)}, bf16[16,1792]{1,0:T(8,128)(2,1)S(1)}, u32[]{:S(2)}, u32[]{:S(2)}) %collective-permute-start.24) | collective-permute-done | bytes 57376 | tf_op jit(solution)/shard_map/ppermute | solution.py:21
  69.3 1.2 %collective-permute-done.25 = bf16[16,1792]{1,0:T(8,128)(2,1)S(1)} collective-permute-done((bf16[16,1792]{1,0:T(8,128)(2,1)S(1)}, bf16[16,1792]{1,0:T(8,128)(2,1)S(1)}, u32[]{:S(2)}, u32[]{:S(2)}) %collective-permute-start.25) | collective-permute-done | bytes 57376 | tf_op jit(solution)/shard_map/ppermute | solution.py:21
  70.5 0.7 add_convert_fusion
  (40 shorter events, 0.4 us)
Async XLA Ops:
  0.0 7.1 %copy-start.4 = (bf16[448,576]{1,0:T(8,128)(2,1)S(1)}, bf16[448,576]{1,0:T(8,128)(2,1)}, u32[]{:S(2)}) copy-start(bf16[448,576]{1,0:T(8,128)(2,1)} %value_ref) | copy-start | bytes 1548292
  1.4 20.4 %collective-permute-start.1 = (bf16[64,1792]{1,0:T(8,128)(2,1)S(1)}, bf16[64,1792]{1,0:T(8,128)(2,1)S(1)}, u32[]{:S(2)}, u32[]{:S(2)}) collective-permute-start(bf16[64,1792]{1,0:T(8,128)(2,1)S(1)} %get-tuple-element.56), channel_id=1, source_target_pairs={{0,8},{4,12},{8,0},{12,4},{1,9},{5,13},{9,1},{13,5},{2,10},{6,14},... | collective-permute-start | bytes 688136 | tf_op jit(solution)/shard_map/ppermute | solution.py:21
  5.5 16.3 %collective-permute-start.2 = (bf16[64,1792]{1,0:T(8,128)(2,1)S(1)}, bf16[64,1792]{1,0:T(8,128)(2,1)S(1)}, u32[]{:S(2)}, u32[]{:S(2)}) collective-permute-start(bf16[64,1792]{1,0:T(8,128)(2,1)S(1)} %get-tuple-element.57), channel_id=1, source_target_pairs={{0,12},{4,8},{8,4},{12,0},{1,13},{5,9},{9,5},{13,1},{2,14},{6,10},... | collective-permute-start | bytes 688136 | tf_op jit(solution)/shard_map/ppermute | solution.py:21
  6.8 15.5 %collective-permute-start.3 = (bf16[64,1792]{1,0:T(8,128)(2,1)S(1)}, bf16[64,1792]{1,0:T(8,128)(2,1)S(1)}, u32[]{:S(2)}, u32[]{:S(2)}) collective-permute-start(bf16[64,1792]{1,0:T(8,128)(2,1)S(1)} %get-tuple-element.58), channel_id=1, source_target_pairs={{0,4},{4,0},{8,12},{12,8},{1,5},{5,1},{9,13},{13,9},{2,6},{6,2},{1... | collective-permute-start | bytes 688136 | tf_op jit(solution)/shard_map/ppermute | solution.py:21
  7.1 2.2 %copy-start.1 = (bf16[32,128,512]{2,1,0:T(8,128)(2,1)S(1)}, bf16[32,128,512]{2,1,0:T(8,128)(2,1)}, u32[]{:S(2)}) copy-start(bf16[32,128,512]{2,1,0:T(8,128)(2,1)} %absorb_hbm.1) | copy-start | bytes 12582916
  7.1 3.5 %copy-start.2 = (bf16[32,512,128]{2,1,0:T(8,128)(2,1)S(1)}, bf16[32,512,128]{2,1,0:T(8,128)(2,1)}, u32[]{:S(2)}) copy-start(bf16[32,512,128]{2,1,0:T(8,128)(2,1)} %value_hbm.1) | copy-start | bytes 12582916
  7.1 4.1 %copy-start.3 = (bf16[8,256,576]{1,2,0:T(8,128)(2,1)S(1)}, bf16[8,256,576]{1,2,0:T(8,128)(2,1)}, u32[]{:S(2)}) copy-start(bf16[8,256,576]{1,2,0:T(8,128)(2,1)} %param.18) | copy-start | bytes 7077892
  7.1 4.1 %copy-start.5 = (bf16[8,2,32,192]{3,2,1,0:T(8,128)(2,1)S(1)}, bf16[8,2,32,192]{3,2,1,0:T(8,128)(2,1)}, u32[]{:S(2)}) copy-start(bf16[8,2,32,192]{3,2,1,0:T(8,128)(2,1)} %param.20) | copy-start | bytes 589828
  7.1 4.1 %copy-start.6 = (bf16[8,2,576]{2,1,0:T(2,128)(2,1)S(1)}, bf16[8,2,576]{2,1,0:T(2,128)(2,1)}, u32[]{:S(2)}) copy-start(bf16[8,2,576]{2,1,0:T(2,128)(2,1)} %fresh_hbm.1) | copy-start | bytes 55300
  7.1 4.1 %copy-start.7 = (s32[1024]{0:T(1024)S(1)}, s32[1024]{0:T(1024)}, u32[]{:S(2)}) copy-start(s32[1024]{0:T(1024)} %param.15) | copy-start | bytes 12292
  7.1 4.1 %copy-start.8 = (s32[16]{0:T(128)S(1)}, s32[16]{0:T(128)}, u32[]{:S(2)}) copy-start(s32[16]{0:T(128)} %length_hbm) | copy-start | bytes 196
  7.1 4.1 %copy-start.9 = (s32[16]{0:T(128)S(1)}, s32[16]{0:T(128)}, u32[]{:S(2)}) copy-start(s32[16]{0:T(128)} %slot_hbm.1) | copy-start | bytes 196
  7.2 13.0 %collective-permute-start = (bf16[2016,128]{1,0:T(8,128)(2,1)S(1)}, bf16[2016,128]{1,0:T(8,128)(2,1)S(1)}, u32[]{:S(2)}, u32[]{:S(2)}) collective-permute-start(bf16[2016,128]{1,0:T(8,128)(2,1)S(1)} %pack_weight.1.refs_0_), channel_id=1, source_target_pairs={{0,2},{1,3},{2,0},{3,1},{4,6},{5,7},{6,4},{7,5},{8,10},{9,11},{10,... | collective-permute-start | bytes 1548296 | tf_op jit(solution)/shard_map/ppermute | solution.py:21
  20.2 17.2 %copy-start = (f32[512]{0:T(512)S(1)}, f32[512]{0:T(512)}, u32[]{:S(2)}) copy-start(f32[512]{0:T(512)} %param.14) | copy-start | bytes 6148
  20.2 2.2 %collective-permute-start.4 = (bf16[2016,128]{1,0:T(8,128)(2,1)S(1)}, bf16[2016,128]{1,0:T(8,128)(2,1)S(1)}, u32[]{:S(2)}, u32[]{:S(2)}) collective-permute-start(bf16[2016,128]{1,0:T(8,128)(2,1)S(1)} %pack_weight.1.refs_0_), channel_id=1, source_target_pairs={{0,1},{1,0},{2,3},{3,2},{4,5},{5,4},{6,7},{7,6},{8,9},{9,8},{10,11... | collective-permute-start | bytes 1548296 | tf_op jit(solution)/shard_map/ppermute | solution.py:21
  20.2 2.6 %collective-permute-start.5 = (bf16[2016,128]{1,0:T(8,128)(2,1)S(1)}, bf16[2016,128]{1,0:T(8,128)(2,1)S(1)}, u32[]{:S(2)}, u32[]{:S(2)}) collective-permute-start(bf16[2016,128]{1,0:T(8,128)(2,1)S(1)} %collective-permute-done.refs_2_), channel_id=1, source_target_pairs={{0,1},{1,0},{2,3},{3,2},{4,5},{5,4},{6,7},{7,6},{8,9},{9,8},{10,11... | collective-permute-start | bytes 1548296 | tf_op jit(solution)/shard_map/ppermute | solution.py:21
  24.5 10.9 %collective-permute-start.6 = (bf16[288,128]{1,0:T(8,128)(2,1)S(1)}, bf16[288,128]{1,0:T(8,128)(2,1)S(1)}, u32[]{:S(2)}, u32[]{:S(2)}) collective-permute-start(bf16[288,128]{1,0:T(8,128)(2,1)S(1)} %get-tuple-element.62), channel_id=1, source_target_pairs={{0,8},{4,12},{8,0},{12,4},{1,9},{5,13},{9,1},{13,5},{2,10},{6,14},... | collective-permute-start | bytes 221192 | tf_op jit(solution)/shard_map/ppermute | solution.py:21
  30.4 7.0 %collective-permute-start.7 = (bf16[288,128]{1,0:T(8,128)(2,1)S(1)}, bf16[288,128]{1,0:T(8,128)(2,1)S(1)}, u32[]{:S(2)}, u32[]{:S(2)}) collective-permute-start(bf16[288,128]{1,0:T(8,128)(2,1)S(1)} %get-tuple-element.63), channel_id=1, source_target_pairs={{0,12},{4,8},{8,4},{12,0},{1,13},{5,9},{9,5},{13,1},{2,14},{6,10},... | collective-permute-start | bytes 221192 | tf_op jit(solution)/shard_map/ppermute | solution.py:21
  30.8 6.6 %collective-permute-start.8 = (bf16[288,128]{1,0:T(8,128)(2,1)S(1)}, bf16[288,128]{1,0:T(8,128)(2,1)S(1)}, u32[]{:S(2)}, u32[]{:S(2)}) collective-permute-start(bf16[288,128]{1,0:T(8,128)(2,1)S(1)} %get-tuple-element.64), channel_id=1, source_target_pairs={{0,4},{4,0},{8,12},{12,8},{1,5},{5,1},{9,13},{13,9},{2,6},{6,2},{1... | collective-permute-start | bytes 221192 | tf_op jit(solution)/shard_map/ppermute | solution.py:21
  31.0 11.6 %collective-permute-start.12 = (bf16[288,128]{1,0:T(8,128)(2,1)S(1)}, bf16[288,128]{1,0:T(8,128)(2,1)S(1)}, u32[]{:S(2)}, u32[]{:S(2)}) collective-permute-start(bf16[288,128]{1,0:T(8,128)(2,1)S(1)} %get-tuple-element.71), channel_id=1, source_target_pairs={{0,8},{4,12},{8,0},{12,4},{1,9},{5,13},{9,1},{13,5},{2,10},{6,14},... | collective-permute-start | bytes 221192 | tf_op jit(solution)/shard_map/ppermute | solution.py:21
  34.7 7.8 %collective-permute-start.13 = (bf16[288,128]{1,0:T(8,128)(2,1)S(1)}, bf16[288,128]{1,0:T(8,128)(2,1)S(1)}, u32[]{:S(2)}, u32[]{:S(2)}) collective-permute-start(bf16[288,128]{1,0:T(8,128)(2,1)S(1)} %get-tuple-element.72), channel_id=1, source_target_pairs={{0,12},{4,8},{8,4},{12,0},{1,13},{5,9},{9,5},{13,1},{2,14},{6,10},... | collective-permute-start | bytes 221192 | tf_op jit(solution)/shard_map/ppermute | solution.py:21
  35.5 7.1 %collective-permute-start.14 = (bf16[288,128]{1,0:T(8,128)(2,1)S(1)}, bf16[288,128]{1,0:T(8,128)(2,1)S(1)}, u32[]{:S(2)}, u32[]{:S(2)}) collective-permute-start(bf16[288,128]{1,0:T(8,128)(2,1)S(1)} %get-tuple-element.73), channel_id=1, source_target_pairs={{0,4},{4,0},{8,12},{12,8},{1,5},{5,1},{9,13},{13,9},{2,6},{6,2},{1... | collective-permute-start | bytes 221192 | tf_op jit(solution)/shard_map/ppermute | solution.py:21
  37.6 7.1 %collective-permute-start.11 = (bf16[288,128]{1,0:T(8,128)(2,1)S(1)}, bf16[288,128]{1,0:T(8,128)(2,1)S(1)}, u32[]{:S(2)}, u32[]{:S(2)}) collective-permute-start(bf16[288,128]{1,0:T(8,128)(2,1)S(1)} %finish_rows.2.refs_0_), channel_id=1, source_target_pairs={{0,2},{1,3},{2,0},{3,1},{4,6},{5,7},{6,4},{7,5},{8,10},{9,11},{10,... | collective-permute-start | bytes 221192 | tf_op jit(solution)/shard_map/ppermute | solution.py:21
  39.2 5.9 %collective-permute-start.10 = (bf16[288,128]{1,0:T(8,128)(2,1)S(1)}, bf16[288,128]{1,0:T(8,128)(2,1)S(1)}, u32[]{:S(2)}, u32[]{:S(2)}) collective-permute-start(bf16[288,128]{1,0:T(8,128)(2,1)S(1)} %finish_rows.2.refs_0_), channel_id=1, source_target_pairs={{0,3},{1,2},{2,1},{3,0},{4,7},{5,6},{6,5},{7,4},{8,11},{9,10},{10,... | collective-permute-start | bytes 221192 | tf_op jit(solution)/shard_map/ppermute | solution.py:21
  42.6 2.4 %collective-permute-start.9 = (bf16[288,128]{1,0:T(8,128)(2,1)S(1)}, bf16[288,128]{1,0:T(8,128)(2,1)S(1)}, u32[]{:S(2)}, u32[]{:S(2)}) collective-permute-start(bf16[288,128]{1,0:T(8,128)(2,1)S(1)} %finish_rows.2.refs_0_), channel_id=1, source_target_pairs={{0,1},{1,0},{2,3},{3,2},{4,5},{5,4},{6,7},{7,6},{8,9},{9,8},{10,11... | collective-permute-start | bytes 221192 | tf_op jit(solution)/shard_map/ppermute | solution.py:21
  42.8 4.9 %collective-permute-start.17 = (bf16[288,128]{1,0:T(8,128)(2,1)S(1)}, bf16[288,128]{1,0:T(8,128)(2,1)S(1)}, u32[]{:S(2)}, u32[]{:S(2)}) collective-permute-start(bf16[288,128]{1,0:T(8,128)(2,1)S(1)} %finish_rows.3.refs_0_), channel_id=1, source_target_pairs={{0,2},{1,3},{2,0},{3,1},{4,6},{5,7},{6,4},{7,5},{8,10},{9,11},{10,... | collective-permute-start | bytes 221192 | tf_op jit(solution)/shard_map/ppermute | solution.py:21
  44.4 4.6 %collective-permute-start.16 = (bf16[288,128]{1,0:T(8,128)(2,1)S(1)}, bf16[288,128]{1,0:T(8,128)(2,1)S(1)}, u32[]{:S(2)}, u32[]{:S(2)}) collective-permute-start(bf16[288,128]{1,0:T(8,128)(2,1)S(1)} %finish_rows.3.refs_0_), channel_id=1, source_target_pairs={{0,3},{1,2},{2,1},{3,0},{4,7},{5,6},{6,5},{7,4},{8,11},{9,10},{10,... | collective-permute-start | bytes 221192 | tf_op jit(solution)/shard_map/ppermute | solution.py:21
  44.7 4.2 %collective-permute-start.15 = (bf16[288,128]{1,0:T(8,128)(2,1)S(1)}, bf16[288,128]{1,0:T(8,128)(2,1)S(1)}, u32[]{:S(2)}, u32[]{:S(2)}) collective-permute-start(bf16[288,128]{1,0:T(8,128)(2,1)S(1)} %finish_rows.3.refs_0_), channel_id=1, source_target_pairs={{0,1},{1,0},{2,3},{3,2},{4,5},{5,4},{6,7},{7,6},{8,9},{9,8},{10,11... | collective-permute-start | bytes 221192 | tf_op jit(solution)/shard_map/ppermute | solution.py:21
  50.1 7.6 %collective-permute-start.22 = (bf16[16,2048]{1,0:T(8,128)(2,1)S(1)}, bf16[16,2048]{1,0:T(8,128)(2,1)S(1)}, u32[]{:S(2)}, u32[]{:S(2)}) collective-permute-start(bf16[16,2048]{1,0:T(8,128)(2,1)S(1)} %attend.3.refs_0_), channel_id=1, source_target_pairs={{0,8},{4,12},{8,0},{12,4},{1,9},{5,13},{9,1},{13,5},{2,10},{6,14},... | collective-permute-start | bytes 196616 | tf_op jit(solution)/shard_map/ppermute | solution.py:21
  52.8 7.0 %collective-permute-start.19 = (bf16[16,2048]{1,0:T(8,128)(2,1)S(1)}, bf16[16,2048]{1,0:T(8,128)(2,1)S(1)}, u32[]{:S(2)}, u32[]{:S(2)}) collective-permute-start(bf16[16,2048]{1,0:T(8,128)(2,1)S(1)} %attend.2.refs_0_), channel_id=1, source_target_pairs={{0,8},{4,12},{8,0},{12,4},{1,9},{5,13},{9,1},{13,5},{2,10},{6,14},... | collective-permute-start | bytes 196616 | tf_op jit(solution)/shard_map/ppermute | solution.py:21
  54.3 6.2 %collective-permute-start.21 = (bf16[16,2048]{1,0:T(8,128)(2,1)S(1)}, bf16[16,2048]{1,0:T(8,128)(2,1)S(1)}, u32[]{:S(2)}, u32[]{:S(2)}) collective-permute-start(bf16[16,2048]{1,0:T(8,128)(2,1)S(1)} %attend.3.refs_0_), channel_id=1, source_target_pairs={{0,4},{4,0},{8,12},{12,8},{1,5},{5,1},{9,13},{13,9},{2,6},{6,2},{1... | collective-permute-start | bytes 196616 | tf_op jit(solution)/shard_map/ppermute | solution.py:21
  57.7 4.3 %collective-permute-start.23 = (bf16[16,2048]{1,0:T(8,128)(2,1)S(1)}, bf16[16,2048]{1,0:T(8,128)(2,1)S(1)}, u32[]{:S(2)}, u32[]{:S(2)}) collective-permute-start(bf16[16,2048]{1,0:T(8,128)(2,1)S(1)} %collective-permute-done.22.refs_2_), channel_id=1, source_target_pairs={{0,4},{4,0},{8,12},{12,8},{1,5},{5,1},{9,13},{13,9},{2,6},{6,2},{1... | collective-permute-start | bytes 196616 | tf_op jit(solution)/shard_map/ppermute | solution.py:21
  57.7 5.7 %collective-permute-start.18 = (bf16[16,2048]{1,0:T(8,128)(2,1)S(1)}, bf16[16,2048]{1,0:T(8,128)(2,1)S(1)}, u32[]{:S(2)}, u32[]{:S(2)}) collective-permute-start(bf16[16,2048]{1,0:T(8,128)(2,1)S(1)} %attend.2.refs_0_), channel_id=1, source_target_pairs={{0,4},{4,0},{8,12},{12,8},{1,5},{5,1},{9,13},{13,9},{2,6},{6,2},{1... | collective-permute-start | bytes 196616 | tf_op jit(solution)/shard_map/ppermute | solution.py:21
  59.7 4.3 %collective-permute-start.20 = (bf16[16,2048]{1,0:T(8,128)(2,1)S(1)}, bf16[16,2048]{1,0:T(8,128)(2,1)S(1)}, u32[]{:S(2)}, u32[]{:S(2)}) collective-permute-start(bf16[16,2048]{1,0:T(8,128)(2,1)S(1)} %collective-permute-done.19.refs_2_), channel_id=1, source_target_pairs={{0,4},{4,0},{8,12},{12,8},{1,5},{5,1},{9,13},{13,9},{2,6},{6,2},{1... | collective-permute-start | bytes 196616 | tf_op jit(solution)/shard_map/ppermute | solution.py:21
  65.5 3.8 %collective-permute-start.24 = (bf16[16,1792]{1,0:T(8,128)(2,1)S(1)}, bf16[16,1792]{1,0:T(8,128)(2,1)S(1)}, u32[]{:S(2)}, u32[]{:S(2)}) collective-permute-start(bf16[16,1792]{1,0:T(8,128)(2,1)S(1)} %get-tuple-element.76), channel_id=1, source_target_pairs={{0,3},{1,2},{2,1},{3,0},{4,7},{5,6},{6,5},{7,4},{8,11},{9,10},{10,... | collective-permute-start | bytes 172040 | tf_op jit(solution)/shard_map/ppermute | solution.py:21
  65.6 4.9 %collective-permute-start.25 = (bf16[16,1792]{1,0:T(8,128)(2,1)S(1)}, bf16[16,1792]{1,0:T(8,128)(2,1)S(1)}, u32[]{:S(2)}, u32[]{:S(2)}) collective-permute-start(bf16[16,1792]{1,0:T(8,128)(2,1)S(1)} %get-tuple-element.77), channel_id=1, source_target_pairs={{0,2},{1,3},{2,0},{3,1},{4,6},{5,7},{6,4},{7,5},{8,10},{9,11},{10,... | collective-permute-start | bytes 172040 | tf_op jit(solution)/shard_map/ppermute | solution.py:21
  67.6 2.9 %collective-permute-start.26 = (bf16[16,1792]{1,0:T(8,128)(2,1)S(1)}, bf16[16,1792]{1,0:T(8,128)(2,1)S(1)}, u32[]{:S(2)}, u32[]{:S(2)}) collective-permute-start(bf16[16,1792]{1,0:T(8,128)(2,1)S(1)} %get-tuple-element.78), channel_id=1, source_target_pairs={{0,1},{1,0},{2,3},{3,2},{4,5},{5,4},{6,7},{7,6},{8,9},{9,8},{10,11... | collective-permute-start | bytes 172040 | tf_op jit(solution)/shard_map/ppermute | solution.py:21

commit v17 on v15

--- a/solution.py
+++ b/solution.py
@@ -698,7 +698,7 @@
         )
         product = products[0]
     result = products[0]
-    for k in sorted(range(1, side_count), reverse=True):
+    for k in piece_order(side_count)[:0:-1]:
         result = result + swap(products[k], "side", k).astype(f32)
     return result.astype(bf16)
 

time: 70.3 us -> 70.6 us (level)
  no operation moved by 1% of the time
where the time goes in v17:
time: 70.6 us; the launch traced here: 70.4 us
  starting transfers between devices  29.8 us (42%)
  waiting for transfers between devices  19.6 us (28%)
  Pallas kernels  17.9 us (25%)
  local copies, waits for them, and re-layouts  2.31 us (3%)
    ppermute x27, starting transfers between devices, swap(): return lax.ppermute(value, axis, [(i, i ^ step) for i in range(count)])  29.8 us
    ppermute x27, waiting for transfers between devices, swap(): return lax.ppermute(value, axis, [(i, i ^ step) for i in range(count)])  19.6 us
    pallas_call x1, Pallas kernels, prepare(): pl.pallas_call(functools.partial(prepare_kernel, scale, steps, (dev_count...  7.61 us
    pallas_call x2, Pallas kernels, output_product(): pl.pallas_call(functools.partial(output_kernel, dev_count, side_count, st...  2.84 us
    pallas_call x2, Pallas kernels, attend(): pl.pallas_call(functools.partial(attend_kernel, layout, which, first_head...  2.36 us
    unnamed x20, local copies, waits for them, and re-layouts  2.31 us
    pallas_call x1, Pallas kernels, project(): pl.pallas_call(functools.partial(project_kernel, dev_count, len(weights))...  1.7 us
    pallas_call x1, Pallas kernels, absorb(): pl.pallas_call(functools.partial(absorb_kernel, layout, which), out_shape...  1.44 us
  transfers between devices with their start and end apart: 27, of which 12 were waited for; matrix products, arithmetic and copies ran while one was open for 0% of the time, Pallas kernels for 17%

profile of v17, /device:TPU:0, one launch (start us, length us, event | category | flops | bytes accessed | tf_op | source)
XLA Modules:
  0.0 70.4 jit_solution(874731348062802475)
XLA Ops:
  0.0 1.4 %split_columns.1 = (bf16[64,1792]{1,0:T(8,128)(2,1)S(1)}, bf16[64,1792]{1,0:T(8,128)(2,1)S(1)}, bf16[64,1792]{1,0:T(8,128)(2,1)S(1)}, bf16[64,1792]{1,0:T(8,128)(2,1)S(1)}) custom-call(bf16[64,7168]{1,0:T(8,128)(2,1)} %prompts_ref.1), custom_call_target="tpu_custom_call" | custom-call | flops 10000000000 | bytes 40000000 | tf_op jit(solution)/shard_map/split_columns/pallas_call | solution.py:100
  1.4 5.1 %collective-permute-start.1 = (bf16[64,1792]{1,0:T(8,128)(2,1)S(1)}, bf16[64,1792]{1,0:T(8,128)(2,1)S(1)}, u32[]{:S(2)}, u32[]{:S(2)}) collective-permute-start(bf16[64,1792]{1,0:T(8,128)(2,1)S(1)} %get-tuple-element.56), channel_id=1, source_target_pairs={{0,12},{4,8},{8,4},{12,0},{1,13},{5,9},{9,5},{13,1},{2,14},{6,10},... | collective-permute-start | bytes 688136 | tf_op jit(solution)/shard_map/ppermute | solution.py:21
  6.5 0.6 collective-permute-start.3
  7.2 0.1 pack_weight.1.refs_0_
  7.3 1.7 %collective-permute-start = (bf16[2016,128]{1,0:T(8,128)(2,1)S(1)}, bf16[2016,128]{1,0:T(8,128)(2,1)S(1)}, u32[]{:S(2)}, u32[]{:S(2)}) collective-permute-start(bf16[2016,128]{1,0:T(8,128)(2,1)S(1)} %pack_weight.1.refs_0_), channel_id=1, source_target_pairs={{0,2},{1,3},{2,0},{3,1},{4,6},{5,7},{6,4},{7,5},{8,10},{9,11},{10,... | collective-permute-start | bytes 1548296 | tf_op jit(solution)/shard_map/ppermute | solution.py:21
  9.0 0.3 copy-done.1
  9.3 1.3 %copy-done.2 = bf16[32,512,128]{2,1,0:T(8,128)(2,1)S(1)} copy-done((bf16[32,512,128]{2,1,0:T(8,128)(2,1)S(1)}, bf16[32,512,128]{2,1,0:T(8,128)(2,1)}, u32[]{:S(2)}) %copy-start.2) | copy-done | bytes 4194328
  10.6 0.7 copy-done.3
  11.3 7.6 %prepare.1 = (bf16[512,576]{1,0:T(8,128)(2,1)S(1)}, f32[512,128]{1,0:T(8,128)S(1)}, f32[512,128]{1,0:T(8,128)S(1)}, f32[4,512,128]{2,1,0:T(8,128)S(1)}, f32[16,1...) custom-call(f32[1,32]{1,0:T(1,128)S(1)} %negate_power_fusion.inverse, ...), custom_call_target="tpu_custom_call" | custom-call | flops 40000000000 | bytes 28000000 | tf_op jit(solution)/shard_map/prepare/pallas_call | solution.py:323
  18.9 1.4 %collective-permute-done.refs_2_ = bf16[2016,128]{1,0:T(8,128)(2,1)S(1)} collective-permute-done((bf16[2016,128]{1,0:T(8,128)(2,1)S(1)}, bf16[2016,128]{1,0:T(8,128)(2,1)S(1)}, u32[]{:S(2)}, u32[]{:S(2)}) %collective-permute-start) | collective-permute-done | bytes 516128 | tf_op jit(solution)/shard_map/ppermute | solution.py:21
  20.3 0.5 collective-permute-start.5
  20.8 5.2 %collective-permute-done.2.refs_2_ = bf16[64,1792]{1,0:T(8,128)(2,1)S(1)} collective-permute-done((bf16[64,1792]{1,0:T(8,128)(2,1)S(1)}, bf16[64,1792]{1,0:T(8,128)(2,1)S(1)}, u32[]{:S(2)}, u32[]{:S(2)}) %collective-permute-start.2) | collective-permute-done | bytes 229408 | tf_op jit(solution)/shard_map/ppermute | solution.py:21
  26.0 0.1 stack_rows.1.x_ref
  26.1 1.7 %project.1 = (f32[288,128]{1,0:T(8,128)S(1)}, bf16[288,128]{1,0:T(8,128)(2,1)S(1)}, bf16[288,128]{1,0:T(8,128)(2,1)S(1)}, bf16[288,128]{1,0:T(8,128)(2,1)S(1)}, ...) custom-call(s32[1,256]{1,0:T(1,128)S(1)} %get-tuple-element.54.targe, ...), custom_call_target="tpu_custom_call" | custom-call | tf_op jit(solution)/shard_map/project/pallas_call | solution.py:405
  27.8 2.5 %collective-permute-start.6 = (bf16[288,128]{1,0:T(8,128)(2,1)S(1)}, bf16[288,128]{1,0:T(8,128)(2,1)S(1)}, u32[]{:S(2)}, u32[]{:S(2)}) collective-permute-start(bf16[288,128]{1,0:T(8,128)(2,1)S(1)} %get-tuple-element.62), channel_id=1, source_target_pairs={{0,12},{4,8},{8,4},{12,0},{1,13},{5,9},{9,5},{13,1},{2,14},{6,10},... | collective-permute-start | bytes 221192 | tf_op jit(solution)/shard_map/ppermute | solution.py:21
  30.3 1.9 %collective-permute-start.8 = (bf16[288,128]{1,0:T(8,128)(2,1)S(1)}, bf16[288,128]{1,0:T(8,128)(2,1)S(1)}, u32[]{:S(2)}, u32[]{:S(2)}) collective-permute-start(bf16[288,128]{1,0:T(8,128)(2,1)S(1)} %get-tuple-element.64), channel_id=1, source_target_pairs={{0,4},{4,0},{8,12},{12,8},{1,5},{5,1},{9,13},{13,9},{2,6},{6,2},{1... | collective-permute-start | bytes 221192 | tf_op jit(solution)/shard_map/ppermute | solution.py:21
  32.2 2.5 %collective-permute-start.12 = (bf16[288,128]{1,0:T(8,128)(2,1)S(1)}, bf16[288,128]{1,0:T(8,128)(2,1)S(1)}, u32[]{:S(2)}, u32[]{:S(2)}) collective-permute-start(bf16[288,128]{1,0:T(8,128)(2,1)S(1)} %get-tuple-element.71), channel_id=1, source_target_pairs={{0,12},{4,8},{8,4},{12,0},{1,13},{5,9},{9,5},{13,1},{2,14},{6,10},... | collective-permute-start | bytes 221192 | tf_op jit(solution)/shard_map/ppermute | solution.py:21
  34.7 1.9 %collective-permute-start.14 = (bf16[288,128]{1,0:T(8,128)(2,1)S(1)}, bf16[288,128]{1,0:T(8,128)(2,1)S(1)}, u32[]{:S(2)}, u32[]{:S(2)}) collective-permute-start(bf16[288,128]{1,0:T(8,128)(2,1)S(1)} %get-tuple-element.73), channel_id=1, source_target_pairs={{0,4},{4,0},{8,12},{12,8},{1,5},{5,1},{9,13},{13,9},{2,6},{6,2},{1... | collective-permute-start | bytes 221192 | tf_op jit(solution)/shard_map/ppermute | solution.py:21
  36.6 2.7 %collective-permute-done.7.refs_2_ = bf16[288,128]{1,0:T(8,128)(2,1)S(1)} collective-permute-done((bf16[288,128]{1,0:T(8,128)(2,1)S(1)}, bf16[288,128]{1,0:T(8,128)(2,1)S(1)}, u32[]{:S(2)}, u32[]{:S(2)}) %collective-permute-start.7) | collective-permute-done | bytes 73760 | tf_op jit(solution)/shard_map/ppermute | solution.py:21
  39.4 0.2 finish_rows.2.refs_0_
  39.6 1.5 %collective-permute-start.11 = (bf16[288,128]{1,0:T(8,128)(2,1)S(1)}, bf16[288,128]{1,0:T(8,128)(2,1)S(1)}, u32[]{:S(2)}, u32[]{:S(2)}) collective-permute-start(bf16[288,128]{1,0:T(8,128)(2,1)S(1)} %finish_rows.2.refs_0_), channel_id=1, source_target_pairs={{0,2},{1,3},{2,0},{3,1},{4,6},{5,7},{6,4},{7,5},{8,10},{9,11},{10,... | collective-permute-start | bytes 221192 | tf_op jit(solution)/shard_map/ppermute | solution.py:21
  41.1 0.7 collective-permute-start.9
  41.8 0.7 collective-permute-done.13.refs_2_
  42.4 0.2 finish_rows.3.refs_0_
  42.7 1.5 %collective-permute-start.17 = (bf16[288,128]{1,0:T(8,128)(2,1)S(1)}, bf16[288,128]{1,0:T(8,128)(2,1)S(1)}, u32[]{:S(2)}, u32[]{:S(2)}) collective-permute-start(bf16[288,128]{1,0:T(8,128)(2,1)S(1)} %finish_rows.3.refs_0_), channel_id=1, source_target_pairs={{0,2},{1,3},{2,0},{3,1},{4,6},{5,7},{6,4},{7,5},{8,10},{9,11},{10,... | collective-permute-start | bytes 221192 | tf_op jit(solution)/shard_map/ppermute | solution.py:21
  44.2 0.6 collective-permute-start.15
  44.9 0.7 %collective-permute-done.10.refs_2_ = bf16[288,128]{1,0:T(8,128)(2,1)S(1)} collective-permute-done((bf16[288,128]{1,0:T(8,128)(2,1)S(1)}, bf16[288,128]{1,0:T(8,128)(2,1)S(1)}, u32[]{:S(2)}, u32[]{:S(2)}) %collective-permute-start.10) | collective-permute-done | bytes 73760 | tf_op jit(solution)/shard_map/ppermute | solution.py:21
  45.6 1.4 %absorb.1 = (f32[512,128]{1,0:T(8,128)S(1)}, f32[512,128]{1,0:T(8,128)S(1)}, f32[4,512,128]{2,1,0:T(8,128)S(1)}) custom-call(bf16[512,576]{1,0:T(8,128)(2,1)S(1)} %get-tuple-element.45.query_ref, s32[1,512]{1,0:T(1,128)S(1)} %get-tuple-element.46.slot_ref, f32[512,128]{1,0:T(8,128)S(1)} %get-tuple-element.49.top_ref, ...), custom_call_target="tpu_custom_call" | custom-call | flops 2000000000 | bytes 1000000 | tf_op jit(solution)/shard_map/absorb/pallas_call | solution.py:513
  47.0 0.1 collective-permute-done.17.refs_3_
  47.2 1.6 %collective-permute-done.16.refs_2_ = bf16[288,128]{1,0:T(8,128)(2,1)S(1)} collective-permute-done((bf16[288,128]{1,0:T(8,128)(2,1)S(1)}, bf16[288,128]{1,0:T(8,128)(2,1)S(1)}, u32[]{:S(2)}, u32[]{:S(2)}) %collective-permute-start.16) | collective-permute-done | bytes 73760 | tf_op jit(solution)/shard_map/ppermute | solution.py:21
  48.7 1.2 %attend.3.refs_0_ = bf16[16,2048]{1,0:T(8,128)(2,1)S(1)} custom-call(bf16[512,576]{1,0:T(8,128)(2,1)S(1)} %get-tuple-element.45.query_ref, s32[1,512]{1,0:T(1,128)S(1)} %get-tuple-element.46.slot_ref, f32[512,128]{1,0:T(8,128)S(1)} %get-tuple-element.65.top_ref, f32[512,128]{1,0:T(8,128)S(1)} %get-tuple-element.66.sum_ref, ...), custom_call_target="tpu_custom_call" | custom-call | tf_op jit(solution)/shard_map/attend/pallas_call | solution.py:546
  49.9 0.6 collective-permute-start.22
  50.6 1.2 %attend.2.refs_0_ = bf16[16,2048]{1,0:T(8,128)(2,1)S(1)} custom-call(bf16[512,576]{1,0:T(8,128)(2,1)S(1)} %get-tuple-element.45.query_ref, s32[1,512]{1,0:T(1,128)S(1)} %get-tuple-element.46.slot_ref, f32[512,128]{1,0:T(8,128)S(1)} %get-tuple-element.65.top_ref, f32[512,128]{1,0:T(8,128)S(1)} %get-tuple-element.66.sum_ref, ...), custom_call_target="tpu_custom_call" | custom-call | tf_op jit(solution)/shard_map/attend/pallas_call | solution.py:546
  51.7 2.4 %collective-permute-start.19 = (bf16[16,2048]{1,0:T(8,128)(2,1)S(1)}, bf16[16,2048]{1,0:T(8,128)(2,1)S(1)}, u32[]{:S(2)}, u32[]{:S(2)}) collective-permute-start(bf16[16,2048]{1,0:T(8,128)(2,1)S(1)} %attend.2.refs_0_), channel_id=1, source_target_pairs={{0,8},{4,12},{8,0},{12,4},{1,9},{5,13},{9,1},{13,5},{2,10},{6,14},... | collective-permute-start | bytes 196616 | tf_op jit(solution)/shard_map/ppermute | solution.py:21
  54.1 1.8 %collective-permute-done.22.refs_2_ = bf16[16,2048]{1,0:T(8,128)(2,1)S(1)} collective-permute-done((bf16[16,2048]{1,0:T(8,128)(2,1)S(1)}, bf16[16,2048]{1,0:T(8,128)(2,1)S(1)}, u32[]{:S(2)}, u32[]{:S(2)}) %collective-permute-start.22) | collective-permute-done | bytes 65568 | tf_op jit(solution)/shard_map/ppermute | solution.py:21
  55.9 0.2 collective-permute-start.23
  56.1 1.8 %collective-permute-start.18 = (bf16[16,2048]{1,0:T(8,128)(2,1)S(1)}, bf16[16,2048]{1,0:T(8,128)(2,1)S(1)}, u32[]{:S(2)}, u32[]{:S(2)}) collective-permute-start(bf16[16,2048]{1,0:T(8,128)(2,1)S(1)} %attend.2.refs_0_), channel_id=1, source_target_pairs={{0,4},{4,0},{8,12},{12,8},{1,5},{5,1},{9,13},{13,9},{2,6},{6,2},{1... | collective-permute-start | bytes 196616 | tf_op jit(solution)/shard_map/ppermute | solution.py:21
  57.9 0.0 collective-permute-done.19.refs_2_
  58.0 1.3 %collective-permute-start.20 = (bf16[16,2048]{1,0:T(8,128)(2,1)S(1)}, bf16[16,2048]{1,0:T(8,128)(2,1)S(1)}, u32[]{:S(2)}, u32[]{:S(2)}) collective-permute-start(bf16[16,2048]{1,0:T(8,128)(2,1)S(1)} %collective-permute-done.19.refs_2_), channel_id=1, source_target_pairs={{0,4},{4,0},{8,12},{12,8},{1,5},{5,1},{9,13},{13,9},{2,6},{6,2},{1... | collective-permute-start | bytes 196616 | tf_op jit(solution)/shard_map/ppermute | solution.py:21
  59.3 1.5 %collective-permute-done.23.refs_3_ = bf16[16,2048]{1,0:T(8,128)(2,1)S(1)} collective-permute-done((bf16[16,2048]{1,0:T(8,128)(2,1)S(1)}, bf16[16,2048]{1,0:T(8,128)(2,1)S(1)}, u32[]{:S(2)}, u32[]{:S(2)}) %collective-permute-start.23) | collective-permute-done | bytes 65568 | tf_op jit(solution)/shard_map/ppermute | solution.py:21
  60.9 1.4 %output_product.2.refs_5_ = f32[64,1792]{1,0:T(8,128)S(1)} custom-call(bf16[16,2048]{1,0:T(8,128)(2,1)S(1)} %attend.3.refs_0_, bf16[16,2048]{1,0:T(8,128)(2,1)S(1)} %collective-permute-done.21.refs_1_, bf16[16,2048]{1,0:T(8,128)(2,1)S(1)} %collective-permute-done.22.refs_2_, bf16[16,2048]{1,0:T(8,128)(2,1)S(1)} %collective-permute-done.23.refs_3_, ...), custom_call_target="tpu_custom_call" | custom-call | tf_op jit(solution)/shard_map/output_product/pallas_call | solution.py:600
  62.3 0.5 collective-permute-done.20.refs_3_
  62.9 1.4 %output_product.3 = (f32[16,1792]{1,0:T(8,128)S(1)}, bf16[16,1792]{1,0:T(8,128)(2,1)S(1)}, bf16[16,1792]{1,0:T(8,128)(2,1)S(1)}, bf16[16,1792]{1,0:T(8,128)(2,1)S(1)}) custom-call(bf16[16,2048]{1,0:T(8,128)(2,1)S(1)} %attend.2.refs_0_, bf16[16,2048]{1,0:T(8,128)(2,1)S(1)} %collective-permute-done.18.refs_1_, ...), custom_call_target="tpu_custom_call" | custom-call | tf_op jit(solution)/shard_map/output_product/pallas_call | solution.py:600
  64.3 1.4 %collective-permute-start.24 = (bf16[16,1792]{1,0:T(8,128)(2,1)S(1)}, bf16[16,1792]{1,0:T(8,128)(2,1)S(1)}, u32[]{:S(2)}, u32[]{:S(2)}) collective-permute-start(bf16[16,1792]{1,0:T(8,128)(2,1)S(1)} %get-tuple-element.76), channel_id=1, source_target_pairs={{0,2},{1,3},{2,0},{3,1},{4,6},{5,7},{6,4},{7,5},{8,10},{9,11},{10,... | collective-permute-start | bytes 172040 | tf_op jit(solution)/shard_map/ppermute | solution.py:21
  65.7 0.8 %collective-permute-start.26 = (bf16[16,1792]{1,0:T(8,128)(2,1)S(1)}, bf16[16,1792]{1,0:T(8,128)(2,1)S(1)}, u32[]{:S(2)}, u32[]{:S(2)}) collective-permute-start(bf16[16,1792]{1,0:T(8,128)(2,1)S(1)} %get-tuple-element.78), channel_id=1, source_target_pairs={{0,1},{1,0},{2,3},{3,2},{4,5},{5,4},{6,7},{7,6},{8,9},{9,8},{10,11... | collective-permute-start | bytes 172040 | tf_op jit(solution)/shard_map/ppermute | solution.py:21
  66.5 2.0 %collective-permute-done.24 = bf16[16,1792]{1,0:T(8,128)(2,1)S(1)} collective-permute-done((bf16[16,1792]{1,0:T(8,128)(2,1)S(1)}, bf16[16,1792]{1,0:T(8,128)(2,1)S(1)}, u32[]{:S(2)}, u32[]{:S(2)}) %collective-permute-start.24) | collective-permute-done | bytes 57376 | tf_op jit(solution)/shard_map/ppermute | solution.py:21
  68.5 1.2 %collective-permute-done.25 = bf16[16,1792]{1,0:T(8,128)(2,1)S(1)} collective-permute-done((bf16[16,1792]{1,0:T(8,128)(2,1)S(1)}, bf16[16,1792]{1,0:T(8,128)(2,1)S(1)}, u32[]{:S(2)}, u32[]{:S(2)}) %collective-permute-start.25) | collective-permute-done | bytes 57376 | tf_op jit(solution)/shard_map/ppermute | solution.py:21
  69.8 0.7 add_convert_fusion
  (40 shorter events, 0.1 us)
Async XLA Ops:
  0.0 7.1 %copy-start.4 = (bf16[448,576]{1,0:T(8,128)(2,1)S(1)}, bf16[448,576]{1,0:T(8,128)(2,1)}, u32[]{:S(2)}) copy-start(bf16[448,576]{1,0:T(8,128)(2,1)} %value_ref) | copy-start | bytes 1548292
  1.4 19.4 %collective-permute-start.1 = (bf16[64,1792]{1,0:T(8,128)(2,1)S(1)}, bf16[64,1792]{1,0:T(8,128)(2,1)S(1)}, u32[]{:S(2)}, u32[]{:S(2)}) collective-permute-start(bf16[64,1792]{1,0:T(8,128)(2,1)S(1)} %get-tuple-element.56), channel_id=1, source_target_pairs={{0,12},{4,8},{8,4},{12,0},{1,13},{5,9},{9,5},{13,1},{2,14},{6,10},... | collective-permute-start | bytes 688136 | tf_op jit(solution)/shard_map/ppermute | solution.py:21
  6.5 19.5 %collective-permute-start.2 = (bf16[64,1792]{1,0:T(8,128)(2,1)S(1)}, bf16[64,1792]{1,0:T(8,128)(2,1)S(1)}, u32[]{:S(2)}, u32[]{:S(2)}) collective-permute-start(bf16[64,1792]{1,0:T(8,128)(2,1)S(1)} %get-tuple-element.57), channel_id=1, source_target_pairs={{0,8},{4,12},{8,0},{12,4},{1,9},{5,13},{9,1},{13,5},{2,10},{6,14},... | collective-permute-start | bytes 688136 | tf_op jit(solution)/shard_map/ppermute | solution.py:21
  6.5 19.5 %collective-permute-start.3 = (bf16[64,1792]{1,0:T(8,128)(2,1)S(1)}, bf16[64,1792]{1,0:T(8,128)(2,1)S(1)}, u32[]{:S(2)}, u32[]{:S(2)}) collective-permute-start(bf16[64,1792]{1,0:T(8,128)(2,1)S(1)} %get-tuple-element.58), channel_id=1, source_target_pairs={{0,4},{4,0},{8,12},{12,8},{1,5},{5,1},{9,13},{13,9},{2,6},{6,2},{1... | collective-permute-start | bytes 688136 | tf_op jit(solution)/shard_map/ppermute | solution.py:21
  7.1 2.2 %copy-start.1 = (bf16[32,128,512]{2,1,0:T(8,128)(2,1)S(1)}, bf16[32,128,512]{2,1,0:T(8,128)(2,1)}, u32[]{:S(2)}) copy-start(bf16[32,128,512]{2,1,0:T(8,128)(2,1)} %absorb_hbm.1) | copy-start | bytes 12582916
  7.1 3.5 %copy-start.2 = (bf16[32,512,128]{2,1,0:T(8,128)(2,1)S(1)}, bf16[32,512,128]{2,1,0:T(8,128)(2,1)}, u32[]{:S(2)}) copy-start(bf16[32,512,128]{2,1,0:T(8,128)(2,1)} %value_hbm.1) | copy-start | bytes 12582916
  7.1 4.1 %copy-start.3 = (bf16[8,256,576]{1,2,0:T(8,128)(2,1)S(1)}, bf16[8,256,576]{1,2,0:T(8,128)(2,1)}, u32[]{:S(2)}) copy-start(bf16[8,256,576]{1,2,0:T(8,128)(2,1)} %param.18) | copy-start | bytes 7077892
  7.1 4.1 %copy-start.5 = (bf16[8,2,32,192]{3,2,1,0:T(8,128)(2,1)S(1)}, bf16[8,2,32,192]{3,2,1,0:T(8,128)(2,1)}, u32[]{:S(2)}) copy-start(bf16[8,2,32,192]{3,2,1,0:T(8,128)(2,1)} %param.20) | copy-start | bytes 589828
  7.2 4.1 %copy-start.6 = (bf16[8,2,576]{2,1,0:T(2,128)(2,1)S(1)}, bf16[8,2,576]{2,1,0:T(2,128)(2,1)}, u32[]{:S(2)}) copy-start(bf16[8,2,576]{2,1,0:T(2,128)(2,1)} %fresh_hbm.1) | copy-start | bytes 55300
  7.2 4.1 %copy-start.7 = (s32[1024]{0:T(1024)S(1)}, s32[1024]{0:T(1024)}, u32[]{:S(2)}) copy-start(s32[1024]{0:T(1024)} %param.15) | copy-start | bytes 12292
  7.2 4.1 %copy-start.8 = (s32[16]{0:T(128)S(1)}, s32[16]{0:T(128)}, u32[]{:S(2)}) copy-start(s32[16]{0:T(128)} %length_hbm) | copy-start | bytes 196
  7.2 4.1 %copy-start.9 = (s32[16]{0:T(128)S(1)}, s32[16]{0:T(128)}, u32[]{:S(2)}) copy-start(s32[16]{0:T(128)} %slot_hbm.1) | copy-start | bytes 196
  7.3 13.0 %collective-permute-start = (bf16[2016,128]{1,0:T(8,128)(2,1)S(1)}, bf16[2016,128]{1,0:T(8,128)(2,1)S(1)}, u32[]{:S(2)}, u32[]{:S(2)}) collective-permute-start(bf16[2016,128]{1,0:T(8,128)(2,1)S(1)} %pack_weight.1.refs_0_), channel_id=1, source_target_pairs={{0,2},{1,3},{2,0},{3,1},{4,6},{5,7},{6,4},{7,5},{8,10},{9,11},{10,... | collective-permute-start | bytes 1548296 | tf_op jit(solution)/shard_map/ppermute | solution.py:21
  20.3 19.1 %copy-start = (f32[512]{0:T(512)S(1)}, f32[512]{0:T(512)}, u32[]{:S(2)}) copy-start(f32[512]{0:T(512)} %param.14) | copy-start | bytes 6148
  20.3 5.8 %collective-permute-start.4 = (bf16[2016,128]{1,0:T(8,128)(2,1)S(1)}, bf16[2016,128]{1,0:T(8,128)(2,1)S(1)}, u32[]{:S(2)}, u32[]{:S(2)}) collective-permute-start(bf16[2016,128]{1,0:T(8,128)(2,1)S(1)} %pack_weight.1.refs_0_), channel_id=1, source_target_pairs={{0,1},{1,0},{2,3},{3,2},{4,5},{5,4},{6,7},{7,6},{8,9},{9,8},{10,11... | collective-permute-start | bytes 1548296 | tf_op jit(solution)/shard_map/ppermute | solution.py:21
  20.3 5.8 %collective-permute-start.5 = (bf16[2016,128]{1,0:T(8,128)(2,1)S(1)}, bf16[2016,128]{1,0:T(8,128)(2,1)S(1)}, u32[]{:S(2)}, u32[]{:S(2)}) collective-permute-start(bf16[2016,128]{1,0:T(8,128)(2,1)S(1)} %collective-permute-done.refs_2_), channel_id=1, source_target_pairs={{0,1},{1,0},{2,3},{3,2},{4,5},{5,4},{6,7},{7,6},{8,9},{9,8},{10,11... | collective-permute-start | bytes 1548296 | tf_op jit(solution)/shard_map/ppermute | solution.py:21
  27.8 6.9 %collective-permute-start.6 = (bf16[288,128]{1,0:T(8,128)(2,1)S(1)}, bf16[288,128]{1,0:T(8,128)(2,1)S(1)}, u32[]{:S(2)}, u32[]{:S(2)}) collective-permute-start(bf16[288,128]{1,0:T(8,128)(2,1)S(1)} %get-tuple-element.62), channel_id=1, source_target_pairs={{0,12},{4,8},{8,4},{12,0},{1,13},{5,9},{9,5},{13,1},{2,14},{6,10},... | collective-permute-start | bytes 221192 | tf_op jit(solution)/shard_map/ppermute | solution.py:21
  30.3 9.0 %collective-permute-start.7 = (bf16[288,128]{1,0:T(8,128)(2,1)S(1)}, bf16[288,128]{1,0:T(8,128)(2,1)S(1)}, u32[]{:S(2)}, u32[]{:S(2)}) collective-permute-start(bf16[288,128]{1,0:T(8,128)(2,1)S(1)} %get-tuple-element.63), channel_id=1, source_target_pairs={{0,8},{4,12},{8,0},{12,4},{1,9},{5,13},{9,1},{13,5},{2,10},{6,14},... | collective-permute-start | bytes 221192 | tf_op jit(solution)/shard_map/ppermute | solution.py:21
  30.3 9.0 %collective-permute-start.8 = (bf16[288,128]{1,0:T(8,128)(2,1)S(1)}, bf16[288,128]{1,0:T(8,128)(2,1)S(1)}, u32[]{:S(2)}, u32[]{:S(2)}) collective-permute-start(bf16[288,128]{1,0:T(8,128)(2,1)S(1)} %get-tuple-element.64), channel_id=1, source_target_pairs={{0,4},{4,0},{8,12},{12,8},{1,5},{5,1},{9,13},{13,9},{2,6},{6,2},{1... | collective-permute-start | bytes 221192 | tf_op jit(solution)/shard_map/ppermute | solution.py:21
  32.2 8.9 %collective-permute-start.12 = (bf16[288,128]{1,0:T(8,128)(2,1)S(1)}, bf16[288,128]{1,0:T(8,128)(2,1)S(1)}, u32[]{:S(2)}, u32[]{:S(2)}) collective-permute-start(bf16[288,128]{1,0:T(8,128)(2,1)S(1)} %get-tuple-element.71), channel_id=1, source_target_pairs={{0,12},{4,8},{8,4},{12,0},{1,13},{5,9},{9,5},{13,1},{2,14},{6,10},... | collective-permute-start | bytes 221192 | tf_op jit(solution)/shard_map/ppermute | solution.py:21
  34.7 7.7 %collective-permute-start.13 = (bf16[288,128]{1,0:T(8,128)(2,1)S(1)}, bf16[288,128]{1,0:T(8,128)(2,1)S(1)}, u32[]{:S(2)}, u32[]{:S(2)}) collective-permute-start(bf16[288,128]{1,0:T(8,128)(2,1)S(1)} %get-tuple-element.72), channel_id=1, source_target_pairs={{0,8},{4,12},{8,0},{12,4},{1,9},{5,13},{9,1},{13,5},{2,10},{6,14},... | collective-permute-start | bytes 221192 | tf_op jit(solution)/shard_map/ppermute | solution.py:21
  34.7 7.7 %collective-permute-start.14 = (bf16[288,128]{1,0:T(8,128)(2,1)S(1)}, bf16[288,128]{1,0:T(8,128)(2,1)S(1)}, u32[]{:S(2)}, u32[]{:S(2)}) collective-permute-start(bf16[288,128]{1,0:T(8,128)(2,1)S(1)} %get-tuple-element.73), channel_id=1, source_target_pairs={{0,4},{4,0},{8,12},{12,8},{1,5},{5,1},{9,13},{13,9},{2,6},{6,2},{1... | collective-permute-start | bytes 221192 | tf_op jit(solution)/shard_map/ppermute | solution.py:21
  39.6 4.6 %collective-permute-start.11 = (bf16[288,128]{1,0:T(8,128)(2,1)S(1)}, bf16[288,128]{1,0:T(8,128)(2,1)S(1)}, u32[]{:S(2)}, u32[]{:S(2)}) collective-permute-start(bf16[288,128]{1,0:T(8,128)(2,1)S(1)} %finish_rows.2.refs_0_), channel_id=1, source_target_pairs={{0,2},{1,3},{2,0},{3,1},{4,6},{5,7},{6,4},{7,5},{8,10},{9,11},{10,... | collective-permute-start | bytes 221192 | tf_op jit(solution)/shard_map/ppermute | solution.py:21
  41.1 4.5 %collective-permute-start.10 = (bf16[288,128]{1,0:T(8,128)(2,1)S(1)}, bf16[288,128]{1,0:T(8,128)(2,1)S(1)}, u32[]{:S(2)}, u32[]{:S(2)}) collective-permute-start(bf16[288,128]{1,0:T(8,128)(2,1)S(1)} %finish_rows.2.refs_0_), channel_id=1, source_target_pairs={{0,3},{1,2},{2,1},{3,0},{4,7},{5,6},{6,5},{7,4},{8,11},{9,10},{10,... | collective-permute-start | bytes 221192 | tf_op jit(solution)/shard_map/ppermute | solution.py:21
  41.1 4.4 %collective-permute-start.9 = (bf16[288,128]{1,0:T(8,128)(2,1)S(1)}, bf16[288,128]{1,0:T(8,128)(2,1)S(1)}, u32[]{:S(2)}, u32[]{:S(2)}) collective-permute-start(bf16[288,128]{1,0:T(8,128)(2,1)S(1)} %finish_rows.2.refs_0_), channel_id=1, source_target_pairs={{0,1},{1,0},{2,3},{3,2},{4,5},{5,4},{6,7},{7,6},{8,9},{9,8},{10,11... | collective-permute-start | bytes 221192 | tf_op jit(solution)/shard_map/ppermute | solution.py:21
  42.7 4.5 %collective-permute-start.17 = (bf16[288,128]{1,0:T(8,128)(2,1)S(1)}, bf16[288,128]{1,0:T(8,128)(2,1)S(1)}, u32[]{:S(2)}, u32[]{:S(2)}) collective-permute-start(bf16[288,128]{1,0:T(8,128)(2,1)S(1)} %finish_rows.3.refs_0_), channel_id=1, source_target_pairs={{0,2},{1,3},{2,0},{3,1},{4,6},{5,7},{6,4},{7,5},{8,10},{9,11},{10,... | collective-permute-start | bytes 221192 | tf_op jit(solution)/shard_map/ppermute | solution.py:21
  44.2 4.5 %collective-permute-start.16 = (bf16[288,128]{1,0:T(8,128)(2,1)S(1)}, bf16[288,128]{1,0:T(8,128)(2,1)S(1)}, u32[]{:S(2)}, u32[]{:S(2)}) collective-permute-start(bf16[288,128]{1,0:T(8,128)(2,1)S(1)} %finish_rows.3.refs_0_), channel_id=1, source_target_pairs={{0,3},{1,2},{2,1},{3,0},{4,7},{5,6},{6,5},{7,4},{8,11},{9,10},{10,... | collective-permute-start | bytes 221192 | tf_op jit(solution)/shard_map/ppermute | solution.py:21
  44.2 4.5 %collective-permute-start.15 = (bf16[288,128]{1,0:T(8,128)(2,1)S(1)}, bf16[288,128]{1,0:T(8,128)(2,1)S(1)}, u32[]{:S(2)}, u32[]{:S(2)}) collective-permute-start(bf16[288,128]{1,0:T(8,128)(2,1)S(1)} %finish_rows.3.refs_0_), channel_id=1, source_target_pairs={{0,1},{1,0},{2,3},{3,2},{4,5},{5,4},{6,7},{7,6},{8,9},{9,8},{10,11... | collective-permute-start | bytes 221192 | tf_op jit(solution)/shard_map/ppermute | solution.py:21
  49.9 6.0 %collective-permute-start.22 = (bf16[16,2048]{1,0:T(8,128)(2,1)S(1)}, bf16[16,2048]{1,0:T(8,128)(2,1)S(1)}, u32[]{:S(2)}, u32[]{:S(2)}) collective-permute-start(bf16[16,2048]{1,0:T(8,128)(2,1)S(1)} %attend.3.refs_0_), channel_id=1, source_target_pairs={{0,8},{4,12},{8,0},{12,4},{1,9},{5,13},{9,1},{13,5},{2,10},{6,14},... | collective-permute-start | bytes 196616 | tf_op jit(solution)/shard_map/ppermute | solution.py:21
  51.7 6.3 %collective-permute-start.19 = (bf16[16,2048]{1,0:T(8,128)(2,1)S(1)}, bf16[16,2048]{1,0:T(8,128)(2,1)S(1)}, u32[]{:S(2)}, u32[]{:S(2)}) collective-permute-start(bf16[16,2048]{1,0:T(8,128)(2,1)S(1)} %attend.2.refs_0_), channel_id=1, source_target_pairs={{0,8},{4,12},{8,0},{12,4},{1,9},{5,13},{9,1},{13,5},{2,10},{6,14},... | collective-permute-start | bytes 196616 | tf_op jit(solution)/shard_map/ppermute | solution.py:21
  54.1 5.2 %collective-permute-start.21 = (bf16[16,2048]{1,0:T(8,128)(2,1)S(1)}, bf16[16,2048]{1,0:T(8,128)(2,1)S(1)}, u32[]{:S(2)}, u32[]{:S(2)}) collective-permute-start(bf16[16,2048]{1,0:T(8,128)(2,1)S(1)} %attend.3.refs_0_), channel_id=1, source_target_pairs={{0,4},{4,0},{8,12},{12,8},{1,5},{5,1},{9,13},{13,9},{2,6},{6,2},{1... | collective-permute-start | bytes 196616 | tf_op jit(solution)/shard_map/ppermute | solution.py:21
  55.9 5.0 %collective-permute-start.23 = (bf16[16,2048]{1,0:T(8,128)(2,1)S(1)}, bf16[16,2048]{1,0:T(8,128)(2,1)S(1)}, u32[]{:S(2)}, u32[]{:S(2)}) collective-permute-start(bf16[16,2048]{1,0:T(8,128)(2,1)S(1)} %collective-permute-done.22.refs_2_), channel_id=1, source_target_pairs={{0,4},{4,0},{8,12},{12,8},{1,5},{5,1},{9,13},{13,9},{2,6},{6,2},{1... | collective-permute-start | bytes 196616 | tf_op jit(solution)/shard_map/ppermute | solution.py:21
  56.1 6.2 %collective-permute-start.18 = (bf16[16,2048]{1,0:T(8,128)(2,1)S(1)}, bf16[16,2048]{1,0:T(8,128)(2,1)S(1)}, u32[]{:S(2)}, u32[]{:S(2)}) collective-permute-start(bf16[16,2048]{1,0:T(8,128)(2,1)S(1)} %attend.2.refs_0_), channel_id=1, source_target_pairs={{0,4},{4,0},{8,12},{12,8},{1,5},{5,1},{9,13},{13,9},{2,6},{6,2},{1... | collective-permute-start | bytes 196616 | tf_op jit(solution)/shard_map/ppermute | solution.py:21
  58.0 4.9 %collective-permute-start.20 = (bf16[16,2048]{1,0:T(8,128)(2,1)S(1)}, bf16[16,2048]{1,0:T(8,128)(2,1)S(1)}, u32[]{:S(2)}, u32[]{:S(2)}) collective-permute-start(bf16[16,2048]{1,0:T(8,128)(2,1)S(1)} %collective-permute-done.19.refs_2_), channel_id=1, source_target_pairs={{0,4},{4,0},{8,12},{12,8},{1,5},{5,1},{9,13},{13,9},{2,6},{6,2},{1... | collective-permute-start | bytes 196616 | tf_op jit(solution)/shard_map/ppermute | solution.py:21
  64.3 4.2 %collective-permute-start.24 = (bf16[16,1792]{1,0:T(8,128)(2,1)S(1)}, bf16[16,1792]{1,0:T(8,128)(2,1)S(1)}, u32[]{:S(2)}, u32[]{:S(2)}) collective-permute-start(bf16[16,1792]{1,0:T(8,128)(2,1)S(1)} %get-tuple-element.76), channel_id=1, source_target_pairs={{0,2},{1,3},{2,0},{3,1},{4,6},{5,7},{6,4},{7,5},{8,10},{9,11},{10,... | collective-permute-start | bytes 172040 | tf_op jit(solution)/shard_map/ppermute | solution.py:21
  65.7 4.1 %collective-permute-start.25 = (bf16[16,1792]{1,0:T(8,128)(2,1)S(1)}, bf16[16,1792]{1,0:T(8,128)(2,1)S(1)}, u32[]{:S(2)}, u32[]{:S(2)}) collective-permute-start(bf16[16,1792]{1,0:T(8,128)(2,1)S(1)} %get-tuple-element.77), channel_id=1, source_target_pairs={{0,3},{1,2},{2,1},{3,0},{4,7},{5,6},{6,5},{7,4},{8,11},{9,10},{10,... | collective-permute-start | bytes 172040 | tf_op jit(solution)/shard_map/ppermute | solution.py:21
  65.7 4.1 %collective-permute-start.26 = (bf16[16,1792]{1,0:T(8,128)(2,1)S(1)}, bf16[16,1792]{1,0:T(8,128)(2,1)S(1)}, u32[]{:S(2)}, u32[]{:S(2)}) collective-permute-start(bf16[16,1792]{1,0:T(8,128)(2,1)S(1)} %get-tuple-element.78), channel_id=1, source_target_pairs={{0,1},{1,0},{2,3},{3,2},{4,5},{5,4},{6,7},{7,6},{8,9},{9,8},{10,11... | collective-permute-start | bytes 172040 | tf_op jit(solution)/shard_map/ppermute | solution.py:21
